TPU v7x, 32 devices: a whole 2x2x4 slice. The times are simulated.
32 devices in a mesh: ctx: 4 (over y, x), head: 8 (over z, core).
Axes of the slice: x: 2, y: 2, z: 4, core: 2. Of those that a mesh axis runs over, the one named last changes fastest.
Arguments:
- queries: bfloat16 [4096, 4096], P('ctx', 'head'), as said below
- keys: bfloat16 [4096, 4096], P('ctx', 'head'), as said below
- values: bfloat16 [4096, 4096], P('ctx', 'head'), may hold values from -6 to 6
- doc_ids: int32 [4096], P('ctx'), may hold values from 0 to 7, as said below
- w_out: bfloat16 [4096, 4096], P('head'), may hold values from -0.125 to 0.125
Outputs:
- mixed: bfloat16 [4096, 4096], P('ctx', 'head')
Inputs may be any that keep to these rules, and one draw needn't show every extreme that they name: `doc_ids`: within every draw the numbers never fall along sequence positions pos(g), so each document is a contiguous run of positions; every number from 0 to the largest names a document; documents have no fixed length. Entries of the queries lie within the stated range. Entries of the keys lie within the stated range.
All inputs are finite; a program needn't handle non-finite values.
Results may differ from a plain program's by a relative error of at most 0.018.
Values may be sent and summed in bfloat16 or wider, within the bound.
No kernel may reach another device: no remote copies, remote signals or barrier semaphores. Data moves between devices by JAX's collectives and lax.ppermute only.
A program may use at most 128 MiB of HBM per device.

v0:
```python
import functools
import math

import jax
import jax.numpy as jnp
from jax import lax
from jax.experimental import pallas as pl
from jax.experimental.pallas import tpu as pltpu
from jax.sharding import PartitionSpec as P

HD = 128


MASKED_SCORE = -1e30
LOG2E = 1.4426950408889634


def passed_along(value, axis, steps):
    count = lax.axis_size(axis)
    pairs = [(source, (source + steps) % count) for source in range(count)]
    return lax.ppermute(value, axis, pairs)


def folded_positions(row_total, offset, shard_rows, devices_ctx):
    flat_index = offset + lax.iota(jnp.int32, row_total)
    owner_dev = flat_index // shard_rows
    within = flat_index % shard_rows
    half_rows = shard_rows // 2
    fold_block = jnp.where(within < half_rows, owner_dev, 2 * devices_ctx - 1 - owner_dev)
    return fold_block * half_rows + within % half_rows


def block_update(
    running, query, query_pos, query_doc, key_block, value_block, pos_block, doc_block
):
    largest, totals, summed = running
    query_rows = query.shape[0]
    local_heads = query.shape[1] // HD
    query_heads = query.reshape(query_rows, local_heads, HD)
    key_heads = key_block.reshape(key_block.shape[0], local_heads, HD)
    value_heads = value_block.reshape(value_block.shape[0], local_heads, HD)
    scores = jnp.einsum(
        "qhd,khd->hqk", query_heads, key_heads, preferred_element_type=jnp.float32
    ) * (1.0 / math.sqrt(HD))
    allowed = (query_doc[:, None] == doc_block[None, :]) & (
        pos_block[None, :] <= query_pos[:, None]
    )
    scores = jnp.where(allowed[None], scores, MASKED_SCORE)
    new_max = jnp.maximum(largest, jnp.max(scores, axis=2))
    weights = jnp.where(allowed[None], jnp.exp(scores - new_max[:, :, None]), 0.0)
    factor = jnp.exp(largest - new_max)
    totals = totals * factor + jnp.sum(weights, axis=2)
    product = jnp.einsum(
        "hqk,khd->qhd",
        weights.astype(jnp.bfloat16),
        value_heads,
        preferred_element_type=jnp.float32,
    )
    summed = summed * factor.T[:, :, None] + product
    return (new_max, totals, summed)


def attend_rows(running, query, query_pos, query_doc, key_rows, value_rows, key_pos, key_doc):
    row_total = key_rows.shape[0]
    block_rows = math.gcd(row_total, query.shape[0])
    block_count = row_total // block_rows
    highest = jnp.max(query_pos)

    def visit(partial_value, blocks):
        key_block, value_block, pos_block, doc_block = blocks
        masked_out = jnp.min(pos_block) > highest
        updated = lax.cond(
            masked_out,
            lambda frozen: frozen,
            lambda frozen: block_update(
                frozen, query, query_pos, query_doc, key_block, value_block, pos_block, doc_block
            ),
            partial_value,
        )
        return (updated, None)

    blocks = (
        key_rows.reshape(block_count, block_rows, key_rows.shape[1]),
        value_rows.reshape(block_count, block_rows, value_rows.shape[1]),
        key_pos.reshape(block_count, block_rows),
        key_doc.reshape(block_count, block_rows),
    )
    running, _ = lax.scan(visit, running, blocks)
    return running


def attend_shard(running, query, query_pos, query_doc, key_rows, value_rows, key_pos, key_doc):
    largest, totals, summed = running
    half_rows = query.shape[0] // 2
    new_largest = []
    new_totals = []
    new_summed = []
    for half_idx in range(2):
        lower = half_idx * half_rows
        part_state = (largest[half_idx], totals[half_idx], summed[half_idx])
        part_state = attend_rows(
            part_state,
            query[lower : lower + half_rows],
            query_pos[lower : lower + half_rows],
            query_doc[lower : lower + half_rows],
            key_rows,
            value_rows,
            key_pos,
            key_doc,
        )
        new_largest.append(part_state[0])
        new_totals.append(part_state[1])
        new_summed.append(part_state[2])
    return (jnp.stack(new_largest), jnp.stack(new_totals), jnp.stack(new_summed))


def ring_local(queries, keys, values, doc_ids, w_out):
    shard_rows = queries.shape[0]
    half_rows = shard_rows // 2
    local_heads = queries.shape[1] // HD
    devices_ctx = lax.axis_size("ctx")
    ctx_index = lax.axis_index("ctx")
    all_docs = lax.all_gather(doc_ids, "ctx", axis=0, tiled=True)
    own_pos = folded_positions(shard_rows, ctx_index * shard_rows, shard_rows, devices_ctx)
    running = (
        jnp.full((2, local_heads, half_rows), MASKED_SCORE, jnp.float32),
        jnp.zeros((2, local_heads, half_rows), jnp.float32),
        jnp.zeros((2, half_rows, local_heads, HD), jnp.float32),
    )
    travel = queries
    for hop_step in range(devices_ctx):
        anchor = (ctx_index - hop_step) % devices_ctx
        query_pos = folded_positions(shard_rows, anchor * shard_rows, shard_rows, devices_ctx)
        query_doc = lax.dynamic_slice_in_dim(all_docs, anchor * shard_rows, shard_rows, 0)
        largest, totals, summed = attend_shard(
            running, travel, query_pos, query_doc, keys, values, own_pos, doc_ids
        )
        running = (
            passed_along(largest.astype(jnp.bfloat16), "ctx", 1).astype(largest.dtype),
            passed_along(totals.astype(jnp.bfloat16), "ctx", 1).astype(totals.dtype),
            passed_along(summed.astype(jnp.bfloat16), "ctx", 1).astype(summed.dtype),
        )
        if hop_step + 1 < devices_ctx:
            travel = passed_along(travel, "ctx", 1)
    largest, totals, summed = running
    attended = summed / totals.transpose(0, 2, 1)[:, :, :, None]
    attended = attended.reshape(shard_rows, local_heads * HD).astype(jnp.bfloat16)
    partial_out = jnp.dot(attended, w_out, preferred_element_type=jnp.float32)
    return lax.psum_scatter(
        partial_out.astype(jnp.bfloat16), "head", scatter_dimension=1, tiled=True
    )


def params(mib):
    return pltpu.CompilerParams(vmem_limit_bytes=mib * 1024 * 1024)


def cost(flops, moved):
    return pl.CostEstimate(flops=flops, bytes_accessed=moved, transcendentals=0)


def pack(ctx_index, half, queries, keys, values, docs):
    rows = queries.shape[0] // 2
    group = queries.shape[1] // HD
    doc_rows = 0 if docs is None else docs.shape[0]
    total = 3 * rows + doc_rows

    def kernel(ctx_ref, *refs):
        outs = refs[len(refs) - (group - 1) :]
        for place in range(group - 1):
            for part in range(3):
                outs[place][part * rows : (part + 1) * rows, :] = refs[place * 3 + part][...]
            if docs is not None:
                outs[place][3 * rows :, :] = refs[3 * (group - 1)][...]

    def piece(distance):
        return pl.BlockSpec((rows, HD), lambda step, ctx: (half, ctx[0] ^ distance))

    in_specs = []
    operands = []
    for distance in range(1, group):
        for array in (queries, keys, values):
            in_specs.append(piece(distance))
            operands.append(array)
    if docs is not None:
        in_specs.append(pl.BlockSpec(docs.shape, lambda step, ctx: (0, 0)))
        operands.append(docs)
    return pl.pallas_call(
        kernel,
        grid_spec=pltpu.PrefetchScalarGridSpec(
            num_scalar_prefetch=1,
            grid=(1,),
            in_specs=in_specs,
            out_specs=[pl.BlockSpec((total, HD), lambda step, ctx: (0, 0))] * (group - 1),
        ),
        out_shape=[jax.ShapeDtypeStruct((total, HD), jnp.bfloat16)] * (group - 1),
        compiler_params=params(24),
        cost_estimate=cost(0, 6 * (group - 1) * rows * HD * 2),
        name="pack",
    )(ctx_index, *operands)


def attend(ctx_index, queries, keys, values, docs, low, high):
    rows = queries.shape[0] // 2
    group = queries.shape[1] // HD
    with_high = high is not None
    blocks = 2 * group if with_high else group
    lanes = rows // HD
    scaling = LOG2E / math.sqrt(HD)

    def kernel(ctx_ref, *refs):
        refs = list(refs)
        own_low = [refs.pop(0) for _ in range(3)]
        own_high = [refs.pop(0) for _ in range(3)] if with_high else None
        own_docs = refs.pop(0)
        low_refs = [refs.pop(0) for _ in range(group - 1)]
        high_refs = [refs.pop(0) for _ in range(group - 1)] if with_high else None
        outs = [refs.pop(0) for _ in range(group)]
        key_buf, value_buf, doc_buf = refs
        ctx = ctx_ref[0]

        def part(upper, distance, index):
            if distance == 0:
                return (own_high if upper else own_low)[index][...]
            source = (high_refs if upper else low_refs)[distance - 1]
            return source[index * rows : (index + 1) * rows, :]

        first_doc = {}
        last_doc = {}
        place = {}
        doc_rows = {}
        for upper in (False, True) if with_high else (False,):
            for distance in range(group):
                source = ctx ^ distance
                block = 2 * group - 1 - source if upper else source
                place[upper, distance] = block
                offset = pl.multiple_of(block * rows, rows)
                key_buf[pl.ds(offset, rows), :] = part(upper, distance, 1)
                value_buf[pl.ds(offset, rows), :] = part(upper, distance, 2)
                if distance == 0:
                    both = own_docs[...]
                else:
                    both = low_refs[distance - 1][3 * rows :, :]
                both = both.astype(jnp.float32)
                begin = lanes if upper else 0
                mine = both[begin : begin + lanes, :]
                doc_rows[upper, distance] = mine
                doc_buf[pl.ds(block, 1), :] = jnp.concatenate(
                    [mine[line : line + 1, :] for line in range(lanes)], axis=1
                )
                first_doc[upper, distance] = jnp.min(mine)
                last_doc[upper, distance] = jnp.max(mine)

        row_index = lax.broadcasted_iota(jnp.int32, (rows, rows), 0)
        column_index = lax.broadcasted_iota(jnp.int32, (rows, rows), 1)
        for distance in range(group):
            me = (with_high, distance)
            block = place[me]
            query = part(with_high, distance, 0)
            mine = doc_rows[me]
            query_doc = jnp.concatenate(
                [
                    jnp.transpose(jnp.broadcast_to(mine[line : line + 1, :], (HD, HD)))
                    for line in range(lanes)
                ],
                axis=0,
            )[:, :1]
            start = jnp.int32(0)
            for other, last in last_doc.items():
                skip = jnp.logical_and(place[other] < block, last < first_doc[me])
                start = start + skip.astype(jnp.int32)

            def scores_of(index):
                offset = pl.multiple_of(index * rows, rows)
                raw = lax.dot_general(
                    query,
                    key_buf[pl.ds(offset, rows), :],
                    (((1,), (1,)), ((), ())),
                    preferred_element_type=jnp.float32,
                )
                same = query_doc == doc_buf[pl.ds(index, 1), :]
                return raw * scaling, same

            def weighted(weights, index):
                offset = pl.multiple_of(index * rows, rows)
                return jnp.dot(
                    weights.astype(jnp.bfloat16),
                    value_buf[pl.ds(offset, rows), :],
                    preferred_element_type=jnp.float32,
                )

            scores, same = scores_of(block)
            scores = jnp.where(same & (column_index <= row_index), scores, MASKED_SCORE)
            largest = jnp.max(scores, axis=1, keepdims=True)
            weights = jnp.exp2(scores - largest)
            totals = jnp.sum(weights, axis=1, keepdims=True)
            summed = weighted(weights, block)

            def visit(index, running):
                largest, totals, summed = running
                scores, same = scores_of(index)
                scores = jnp.where(same, scores, MASKED_SCORE)
                new_max = jnp.maximum(largest, jnp.max(scores, axis=1, keepdims=True))
                factor = jnp.exp2(largest - new_max)
                weights = jnp.exp2(scores - new_max)
                totals = totals * factor + jnp.sum(weights, axis=1, keepdims=True)
                summed = summed * factor + weighted(weights, index)
                return new_max, totals, summed

            largest, totals, summed = lax.fori_loop(
                start, block, visit, (largest, totals, summed)
            )
            outs[distance][...] = (summed / totals).astype(jnp.bfloat16)

    def own(upper):
        return pl.BlockSpec((rows, HD), lambda step, ctx: (int(upper), ctx[0]))

    def whole(array):
        return pl.BlockSpec(array.shape, lambda step, ctx: (0, 0))

    in_specs = [own(False)] * 3
    operands = [queries, keys, values]
    if with_high:
        in_specs += [own(True)] * 3
        operands += [queries, keys, values]
    operands += [docs, *low]
    in_specs += [whole(array) for array in (docs, *low)]
    if with_high:
        operands += list(high)
        in_specs += [whole(array) for array in high]
    pairs = group * 2 * rows * rows * HD * 2 * (3 if with_high else 2)
    return pl.pallas_call(
        kernel,
        grid_spec=pltpu.PrefetchScalarGridSpec(
            num_scalar_prefetch=1,
            grid=(1,),
            in_specs=in_specs,
            out_specs=[pl.BlockSpec((rows, HD), lambda step, ctx: (0, 0))] * group,
            scratch_shapes=[
                pltpu.VMEM((blocks * rows, HD), jnp.bfloat16),
                pltpu.VMEM((blocks * rows, HD), jnp.bfloat16),
                pltpu.VMEM((max(blocks, 8), rows), jnp.float32),
            ],
        ),
        out_shape=[jax.ShapeDtypeStruct((rows, HD), jnp.bfloat16)] * group,
        compiler_params=params(40),
        cost_estimate=cost(pairs, 8 * rows * HD * 2 * group),
        name="attend_high" if with_high else "attend_low",
    )(ctx_index, *operands)


def assemble(ctx_index, pieces):
    rows = pieces[0].shape[0]
    group = len(pieces)

    def kernel(ctx_ref, *refs):
        for distance in range(group):
            column = pl.multiple_of((ctx_ref[0] ^ distance) * HD, HD)
            refs[-1][:, pl.ds(column, HD)] = refs[distance][...]

    return pl.pallas_call(
        kernel,
        grid_spec=pltpu.PrefetchScalarGridSpec(
            num_scalar_prefetch=1,
            grid=(1,),
            in_specs=[pl.BlockSpec((rows, HD), lambda step, ctx: (0, 0))] * group,
            out_specs=pl.BlockSpec((rows, group * HD), lambda step, ctx: (0, 0)),
        ),
        out_shape=jax.ShapeDtypeStruct((rows, group * HD), jnp.bfloat16),
        compiler_params=params(16),
        cost_estimate=cost(0, 4 * rows * group * HD),
        name="assemble",
    )(ctx_index, *pieces)


def project(core, mine, sibling, w_mine, w_sibling, chips):
    rows, depth = mine.shape
    columns = w_mine.shape[1] // (2 * chips)

    def kernel(core_ref, mine_ref, sibling_ref, w_mine_ref, w_sibling_ref, out_ref):
        total = jnp.dot(mine_ref[...], w_mine_ref[...], preferred_element_type=jnp.float32)
        total += jnp.dot(sibling_ref[...], w_sibling_ref[...], preferred_element_type=jnp.float32)
        out_ref[0] = total.astype(jnp.bfloat16)

    return pl.pallas_call(
        kernel,
        grid_spec=pltpu.PrefetchScalarGridSpec(
            num_scalar_prefetch=1,
            grid=(chips,),
            in_specs=[
                pl.BlockSpec((rows, depth), lambda chip, core: (0, 0)),
                pl.BlockSpec((rows, depth), lambda chip, core: (0, 0)),
                pl.BlockSpec((depth, columns), lambda chip, core: (0, 2 * chip + core[0])),
                pl.BlockSpec((depth, columns), lambda chip, core: (0, chip)),
            ],
            out_specs=pl.BlockSpec((1, rows, columns), lambda chip, core: (chip, 0, 0)),
        ),
        out_shape=jax.ShapeDtypeStruct((chips, rows, columns), jnp.bfloat16),
        compiler_params=params(24),
        cost_estimate=cost(
            4 * rows * depth * columns * chips, 2 * chips * (rows + 2 * depth) * columns
        ),
        name="project",
    )(core, mine, sibling, w_mine, w_sibling)


def swap(value, axis, distance):
    count = lax.axis_size(axis)
    return lax.ppermute(value, axis, [(source, source ^ distance) for source in range(count)])


def line_reduce_scatter(shares, chip, chips):
    def share(index):
        return lax.dynamic_index_in_dim(shares, jnp.clip(index, 0, chips - 1), 0, keepdims=False)

    from_left = None
    from_right = None
    for step in range(1, chips):
        to_right = share(chips - step + chip)
        to_left = share(chip + step - chips)
        if step > 1:
            to_right = (to_right.astype(jnp.float32) + from_left.astype(jnp.float32)).astype(
                jnp.bfloat16
            )
            to_left = (to_left.astype(jnp.float32) + from_right.astype(jnp.float32)).astype(
                jnp.bfloat16
            )
        right_pairs = []
        left_pairs = []
        for source in range(step):
            for core in range(2):
                right_pairs.append((2 * source + core, 2 * source + 2 + core))
                mirrored = chips - 1 - source
                left_pairs.append((2 * mirrored + core, 2 * mirrored - 2 + core))
        from_left = lax.ppermute(to_right, "head", right_pairs)
        from_right = lax.ppermute(to_left, "head", left_pairs)
    total = share(chip).astype(jnp.float32)
    total = total + from_left.astype(jnp.float32) + from_right.astype(jnp.float32)
    return total.astype(jnp.bfloat16)


def exchange_local(queries, keys, values, doc_ids, w_out):
    shard_rows = queries.shape[0]
    group = queries.shape[1] // HD
    chips = lax.axis_size("head") // 2
    ctx_index = lax.axis_index("ctx").astype(jnp.int32).reshape(1)
    head_index = lax.axis_index("head").astype(jnp.int32)
    chip = head_index // 2
    core = head_index % 2

    docs = doc_ids.astype(jnp.bfloat16).reshape(shard_rows // HD, HD)
    docs = jnp.pad(docs, ((0, -docs.shape[0] % 16), (0, 0)))

    low_out = pack(ctx_index, 0, queries, keys, values, docs)
    low = [swap(low_out[distance - 1], "ctx", distance) for distance in range(1, group)]

    depth, width = w_out.shape
    w_split = w_out.reshape(depth, chips, 2, width // (2 * chips))
    w_give = lax.dynamic_index_in_dim(w_split, 1 - core, 2, keepdims=False)
    w_sibling = swap(w_give.reshape(depth, width // 2), "head", 1)

    high_out = pack(ctx_index, 1, queries, keys, values, None)
    *high_out, low[0], low[1], low[2] = lax.optimization_barrier((*high_out, *low))
    high = [swap(high_out[distance - 1], "ctx", distance) for distance in range(1, group)]

    results = []
    for half in range(2):
        pieces = attend(ctx_index, queries, keys, values, docs, low, high if half else None)
        back = [swap(pieces[distance], "ctx", distance) for distance in range(1, group)]
        mine = assemble(ctx_index, [pieces[0], *back])
        sibling = swap(mine, "head", 1)
        shares = project(core.reshape(1), mine, sibling, w_out, w_sibling, chips)
        results.append(line_reduce_scatter(shares, chip, chips))
    return jnp.concatenate(results, axis=0)


def solution(mesh):
    in_specs = (P("ctx", "head"), P("ctx", "head"), P("ctx", "head"), P("ctx"), P("head", None))
    out_specs = P("ctx", "head")
    ctx_count = mesh.shape["ctx"]
    head_count = mesh.shape["head"]

    def local(queries, keys, values, doc_ids, w_out):
        heads = queries.shape[1] // HD
        exchange = heads == ctx_count and heads == 4 and head_count % 2 == 0 and head_count > 2
        body = exchange_local if exchange else ring_local
        return body(queries, keys, values, doc_ids, w_out)

    return jax.shard_map(
        local, mesh=mesh, in_specs=in_specs, out_specs=out_specs, check_vma=False
    )
```

profile of v0, /device:TPU:8, one launch (start us, length us, event | category | flops | bytes accessed | tf_op | source)
XLA Modules:
  0.0 202.0 jit_solution(12934715665000151733)
XLA Ops:
  0.0 7.8 %reshape.40 = bf16[512,4,2,512]{3,2,1,0:T(2,128)(2,1)} reshape(bf16[512,4096]{1,0:T(8,128)(2,1)} %w_mine_ref.3) | data formatting | bytes 8388608 | tf_op jit(solution)/shard_map/reshape | solution.py:458
  7.8 14.3 %dynamic-slice_reduce_fusion = bf16[512,4,512]{2,1,0:T(4,128)(2,1)S(1)} fusion(bf16[512,4,2,512]{3,2,1,0:T(2,128)(2,1)} %reshape.40, s32[]{:T(128)S(6)} %select_n.31), kind=kLoop, calls=%fused_computation | loop fusion | bytes 4194308 | tf_op jit(solution)/shard_map/jit(dynamic_index_in_dim)/dynamic_slice | solution.py:459
  22.1 2.0 copy.8
  24.1 0.5 copy-done.2
  24.6 0.3 pack.3
  24.9 1.6 collective-permute-start
  26.5 1.5 collective-permute-start.1
  28.0 0.5 collective-permute-start.2
  28.5 0.3 pack.2
  28.8 8.3 %collective-permute-done.refs_4_.refs_7_ = bf16[1552,128]{1,0:T(8,128)(2,1)S(1)} collective-permute-done((bf16[1552,128]{1,0:T(8,128)(2,1)S(1)}, bf16[1552,128]{1,0:T(8,128)(2,1)S(1)}, u32[]{:S(2)}, u32[]{:S(2)}) %collective-permute-start) | collective-permute-done | bytes 397344 | tf_op jit(solution)/shard_map/ppermute | solution.py:409
  37.0 8.8 %collective-permute-done.1.refs_5_.refs_8_ = bf16[1552,128]{1,0:T(8,128)(2,1)S(1)} collective-permute-done((bf16[1552,128]{1,0:T(8,128)(2,1)S(1)}, bf16[1552,128]{1,0:T(8,128)(2,1)S(1)}, u32[]{:S(2)}, u32[]{:S(2)}) %collective-permute-start.1) | collective-permute-done | bytes 397344 | tf_op jit(solution)/shard_map/ppermute | solution.py:409
  45.9 6.5 %attend_low.1 = (bf16[512,128]{1,0:T(8,128)(2,1)S(1)}, bf16[512,128]{1,0:T(8,128)(2,1)S(1)}, bf16[512,128]{1,0:T(8,128)(2,1)S(1)}, bf16[512,128]{1,0:T(8,128)(2,1)S(1)}) custom-call(s32[1]{0:T(128)} %bitcast.1.ctx_ref, bf16[1024,512]{1,0:T(8,128)(2,1)S(1)} %copy-done, bf16[1024,512]{1,0:T(8,128)(2,1)S(1)} %copy-done.1, bf16[1024,512]{1,0:T(8,128)(2,1)S(1)} %copy-done.2, ...), custom_call_target="tpu_custom_call" | custom-call | flops 1073741824 | bytes 4194304 | tf_op jit(solution)/shard_map/attend_low/pallas_call | solution.py:332
  52.4 1.3 collective-permute-start.3
  53.7 0.8 collective-permute-start.14
  54.4 1.5 collective-permute-start.15
  56.0 1.2 collective-permute-start.16
  57.2 1.7 collective-permute-done.3.refs_1_
  58.9 1.5 collective-permute-start.4
  60.4 16.2 %collective-permute-done.4.refs_2_ = bf16[512,128]{1,0:T(8,128)(2,1)S(1)} collective-permute-done((bf16[512,128]{1,0:T(8,128)(2,1)S(1)}, bf16[512,128]{1,0:T(8,128)(2,1)S(1)}, u32[]{:S(2)}, u32[]{:S(2)}) %collective-permute-start.4) | collective-permute-done | bytes 131104 | tf_op jit(solution)/shard_map/ppermute | solution.py:409
  76.5 1.4 collective-permute-start.5
  78.0 4.4 %collective-permute-done.5.refs_3_ = bf16[512,128]{1,0:T(8,128)(2,1)S(1)} collective-permute-done((bf16[512,128]{1,0:T(8,128)(2,1)S(1)}, bf16[512,128]{1,0:T(8,128)(2,1)S(1)}, u32[]{:S(2)}, u32[]{:S(2)}) %collective-permute-start.5) | collective-permute-done | bytes 131104 | tf_op jit(solution)/shard_map/ppermute | solution.py:409
  82.4 0.9 assemble.2.mine_ref
  83.3 7.2 %attend_high.1 = (bf16[512,128]{1,0:T(8,128)(2,1)S(1)}, bf16[512,128]{1,0:T(8,128)(2,1)S(1)}, bf16[512,128]{1,0:T(8,128)(2,1)S(1)}, bf16[512,128]{1,0:T(8,128)(2,1)S(1)}) custom-call(s32[1]{0:T(128)} %bitcast.1.ctx_ref, bf16[1024,512]{1,0:T(8,128)(2,1)S(1)} %copy-done, bf16[1024,512]{1,0:T(8,128)(2,1)S(1)} %copy-done.1, bf16[1024,512]{1,0:T(8,128)(2,1)S(1)} %copy-done.2, ...), custom_call_target="tpu_custom_call" | custom-call | flops 1610612736 | bytes 4194304 | tf_op jit(solution)/shard_map/attend_high/pallas_call | solution.py:332
  90.5 1.5 collective-permute-start.17
  92.0 0.6 collective-permute-start.18
  92.6 1.5 collective-permute-start.19
  94.1 2.8 %collective-permute-done.17.refs_1_ = bf16[512,128]{1,0:T(8,128)(2,1)S(1)} collective-permute-done((bf16[512,128]{1,0:T(8,128)(2,1)S(1)}, bf16[512,128]{1,0:T(8,128)(2,1)S(1)}, u32[]{:S(2)}, u32[]{:S(2)}) %collective-permute-start.17) | collective-permute-done | bytes 131104 | tf_op jit(solution)/shard_map/ppermute | solution.py:409
  96.9 3.6 %collective-permute-done.18.refs_2_ = bf16[512,128]{1,0:T(8,128)(2,1)S(1)} collective-permute-done((bf16[512,128]{1,0:T(8,128)(2,1)S(1)}, bf16[512,128]{1,0:T(8,128)(2,1)S(1)}, u32[]{:S(2)}, u32[]{:S(2)}) %collective-permute-start.18) | collective-permute-done | bytes 131104 | tf_op jit(solution)/shard_map/ppermute | solution.py:409
  100.5 0.1 assemble.3.mine_ref
  100.6 0.1 collective-permute-start.20
  100.7 2.2 %copy-done.3 = bf16[512,4096]{1,0:T(8,128)(2,1)S(1)} copy-done((bf16[512,4096]{1,0:T(8,128)(2,1)S(1)}, bf16[512,4096]{1,0:T(8,128)(2,1)}, u32[]{:S(2)}) %copy-start.3) | copy-done | bytes 4194328
  102.9 4.7 %project.2 = bf16[4,512,512]{2,1,0:T(8,128)(2,1)S(1)} custom-call(s32[1]{0:T(128)} %bitcast.core_ref, bf16[512,512]{1,0:T(8,128)(2,1)} %assemble.2.mine_ref, bf16[512,512]{1,0:T(8,128)(2,1)} %collective-permute-done.6.sibling_ref, bf16[512,4096]{1,0:T(8,128)(2,1)S(1)} %copy-done.3, bf16[512,2048]{1,0:T(8,128)(2,1)} %collective-permute-done.7.w_sibling_ref), custom_call_target="tpu_custom_call" | custom-call | flops 2147483648 | bytes 6291456 | tf_op jit(solution)/shard_map/project/pallas_call | solution.py:385
  107.6 1.1 dynamic-slice_bitcast_fusion.3
  108.7 1.3 collective-permute-start.8
  110.0 4.4 %project.3 = bf16[4,512,512]{2,1,0:T(8,128)(2,1)S(1)} custom-call(s32[1]{0:T(128)} %bitcast.core_ref, bf16[512,512]{1,0:T(8,128)(2,1)S(1)} %assemble.3.mine_ref, bf16[512,512]{1,0:T(8,128)(2,1)S(1)} %collective-permute-done.20.sibling_ref, bf16[512,4096]{1,0:T(8,128)(2,1)S(1)} %copy-done.3, bf16[512,2048]{1,0:T(8,128)(2,1)} %collective-permute-done.7.w_sibling_ref), custom_call_target="tpu_custom_call" | custom-call | flops 2147483648 | bytes 6291456 | tf_op jit(solution)/shard_map/project/pallas_call | solution.py:385
  114.4 1.4 copy-done.4
  115.8 0.9 dynamic-slice_bitcast_fusion.1
  116.6 1.3 collective-permute-start.21
  117.9 1.5 collective-permute-start.11
  119.4 6.2 %collective-permute-done.8 = bf16[512,512]{1,0:T(8,128)(2,1)} collective-permute-done((bf16[512,512]{1,0:T(8,128)(2,1)}, bf16[512,512]{1,0:T(8,128)(2,1)}, u32[]{:S(2)}, u32[]{:S(2)}) %collective-permute-start.8) | collective-permute-done | bytes 524320 | tf_op jit(solution)/shard_map/ppermute | solution.py:435
  125.6 1.2 fusion.8
  126.8 1.9 collective-permute-start.9
  128.7 1.5 collective-permute-start.24
  130.2 6.7 %collective-permute-done.21 = bf16[512,512]{1,0:T(8,128)(2,1)} collective-permute-done((bf16[512,512]{1,0:T(8,128)(2,1)S(1)}, bf16[512,512]{1,0:T(8,128)(2,1)}, u32[]{:S(2)}, u32[]{:S(2)}) %collective-permute-start.21) | collective-permute-done | bytes 524320 | tf_op jit(solution)/shard_map/ppermute | solution.py:435
  136.8 1.3 fusion.2
  138.2 1.9 collective-permute-start.22
  140.1 7.9 %collective-permute-done.9 = bf16[512,512]{1,0:T(8,128)(2,1)} collective-permute-done((bf16[512,512]{1,0:T(8,128)(2,1)S(1)}, bf16[512,512]{1,0:T(8,128)(2,1)}, u32[]{:S(2)}, u32[]{:S(2)}) %collective-permute-start.9) | collective-permute-done | bytes 524320 | tf_op jit(solution)/shard_map/ppermute | solution.py:435
  148.1 2.5 %fusion.9 = (bf16[512,512]{1,0:T(8,128)(2,1)}, bf16[512,512]{1,0:T(8,128)(2,1)}) fusion(bf16[512,512]{1,0:T(8,128)(2,1)} %collective-permute-done.9, bf16[4,512,512]{2,1,0:T(8,128)(2,1)S(1)} %project.2, s32[]{:T(128)S(6)} %min.30, bf16[512,512]{1,0:T(8,128)(2,1)} %collective-permute-done.11, s32[]{:T(128)S(6)} %min.34), kind=kLoop, calls=%fused_computation.20 | loop fusion | flops 2097152 | bytes 3145736 | tf_op jit(solution)/shard_map/convert_element_type | solution.py:422
  150.6 1.3 collective-permute-start.12
  151.9 7.0 %collective-permute-done.22 = bf16[512,512]{1,0:T(8,128)(2,1)} collective-permute-done((bf16[512,512]{1,0:T(8,128)(2,1)S(1)}, bf16[512,512]{1,0:T(8,128)(2,1)}, u32[]{:S(2)}, u32[]{:S(2)}) %collective-permute-start.22) | collective-permute-done | bytes 524320 | tf_op jit(solution)/shard_map/ppermute | solution.py:435
  158.9 2.5 %fusion.3 = (bf16[512,512]{1,0:T(8,128)(2,1)}, bf16[512,512]{1,0:T(8,128)(2,1)}) fusion(bf16[512,512]{1,0:T(8,128)(2,1)} %collective-permute-done.22, bf16[4,512,512]{2,1,0:T(8,128)(2,1)S(1)} %copy-done.5, s32[]{:T(128)S(6)} %min.30, bf16[512,512]{1,0:T(8,128)(2,1)} %collective-permute-done.24, s32[]{:T(128)S(6)} %min.34), kind=kLoop, calls=%fused_computation.9 | loop fusion | flops 2097152 | bytes 3145736 | tf_op jit(solution)/shard_map/convert_element_type | solution.py:422
  161.3 1.3 collective-permute-start.25
  162.6 4.6 %collective-permute-start.10 = (bf16[512,512]{1,0:T(8,128)(2,1)}, bf16[512,512]{1,0:T(8,128)(2,1)S(1)}, u32[]{:S(2)}, u32[]{:S(2)}) collective-permute-start(bf16[512,512]{1,0:T(8,128)(2,1)} %get-tuple-element.45), channel_id=1, source_target_pairs={{0,2},{1,3},{2,4},{3,5},{4,6},{5,7},{8,10},{9,11},{10,12},{11,13},... | collective-permute-start | bytes 1572872 | tf_op jit(solution)/shard_map/ppermute | solution.py:435
  167.2 0.9 fusion.7
  168.1 1.9 collective-permute-start.13
  170.0 3.9 %collective-permute-start.23 = (bf16[512,512]{1,0:T(8,128)(2,1)}, bf16[512,512]{1,0:T(8,128)(2,1)S(1)}, u32[]{:S(2)}, u32[]{:S(2)}) collective-permute-start(bf16[512,512]{1,0:T(8,128)(2,1)} %get-tuple-element.49), channel_id=1, source_target_pairs={{0,2},{1,3},{2,4},{3,5},{4,6},{5,7},{8,10},{9,11},{10,12},{11,13},... | collective-permute-start | bytes 1572872 | tf_op jit(solution)/shard_map/ppermute | solution.py:435
  174.0 4.4 %collective-permute-done.25 = bf16[512,512]{1,0:T(8,128)(2,1)} collective-permute-done((bf16[512,512]{1,0:T(8,128)(2,1)}, bf16[512,512]{1,0:T(8,128)(2,1)}, u32[]{:S(2)}, u32[]{:S(2)}) %collective-permute-start.25) | collective-permute-done | bytes 524320 | tf_op jit(solution)/shard_map/ppermute | solution.py:436
  178.4 2.1 %fusion.1 = bf16[512,512]{1,0:T(8,128)(2,1)} fusion(bf16[512,512]{1,0:T(8,128)(2,1)} %collective-permute-done.25, bf16[4,512,512]{2,1,0:T(8,128)(2,1)} %copy-done.4, s32[]{:T(128)S(6)} %min.33), kind=kLoop, calls=%fused_computation.5 | loop fusion | flops 1048576 | bytes 1572868 | tf_op jit(solution)/shard_map/convert_element_type | solution.py:425
  180.5 1.9 collective-permute-start.26
  182.4 7.2 %collective-permute-done.13 = bf16[512,512]{1,0:T(8,128)(2,1)} collective-permute-done((bf16[512,512]{1,0:T(8,128)(2,1)}, bf16[512,512]{1,0:T(8,128)(2,1)}, u32[]{:S(2)}, u32[]{:S(2)}) %collective-permute-start.13) | collective-permute-done | bytes 524320 | tf_op jit(solution)/shard_map/ppermute | solution.py:436
  189.6 1.2 fusion.11
  190.9 8.7 %collective-permute-done.26 = bf16[512,512]{1,0:T(8,128)(2,1)} collective-permute-done((bf16[512,512]{1,0:T(8,128)(2,1)}, bf16[512,512]{1,0:T(8,128)(2,1)}, u32[]{:S(2)}, u32[]{:S(2)}) %collective-permute-start.26) | collective-permute-done | bytes 524320 | tf_op jit(solution)/shard_map/ppermute | solution.py:436
  199.5 1.4 fusion.5
  201.0 1.0 pad_maximum_fusion
  (28 shorter events, 0.1 us)
Async XLA Ops:
  22.1 2.0 copy-start.6
  22.1 2.0 %copy-start = (bf16[1024,512]{1,0:T(8,128)(2,1)S(1)}, bf16[1024,512]{1,0:T(8,128)(2,1)}, u32[]{:S(2)}) copy-start(bf16[1024,512]{1,0:T(8,128)(2,1)} %refs_3_.5) | copy-start | bytes 3145732
  22.1 2.0 %copy-start.1 = (bf16[1024,512]{1,0:T(8,128)(2,1)S(1)}, bf16[1024,512]{1,0:T(8,128)(2,1)}, u32[]{:S(2)}) copy-start(bf16[1024,512]{1,0:T(8,128)(2,1)} %refs_4_.5) | copy-start | bytes 3145732
  22.1 2.5 %copy-start.2 = (bf16[1024,512]{1,0:T(8,128)(2,1)S(1)}, bf16[1024,512]{1,0:T(8,128)(2,1)}, u32[]{:S(2)}) copy-start(bf16[1024,512]{1,0:T(8,128)(2,1)} %refs_5_.5) | copy-start | bytes 3145732
  24.1 76.6 %collective-permute-start.7 = (bf16[512,2048]{1,0:T(8,128)(2,1)}, bf16[512,2048]{1,0:T(8,128)(2,1)}, u32[]{:S(2)}, u32[]{:S(2)}) collective-permute-start(bf16[512,2048]{1,0:T(8,128)(2,1)} %bitcast.28), channel_id=1, source_target_pairs={{0,1},{1,0},{2,3},{3,2},{4,5},{5,4},{6,7},{7,6},{8,9},{9,8},{10,11... | collective-permute-start | bytes 6291464 | tf_op jit(solution)/shard_map/ppermute | solution.py:409
  24.9 12.1 %collective-permute-start = (bf16[1552,128]{1,0:T(8,128)(2,1)S(1)}, bf16[1552,128]{1,0:T(8,128)(2,1)S(1)}, u32[]{:S(2)}, u32[]{:S(2)}) collective-permute-start(bf16[1552,128]{1,0:T(8,128)(2,1)S(1)} %get-tuple-element.28), channel_id=1, source_target_pairs={{0,8},{8,0},{16,24},{24,16},{1,9},{9,1},{17,25},{25,17},{2,10},{10... | collective-permute-start | bytes 1191944 | tf_op jit(solution)/shard_map/ppermute | solution.py:409
  26.5 19.4 %collective-permute-start.1 = (bf16[1552,128]{1,0:T(8,128)(2,1)S(1)}, bf16[1552,128]{1,0:T(8,128)(2,1)S(1)}, u32[]{:S(2)}, u32[]{:S(2)}) collective-permute-start(bf16[1552,128]{1,0:T(8,128)(2,1)S(1)} %get-tuple-element.29), channel_id=1, source_target_pairs={{0,16},{8,24},{16,0},{24,8},{1,17},{9,25},{17,1},{25,9},{2,18},{10... | collective-permute-start | bytes 1191944 | tf_op jit(solution)/shard_map/ppermute | solution.py:409
  28.0 17.9 %collective-permute-start.2 = (bf16[1552,128]{1,0:T(8,128)(2,1)S(1)}, bf16[1552,128]{1,0:T(8,128)(2,1)S(1)}, u32[]{:S(2)}, u32[]{:S(2)}) collective-permute-start(bf16[1552,128]{1,0:T(8,128)(2,1)S(1)} %get-tuple-element.30), channel_id=1, source_target_pairs={{0,24},{8,16},{16,8},{24,0},{1,25},{9,17},{17,9},{25,1},{2,26},{10... | collective-permute-start | bytes 1191944 | tf_op jit(solution)/shard_map/ppermute | solution.py:409
  52.4 6.5 %collective-permute-start.3 = (bf16[512,128]{1,0:T(8,128)(2,1)S(1)}, bf16[512,128]{1,0:T(8,128)(2,1)S(1)}, u32[]{:S(2)}, u32[]{:S(2)}) collective-permute-start(bf16[512,128]{1,0:T(8,128)(2,1)S(1)} %get-tuple-element.35), channel_id=1, source_target_pairs={{0,8},{8,0},{16,24},{24,16},{1,9},{9,1},{17,25},{25,17},{2,10},{10... | collective-permute-start | bytes 393224 | tf_op jit(solution)/shard_map/ppermute | solution.py:409
  53.7 29.6 %collective-permute-start.14 = (bf16[1536,128]{1,0:T(8,128)(2,1)S(1)}, bf16[1536,128]{1,0:T(8,128)(2,1)S(1)}, u32[]{:S(2)}, u32[]{:S(2)}) collective-permute-start(bf16[1536,128]{1,0:T(8,128)(2,1)S(1)} %get-tuple-element.38), channel_id=1, source_target_pairs={{0,8},{8,0},{16,24},{24,16},{1,9},{9,1},{17,25},{25,17},{2,10},{10... | collective-permute-start | bytes 1179656 | tf_op jit(solution)/shard_map/ppermute | solution.py:409
  54.4 28.8 %collective-permute-start.15 = (bf16[1536,128]{1,0:T(8,128)(2,1)S(1)}, bf16[1536,128]{1,0:T(8,128)(2,1)S(1)}, u32[]{:S(2)}, u32[]{:S(2)}) collective-permute-start(bf16[1536,128]{1,0:T(8,128)(2,1)S(1)} %get-tuple-element.39), channel_id=1, source_target_pairs={{0,16},{8,24},{16,0},{24,8},{1,17},{9,25},{17,1},{25,9},{2,18},{10... | collective-permute-start | bytes 1179656 | tf_op jit(solution)/shard_map/ppermute | solution.py:409
  56.0 27.3 %collective-permute-start.16 = (bf16[1536,128]{1,0:T(8,128)(2,1)S(1)}, bf16[1536,128]{1,0:T(8,128)(2,1)S(1)}, u32[]{:S(2)}, u32[]{:S(2)}) collective-permute-start(bf16[1536,128]{1,0:T(8,128)(2,1)S(1)} %get-tuple-element.40), channel_id=1, source_target_pairs={{0,24},{8,16},{16,8},{24,0},{1,25},{9,17},{17,9},{25,1},{2,26},{10... | collective-permute-start | bytes 1179656 | tf_op jit(solution)/shard_map/ppermute | solution.py:409
  58.9 17.7 %collective-permute-start.4 = (bf16[512,128]{1,0:T(8,128)(2,1)S(1)}, bf16[512,128]{1,0:T(8,128)(2,1)S(1)}, u32[]{:S(2)}, u32[]{:S(2)}) collective-permute-start(bf16[512,128]{1,0:T(8,128)(2,1)S(1)} %get-tuple-element.36), channel_id=1, source_target_pairs={{0,16},{8,24},{16,0},{24,8},{1,17},{9,25},{17,1},{25,9},{2,18},{10... | collective-permute-start | bytes 393224 | tf_op jit(solution)/shard_map/ppermute | solution.py:409
  76.5 5.9 %collective-permute-start.5 = (bf16[512,128]{1,0:T(8,128)(2,1)S(1)}, bf16[512,128]{1,0:T(8,128)(2,1)S(1)}, u32[]{:S(2)}, u32[]{:S(2)}) collective-permute-start(bf16[512,128]{1,0:T(8,128)(2,1)S(1)} %get-tuple-element.37), channel_id=1, source_target_pairs={{0,24},{8,16},{16,8},{24,0},{1,25},{9,17},{17,9},{25,1},{2,26},{10... | collective-permute-start | bytes 393224 | tf_op jit(solution)/shard_map/ppermute | solution.py:409
  83.3 17.4 %collective-permute-start.6 = (bf16[512,512]{1,0:T(8,128)(2,1)}, bf16[512,512]{1,0:T(8,128)(2,1)}, u32[]{:S(2)}, u32[]{:S(2)}) collective-permute-start(bf16[512,512]{1,0:T(8,128)(2,1)} %assemble.2.mine_ref), channel_id=1, source_target_pairs={{0,1},{1,0},{2,3},{3,2},{4,5},{5,4},{6,7},{7,6},{8,9},{9,8},{10,11... | collective-permute-start | bytes 1572872 | tf_op jit(solution)/shard_map/ppermute | solution.py:409
  90.5 6.4 %collective-permute-start.17 = (bf16[512,128]{1,0:T(8,128)(2,1)S(1)}, bf16[512,128]{1,0:T(8,128)(2,1)S(1)}, u32[]{:S(2)}, u32[]{:S(2)}) collective-permute-start(bf16[512,128]{1,0:T(8,128)(2,1)S(1)} %get-tuple-element.42), channel_id=1, source_target_pairs={{0,8},{8,0},{16,24},{24,16},{1,9},{9,1},{17,25},{25,17},{2,10},{10... | collective-permute-start | bytes 393224 | tf_op jit(solution)/shard_map/ppermute | solution.py:409
  92.0 8.4 %collective-permute-start.18 = (bf16[512,128]{1,0:T(8,128)(2,1)S(1)}, bf16[512,128]{1,0:T(8,128)(2,1)S(1)}, u32[]{:S(2)}, u32[]{:S(2)}) collective-permute-start(bf16[512,128]{1,0:T(8,128)(2,1)S(1)} %get-tuple-element.43), channel_id=1, source_target_pairs={{0,16},{8,24},{16,0},{24,8},{1,17},{9,25},{17,1},{25,9},{2,18},{10... | collective-permute-start | bytes 393224 | tf_op jit(solution)/shard_map/ppermute | solution.py:409
  92.6 7.9 %collective-permute-start.19 = (bf16[512,128]{1,0:T(8,128)(2,1)S(1)}, bf16[512,128]{1,0:T(8,128)(2,1)S(1)}, u32[]{:S(2)}, u32[]{:S(2)}) collective-permute-start(bf16[512,128]{1,0:T(8,128)(2,1)S(1)} %get-tuple-element.44), channel_id=1, source_target_pairs={{0,24},{8,16},{16,8},{24,0},{1,25},{9,17},{17,9},{25,1},{2,26},{10... | collective-permute-start | bytes 393224 | tf_op jit(solution)/shard_map/ppermute | solution.py:409
  100.6 9.4 %collective-permute-start.20 = (bf16[512,512]{1,0:T(8,128)(2,1)S(1)}, bf16[512,512]{1,0:T(8,128)(2,1)S(1)}, u32[]{:S(2)}, u32[]{:S(2)}) collective-permute-start(bf16[512,512]{1,0:T(8,128)(2,1)S(1)} %assemble.3.mine_ref), channel_id=1, source_target_pairs={{0,1},{1,0},{2,3},{3,2},{4,5},{5,4},{6,7},{7,6},{8,9},{9,8},{10,11... | collective-permute-start | bytes 1572872 | tf_op jit(solution)/shard_map/ppermute | solution.py:409
  100.7 2.2 %copy-start.3 = (bf16[512,4096]{1,0:T(8,128)(2,1)S(1)}, bf16[512,4096]{1,0:T(8,128)(2,1)}, u32[]{:S(2)}) copy-start(bf16[512,4096]{1,0:T(8,128)(2,1)} %w_mine_ref.3) | copy-start | bytes 12582916
  108.7 16.9 %collective-permute-start.8 = (bf16[512,512]{1,0:T(8,128)(2,1)}, bf16[512,512]{1,0:T(8,128)(2,1)}, u32[]{:S(2)}, u32[]{:S(2)}) collective-permute-start(bf16[512,512]{1,0:T(8,128)(2,1)} %get-tuple-element.47), channel_id=1, source_target_pairs={{0,2},{1,3},{8,10},{9,11},{16,18},{17,19},{24,26},{25,27}} | collective-permute-start | bytes 1572872 | tf_op jit(solution)/shard_map/ppermute | solution.py:435
  114.4 1.4 copy-start.4
  116.6 20.2 %collective-permute-start.21 = (bf16[512,512]{1,0:T(8,128)(2,1)S(1)}, bf16[512,512]{1,0:T(8,128)(2,1)}, u32[]{:S(2)}, u32[]{:S(2)}) collective-permute-start(bf16[512,512]{1,0:T(8,128)(2,1)S(1)} %get-tuple-element.51), channel_id=1, source_target_pairs={{0,2},{1,3},{8,10},{9,11},{16,18},{17,19},{24,26},{25,27}} | collective-permute-start | bytes 1572872 | tf_op jit(solution)/shard_map/ppermute | solution.py:435
  117.9 22.2 %collective-permute-start.11 = (bf16[512,512]{1,0:T(8,128)(2,1)}, bf16[512,512]{1,0:T(8,128)(2,1)}, u32[]{:S(2)}, u32[]{:S(2)}) collective-permute-start(bf16[512,512]{1,0:T(8,128)(2,1)} %get-tuple-element.48), channel_id=1, source_target_pairs={{6,4},{7,5},{14,12},{15,13},{22,20},{23,21},{30,28},{31,29}} | collective-permute-start | bytes 1572872 | tf_op jit(solution)/shard_map/ppermute | solution.py:436
  126.8 21.3 %collective-permute-start.9 = (bf16[512,512]{1,0:T(8,128)(2,1)S(1)}, bf16[512,512]{1,0:T(8,128)(2,1)}, u32[]{:S(2)}, u32[]{:S(2)}) collective-permute-start(bf16[512,512]{1,0:T(8,128)(2,1)S(1)} %fusion.8), channel_id=1, source_target_pairs={{0,2},{1,3},{2,4},{3,5},{8,10},{9,11},{10,12},{11,13},{16,18},{17,... | collective-permute-start | bytes 1572872 | tf_op jit(solution)/shard_map/ppermute | solution.py:435
  128.7 23.2 %collective-permute-start.24 = (bf16[512,512]{1,0:T(8,128)(2,1)}, bf16[512,512]{1,0:T(8,128)(2,1)}, u32[]{:S(2)}, u32[]{:S(2)}) collective-permute-start(bf16[512,512]{1,0:T(8,128)(2,1)} %get-tuple-element.52), channel_id=1, source_target_pairs={{6,4},{7,5},{14,12},{15,13},{22,20},{23,21},{30,28},{31,29}} | collective-permute-start | bytes 1572872 | tf_op jit(solution)/shard_map/ppermute | solution.py:436
  138.2 20.7 %collective-permute-start.22 = (bf16[512,512]{1,0:T(8,128)(2,1)S(1)}, bf16[512,512]{1,0:T(8,128)(2,1)}, u32[]{:S(2)}, u32[]{:S(2)}) collective-permute-start(bf16[512,512]{1,0:T(8,128)(2,1)S(1)} %fusion.2), channel_id=1, source_target_pairs={{0,2},{1,3},{2,4},{3,5},{8,10},{9,11},{10,12},{11,13},{16,18},{17,... | collective-permute-start | bytes 1572872 | tf_op jit(solution)/shard_map/ppermute | solution.py:435
  140.1 18.8 %copy-start.5 = (bf16[4,512,512]{2,1,0:T(8,128)(2,1)S(1)}, bf16[4,512,512]{2,1,0:T(8,128)(2,1)}, u32[]{:S(2)}) copy-start(bf16[4,512,512]{2,1,0:T(8,128)(2,1)} %copy-done.4) | copy-start | bytes 6291460
  150.6 16.6 %collective-permute-start.12 = (bf16[512,512]{1,0:T(8,128)(2,1)}, bf16[512,512]{1,0:T(8,128)(2,1)S(1)}, u32[]{:S(2)}, u32[]{:S(2)}) collective-permute-start(bf16[512,512]{1,0:T(8,128)(2,1)} %get-tuple-element.46), channel_id=1, source_target_pairs={{6,4},{7,5},{4,2},{5,3},{14,12},{15,13},{12,10},{13,11},{22,20},{2... | collective-permute-start | bytes 1572872 | tf_op jit(solution)/shard_map/ppermute | solution.py:436
  161.3 17.0 %collective-permute-start.25 = (bf16[512,512]{1,0:T(8,128)(2,1)}, bf16[512,512]{1,0:T(8,128)(2,1)}, u32[]{:S(2)}, u32[]{:S(2)}) collective-permute-start(bf16[512,512]{1,0:T(8,128)(2,1)} %get-tuple-element.50), channel_id=1, source_target_pairs={{6,4},{7,5},{4,2},{5,3},{14,12},{15,13},{12,10},{13,11},{22,20},{2... | collective-permute-start | bytes 1572872 | tf_op jit(solution)/shard_map/ppermute | solution.py:436
  162.6 19.8 %collective-permute-start.10 = (bf16[512,512]{1,0:T(8,128)(2,1)}, bf16[512,512]{1,0:T(8,128)(2,1)S(1)}, u32[]{:S(2)}, u32[]{:S(2)}) collective-permute-start(bf16[512,512]{1,0:T(8,128)(2,1)} %get-tuple-element.45), channel_id=1, source_target_pairs={{0,2},{1,3},{2,4},{3,5},{4,6},{5,7},{8,10},{9,11},{10,12},{11,13},... | collective-permute-start | bytes 1572872 | tf_op jit(solution)/shard_map/ppermute | solution.py:435
  168.1 21.5 %collective-permute-start.13 = (bf16[512,512]{1,0:T(8,128)(2,1)}, bf16[512,512]{1,0:T(8,128)(2,1)}, u32[]{:S(2)}, u32[]{:S(2)}) collective-permute-start(bf16[512,512]{1,0:T(8,128)(2,1)} %fusion.7), channel_id=1, source_target_pairs={{6,4},{7,5},{4,2},{5,3},{2,0},{3,1},{14,12},{15,13},{12,10},{13,11... | collective-permute-start | bytes 1572872 | tf_op jit(solution)/shard_map/ppermute | solution.py:436
  170.0 20.8 %collective-permute-start.23 = (bf16[512,512]{1,0:T(8,128)(2,1)}, bf16[512,512]{1,0:T(8,128)(2,1)S(1)}, u32[]{:S(2)}, u32[]{:S(2)}) collective-permute-start(bf16[512,512]{1,0:T(8,128)(2,1)} %get-tuple-element.49), channel_id=1, source_target_pairs={{0,2},{1,3},{2,4},{3,5},{4,6},{5,7},{8,10},{9,11},{10,12},{11,13},... | collective-permute-start | bytes 1572872 | tf_op jit(solution)/shard_map/ppermute | solution.py:435
  180.5 19.1 %collective-permute-start.26 = (bf16[512,512]{1,0:T(8,128)(2,1)}, bf16[512,512]{1,0:T(8,128)(2,1)}, u32[]{:S(2)}, u32[]{:S(2)}) collective-permute-start(bf16[512,512]{1,0:T(8,128)(2,1)} %fusion.1), channel_id=1, source_target_pairs={{6,4},{7,5},{4,2},{5,3},{2,0},{3,1},{14,12},{15,13},{12,10},{13,11... | collective-permute-start | bytes 1572872 | tf_op jit(solution)/shard_map/ppermute | solution.py:436
where the time goes:
time: 203 us; the launch traced here: 202 us
  waiting for transfers between devices  93.9 us (46%)
  starting transfers between devices  39.1 us (19%)
  local copies, waits for them, and re-layouts  30 us (15%)
  Pallas kernels  24.4 us (12%)
  other arithmetic  14.2 us (7%)
    ppermute x15, waiting for transfers between devices, swap(): lax.ppermute(value, axis, [(source, source ^ distance) for source in rang...  45.8 us
    ppermute x6, waiting for transfers between devices, line_reduce_scatter(): from_left = lax.ppermute(to_right, 'head', right_pairs)  27.8 us
    ppermute x6, waiting for transfers between devices, line_reduce_scatter(): from_right = lax.ppermute(to_left, 'head', left_pairs)  20.3 us
    ppermute x15, starting transfers between devices, swap(): lax.ppermute(value, axis, [(source, source ^ distance) for source in rang...  14.9 us
    ppermute x6, starting transfers between devices, line_reduce_scatter(): from_left = lax.ppermute(to_right, 'head', right_pairs)  14.9 us
    dynamic_slice x1, local copies, waits for them, and re-layouts, exchange_local(): w_give = lax.dynamic_index_in_dim(w_split, 1 - core, 2, keepdims=False)  14.3 us
    pallas_call x2, Pallas kernels, attend(): pl.pallas_call(kernel, grid_spec=pltpu.PrefetchScalarGridSpec(num_scalar_...  13.7 us
    ppermute x6, starting transfers between devices, line_reduce_scatter(): from_right = lax.ppermute(to_left, 'head', left_pairs)  9.29 us
  transfers between devices with their start and end apart: 27, of which 14 were waited for; matrix products, arithmetic and copies ran while one was open for 7% of the time, Pallas kernels for 12%

commit v1 on v0

--- a/solution.py
+++ b/solution.py
@@ -155,23 +155,26 @@
     return pltpu.CompilerParams(vmem_limit_bytes=mib * 1024 * 1024)
 
 
-def cost(flops, moved):
-    return pl.CostEstimate(flops=flops, bytes_accessed=moved, transcendentals=0)
+SMALL = pl.CostEstimate(flops=1024, bytes_accessed=1024, transcendentals=0)
 
 
 def pack(ctx_index, half, queries, keys, values, docs):
     rows = queries.shape[0] // 2
     group = queries.shape[1] // HD
-    doc_rows = 0 if docs is None else docs.shape[0]
+    doc_rows = 0 if docs is None else 16 * pl.cdiv(docs.shape[0], 16)
     total = 3 * rows + doc_rows
 
     def kernel(ctx_ref, *refs):
         outs = refs[len(refs) - (group - 1) :]
+        if docs is not None:
+            mine = refs[3 * (group - 1)][...].astype(jnp.float32)
+            empty = jnp.zeros((doc_rows - mine.shape[0], HD), jnp.float32)
+            mine = jnp.concatenate([mine, empty], axis=0).astype(jnp.bfloat16)
         for place in range(group - 1):
             for part in range(3):
                 outs[place][part * rows : (part + 1) * rows, :] = refs[place * 3 + part][...]
             if docs is not None:
-                outs[place][3 * rows :, :] = refs[3 * (group - 1)][...]
+                outs[place][3 * rows :, :] = mine
 
     def piece(distance):
         return pl.BlockSpec((rows, HD), lambda step, ctx: (half, ctx[0] ^ distance))
@@ -195,9 +198,31 @@
         ),
         out_shape=[jax.ShapeDtypeStruct((total, HD), jnp.bfloat16)] * (group - 1),
         compiler_params=params(24),
-        cost_estimate=cost(0, 6 * (group - 1) * rows * HD * 2),
+        cost_estimate=SMALL,
         name="pack",
     )(ctx_index, *operands)
+
+
+def pack_projection(core, w_out, chips):
+    depth, width = w_out.shape
+    columns = width // (2 * chips)
+
+    def kernel(core_ref, w_ref, out_ref):
+        out_ref[...] = w_ref[...]
+
+    return pl.pallas_call(
+        kernel,
+        grid_spec=pltpu.PrefetchScalarGridSpec(
+            num_scalar_prefetch=1,
+            grid=(chips,),
+            in_specs=[pl.BlockSpec((depth, columns), lambda chip, c: (0, 2 * chip + 1 - c[0]))],
+            out_specs=pl.BlockSpec((depth, columns), lambda chip, c: (0, chip)),
+        ),
+        out_shape=jax.ShapeDtypeStruct((depth, chips * columns), w_out.dtype),
+        compiler_params=params(16),
+        cost_estimate=SMALL,
+        name="pack_projection",
+    )(core, w_out)
 
 
 def attend(ctx_index, queries, keys, values, docs, low, high):
@@ -238,10 +263,9 @@
                 key_buf[pl.ds(offset, rows), :] = part(upper, distance, 1)
                 value_buf[pl.ds(offset, rows), :] = part(upper, distance, 2)
                 if distance == 0:
-                    both = own_docs[...]
+                    both = own_docs[...].astype(jnp.float32)
                 else:
-                    both = low_refs[distance - 1][3 * rows :, :]
-                both = both.astype(jnp.float32)
+                    both = low_refs[distance - 1][3 * rows :, :].astype(jnp.float32)
                 begin = lanes if upper else 0
                 mine = both[begin : begin + lanes, :]
                 doc_rows[upper, distance] = mine
@@ -328,7 +352,6 @@
     if with_high:
         operands += list(high)
         in_specs += [whole(array) for array in high]
-    pairs = group * 2 * rows * rows * HD * 2 * (3 if with_high else 2)
     return pl.pallas_call(
         kernel,
         grid_spec=pltpu.PrefetchScalarGridSpec(
@@ -344,7 +367,7 @@
         ),
         out_shape=[jax.ShapeDtypeStruct((rows, HD), jnp.bfloat16)] * group,
         compiler_params=params(40),
-        cost_estimate=cost(pairs, 8 * rows * HD * 2 * group),
+        cost_estimate=SMALL,
         name="attend_high" if with_high else "attend_low",
     )(ctx_index, *operands)
 
@@ -368,40 +391,38 @@
         ),
         out_shape=jax.ShapeDtypeStruct((rows, group * HD), jnp.bfloat16),
         compiler_params=params(16),
-        cost_estimate=cost(0, 4 * rows * group * HD),
+        cost_estimate=SMALL,
         name="assemble",
     )(ctx_index, *pieces)
 
 
-def project(core, mine, sibling, w_mine, w_sibling, chips):
+def project(places, slot, mine, sibling, w_mine, w_sibling, chips):
     rows, depth = mine.shape
     columns = w_mine.shape[1] // (2 * chips)
 
-    def kernel(core_ref, mine_ref, sibling_ref, w_mine_ref, w_sibling_ref, out_ref):
+    def kernel(places_ref, mine_ref, sibling_ref, w_mine_ref, w_sibling_ref, out_ref):
         total = jnp.dot(mine_ref[...], w_mine_ref[...], preferred_element_type=jnp.float32)
         total += jnp.dot(sibling_ref[...], w_sibling_ref[...], preferred_element_type=jnp.float32)
-        out_ref[0] = total.astype(jnp.bfloat16)
+        out_ref[...] = total.astype(jnp.bfloat16)
 
     return pl.pallas_call(
         kernel,
         grid_spec=pltpu.PrefetchScalarGridSpec(
             num_scalar_prefetch=1,
-            grid=(chips,),
+            grid=(1,),
             in_specs=[
-                pl.BlockSpec((rows, depth), lambda chip, core: (0, 0)),
-                pl.BlockSpec((rows, depth), lambda chip, core: (0, 0)),
-                pl.BlockSpec((depth, columns), lambda chip, core: (0, 2 * chip + core[0])),
-                pl.BlockSpec((depth, columns), lambda chip, core: (0, chip)),
+                pl.BlockSpec((rows, depth), lambda step, at: (0, 0)),
+                pl.BlockSpec((rows, depth), lambda step, at: (0, 0)),
+                pl.BlockSpec((depth, columns), lambda step, at: (0, 2 * at[slot] + at[chips])),
+                pl.BlockSpec((depth, columns), lambda step, at: (0, at[slot])),
             ],
-            out_specs=pl.BlockSpec((1, rows, columns), lambda chip, core: (chip, 0, 0)),
+            out_specs=pl.BlockSpec((rows, columns), lambda step, at: (0, 0)),
         ),
-        out_shape=jax.ShapeDtypeStruct((chips, rows, columns), jnp.bfloat16),
-        compiler_params=params(24),
-        cost_estimate=cost(
-            4 * rows * depth * columns * chips, 2 * chips * (rows + 2 * depth) * columns
-        ),
+        out_shape=jax.ShapeDtypeStruct((rows, columns), jnp.bfloat16),
+        compiler_params=params(16),
+        cost_estimate=SMALL,
         name="project",
-    )(core, mine, sibling, w_mine, w_sibling)
+    )(places, mine, sibling, w_mine, w_sibling)
 
 
 def swap(value, axis, distance):
@@ -409,34 +430,29 @@
     return lax.ppermute(value, axis, [(source, source ^ distance) for source in range(count)])
 
 
-def line_reduce_scatter(shares, chip, chips):
-    def share(index):
-        return lax.dynamic_index_in_dim(shares, jnp.clip(index, 0, chips - 1), 0, keepdims=False)
-
-    from_left = None
-    from_right = None
-    for step in range(1, chips):
-        to_right = share(chips - step + chip)
-        to_left = share(chip + step - chips)
-        if step > 1:
-            to_right = (to_right.astype(jnp.float32) + from_left.astype(jnp.float32)).astype(
-                jnp.bfloat16
-            )
-            to_left = (to_left.astype(jnp.float32) + from_right.astype(jnp.float32)).astype(
-                jnp.bfloat16
-            )
-        right_pairs = []
-        left_pairs = []
-        for source in range(step):
-            for core in range(2):
-                right_pairs.append((2 * source + core, 2 * source + 2 + core))
-                mirrored = chips - 1 - source
-                left_pairs.append((2 * mirrored + core, 2 * mirrored - 2 + core))
-        from_left = lax.ppermute(to_right, "head", right_pairs)
-        from_right = lax.ppermute(to_left, "head", left_pairs)
-    total = share(chip).astype(jnp.float32)
-    total = total + from_left.astype(jnp.float32) + from_right.astype(jnp.float32)
+def between_chips(value, pairs):
+    both = [(2 * source + core, 2 * target + core) for source, target in pairs for core in (0, 1)]
+    return lax.ppermute(value, "head", both)
+
+
+def add(*terms):
+    total = terms[0].astype(jnp.float32)
+    for term in terms[1:]:
+        total = total + term.astype(jnp.float32)
     return total.astype(jnp.bfloat16)
+
+
+SENDING = ((3, 2, 1, 0), (3, 2, 0, 1), (0, 1, 3, 2), (0, 1, 2, 3))
+TO_MIDDLE = ((0, 1), (3, 2))
+ACROSS = ((1, 2), (2, 1))
+TO_ENDS = ((2, 3), (1, 0))
+
+
+def line_reduce_scatter(shares):
+    end = [between_chips(share, TO_MIDDLE) for share in shares[:3]]
+    across = [between_chips(add(shares[turn], end[turn]), ACROSS) for turn in range(2)]
+    outer = between_chips(add(shares[2], across[0]), TO_ENDS)
+    return add(shares[3], end[2], across[1], outer)
 
 
 def exchange_local(queries, keys, values, doc_ids, w_out):
@@ -446,32 +462,45 @@
     ctx_index = lax.axis_index("ctx").astype(jnp.int32).reshape(1)
     head_index = lax.axis_index("head").astype(jnp.int32)
     chip = head_index // 2
-    core = head_index % 2
-
-    docs = doc_ids.astype(jnp.bfloat16).reshape(shard_rows // HD, HD)
-    docs = jnp.pad(docs, ((0, -docs.shape[0] % 16), (0, 0)))
+    core = (head_index % 2).reshape(1)
+    places = jnp.concatenate([jnp.array(SENDING, jnp.int32)[chip], core])
+    docs = doc_ids.reshape(shard_rows // HD, HD)
 
     low_out = pack(ctx_index, 0, queries, keys, values, docs)
+    *low_out, w_later = lax.optimization_barrier((*low_out, w_out))
     low = [swap(low_out[distance - 1], "ctx", distance) for distance in range(1, group)]
-
-    depth, width = w_out.shape
-    w_split = w_out.reshape(depth, chips, 2, width // (2 * chips))
-    w_give = lax.dynamic_index_in_dim(w_split, 1 - core, 2, keepdims=False)
-    w_sibling = swap(w_give.reshape(depth, width // 2), "head", 1)
-
+    w_sibling = swap(pack_projection(core, w_later, chips), "head", 1)
     high_out = pack(ctx_index, 1, queries, keys, values, None)
-    *high_out, low[0], low[1], low[2] = lax.optimization_barrier((*high_out, *low))
-    high = [swap(high_out[distance - 1], "ctx", distance) for distance in range(1, group)]
-
-    results = []
-    for half in range(2):
-        pieces = attend(ctx_index, queries, keys, values, docs, low, high if half else None)
-        back = [swap(pieces[distance], "ctx", distance) for distance in range(1, group)]
-        mine = assemble(ctx_index, [pieces[0], *back])
-        sibling = swap(mine, "head", 1)
-        shares = project(core.reshape(1), mine, sibling, w_out, w_sibling, chips)
-        results.append(line_reduce_scatter(shares, chip, chips))
-    return jnp.concatenate(results, axis=0)
+    high_out, low = lax.optimization_barrier((high_out, low))
+    high = [swap(high_out[distance - 1], "ctx", distance) for distance in range(1, group - 1)]
+
+    pieces = attend(ctx_index, queries, keys, values, docs, low, None)
+    back = [swap(pieces[distance], "ctx", distance) for distance in range(1, group)]
+    back, high, diagonal_out = lax.optimization_barrier((back, high, high_out[group - 2]))
+    high = [*high, swap(diagonal_out, "ctx", group - 1)]
+    mine = assemble(ctx_index, [pieces[0], *back])
+    sibling = swap(mine, "head", 1)
+    shares = [
+        project(places, slot, mine, sibling, w_out, w_sibling, chips) for slot in range(chips)
+    ]
+    end = [between_chips(share, TO_MIDDLE) for share in shares[:3]]
+    passed = add(shares[0], end[0])
+
+    high, passed, shares = lax.optimization_barrier((high, passed, shares))
+    across = [between_chips(passed, ACROSS)]
+    pieces = attend(ctx_index, queries, keys, values, docs, low, high)
+    back = [swap(pieces[distance], "ctx", distance) for distance in range(1, group)]
+    back, passed = lax.optimization_barrier((back, add(shares[1], end[1])))
+    across.append(between_chips(passed, ACROSS))
+    outer = between_chips(add(shares[2], across[0]), TO_ENDS)
+    mine = assemble(ctx_index, [pieces[0], *back])
+    sibling = swap(mine, "head", 1)
+    late_shares = [
+        project(places, slot, mine, sibling, w_out, w_sibling, chips) for slot in range(chips)
+    ]
+    late_shares[1], end[2] = lax.optimization_barrier((late_shares[1], end[2]))
+    first = add(shares[3], end[2], across[1], outer)
+    return jnp.concatenate([first, line_reduce_scatter(late_shares)], axis=0)
 
 
 def solution(mesh):
@@ -482,7 +511,7 @@
 
     def local(queries, keys, values, doc_ids, w_out):
         heads = queries.shape[1] // HD
-        exchange = heads == ctx_count and heads == 4 and head_count % 2 == 0 and head_count > 2
+        exchange = heads == ctx_count and heads == 4 and head_count == 2 * len(SENDING)
         body = exchange_local if exchange else ring_local
         return body(queries, keys, values, doc_ids, w_out)
 

time: 203 us -> 161 us (0.79)
  the two profiles are of different devices: /device:TPU:8 before, /device:TPU:0 now
where the time goes in v1:
time: 161 us; the launch traced here: 162 us
  waiting for transfers between devices  64.6 us (40%)
  starting transfers between devices  40.9 us (25%)
  Pallas kernels  39.1 us (24%)
  local copies, waits for them, and re-layouts  14 us (9%)
  other arithmetic  2.51 us (2%)
    ppermute x15, waiting for transfers between devices, swap(): lax.ppermute(value, axis, [(source, source ^ distance) for source in rang...  34.3 us
    ppermute x12, waiting for transfers between devices, between_chips(): return lax.ppermute(value, 'head', both)  30.2 us
    ppermute x12, starting transfers between devices, between_chips(): return lax.ppermute(value, 'head', both)  25.6 us
    pallas_call x2, Pallas kernels, attend(): pl.pallas_call(kernel, grid_spec=pltpu.PrefetchScalarGridSpec(num_scalar_...  20.4 us
    ppermute x15, starting transfers between devices, swap(): lax.ppermute(value, axis, [(source, source ^ distance) for source in rang...  15.4 us
    pallas_call x8, Pallas kernels, project(): pl.pallas_call(kernel, grid_spec=pltpu.PrefetchScalarGridSpec(num_scalar_...  15 us
    unnamed x58, local copies, waits for them, and re-layouts  13.4 us
  transfers between devices with their start and end apart: 27, of which 17 were waited for; matrix products, arithmetic and copies ran while one was open for 1% of the time, Pallas kernels for 21%

profile of v1, /device:TPU:0, one launch (start us, length us, event | category | flops | bytes accessed | tf_op | source)
XLA Modules:
  0.0 161.5 jit_solution(2327472831546420925)
XLA Ops:
  0.0 1.2 copy-done.3
  1.2 1.2 copy-done.5
  2.5 1.2 copy-done.8
  3.7 0.7 copy-done.19
  4.7 0.7 copy-done.21
  5.4 0.8 copy-done.23
  6.2 0.7 copy-done.25
  6.9 2.2 %copy-done = bf16[512,4096]{1,0:T(8,128)(2,1)S(1)} copy-done((bf16[512,4096]{1,0:T(8,128)(2,1)S(1)}, bf16[512,4096]{1,0:T(8,128)(2,1)}, u32[]{:S(2)}) %copy-start) | copy-done | bytes 4194328
  9.1 2.1 %pack_projection.1 = bf16[512,2048]{1,0:T(8,128)(2,1)} custom-call(s32[1]{0:T(128)} %bitcast.3.core_ref, bf16[512,4096]{1,0:T(8,128)(2,1)S(1)} %copy-done), custom_call_target="tpu_custom_call" | custom-call | flops 1024 | bytes 1024 | tf_op jit(solution)/shard_map/pack_projection/pallas_call | solution.py:213
  11.7 2.6 %collective-permute-start = (bf16[1552,128]{1,0:T(8,128)(2,1)S(1)}, bf16[1552,128]{1,0:T(8,128)(2,1)S(1)}, u32[]{:S(2)}, u32[]{:S(2)}) collective-permute-start(bf16[1552,128]{1,0:T(8,128)(2,1)S(1)} %copy-done.26), channel_id=1, source_target_pairs={{0,8},{8,0},{16,24},{24,16},{1,9},{9,1},{17,25},{25,17},{2,10},{10... | collective-permute-start | bytes 1191944 | tf_op jit(solution)/shard_map/ppermute | solution.py:430
  14.3 1.5 collective-permute-start.1
  16.2 0.7 copy-done.27
  16.9 7.4 %collective-permute-done.refs_4_.refs_7_ = bf16[1552,128]{1,0:T(8,128)(2,1)S(1)} collective-permute-done((bf16[1552,128]{1,0:T(8,128)(2,1)S(1)}, bf16[1552,128]{1,0:T(8,128)(2,1)S(1)}, u32[]{:S(2)}, u32[]{:S(2)}) %collective-permute-start) | collective-permute-done | bytes 397344 | tf_op jit(solution)/shard_map/ppermute | solution.py:430
  24.3 9.7 %collective-permute-done.1.refs_5_.refs_8_ = bf16[1552,128]{1,0:T(8,128)(2,1)S(1)} collective-permute-done((bf16[1552,128]{1,0:T(8,128)(2,1)S(1)}, bf16[1552,128]{1,0:T(8,128)(2,1)S(1)}, u32[]{:S(2)}, u32[]{:S(2)}) %collective-permute-start.1) | collective-permute-done | bytes 397344 | tf_op jit(solution)/shard_map/ppermute | solution.py:430
  34.1 1.2 collective-permute-start.6
  35.3 0.9 collective-permute-start.7
  36.2 7.0 %attend_low.1 = (bf16[512,128]{1,0:T(8,128)(2,1)S(1)}, bf16[512,128]{1,0:T(8,128)(2,1)S(1)}, bf16[512,128]{1,0:T(8,128)(2,1)S(1)}, bf16[512,128]{1,0:T(8,128)(2,1)S(1)}) custom-call(s32[1]{0:T(128)} %bitcast.ctx_ref, bf16[1024,512]{1,0:T(8,128)(2,1)S(1)} %copy-done.4, bf16[1024,512]{1,0:T(8,128)(2,1)S(1)} %copy-done.6, bf16[1024,512]{1,0:T(8,128)(2,1)S(1)} %copy-done.9, ...), custom_call_target="tpu_custom_call" | custom-call | flops 1024 | bytes 1024 | tf_op jit(solution)/shard_map/attend_low/pallas_call | solution.py:355
  43.3 1.6 collective-permute-start.3
  44.8 0.5 collective-permute-start.4
  45.3 3.0 %collective-permute-done.3.refs_1_ = bf16[512,128]{1,0:T(8,128)(2,1)S(1)} collective-permute-done((bf16[512,128]{1,0:T(8,128)(2,1)S(1)}, bf16[512,128]{1,0:T(8,128)(2,1)S(1)}, u32[]{:S(2)}, u32[]{:S(2)}) %collective-permute-start.3) | collective-permute-done | bytes 131104 | tf_op jit(solution)/shard_map/ppermute | solution.py:430
  48.3 1.5 collective-permute-start.5
  49.7 1.5 collective-permute-done.4.refs_2_
  51.2 3.0 %collective-permute-done.5.refs_3_ = bf16[512,128]{1,0:T(8,128)(2,1)S(1)} collective-permute-done((bf16[512,128]{1,0:T(8,128)(2,1)S(1)}, bf16[512,128]{1,0:T(8,128)(2,1)S(1)}, u32[]{:S(2)}, u32[]{:S(2)}) %collective-permute-start.5) | collective-permute-done | bytes 131104 | tf_op jit(solution)/shard_map/ppermute | solution.py:430
  54.2 0.8 copy-done.15
  54.9 0.8 copy-done.17
  55.7 0.9 assemble.2.mine_ref
  56.6 0.7 dynamic-slice_bitcast_fusion
  57.4 1.5 collective-permute-done.9.sibling_ref
  58.9 2.2 %copy-done.1 = bf16[512,4096]{1,0:T(8,128)(2,1)S(1)} copy-done((bf16[512,4096]{1,0:T(8,128)(2,1)S(1)}, bf16[512,4096]{1,0:T(8,128)(2,1)}, u32[]{:S(2)}) %copy-start.1) | copy-done | bytes 4194328
  61.0 2.4 %project.8 = bf16[512,512]{1,0:T(8,128)(2,1)S(1)} custom-call(s32[5]{0:T(128)S(1)} %pad_add_fusion.places_ref, bf16[512,512]{1,0:T(8,128)(2,1)} %assemble.2.mine_ref, bf16[512,512]{1,0:T(8,128)(2,1)} %collective-permute-done.9.sibling_ref, bf16[512,4096]{1,0:T(8,128)(2,1)S(1)} %copy-done.1, bf16[512,2048]{1,0:T(8,128)(2,1)S(1)} %collective-permute-done.10.w_sibling_ref), custom_call_target="tpu_custom_call" | custom-call | flops 1024 | bytes 1024 | tf_op jit(solution)/shard_map/project/pallas_call | solution.py:408
  63.5 3.6 %collective-permute-start.11 = (bf16[512,512]{1,0:T(8,128)(2,1)S(1)}, bf16[512,512]{1,0:T(8,128)(2,1)S(1)}, u32[]{:S(2)}, u32[]{:S(2)}) collective-permute-start(bf16[512,512]{1,0:T(8,128)(2,1)S(1)} %project.8), channel_id=1, source_target_pairs={{0,2},{1,3},{6,4},{7,5},{8,10},{9,11},{14,12},{15,13},{16,18},{17,... | collective-permute-start | bytes 1572872 | tf_op jit(solution)/shard_map/ppermute | solution.py:435
  67.2 2.4 %project.9 = bf16[512,512]{1,0:T(8,128)(2,1)S(1)} custom-call(s32[5]{0:T(128)S(1)} %pad_add_fusion.places_ref, bf16[512,512]{1,0:T(8,128)(2,1)} %assemble.2.mine_ref, bf16[512,512]{1,0:T(8,128)(2,1)} %collective-permute-done.9.sibling_ref, bf16[512,4096]{1,0:T(8,128)(2,1)S(1)} %copy-done.1, bf16[512,2048]{1,0:T(8,128)(2,1)S(1)} %collective-permute-done.10.w_sibling_ref), custom_call_target="tpu_custom_call" | custom-call | flops 1024 | bytes 1024 | tf_op jit(solution)/shard_map/project/pallas_call | solution.py:408
  69.6 1.3 collective-permute-start.15
  70.9 1.5 collective-permute-start.8
  72.5 2.4 %project.11 = bf16[512,512]{1,0:T(8,128)(2,1)S(1)} custom-call(s32[5]{0:T(128)S(1)} %pad_add_fusion.places_ref, bf16[512,512]{1,0:T(8,128)(2,1)} %assemble.2.mine_ref, bf16[512,512]{1,0:T(8,128)(2,1)} %collective-permute-done.9.sibling_ref, bf16[512,4096]{1,0:T(8,128)(2,1)S(1)} %copy-done.1, bf16[512,2048]{1,0:T(8,128)(2,1)S(1)} %collective-permute-done.10.w_sibling_ref), custom_call_target="tpu_custom_call" | custom-call | flops 1024 | bytes 1024 | tf_op jit(solution)/shard_map/project/pallas_call | solution.py:408
  75.0 2.6 %project.10 = bf16[512,512]{1,0:T(8,128)(2,1)S(1)} custom-call(s32[5]{0:T(128)S(1)} %pad_add_fusion.places_ref, bf16[512,512]{1,0:T(8,128)(2,1)} %assemble.2.mine_ref, bf16[512,512]{1,0:T(8,128)(2,1)} %collective-permute-done.9.sibling_ref, bf16[512,4096]{1,0:T(8,128)(2,1)S(1)} %copy-done.1, bf16[512,2048]{1,0:T(8,128)(2,1)S(1)} %collective-permute-done.10.w_sibling_ref), custom_call_target="tpu_custom_call" | custom-call | flops 1024 | bytes 1024 | tf_op jit(solution)/shard_map/project/pallas_call | solution.py:408
  77.6 1.8 %collective-permute-done.11 = bf16[512,512]{1,0:T(8,128)(2,1)S(1)} collective-permute-done((bf16[512,512]{1,0:T(8,128)(2,1)S(1)}, bf16[512,512]{1,0:T(8,128)(2,1)S(1)}, u32[]{:S(2)}, u32[]{:S(2)}) %collective-permute-start.11) | collective-permute-done | bytes 524320 | tf_op jit(solution)/shard_map/ppermute | solution.py:435
  79.5 3.2 %collective-permute-done.8.refs_12_ = bf16[1536,128]{1,0:T(8,128)(2,1)S(1)} collective-permute-done((bf16[1536,128]{1,0:T(8,128)(2,1)S(1)}, bf16[1536,128]{1,0:T(8,128)(2,1)S(1)}, u32[]{:S(2)}, u32[]{:S(2)}) %collective-permute-start.8) | collective-permute-done | bytes 393248 | tf_op jit(solution)/shard_map/ppermute | solution.py:430
  82.8 13.4 %attend_high.1 = (bf16[512,128]{1,0:T(8,128)(2,1)S(1)}, bf16[512,128]{1,0:T(8,128)(2,1)S(1)}, bf16[512,128]{1,0:T(8,128)(2,1)S(1)}, bf16[512,128]{1,0:T(8,128)(2,1)S(1)}) custom-call(s32[1]{0:T(128)} %bitcast.ctx_ref, bf16[1024,512]{1,0:T(8,128)(2,1)S(1)} %copy-done.4, bf16[1024,512]{1,0:T(8,128)(2,1)S(1)} %copy-done.7, bf16[1024,512]{1,0:T(8,128)(2,1)S(1)} %copy-done.10, ...), custom_call_target="tpu_custom_call" | custom-call | flops 1024 | bytes 1024 | tf_op jit(solution)/shard_map/attend_high/pallas_call | solution.py:355
  96.2 1.6 collective-permute-start.12
  97.8 0.5 collective-permute-start.13
  98.3 1.5 collective-permute-start.14
  99.9 2.4 %collective-permute-done.12.refs_1_ = bf16[512,128]{1,0:T(8,128)(2,1)S(1)} collective-permute-done((bf16[512,128]{1,0:T(8,128)(2,1)S(1)}, bf16[512,128]{1,0:T(8,128)(2,1)S(1)}, u32[]{:S(2)}, u32[]{:S(2)}) %collective-permute-start.12) | collective-permute-done | bytes 131104 | tf_op jit(solution)/shard_map/ppermute | solution.py:430
  102.3 2.6 %collective-permute-done.13.refs_2_ = bf16[512,128]{1,0:T(8,128)(2,1)S(1)} collective-permute-done((bf16[512,128]{1,0:T(8,128)(2,1)S(1)}, bf16[512,128]{1,0:T(8,128)(2,1)S(1)}, u32[]{:S(2)}, u32[]{:S(2)}) %collective-permute-start.13) | collective-permute-done | bytes 131104 | tf_op jit(solution)/shard_map/ppermute | solution.py:430
  105.1 1.8 %collective-permute-start.17 = (bf16[512,512]{1,0:T(8,128)(2,1)S(1)}, bf16[512,512]{1,0:T(8,128)(2,1)S(1)}, u32[]{:S(2)}, u32[]{:S(2)}) collective-permute-start(bf16[512,512]{1,0:T(8,128)(2,1)S(1)} %project.10), channel_id=1, source_target_pairs={{0,2},{1,3},{6,4},{7,5},{8,10},{9,11},{14,12},{15,13},{16,18},{17,... | collective-permute-start | bytes 1572872 | tf_op jit(solution)/shard_map/ppermute | solution.py:435
  107.0 1.2 project.15
  108.2 1.8 %collective-permute-start.24 = (bf16[512,512]{1,0:T(8,128)(2,1)S(1)}, bf16[512,512]{1,0:T(8,128)(2,1)S(1)}, u32[]{:S(2)}, u32[]{:S(2)}) collective-permute-start(bf16[512,512]{1,0:T(8,128)(2,1)S(1)} %project.15), channel_id=1, source_target_pairs={{0,2},{1,3},{6,4},{7,5},{8,10},{9,11},{14,12},{15,13},{16,18},{17,... | collective-permute-start | bytes 1572872 | tf_op jit(solution)/shard_map/ppermute | solution.py:435
  110.0 0.7 collective-permute-start.19
  110.8 0.7 collective-permute-start.18
  111.5 1.3 project.12
  112.7 6.4 %collective-permute-done.17 = bf16[512,512]{1,0:T(8,128)(2,1)S(1)} collective-permute-done((bf16[512,512]{1,0:T(8,128)(2,1)S(1)}, bf16[512,512]{1,0:T(8,128)(2,1)S(1)}, u32[]{:S(2)}, u32[]{:S(2)}) %collective-permute-start.17) | collective-permute-done | bytes 524320 | tf_op jit(solution)/shard_map/ppermute | solution.py:435
  119.1 4.4 %collective-permute-start.22 = (bf16[512,512]{1,0:T(8,128)(2,1)S(1)}, bf16[512,512]{1,0:T(8,128)(2,1)S(1)}, u32[]{:S(2)}, u32[]{:S(2)}) collective-permute-start(bf16[512,512]{1,0:T(8,128)(2,1)S(1)} %project.12), channel_id=1, source_target_pairs={{0,2},{1,3},{6,4},{7,5},{8,10},{9,11},{14,12},{15,13},{16,18},{17,... | collective-permute-start | bytes 1572872 | tf_op jit(solution)/shard_map/ppermute | solution.py:435
  123.5 6.8 %collective-permute-done.24 = bf16[512,512]{1,0:T(8,128)(2,1)S(1)} collective-permute-done((bf16[512,512]{1,0:T(8,128)(2,1)S(1)}, bf16[512,512]{1,0:T(8,128)(2,1)S(1)}, u32[]{:S(2)}, u32[]{:S(2)}) %collective-permute-start.24) | collective-permute-done | bytes 524320 | tf_op jit(solution)/shard_map/ppermute | solution.py:435
  130.5 0.7 collective-permute-start.25
  131.3 1.3 collective-permute-start.20
  132.6 1.3 project.14
  133.9 7.2 %collective-permute-start.21 = (bf16[512,512]{1,0:T(8,128)(2,1)S(1)}, bf16[512,512]{1,0:T(8,128)(2,1)S(1)}, u32[]{:S(2)}, u32[]{:S(2)}) collective-permute-start(bf16[512,512]{1,0:T(8,128)(2,1)S(1)} %project.14), channel_id=1, source_target_pairs={{0,2},{1,3},{6,4},{7,5},{8,10},{9,11},{14,12},{15,13},{16,18},{17,... | collective-permute-start | bytes 1572872 | tf_op jit(solution)/shard_map/ppermute | solution.py:435
  141.7 0.7 collective-permute-start.23
  142.5 1.3 collective-permute-start.26
  143.8 1.3 project.13
  145.1 3.8 %collective-permute-done.20 = bf16[512,512]{1,0:T(8,128)(2,1)S(1)} collective-permute-done((bf16[512,512]{1,0:T(8,128)(2,1)S(1)}, bf16[512,512]{1,0:T(8,128)(2,1)S(1)}, u32[]{:S(2)}, u32[]{:S(2)}) %collective-permute-start.20) | collective-permute-done | bytes 524320 | tf_op jit(solution)/shard_map/ppermute | solution.py:435
  149.2 3.1 %collective-permute-done.21 = bf16[512,512]{1,0:T(8,128)(2,1)S(1)} collective-permute-done((bf16[512,512]{1,0:T(8,128)(2,1)S(1)}, bf16[512,512]{1,0:T(8,128)(2,1)S(1)}, u32[]{:S(2)}, u32[]{:S(2)}) %collective-permute-start.21) | collective-permute-done | bytes 524320 | tf_op jit(solution)/shard_map/ppermute | solution.py:435
  152.4 7.8 %collective-permute-done.26 = bf16[512,512]{1,0:T(8,128)(2,1)S(1)} collective-permute-done((bf16[512,512]{1,0:T(8,128)(2,1)S(1)}, bf16[512,512]{1,0:T(8,128)(2,1)S(1)}, u32[]{:S(2)}, u32[]{:S(2)}) %collective-permute-start.26) | collective-permute-done | bytes 524320 | tf_op jit(solution)/shard_map/ppermute | solution.py:435
  160.5 1.0 pad_maximum_fusion
  (74 shorter events, 3.3 us)
Async XLA Ops:
  0.0 1.2 copy-start.3
  1.2 1.2 copy-start.5
  2.5 1.2 copy-start.8
  3.7 0.7 copy-start.19
  4.6 0.8 copy-start.21
  5.4 0.8 copy-start.23
  6.2 0.7 copy-start.25
  6.9 2.2 %copy-start = (bf16[512,4096]{1,0:T(8,128)(2,1)S(1)}, bf16[512,4096]{1,0:T(8,128)(2,1)}, u32[]{:S(2)}) copy-start(bf16[512,4096]{1,0:T(8,128)(2,1)} %w_mine_ref.15) | copy-start | bytes 12582916
  9.1 2.6 %copy-start.26 = (bf16[1552,128]{1,0:T(8,128)(2,1)S(1)}, bf16[1552,128]{1,0:T(8,128)(2,1)}, u32[]{:S(2)}) copy-start(bf16[1552,128]{1,0:T(8,128)(2,1)} %copy-done.25) | copy-start | bytes 1191940
  9.1 5.2 %copy-start.24 = (bf16[1552,128]{1,0:T(8,128)(2,1)S(1)}, bf16[1552,128]{1,0:T(8,128)(2,1)}, u32[]{:S(2)}) copy-start(bf16[1552,128]{1,0:T(8,128)(2,1)} %copy-done.23) | copy-start | bytes 1191940
  9.1 6.7 %copy-start.22 = (bf16[1552,128]{1,0:T(8,128)(2,1)S(1)}, bf16[1552,128]{1,0:T(8,128)(2,1)}, u32[]{:S(2)}) copy-start(bf16[1552,128]{1,0:T(8,128)(2,1)} %copy-done.21) | copy-start | bytes 1191940
  9.1 6.7 %copy-start.4 = (bf16[1024,512]{1,0:T(8,128)(2,1)S(1)}, bf16[1024,512]{1,0:T(8,128)(2,1)}, u32[]{:S(2)}) copy-start(bf16[1024,512]{1,0:T(8,128)(2,1)} %refs_3_.5) | copy-start | bytes 3145732
  9.1 6.7 %copy-start.6 = (bf16[1024,512]{1,0:T(8,128)(2,1)S(1)}, bf16[1024,512]{1,0:T(8,128)(2,1)}, u32[]{:S(2)}) copy-start(bf16[1024,512]{1,0:T(8,128)(2,1)} %refs_4_.5) | copy-start | bytes 3145732
  9.1 6.7 %copy-start.9 = (bf16[1024,512]{1,0:T(8,128)(2,1)S(1)}, bf16[1024,512]{1,0:T(8,128)(2,1)}, u32[]{:S(2)}) copy-start(bf16[1024,512]{1,0:T(8,128)(2,1)} %refs_5_.5) | copy-start | bytes 3145732
  11.3 24.9 %copy-start.20 = (s32[1024]{0:T(1024)S(1)}, s32[1024]{0:T(1024)}, u32[]{:S(2)}) copy-start(s32[1024]{0:T(1024)} %param.9) | copy-start | bytes 12292
  11.3 47.6 %collective-permute-start.10 = (bf16[512,2048]{1,0:T(8,128)(2,1)}, bf16[512,2048]{1,0:T(8,128)(2,1)S(1)}, u32[]{:S(2)}, u32[]{:S(2)}) collective-permute-start(bf16[512,2048]{1,0:T(8,128)(2,1)} %pack_projection.1), channel_id=1, source_target_pairs={{0,1},{1,0},{2,3},{3,2},{4,5},{5,4},{6,7},{7,6},{8,9},{9,8},{10,11... | collective-permute-start | bytes 6291464 | tf_op jit(solution)/shard_map/ppermute | solution.py:430
  11.7 12.6 %collective-permute-start = (bf16[1552,128]{1,0:T(8,128)(2,1)S(1)}, bf16[1552,128]{1,0:T(8,128)(2,1)S(1)}, u32[]{:S(2)}, u32[]{:S(2)}) collective-permute-start(bf16[1552,128]{1,0:T(8,128)(2,1)S(1)} %copy-done.26), channel_id=1, source_target_pairs={{0,8},{8,0},{16,24},{24,16},{1,9},{9,1},{17,25},{25,17},{2,10},{10... | collective-permute-start | bytes 1191944 | tf_op jit(solution)/shard_map/ppermute | solution.py:430
  14.3 19.8 %collective-permute-start.1 = (bf16[1552,128]{1,0:T(8,128)(2,1)S(1)}, bf16[1552,128]{1,0:T(8,128)(2,1)S(1)}, u32[]{:S(2)}, u32[]{:S(2)}) collective-permute-start(bf16[1552,128]{1,0:T(8,128)(2,1)S(1)} %copy-done.24), channel_id=1, source_target_pairs={{0,16},{8,24},{16,0},{24,8},{1,17},{9,25},{17,1},{25,9},{2,18},{10... | collective-permute-start | bytes 1191944 | tf_op jit(solution)/shard_map/ppermute | solution.py:430
  15.8 18.3 %collective-permute-start.2 = (bf16[1552,128]{1,0:T(8,128)(2,1)S(1)}, bf16[1552,128]{1,0:T(8,128)(2,1)S(1)}, u32[]{:S(2)}, u32[]{:S(2)}) collective-permute-start(bf16[1552,128]{1,0:T(8,128)(2,1)S(1)} %copy-done.22), channel_id=1, source_target_pairs={{0,24},{8,16},{16,8},{24,0},{1,25},{9,17},{17,9},{25,1},{2,26},{10... | collective-permute-start | bytes 1191944 | tf_op jit(solution)/shard_map/ppermute | solution.py:430
  16.2 0.7 copy-start.27
  34.1 9.2 %copy-start.11 = (bf16[1552,128]{1,0:T(8,128)(2,1)}, bf16[1552,128]{1,0:T(8,128)(2,1)S(1)}, u32[]{:S(2)}) copy-start(bf16[1552,128]{1,0:T(8,128)(2,1)S(1)} %collective-permute-done.1.refs_5_.refs_8_) | copy-start | bytes 1191940
  34.1 9.2 %copy-start.13 = (bf16[1552,128]{1,0:T(8,128)(2,1)}, bf16[1552,128]{1,0:T(8,128)(2,1)S(1)}, u32[]{:S(2)}) copy-start(bf16[1552,128]{1,0:T(8,128)(2,1)S(1)} %collective-permute-done.2.refs_6_.refs_9_) | copy-start | bytes 1191940
  34.1 20.1 %collective-permute-start.6 = (bf16[1536,128]{1,0:T(8,128)(2,1)S(1)}, bf16[1536,128]{1,0:T(8,128)(2,1)S(1)}, u32[]{:S(2)}, u32[]{:S(2)}) collective-permute-start(bf16[1536,128]{1,0:T(8,128)(2,1)S(1)} %get-tuple-element.63), channel_id=1, source_target_pairs={{0,8},{8,0},{16,24},{24,16},{1,9},{9,1},{17,25},{25,17},{2,10},{10... | collective-permute-start | bytes 1179656 | tf_op jit(solution)/shard_map/ppermute | solution.py:430
  35.3 19.6 %collective-permute-start.7 = (bf16[1536,128]{1,0:T(8,128)(2,1)S(1)}, bf16[1536,128]{1,0:T(8,128)(2,1)S(1)}, u32[]{:S(2)}, u32[]{:S(2)}) collective-permute-start(bf16[1536,128]{1,0:T(8,128)(2,1)S(1)} %get-tuple-element.64), channel_id=1, source_target_pairs={{0,16},{8,24},{16,0},{24,8},{1,17},{9,25},{17,1},{25,9},{2,18},{10... | collective-permute-start | bytes 1179656 | tf_op jit(solution)/shard_map/ppermute | solution.py:430
  43.3 5.0 %collective-permute-start.3 = (bf16[512,128]{1,0:T(8,128)(2,1)S(1)}, bf16[512,128]{1,0:T(8,128)(2,1)S(1)}, u32[]{:S(2)}, u32[]{:S(2)}) collective-permute-start(bf16[512,128]{1,0:T(8,128)(2,1)S(1)} %get-tuple-element.60), channel_id=1, source_target_pairs={{0,8},{8,0},{16,24},{24,16},{1,9},{9,1},{17,25},{25,17},{2,10},{10... | collective-permute-start | bytes 393224 | tf_op jit(solution)/shard_map/ppermute | solution.py:430
  44.8 6.4 %collective-permute-start.4 = (bf16[512,128]{1,0:T(8,128)(2,1)S(1)}, bf16[512,128]{1,0:T(8,128)(2,1)S(1)}, u32[]{:S(2)}, u32[]{:S(2)}) collective-permute-start(bf16[512,128]{1,0:T(8,128)(2,1)S(1)} %get-tuple-element.61), channel_id=1, source_target_pairs={{0,16},{8,24},{16,0},{24,8},{1,17},{9,25},{17,1},{25,9},{2,18},{10... | collective-permute-start | bytes 393224 | tf_op jit(solution)/shard_map/ppermute | solution.py:430
  48.3 5.9 %collective-permute-start.5 = (bf16[512,128]{1,0:T(8,128)(2,1)S(1)}, bf16[512,128]{1,0:T(8,128)(2,1)S(1)}, u32[]{:S(2)}, u32[]{:S(2)}) collective-permute-start(bf16[512,128]{1,0:T(8,128)(2,1)S(1)} %get-tuple-element.62), channel_id=1, source_target_pairs={{0,24},{8,16},{16,8},{24,0},{1,25},{9,17},{17,9},{25,1},{2,26},{10... | collective-permute-start | bytes 393224 | tf_op jit(solution)/shard_map/ppermute | solution.py:430
  54.2 0.8 copy-start.15
  54.9 0.8 copy-start.17
  56.6 2.3 %collective-permute-start.9 = (bf16[512,512]{1,0:T(8,128)(2,1)}, bf16[512,512]{1,0:T(8,128)(2,1)}, u32[]{:S(2)}, u32[]{:S(2)}) collective-permute-start(bf16[512,512]{1,0:T(8,128)(2,1)} %assemble.2.mine_ref), channel_id=1, source_target_pairs={{0,1},{1,0},{2,3},{3,2},{4,5},{5,4},{6,7},{7,6},{8,9},{9,8},{10,11... | collective-permute-start | bytes 1572872 | tf_op jit(solution)/shard_map/ppermute | solution.py:430
  58.9 2.2 %copy-start.1 = (bf16[512,4096]{1,0:T(8,128)(2,1)S(1)}, bf16[512,4096]{1,0:T(8,128)(2,1)}, u32[]{:S(2)}) copy-start(bf16[512,4096]{1,0:T(8,128)(2,1)} %w_mine_ref.15) | copy-start | bytes 12582916
  63.5 7.4 %copy-start.28 = (bf16[1536,128]{1,0:T(8,128)(2,1)S(1)}, bf16[1536,128]{1,0:T(8,128)(2,1)}, u32[]{:S(2)}) copy-start(bf16[1536,128]{1,0:T(8,128)(2,1)} %copy-done.27) | copy-start | bytes 1179652
  63.5 15.9 %collective-permute-start.11 = (bf16[512,512]{1,0:T(8,128)(2,1)S(1)}, bf16[512,512]{1,0:T(8,128)(2,1)S(1)}, u32[]{:S(2)}, u32[]{:S(2)}) collective-permute-start(bf16[512,512]{1,0:T(8,128)(2,1)S(1)} %project.8), channel_id=1, source_target_pairs={{0,2},{1,3},{6,4},{7,5},{8,10},{9,11},{14,12},{15,13},{16,18},{17,... | collective-permute-start | bytes 1572872 | tf_op jit(solution)/shard_map/ppermute | solution.py:435
  69.6 30.2 %collective-permute-start.15 = (bf16[512,512]{1,0:T(8,128)(2,1)S(1)}, bf16[512,512]{1,0:T(8,128)(2,1)S(1)}, u32[]{:S(2)}, u32[]{:S(2)}) collective-permute-start(bf16[512,512]{1,0:T(8,128)(2,1)S(1)} %project.9), channel_id=1, source_target_pairs={{0,2},{1,3},{6,4},{7,5},{8,10},{9,11},{14,12},{15,13},{16,18},{17,... | collective-permute-start | bytes 1572872 | tf_op jit(solution)/shard_map/ppermute | solution.py:435
  70.9 11.8 %collective-permute-start.8 = (bf16[1536,128]{1,0:T(8,128)(2,1)S(1)}, bf16[1536,128]{1,0:T(8,128)(2,1)S(1)}, u32[]{:S(2)}, u32[]{:S(2)}) collective-permute-start(bf16[1536,128]{1,0:T(8,128)(2,1)S(1)} %copy-done.28), channel_id=1, source_target_pairs={{0,24},{8,16},{16,8},{24,0},{1,25},{9,17},{17,9},{25,1},{2,26},{10... | collective-permute-start | bytes 1179656 | tf_op jit(solution)/shard_map/ppermute | solution.py:430
  74.9 7.9 %copy-start.10 = (bf16[1024,512]{1,0:T(8,128)(2,1)S(1)}, bf16[1024,512]{1,0:T(8,128)(2,1)}, u32[]{:S(2)}) copy-start(bf16[1024,512]{1,0:T(8,128)(2,1)} %refs_5_.5) | copy-start | bytes 3145732
  74.9 7.9 %copy-start.12 = (bf16[1552,128]{1,0:T(8,128)(2,1)S(1)}, bf16[1552,128]{1,0:T(8,128)(2,1)}, u32[]{:S(2)}) copy-start(bf16[1552,128]{1,0:T(8,128)(2,1)} %copy-done.11) | copy-start | bytes 1191940
  74.9 7.9 %copy-start.14 = (bf16[1552,128]{1,0:T(8,128)(2,1)S(1)}, bf16[1552,128]{1,0:T(8,128)(2,1)}, u32[]{:S(2)}) copy-start(bf16[1552,128]{1,0:T(8,128)(2,1)} %copy-done.13) | copy-start | bytes 1191940
  74.9 7.9 %copy-start.16 = (bf16[1536,128]{1,0:T(8,128)(2,1)S(1)}, bf16[1536,128]{1,0:T(8,128)(2,1)}, u32[]{:S(2)}) copy-start(bf16[1536,128]{1,0:T(8,128)(2,1)} %copy-done.15) | copy-start | bytes 1179652
  74.9 7.9 %copy-start.18 = (bf16[1536,128]{1,0:T(8,128)(2,1)S(1)}, bf16[1536,128]{1,0:T(8,128)(2,1)}, u32[]{:S(2)}) copy-start(bf16[1536,128]{1,0:T(8,128)(2,1)} %copy-done.17) | copy-start | bytes 1179652
  77.6 5.2 %copy-start.7 = (bf16[1024,512]{1,0:T(8,128)(2,1)S(1)}, bf16[1024,512]{1,0:T(8,128)(2,1)}, u32[]{:S(2)}) copy-start(bf16[1024,512]{1,0:T(8,128)(2,1)} %refs_4_.5) | copy-start | bytes 3145732
  82.8 24.2 %copy-start.2 = (bf16[512,4096]{1,0:T(8,128)(2,1)S(1)}, bf16[512,4096]{1,0:T(8,128)(2,1)}, u32[]{:S(2)}) copy-start(bf16[512,4096]{1,0:T(8,128)(2,1)} %w_mine_ref.15) | copy-start | bytes 12582916
  96.2 6.1 %collective-permute-start.12 = (bf16[512,128]{1,0:T(8,128)(2,1)S(1)}, bf16[512,128]{1,0:T(8,128)(2,1)S(1)}, u32[]{:S(2)}, u32[]{:S(2)}) collective-permute-start(bf16[512,128]{1,0:T(8,128)(2,1)S(1)} %get-tuple-element.79), channel_id=1, source_target_pairs={{0,8},{8,0},{16,24},{24,16},{1,9},{9,1},{17,25},{25,17},{2,10},{10... | collective-permute-start | bytes 393224 | tf_op jit(solution)/shard_map/ppermute | solution.py:430
  97.8 7.1 %collective-permute-start.13 = (bf16[512,128]{1,0:T(8,128)(2,1)S(1)}, bf16[512,128]{1,0:T(8,128)(2,1)S(1)}, u32[]{:S(2)}, u32[]{:S(2)}) collective-permute-start(bf16[512,128]{1,0:T(8,128)(2,1)S(1)} %get-tuple-element.80), channel_id=1, source_target_pairs={{0,16},{8,24},{16,0},{24,8},{1,17},{9,25},{17,1},{25,9},{2,18},{10... | collective-permute-start | bytes 393224 | tf_op jit(solution)/shard_map/ppermute | solution.py:430
  98.3 6.6 %collective-permute-start.14 = (bf16[512,128]{1,0:T(8,128)(2,1)S(1)}, bf16[512,128]{1,0:T(8,128)(2,1)S(1)}, u32[]{:S(2)}, u32[]{:S(2)}) collective-permute-start(bf16[512,128]{1,0:T(8,128)(2,1)S(1)} %get-tuple-element.81), channel_id=1, source_target_pairs={{0,24},{8,16},{16,8},{24,0},{1,25},{9,17},{17,9},{25,1},{2,26},{10... | collective-permute-start | bytes 393224 | tf_op jit(solution)/shard_map/ppermute | solution.py:430
  105.0 2.0 %collective-permute-start.16 = (bf16[512,512]{1,0:T(8,128)(2,1)S(1)}, bf16[512,512]{1,0:T(8,128)(2,1)S(1)}, u32[]{:S(2)}, u32[]{:S(2)}) collective-permute-start(bf16[512,512]{1,0:T(8,128)(2,1)S(1)} %assemble.3.mine_ref), channel_id=1, source_target_pairs={{0,1},{1,0},{2,3},{3,2},{4,5},{5,4},{6,7},{7,6},{8,9},{9,8},{10,11... | collective-permute-start | bytes 1572872 | tf_op jit(solution)/shard_map/ppermute | solution.py:430
  105.1 14.0 %collective-permute-start.17 = (bf16[512,512]{1,0:T(8,128)(2,1)S(1)}, bf16[512,512]{1,0:T(8,128)(2,1)S(1)}, u32[]{:S(2)}, u32[]{:S(2)}) collective-permute-start(bf16[512,512]{1,0:T(8,128)(2,1)S(1)} %project.10), channel_id=1, source_target_pairs={{0,2},{1,3},{6,4},{7,5},{8,10},{9,11},{14,12},{15,13},{16,18},{17,... | collective-permute-start | bytes 1572872 | tf_op jit(solution)/shard_map/ppermute | solution.py:435
  108.2 22.1 %collective-permute-start.24 = (bf16[512,512]{1,0:T(8,128)(2,1)S(1)}, bf16[512,512]{1,0:T(8,128)(2,1)S(1)}, u32[]{:S(2)}, u32[]{:S(2)}) collective-permute-start(bf16[512,512]{1,0:T(8,128)(2,1)S(1)} %project.15), channel_id=1, source_target_pairs={{0,2},{1,3},{6,4},{7,5},{8,10},{9,11},{14,12},{15,13},{16,18},{17,... | collective-permute-start | bytes 1572872 | tf_op jit(solution)/shard_map/ppermute | solution.py:435
  110.0 21.1 %collective-permute-start.19 = (bf16[512,512]{1,0:T(8,128)(2,1)S(1)}, bf16[512,512]{1,0:T(8,128)(2,1)S(1)}, u32[]{:S(2)}, u32[]{:S(2)}) collective-permute-start(bf16[512,512]{1,0:T(8,128)(2,1)S(1)} %add_convert_fusion.7), channel_id=1, source_target_pairs={{2,4},{3,5},{4,2},{5,3},{10,12},{11,13},{12,10},{13,11},{18,20},{1... | collective-permute-start | bytes 1572872 | tf_op jit(solution)/shard_map/ppermute | solution.py:435
  110.8 34.4 %collective-permute-start.18 = (bf16[512,512]{1,0:T(8,128)(2,1)S(1)}, bf16[512,512]{1,0:T(8,128)(2,1)S(1)}, u32[]{:S(2)}, u32[]{:S(2)}) collective-permute-start(bf16[512,512]{1,0:T(8,128)(2,1)S(1)} %add_convert_fusion.6), channel_id=1, source_target_pairs={{2,4},{3,5},{4,2},{5,3},{10,12},{11,13},{12,10},{13,11},{18,20},{1... | collective-permute-start | bytes 1572872 | tf_op jit(solution)/shard_map/ppermute | solution.py:435
  119.1 22.5 %collective-permute-start.22 = (bf16[512,512]{1,0:T(8,128)(2,1)S(1)}, bf16[512,512]{1,0:T(8,128)(2,1)S(1)}, u32[]{:S(2)}, u32[]{:S(2)}) collective-permute-start(bf16[512,512]{1,0:T(8,128)(2,1)S(1)} %project.12), channel_id=1, source_target_pairs={{0,2},{1,3},{6,4},{7,5},{8,10},{9,11},{14,12},{15,13},{16,18},{17,... | collective-permute-start | bytes 1572872 | tf_op jit(solution)/shard_map/ppermute | solution.py:435
  130.5 11.9 %collective-permute-start.25 = (bf16[512,512]{1,0:T(8,128)(2,1)S(1)}, bf16[512,512]{1,0:T(8,128)(2,1)S(1)}, u32[]{:S(2)}, u32[]{:S(2)}) collective-permute-start(bf16[512,512]{1,0:T(8,128)(2,1)S(1)} %add_convert_fusion.2), channel_id=1, source_target_pairs={{2,4},{3,5},{4,2},{5,3},{10,12},{11,13},{12,10},{13,11},{18,20},{1... | collective-permute-start | bytes 1572872 | tf_op jit(solution)/shard_map/ppermute | solution.py:435
  131.3 17.7 %collective-permute-start.20 = (bf16[512,512]{1,0:T(8,128)(2,1)S(1)}, bf16[512,512]{1,0:T(8,128)(2,1)S(1)}, u32[]{:S(2)}, u32[]{:S(2)}) collective-permute-start(bf16[512,512]{1,0:T(8,128)(2,1)S(1)} %add_convert_fusion.5), channel_id=1, source_target_pairs={{4,6},{5,7},{2,0},{3,1},{12,14},{13,15},{10,8},{11,9},{20,22},{21,... | collective-permute-start | bytes 1572872 | tf_op jit(solution)/shard_map/ppermute | solution.py:435
  133.9 18.5 %collective-permute-start.21 = (bf16[512,512]{1,0:T(8,128)(2,1)S(1)}, bf16[512,512]{1,0:T(8,128)(2,1)S(1)}, u32[]{:S(2)}, u32[]{:S(2)}) collective-permute-start(bf16[512,512]{1,0:T(8,128)(2,1)S(1)} %project.14), channel_id=1, source_target_pairs={{0,2},{1,3},{6,4},{7,5},{8,10},{9,11},{14,12},{15,13},{16,18},{17,... | collective-permute-start | bytes 1572872 | tf_op jit(solution)/shard_map/ppermute | solution.py:435
  141.7 10.7 %collective-permute-start.23 = (bf16[512,512]{1,0:T(8,128)(2,1)S(1)}, bf16[512,512]{1,0:T(8,128)(2,1)S(1)}, u32[]{:S(2)}, u32[]{:S(2)}) collective-permute-start(bf16[512,512]{1,0:T(8,128)(2,1)S(1)} %add_convert_fusion.3), channel_id=1, source_target_pairs={{2,4},{3,5},{4,2},{5,3},{10,12},{11,13},{12,10},{13,11},{18,20},{1... | collective-permute-start | bytes 1572872 | tf_op jit(solution)/shard_map/ppermute | solution.py:435
  142.5 17.7 %collective-permute-start.26 = (bf16[512,512]{1,0:T(8,128)(2,1)S(1)}, bf16[512,512]{1,0:T(8,128)(2,1)S(1)}, u32[]{:S(2)}, u32[]{:S(2)}) collective-permute-start(bf16[512,512]{1,0:T(8,128)(2,1)S(1)} %add_convert_fusion.1), channel_id=1, source_target_pairs={{4,6},{5,7},{2,0},{3,1},{12,14},{13,15},{10,8},{11,9},{20,22},{21,... | collective-permute-start | bytes 1572872 | tf_op jit(solution)/shard_map/ppermute | solution.py:435

commit v2 on v1

v2 whole, which is shorter than its diff:
```python
import functools
import math

import jax
import jax.numpy as jnp
from jax import lax
from jax.experimental import pallas as pl
from jax.experimental.pallas import tpu as pltpu
from jax.sharding import PartitionSpec as P

HD = 128


MASKED_SCORE = -1e30
LOG2E = 1.4426950408889634


def passed_along(value, axis, steps):
    count = lax.axis_size(axis)
    pairs = [(source, (source + steps) % count) for source in range(count)]
    return lax.ppermute(value, axis, pairs)


def folded_positions(row_total, offset, shard_rows, devices_ctx):
    flat_index = offset + lax.iota(jnp.int32, row_total)
    owner_dev = flat_index // shard_rows
    within = flat_index % shard_rows
    half_rows = shard_rows // 2
    fold_block = jnp.where(within < half_rows, owner_dev, 2 * devices_ctx - 1 - owner_dev)
    return fold_block * half_rows + within % half_rows


def block_update(
    running, query, query_pos, query_doc, key_block, value_block, pos_block, doc_block
):
    largest, totals, summed = running
    query_rows = query.shape[0]
    local_heads = query.shape[1] // HD
    query_heads = query.reshape(query_rows, local_heads, HD)
    key_heads = key_block.reshape(key_block.shape[0], local_heads, HD)
    value_heads = value_block.reshape(value_block.shape[0], local_heads, HD)
    scores = jnp.einsum(
        "qhd,khd->hqk", query_heads, key_heads, preferred_element_type=jnp.float32
    ) * (1.0 / math.sqrt(HD))
    allowed = (query_doc[:, None] == doc_block[None, :]) & (
        pos_block[None, :] <= query_pos[:, None]
    )
    scores = jnp.where(allowed[None], scores, MASKED_SCORE)
    new_max = jnp.maximum(largest, jnp.max(scores, axis=2))
    weights = jnp.where(allowed[None], jnp.exp(scores - new_max[:, :, None]), 0.0)
    factor = jnp.exp(largest - new_max)
    totals = totals * factor + jnp.sum(weights, axis=2)
    product = jnp.einsum(
        "hqk,khd->qhd",
        weights.astype(jnp.bfloat16),
        value_heads,
        preferred_element_type=jnp.float32,
    )
    summed = summed * factor.T[:, :, None] + product
    return (new_max, totals, summed)


def attend_rows(running, query, query_pos, query_doc, key_rows, value_rows, key_pos, key_doc):
    row_total = key_rows.shape[0]
    block_rows = math.gcd(row_total, query.shape[0])
    block_count = row_total // block_rows
    highest = jnp.max(query_pos)

    def visit(partial_value, blocks):
        key_block, value_block, pos_block, doc_block = blocks
        masked_out = jnp.min(pos_block) > highest
        updated = lax.cond(
            masked_out,
            lambda frozen: frozen,
            lambda frozen: block_update(
                frozen, query, query_pos, query_doc, key_block, value_block, pos_block, doc_block
            ),
            partial_value,
        )
        return (updated, None)

    blocks = (
        key_rows.reshape(block_count, block_rows, key_rows.shape[1]),
        value_rows.reshape(block_count, block_rows, value_rows.shape[1]),
        key_pos.reshape(block_count, block_rows),
        key_doc.reshape(block_count, block_rows),
    )
    running, _ = lax.scan(visit, running, blocks)
    return running


def attend_shard(running, query, query_pos, query_doc, key_rows, value_rows, key_pos, key_doc):
    largest, totals, summed = running
    half_rows = query.shape[0] // 2
    new_largest = []
    new_totals = []
    new_summed = []
    for half_idx in range(2):
        lower = half_idx * half_rows
        part_state = (largest[half_idx], totals[half_idx], summed[half_idx])
        part_state = attend_rows(
            part_state,
            query[lower : lower + half_rows],
            query_pos[lower : lower + half_rows],
            query_doc[lower : lower + half_rows],
            key_rows,
            value_rows,
            key_pos,
            key_doc,
        )
        new_largest.append(part_state[0])
        new_totals.append(part_state[1])
        new_summed.append(part_state[2])
    return (jnp.stack(new_largest), jnp.stack(new_totals), jnp.stack(new_summed))


def ring_local(queries, keys, values, doc_ids, w_out):
    shard_rows = queries.shape[0]
    half_rows = shard_rows // 2
    local_heads = queries.shape[1] // HD
    devices_ctx = lax.axis_size("ctx")
    ctx_index = lax.axis_index("ctx")
    all_docs = lax.all_gather(doc_ids, "ctx", axis=0, tiled=True)
    own_pos = folded_positions(shard_rows, ctx_index * shard_rows, shard_rows, devices_ctx)
    running = (
        jnp.full((2, local_heads, half_rows), MASKED_SCORE, jnp.float32),
        jnp.zeros((2, local_heads, half_rows), jnp.float32),
        jnp.zeros((2, half_rows, local_heads, HD), jnp.float32),
    )
    travel = queries
    for hop_step in range(devices_ctx):
        anchor = (ctx_index - hop_step) % devices_ctx
        query_pos = folded_positions(shard_rows, anchor * shard_rows, shard_rows, devices_ctx)
        query_doc = lax.dynamic_slice_in_dim(all_docs, anchor * shard_rows, shard_rows, 0)
        largest, totals, summed = attend_shard(
            running, travel, query_pos, query_doc, keys, values, own_pos, doc_ids
        )
        running = (
            passed_along(largest.astype(jnp.bfloat16), "ctx", 1).astype(largest.dtype),
            passed_along(totals.astype(jnp.bfloat16), "ctx", 1).astype(totals.dtype),
            passed_along(summed.astype(jnp.bfloat16), "ctx", 1).astype(summed.dtype),
        )
        if hop_step + 1 < devices_ctx:
            travel = passed_along(travel, "ctx", 1)
    largest, totals, summed = running
    attended = summed / totals.transpose(0, 2, 1)[:, :, :, None]
    attended = attended.reshape(shard_rows, local_heads * HD).astype(jnp.bfloat16)
    partial_out = jnp.dot(attended, w_out, preferred_element_type=jnp.float32)
    return lax.psum_scatter(
        partial_out.astype(jnp.bfloat16), "head", scatter_dimension=1, tiled=True
    )


SMALL = pl.CostEstimate(flops=1024, bytes_accessed=1024, transcendentals=0)
TILE = 256


def params(mib):
    return pltpu.CompilerParams(vmem_limit_bytes=mib * 1024 * 1024)


def whole(shape):
    return pl.BlockSpec(shape, lambda step, scalars: (0,) * len(shape))


def pack(ctx_index, half, queries, keys, values, docs):
    rows = queries.shape[0] // 2
    group = queries.shape[1] // HD
    doc_rows = 0 if docs is None else 16 * pl.cdiv(docs.shape[0], 16)
    total = 3 * rows + doc_rows

    def kernel(ctx_ref, *refs):
        outs = refs[len(refs) - (group - 1) :]
        if docs is not None:
            mine = refs[3 * (group - 1)][...].astype(jnp.float32)
            empty = jnp.zeros((doc_rows - mine.shape[0], HD), jnp.float32)
            mine = jnp.concatenate([mine, empty], axis=0).astype(jnp.bfloat16)
        for place in range(group - 1):
            for part in range(3):
                outs[place][part * rows : (part + 1) * rows, :] = refs[place * 3 + part][...]
            if docs is not None:
                outs[place][3 * rows :, :] = mine

    def piece(distance):
        return pl.BlockSpec((rows, HD), lambda step, ctx: (half, ctx[0] ^ distance))

    in_specs = []
    operands = []
    for distance in range(1, group):
        for array in (queries, keys, values):
            in_specs.append(piece(distance))
            operands.append(array)
    if docs is not None:
        in_specs.append(whole(docs.shape))
        operands.append(docs)
    return pl.pallas_call(
        kernel,
        grid_spec=pltpu.PrefetchScalarGridSpec(
            num_scalar_prefetch=1,
            grid=(1,),
            in_specs=in_specs,
            out_specs=[whole((total, HD))] * (group - 1),
        ),
        out_shape=[jax.ShapeDtypeStruct((total, HD), jnp.bfloat16)] * (group - 1),
        compiler_params=params(56),
        cost_estimate=SMALL,
        name="pack",
    )(ctx_index, *operands)


def pack_projection(places, w_out, chips):
    depth, width = w_out.shape
    columns = width // (2 * chips)

    def kernel(places_ref, keep_in, give_in, keep_out, give_out):
        keep_out[...] = keep_in[...]
        give_out[...] = give_in[...]

    def block(other):
        def index_map(turn, at):
            parity = 1 - at[chips] if other else at[chips]
            return (0, 2 * at[turn] + parity)

        return pl.BlockSpec((depth, columns), index_map)

    out_spec = pl.BlockSpec((depth, columns), lambda turn, at: (0, turn))
    return pl.pallas_call(
        kernel,
        grid_spec=pltpu.PrefetchScalarGridSpec(
            num_scalar_prefetch=1,
            grid=(chips,),
            in_specs=[block(False), block(True)],
            out_specs=[out_spec] * 2,
        ),
        out_shape=[jax.ShapeDtypeStruct((depth, chips * columns), w_out.dtype)] * 2,
        compiler_params=params(56),
        cost_estimate=SMALL,
        name="pack_projection",
    )(places, w_out, w_out)


def attend(ctx_index, queries, keys, values, docs, low, high, tiles):
    rows = queries.shape[0] // 2
    group = queries.shape[1] // HD
    with_high = high is not None
    per_block = rows // TILE
    key_rows = (2 * group if with_high else group) * rows
    key_tiles = key_rows // TILE
    lanes = TILE // HD
    scaling = LOG2E / math.sqrt(HD)

    def kernel(ctx_ref, *refs):
        refs = list(refs)
        own_low = [refs.pop(0) for _ in range(3)]
        own_high = [refs.pop(0) for _ in range(3)] if with_high else None
        own_docs = refs.pop(0)
        low_refs = [refs.pop(0) for _ in range(group - 1)]
        high_refs = [refs.pop(0) for _ in range(group - 1)] if with_high else None
        outs = [refs.pop(0) for _ in range(group)]
        key_buf, value_buf, doc_buf = refs
        ctx = ctx_ref[0]

        def part(upper, distance, index, lower=0, count=rows):
            if distance == 0:
                return (own_high if upper else own_low)[index][lower : lower + count, :]
            source = (high_refs if upper else low_refs)[distance - 1]
            return source[index * rows + lower : index * rows + lower + count, :]

        place = {}
        doc_lines = {}
        for upper in (False, True) if with_high else (False,):
            for distance in range(group):
                source = ctx ^ distance
                block = 2 * group - 1 - source if upper else source
                place[upper, distance] = block
                offset = pl.multiple_of(block * rows, rows)
                key_buf[pl.ds(offset, rows), :] = part(upper, distance, 1)
                value_buf[pl.ds(offset, rows), :HD] = part(upper, distance, 2)
                if distance == 0:
                    both = own_docs[...].astype(jnp.float32)
                else:
                    both = low_refs[distance - 1][3 * rows :, :].astype(jnp.float32)
                begin = rows // HD if upper else 0
                for tile in range(per_block):
                    first = begin + tile * lanes
                    lines = [both[line : line + 1, :] for line in range(first, first + lanes)]
                    doc_lines[upper, distance, tile] = lines
                    doc_buf[pl.ds(block * per_block + tile, 1), :] = jnp.concatenate(lines, axis=1)
        value_buf[:, HD:] = jnp.ones((key_rows, HD), jnp.bfloat16)
        last_docs = doc_buf[:, TILE - 1 : TILE]

        def scores_of(query, index):
            offset = pl.multiple_of(index * TILE, TILE)
            raw = lax.dot_general(
                query,
                key_buf[pl.ds(offset, TILE), :],
                (((1,), (1,)), ((), ())),
                preferred_element_type=jnp.float32,
            )
            return raw * scaling

        def weighted(weights, index):
            offset = pl.multiple_of(index * TILE, TILE)
            return jnp.dot(
                weights.astype(jnp.bfloat16),
                value_buf[pl.ds(offset, TILE), :],
                preferred_element_type=jnp.float32,
            )

        causal = lax.broadcasted_iota(jnp.int32, (TILE, TILE), 1) <= lax.broadcasted_iota(
            jnp.int32, (TILE, TILE), 0
        )
        for number, tile in enumerate(tiles):
            state = []
            starts = []
            ends = []
            queries_of = []
            docs_of = []
            for distance in range(group):
                lines = doc_lines[with_high, distance, tile]
                column = jnp.concatenate(
                    [jnp.transpose(jnp.broadcast_to(line, (HD, HD))) for line in lines], axis=0
                )
                query_doc = jnp.concatenate([column] * lanes, axis=1)
                end = place[with_high, distance] * per_block + tile
                earlier = last_docs < lines[0][:, :1]
                starts.append(jnp.sum(earlier.astype(jnp.int32)))
                ends.append(end)
                query = part(with_high, distance, 0, tile * TILE, TILE)
                queries_of.append(query)
                docs_of.append(query_doc)
                same = query_doc == jnp.concatenate(lines, axis=1)
                scores = jnp.where(same & causal, scores_of(query, end), MASKED_SCORE)
                largest = jnp.max(scores, axis=1, keepdims=True)
                summed = weighted(jnp.exp2(scores - largest), end)
                state.append((largest, summed))

            longest = ends[0] - starts[0]
            for distance in range(1, group):
                longest = jnp.maximum(longest, ends[distance] - starts[distance])

            def visit(step, running):
                renewed = []
                for distance in range(group):
                    largest, summed = running[distance]
                    wanted = starts[distance] + step
                    index = jnp.minimum(wanted, ends[distance])
                    key_doc = doc_buf[pl.ds(index, 1), :]
                    key_doc = jnp.where(wanted < ends[distance], key_doc, -1.0)
                    scores = scores_of(queries_of[distance], index)
                    scores = jnp.where(docs_of[distance] == key_doc, scores, MASKED_SCORE)
                    new_max = jnp.maximum(largest, jnp.max(scores, axis=1, keepdims=True))
                    factor = jnp.exp2(largest - new_max)
                    product = weighted(jnp.exp2(scores - new_max), index)
                    renewed.append((new_max, summed * factor + product))
                return tuple(renewed)

            state = lax.fori_loop(0, longest, visit, tuple(state))
            for distance in range(group):
                summed = state[distance][1]
                outs[distance][number * TILE : (number + 1) * TILE, :] = (
                    summed[:, :HD] / summed[:, HD:]
                ).astype(jnp.bfloat16)

    def own(upper):
        return pl.BlockSpec((rows, HD), lambda step, ctx: (int(upper), ctx[0]))

    in_specs = [own(False)] * 3
    operands = [queries, keys, values]
    if with_high:
        in_specs += [own(True)] * 3
        operands += [queries, keys, values]
    received = [docs, *low, *(high if with_high else ())]
    operands += received
    in_specs += [whole(array.shape) for array in received]
    out_rows = len(tiles) * TILE
    return pl.pallas_call(
        kernel,
        grid_spec=pltpu.PrefetchScalarGridSpec(
            num_scalar_prefetch=1,
            grid=(1,),
            in_specs=in_specs,
            out_specs=[whole((out_rows, HD))] * group,
            scratch_shapes=[
                pltpu.VMEM((key_rows, HD), jnp.bfloat16),
                pltpu.VMEM((key_rows, 2 * HD), jnp.bfloat16),
                pltpu.VMEM((key_tiles, TILE), jnp.float32),
            ],
        ),
        out_shape=[jax.ShapeDtypeStruct((out_rows, HD), jnp.bfloat16)] * group,
        compiler_params=params(40),
        cost_estimate=SMALL,
        name="attend",
    )(ctx_index, *operands)


def assemble(ctx_index, pieces):
    rows = pieces[0].shape[0]
    group = len(pieces)

    def kernel(ctx_ref, *refs):
        for distance in range(group):
            column = pl.multiple_of((ctx_ref[0] ^ distance) * HD, HD)
            refs[-1][:, pl.ds(column, HD)] = refs[distance][...]

    return pl.pallas_call(
        kernel,
        grid_spec=pltpu.PrefetchScalarGridSpec(
            num_scalar_prefetch=1,
            grid=(1,),
            in_specs=[whole((rows, HD))] * group,
            out_specs=whole((rows, group * HD)),
        ),
        out_shape=jax.ShapeDtypeStruct((rows, group * HD), jnp.bfloat16),
        compiler_params=params(16),
        cost_estimate=SMALL,
        name="assemble",
    )(ctx_index, *pieces)


def project(mine, sibling, w_mine, w_sibling, first, count, chips):
    rows, depth = mine.shape
    columns = w_mine.shape[1] // chips

    def kernel(mine_ref, sibling_ref, w_mine_ref, w_sibling_ref, out_ref):
        total = jnp.dot(mine_ref[...], w_mine_ref[...], preferred_element_type=jnp.float32)
        total += jnp.dot(sibling_ref[...], w_sibling_ref[...], preferred_element_type=jnp.float32)
        out_ref[...] = total.astype(jnp.bfloat16)

    weights = pl.BlockSpec((depth, columns), lambda turn: (0, first + turn))
    attended = pl.BlockSpec((rows, depth), lambda turn: (0, 0))
    return pl.pallas_call(
        kernel,
        grid=(count,),
        in_specs=[attended, attended, weights, weights],
        out_specs=pl.BlockSpec((rows, columns), lambda turn: (0, turn)),
        out_shape=jax.ShapeDtypeStruct((rows, count * columns), jnp.bfloat16),
        compiler_params=params(16),
        cost_estimate=SMALL,
        name="project",
    )(mine, sibling, w_mine, w_sibling)


def swap(value, axis, distance):
    count = lax.axis_size(axis)
    return lax.ppermute(value, axis, [(source, source ^ distance) for source in range(count)])


def between_chips(value, pairs):
    both = [(2 * source + core, 2 * target + core) for source, target in pairs for core in (0, 1)]
    return lax.ppermute(value, "head", both)


def add(*terms):
    total = terms[0].astype(jnp.float32)
    for term in terms[1:]:
        total = total + term.astype(jnp.float32)
    return total.astype(jnp.bfloat16)


SENDING = ((3, 2, 1, 0), (3, 2, 0, 1), (0, 1, 3, 2), (0, 1, 2, 3))
TO_MIDDLE = ((0, 1), (3, 2))
ACROSS = ((1, 2), (2, 1))
TO_ENDS = ((2, 3), (1, 0))


def tie(*values):
    return lax.optimization_barrier(values)


def exchange_local(queries, keys, values, doc_ids, w_out):
    shard_rows = queries.shape[0]
    group = queries.shape[1] // HD
    chips = lax.axis_size("head") // 2
    columns = w_out.shape[1] // (2 * chips)
    ctx_index = lax.axis_index("ctx").astype(jnp.int32).reshape(1)
    head_index = lax.axis_index("head").astype(jnp.int32)
    chip = head_index // 2
    core = (head_index % 2).reshape(1)
    places = jnp.concatenate([jnp.array(SENDING, jnp.int32)[chip], core])
    docs = doc_ids.reshape(shard_rows // HD, HD)
    near = range(1, group)

    low_out = pack(ctx_index, 0, queries, keys, values, docs)
    low = [swap(low_out[distance - 1], "ctx", distance) for distance in near]
    w_mine, w_give = pack_projection(places, w_out, chips)
    low, w_give = tie(low, w_give)
    w_sibling = swap(w_give, "head", 1)
    high_out = pack(ctx_index, 1, queries, keys, values, None)

    def attend_rows(high, tiles):
        return attend(ctx_index, queries, keys, values, docs, low, high, tiles)

    def send_back(pieces):
        return [swap(pieces[distance], "ctx", distance) for distance in near]

    def share_of(mine, sibling, first, count):
        return project(mine, sibling, w_mine, w_sibling, first, count, chips)

    pieces = attend_rows(None, (0,))
    back = send_back(pieces)
    pieces, high_out = tie(pieces, high_out)
    high = [swap(high_out[0], "ctx", 1), swap(high_out[1], "ctx", 2)]
    mine = [assemble(ctx_index, [pieces[0], *back])]
    mine[0], diagonal_out = tie(mine[0], high_out[2])
    high.append(swap(diagonal_out, "ctx", 3))
    sibling = [swap(mine[0], "head", 1)]
    shares = [share_of(mine[0], sibling[0], 0, 2)]
    end = [between_chips(shares[0], TO_MIDDLE)]

    pieces = attend_rows(None, tuple(range(1, shard_rows // 2 // TILE)))
    back = send_back(pieces)
    back, shares, high = tie(back, shares, high)
    mine.append(assemble(ctx_index, [pieces[0], *back]))
    sibling.append(swap(mine[1], "head", 1))
    shares.append(share_of(mine[1], sibling[1], 0, 2))
    end.append(between_chips(shares[1], TO_MIDDLE))
    rest = [share_of(mine[turn], sibling[turn], 2, 2) for turn in range(2)]
    rest = jnp.concatenate(rest, axis=0)
    passed = add(shares[0], end[0])

    high, passed, rest, shares = tie(high, passed, rest, shares)
    across = [between_chips(passed, ACROSS)]
    pieces = attend_rows(high, tuple(range(shard_rows // 2 // TILE)))
    back = send_back(pieces)
    passed = add(shares[1], end[1])
    back, passed, kept, across[0] = tie(back, passed, rest[:, :columns], across[0])
    across.append(between_chips(passed, ACROSS))
    end_low = between_chips(kept, TO_MIDDLE)
    mine_high = assemble(ctx_index, [pieces[0], *back])
    sibling_high = swap(mine_high, "head", 1)
    late = [share_of(mine_high, sibling_high, turn, 1) for turn in range(4)]
    end_high = [between_chips(late[0], TO_MIDDLE)]
    across_low = jnp.concatenate(across, axis=0)
    outer_low = between_chips(add(rest[:, :columns], across_low[:, :columns]), TO_ENDS)
    passed = add(late[0], end_high[0])
    late[1], passed = tie(late[1], passed)
    across_high = [between_chips(passed, ACROSS)]
    end_high.append(between_chips(late[1], TO_MIDDLE))
    passed = add(late[1], end_high[1])
    late[2], passed = tie(late[2], passed)
    across_high.append(between_chips(passed, ACROSS))
    end_high.append(between_chips(late[2], TO_MIDDLE))
    outer_high = between_chips(add(late[2], across_high[0]), TO_ENDS)
    first = add(rest[:, columns:], end_low, across_low[:, columns:], outer_low)
    second = add(late[3], end_high[2], across_high[1], outer_high)
    return jnp.concatenate([first, second], axis=0)


def solution(mesh):
    in_specs = (P("ctx", "head"), P("ctx", "head"), P("ctx", "head"), P("ctx"), P("head", None))
    out_specs = P("ctx", "head")
    ctx_count = mesh.shape["ctx"]
    head_count = mesh.shape["head"]

    def local(queries, keys, values, doc_ids, w_out):
        heads = queries.shape[1] // HD
        exchange = heads == ctx_count and heads == 4 and head_count == 2 * len(SENDING)
        exchange = exchange and queries.shape[0] % (4 * TILE) == 0
        body = exchange_local if exchange else ring_local
        return body(queries, keys, values, doc_ids, w_out)

    return jax.shard_map(
        local, mesh=mesh, in_specs=in_specs, out_specs=out_specs, check_vma=False
    )
```

time: 161 us -> 152 us (0.944); the launches traced: 162 us -> 150 us
  local copies, waits for them, and re-layouts: 14 us -> 0.82 us
  starting transfers between devices: 40.9 us -> 48.6 us
  Pallas kernels: 39.1 us -> 32.6 us
    unnamed x58 -> x17, local copies, waits for them, and re-layouts: 13.4 us -> 0.07 us
    pallas_call x8, Pallas kernels: 15 us -> 7.25 us  [project(): pl.pallas_call(kernel, grid=(count,), in_specs=[attended, attended, weigh...]
    pallas_call x2 -> x3, Pallas kernels: 20.4 us -> 14.7 us  [attend(): pl.pallas_call(kernel, grid_spec=pltpu.PrefetchScalarGridSpec(num_scalar_...]
    pallas_call x2, Pallas kernels: 0.56 us -> 4.8 us  [pack(): pl.pallas_call(kernel, grid_spec=pltpu.PrefetchScalarGridSpec(num_scalar_...]
    ppermute x12, starting transfers between devices: 25.6 us -> 29.7 us  [between_chips(): return lax.ppermute(value, 'head', both)]
    pallas_call x1, Pallas kernels: 2.12 us -> 5.69 us  [pack_projection(): pl.pallas_call(kernel, grid_spec=pltpu.PrefetchScalarGridSpec(num_scalar_...]
    ppermute x15 -> x19, starting transfers between devices: 15.4 us -> 18.9 us  [swap(): lax.ppermute(value, axis, [(source, source ^ distance) for source in rang...]
    ppermute x15 -> x19, waiting for transfers between devices: 34.3 us -> 34.6 us  [swap(): lax.ppermute(value, axis, [(source, source ^ distance) for source in rang...]
  transfers between devices with their start and end apart: 27 -> 31, of which waited for: 17 -> 15; matrix products, arithmetic and copies ran while one was open for 1% -> 2% of each run, Pallas kernels for 21% -> 20%
where the time goes in v2:
time: 152 us; the launch traced here: 150 us
  waiting for transfers between devices  64.4 us (42%)
  starting transfers between devices  48.6 us (32%)
  Pallas kernels  32.6 us (21%)
  other arithmetic  3.45 us (2%)
    ppermute x19, waiting for transfers between devices, swap(): lax.ppermute(value, axis, [(source, source ^ distance) for source in rang...  34.6 us
    ppermute x12, waiting for transfers between devices, between_chips(): return lax.ppermute(value, 'head', both)  29.9 us
    ppermute x12, starting transfers between devices, between_chips(): return lax.ppermute(value, 'head', both)  29.7 us
    ppermute x19, starting transfers between devices, swap(): lax.ppermute(value, axis, [(source, source ^ distance) for source in rang...  18.9 us
    pallas_call x3, Pallas kernels, attend(): pl.pallas_call(kernel, grid_spec=pltpu.PrefetchScalarGridSpec(num_scalar_...  14.7 us
    pallas_call x8, Pallas kernels, project(): pl.pallas_call(kernel, grid=(count,), in_specs=[attended, attended, weigh...  7.25 us
    pallas_call x1, Pallas kernels, pack_projection(): pl.pallas_call(kernel, grid_spec=pltpu.PrefetchScalarGridSpec(num_scalar_...  5.69 us
    pallas_call x2, Pallas kernels, pack(): pl.pallas_call(kernel, grid_spec=pltpu.PrefetchScalarGridSpec(num_scalar_...  4.8 us
  transfers between devices with their start and end apart: 31, of which 15 were waited for; matrix products, arithmetic and copies ran while one was open for 2% of the time, Pallas kernels for 20%

profile of v2, /device:TPU:0, one launch (start us, length us, event | category | flops | bytes accessed | tf_op | source)
XLA Modules:
  0.0 150.3 jit_solution(9799553295478686530)
XLA Ops:
  0.0 2.4 %pack.2 = (bf16[1552,128]{1,0:T(8,128)(2,1)}, bf16[1552,128]{1,0:T(8,128)(2,1)}, bf16[1552,128]{1,0:T(8,128)(2,1)}) custom-call(s32[1]{0:T(128)} %bitcast.ctx_ref, bf16[1024,512]{1,0:T(8,128)(2,1)} %refs_3_.5, bf16[1024,512]{1,0:T(8,128)(2,1)} %refs_4_.5, bf16[1024,512]{1,0:T(8,128)(2,1)} %refs_5_.5, bf16[1024,512]{1,0:T(8,128)(2,1)} %refs_3_.5, ...), custom_call_target="tpu_custom_call" | custom-call | flops 1024 | bytes 1024 | tf_op jit(solution)/shard_map/pack/pallas_call | solution.py:196
  2.4 2.9 %collective-permute-start = (bf16[1552,128]{1,0:T(8,128)(2,1)}, bf16[1552,128]{1,0:T(8,128)(2,1)S(1)}, u32[]{:S(2)}, u32[]{:S(2)}) collective-permute-start(bf16[1552,128]{1,0:T(8,128)(2,1)} %get-tuple-element.58), channel_id=1, source_target_pairs={{0,8},{8,0},{16,24},{24,16},{1,9},{9,1},{17,25},{25,17},{2,10},{10... | collective-permute-start | bytes 1191944 | tf_op jit(solution)/shard_map/ppermute | solution.py:446
  5.3 1.5 %collective-permute-start.1 = (bf16[1552,128]{1,0:T(8,128)(2,1)}, bf16[1552,128]{1,0:T(8,128)(2,1)S(1)}, u32[]{:S(2)}, u32[]{:S(2)}) collective-permute-start(bf16[1552,128]{1,0:T(8,128)(2,1)} %get-tuple-element.59), channel_id=1, source_target_pairs={{0,16},{8,24},{16,0},{24,8},{1,17},{9,25},{17,1},{25,9},{2,18},{10... | collective-permute-start | bytes 1191944 | tf_op jit(solution)/shard_map/ppermute | solution.py:446
  6.9 0.7 dynamic-slice_bitcast_fusion
  7.6 0.7 pad_add_fusion.places_ref
  8.2 5.7 %pack_projection.1 = (bf16[512,2048]{1,0:T(8,128)(2,1)}, bf16[512,2048]{1,0:T(8,128)(2,1)}) custom-call(s32[5]{0:T(128)} %pad_add_fusion.places_ref, bf16[512,4096]{1,0:T(8,128)(2,1)} %give_in.1, bf16[512,4096]{1,0:T(8,128)(2,1)} %give_in.1), custom_call_target="tpu_custom_call" | custom-call | flops 1024 | bytes 1024 | tf_op jit(solution)/shard_map/pack_projection/pallas_call | solution.py:227
  13.9 1.7 %collective-permute-done.refs_4_.refs_7_ = bf16[1552,128]{1,0:T(8,128)(2,1)S(1)} collective-permute-done((bf16[1552,128]{1,0:T(8,128)(2,1)}, bf16[1552,128]{1,0:T(8,128)(2,1)S(1)}, u32[]{:S(2)}, u32[]{:S(2)}) %collective-permute-start) | collective-permute-done | bytes 397344 | tf_op jit(solution)/shard_map/ppermute | solution.py:446
  15.6 9.1 %collective-permute-done.1.refs_5_.refs_8_ = bf16[1552,128]{1,0:T(8,128)(2,1)S(1)} collective-permute-done((bf16[1552,128]{1,0:T(8,128)(2,1)}, bf16[1552,128]{1,0:T(8,128)(2,1)S(1)}, u32[]{:S(2)}, u32[]{:S(2)}) %collective-permute-start.1) | collective-permute-done | bytes 397344 | tf_op jit(solution)/shard_map/ppermute | solution.py:446
  24.8 3.9 %attend.4 = (bf16[256,128]{1,0:T(8,128)(2,1)S(1)}, bf16[256,128]{1,0:T(8,128)(2,1)S(1)}, bf16[256,128]{1,0:T(8,128)(2,1)S(1)}, bf16[256,128]{1,0:T(8,128)(2,1)S(1)}) custom-call(s32[1]{0:T(128)} %bitcast.ctx_ref, bf16[1024,512]{1,0:T(8,128)(2,1)S(1)} %copy-done.1, bf16[1024,512]{1,0:T(8,128)(2,1)S(1)} %copy-done.3, bf16[1024,512]{1,0:T(8,128)(2,1)S(1)} %copy-done.5, ...), custom_call_target="tpu_custom_call" | custom-call | flops 1024 | bytes 1024 | tf_op jit(solution)/shard_map/attend/pallas_call | solution.py:377
  28.6 1.3 collective-permute-start.6
  29.9 0.8 collective-permute-start.7
  30.8 1.4 collective-permute-start.8
  32.2 2.4 %pack.3 = (bf16[1536,128]{1,0:T(8,128)(2,1)}, bf16[1536,128]{1,0:T(8,128)(2,1)}, bf16[1536,128]{1,0:T(8,128)(2,1)}) custom-call(s32[1]{0:T(128)} %bitcast.ctx_ref, bf16[1024,512]{1,0:T(8,128)(2,1)} %refs_3_.5, bf16[1024,512]{1,0:T(8,128)(2,1)} %refs_4_.5, bf16[1024,512]{1,0:T(8,128)(2,1)} %refs_5_.5, bf16[1024,512]{1,0:T(8,128)(2,1)} %refs_3_.5, ...), custom_call_target="tpu_custom_call" | custom-call | flops 1024 | bytes 1024 | tf_op jit(solution)/shard_map/pack/pallas_call | solution.py:196
  34.6 1.3 collective-permute-done.8.refs_3_
  36.1 1.6 %collective-permute-start.11 = (bf16[1536,128]{1,0:T(8,128)(2,1)}, bf16[1536,128]{1,0:T(8,128)(2,1)S(1)}, u32[]{:S(2)}, u32[]{:S(2)}) collective-permute-start(bf16[1536,128]{1,0:T(8,128)(2,1)} %get-tuple-element.80), channel_id=1, source_target_pairs={{0,8},{8,0},{16,24},{24,16},{1,9},{9,1},{17,25},{25,17},{2,10},{10... | collective-permute-start | bytes 1179656 | tf_op jit(solution)/shard_map/ppermute | solution.py:446
  37.6 0.5 collective-permute-start.12
  38.1 1.5 collective-permute-start.13
  39.6 3.0 %attend.3 = (bf16[256,128]{1,0:T(8,128)(2,1)S(1)}, bf16[256,128]{1,0:T(8,128)(2,1)S(1)}, bf16[256,128]{1,0:T(8,128)(2,1)S(1)}, bf16[256,128]{1,0:T(8,128)(2,1)S(1)}) custom-call(s32[1]{0:T(128)} %bitcast.ctx_ref, bf16[1024,512]{1,0:T(8,128)(2,1)S(1)} %copy-done.2, bf16[1024,512]{1,0:T(8,128)(2,1)S(1)} %copy-done.4, bf16[1024,512]{1,0:T(8,128)(2,1)S(1)} %copy-done.6, ...), custom_call_target="tpu_custom_call" | custom-call | flops 1024 | bytes 1024 | tf_op jit(solution)/shard_map/attend/pallas_call | solution.py:377
  42.7 1.6 %collective-permute-start.3 = (bf16[256,128]{1,0:T(8,128)(2,1)S(1)}, bf16[256,128]{1,0:T(8,128)(2,1)S(1)}, u32[]{:S(2)}, u32[]{:S(2)}) collective-permute-start(bf16[256,128]{1,0:T(8,128)(2,1)S(1)} %get-tuple-element.65), channel_id=1, source_target_pairs={{0,8},{8,0},{16,24},{24,16},{1,9},{9,1},{17,25},{25,17},{2,10},{10... | collective-permute-start | bytes 196616 | tf_op jit(solution)/shard_map/ppermute | solution.py:446
  44.2 0.5 collective-permute-start.4
  44.7 1.1 project.8
  45.8 11.9 %collective-permute-done.3.refs_1_ = bf16[256,128]{1,0:T(8,128)(2,1)S(1)} collective-permute-done((bf16[256,128]{1,0:T(8,128)(2,1)S(1)}, bf16[256,128]{1,0:T(8,128)(2,1)S(1)}, u32[]{:S(2)}, u32[]{:S(2)}) %collective-permute-start.3) | collective-permute-done | bytes 65568 | tf_op jit(solution)/shard_map/ppermute | solution.py:446
  57.7 3.5 %collective-permute-start.14 = (bf16[256,1024]{1,0:T(8,128)(2,1)S(1)}, bf16[256,1024]{1,0:T(8,128)(2,1)S(1)}, u32[]{:S(2)}, u32[]{:S(2)}) collective-permute-start(bf16[256,1024]{1,0:T(8,128)(2,1)S(1)} %project.8), channel_id=1, source_target_pairs={{0,2},{1,3},{6,4},{7,5},{8,10},{9,11},{14,12},{15,13},{16,18},{17,... | collective-permute-start | bytes 1572872 | tf_op jit(solution)/shard_map/ppermute | solution.py:451
  61.2 1.5 collective-permute-start.5
  62.7 3.7 %collective-permute-done.5.refs_3_ = bf16[256,128]{1,0:T(8,128)(2,1)S(1)} collective-permute-done((bf16[256,128]{1,0:T(8,128)(2,1)S(1)}, bf16[256,128]{1,0:T(8,128)(2,1)S(1)}, u32[]{:S(2)}, u32[]{:S(2)}) %collective-permute-start.5) | collective-permute-done | bytes 65568 | tf_op jit(solution)/shard_map/ppermute | solution.py:446
  66.6 1.1 project.9
  67.7 0.4 collective-permute-done.15.sibling_ref
  68.1 1.1 project.11
  69.2 1.3 collective-permute-start.19
  70.5 1.1 project.10
  71.7 1.5 collective-permute-done.14
  73.2 0.2 add_convert_fusion.7
  73.4 0.7 collective-permute-start.20
  74.1 7.8 %attend.5 = (bf16[512,128]{1,0:T(8,128)(2,1)S(1)}, bf16[512,128]{1,0:T(8,128)(2,1)S(1)}, bf16[512,128]{1,0:T(8,128)(2,1)S(1)}, bf16[512,128]{1,0:T(8,128)(2,1)S(1)}) custom-call(s32[1]{0:T(128)} %bitcast.ctx_ref, bf16[1024,512]{1,0:T(8,128)(2,1)S(1)} %copy-done.2, bf16[1024,512]{1,0:T(8,128)(2,1)S(1)} %copy-done.4, bf16[1024,512]{1,0:T(8,128)(2,1)S(1)} %copy-done.6, ...), custom_call_target="tpu_custom_call" | custom-call | flops 1024 | bytes 1024 | tf_op jit(solution)/shard_map/attend/pallas_call | solution.py:377
  81.9 1.6 %collective-permute-start.16 = (bf16[512,128]{1,0:T(8,128)(2,1)S(1)}, bf16[512,128]{1,0:T(8,128)(2,1)S(1)}, u32[]{:S(2)}, u32[]{:S(2)}) collective-permute-start(bf16[512,128]{1,0:T(8,128)(2,1)S(1)} %get-tuple-element.95), channel_id=1, source_target_pairs={{0,8},{8,0},{16,24},{24,16},{1,9},{9,1},{17,25},{25,17},{2,10},{10... | collective-permute-start | bytes 393224 | tf_op jit(solution)/shard_map/ppermute | solution.py:446
  83.5 0.5 collective-permute-start.17
  84.0 1.5 collective-permute-start.18
  85.5 0.2 add_convert_fusion.6
  85.7 2.5 %collective-permute-done.16.refs_1_ = bf16[512,128]{1,0:T(8,128)(2,1)S(1)} collective-permute-done((bf16[512,128]{1,0:T(8,128)(2,1)S(1)}, bf16[512,128]{1,0:T(8,128)(2,1)S(1)}, u32[]{:S(2)}, u32[]{:S(2)}) %collective-permute-start.16) | collective-permute-done | bytes 131104 | tf_op jit(solution)/shard_map/ppermute | solution.py:446
  88.3 2.0 %collective-permute-done.17.refs_2_ = bf16[512,128]{1,0:T(8,128)(2,1)S(1)} collective-permute-done((bf16[512,128]{1,0:T(8,128)(2,1)S(1)}, bf16[512,128]{1,0:T(8,128)(2,1)S(1)}, u32[]{:S(2)}, u32[]{:S(2)}) %collective-permute-start.17) | collective-permute-done | bytes 131104 | tf_op jit(solution)/shard_map/ppermute | solution.py:446
  90.4 1.9 %collective-permute-done.24.sibling_ref = bf16[512,512]{1,0:T(8,128)(2,1)S(1)} collective-permute-done((bf16[512,512]{1,0:T(8,128)(2,1)S(1)}, bf16[512,512]{1,0:T(8,128)(2,1)S(1)}, u32[]{:S(2)}, u32[]{:S(2)}) %collective-permute-start.24) | collective-permute-done | bytes 524320 | tf_op jit(solution)/shard_map/ppermute | solution.py:446
  92.3 0.7 project.15
  93.0 6.8 %collective-permute-start.25 = (bf16[512,512]{1,0:T(8,128)(2,1)S(1)}, bf16[512,512]{1,0:T(8,128)(2,1)S(1)}, u32[]{:S(2)}, u32[]{:S(2)}) collective-permute-start(bf16[512,512]{1,0:T(8,128)(2,1)S(1)} %project.15), channel_id=1, source_target_pairs={{0,2},{1,3},{6,4},{7,5},{8,10},{9,11},{14,12},{15,13},{16,18},{17,... | collective-permute-start | bytes 1572872 | tf_op jit(solution)/shard_map/ppermute | solution.py:451
  99.9 0.7 collective-permute-start.22
  100.6 0.7 project.14
  101.3 10.0 %collective-permute-done.25 = bf16[512,512]{1,0:T(8,128)(2,1)S(1)} collective-permute-done((bf16[512,512]{1,0:T(8,128)(2,1)S(1)}, bf16[512,512]{1,0:T(8,128)(2,1)S(1)}, u32[]{:S(2)}, u32[]{:S(2)}) %collective-permute-start.25) | collective-permute-done | bytes 524320 | tf_op jit(solution)/shard_map/ppermute | solution.py:451
  111.4 4.4 %collective-permute-start.26 = (bf16[512,512]{1,0:T(8,128)(2,1)S(1)}, bf16[512,512]{1,0:T(8,128)(2,1)S(1)}, u32[]{:S(2)}, u32[]{:S(2)}) collective-permute-start(bf16[512,512]{1,0:T(8,128)(2,1)S(1)} %project.14), channel_id=1, source_target_pairs={{0,2},{1,3},{6,4},{7,5},{8,10},{9,11},{14,12},{15,13},{16,18},{17,... | collective-permute-start | bytes 1572872 | tf_op jit(solution)/shard_map/ppermute | solution.py:451
  115.9 1.3 collective-permute-start.21
  117.3 0.7 collective-permute-start.29
  118.0 0.2 add_convert_fusion.5
  118.2 1.3 collective-permute-start.23
  119.5 0.7 project.13
  120.2 8.0 %collective-permute-done.26 = bf16[512,512]{1,0:T(8,128)(2,1)S(1)} collective-permute-done((bf16[512,512]{1,0:T(8,128)(2,1)S(1)}, bf16[512,512]{1,0:T(8,128)(2,1)S(1)}, u32[]{:S(2)}, u32[]{:S(2)}) %collective-permute-start.26) | collective-permute-done | bytes 524320 | tf_op jit(solution)/shard_map/ppermute | solution.py:451
  128.3 0.1 add_convert_fusion.1
  128.5 1.3 collective-permute-start.30
  129.8 0.7 collective-permute-start.28
  130.5 6.9 %collective-permute-start.27 = (bf16[512,512]{1,0:T(8,128)(2,1)S(1)}, bf16[512,512]{1,0:T(8,128)(2,1)S(1)}, u32[]{:S(2)}, u32[]{:S(2)}) collective-permute-start(bf16[512,512]{1,0:T(8,128)(2,1)S(1)} %project.13), channel_id=1, source_target_pairs={{0,2},{1,3},{6,4},{7,5},{8,10},{9,11},{14,12},{15,13},{16,18},{17,... | collective-permute-start | bytes 1572872 | tf_op jit(solution)/shard_map/ppermute | solution.py:451
  137.4 0.7 project.12
  138.1 1.3 collective-permute-done.21
  139.4 0.4 add_convert_fusion.4
  139.8 4.4 %collective-permute-done.30 = bf16[512,512]{1,0:T(8,128)(2,1)S(1)} collective-permute-done((bf16[512,512]{1,0:T(8,128)(2,1)S(1)}, bf16[512,512]{1,0:T(8,128)(2,1)S(1)}, u32[]{:S(2)}, u32[]{:S(2)}) %collective-permute-start.30) | collective-permute-done | bytes 524320 | tf_op jit(solution)/shard_map/ppermute | solution.py:451
  144.2 4.7 %collective-permute-done.27 = bf16[512,512]{1,0:T(8,128)(2,1)S(1)} collective-permute-done((bf16[512,512]{1,0:T(8,128)(2,1)S(1)}, bf16[512,512]{1,0:T(8,128)(2,1)S(1)}, u32[]{:S(2)}, u32[]{:S(2)}) %collective-permute-start.27) | collective-permute-done | bytes 524320 | tf_op jit(solution)/shard_map/ppermute | solution.py:451
  148.9 0.3 add_convert_fusion
  149.2 1.0 pad_maximum_fusion.1
  (46 shorter events, 0.9 us)
Async XLA Ops:
  2.4 13.2 %collective-permute-start = (bf16[1552,128]{1,0:T(8,128)(2,1)}, bf16[1552,128]{1,0:T(8,128)(2,1)S(1)}, u32[]{:S(2)}, u32[]{:S(2)}) collective-permute-start(bf16[1552,128]{1,0:T(8,128)(2,1)} %get-tuple-element.58), channel_id=1, source_target_pairs={{0,8},{8,0},{16,24},{24,16},{1,9},{9,1},{17,25},{25,17},{2,10},{10... | collective-permute-start | bytes 1191944 | tf_op jit(solution)/shard_map/ppermute | solution.py:446
  5.3 19.4 %collective-permute-start.1 = (bf16[1552,128]{1,0:T(8,128)(2,1)}, bf16[1552,128]{1,0:T(8,128)(2,1)S(1)}, u32[]{:S(2)}, u32[]{:S(2)}) collective-permute-start(bf16[1552,128]{1,0:T(8,128)(2,1)} %get-tuple-element.59), channel_id=1, source_target_pairs={{0,16},{8,24},{16,0},{24,8},{1,17},{9,25},{17,1},{25,9},{2,18},{10... | collective-permute-start | bytes 1191944 | tf_op jit(solution)/shard_map/ppermute | solution.py:446
  6.9 17.9 %collective-permute-start.2 = (bf16[1552,128]{1,0:T(8,128)(2,1)}, bf16[1552,128]{1,0:T(8,128)(2,1)S(1)}, u32[]{:S(2)}, u32[]{:S(2)}) collective-permute-start(bf16[1552,128]{1,0:T(8,128)(2,1)} %get-tuple-element.60), channel_id=1, source_target_pairs={{0,24},{8,16},{16,8},{24,0},{1,25},{9,17},{17,9},{25,1},{2,26},{10... | collective-permute-start | bytes 1191944 | tf_op jit(solution)/shard_map/ppermute | solution.py:446
  8.2 16.5 %copy-start.1 = (bf16[1024,512]{1,0:T(8,128)(2,1)S(1)}, bf16[1024,512]{1,0:T(8,128)(2,1)}, u32[]{:S(2)}) copy-start(bf16[1024,512]{1,0:T(8,128)(2,1)} %refs_3_.5) | copy-start | bytes 3145732
  8.2 16.5 %copy-start.3 = (bf16[1024,512]{1,0:T(8,128)(2,1)S(1)}, bf16[1024,512]{1,0:T(8,128)(2,1)}, u32[]{:S(2)}) copy-start(bf16[1024,512]{1,0:T(8,128)(2,1)} %refs_4_.5) | copy-start | bytes 3145732
  8.2 16.5 %copy-start.5 = (bf16[1024,512]{1,0:T(8,128)(2,1)S(1)}, bf16[1024,512]{1,0:T(8,128)(2,1)}, u32[]{:S(2)}) copy-start(bf16[1024,512]{1,0:T(8,128)(2,1)} %refs_5_.5) | copy-start | bytes 3145732
  8.2 16.5 %copy-start.7 = (s32[1024]{0:T(1024)S(1)}, s32[1024]{0:T(1024)}, u32[]{:S(2)}) copy-start(s32[1024]{0:T(1024)} %param.9) | copy-start | bytes 12292
  24.7 19.5 %collective-permute-start.10 = (bf16[512,2048]{1,0:T(8,128)(2,1)}, bf16[512,2048]{1,0:T(8,128)(2,1)S(1)}, u32[]{:S(2)}, u32[]{:S(2)}) collective-permute-start(bf16[512,2048]{1,0:T(8,128)(2,1)} %get-tuple-element.79), channel_id=1, source_target_pairs={{0,1},{1,0},{2,3},{3,2},{4,5},{5,4},{6,7},{7,6},{8,9},{9,8},{10,11... | collective-permute-start | bytes 6291464 | tf_op jit(solution)/shard_map/ppermute | solution.py:446
  28.6 6.0 %collective-permute-start.6 = (bf16[256,128]{1,0:T(8,128)(2,1)S(1)}, bf16[256,128]{1,0:T(8,128)(2,1)S(1)}, u32[]{:S(2)}, u32[]{:S(2)}) collective-permute-start(bf16[256,128]{1,0:T(8,128)(2,1)S(1)} %get-tuple-element.69), channel_id=1, source_target_pairs={{0,8},{8,0},{16,24},{24,16},{1,9},{9,1},{17,25},{25,17},{2,10},{10... | collective-permute-start | bytes 196616 | tf_op jit(solution)/shard_map/ppermute | solution.py:446
  29.9 4.7 %collective-permute-start.7 = (bf16[256,128]{1,0:T(8,128)(2,1)S(1)}, bf16[256,128]{1,0:T(8,128)(2,1)S(1)}, u32[]{:S(2)}, u32[]{:S(2)}) collective-permute-start(bf16[256,128]{1,0:T(8,128)(2,1)S(1)} %get-tuple-element.70), channel_id=1, source_target_pairs={{0,16},{8,24},{16,0},{24,8},{1,17},{9,25},{17,1},{25,9},{2,18},{10... | collective-permute-start | bytes 196616 | tf_op jit(solution)/shard_map/ppermute | solution.py:446
  30.8 8.9 %copy-start.2 = (bf16[1024,512]{1,0:T(8,128)(2,1)S(1)}, bf16[1024,512]{1,0:T(8,128)(2,1)}, u32[]{:S(2)}) copy-start(bf16[1024,512]{1,0:T(8,128)(2,1)} %refs_3_.5) | copy-start | bytes 3145732
  30.8 8.9 %copy-start.4 = (bf16[1024,512]{1,0:T(8,128)(2,1)S(1)}, bf16[1024,512]{1,0:T(8,128)(2,1)}, u32[]{:S(2)}) copy-start(bf16[1024,512]{1,0:T(8,128)(2,1)} %refs_4_.5) | copy-start | bytes 3145732
  30.8 8.9 %copy-start.6 = (bf16[1024,512]{1,0:T(8,128)(2,1)S(1)}, bf16[1024,512]{1,0:T(8,128)(2,1)}, u32[]{:S(2)}) copy-start(bf16[1024,512]{1,0:T(8,128)(2,1)} %refs_5_.5) | copy-start | bytes 3145732
  30.8 5.2 %collective-permute-start.8 = (bf16[256,128]{1,0:T(8,128)(2,1)S(1)}, bf16[256,128]{1,0:T(8,128)(2,1)S(1)}, u32[]{:S(2)}, u32[]{:S(2)}) collective-permute-start(bf16[256,128]{1,0:T(8,128)(2,1)S(1)} %get-tuple-element.71), channel_id=1, source_target_pairs={{0,24},{8,16},{16,8},{24,0},{1,25},{9,17},{17,9},{25,1},{2,26},{10... | collective-permute-start | bytes 196616 | tf_op jit(solution)/shard_map/ppermute | solution.py:446
  36.0 8.8 %copy-start = (bf16[512,2048]{1,0:T(8,128)(2,1)S(1)}, bf16[512,2048]{1,0:T(8,128)(2,1)}, u32[]{:S(2)}) copy-start(bf16[512,2048]{1,0:T(8,128)(2,1)} %get-tuple-element.78.w_mine_ref) | copy-start | bytes 6291460
  36.0 6.7 %collective-permute-start.9 = (bf16[256,512]{1,0:T(8,128)(2,1)S(1)}, bf16[256,512]{1,0:T(8,128)(2,1)S(1)}, u32[]{:S(2)}, u32[]{:S(2)}) collective-permute-start(bf16[256,512]{1,0:T(8,128)(2,1)S(1)} %assemble.3.mine_ref), channel_id=1, source_target_pairs={{0,1},{1,0},{2,3},{3,2},{4,5},{5,4},{6,7},{7,6},{8,9},{9,8},{10,11... | collective-permute-start | bytes 786440 | tf_op jit(solution)/shard_map/ppermute | solution.py:446
  36.1 30.4 %collective-permute-start.11 = (bf16[1536,128]{1,0:T(8,128)(2,1)}, bf16[1536,128]{1,0:T(8,128)(2,1)S(1)}, u32[]{:S(2)}, u32[]{:S(2)}) collective-permute-start(bf16[1536,128]{1,0:T(8,128)(2,1)} %get-tuple-element.80), channel_id=1, source_target_pairs={{0,8},{8,0},{16,24},{24,16},{1,9},{9,1},{17,25},{25,17},{2,10},{10... | collective-permute-start | bytes 1179656 | tf_op jit(solution)/shard_map/ppermute | solution.py:446
  37.6 28.8 %collective-permute-start.12 = (bf16[1536,128]{1,0:T(8,128)(2,1)}, bf16[1536,128]{1,0:T(8,128)(2,1)S(1)}, u32[]{:S(2)}, u32[]{:S(2)}) collective-permute-start(bf16[1536,128]{1,0:T(8,128)(2,1)} %get-tuple-element.81), channel_id=1, source_target_pairs={{0,16},{8,24},{16,0},{24,8},{1,17},{9,25},{17,1},{25,9},{2,18},{10... | collective-permute-start | bytes 1179656 | tf_op jit(solution)/shard_map/ppermute | solution.py:446
  38.1 28.3 %collective-permute-start.13 = (bf16[1536,128]{1,0:T(8,128)(2,1)}, bf16[1536,128]{1,0:T(8,128)(2,1)S(1)}, u32[]{:S(2)}, u32[]{:S(2)}) collective-permute-start(bf16[1536,128]{1,0:T(8,128)(2,1)} %get-tuple-element.82), channel_id=1, source_target_pairs={{0,24},{8,16},{16,8},{24,0},{1,25},{9,17},{17,9},{25,1},{2,26},{10... | collective-permute-start | bytes 1179656 | tf_op jit(solution)/shard_map/ppermute | solution.py:446
  42.7 15.0 %collective-permute-start.3 = (bf16[256,128]{1,0:T(8,128)(2,1)S(1)}, bf16[256,128]{1,0:T(8,128)(2,1)S(1)}, u32[]{:S(2)}, u32[]{:S(2)}) collective-permute-start(bf16[256,128]{1,0:T(8,128)(2,1)S(1)} %get-tuple-element.65), channel_id=1, source_target_pairs={{0,8},{8,0},{16,24},{24,16},{1,9},{9,1},{17,25},{25,17},{2,10},{10... | collective-permute-start | bytes 196616 | tf_op jit(solution)/shard_map/ppermute | solution.py:446
  44.2 17.0 %collective-permute-start.4 = (bf16[256,128]{1,0:T(8,128)(2,1)S(1)}, bf16[256,128]{1,0:T(8,128)(2,1)S(1)}, u32[]{:S(2)}, u32[]{:S(2)}) collective-permute-start(bf16[256,128]{1,0:T(8,128)(2,1)S(1)} %get-tuple-element.66), channel_id=1, source_target_pairs={{0,16},{8,24},{16,0},{24,8},{1,17},{9,25},{17,1},{25,9},{2,18},{10... | collective-permute-start | bytes 196616 | tf_op jit(solution)/shard_map/ppermute | solution.py:446
  57.7 15.5 %collective-permute-start.14 = (bf16[256,1024]{1,0:T(8,128)(2,1)S(1)}, bf16[256,1024]{1,0:T(8,128)(2,1)S(1)}, u32[]{:S(2)}, u32[]{:S(2)}) collective-permute-start(bf16[256,1024]{1,0:T(8,128)(2,1)S(1)} %project.8), channel_id=1, source_target_pairs={{0,2},{1,3},{6,4},{7,5},{8,10},{9,11},{14,12},{15,13},{16,18},{17,... | collective-permute-start | bytes 1572872 | tf_op jit(solution)/shard_map/ppermute | solution.py:451
  61.2 5.2 %collective-permute-start.5 = (bf16[256,128]{1,0:T(8,128)(2,1)S(1)}, bf16[256,128]{1,0:T(8,128)(2,1)S(1)}, u32[]{:S(2)}, u32[]{:S(2)}) collective-permute-start(bf16[256,128]{1,0:T(8,128)(2,1)S(1)} %get-tuple-element.67), channel_id=1, source_target_pairs={{0,24},{8,16},{16,8},{24,0},{1,25},{9,17},{17,9},{25,1},{2,26},{10... | collective-permute-start | bytes 196616 | tf_op jit(solution)/shard_map/ppermute | solution.py:446
  66.5 1.6 %collective-permute-start.15 = (bf16[256,512]{1,0:T(8,128)(2,1)S(1)}, bf16[256,512]{1,0:T(8,128)(2,1)S(1)}, u32[]{:S(2)}, u32[]{:S(2)}) collective-permute-start(bf16[256,512]{1,0:T(8,128)(2,1)S(1)} %assemble.4.mine_ref), channel_id=1, source_target_pairs={{0,1},{1,0},{2,3},{3,2},{4,5},{5,4},{6,7},{7,6},{8,9},{9,8},{10,11... | collective-permute-start | bytes 786440 | tf_op jit(solution)/shard_map/ppermute | solution.py:446
  69.2 16.3 %collective-permute-start.19 = (bf16[256,1024]{1,0:T(8,128)(2,1)S(1)}, bf16[256,1024]{1,0:T(8,128)(2,1)S(1)}, u32[]{:S(2)}, u32[]{:S(2)}) collective-permute-start(bf16[256,1024]{1,0:T(8,128)(2,1)S(1)} %project.11), channel_id=1, source_target_pairs={{0,2},{1,3},{6,4},{7,5},{8,10},{9,11},{14,12},{15,13},{16,18},{17,... | collective-permute-start | bytes 1572872 | tf_op jit(solution)/shard_map/ppermute | solution.py:451
  73.4 16.8 %collective-permute-start.20 = (bf16[256,1024]{1,0:T(8,128)(2,1)S(1)}, bf16[256,1024]{1,0:T(8,128)(2,1)S(1)}, u32[]{:S(2)}, u32[]{:S(2)}) collective-permute-start(bf16[256,1024]{1,0:T(8,128)(2,1)S(1)} %add_convert_fusion.7), channel_id=1, source_target_pairs={{2,4},{3,5},{4,2},{5,3},{10,12},{11,13},{12,10},{13,11},{18,20},{1... | collective-permute-start | bytes 1572872 | tf_op jit(solution)/shard_map/ppermute | solution.py:451
  81.9 6.3 %collective-permute-start.16 = (bf16[512,128]{1,0:T(8,128)(2,1)S(1)}, bf16[512,128]{1,0:T(8,128)(2,1)S(1)}, u32[]{:S(2)}, u32[]{:S(2)}) collective-permute-start(bf16[512,128]{1,0:T(8,128)(2,1)S(1)} %get-tuple-element.95), channel_id=1, source_target_pairs={{0,8},{8,0},{16,24},{24,16},{1,9},{9,1},{17,25},{25,17},{2,10},{10... | collective-permute-start | bytes 393224 | tf_op jit(solution)/shard_map/ppermute | solution.py:446
  83.5 6.8 %collective-permute-start.17 = (bf16[512,128]{1,0:T(8,128)(2,1)S(1)}, bf16[512,128]{1,0:T(8,128)(2,1)S(1)}, u32[]{:S(2)}, u32[]{:S(2)}) collective-permute-start(bf16[512,128]{1,0:T(8,128)(2,1)S(1)} %get-tuple-element.96), channel_id=1, source_target_pairs={{0,16},{8,24},{16,0},{24,8},{1,17},{9,25},{17,1},{25,9},{2,18},{10... | collective-permute-start | bytes 393224 | tf_op jit(solution)/shard_map/ppermute | solution.py:446
  84.0 6.3 %collective-permute-start.18 = (bf16[512,128]{1,0:T(8,128)(2,1)S(1)}, bf16[512,128]{1,0:T(8,128)(2,1)S(1)}, u32[]{:S(2)}, u32[]{:S(2)}) collective-permute-start(bf16[512,128]{1,0:T(8,128)(2,1)S(1)} %get-tuple-element.97), channel_id=1, source_target_pairs={{0,24},{8,16},{16,8},{24,0},{1,25},{9,17},{17,9},{25,1},{2,26},{10... | collective-permute-start | bytes 393224 | tf_op jit(solution)/shard_map/ppermute | solution.py:446
  90.4 2.0 %collective-permute-start.24 = (bf16[512,512]{1,0:T(8,128)(2,1)S(1)}, bf16[512,512]{1,0:T(8,128)(2,1)S(1)}, u32[]{:S(2)}, u32[]{:S(2)}) collective-permute-start(bf16[512,512]{1,0:T(8,128)(2,1)S(1)} %assemble.5.mine_ref), channel_id=1, source_target_pairs={{0,1},{1,0},{2,3},{3,2},{4,5},{5,4},{6,7},{7,6},{8,9},{9,8},{10,11... | collective-permute-start | bytes 1572872 | tf_op jit(solution)/shard_map/ppermute | solution.py:446
  93.0 18.2 %collective-permute-start.25 = (bf16[512,512]{1,0:T(8,128)(2,1)S(1)}, bf16[512,512]{1,0:T(8,128)(2,1)S(1)}, u32[]{:S(2)}, u32[]{:S(2)}) collective-permute-start(bf16[512,512]{1,0:T(8,128)(2,1)S(1)} %project.15), channel_id=1, source_target_pairs={{0,2},{1,3},{6,4},{7,5},{8,10},{9,11},{14,12},{15,13},{16,18},{17,... | collective-permute-start | bytes 1572872 | tf_op jit(solution)/shard_map/ppermute | solution.py:451
  99.9 17.4 %collective-permute-start.22 = (bf16[256,1024]{1,0:T(8,128)(2,1)S(1)}, bf16[256,1024]{1,0:T(8,128)(2,1)S(1)}, u32[]{:S(2)}, u32[]{:S(2)}) collective-permute-start(bf16[256,1024]{1,0:T(8,128)(2,1)S(1)} %add_convert_fusion.6), channel_id=1, source_target_pairs={{2,4},{3,5},{4,2},{5,3},{10,12},{11,13},{12,10},{13,11},{18,20},{1... | collective-permute-start | bytes 1572872 | tf_op jit(solution)/shard_map/ppermute | solution.py:451
  111.4 16.8 %collective-permute-start.26 = (bf16[512,512]{1,0:T(8,128)(2,1)S(1)}, bf16[512,512]{1,0:T(8,128)(2,1)S(1)}, u32[]{:S(2)}, u32[]{:S(2)}) collective-permute-start(bf16[512,512]{1,0:T(8,128)(2,1)S(1)} %project.14), channel_id=1, source_target_pairs={{0,2},{1,3},{6,4},{7,5},{8,10},{9,11},{14,12},{15,13},{16,18},{17,... | collective-permute-start | bytes 1572872 | tf_op jit(solution)/shard_map/ppermute | solution.py:451
  115.9 23.6 %collective-permute-start.21 = (bf16[512,512]{1,0:T(8,128)(2,1)S(1)}, bf16[512,512]{1,0:T(8,128)(2,1)S(1)}, u32[]{:S(2)}, u32[]{:S(2)}) collective-permute-start(bf16[512,512]{1,0:T(8,128)(2,1)S(1)} %slice.14), channel_id=1, source_target_pairs={{0,2},{1,3},{6,4},{7,5},{8,10},{9,11},{14,12},{15,13},{16,18},{17,... | collective-permute-start | bytes 1572872 | tf_op jit(solution)/shard_map/ppermute | solution.py:451
  117.3 11.0 %collective-permute-start.29 = (bf16[512,512]{1,0:T(8,128)(2,1)S(1)}, bf16[512,512]{1,0:T(8,128)(2,1)S(1)}, u32[]{:S(2)}, u32[]{:S(2)}) collective-permute-start(bf16[512,512]{1,0:T(8,128)(2,1)S(1)} %add_convert_fusion.3), channel_id=1, source_target_pairs={{2,4},{3,5},{4,2},{5,3},{10,12},{11,13},{12,10},{13,11},{18,20},{1... | collective-permute-start | bytes 1572872 | tf_op jit(solution)/shard_map/ppermute | solution.py:451
  118.2 21.2 %collective-permute-start.23 = (bf16[512,512]{1,0:T(8,128)(2,1)S(1)}, bf16[512,512]{1,0:T(8,128)(2,1)S(1)}, u32[]{:S(2)}, u32[]{:S(2)}) collective-permute-start(bf16[512,512]{1,0:T(8,128)(2,1)S(1)} %add_convert_fusion.5), channel_id=1, source_target_pairs={{4,6},{5,7},{2,0},{3,1},{12,14},{13,15},{10,8},{11,9},{20,22},{21,... | collective-permute-start | bytes 1572872 | tf_op jit(solution)/shard_map/ppermute | solution.py:451
  128.5 15.7 %collective-permute-start.30 = (bf16[512,512]{1,0:T(8,128)(2,1)S(1)}, bf16[512,512]{1,0:T(8,128)(2,1)S(1)}, u32[]{:S(2)}, u32[]{:S(2)}) collective-permute-start(bf16[512,512]{1,0:T(8,128)(2,1)S(1)} %add_convert_fusion.1), channel_id=1, source_target_pairs={{4,6},{5,7},{2,0},{3,1},{12,14},{13,15},{10,8},{11,9},{20,22},{21,... | collective-permute-start | bytes 1572872 | tf_op jit(solution)/shard_map/ppermute | solution.py:451
  129.8 14.4 %collective-permute-start.28 = (bf16[512,512]{1,0:T(8,128)(2,1)S(1)}, bf16[512,512]{1,0:T(8,128)(2,1)S(1)}, u32[]{:S(2)}, u32[]{:S(2)}) collective-permute-start(bf16[512,512]{1,0:T(8,128)(2,1)S(1)} %add_convert_fusion.2), channel_id=1, source_target_pairs={{2,4},{3,5},{4,2},{5,3},{10,12},{11,13},{12,10},{13,11},{18,20},{1... | collective-permute-start | bytes 1572872 | tf_op jit(solution)/shard_map/ppermute | solution.py:451
  130.5 18.4 %collective-permute-start.27 = (bf16[512,512]{1,0:T(8,128)(2,1)S(1)}, bf16[512,512]{1,0:T(8,128)(2,1)S(1)}, u32[]{:S(2)}, u32[]{:S(2)}) collective-permute-start(bf16[512,512]{1,0:T(8,128)(2,1)S(1)} %project.13), channel_id=1, source_target_pairs={{0,2},{1,3},{6,4},{7,5},{8,10},{9,11},{14,12},{15,13},{16,18},{17,... | collective-permute-start | bytes 1572872 | tf_op jit(solution)/shard_map/ppermute | solution.py:451

commit v3 on v2

--- a/solution.py
+++ b/solution.py
@@ -487,62 +487,53 @@
     low, w_give = tie(low, w_give)
     w_sibling = swap(w_give, "head", 1)
     high_out = pack(ctx_index, 1, queries, keys, values, None)
-
-    def attend_rows(high, tiles):
-        return attend(ctx_index, queries, keys, values, docs, low, high, tiles)
+    tiles = tuple(range(shard_rows // 2 // TILE))
 
     def send_back(pieces):
         return [swap(pieces[distance], "ctx", distance) for distance in near]
 
-    def share_of(mine, sibling, first, count):
-        return project(mine, sibling, w_mine, w_sibling, first, count, chips)
-
-    pieces = attend_rows(None, (0,))
+    def share_of(mine, sibling, turn):
+        return project(mine, sibling, w_mine, w_sibling, turn, 1, chips)
+
+    pieces = attend(ctx_index, queries, keys, values, docs, low, None, tiles)
     back = send_back(pieces)
     pieces, high_out = tie(pieces, high_out)
     high = [swap(high_out[0], "ctx", 1), swap(high_out[1], "ctx", 2)]
-    mine = [assemble(ctx_index, [pieces[0], *back])]
-    mine[0], diagonal_out = tie(mine[0], high_out[2])
+    mine = assemble(ctx_index, [pieces[0], *back])
+    mine, diagonal_out = tie(mine, high_out[2])
     high.append(swap(diagonal_out, "ctx", 3))
-    sibling = [swap(mine[0], "head", 1)]
-    shares = [share_of(mine[0], sibling[0], 0, 2)]
+    sibling = swap(mine, "head", 1)
+    shares = [share_of(mine, sibling, turn) for turn in range(chips)]
     end = [between_chips(shares[0], TO_MIDDLE)]
-
-    pieces = attend_rows(None, tuple(range(1, shard_rows // 2 // TILE)))
-    back = send_back(pieces)
-    back, shares, high = tie(back, shares, high)
-    mine.append(assemble(ctx_index, [pieces[0], *back]))
-    sibling.append(swap(mine[1], "head", 1))
-    shares.append(share_of(mine[1], sibling[1], 0, 2))
+    end[0], shares[1] = tie(end[0], shares[1])
     end.append(between_chips(shares[1], TO_MIDDLE))
-    rest = [share_of(mine[turn], sibling[turn], 2, 2) for turn in range(2)]
-    rest = jnp.concatenate(rest, axis=0)
     passed = add(shares[0], end[0])
 
-    high, passed, rest, shares = tie(high, passed, rest, shares)
+    high, passed, shares[1:] = tie(high, passed, shares[1:])
     across = [between_chips(passed, ACROSS)]
-    pieces = attend_rows(high, tuple(range(shard_rows // 2 // TILE)))
+    pieces = attend(ctx_index, queries, keys, values, docs, low, high, tiles)
     back = send_back(pieces)
     passed = add(shares[1], end[1])
-    back, passed, kept, across[0] = tie(back, passed, rest[:, :columns], across[0])
+    back, passed, shares[2] = tie(back, passed, shares[2])
     across.append(between_chips(passed, ACROSS))
-    end_low = between_chips(kept, TO_MIDDLE)
-    mine_high = assemble(ctx_index, [pieces[0], *back])
-    sibling_high = swap(mine_high, "head", 1)
-    late = [share_of(mine_high, sibling_high, turn, 1) for turn in range(4)]
+    end.append(between_chips(shares[2], TO_MIDDLE))
+    mine = assemble(ctx_index, [pieces[0], *back])
+    mine, across[0] = tie(mine, across[0])
+    sibling = swap(mine, "head", 1)
+    outer = between_chips(add(shares[2], across[0]), TO_ENDS)
+    late = [share_of(mine, sibling, turn) for turn in range(chips)]
+    late[0], end[2] = tie(late[0], end[2])
     end_high = [between_chips(late[0], TO_MIDDLE)]
-    across_low = jnp.concatenate(across, axis=0)
-    outer_low = between_chips(add(rest[:, :columns], across_low[:, :columns]), TO_ENDS)
     passed = add(late[0], end_high[0])
-    late[1], passed = tie(late[1], passed)
+    late[1], passed, across[1], outer = tie(late[1], passed, across[1], outer)
     across_high = [between_chips(passed, ACROSS)]
     end_high.append(between_chips(late[1], TO_MIDDLE))
+    first = add(shares[3], end[2], across[1], outer)
     passed = add(late[1], end_high[1])
-    late[2], passed = tie(late[2], passed)
+    late[2], passed, first = tie(late[2], passed, first)
     across_high.append(between_chips(passed, ACROSS))
     end_high.append(between_chips(late[2], TO_MIDDLE))
     outer_high = between_chips(add(late[2], across_high[0]), TO_ENDS)
-    first = add(rest[:, columns:], end_low, across_low[:, columns:], outer_low)
     second = add(late[3], end_high[2], across_high[1], outer_high)
     return jnp.concatenate([first, second], axis=0)
 

time: 152 us -> 161 us (1.059); the launches traced: 150 us -> 161 us
  Pallas kernels: 32.6 us -> 38.4 us
  waiting for transfers between devices: 64.4 us -> 69.3 us
    ppermute x12, waiting for transfers between devices: 29.9 us -> 45.7 us  [between_chips(): return lax.ppermute(value, 'head', both)]
    ppermute x19 -> x15, waiting for transfers between devices: 34.6 us -> 23.5 us  [swap(): lax.ppermute(value, axis, [(source, source ^ distance) for source in rang...]
    pallas_call x3 -> x2, Pallas kernels: 14.7 us -> 21.9 us  [attend(): pl.pallas_call(kernel, grid_spec=pltpu.PrefetchScalarGridSpec(num_scalar_...]
    ppermute x12, starting transfers between devices: 29.7 us -> 34 us  [between_chips(): return lax.ppermute(value, 'head', both)]
    ppermute x19 -> x15, starting transfers between devices: 18.9 us -> 15.2 us  [swap(): lax.ppermute(value, axis, [(source, source ^ distance) for source in rang...]
  transfers between devices with their start and end apart: 31 -> 27, of which waited for: 15 -> 16; matrix products, arithmetic and copies ran while one was open for 2% -> 2% of each run, Pallas kernels for 20% -> 22%
where the time goes in v3:
time: 161 us
  waiting for transfers between devices  69.3 us (43%)
  starting transfers between devices  49.2 us (31%)
  Pallas kernels  38.4 us (24%)
  other arithmetic  3.1 us (2%)
    ppermute x12, waiting for transfers between devices, between_chips(): return lax.ppermute(value, 'head', both)  45.7 us
    ppermute x12, starting transfers between devices, between_chips(): return lax.ppermute(value, 'head', both)  34 us
    ppermute x15, waiting for transfers between devices, swap(): lax.ppermute(value, axis, [(source, source ^ distance) for source in rang...  23.5 us
    pallas_call x2, Pallas kernels, attend(): pl.pallas_call(kernel, grid_spec=pltpu.PrefetchScalarGridSpec(num_scalar_...  21.9 us
    ppermute x15, starting transfers between devices, swap(): lax.ppermute(value, axis, [(source, source ^ distance) for source in rang...  15.2 us
    pallas_call x1, Pallas kernels, pack_projection(): pl.pallas_call(kernel, grid_spec=pltpu.PrefetchScalarGridSpec(num_scalar_...  5.69 us
    pallas_call x8, Pallas kernels, project(): pl.pallas_call(kernel, grid=(count,), in_specs=[attended, attended, weigh...  5.66 us
    pallas_call x2, Pallas kernels, pack(): pl.pallas_call(kernel, grid_spec=pltpu.PrefetchScalarGridSpec(num_scalar_...  4.94 us
  transfers between devices with their start and end apart: 27, of which 16 were waited for; matrix products, arithmetic and copies ran while one was open for 2% of the time, Pallas kernels for 22%

profile of v3, /device:TPU:0, one launch (start us, length us, event | category | flops | bytes accessed | tf_op | source)
XLA Modules:
  0.0 161.0 jit_solution(12632761514335445649)
XLA Ops:
  0.0 2.4 %pack.2 = (bf16[1552,128]{1,0:T(8,128)(2,1)}, bf16[1552,128]{1,0:T(8,128)(2,1)}, bf16[1552,128]{1,0:T(8,128)(2,1)}) custom-call(s32[1]{0:T(128)} %bitcast.ctx_ref, bf16[1024,512]{1,0:T(8,128)(2,1)} %refs_3_.5, bf16[1024,512]{1,0:T(8,128)(2,1)} %refs_4_.5, bf16[1024,512]{1,0:T(8,128)(2,1)} %refs_5_.5, bf16[1024,512]{1,0:T(8,128)(2,1)} %refs_3_.5, ...), custom_call_target="tpu_custom_call" | custom-call | flops 1024 | bytes 1024 | tf_op jit(solution)/shard_map/pack/pallas_call | solution.py:196
  2.4 2.9 %collective-permute-start = (bf16[1552,128]{1,0:T(8,128)(2,1)}, bf16[1552,128]{1,0:T(8,128)(2,1)S(1)}, u32[]{:S(2)}, u32[]{:S(2)}) collective-permute-start(bf16[1552,128]{1,0:T(8,128)(2,1)} %get-tuple-element.56), channel_id=1, source_target_pairs={{0,8},{8,0},{16,24},{24,16},{1,9},{9,1},{17,25},{25,17},{2,10},{10... | collective-permute-start | bytes 1191944 | tf_op jit(solution)/shard_map/ppermute | solution.py:446
  5.3 1.5 collective-permute-start.1
  6.9 0.7 dynamic-slice_bitcast_fusion
  7.6 0.7 pad_add_fusion.places_ref
  8.2 5.7 %pack_projection.1 = (bf16[512,2048]{1,0:T(8,128)(2,1)}, bf16[512,2048]{1,0:T(8,128)(2,1)}) custom-call(s32[5]{0:T(128)} %pad_add_fusion.places_ref, bf16[512,4096]{1,0:T(8,128)(2,1)} %give_in.1, bf16[512,4096]{1,0:T(8,128)(2,1)} %give_in.1), custom_call_target="tpu_custom_call" | custom-call | flops 1024 | bytes 1024 | tf_op jit(solution)/shard_map/pack_projection/pallas_call | solution.py:227
  13.9 1.7 %collective-permute-done.refs_4_.refs_7_ = bf16[1552,128]{1,0:T(8,128)(2,1)S(1)} collective-permute-done((bf16[1552,128]{1,0:T(8,128)(2,1)}, bf16[1552,128]{1,0:T(8,128)(2,1)S(1)}, u32[]{:S(2)}, u32[]{:S(2)}) %collective-permute-start) | collective-permute-done | bytes 397344 | tf_op jit(solution)/shard_map/ppermute | solution.py:446
  15.6 9.1 %collective-permute-done.1.refs_5_.refs_8_ = bf16[1552,128]{1,0:T(8,128)(2,1)S(1)} collective-permute-done((bf16[1552,128]{1,0:T(8,128)(2,1)}, bf16[1552,128]{1,0:T(8,128)(2,1)S(1)}, u32[]{:S(2)}, u32[]{:S(2)}) %collective-permute-start.1) | collective-permute-done | bytes 397344 | tf_op jit(solution)/shard_map/ppermute | solution.py:446
  24.8 9.1 %attend.2 = (bf16[512,128]{1,0:T(8,128)(2,1)S(1)}, bf16[512,128]{1,0:T(8,128)(2,1)}, bf16[512,128]{1,0:T(8,128)(2,1)}, bf16[512,128]{1,0:T(8,128)(2,1)}) custom-call(s32[1]{0:T(128)} %bitcast.ctx_ref, bf16[1024,512]{1,0:T(8,128)(2,1)S(1)} %copy-done.1, bf16[1024,512]{1,0:T(8,128)(2,1)S(1)} %copy-done.3, bf16[1024,512]{1,0:T(8,128)(2,1)S(1)} %copy-done.5, ...), custom_call_target="tpu_custom_call" | custom-call | flops 1024 | bytes 1024 | tf_op jit(solution)/shard_map/attend/pallas_call | solution.py:377
  33.8 1.3 collective-permute-start.5
  35.2 0.7 collective-permute-start.6
  35.9 1.4 collective-permute-start.7
  37.3 2.5 %pack.3 = (bf16[1536,128]{1,0:T(8,128)(2,1)}, bf16[1536,128]{1,0:T(8,128)(2,1)}, bf16[1536,128]{1,0:T(8,128)(2,1)}) custom-call(s32[1]{0:T(128)} %bitcast.ctx_ref, bf16[1024,512]{1,0:T(8,128)(2,1)} %refs_3_.5, bf16[1024,512]{1,0:T(8,128)(2,1)} %refs_4_.5, bf16[1024,512]{1,0:T(8,128)(2,1)} %refs_5_.5, bf16[1024,512]{1,0:T(8,128)(2,1)} %refs_3_.5, ...), custom_call_target="tpu_custom_call" | custom-call | flops 1024 | bytes 1024 | tf_op jit(solution)/shard_map/pack/pallas_call | solution.py:196
  39.9 0.5 collective-permute-done.5.refs_1_
  40.4 1.8 %collective-permute-done.6.refs_2_ = bf16[512,128]{1,0:T(8,128)(2,1)S(1)} collective-permute-done((bf16[512,128]{1,0:T(8,128)(2,1)}, bf16[512,128]{1,0:T(8,128)(2,1)S(1)}, u32[]{:S(2)}, u32[]{:S(2)}) %collective-permute-start.6) | collective-permute-done | bytes 131104 | tf_op jit(solution)/shard_map/ppermute | solution.py:446
  42.2 1.6 %collective-permute-done.7.refs_3_ = bf16[512,128]{1,0:T(8,128)(2,1)S(1)} collective-permute-done((bf16[512,128]{1,0:T(8,128)(2,1)}, bf16[512,128]{1,0:T(8,128)(2,1)S(1)}, u32[]{:S(2)}, u32[]{:S(2)}) %collective-permute-start.7) | collective-permute-done | bytes 131104 | tf_op jit(solution)/shard_map/ppermute | solution.py:446
  43.8 0.1 assemble.2.mine_ref
  44.0 1.9 %collective-permute-done.9.sibling_ref = bf16[512,512]{1,0:T(8,128)(2,1)S(1)} collective-permute-done((bf16[512,512]{1,0:T(8,128)(2,1)S(1)}, bf16[512,512]{1,0:T(8,128)(2,1)S(1)}, u32[]{:S(2)}, u32[]{:S(2)}) %collective-permute-start.9) | collective-permute-done | bytes 524320 | tf_op jit(solution)/shard_map/ppermute | solution.py:446
  45.9 0.7 project.8
  46.6 3.5 %collective-permute-start.11 = (bf16[512,512]{1,0:T(8,128)(2,1)S(1)}, bf16[512,512]{1,0:T(8,128)(2,1)S(1)}, u32[]{:S(2)}, u32[]{:S(2)}) collective-permute-start(bf16[512,512]{1,0:T(8,128)(2,1)S(1)} %project.8), channel_id=1, source_target_pairs={{0,2},{1,3},{6,4},{7,5},{8,10},{9,11},{14,12},{15,13},{16,18},{17,... | collective-permute-start | bytes 1572872 | tf_op jit(solution)/shard_map/ppermute | solution.py:451
  50.2 0.8 collective-permute-start.3
  50.9 1.5 collective-permute-start.4
  52.4 1.3 collective-permute-start.8
  53.7 0.7 project.9
  54.4 7.1 %collective-permute-done.11 = bf16[512,512]{1,0:T(8,128)(2,1)S(1)} collective-permute-done((bf16[512,512]{1,0:T(8,128)(2,1)S(1)}, bf16[512,512]{1,0:T(8,128)(2,1)S(1)}, u32[]{:S(2)}, u32[]{:S(2)}) %collective-permute-start.11) | collective-permute-done | bytes 524320 | tf_op jit(solution)/shard_map/ppermute | solution.py:451
  61.6 4.4 %collective-permute-start.15 = (bf16[512,512]{1,0:T(8,128)(2,1)S(1)}, bf16[512,512]{1,0:T(8,128)(2,1)S(1)}, u32[]{:S(2)}, u32[]{:S(2)}) collective-permute-start(bf16[512,512]{1,0:T(8,128)(2,1)S(1)} %project.9), channel_id=1, source_target_pairs={{0,2},{1,3},{6,4},{7,5},{8,10},{9,11},{14,12},{15,13},{16,18},{17,... | collective-permute-start | bytes 1572872 | tf_op jit(solution)/shard_map/ppermute | solution.py:451
  66.0 0.7 project.11
  66.7 0.7 project.10
  67.5 0.1 add_convert_fusion.7
  67.6 2.3 %collective-permute-done.4.refs_11_ = bf16[1536,128]{1,0:T(8,128)(2,1)S(1)} collective-permute-done((bf16[1536,128]{1,0:T(8,128)(2,1)S(1)}, bf16[1536,128]{1,0:T(8,128)(2,1)S(1)}, u32[]{:S(2)}, u32[]{:S(2)}) %collective-permute-start.4) | collective-permute-done | bytes 393248 | tf_op jit(solution)/shard_map/ppermute | solution.py:446
  69.9 0.7 collective-permute-start.16
  70.7 12.8 %attend.3 = (bf16[512,128]{1,0:T(8,128)(2,1)S(1)}, bf16[512,128]{1,0:T(8,128)(2,1)S(1)}, bf16[512,128]{1,0:T(8,128)(2,1)S(1)}, bf16[512,128]{1,0:T(8,128)(2,1)S(1)}) custom-call(s32[1]{0:T(128)} %bitcast.ctx_ref, bf16[1024,512]{1,0:T(8,128)(2,1)S(1)} %copy-done.2, bf16[1024,512]{1,0:T(8,128)(2,1)S(1)} %copy-done.4, bf16[1024,512]{1,0:T(8,128)(2,1)S(1)} %copy-done.6, ...), custom_call_target="tpu_custom_call" | custom-call | flops 1024 | bytes 1024 | tf_op jit(solution)/shard_map/attend/pallas_call | solution.py:377
  83.5 1.4 collective-permute-start.12
  84.9 0.7 collective-permute-start.13
  85.6 1.4 collective-permute-start.14
  87.0 0.1 add_convert_fusion.6
  87.2 2.6 %collective-permute-done.12.refs_1_ = bf16[512,128]{1,0:T(8,128)(2,1)S(1)} collective-permute-done((bf16[512,128]{1,0:T(8,128)(2,1)S(1)}, bf16[512,128]{1,0:T(8,128)(2,1)S(1)}, u32[]{:S(2)}, u32[]{:S(2)}) %collective-permute-start.12) | collective-permute-done | bytes 131104 | tf_op jit(solution)/shard_map/ppermute | solution.py:446
  89.7 2.0 %collective-permute-done.13.refs_2_ = bf16[512,128]{1,0:T(8,128)(2,1)S(1)} collective-permute-done((bf16[512,128]{1,0:T(8,128)(2,1)S(1)}, bf16[512,128]{1,0:T(8,128)(2,1)S(1)}, u32[]{:S(2)}, u32[]{:S(2)}) %collective-permute-start.13) | collective-permute-done | bytes 131104 | tf_op jit(solution)/shard_map/ppermute | solution.py:446
  91.9 4.6 %collective-permute-start.18 = (bf16[512,512]{1,0:T(8,128)(2,1)S(1)}, bf16[512,512]{1,0:T(8,128)(2,1)S(1)}, u32[]{:S(2)}, u32[]{:S(2)}) collective-permute-start(bf16[512,512]{1,0:T(8,128)(2,1)S(1)} %project.10), channel_id=1, source_target_pairs={{0,2},{1,3},{6,4},{7,5},{8,10},{9,11},{14,12},{15,13},{16,18},{17,... | collective-permute-start | bytes 1572872 | tf_op jit(solution)/shard_map/ppermute | solution.py:451
  96.5 0.7 project.14
  97.2 10.9 %collective-permute-done.18 = bf16[512,512]{1,0:T(8,128)(2,1)S(1)} collective-permute-done((bf16[512,512]{1,0:T(8,128)(2,1)S(1)}, bf16[512,512]{1,0:T(8,128)(2,1)S(1)}, u32[]{:S(2)}, u32[]{:S(2)}) %collective-permute-start.18) | collective-permute-done | bytes 524320 | tf_op jit(solution)/shard_map/ppermute | solution.py:451
  108.1 4.4 %collective-permute-start.19 = (bf16[512,512]{1,0:T(8,128)(2,1)S(1)}, bf16[512,512]{1,0:T(8,128)(2,1)S(1)}, u32[]{:S(2)}, u32[]{:S(2)}) collective-permute-start(bf16[512,512]{1,0:T(8,128)(2,1)S(1)} %project.14), channel_id=1, source_target_pairs={{0,2},{1,3},{6,4},{7,5},{8,10},{9,11},{14,12},{15,13},{16,18},{17,... | collective-permute-start | bytes 1572872 | tf_op jit(solution)/shard_map/ppermute | solution.py:451
  112.5 0.1 add_convert_fusion.4
  112.7 1.3 collective-permute-start.21
  114.0 0.7 collective-permute-start.20
  114.7 0.7 project.13
  115.4 8.1 %collective-permute-done.19 = bf16[512,512]{1,0:T(8,128)(2,1)S(1)} collective-permute-done((bf16[512,512]{1,0:T(8,128)(2,1)S(1)}, bf16[512,512]{1,0:T(8,128)(2,1)S(1)}, u32[]{:S(2)}, u32[]{:S(2)}) %collective-permute-start.19) | collective-permute-done | bytes 524320 | tf_op jit(solution)/shard_map/ppermute | solution.py:451
  123.5 0.1 add_convert_fusion.5
  123.7 4.1 %collective-permute-done.21 = bf16[512,512]{1,0:T(8,128)(2,1)S(1)} collective-permute-done((bf16[512,512]{1,0:T(8,128)(2,1)S(1)}, bf16[512,512]{1,0:T(8,128)(2,1)S(1)}, u32[]{:S(2)}, u32[]{:S(2)}) %collective-permute-start.21) | collective-permute-done | bytes 524320 | tf_op jit(solution)/shard_map/ppermute | solution.py:451
  127.8 5.6 %collective-permute-start.22 = (bf16[512,512]{1,0:T(8,128)(2,1)S(1)}, bf16[512,512]{1,0:T(8,128)(2,1)S(1)}, u32[]{:S(2)}, u32[]{:S(2)}) collective-permute-start(bf16[512,512]{1,0:T(8,128)(2,1)S(1)} %project.13), channel_id=1, source_target_pairs={{0,2},{1,3},{6,4},{7,5},{8,10},{9,11},{14,12},{15,13},{16,18},{17,... | collective-permute-start | bytes 1572872 | tf_op jit(solution)/shard_map/ppermute | solution.py:451
  133.4 0.7 project.12
  134.1 0.7 collective-permute-start.25
  134.8 0.3 add_convert_fusion.2
  135.1 7.8 %collective-permute-done.22 = bf16[512,512]{1,0:T(8,128)(2,1)S(1)} collective-permute-done((bf16[512,512]{1,0:T(8,128)(2,1)S(1)}, bf16[512,512]{1,0:T(8,128)(2,1)S(1)}, u32[]{:S(2)}, u32[]{:S(2)}) %collective-permute-start.22) | collective-permute-done | bytes 524320 | tf_op jit(solution)/shard_map/ppermute | solution.py:451
  142.9 0.1 add_convert_fusion.3
  143.1 0.7 collective-permute-start.24
  143.8 0.1 add_convert_fusion.1
  143.9 1.3 collective-permute-start.26
  145.2 6.1 %collective-permute-start.23 = (bf16[512,512]{1,0:T(8,128)(2,1)S(1)}, bf16[512,512]{1,0:T(8,128)(2,1)S(1)}, u32[]{:S(2)}, u32[]{:S(2)}) collective-permute-start(bf16[512,512]{1,0:T(8,128)(2,1)S(1)} %project.12), channel_id=1, source_target_pairs={{0,2},{1,3},{6,4},{7,5},{8,10},{9,11},{14,12},{15,13},{16,18},{17,... | collective-permute-start | bytes 1572872 | tf_op jit(solution)/shard_map/ppermute | solution.py:451
  151.4 0.7 project.15
  152.1 6.4 %collective-permute-done.26 = bf16[512,512]{1,0:T(8,128)(2,1)S(1)} collective-permute-done((bf16[512,512]{1,0:T(8,128)(2,1)S(1)}, bf16[512,512]{1,0:T(8,128)(2,1)S(1)}, u32[]{:S(2)}, u32[]{:S(2)}) %collective-permute-start.26) | collective-permute-done | bytes 524320 | tf_op jit(solution)/shard_map/ppermute | solution.py:451
  158.5 1.2 collective-permute-done.23
  159.7 0.3 add_convert_fusion
  160.0 1.0 pad_maximum_fusion
  (38 shorter events, 0.3 us)
Async XLA Ops:
  2.4 13.2 %collective-permute-start = (bf16[1552,128]{1,0:T(8,128)(2,1)}, bf16[1552,128]{1,0:T(8,128)(2,1)S(1)}, u32[]{:S(2)}, u32[]{:S(2)}) collective-permute-start(bf16[1552,128]{1,0:T(8,128)(2,1)} %get-tuple-element.56), channel_id=1, source_target_pairs={{0,8},{8,0},{16,24},{24,16},{1,9},{9,1},{17,25},{25,17},{2,10},{10... | collective-permute-start | bytes 1191944 | tf_op jit(solution)/shard_map/ppermute | solution.py:446
  5.3 19.4 %collective-permute-start.1 = (bf16[1552,128]{1,0:T(8,128)(2,1)}, bf16[1552,128]{1,0:T(8,128)(2,1)S(1)}, u32[]{:S(2)}, u32[]{:S(2)}) collective-permute-start(bf16[1552,128]{1,0:T(8,128)(2,1)} %get-tuple-element.57), channel_id=1, source_target_pairs={{0,16},{8,24},{16,0},{24,8},{1,17},{9,25},{17,1},{25,9},{2,18},{10... | collective-permute-start | bytes 1191944 | tf_op jit(solution)/shard_map/ppermute | solution.py:446
  6.9 17.9 %collective-permute-start.2 = (bf16[1552,128]{1,0:T(8,128)(2,1)}, bf16[1552,128]{1,0:T(8,128)(2,1)}, u32[]{:S(2)}, u32[]{:S(2)}) collective-permute-start(bf16[1552,128]{1,0:T(8,128)(2,1)} %get-tuple-element.58), channel_id=1, source_target_pairs={{0,24},{8,16},{16,8},{24,0},{1,25},{9,17},{17,9},{25,1},{2,26},{10... | collective-permute-start | bytes 1191944 | tf_op jit(solution)/shard_map/ppermute | solution.py:446
  8.2 16.5 %copy-start.1 = (bf16[1024,512]{1,0:T(8,128)(2,1)S(1)}, bf16[1024,512]{1,0:T(8,128)(2,1)}, u32[]{:S(2)}) copy-start(bf16[1024,512]{1,0:T(8,128)(2,1)} %refs_3_.5) | copy-start | bytes 3145732
  8.2 16.5 %copy-start.3 = (bf16[1024,512]{1,0:T(8,128)(2,1)S(1)}, bf16[1024,512]{1,0:T(8,128)(2,1)}, u32[]{:S(2)}) copy-start(bf16[1024,512]{1,0:T(8,128)(2,1)} %refs_4_.5) | copy-start | bytes 3145732
  8.2 16.5 %copy-start.5 = (bf16[1024,512]{1,0:T(8,128)(2,1)S(1)}, bf16[1024,512]{1,0:T(8,128)(2,1)}, u32[]{:S(2)}) copy-start(bf16[1024,512]{1,0:T(8,128)(2,1)} %refs_5_.5) | copy-start | bytes 3145732
  8.2 16.5 %copy-start.7 = (s32[1024]{0:T(1024)S(1)}, s32[1024]{0:T(1024)}, u32[]{:S(2)}) copy-start(s32[1024]{0:T(1024)} %param.9) | copy-start | bytes 12292
  24.7 21.2 %collective-permute-start.10 = (bf16[512,2048]{1,0:T(8,128)(2,1)}, bf16[512,2048]{1,0:T(8,128)(2,1)S(1)}, u32[]{:S(2)}, u32[]{:S(2)}) collective-permute-start(bf16[512,2048]{1,0:T(8,128)(2,1)} %get-tuple-element.77), channel_id=1, source_target_pairs={{0,1},{1,0},{2,3},{3,2},{4,5},{5,4},{6,7},{7,6},{8,9},{9,8},{10,11... | collective-permute-start | bytes 6291464 | tf_op jit(solution)/shard_map/ppermute | solution.py:446
  33.8 6.5 %collective-permute-start.5 = (bf16[512,128]{1,0:T(8,128)(2,1)}, bf16[512,128]{1,0:T(8,128)(2,1)S(1)}, u32[]{:S(2)}, u32[]{:S(2)}) collective-permute-start(bf16[512,128]{1,0:T(8,128)(2,1)} %get-tuple-element.64), channel_id=1, source_target_pairs={{0,8},{8,0},{16,24},{24,16},{1,9},{9,1},{17,25},{25,17},{2,10},{10... | collective-permute-start | bytes 393224 | tf_op jit(solution)/shard_map/ppermute | solution.py:446
  35.2 7.0 %collective-permute-start.6 = (bf16[512,128]{1,0:T(8,128)(2,1)}, bf16[512,128]{1,0:T(8,128)(2,1)S(1)}, u32[]{:S(2)}, u32[]{:S(2)}) collective-permute-start(bf16[512,128]{1,0:T(8,128)(2,1)} %get-tuple-element.65), channel_id=1, source_target_pairs={{0,16},{8,24},{16,0},{24,8},{1,17},{9,25},{17,1},{25,9},{2,18},{10... | collective-permute-start | bytes 393224 | tf_op jit(solution)/shard_map/ppermute | solution.py:446
  35.9 7.9 %collective-permute-start.7 = (bf16[512,128]{1,0:T(8,128)(2,1)}, bf16[512,128]{1,0:T(8,128)(2,1)S(1)}, u32[]{:S(2)}, u32[]{:S(2)}) collective-permute-start(bf16[512,128]{1,0:T(8,128)(2,1)} %get-tuple-element.66), channel_id=1, source_target_pairs={{0,24},{8,16},{16,8},{24,0},{1,25},{9,17},{17,9},{25,1},{2,26},{10... | collective-permute-start | bytes 393224 | tf_op jit(solution)/shard_map/ppermute | solution.py:446
  37.3 8.6 %copy-start = (bf16[512,2048]{1,0:T(8,128)(2,1)S(1)}, bf16[512,2048]{1,0:T(8,128)(2,1)}, u32[]{:S(2)}) copy-start(bf16[512,2048]{1,0:T(8,128)(2,1)} %get-tuple-element.76.w_mine_ref) | copy-start | bytes 6291460
  43.9 2.0 %collective-permute-start.9 = (bf16[512,512]{1,0:T(8,128)(2,1)S(1)}, bf16[512,512]{1,0:T(8,128)(2,1)S(1)}, u32[]{:S(2)}, u32[]{:S(2)}) collective-permute-start(bf16[512,512]{1,0:T(8,128)(2,1)S(1)} %assemble.2.mine_ref), channel_id=1, source_target_pairs={{0,1},{1,0},{2,3},{3,2},{4,5},{5,4},{6,7},{7,6},{8,9},{9,8},{10,11... | collective-permute-start | bytes 1572872 | tf_op jit(solution)/shard_map/ppermute | solution.py:446
  45.9 4.3 %copy-start.10 = (bf16[1536,128]{1,0:T(8,128)(2,1)S(1)}, bf16[1536,128]{1,0:T(8,128)(2,1)}, u32[]{:S(2)}) copy-start(bf16[1536,128]{1,0:T(8,128)(2,1)} %get-tuple-element.70) | copy-start | bytes 1179652
  45.9 5.0 %copy-start.9 = (bf16[1536,128]{1,0:T(8,128)(2,1)S(1)}, bf16[1536,128]{1,0:T(8,128)(2,1)}, u32[]{:S(2)}) copy-start(bf16[1536,128]{1,0:T(8,128)(2,1)} %get-tuple-element.71) | copy-start | bytes 1179652
  45.9 6.5 %copy-start.8 = (bf16[1536,128]{1,0:T(8,128)(2,1)S(1)}, bf16[1536,128]{1,0:T(8,128)(2,1)}, u32[]{:S(2)}) copy-start(bf16[1536,128]{1,0:T(8,128)(2,1)} %get-tuple-element.74) | copy-start | bytes 1179652
  46.6 14.9 %collective-permute-start.11 = (bf16[512,512]{1,0:T(8,128)(2,1)S(1)}, bf16[512,512]{1,0:T(8,128)(2,1)S(1)}, u32[]{:S(2)}, u32[]{:S(2)}) collective-permute-start(bf16[512,512]{1,0:T(8,128)(2,1)S(1)} %project.8), channel_id=1, source_target_pairs={{0,2},{1,3},{6,4},{7,5},{8,10},{9,11},{14,12},{15,13},{16,18},{17,... | collective-permute-start | bytes 1572872 | tf_op jit(solution)/shard_map/ppermute | solution.py:451
  50.2 17.4 %collective-permute-start.3 = (bf16[1536,128]{1,0:T(8,128)(2,1)S(1)}, bf16[1536,128]{1,0:T(8,128)(2,1)S(1)}, u32[]{:S(2)}, u32[]{:S(2)}) collective-permute-start(bf16[1536,128]{1,0:T(8,128)(2,1)S(1)} %copy-done.10), channel_id=1, source_target_pairs={{0,8},{8,0},{16,24},{24,16},{1,9},{9,1},{17,25},{25,17},{2,10},{10... | collective-permute-start | bytes 1179656 | tf_op jit(solution)/shard_map/ppermute | solution.py:446
  50.9 19.0 %collective-permute-start.4 = (bf16[1536,128]{1,0:T(8,128)(2,1)S(1)}, bf16[1536,128]{1,0:T(8,128)(2,1)S(1)}, u32[]{:S(2)}, u32[]{:S(2)}) collective-permute-start(bf16[1536,128]{1,0:T(8,128)(2,1)S(1)} %copy-done.9), channel_id=1, source_target_pairs={{0,16},{8,24},{16,0},{24,8},{1,17},{9,25},{17,1},{25,9},{2,18},{10... | collective-permute-start | bytes 1179656 | tf_op jit(solution)/shard_map/ppermute | solution.py:446
  52.4 17.5 %collective-permute-start.8 = (bf16[1536,128]{1,0:T(8,128)(2,1)S(1)}, bf16[1536,128]{1,0:T(8,128)(2,1)S(1)}, u32[]{:S(2)}, u32[]{:S(2)}) collective-permute-start(bf16[1536,128]{1,0:T(8,128)(2,1)S(1)} %copy-done.8), channel_id=1, source_target_pairs={{0,24},{8,16},{16,8},{24,0},{1,25},{9,17},{17,9},{25,1},{2,26},{10... | collective-permute-start | bytes 1179656 | tf_op jit(solution)/shard_map/ppermute | solution.py:446
  61.6 25.5 %collective-permute-start.15 = (bf16[512,512]{1,0:T(8,128)(2,1)S(1)}, bf16[512,512]{1,0:T(8,128)(2,1)S(1)}, u32[]{:S(2)}, u32[]{:S(2)}) collective-permute-start(bf16[512,512]{1,0:T(8,128)(2,1)S(1)} %project.9), channel_id=1, source_target_pairs={{0,2},{1,3},{6,4},{7,5},{8,10},{9,11},{14,12},{15,13},{16,18},{17,... | collective-permute-start | bytes 1572872 | tf_op jit(solution)/shard_map/ppermute | solution.py:451
  66.7 3.9 %copy-start.4 = (bf16[1024,512]{1,0:T(8,128)(2,1)S(1)}, bf16[1024,512]{1,0:T(8,128)(2,1)}, u32[]{:S(2)}) copy-start(bf16[1024,512]{1,0:T(8,128)(2,1)} %refs_4_.5) | copy-start | bytes 3145732
  66.7 3.9 %copy-start.6 = (bf16[1024,512]{1,0:T(8,128)(2,1)S(1)}, bf16[1024,512]{1,0:T(8,128)(2,1)}, u32[]{:S(2)}) copy-start(bf16[1024,512]{1,0:T(8,128)(2,1)} %refs_5_.5) | copy-start | bytes 3145732
  67.4 3.2 %copy-start.2 = (bf16[1024,512]{1,0:T(8,128)(2,1)S(1)}, bf16[1024,512]{1,0:T(8,128)(2,1)}, u32[]{:S(2)}) copy-start(bf16[1024,512]{1,0:T(8,128)(2,1)} %refs_3_.5) | copy-start | bytes 3145732
  69.9 21.9 %collective-permute-start.16 = (bf16[512,512]{1,0:T(8,128)(2,1)S(1)}, bf16[512,512]{1,0:T(8,128)(2,1)S(1)}, u32[]{:S(2)}, u32[]{:S(2)}) collective-permute-start(bf16[512,512]{1,0:T(8,128)(2,1)S(1)} %add_convert_fusion.7), channel_id=1, source_target_pairs={{2,4},{3,5},{4,2},{5,3},{10,12},{11,13},{12,10},{13,11},{18,20},{1... | collective-permute-start | bytes 1572872 | tf_op jit(solution)/shard_map/ppermute | solution.py:451
  83.5 6.3 %collective-permute-start.12 = (bf16[512,128]{1,0:T(8,128)(2,1)S(1)}, bf16[512,128]{1,0:T(8,128)(2,1)S(1)}, u32[]{:S(2)}, u32[]{:S(2)}) collective-permute-start(bf16[512,128]{1,0:T(8,128)(2,1)S(1)} %get-tuple-element.84), channel_id=1, source_target_pairs={{0,8},{8,0},{16,24},{24,16},{1,9},{9,1},{17,25},{25,17},{2,10},{10... | collective-permute-start | bytes 393224 | tf_op jit(solution)/shard_map/ppermute | solution.py:446
  84.9 6.8 %collective-permute-start.13 = (bf16[512,128]{1,0:T(8,128)(2,1)S(1)}, bf16[512,128]{1,0:T(8,128)(2,1)S(1)}, u32[]{:S(2)}, u32[]{:S(2)}) collective-permute-start(bf16[512,128]{1,0:T(8,128)(2,1)S(1)} %get-tuple-element.85), channel_id=1, source_target_pairs={{0,16},{8,24},{16,0},{24,8},{1,17},{9,25},{17,1},{25,9},{2,18},{10... | collective-permute-start | bytes 393224 | tf_op jit(solution)/shard_map/ppermute | solution.py:446
  85.6 6.1 %collective-permute-start.14 = (bf16[512,128]{1,0:T(8,128)(2,1)S(1)}, bf16[512,128]{1,0:T(8,128)(2,1)S(1)}, u32[]{:S(2)}, u32[]{:S(2)}) collective-permute-start(bf16[512,128]{1,0:T(8,128)(2,1)S(1)} %get-tuple-element.86), channel_id=1, source_target_pairs={{0,24},{8,16},{16,8},{24,0},{1,25},{9,17},{17,9},{25,1},{2,26},{10... | collective-permute-start | bytes 393224 | tf_op jit(solution)/shard_map/ppermute | solution.py:446
  91.8 4.7 %collective-permute-start.17 = (bf16[512,512]{1,0:T(8,128)(2,1)S(1)}, bf16[512,512]{1,0:T(8,128)(2,1)S(1)}, u32[]{:S(2)}, u32[]{:S(2)}) collective-permute-start(bf16[512,512]{1,0:T(8,128)(2,1)S(1)} %assemble.3.mine_ref), channel_id=1, source_target_pairs={{0,1},{1,0},{2,3},{3,2},{4,5},{5,4},{6,7},{7,6},{8,9},{9,8},{10,11... | collective-permute-start | bytes 1572872 | tf_op jit(solution)/shard_map/ppermute | solution.py:446
  91.9 16.2 %collective-permute-start.18 = (bf16[512,512]{1,0:T(8,128)(2,1)S(1)}, bf16[512,512]{1,0:T(8,128)(2,1)S(1)}, u32[]{:S(2)}, u32[]{:S(2)}) collective-permute-start(bf16[512,512]{1,0:T(8,128)(2,1)S(1)} %project.10), channel_id=1, source_target_pairs={{0,2},{1,3},{6,4},{7,5},{8,10},{9,11},{14,12},{15,13},{16,18},{17,... | collective-permute-start | bytes 1572872 | tf_op jit(solution)/shard_map/ppermute | solution.py:451
  108.1 15.4 %collective-permute-start.19 = (bf16[512,512]{1,0:T(8,128)(2,1)S(1)}, bf16[512,512]{1,0:T(8,128)(2,1)S(1)}, u32[]{:S(2)}, u32[]{:S(2)}) collective-permute-start(bf16[512,512]{1,0:T(8,128)(2,1)S(1)} %project.14), channel_id=1, source_target_pairs={{0,2},{1,3},{6,4},{7,5},{8,10},{9,11},{14,12},{15,13},{16,18},{17,... | collective-permute-start | bytes 1572872 | tf_op jit(solution)/shard_map/ppermute | solution.py:451
  112.7 15.1 %collective-permute-start.21 = (bf16[512,512]{1,0:T(8,128)(2,1)S(1)}, bf16[512,512]{1,0:T(8,128)(2,1)S(1)}, u32[]{:S(2)}, u32[]{:S(2)}) collective-permute-start(bf16[512,512]{1,0:T(8,128)(2,1)S(1)} %add_convert_fusion.4), channel_id=1, source_target_pairs={{4,6},{5,7},{2,0},{3,1},{12,14},{13,15},{10,8},{11,9},{20,22},{21,... | collective-permute-start | bytes 1572872 | tf_op jit(solution)/shard_map/ppermute | solution.py:451
  114.0 13.8 %collective-permute-start.20 = (bf16[512,512]{1,0:T(8,128)(2,1)S(1)}, bf16[512,512]{1,0:T(8,128)(2,1)S(1)}, u32[]{:S(2)}, u32[]{:S(2)}) collective-permute-start(bf16[512,512]{1,0:T(8,128)(2,1)S(1)} %add_convert_fusion.6), channel_id=1, source_target_pairs={{2,4},{3,5},{4,2},{5,3},{10,12},{11,13},{12,10},{13,11},{18,20},{1... | collective-permute-start | bytes 1572872 | tf_op jit(solution)/shard_map/ppermute | solution.py:451
  127.8 15.1 %collective-permute-start.22 = (bf16[512,512]{1,0:T(8,128)(2,1)S(1)}, bf16[512,512]{1,0:T(8,128)(2,1)S(1)}, u32[]{:S(2)}, u32[]{:S(2)}) collective-permute-start(bf16[512,512]{1,0:T(8,128)(2,1)S(1)} %project.13), channel_id=1, source_target_pairs={{0,2},{1,3},{6,4},{7,5},{8,10},{9,11},{14,12},{15,13},{16,18},{17,... | collective-permute-start | bytes 1572872 | tf_op jit(solution)/shard_map/ppermute | solution.py:451
  134.1 9.7 %collective-permute-start.25 = (bf16[512,512]{1,0:T(8,128)(2,1)S(1)}, bf16[512,512]{1,0:T(8,128)(2,1)S(1)}, u32[]{:S(2)}, u32[]{:S(2)}) collective-permute-start(bf16[512,512]{1,0:T(8,128)(2,1)S(1)} %add_convert_fusion.5), channel_id=1, source_target_pairs={{2,4},{3,5},{4,2},{5,3},{10,12},{11,13},{12,10},{13,11},{18,20},{1... | collective-permute-start | bytes 1572872 | tf_op jit(solution)/shard_map/ppermute | solution.py:451
  143.1 9.0 %collective-permute-start.24 = (bf16[512,512]{1,0:T(8,128)(2,1)S(1)}, bf16[512,512]{1,0:T(8,128)(2,1)S(1)}, u32[]{:S(2)}, u32[]{:S(2)}) collective-permute-start(bf16[512,512]{1,0:T(8,128)(2,1)S(1)} %add_convert_fusion.3), channel_id=1, source_target_pairs={{2,4},{3,5},{4,2},{5,3},{10,12},{11,13},{12,10},{13,11},{18,20},{1... | collective-permute-start | bytes 1572872 | tf_op jit(solution)/shard_map/ppermute | solution.py:451
  143.9 14.5 %collective-permute-start.26 = (bf16[512,512]{1,0:T(8,128)(2,1)S(1)}, bf16[512,512]{1,0:T(8,128)(2,1)S(1)}, u32[]{:S(2)}, u32[]{:S(2)}) collective-permute-start(bf16[512,512]{1,0:T(8,128)(2,1)S(1)} %add_convert_fusion.1), channel_id=1, source_target_pairs={{4,6},{5,7},{2,0},{3,1},{12,14},{13,15},{10,8},{11,9},{20,22},{21,... | collective-permute-start | bytes 1572872 | tf_op jit(solution)/shard_map/ppermute | solution.py:451
  145.2 14.4 %collective-permute-start.23 = (bf16[512,512]{1,0:T(8,128)(2,1)S(1)}, bf16[512,512]{1,0:T(8,128)(2,1)S(1)}, u32[]{:S(2)}, u32[]{:S(2)}) collective-permute-start(bf16[512,512]{1,0:T(8,128)(2,1)S(1)} %project.12), channel_id=1, source_target_pairs={{0,2},{1,3},{6,4},{7,5},{8,10},{9,11},{14,12},{15,13},{16,18},{17,... | collective-permute-start | bytes 1572872 | tf_op jit(solution)/shard_map/ppermute | solution.py:451

commit v4 on v3

--- a/solution.py
+++ b/solution.py
@@ -208,18 +208,18 @@
     )(ctx_index, *operands)
 
 
-def pack_projection(places, w_out, chips):
+def pack_projection(core, w_out, chips):
     depth, width = w_out.shape
     columns = width // (2 * chips)
 
-    def kernel(places_ref, keep_in, give_in, keep_out, give_out):
+    def kernel(core_ref, keep_in, give_in, keep_out, give_out):
         keep_out[...] = keep_in[...]
         give_out[...] = give_in[...]
 
     def block(other):
         def index_map(turn, at):
-            parity = 1 - at[chips] if other else at[chips]
-            return (0, 2 * at[turn] + parity)
+            parity = 1 - at[0] if other else at[0]
+            return (0, 2 * turn + parity)
 
         return pl.BlockSpec((depth, columns), index_map)
 
@@ -236,7 +236,7 @@
         compiler_params=params(56),
         cost_estimate=SMALL,
         name="pack_projection",
-    )(places, w_out, w_out)
+    )(core, w_out, w_out)
 
 
 def attend(ctx_index, queries, keys, values, docs, low, high, tiles):
@@ -446,24 +446,6 @@
     return lax.ppermute(value, axis, [(source, source ^ distance) for source in range(count)])
 
 
-def between_chips(value, pairs):
-    both = [(2 * source + core, 2 * target + core) for source, target in pairs for core in (0, 1)]
-    return lax.ppermute(value, "head", both)
-
-
-def add(*terms):
-    total = terms[0].astype(jnp.float32)
-    for term in terms[1:]:
-        total = total + term.astype(jnp.float32)
-    return total.astype(jnp.bfloat16)
-
-
-SENDING = ((3, 2, 1, 0), (3, 2, 0, 1), (0, 1, 3, 2), (0, 1, 2, 3))
-TO_MIDDLE = ((0, 1), (3, 2))
-ACROSS = ((1, 2), (2, 1))
-TO_ENDS = ((2, 3), (1, 0))
-
-
 def tie(*values):
     return lax.optimization_barrier(values)
 
@@ -475,15 +457,13 @@
     columns = w_out.shape[1] // (2 * chips)
     ctx_index = lax.axis_index("ctx").astype(jnp.int32).reshape(1)
     head_index = lax.axis_index("head").astype(jnp.int32)
-    chip = head_index // 2
     core = (head_index % 2).reshape(1)
-    places = jnp.concatenate([jnp.array(SENDING, jnp.int32)[chip], core])
     docs = doc_ids.reshape(shard_rows // HD, HD)
     near = range(1, group)
 
     low_out = pack(ctx_index, 0, queries, keys, values, docs)
     low = [swap(low_out[distance - 1], "ctx", distance) for distance in near]
-    w_mine, w_give = pack_projection(places, w_out, chips)
+    w_mine, w_give = pack_projection(core, w_out, chips)
     low, w_give = tie(low, w_give)
     w_sibling = swap(w_give, "head", 1)
     high_out = pack(ctx_index, 1, queries, keys, values, None)
@@ -492,8 +472,15 @@
     def send_back(pieces):
         return [swap(pieces[distance], "ctx", distance) for distance in near]
 
-    def share_of(mine, sibling, turn):
-        return project(mine, sibling, w_mine, w_sibling, turn, 1, chips)
+    def shares_of(mine):
+        sibling = swap(mine, "head", 1)
+        return project(mine, sibling, w_mine, w_sibling, 0, chips, chips)
+
+    def sum_over_chips(shares):
+        groups = [[2 * other + parity for other in range(chips)] for parity in range(2)]
+        return lax.psum_scatter(
+            shares, "head", scatter_dimension=1, axis_index_groups=groups, tiled=True
+        )
 
     pieces = attend(ctx_index, queries, keys, values, docs, low, None, tiles)
     back = send_back(pieces)
@@ -502,40 +489,14 @@
     mine = assemble(ctx_index, [pieces[0], *back])
     mine, diagonal_out = tie(mine, high_out[2])
     high.append(swap(diagonal_out, "ctx", 3))
-    sibling = swap(mine, "head", 1)
-    shares = [share_of(mine, sibling, turn) for turn in range(chips)]
-    end = [between_chips(shares[0], TO_MIDDLE)]
-    end[0], shares[1] = tie(end[0], shares[1])
-    end.append(between_chips(shares[1], TO_MIDDLE))
-    passed = add(shares[0], end[0])
-
-    high, passed, shares[1:] = tie(high, passed, shares[1:])
-    across = [between_chips(passed, ACROSS)]
+    shares = shares_of(mine)
+    shares, high = tie(shares, high)
+    first = sum_over_chips(shares)
+
     pieces = attend(ctx_index, queries, keys, values, docs, low, high, tiles)
-    back = send_back(pieces)
-    passed = add(shares[1], end[1])
-    back, passed, shares[2] = tie(back, passed, shares[2])
-    across.append(between_chips(passed, ACROSS))
-    end.append(between_chips(shares[2], TO_MIDDLE))
-    mine = assemble(ctx_index, [pieces[0], *back])
-    mine, across[0] = tie(mine, across[0])
-    sibling = swap(mine, "head", 1)
-    outer = between_chips(add(shares[2], across[0]), TO_ENDS)
-    late = [share_of(mine, sibling, turn) for turn in range(chips)]
-    late[0], end[2] = tie(late[0], end[2])
-    end_high = [between_chips(late[0], TO_MIDDLE)]
-    passed = add(late[0], end_high[0])
-    late[1], passed, across[1], outer = tie(late[1], passed, across[1], outer)
-    across_high = [between_chips(passed, ACROSS)]
-    end_high.append(between_chips(late[1], TO_MIDDLE))
-    first = add(shares[3], end[2], across[1], outer)
-    passed = add(late[1], end_high[1])
-    late[2], passed, first = tie(late[2], passed, first)
-    across_high.append(between_chips(passed, ACROSS))
-    end_high.append(between_chips(late[2], TO_MIDDLE))
-    outer_high = between_chips(add(late[2], across_high[0]), TO_ENDS)
-    second = add(late[3], end_high[2], across_high[1], outer_high)
-    return jnp.concatenate([first, second], axis=0)
+    shares = shares_of(assemble(ctx_index, [pieces[0], *send_back(pieces)]))
+    shares, first = tie(shares, first)
+    return jnp.concatenate([first, sum_over_chips(shares)], axis=0)
 
 
 def solution(mesh):
@@ -546,7 +507,7 @@
 
     def local(queries, keys, values, doc_ids, w_out):
         heads = queries.shape[1] // HD
-        exchange = heads == ctx_count and heads == 4 and head_count == 2 * len(SENDING)
+        exchange = heads == ctx_count and heads == 4 and head_count % 2 == 0
         exchange = exchange and queries.shape[0] % (4 * TILE) == 0
         body = exchange_local if exchange else ring_local
         return body(queries, keys, values, doc_ids, w_out)

time: 161 us -> 170 us (1.056)
  starting transfers between devices: 49.2 us -> 15.4 us
  waiting for transfers between devices: 69.3 us -> 99.5 us
  between operations: 0.37 us -> 13.6 us
  local copies, waits for them, and re-layouts: 0.74 us -> 4.75 us
  Pallas kernels: 38.4 us -> 35.6 us
    reduce_scatter x0 -> x2, waiting for transfers between devices: none -> 64.7 us  [sum_over_chips(): lax.psum_scatter(shares, 'head', scatter_dimension=1, axis_index_groups=g...]
    ppermute x12 -> x0, waiting for transfers between devices: 45.7 us -> none  [between_chips(): return lax.ppermute(value, 'head', both)]
    ppermute x12 -> x0, starting transfers between devices: 34 us -> none  [between_chips(): return lax.ppermute(value, 'head', both)]
    ppermute x15, waiting for transfers between devices: 23.5 us -> 34.7 us  [swap(): lax.ppermute(value, axis, [(source, source ^ distance) for source in rang...]
    unnamed x22 -> x34, local copies, waits for them, and re-layouts: 0.05 us -> 4.75 us
    pallas_call x2, Pallas kernels: 21.9 us -> 17.9 us  [attend(): pl.pallas_call(kernel, grid_spec=pltpu.PrefetchScalarGridSpec(num_scalar_...]
    pallas_call x8 -> x2, Pallas kernels: 5.66 us -> 7.42 us  [project(): pl.pallas_call(kernel, grid=(count,), in_specs=[attended, attended, weigh...]
  transfers between devices with their start and end apart: 27 -> 17, of which waited for: 16 -> 12; matrix products, arithmetic and copies ran while one was open for 2% -> 0% of each run, Pallas kernels for 22% -> 19%
where the time goes in v4:
time: 170 us; the launch traced here: 171 us
  waiting for transfers between devices  99.5 us (59%)
  Pallas kernels  35.6 us (21%)
  starting transfers between devices  15.4 us (9%)
  between operations  13.6 us (8%)
  local copies, waits for them, and re-layouts  4.75 us (3%)
  other arithmetic  2.08 us (1%)
    reduce_scatter x2, waiting for transfers between devices, sum_over_chips(): lax.psum_scatter(shares, 'head', scatter_dimension=1, axis_index_groups=g...  64.7 us
    ppermute x15, waiting for transfers between devices, swap(): lax.ppermute(value, axis, [(source, source ^ distance) for source in rang...  34.7 us
    pallas_call x2, Pallas kernels, attend(): pl.pallas_call(kernel, grid_spec=pltpu.PrefetchScalarGridSpec(num_scalar_...  17.9 us
    ppermute x15, starting transfers between devices, swap(): lax.ppermute(value, axis, [(source, source ^ distance) for source in rang...  15.3 us
    pallas_call x2, Pallas kernels, project(): pl.pallas_call(kernel, grid=(count,), in_specs=[attended, attended, weigh...  7.42 us
    pallas_call x1, Pallas kernels, pack_projection(): pl.pallas_call(kernel, grid_spec=pltpu.PrefetchScalarGridSpec(num_scalar_...  5.06 us
    pallas_call x2, Pallas kernels, pack(): pl.pallas_call(kernel, grid_spec=pltpu.PrefetchScalarGridSpec(num_scalar_...  5.01 us
    unnamed x34, local copies, waits for them, and re-layouts  4.75 us
  transfers between devices with their start and end apart: 17, of which 12 were waited for; matrix products, arithmetic and copies ran while one was open for 0% of the time, Pallas kernels for 19%

profile of v4, /device:TPU:0, one launch (start us, length us, event | category | flops | bytes accessed | tf_op | source)
XLA Modules:
  0.0 170.9 jit_solution(10837136732478982605)
XLA Ops:
  6.5 0.0 reduce-scatter.3.cloned.1.call-start
  6.5 2.4 %pack.2 = (bf16[1552,128]{1,0:T(8,128)(2,1)}, bf16[1552,128]{1,0:T(8,128)(2,1)}, bf16[1552,128]{1,0:T(8,128)(2,1)}) custom-call(s32[1]{0:T(128)} %bitcast.ctx_ref, bf16[1024,512]{1,0:T(8,128)(2,1)} %refs_3_.5, bf16[1024,512]{1,0:T(8,128)(2,1)} %refs_4_.5, bf16[1024,512]{1,0:T(8,128)(2,1)} %refs_5_.5, bf16[1024,512]{1,0:T(8,128)(2,1)} %refs_3_.5, ...), custom_call_target="tpu_custom_call" | custom-call | flops 1024 | bytes 1024 | tf_op jit(solution)/shard_map/pack/pallas_call | solution.py:196
  8.9 2.9 %collective-permute-start = (bf16[1552,128]{1,0:T(8,128)(2,1)}, bf16[1552,128]{1,0:T(8,128)(2,1)S(1)}, u32[]{:S(2)}, u32[]{:S(2)}) collective-permute-start(bf16[1552,128]{1,0:T(8,128)(2,1)} %get-tuple-element.37), channel_id=1, source_target_pairs={{0,8},{8,0},{16,24},{24,16},{1,9},{9,1},{17,25},{25,17},{2,10},{10... | collective-permute-start | bytes 1191944 | tf_op jit(solution)/shard_map/ppermute | solution.py:446
  11.9 1.5 collective-permute-start.1
  13.4 0.0 collective-permute-start.2
  13.4 0.0 copy-start.15
  13.4 5.1 %pack_projection.1 = (bf16[512,2048]{1,0:T(8,128)(2,1)}, bf16[512,2048]{1,0:T(8,128)(2,1)}) custom-call(s32[1]{0:T(128)} %bitcast.2.core_ref, bf16[512,4096]{1,0:T(8,128)(2,1)} %give_in.1, bf16[512,4096]{1,0:T(8,128)(2,1)} %give_in.1), custom_call_target="tpu_custom_call" | custom-call | flops 1024 | bytes 1024 | tf_op jit(solution)/shard_map/pack_projection/pallas_call | solution.py:227
  18.5 3.6 %collective-permute-done.refs_4_.refs_7_ = bf16[1552,128]{1,0:T(8,128)(2,1)S(1)} collective-permute-done((bf16[1552,128]{1,0:T(8,128)(2,1)}, bf16[1552,128]{1,0:T(8,128)(2,1)S(1)}, u32[]{:S(2)}, u32[]{:S(2)}) %collective-permute-start) | collective-permute-done | bytes 397344 | tf_op jit(solution)/shard_map/ppermute | solution.py:446
  22.1 9.1 %collective-permute-done.1.refs_5_.refs_8_ = bf16[1552,128]{1,0:T(8,128)(2,1)S(1)} collective-permute-done((bf16[1552,128]{1,0:T(8,128)(2,1)}, bf16[1552,128]{1,0:T(8,128)(2,1)S(1)}, u32[]{:S(2)}, u32[]{:S(2)}) %collective-permute-start.1) | collective-permute-done | bytes 397344 | tf_op jit(solution)/shard_map/ppermute | solution.py:446
  31.3 0.0 collective-permute-done.2.refs_6_.refs_9_
  31.3 0.1 collective-permute-start.7
  31.3 0.0 copy-done
  31.4 0.0 copy-done.2
  31.4 0.0 copy-done.4
  31.4 0.0 copy-done.15
  31.4 9.9 %attend.2 = (bf16[512,128]{1,0:T(8,128)(2,1)S(1)}, bf16[512,128]{1,0:T(8,128)(2,1)S(1)}, bf16[512,128]{1,0:T(8,128)(2,1)S(1)}, bf16[512,128]{1,0:T(8,128)(2,1)S(1)}) custom-call(s32[1]{0:T(128)} %bitcast.ctx_ref, bf16[1024,512]{1,0:T(8,128)(2,1)S(1)} %copy-done, bf16[1024,512]{1,0:T(8,128)(2,1)S(1)} %copy-done.2, bf16[1024,512]{1,0:T(8,128)(2,1)S(1)} %copy-done.4, ...), custom_call_target="tpu_custom_call" | custom-call | flops 1024 | bytes 1024 | tf_op jit(solution)/shard_map/attend/pallas_call | solution.py:377
  41.3 0.0 copy-done.11
  41.3 0.0 copy-done.13
  41.3 1.2 collective-permute-start.3
  42.5 0.9 collective-permute-start.4
  43.4 1.4 collective-permute-start.5
  44.8 2.6 %pack.3 = (bf16[1536,128]{1,0:T(8,128)(2,1)}, bf16[1536,128]{1,0:T(8,128)(2,1)}, bf16[1536,128]{1,0:T(8,128)(2,1)}) custom-call(s32[1]{0:T(128)} %bitcast.ctx_ref, bf16[1024,512]{1,0:T(8,128)(2,1)} %refs_3_.5, bf16[1024,512]{1,0:T(8,128)(2,1)} %refs_4_.5, bf16[1024,512]{1,0:T(8,128)(2,1)} %refs_5_.5, bf16[1024,512]{1,0:T(8,128)(2,1)} %refs_3_.5, ...), custom_call_target="tpu_custom_call" | custom-call | flops 1024 | bytes 1024 | tf_op jit(solution)/shard_map/pack/pallas_call | solution.py:196
  47.4 0.2 collective-permute-done.3.refs_1_
  47.6 1.7 %collective-permute-done.4.refs_2_ = bf16[512,128]{1,0:T(8,128)(2,1)S(1)} collective-permute-done((bf16[512,128]{1,0:T(8,128)(2,1)S(1)}, bf16[512,128]{1,0:T(8,128)(2,1)S(1)}, u32[]{:S(2)}, u32[]{:S(2)}) %collective-permute-start.4) | collective-permute-done | bytes 131104 | tf_op jit(solution)/shard_map/ppermute | solution.py:446
  49.4 1.6 collective-permute-done.5.refs_3_
  51.0 0.1 assemble.2.mine_ref
  51.1 0.1 collective-permute-start.6
  51.2 0.9 collective-permute-start.8
  52.0 1.5 collective-permute-start.9
  53.5 1.2 collective-permute-start.10
  54.7 0.0 collective-permute-done.6.sibling_ref
  54.7 0.0 collective-permute-done.7.w_sibling_ref
  54.7 0.0 copy-done.6
  54.7 0.0 copy-start.5
  54.7 3.3 %project.2 = bf16[512,2048]{1,0:T(8,128)(2,1)S(1)} custom-call(bf16[512,512]{1,0:T(8,128)(2,1)S(1)} %assemble.2.mine_ref, bf16[512,512]{1,0:T(8,128)(2,1)S(1)} %collective-permute-done.6.sibling_ref, bf16[512,2048]{1,0:T(8,128)(2,1)S(1)} %copy-done.6, bf16[512,2048]{1,0:T(8,128)(2,1)S(1)} %collective-permute-done.7.w_sibling_ref), custom_call_target="tpu_custom_call" | custom-call | flops 1024 | bytes 1024 | tf_op jit(solution)/shard_map/project/pallas_call | solution.py:432
  58.1 0.0 copy-start.8
  58.1 1.4 copy-done.8
  59.4 1.3 copy-done.10
  60.8 2.7 %collective-permute-done.8.refs_10_ = bf16[1536,128]{1,0:T(8,128)(2,1)} collective-permute-done((bf16[1536,128]{1,0:T(8,128)(2,1)}, bf16[1536,128]{1,0:T(8,128)(2,1)}, u32[]{:S(2)}, u32[]{:S(2)}) %collective-permute-start.8) | collective-permute-done | bytes 393248 | tf_op jit(solution)/shard_map/ppermute | solution.py:446
  63.5 8.5 %collective-permute-done.9.refs_11_ = bf16[1536,128]{1,0:T(8,128)(2,1)} collective-permute-done((bf16[1536,128]{1,0:T(8,128)(2,1)}, bf16[1536,128]{1,0:T(8,128)(2,1)}, u32[]{:S(2)}, u32[]{:S(2)}) %collective-permute-start.9) | collective-permute-done | bytes 393248 | tf_op jit(solution)/shard_map/ppermute | solution.py:446
  71.9 0.0 collective-permute-done.10.refs_12_
  71.9 0.0 reduce-scatter.3.cloned.1.call-update
  72.0 0.0 reduce-scatter.5.cloned.1.call-start
  72.0 0.0 copy-done.5
  72.0 0.0 copy-done.1
  72.0 0.0 copy-done.3
  72.0 0.0 copy-start.12
  72.1 1.0 copy-done.12
  73.0 1.0 copy-done.14
  74.0 8.0 %attend.3 = (bf16[512,128]{1,0:T(8,128)(2,1)S(1)}, bf16[512,128]{1,0:T(8,128)(2,1)S(1)}, bf16[512,128]{1,0:T(8,128)(2,1)S(1)}, bf16[512,128]{1,0:T(8,128)(2,1)S(1)}) custom-call(s32[1]{0:T(128)} %bitcast.ctx_ref, bf16[1024,512]{1,0:T(8,128)(2,1)S(1)} %copy-done.1, bf16[1024,512]{1,0:T(8,128)(2,1)S(1)} %copy-done.3, bf16[1024,512]{1,0:T(8,128)(2,1)S(1)} %copy-done.5, ...), custom_call_target="tpu_custom_call" | custom-call | flops 1024 | bytes 1024 | tf_op jit(solution)/shard_map/attend/pallas_call | solution.py:377
  82.1 1.3 collective-permute-start.11
  83.4 0.8 collective-permute-start.12
  84.2 1.4 collective-permute-start.13
  85.7 2.1 %collective-permute-done.11.refs_1_ = bf16[512,128]{1,0:T(8,128)(2,1)S(1)} collective-permute-done((bf16[512,128]{1,0:T(8,128)(2,1)S(1)}, bf16[512,128]{1,0:T(8,128)(2,1)S(1)}, u32[]{:S(2)}, u32[]{:S(2)}) %collective-permute-start.11) | collective-permute-done | bytes 131104 | tf_op jit(solution)/shard_map/ppermute | solution.py:446
  87.7 3.3 %collective-permute-done.12.refs_2_ = bf16[512,128]{1,0:T(8,128)(2,1)S(1)} collective-permute-done((bf16[512,128]{1,0:T(8,128)(2,1)S(1)}, bf16[512,128]{1,0:T(8,128)(2,1)S(1)}, u32[]{:S(2)}, u32[]{:S(2)}) %collective-permute-start.12) | collective-permute-done | bytes 131104 | tf_op jit(solution)/shard_map/ppermute | solution.py:446
  91.0 0.0 collective-permute-done.13.refs_3_
  91.0 0.1 assemble.3.mine_ref
  91.1 0.1 collective-permute-start.14
  91.2 1.9 %collective-permute-done.14.sibling_ref = bf16[512,512]{1,0:T(8,128)(2,1)S(1)} collective-permute-done((bf16[512,512]{1,0:T(8,128)(2,1)S(1)}, bf16[512,512]{1,0:T(8,128)(2,1)S(1)}, u32[]{:S(2)}, u32[]{:S(2)}) %collective-permute-start.14) | collective-permute-done | bytes 524320 | tf_op jit(solution)/shard_map/ppermute | solution.py:446
  93.1 4.1 %project.3 = bf16[512,2048]{1,0:T(8,128)(2,1)} custom-call(bf16[512,512]{1,0:T(8,128)(2,1)S(1)} %assemble.3.mine_ref, bf16[512,512]{1,0:T(8,128)(2,1)S(1)} %collective-permute-done.14.sibling_ref, bf16[512,2048]{1,0:T(8,128)(2,1)S(1)} %copy-done.7, bf16[512,2048]{1,0:T(8,128)(2,1)S(1)} %copy-done.9), custom_call_target="tpu_custom_call" | custom-call | flops 1024 | bytes 1024 | tf_op jit(solution)/shard_map/project/pallas_call | solution.py:432
  97.2 19.1 %reduce-scatter.3.cloned.1.call-done = bf16[512,512]{1,0:T(8,128)(2,1)} async-done(((bf16[512,2048]{1,0:T(8,128)(2,1)}), bf16[512,512]{1,0:T(8,128)(2,1)}) %reduce-scatter.3.cloned.1.call-update) | async-done | bytes 524304 | tf_op jit(solution)/shard_map/reduce_scatter | solution.py:481
  116.3 0.0 reduce-scatter.5.cloned.1.call-update
  116.3 45.7 %reduce-scatter.5.cloned.1.call-done = bf16[512,512]{1,0:T(8,128)(2,1)} async-done(((bf16[512,2048]{1,0:T(8,128)(2,1)}), bf16[512,512]{1,0:T(8,128)(2,1)}) %reduce-scatter.5.cloned.1.call-update) | async-done | bytes 524304 | tf_op jit(solution)/shard_map/reduce_scatter | solution.py:481
  161.9 2.1 %pad_maximum_fusion = bf16[1024,512]{1,0:T(8,128)(2,1)} fusion(bf16[512,512]{1,0:T(8,128)(2,1)} %reduce-scatter.5.cloned.1.call-done, bf16[512,512]{1,0:T(8,128)(2,1)S(1)} %copy-done.16), kind=kLoop, calls=%fused_computation | loop fusion | flops 2097152 | bytes 2097152 | tf_op jit(solution)/shard_map/concatenate | solution.py:499
  (16 shorter events, 0.0 us)
Async XLA Ops:
  6.5 109.7 %reduce-scatter.3.cloned.1.call-start = ((), (), s32[]{:S(2)}) async-start(), calls=%async_computation.2 | async-start | bytes 2621440 | tf_op jit(solution)/shard_map/reduce_scatter | solution.py:481
  8.9 13.2 %collective-permute-start = (bf16[1552,128]{1,0:T(8,128)(2,1)}, bf16[1552,128]{1,0:T(8,128)(2,1)S(1)}, u32[]{:S(2)}, u32[]{:S(2)}) collective-permute-start(bf16[1552,128]{1,0:T(8,128)(2,1)} %get-tuple-element.37), channel_id=1, source_target_pairs={{0,8},{8,0},{16,24},{24,16},{1,9},{9,1},{17,25},{25,17},{2,10},{10... | collective-permute-start | bytes 1191944 | tf_op jit(solution)/shard_map/ppermute | solution.py:446
  11.9 19.4 %collective-permute-start.1 = (bf16[1552,128]{1,0:T(8,128)(2,1)}, bf16[1552,128]{1,0:T(8,128)(2,1)S(1)}, u32[]{:S(2)}, u32[]{:S(2)}) collective-permute-start(bf16[1552,128]{1,0:T(8,128)(2,1)} %get-tuple-element.38), channel_id=1, source_target_pairs={{0,16},{8,24},{16,0},{24,8},{1,17},{9,25},{17,1},{25,9},{2,18},{10... | collective-permute-start | bytes 1191944 | tf_op jit(solution)/shard_map/ppermute | solution.py:446
  13.4 17.9 %collective-permute-start.2 = (bf16[1552,128]{1,0:T(8,128)(2,1)}, bf16[1552,128]{1,0:T(8,128)(2,1)S(1)}, u32[]{:S(2)}, u32[]{:S(2)}) collective-permute-start(bf16[1552,128]{1,0:T(8,128)(2,1)} %get-tuple-element.39), channel_id=1, source_target_pairs={{0,24},{8,16},{16,8},{24,0},{1,25},{9,17},{17,9},{25,1},{2,26},{10... | collective-permute-start | bytes 1191944 | tf_op jit(solution)/shard_map/ppermute | solution.py:446
  13.4 17.9 %copy-start = (bf16[1024,512]{1,0:T(8,128)(2,1)S(1)}, bf16[1024,512]{1,0:T(8,128)(2,1)}, u32[]{:S(2)}) copy-start(bf16[1024,512]{1,0:T(8,128)(2,1)} %refs_3_.5) | copy-start | bytes 3145732
  13.4 18.0 %copy-start.2 = (bf16[1024,512]{1,0:T(8,128)(2,1)S(1)}, bf16[1024,512]{1,0:T(8,128)(2,1)}, u32[]{:S(2)}) copy-start(bf16[1024,512]{1,0:T(8,128)(2,1)} %refs_4_.5) | copy-start | bytes 3145732
  13.4 18.0 %copy-start.4 = (bf16[1024,512]{1,0:T(8,128)(2,1)S(1)}, bf16[1024,512]{1,0:T(8,128)(2,1)}, u32[]{:S(2)}) copy-start(bf16[1024,512]{1,0:T(8,128)(2,1)} %refs_5_.5) | copy-start | bytes 3145732
  13.4 18.0 %copy-start.15 = (s32[1024]{0:T(1024)S(1)}, s32[1024]{0:T(1024)}, u32[]{:S(2)}) copy-start(s32[1024]{0:T(1024)} %param.8) | copy-start | bytes 12292
  31.3 10.0 %copy-start.11 = (bf16[1552,128]{1,0:T(8,128)(2,1)}, bf16[1552,128]{1,0:T(8,128)(2,1)S(1)}, u32[]{:S(2)}) copy-start(bf16[1552,128]{1,0:T(8,128)(2,1)S(1)} %collective-permute-done.1.refs_5_.refs_8_) | copy-start | bytes 1191940
  31.3 10.0 %copy-start.13 = (bf16[1552,128]{1,0:T(8,128)(2,1)}, bf16[1552,128]{1,0:T(8,128)(2,1)S(1)}, u32[]{:S(2)}) copy-start(bf16[1552,128]{1,0:T(8,128)(2,1)S(1)} %collective-permute-done.2.refs_6_.refs_9_) | copy-start | bytes 1191940
  31.3 23.4 %collective-permute-start.7 = (bf16[512,2048]{1,0:T(8,128)(2,1)}, bf16[512,2048]{1,0:T(8,128)(2,1)S(1)}, u32[]{:S(2)}, u32[]{:S(2)}) collective-permute-start(bf16[512,2048]{1,0:T(8,128)(2,1)} %get-tuple-element.55), channel_id=1, source_target_pairs={{0,1},{1,0},{2,3},{3,2},{4,5},{5,4},{6,7},{7,6},{8,9},{9,8},{10,11... | collective-permute-start | bytes 6291464 | tf_op jit(solution)/shard_map/ppermute | solution.py:446
  41.3 6.4 %collective-permute-start.3 = (bf16[512,128]{1,0:T(8,128)(2,1)S(1)}, bf16[512,128]{1,0:T(8,128)(2,1)S(1)}, u32[]{:S(2)}, u32[]{:S(2)}) collective-permute-start(bf16[512,128]{1,0:T(8,128)(2,1)S(1)} %get-tuple-element.45), channel_id=1, source_target_pairs={{0,8},{8,0},{16,24},{24,16},{1,9},{9,1},{17,25},{25,17},{2,10},{10... | collective-permute-start | bytes 393224 | tf_op jit(solution)/shard_map/ppermute | solution.py:446
  42.5 6.9 %collective-permute-start.4 = (bf16[512,128]{1,0:T(8,128)(2,1)S(1)}, bf16[512,128]{1,0:T(8,128)(2,1)S(1)}, u32[]{:S(2)}, u32[]{:S(2)}) collective-permute-start(bf16[512,128]{1,0:T(8,128)(2,1)S(1)} %get-tuple-element.46), channel_id=1, source_target_pairs={{0,16},{8,24},{16,0},{24,8},{1,17},{9,25},{17,1},{25,9},{2,18},{10... | collective-permute-start | bytes 393224 | tf_op jit(solution)/shard_map/ppermute | solution.py:446
  43.4 7.6 %collective-permute-start.5 = (bf16[512,128]{1,0:T(8,128)(2,1)S(1)}, bf16[512,128]{1,0:T(8,128)(2,1)S(1)}, u32[]{:S(2)}, u32[]{:S(2)}) collective-permute-start(bf16[512,128]{1,0:T(8,128)(2,1)S(1)} %get-tuple-element.47), channel_id=1, source_target_pairs={{0,24},{8,16},{16,8},{24,0},{1,25},{9,17},{17,9},{25,1},{2,26},{10... | collective-permute-start | bytes 393224 | tf_op jit(solution)/shard_map/ppermute | solution.py:446
  44.8 9.9 %copy-start.6 = (bf16[512,2048]{1,0:T(8,128)(2,1)S(1)}, bf16[512,2048]{1,0:T(8,128)(2,1)}, u32[]{:S(2)}) copy-start(bf16[512,2048]{1,0:T(8,128)(2,1)} %get-tuple-element.54.w_mine_ref) | copy-start | bytes 6291460
  51.1 3.6 %collective-permute-start.6 = (bf16[512,512]{1,0:T(8,128)(2,1)S(1)}, bf16[512,512]{1,0:T(8,128)(2,1)S(1)}, u32[]{:S(2)}, u32[]{:S(2)}) collective-permute-start(bf16[512,512]{1,0:T(8,128)(2,1)S(1)} %assemble.2.mine_ref), channel_id=1, source_target_pairs={{0,1},{1,0},{2,3},{3,2},{4,5},{5,4},{6,7},{7,6},{8,9},{9,8},{10,11... | collective-permute-start | bytes 1572872 | tf_op jit(solution)/shard_map/ppermute | solution.py:446
  51.2 12.3 %collective-permute-start.8 = (bf16[1536,128]{1,0:T(8,128)(2,1)}, bf16[1536,128]{1,0:T(8,128)(2,1)}, u32[]{:S(2)}, u32[]{:S(2)}) collective-permute-start(bf16[1536,128]{1,0:T(8,128)(2,1)} %get-tuple-element.56), channel_id=1, source_target_pairs={{0,8},{8,0},{16,24},{24,16},{1,9},{9,1},{17,25},{25,17},{2,10},{10... | collective-permute-start | bytes 1179656 | tf_op jit(solution)/shard_map/ppermute | solution.py:446
  52.0 19.9 %collective-permute-start.9 = (bf16[1536,128]{1,0:T(8,128)(2,1)}, bf16[1536,128]{1,0:T(8,128)(2,1)}, u32[]{:S(2)}, u32[]{:S(2)}) collective-permute-start(bf16[1536,128]{1,0:T(8,128)(2,1)} %get-tuple-element.57), channel_id=1, source_target_pairs={{0,16},{8,24},{16,0},{24,8},{1,17},{9,25},{17,1},{25,9},{2,18},{10... | collective-permute-start | bytes 1179656 | tf_op jit(solution)/shard_map/ppermute | solution.py:446
  53.5 18.4 %collective-permute-start.10 = (bf16[1536,128]{1,0:T(8,128)(2,1)}, bf16[1536,128]{1,0:T(8,128)(2,1)}, u32[]{:S(2)}, u32[]{:S(2)}) collective-permute-start(bf16[1536,128]{1,0:T(8,128)(2,1)} %get-tuple-element.58), channel_id=1, source_target_pairs={{0,24},{8,16},{16,8},{24,0},{1,25},{9,17},{17,9},{25,1},{2,26},{10... | collective-permute-start | bytes 1179656 | tf_op jit(solution)/shard_map/ppermute | solution.py:446
  54.7 17.3 %copy-start.5 = (bf16[1024,512]{1,0:T(8,128)(2,1)S(1)}, bf16[1024,512]{1,0:T(8,128)(2,1)}, u32[]{:S(2)}) copy-start(bf16[1024,512]{1,0:T(8,128)(2,1)} %refs_5_.5) | copy-start | bytes 3145732
  58.1 1.4 copy-start.8
  59.4 1.3 copy-start.10
  60.8 11.3 %copy-start.1 = (bf16[1024,512]{1,0:T(8,128)(2,1)S(1)}, bf16[1024,512]{1,0:T(8,128)(2,1)}, u32[]{:S(2)}) copy-start(bf16[1024,512]{1,0:T(8,128)(2,1)} %refs_3_.5) | copy-start | bytes 3145732
  60.8 11.3 %copy-start.3 = (bf16[1024,512]{1,0:T(8,128)(2,1)S(1)}, bf16[1024,512]{1,0:T(8,128)(2,1)}, u32[]{:S(2)}) copy-start(bf16[1024,512]{1,0:T(8,128)(2,1)} %refs_4_.5) | copy-start | bytes 3145732
  72.0 90.0 %reduce-scatter.5.cloned.1.call-start = ((), (), s32[]{:S(2)}) async-start(), calls=%async_computation.3 | async-start | bytes 2621440 | tf_op jit(solution)/shard_map/reduce_scatter | solution.py:481
  72.0 1.0 copy-start.12
  73.0 1.0 copy-start.14
  74.0 19.0 %copy-start.7 = (bf16[512,2048]{1,0:T(8,128)(2,1)S(1)}, bf16[512,2048]{1,0:T(8,128)(2,1)}, u32[]{:S(2)}) copy-start(bf16[512,2048]{1,0:T(8,128)(2,1)} %get-tuple-element.54.w_mine_ref) | copy-start | bytes 6291460
  74.0 19.0 %copy-start.9 = (bf16[512,2048]{1,0:T(8,128)(2,1)S(1)}, bf16[512,2048]{1,0:T(8,128)(2,1)}, u32[]{:S(2)}) copy-start(bf16[512,2048]{1,0:T(8,128)(2,1)} %copy-done.8) | copy-start | bytes 6291460
  82.1 5.6 %collective-permute-start.11 = (bf16[512,128]{1,0:T(8,128)(2,1)S(1)}, bf16[512,128]{1,0:T(8,128)(2,1)S(1)}, u32[]{:S(2)}, u32[]{:S(2)}) collective-permute-start(bf16[512,128]{1,0:T(8,128)(2,1)S(1)} %get-tuple-element.63), channel_id=1, source_target_pairs={{0,8},{8,0},{16,24},{24,16},{1,9},{9,1},{17,25},{25,17},{2,10},{10... | collective-permute-start | bytes 393224 | tf_op jit(solution)/shard_map/ppermute | solution.py:446
  83.4 7.6 %collective-permute-start.12 = (bf16[512,128]{1,0:T(8,128)(2,1)S(1)}, bf16[512,128]{1,0:T(8,128)(2,1)S(1)}, u32[]{:S(2)}, u32[]{:S(2)}) collective-permute-start(bf16[512,128]{1,0:T(8,128)(2,1)S(1)} %get-tuple-element.64), channel_id=1, source_target_pairs={{0,16},{8,24},{16,0},{24,8},{1,17},{9,25},{17,1},{25,9},{2,18},{10... | collective-permute-start | bytes 393224 | tf_op jit(solution)/shard_map/ppermute | solution.py:446
  84.2 6.8 %collective-permute-start.13 = (bf16[512,128]{1,0:T(8,128)(2,1)S(1)}, bf16[512,128]{1,0:T(8,128)(2,1)S(1)}, u32[]{:S(2)}, u32[]{:S(2)}) collective-permute-start(bf16[512,128]{1,0:T(8,128)(2,1)S(1)} %get-tuple-element.65), channel_id=1, source_target_pairs={{0,24},{8,16},{16,8},{24,0},{1,25},{9,17},{17,9},{25,1},{2,26},{10... | collective-permute-start | bytes 393224 | tf_op jit(solution)/shard_map/ppermute | solution.py:446
  91.1 2.0 %collective-permute-start.14 = (bf16[512,512]{1,0:T(8,128)(2,1)S(1)}, bf16[512,512]{1,0:T(8,128)(2,1)S(1)}, u32[]{:S(2)}, u32[]{:S(2)}) collective-permute-start(bf16[512,512]{1,0:T(8,128)(2,1)S(1)} %assemble.3.mine_ref), channel_id=1, source_target_pairs={{0,1},{1,0},{2,3},{3,2},{4,5},{5,4},{6,7},{7,6},{8,9},{9,8},{10,11... | collective-permute-start | bytes 1572872 | tf_op jit(solution)/shard_map/ppermute | solution.py:446
  116.3 45.7 %copy-start.16 = (bf16[512,512]{1,0:T(8,128)(2,1)S(1)}, bf16[512,512]{1,0:T(8,128)(2,1)}, u32[]{:S(2)}) copy-start(bf16[512,512]{1,0:T(8,128)(2,1)} %reduce-scatter.3.cloned.1.call-done) | copy-start | bytes 1572868
Sparse Core Ops, SparseCore 0:
  72.1 44.1 reduce-scatter.2
  118.6 43.2 reduce-scatter.4

commit v5 on v3

--- a/solution.py
+++ b/solution.py
@@ -153,6 +153,7 @@
 
 SMALL = pl.CostEstimate(flops=1024, bytes_accessed=1024, transcendentals=0)
 TILE = 256
+MOST_DOCS = 16
 
 
 def params(mib):
@@ -176,8 +177,12 @@
             empty = jnp.zeros((doc_rows - mine.shape[0], HD), jnp.float32)
             mine = jnp.concatenate([mine, empty], axis=0).astype(jnp.bfloat16)
         for place in range(group - 1):
-            for part in range(3):
+            for part in range(2):
                 outs[place][part * rows : (part + 1) * rows, :] = refs[place * 3 + part][...]
+            for block in range(rows // HD):
+                taken = refs[place * 3 + 2][block * HD : (block + 1) * HD, :]
+                lower = 2 * rows + block * HD
+                outs[place][lower : lower + HD, :] = jnp.transpose(taken)
             if docs is not None:
                 outs[place][3 * rows :, :] = mine
 
@@ -239,14 +244,13 @@
     )(places, w_out, w_out)
 
 
-def attend(ctx_index, queries, keys, values, docs, low, high, tiles):
+def attend(ctx_index, queries, keys, values, docs, low, high):
     rows = queries.shape[0] // 2
     group = queries.shape[1] // HD
     with_high = high is not None
     per_block = rows // TILE
+    lines = rows // HD
     key_rows = (2 * group if with_high else group) * rows
-    key_tiles = key_rows // TILE
-    lanes = TILE // HD
     scaling = LOG2E / math.sqrt(HD)
 
     def kernel(ctx_ref, *refs):
@@ -257,7 +261,7 @@
         low_refs = [refs.pop(0) for _ in range(group - 1)]
         high_refs = [refs.pop(0) for _ in range(group - 1)] if with_high else None
         outs = [refs.pop(0) for _ in range(group)]
-        key_buf, value_buf, doc_buf = refs
+        key_buf, value_buf, doc_buf, summed = refs
         ctx = ctx_ref[0]
 
         def part(upper, distance, index, lower=0, count=rows):
@@ -267,7 +271,7 @@
             return source[index * rows + lower : index * rows + lower + count, :]
 
         place = {}
-        doc_lines = {}
+        doc_rows = {}
         for upper in (False, True) if with_high else (False,):
             for distance in range(group):
                 source = ctx ^ distance
@@ -275,92 +279,92 @@
                 place[upper, distance] = block
                 offset = pl.multiple_of(block * rows, rows)
                 key_buf[pl.ds(offset, rows), :] = part(upper, distance, 1)
-                value_buf[pl.ds(offset, rows), :HD] = part(upper, distance, 2)
                 if distance == 0:
                     both = own_docs[...].astype(jnp.float32)
                 else:
                     both = low_refs[distance - 1][3 * rows :, :].astype(jnp.float32)
-                begin = rows // HD if upper else 0
-                for tile in range(per_block):
-                    first = begin + tile * lanes
-                    lines = [both[line : line + 1, :] for line in range(first, first + lanes)]
-                    doc_lines[upper, distance, tile] = lines
-                    doc_buf[pl.ds(block * per_block + tile, 1), :] = jnp.concatenate(lines, axis=1)
-        value_buf[:, HD:] = jnp.ones((key_rows, HD), jnp.bfloat16)
-        last_docs = doc_buf[:, TILE - 1 : TILE]
-
-        def scores_of(query, index):
-            offset = pl.multiple_of(index * TILE, TILE)
+                begin = lines if upper else 0
+                mine = []
+                for line in range(lines):
+                    taken = part(upper, distance, 2, line * HD, HD)
+                    if distance == 0:
+                        taken = jnp.transpose(taken)
+                    column = pl.multiple_of(block * rows + line * HD, HD)
+                    value_buf[:HD, pl.ds(column, HD)] = taken
+                    mine.append(both[begin + line : begin + line + 1, :])
+                    doc_buf[pl.ds(block * lines + line, 1), :] = mine[-1]
+                doc_rows[upper, distance] = jnp.concatenate(mine, axis=1)
+        value_buf[HD:, :] = jnp.ones((value_buf.shape[0] - HD, key_rows), jnp.bfloat16)
+
+        all_docs = doc_buf[...]
+        starts = [jnp.zeros((1, rows), jnp.float32)] * group
+        for number in range(1, MOST_DOCS):
+            smaller = jnp.where(all_docs < number, 1.0, 0.0)
+            count = jnp.sum(jnp.sum(smaller, axis=0, keepdims=True), axis=1, keepdims=True)
+            for distance in range(group):
+                reached = doc_rows[with_high, distance] >= number
+                starts[distance] = jnp.where(reached, count, starts[distance])
+
+        def scores_of(distance, offset, count):
             raw = lax.dot_general(
-                query,
-                key_buf[pl.ds(offset, TILE), :],
+                key_buf[pl.ds(offset, count), :],
+                part(with_high, distance, 0),
                 (((1,), (1,)), ((), ())),
                 preferred_element_type=jnp.float32,
             )
             return raw * scaling
 
-        def weighted(weights, index):
-            offset = pl.multiple_of(index * TILE, TILE)
+        def weighted(weights, offset, count):
             return jnp.dot(
+                value_buf[:, pl.ds(offset, count)],
                 weights.astype(jnp.bfloat16),
-                value_buf[pl.ds(offset, TILE), :],
                 preferred_element_type=jnp.float32,
             )
 
-        causal = lax.broadcasted_iota(jnp.int32, (TILE, TILE), 1) <= lax.broadcasted_iota(
-            jnp.int32, (TILE, TILE), 0
-        )
-        for number, tile in enumerate(tiles):
-            state = []
-            starts = []
-            ends = []
-            queries_of = []
-            docs_of = []
+        key_row = lax.broadcasted_iota(jnp.int32, (rows, rows), 0)
+        causal = key_row <= lax.broadcasted_iota(jnp.int32, (rows, rows), 1)
+        key_row = key_row.astype(jnp.float32)
+        largest = []
+        first_tiles = []
+        ends = []
+        for distance in range(group):
+            block = place[with_high, distance]
+            offset = pl.multiple_of(block * rows, rows)
+            least = starts[distance] - offset.astype(jnp.float32)
+            scores = scores_of(distance, offset, rows)
+            scores = jnp.where((key_row >= least) & causal, scores, MASKED_SCORE)
+            largest.append(jnp.max(scores, axis=0, keepdims=True))
+            summed[distance] = weighted(jnp.exp2(scores - largest[-1]), offset, rows)
+            first_tiles.append(jnp.min(starts[distance]).astype(jnp.int32) // TILE)
+            ends.append(block * per_block)
+
+        longest = ends[0] - first_tiles[0]
+        for distance in range(1, group):
+            longest = jnp.maximum(longest, ends[distance] - first_tiles[distance])
+        tile_row = lax.broadcasted_iota(jnp.int32, (TILE, rows), 0).astype(jnp.float32)
+
+        def visit(step, running):
+            renewed = []
             for distance in range(group):
-                lines = doc_lines[with_high, distance, tile]
-                column = jnp.concatenate(
-                    [jnp.transpose(jnp.broadcast_to(line, (HD, HD))) for line in lines], axis=0
+                wanted = first_tiles[distance] + step
+                index = jnp.maximum(jnp.minimum(wanted, ends[distance] - 1), 0)
+                offset = pl.multiple_of(index * TILE, TILE)
+                least = jnp.where(
+                    wanted < ends[distance], starts[distance] - offset.astype(jnp.float32), 1e9
                 )
-                query_doc = jnp.concatenate([column] * lanes, axis=1)
-                end = place[with_high, distance] * per_block + tile
-                earlier = last_docs < lines[0][:, :1]
-                starts.append(jnp.sum(earlier.astype(jnp.int32)))
-                ends.append(end)
-                query = part(with_high, distance, 0, tile * TILE, TILE)
-                queries_of.append(query)
-                docs_of.append(query_doc)
-                same = query_doc == jnp.concatenate(lines, axis=1)
-                scores = jnp.where(same & causal, scores_of(query, end), MASKED_SCORE)
-                largest = jnp.max(scores, axis=1, keepdims=True)
-                summed = weighted(jnp.exp2(scores - largest), end)
-                state.append((largest, summed))
-
-            longest = ends[0] - starts[0]
-            for distance in range(1, group):
-                longest = jnp.maximum(longest, ends[distance] - starts[distance])
-
-            def visit(step, running):
-                renewed = []
-                for distance in range(group):
-                    largest, summed = running[distance]
-                    wanted = starts[distance] + step
-                    index = jnp.minimum(wanted, ends[distance])
-                    key_doc = doc_buf[pl.ds(index, 1), :]
-                    key_doc = jnp.where(wanted < ends[distance], key_doc, -1.0)
-                    scores = scores_of(queries_of[distance], index)
-                    scores = jnp.where(docs_of[distance] == key_doc, scores, MASKED_SCORE)
-                    new_max = jnp.maximum(largest, jnp.max(scores, axis=1, keepdims=True))
-                    factor = jnp.exp2(largest - new_max)
-                    product = weighted(jnp.exp2(scores - new_max), index)
-                    renewed.append((new_max, summed * factor + product))
-                return tuple(renewed)
-
-            state = lax.fori_loop(0, longest, visit, tuple(state))
-            for distance in range(group):
-                summed = state[distance][1]
-                outs[distance][number * TILE : (number + 1) * TILE, :] = (
-                    summed[:, :HD] / summed[:, HD:]
-                ).astype(jnp.bfloat16)
+                scores = scores_of(distance, offset, TILE)
+                scores = jnp.where(tile_row >= least, scores, MASKED_SCORE)
+                new_max = jnp.maximum(running[distance], jnp.max(scores, axis=0, keepdims=True))
+                factor = jnp.exp2(running[distance] - new_max)
+                product = weighted(jnp.exp2(scores - new_max), offset, TILE)
+                summed[distance] = summed[distance] * factor + product
+                renewed.append(new_max)
+            return tuple(renewed)
+
+        lax.fori_loop(0, longest, visit, tuple(largest))
+        for distance in range(group):
+            attended = summed[distance, :HD, :] / summed[distance, HD : HD + 1, :]
+            outs[distance][...] = jnp.transpose(attended).astype(jnp.bfloat16)
 
     def own(upper):
         return pl.BlockSpec((rows, HD), lambda step, ctx: (int(upper), ctx[0]))
@@ -373,24 +377,24 @@
     received = [docs, *low, *(high if with_high else ())]
     operands += received
     in_specs += [whole(array.shape) for array in received]
-    out_rows = len(tiles) * TILE
     return pl.pallas_call(
         kernel,
         grid_spec=pltpu.PrefetchScalarGridSpec(
             num_scalar_prefetch=1,
             grid=(1,),
             in_specs=in_specs,
-            out_specs=[whole((out_rows, HD))] * group,
+            out_specs=[whole((rows, HD))] * group,
             scratch_shapes=[
                 pltpu.VMEM((key_rows, HD), jnp.bfloat16),
-                pltpu.VMEM((key_rows, 2 * HD), jnp.bfloat16),
-                pltpu.VMEM((key_tiles, TILE), jnp.float32),
+                pltpu.VMEM((HD + 16, key_rows), jnp.bfloat16),
+                pltpu.VMEM((key_rows // HD, HD), jnp.float32),
+                pltpu.VMEM((group, HD + 16, rows), jnp.float32),
             ],
         ),
-        out_shape=[jax.ShapeDtypeStruct((out_rows, HD), jnp.bfloat16)] * group,
+        out_shape=[jax.ShapeDtypeStruct((rows, HD), jnp.bfloat16)] * group,
         compiler_params=params(40),
         cost_estimate=SMALL,
-        name="attend",
+        name="attend_high" if with_high else "attend_low",
     )(ctx_index, *operands)
 
 
@@ -487,52 +491,49 @@
     low, w_give = tie(low, w_give)
     w_sibling = swap(w_give, "head", 1)
     high_out = pack(ctx_index, 1, queries, keys, values, None)
-    tiles = tuple(range(shard_rows // 2 // TILE))
+    high_out, low = tie(high_out, low)
+    high = [swap(high_out[0], "ctx", 1), swap(high_out[1], "ctx", 2)]
 
     def send_back(pieces):
         return [swap(pieces[distance], "ctx", distance) for distance in near]
 
-    def share_of(mine, sibling, turn):
-        return project(mine, sibling, w_mine, w_sibling, turn, 1, chips)
-
-    pieces = attend(ctx_index, queries, keys, values, docs, low, None, tiles)
+    def share_of(mine, sibling, turn, count=1):
+        return project(mine, sibling, w_mine, w_sibling, turn, count, chips)
+
+    pieces = attend(ctx_index, queries, keys, values, docs, low, None)
     back = send_back(pieces)
-    pieces, high_out = tie(pieces, high_out)
-    high = [swap(high_out[0], "ctx", 1), swap(high_out[1], "ctx", 2)]
+    pieces, diagonal_out = tie(pieces, high_out[2])
+    back, high = tie(back, high)
+    high.append(swap(diagonal_out, "ctx", 3))
     mine = assemble(ctx_index, [pieces[0], *back])
-    mine, diagonal_out = tie(mine, high_out[2])
-    high.append(swap(diagonal_out, "ctx", 3))
     sibling = swap(mine, "head", 1)
-    shares = [share_of(mine, sibling, turn) for turn in range(chips)]
-    end = [between_chips(shares[0], TO_MIDDLE)]
-    end[0], shares[1] = tie(end[0], shares[1])
-    end.append(between_chips(shares[1], TO_MIDDLE))
-    passed = add(shares[0], end[0])
-
-    high, passed, shares[1:] = tie(high, passed, shares[1:])
+    share = share_of(mine, sibling, 0)
+    shares = share_of(mine, sibling, 1, 2)
+    kept = share_of(mine, sibling, 3)
+    end = between_chips(share, TO_MIDDLE)
+    ends = between_chips(shares, TO_MIDDLE)
+
+    high, share, shares, kept = tie(high, share, shares, kept)
+    pieces = attend(ctx_index, queries, keys, values, docs, low, high)
+    back = send_back(pieces)
+    passed = add(share, end)
+    back, passed = tie(back, passed)
     across = [between_chips(passed, ACROSS)]
-    pieces = attend(ctx_index, queries, keys, values, docs, low, high, tiles)
-    back = send_back(pieces)
-    passed = add(shares[1], end[1])
-    back, passed, shares[2] = tie(back, passed, shares[2])
-    across.append(between_chips(passed, ACROSS))
-    end.append(between_chips(shares[2], TO_MIDDLE))
     mine = assemble(ctx_index, [pieces[0], *back])
-    mine, across[0] = tie(mine, across[0])
     sibling = swap(mine, "head", 1)
-    outer = between_chips(add(shares[2], across[0]), TO_ENDS)
     late = [share_of(mine, sibling, turn) for turn in range(chips)]
-    late[0], end[2] = tie(late[0], end[2])
     end_high = [between_chips(late[0], TO_MIDDLE)]
+    late[1], ends, across[0] = tie(late[1], ends, across[0])
+    end_high.append(between_chips(late[1], TO_MIDDLE))
+    across.append(between_chips(add(shares[:, :columns], ends[:, :columns]), ACROSS))
+    outer = between_chips(add(shares[:, columns:], across[0]), TO_ENDS)
     passed = add(late[0], end_high[0])
-    late[1], passed, across[1], outer = tie(late[1], passed, across[1], outer)
+    late[2], passed, across[1], outer = tie(late[2], passed, across[1], outer)
     across_high = [between_chips(passed, ACROSS)]
-    end_high.append(between_chips(late[1], TO_MIDDLE))
-    first = add(shares[3], end[2], across[1], outer)
+    end_high.append(between_chips(late[2], TO_MIDDLE))
+    first = add(kept, ends[:, columns:], across[1], outer)
     passed = add(late[1], end_high[1])
-    late[2], passed, first = tie(late[2], passed, first)
     across_high.append(between_chips(passed, ACROSS))
-    end_high.append(between_chips(late[2], TO_MIDDLE))
     outer_high = between_chips(add(late[2], across_high[0]), TO_ENDS)
     second = add(late[3], end_high[2], across_high[1], outer_high)
     return jnp.concatenate([first, second], axis=0)

time: 161 us -> 146 us (0.907); the launches traced: 161 us -> 143 us
  waiting for transfers between devices: 69.3 us -> 57.3 us
  Pallas kernels: 38.4 us -> 30.1 us
  starting transfers between devices: 49.2 us -> 51.7 us
    ppermute x12 -> x11, waiting for transfers between devices: 45.7 us -> 22.4 us  [between_chips(): return lax.ppermute(value, 'head', both)]
    ppermute x15, waiting for transfers between devices: 23.5 us -> 34.9 us  [swap(): lax.ppermute(value, axis, [(source, source ^ distance) for source in rang...]
    pallas_call x2, Pallas kernels: 21.9 us -> 13.4 us  [attend(): pl.pallas_call(kernel, grid_spec=pltpu.PrefetchScalarGridSpec(num_scalar_...]
    ppermute x12 -> x11, starting transfers between devices: 34 us -> 36.4 us  [between_chips(): return lax.ppermute(value, 'head', both)]
    pallas_call x8 -> x7, Pallas kernels: 5.66 us -> 5.95 us  [project(): pl.pallas_call(kernel, grid=(count,), in_specs=[attended, attended, weigh...]
  transfers between devices with their start and end apart: 27 -> 26, of which waited for: 16 -> 12; matrix products, arithmetic and copies ran while one was open for 2% -> 2% of each run, Pallas kernels for 22% -> 19%
where the time goes in v5:
time: 146 us; the launch traced here: 143 us
  waiting for transfers between devices  57.3 us (39%)
  starting transfers between devices  51.7 us (35%)
  Pallas kernels  30.1 us (21%)
  other arithmetic  3.11 us (2%)
    ppermute x11, starting transfers between devices, between_chips(): return lax.ppermute(value, 'head', both)  36.4 us
    ppermute x15, waiting for transfers between devices, swap(): lax.ppermute(value, axis, [(source, source ^ distance) for source in rang...  34.9 us
    ppermute x11, waiting for transfers between devices, between_chips(): return lax.ppermute(value, 'head', both)  22.4 us
    ppermute x15, starting transfers between devices, swap(): lax.ppermute(value, axis, [(source, source ^ distance) for source in rang...  15.4 us
    pallas_call x2, Pallas kernels, attend(): pl.pallas_call(kernel, grid_spec=pltpu.PrefetchScalarGridSpec(num_scalar_...  13.4 us
    pallas_call x7, Pallas kernels, project(): pl.pallas_call(kernel, grid=(count,), in_specs=[attended, attended, weigh...  5.95 us
    pallas_call x1, Pallas kernels, pack_projection(): pl.pallas_call(kernel, grid_spec=pltpu.PrefetchScalarGridSpec(num_scalar_...  5.45 us
    pallas_call x2, Pallas kernels, pack(): pl.pallas_call(kernel, grid_spec=pltpu.PrefetchScalarGridSpec(num_scalar_...  5.15 us
  transfers between devices with their start and end apart: 26, of which 12 were waited for; matrix products, arithmetic and copies ran while one was open for 2% of the time, Pallas kernels for 19%

profile of v5, /device:TPU:0, one launch (start us, length us, event | category | flops | bytes accessed | tf_op | source)
XLA Modules:
  0.0 143.3 jit_solution(16117752722753636902)
XLA Ops:
  0.0 2.5 %pack.3 = (bf16[1552,128]{1,0:T(8,128)(2,1)}, bf16[1552,128]{1,0:T(8,128)(2,1)}, bf16[1552,128]{1,0:T(8,128)(2,1)}) custom-call(s32[1]{0:T(128)} %bitcast.ctx_ref, bf16[1024,512]{1,0:T(8,128)(2,1)} %refs_3_.5, bf16[1024,512]{1,0:T(8,128)(2,1)} %refs_4_.5, bf16[1024,512]{1,0:T(8,128)(2,1)} %refs_5_.5, bf16[1024,512]{1,0:T(8,128)(2,1)} %refs_3_.5, ...), custom_call_target="tpu_custom_call" | custom-call | flops 1024 | bytes 1024 | tf_op jit(solution)/shard_map/pack/pallas_call | solution.py:201
  2.5 2.9 %collective-permute-start = (bf16[1552,128]{1,0:T(8,128)(2,1)}, bf16[1552,128]{1,0:T(8,128)(2,1)S(1)}, u32[]{:S(2)}, u32[]{:S(2)}) collective-permute-start(bf16[1552,128]{1,0:T(8,128)(2,1)} %get-tuple-element.58), channel_id=1, source_target_pairs={{0,8},{8,0},{16,24},{24,16},{1,9},{9,1},{17,25},{25,17},{2,10},{10... | collective-permute-start | bytes 1191944 | tf_op jit(solution)/shard_map/ppermute | solution.py:450
  5.4 1.5 %collective-permute-start.1 = (bf16[1552,128]{1,0:T(8,128)(2,1)}, bf16[1552,128]{1,0:T(8,128)(2,1)S(1)}, u32[]{:S(2)}, u32[]{:S(2)}) collective-permute-start(bf16[1552,128]{1,0:T(8,128)(2,1)} %get-tuple-element.59), channel_id=1, source_target_pairs={{0,16},{8,24},{16,0},{24,8},{1,17},{9,25},{17,1},{25,9},{2,18},{10... | collective-permute-start | bytes 1191944 | tf_op jit(solution)/shard_map/ppermute | solution.py:450
  7.0 0.7 dynamic-slice_bitcast_fusion
  7.6 0.6 pad_add_fusion.places_ref
  8.2 5.4 %pack_projection.1 = (bf16[512,2048]{1,0:T(8,128)(2,1)}, bf16[512,2048]{1,0:T(8,128)(2,1)}) custom-call(s32[5]{0:T(128)} %pad_add_fusion.places_ref, bf16[512,4096]{1,0:T(8,128)(2,1)} %give_in.1, bf16[512,4096]{1,0:T(8,128)(2,1)} %give_in.1), custom_call_target="tpu_custom_call" | custom-call | flops 1024 | bytes 1024 | tf_op jit(solution)/shard_map/pack_projection/pallas_call | solution.py:232
  13.7 2.0 %collective-permute-done.refs_4_.refs_7_ = bf16[1552,128]{1,0:T(8,128)(2,1)S(1)} collective-permute-done((bf16[1552,128]{1,0:T(8,128)(2,1)}, bf16[1552,128]{1,0:T(8,128)(2,1)S(1)}, u32[]{:S(2)}, u32[]{:S(2)}) %collective-permute-start) | collective-permute-done | bytes 397344 | tf_op jit(solution)/shard_map/ppermute | solution.py:450
  15.7 9.1 %collective-permute-done.1.refs_5_.refs_8_ = bf16[1552,128]{1,0:T(8,128)(2,1)S(1)} collective-permute-done((bf16[1552,128]{1,0:T(8,128)(2,1)}, bf16[1552,128]{1,0:T(8,128)(2,1)S(1)}, u32[]{:S(2)}, u32[]{:S(2)}) %collective-permute-start.1) | collective-permute-done | bytes 397344 | tf_op jit(solution)/shard_map/ppermute | solution.py:450
  24.8 0.0 copy-start.4
  24.8 0.1 collective-permute-start.10
  24.9 2.7 %pack.2 = (bf16[1536,128]{1,0:T(8,128)(2,1)}, bf16[1536,128]{1,0:T(8,128)(2,1)}, bf16[1536,128]{1,0:T(8,128)(2,1)}) custom-call(s32[1]{0:T(128)} %bitcast.ctx_ref, bf16[1024,512]{1,0:T(8,128)(2,1)} %refs_3_.5, bf16[1024,512]{1,0:T(8,128)(2,1)} %refs_4_.5, bf16[1024,512]{1,0:T(8,128)(2,1)} %refs_5_.5, bf16[1024,512]{1,0:T(8,128)(2,1)} %refs_3_.5, ...), custom_call_target="tpu_custom_call" | custom-call | flops 1024 | bytes 1024 | tf_op jit(solution)/shard_map/pack/pallas_call | solution.py:201
  27.6 1.2 collective-permute-start.6
  28.8 0.8 collective-permute-start.7
  29.7 5.2 %attend_low.1 = (bf16[512,128]{1,0:T(8,128)(2,1)S(1)}, bf16[512,128]{1,0:T(8,128)(2,1)S(1)}, bf16[512,128]{1,0:T(8,128)(2,1)S(1)}, bf16[512,128]{1,0:T(8,128)(2,1)S(1)}) custom-call(s32[1]{0:T(128)} %bitcast.ctx_ref, bf16[1024,512]{1,0:T(8,128)(2,1)S(1)} %copy-done.1, bf16[1024,512]{1,0:T(8,128)(2,1)S(1)} %copy-done.2, bf16[1024,512]{1,0:T(8,128)(2,1)S(1)} %copy-done.3, ...), custom_call_target="tpu_custom_call" | custom-call | flops 1024 | bytes 1024 | tf_op jit(solution)/shard_map/attend_low/pallas_call | solution.py:380
  34.8 1.5 %collective-permute-start.3 = (bf16[512,128]{1,0:T(8,128)(2,1)S(1)}, bf16[512,128]{1,0:T(8,128)(2,1)S(1)}, u32[]{:S(2)}, u32[]{:S(2)}) collective-permute-start(bf16[512,128]{1,0:T(8,128)(2,1)S(1)} %get-tuple-element.68), channel_id=1, source_target_pairs={{0,8},{8,0},{16,24},{24,16},{1,9},{9,1},{17,25},{25,17},{2,10},{10... | collective-permute-start | bytes 393224 | tf_op jit(solution)/shard_map/ppermute | solution.py:450
  36.4 0.5 collective-permute-start.4
  36.9 5.1 %collective-permute-done.3.refs_1_ = bf16[512,128]{1,0:T(8,128)(2,1)S(1)} collective-permute-done((bf16[512,128]{1,0:T(8,128)(2,1)S(1)}, bf16[512,128]{1,0:T(8,128)(2,1)S(1)}, u32[]{:S(2)}, u32[]{:S(2)}) %collective-permute-start.3) | collective-permute-done | bytes 131104 | tf_op jit(solution)/shard_map/ppermute | solution.py:450
  42.0 1.5 %collective-permute-start.5 = (bf16[512,128]{1,0:T(8,128)(2,1)S(1)}, bf16[512,128]{1,0:T(8,128)(2,1)S(1)}, u32[]{:S(2)}, u32[]{:S(2)}) collective-permute-start(bf16[512,128]{1,0:T(8,128)(2,1)S(1)} %get-tuple-element.70), channel_id=1, source_target_pairs={{0,24},{8,16},{16,8},{24,0},{1,25},{9,17},{17,9},{25,1},{2,26},{10... | collective-permute-start | bytes 393224 | tf_op jit(solution)/shard_map/ppermute | solution.py:450
  43.5 0.0 collective-permute-done.4.refs_2_
  43.5 4.4 %collective-permute-done.5.refs_3_ = bf16[512,128]{1,0:T(8,128)(2,1)S(1)} collective-permute-done((bf16[512,128]{1,0:T(8,128)(2,1)S(1)}, bf16[512,128]{1,0:T(8,128)(2,1)S(1)}, u32[]{:S(2)}, u32[]{:S(2)}) %collective-permute-start.5) | collective-permute-done | bytes 131104 | tf_op jit(solution)/shard_map/ppermute | solution.py:450
  47.8 0.0 collective-permute-done.6.refs_10_
  47.8 0.1 assemble.2.mine_ref
  47.9 0.1 collective-permute-start.9
  48.0 1.9 %collective-permute-done.9.sibling_ref = bf16[512,512]{1,0:T(8,128)(2,1)S(1)} collective-permute-done((bf16[512,512]{1,0:T(8,128)(2,1)S(1)}, bf16[512,512]{1,0:T(8,128)(2,1)S(1)}, u32[]{:S(2)}, u32[]{:S(2)}) %collective-permute-start.9) | collective-permute-done | bytes 524320 | tf_op jit(solution)/shard_map/ppermute | solution.py:450
  49.9 0.7 project.7
  50.6 3.5 %collective-permute-start.14 = (bf16[512,512]{1,0:T(8,128)(2,1)S(1)}, bf16[512,512]{1,0:T(8,128)(2,1)S(1)}, u32[]{:S(2)}, u32[]{:S(2)}) collective-permute-start(bf16[512,512]{1,0:T(8,128)(2,1)S(1)} %project.7), channel_id=1, source_target_pairs={{0,2},{1,3},{6,4},{7,5},{8,10},{9,11},{14,12},{15,13},{16,18},{17,... | collective-permute-start | bytes 1572872 | tf_op jit(solution)/shard_map/ppermute | solution.py:455
  54.2 1.6 %collective-permute-start.8 = (bf16[1536,128]{1,0:T(8,128)(2,1)S(1)}, bf16[1536,128]{1,0:T(8,128)(2,1)S(1)}, u32[]{:S(2)}, u32[]{:S(2)}) collective-permute-start(bf16[1536,128]{1,0:T(8,128)(2,1)S(1)} %copy-done.5), channel_id=1, source_target_pairs={{0,24},{8,16},{16,8},{24,0},{1,25},{9,17},{17,9},{25,1},{2,26},{10... | collective-permute-start | bytes 1179656 | tf_op jit(solution)/shard_map/ppermute | solution.py:450
  55.7 1.7 %project.8 = bf16[512,1024]{1,0:T(8,128)(2,1)S(1)} custom-call(bf16[512,512]{1,0:T(8,128)(2,1)S(1)} %assemble.2.mine_ref, bf16[512,512]{1,0:T(8,128)(2,1)S(1)} %collective-permute-done.9.sibling_ref, bf16[512,2048]{1,0:T(8,128)(2,1)S(1)} %copy-done, bf16[512,2048]{1,0:T(8,128)(2,1)S(1)} %collective-permute-done.10.w_sibling_ref), custom_call_target="tpu_custom_call" | custom-call | flops 1024 | bytes 1024 | tf_op jit(solution)/shard_map/project/pallas_call | solution.py:436
  57.4 1.4 collective-permute-start.16
  58.8 0.7 project.9
  59.5 6.5 %collective-permute-done.8.refs_12_ = bf16[1536,128]{1,0:T(8,128)(2,1)S(1)} collective-permute-done((bf16[1536,128]{1,0:T(8,128)(2,1)S(1)}, bf16[1536,128]{1,0:T(8,128)(2,1)S(1)}, u32[]{:S(2)}, u32[]{:S(2)}) %collective-permute-start.8) | collective-permute-done | bytes 393248 | tf_op jit(solution)/shard_map/ppermute | solution.py:450
  66.0 8.2 %attend_high.1 = (bf16[512,128]{1,0:T(8,128)(2,1)S(1)}, bf16[512,128]{1,0:T(8,128)(2,1)S(1)}, bf16[512,128]{1,0:T(8,128)(2,1)S(1)}, bf16[512,128]{1,0:T(8,128)(2,1)S(1)}) custom-call(s32[1]{0:T(128)} %bitcast.ctx_ref, bf16[1024,512]{1,0:T(8,128)(2,1)S(1)} %copy-done.1, bf16[1024,512]{1,0:T(8,128)(2,1)S(1)} %copy-done.2, bf16[1024,512]{1,0:T(8,128)(2,1)S(1)} %copy-done.3, ...), custom_call_target="tpu_custom_call" | custom-call | flops 1024 | bytes 1024 | tf_op jit(solution)/shard_map/attend_high/pallas_call | solution.py:380
  74.2 1.3 collective-permute-start.11
  75.5 0.8 collective-permute-start.12
  76.4 1.4 collective-permute-start.13
  77.8 0.1 add_convert_fusion.7
  77.9 2.6 %collective-permute-done.11.refs_1_ = bf16[512,128]{1,0:T(8,128)(2,1)S(1)} collective-permute-done((bf16[512,128]{1,0:T(8,128)(2,1)S(1)}, bf16[512,128]{1,0:T(8,128)(2,1)S(1)}, u32[]{:S(2)}, u32[]{:S(2)}) %collective-permute-start.11) | collective-permute-done | bytes 131104 | tf_op jit(solution)/shard_map/ppermute | solution.py:450
  80.5 2.1 %collective-permute-done.12.refs_2_ = bf16[512,128]{1,0:T(8,128)(2,1)S(1)} collective-permute-done((bf16[512,128]{1,0:T(8,128)(2,1)S(1)}, bf16[512,128]{1,0:T(8,128)(2,1)S(1)}, u32[]{:S(2)}, u32[]{:S(2)}) %collective-permute-start.12) | collective-permute-done | bytes 131104 | tf_op jit(solution)/shard_map/ppermute | solution.py:450
  82.7 0.1 assemble.3.mine_ref
  82.8 0.1 collective-permute-start.15
  82.8 0.7 collective-permute-start.17
  83.5 1.2 collective-permute-done.15.sibling_ref
  84.7 0.7 project.12
  85.5 3.5 %collective-permute-start.18 = (bf16[512,512]{1,0:T(8,128)(2,1)S(1)}, bf16[512,512]{1,0:T(8,128)(2,1)S(1)}, u32[]{:S(2)}, u32[]{:S(2)}) collective-permute-start(bf16[512,512]{1,0:T(8,128)(2,1)S(1)} %project.12), channel_id=1, source_target_pairs={{0,2},{1,3},{6,4},{7,5},{8,10},{9,11},{14,12},{15,13},{16,18},{17,... | collective-permute-start | bytes 1572872 | tf_op jit(solution)/shard_map/ppermute | solution.py:455
  88.9 0.7 project.10
  89.7 0.3 add_convert_fusion.4
  90.0 1.3 collective-permute-start.20
  91.3 0.7 collective-permute-start.19
  92.0 14.2 %collective-permute-start.22 = (bf16[512,512]{1,0:T(8,128)(2,1)S(1)}, bf16[512,512]{1,0:T(8,128)(2,1)S(1)}, u32[]{:S(2)}, u32[]{:S(2)}) collective-permute-start(bf16[512,512]{1,0:T(8,128)(2,1)S(1)} %project.10), channel_id=1, source_target_pairs={{0,2},{1,3},{6,4},{7,5},{8,10},{9,11},{14,12},{15,13},{16,18},{17,... | collective-permute-start | bytes 1572872 | tf_op jit(solution)/shard_map/ppermute | solution.py:455
  106.3 0.7 project.11
  107.0 0.1 add_convert_fusion.6
  107.1 5.2 %collective-permute-done.20 = bf16[512,512]{1,0:T(8,128)(2,1)S(1)} collective-permute-done((bf16[512,512]{1,0:T(8,128)(2,1)S(1)}, bf16[512,512]{1,0:T(8,128)(2,1)S(1)}, u32[]{:S(2)}, u32[]{:S(2)}) %collective-permute-start.20) | collective-permute-done | bytes 524320 | tf_op jit(solution)/shard_map/ppermute | solution.py:455
  112.4 0.7 collective-permute-start.24
  113.1 8.4 %collective-permute-start.21 = (bf16[512,512]{1,0:T(8,128)(2,1)S(1)}, bf16[512,512]{1,0:T(8,128)(2,1)S(1)}, u32[]{:S(2)}, u32[]{:S(2)}) collective-permute-start(bf16[512,512]{1,0:T(8,128)(2,1)S(1)} %project.11), channel_id=1, source_target_pairs={{0,2},{1,3},{6,4},{7,5},{8,10},{9,11},{14,12},{15,13},{16,18},{17,... | collective-permute-start | bytes 1572872 | tf_op jit(solution)/shard_map/ppermute | solution.py:455
  121.5 0.1 add_convert_fusion.2
  121.7 0.7 collective-permute-start.23
  122.4 0.1 add_convert_fusion.1
  122.5 1.3 collective-permute-start.25
  123.8 0.7 project.13
  124.5 0.3 add_convert_fusion.3
  124.9 6.5 %collective-permute-done.21 = bf16[512,512]{1,0:T(8,128)(2,1)S(1)} collective-permute-done((bf16[512,512]{1,0:T(8,128)(2,1)S(1)}, bf16[512,512]{1,0:T(8,128)(2,1)S(1)}, u32[]{:S(2)}, u32[]{:S(2)}) %collective-permute-start.21) | collective-permute-done | bytes 524320 | tf_op jit(solution)/shard_map/ppermute | solution.py:455
  131.3 10.6 %collective-permute-done.25 = bf16[512,512]{1,0:T(8,128)(2,1)S(1)} collective-permute-done((bf16[512,512]{1,0:T(8,128)(2,1)S(1)}, bf16[512,512]{1,0:T(8,128)(2,1)S(1)}, u32[]{:S(2)}, u32[]{:S(2)}) %collective-permute-start.25) | collective-permute-done | bytes 524320 | tf_op jit(solution)/shard_map/ppermute | solution.py:455
  142.0 0.3 add_convert_fusion
  142.3 1.0 pad_maximum_fusion
  (24 shorter events, 0.1 us)
Async XLA Ops:
  2.5 13.2 %collective-permute-start = (bf16[1552,128]{1,0:T(8,128)(2,1)}, bf16[1552,128]{1,0:T(8,128)(2,1)S(1)}, u32[]{:S(2)}, u32[]{:S(2)}) collective-permute-start(bf16[1552,128]{1,0:T(8,128)(2,1)} %get-tuple-element.58), channel_id=1, source_target_pairs={{0,8},{8,0},{16,24},{24,16},{1,9},{9,1},{17,25},{25,17},{2,10},{10... | collective-permute-start | bytes 1191944 | tf_op jit(solution)/shard_map/ppermute | solution.py:450
  5.4 19.4 %collective-permute-start.1 = (bf16[1552,128]{1,0:T(8,128)(2,1)}, bf16[1552,128]{1,0:T(8,128)(2,1)S(1)}, u32[]{:S(2)}, u32[]{:S(2)}) collective-permute-start(bf16[1552,128]{1,0:T(8,128)(2,1)} %get-tuple-element.59), channel_id=1, source_target_pairs={{0,16},{8,24},{16,0},{24,8},{1,17},{9,25},{17,1},{25,9},{2,18},{10... | collective-permute-start | bytes 1191944 | tf_op jit(solution)/shard_map/ppermute | solution.py:450
  7.0 17.9 %collective-permute-start.2 = (bf16[1552,128]{1,0:T(8,128)(2,1)}, bf16[1552,128]{1,0:T(8,128)(2,1)S(1)}, u32[]{:S(2)}, u32[]{:S(2)}) collective-permute-start(bf16[1552,128]{1,0:T(8,128)(2,1)} %get-tuple-element.60), channel_id=1, source_target_pairs={{0,24},{8,16},{16,8},{24,0},{1,25},{9,17},{17,9},{25,1},{2,26},{10... | collective-permute-start | bytes 1191944 | tf_op jit(solution)/shard_map/ppermute | solution.py:450
  24.8 4.8 %copy-start.1 = (bf16[1024,512]{1,0:T(8,128)(2,1)S(1)}, bf16[1024,512]{1,0:T(8,128)(2,1)}, u32[]{:S(2)}) copy-start(bf16[1024,512]{1,0:T(8,128)(2,1)} %refs_3_.5) | copy-start | bytes 3145732
  24.8 4.8 %copy-start.2 = (bf16[1024,512]{1,0:T(8,128)(2,1)S(1)}, bf16[1024,512]{1,0:T(8,128)(2,1)}, u32[]{:S(2)}) copy-start(bf16[1024,512]{1,0:T(8,128)(2,1)} %refs_4_.5) | copy-start | bytes 3145732
  24.8 4.8 %copy-start.3 = (bf16[1024,512]{1,0:T(8,128)(2,1)S(1)}, bf16[1024,512]{1,0:T(8,128)(2,1)}, u32[]{:S(2)}) copy-start(bf16[1024,512]{1,0:T(8,128)(2,1)} %refs_5_.5) | copy-start | bytes 3145732
  24.8 4.8 %copy-start.4 = (s32[1024]{0:T(1024)S(1)}, s32[1024]{0:T(1024)}, u32[]{:S(2)}) copy-start(s32[1024]{0:T(1024)} %param.9) | copy-start | bytes 12292
  24.8 25.1 %collective-permute-start.10 = (bf16[512,2048]{1,0:T(8,128)(2,1)}, bf16[512,2048]{1,0:T(8,128)(2,1)S(1)}, u32[]{:S(2)}, u32[]{:S(2)}) collective-permute-start(bf16[512,2048]{1,0:T(8,128)(2,1)} %get-tuple-element.83), channel_id=1, source_target_pairs={{0,1},{1,0},{2,3},{3,2},{4,5},{5,4},{6,7},{7,6},{8,9},{9,8},{10,11... | collective-permute-start | bytes 6291464 | tf_op jit(solution)/shard_map/ppermute | solution.py:450
  27.6 22.3 %copy-start = (bf16[512,2048]{1,0:T(8,128)(2,1)S(1)}, bf16[512,2048]{1,0:T(8,128)(2,1)}, u32[]{:S(2)}) copy-start(bf16[512,2048]{1,0:T(8,128)(2,1)} %get-tuple-element.82.w_mine_ref) | copy-start | bytes 6291460
  27.6 20.3 %collective-permute-start.6 = (bf16[1536,128]{1,0:T(8,128)(2,1)}, bf16[1536,128]{1,0:T(8,128)(2,1)S(1)}, u32[]{:S(2)}, u32[]{:S(2)}) collective-permute-start(bf16[1536,128]{1,0:T(8,128)(2,1)} %get-tuple-element.71), channel_id=1, source_target_pairs={{0,8},{8,0},{16,24},{24,16},{1,9},{9,1},{17,25},{25,17},{2,10},{10... | collective-permute-start | bytes 1179656 | tf_op jit(solution)/shard_map/ppermute | solution.py:450
  28.8 19.0 %collective-permute-start.7 = (bf16[1536,128]{1,0:T(8,128)(2,1)}, bf16[1536,128]{1,0:T(8,128)(2,1)S(1)}, u32[]{:S(2)}, u32[]{:S(2)}) collective-permute-start(bf16[1536,128]{1,0:T(8,128)(2,1)} %get-tuple-element.72), channel_id=1, source_target_pairs={{0,16},{8,24},{16,0},{24,8},{1,17},{9,25},{17,1},{25,9},{2,18},{10... | collective-permute-start | bytes 1179656 | tf_op jit(solution)/shard_map/ppermute | solution.py:450
  34.8 7.2 %collective-permute-start.3 = (bf16[512,128]{1,0:T(8,128)(2,1)S(1)}, bf16[512,128]{1,0:T(8,128)(2,1)S(1)}, u32[]{:S(2)}, u32[]{:S(2)}) collective-permute-start(bf16[512,128]{1,0:T(8,128)(2,1)S(1)} %get-tuple-element.68), channel_id=1, source_target_pairs={{0,8},{8,0},{16,24},{24,16},{1,9},{9,1},{17,25},{25,17},{2,10},{10... | collective-permute-start | bytes 393224 | tf_op jit(solution)/shard_map/ppermute | solution.py:450
  36.4 7.1 %collective-permute-start.4 = (bf16[512,128]{1,0:T(8,128)(2,1)S(1)}, bf16[512,128]{1,0:T(8,128)(2,1)S(1)}, u32[]{:S(2)}, u32[]{:S(2)}) collective-permute-start(bf16[512,128]{1,0:T(8,128)(2,1)S(1)} %get-tuple-element.69), channel_id=1, source_target_pairs={{0,16},{8,24},{16,0},{24,8},{1,17},{9,25},{17,1},{25,9},{2,18},{10... | collective-permute-start | bytes 393224 | tf_op jit(solution)/shard_map/ppermute | solution.py:450
  42.0 5.9 %collective-permute-start.5 = (bf16[512,128]{1,0:T(8,128)(2,1)S(1)}, bf16[512,128]{1,0:T(8,128)(2,1)S(1)}, u32[]{:S(2)}, u32[]{:S(2)}) collective-permute-start(bf16[512,128]{1,0:T(8,128)(2,1)S(1)} %get-tuple-element.70), channel_id=1, source_target_pairs={{0,24},{8,16},{16,8},{24,0},{1,25},{9,17},{17,9},{25,1},{2,26},{10... | collective-permute-start | bytes 393224 | tf_op jit(solution)/shard_map/ppermute | solution.py:450
  47.9 2.0 %collective-permute-start.9 = (bf16[512,512]{1,0:T(8,128)(2,1)S(1)}, bf16[512,512]{1,0:T(8,128)(2,1)S(1)}, u32[]{:S(2)}, u32[]{:S(2)}) collective-permute-start(bf16[512,512]{1,0:T(8,128)(2,1)S(1)} %assemble.2.mine_ref), channel_id=1, source_target_pairs={{0,1},{1,0},{2,3},{3,2},{4,5},{5,4},{6,7},{7,6},{8,9},{9,8},{10,11... | collective-permute-start | bytes 1572872 | tf_op jit(solution)/shard_map/ppermute | solution.py:450
  49.9 4.2 %copy-start.5 = (bf16[1536,128]{1,0:T(8,128)(2,1)S(1)}, bf16[1536,128]{1,0:T(8,128)(2,1)}, u32[]{:S(2)}) copy-start(bf16[1536,128]{1,0:T(8,128)(2,1)} %get-tuple-element.77) | copy-start | bytes 1179652
  50.6 27.2 %collective-permute-start.14 = (bf16[512,512]{1,0:T(8,128)(2,1)S(1)}, bf16[512,512]{1,0:T(8,128)(2,1)S(1)}, u32[]{:S(2)}, u32[]{:S(2)}) collective-permute-start(bf16[512,512]{1,0:T(8,128)(2,1)S(1)} %project.7), channel_id=1, source_target_pairs={{0,2},{1,3},{6,4},{7,5},{8,10},{9,11},{14,12},{15,13},{16,18},{17,... | collective-permute-start | bytes 1572872 | tf_op jit(solution)/shard_map/ppermute | solution.py:455
  54.2 11.8 %collective-permute-start.8 = (bf16[1536,128]{1,0:T(8,128)(2,1)S(1)}, bf16[1536,128]{1,0:T(8,128)(2,1)S(1)}, u32[]{:S(2)}, u32[]{:S(2)}) collective-permute-start(bf16[1536,128]{1,0:T(8,128)(2,1)S(1)} %copy-done.5), channel_id=1, source_target_pairs={{0,24},{8,16},{16,8},{24,0},{1,25},{9,17},{17,9},{25,1},{2,26},{10... | collective-permute-start | bytes 1179656 | tf_op jit(solution)/shard_map/ppermute | solution.py:450
  57.4 32.3 %collective-permute-start.16 = (bf16[512,1024]{1,0:T(8,128)(2,1)S(1)}, bf16[512,1024]{1,0:T(8,128)(2,1)S(1)}, u32[]{:S(2)}, u32[]{:S(2)}) collective-permute-start(bf16[512,1024]{1,0:T(8,128)(2,1)S(1)} %project.8), channel_id=1, source_target_pairs={{0,2},{1,3},{6,4},{7,5},{8,10},{9,11},{14,12},{15,13},{16,18},{17,... | collective-permute-start | bytes 3145736 | tf_op jit(solution)/shard_map/ppermute | solution.py:455
  74.2 6.3 %collective-permute-start.11 = (bf16[512,128]{1,0:T(8,128)(2,1)S(1)}, bf16[512,128]{1,0:T(8,128)(2,1)S(1)}, u32[]{:S(2)}, u32[]{:S(2)}) collective-permute-start(bf16[512,128]{1,0:T(8,128)(2,1)S(1)} %get-tuple-element.89), channel_id=1, source_target_pairs={{0,8},{8,0},{16,24},{24,16},{1,9},{9,1},{17,25},{25,17},{2,10},{10... | collective-permute-start | bytes 393224 | tf_op jit(solution)/shard_map/ppermute | solution.py:450
  75.5 7.1 %collective-permute-start.12 = (bf16[512,128]{1,0:T(8,128)(2,1)S(1)}, bf16[512,128]{1,0:T(8,128)(2,1)S(1)}, u32[]{:S(2)}, u32[]{:S(2)}) collective-permute-start(bf16[512,128]{1,0:T(8,128)(2,1)S(1)} %get-tuple-element.90), channel_id=1, source_target_pairs={{0,16},{8,24},{16,0},{24,8},{1,17},{9,25},{17,1},{25,9},{2,18},{10... | collective-permute-start | bytes 393224 | tf_op jit(solution)/shard_map/ppermute | solution.py:450
  76.4 6.3 %collective-permute-start.13 = (bf16[512,128]{1,0:T(8,128)(2,1)S(1)}, bf16[512,128]{1,0:T(8,128)(2,1)S(1)}, u32[]{:S(2)}, u32[]{:S(2)}) collective-permute-start(bf16[512,128]{1,0:T(8,128)(2,1)S(1)} %get-tuple-element.91), channel_id=1, source_target_pairs={{0,24},{8,16},{16,8},{24,0},{1,25},{9,17},{17,9},{25,1},{2,26},{10... | collective-permute-start | bytes 393224 | tf_op jit(solution)/shard_map/ppermute | solution.py:450
  82.8 2.0 %collective-permute-start.15 = (bf16[512,512]{1,0:T(8,128)(2,1)S(1)}, bf16[512,512]{1,0:T(8,128)(2,1)S(1)}, u32[]{:S(2)}, u32[]{:S(2)}) collective-permute-start(bf16[512,512]{1,0:T(8,128)(2,1)S(1)} %assemble.3.mine_ref), channel_id=1, source_target_pairs={{0,1},{1,0},{2,3},{3,2},{4,5},{5,4},{6,7},{7,6},{8,9},{9,8},{10,11... | collective-permute-start | bytes 1572872 | tf_op jit(solution)/shard_map/ppermute | solution.py:450
  82.8 6.8 %collective-permute-start.17 = (bf16[512,512]{1,0:T(8,128)(2,1)S(1)}, bf16[512,512]{1,0:T(8,128)(2,1)S(1)}, u32[]{:S(2)}, u32[]{:S(2)}) collective-permute-start(bf16[512,512]{1,0:T(8,128)(2,1)S(1)} %add_convert_fusion.7), channel_id=1, source_target_pairs={{2,4},{3,5},{4,2},{5,3},{10,12},{11,13},{12,10},{13,11},{18,20},{1... | collective-permute-start | bytes 1572872 | tf_op jit(solution)/shard_map/ppermute | solution.py:455
  85.5 21.5 %collective-permute-start.18 = (bf16[512,512]{1,0:T(8,128)(2,1)S(1)}, bf16[512,512]{1,0:T(8,128)(2,1)S(1)}, u32[]{:S(2)}, u32[]{:S(2)}) collective-permute-start(bf16[512,512]{1,0:T(8,128)(2,1)S(1)} %project.12), channel_id=1, source_target_pairs={{0,2},{1,3},{6,4},{7,5},{8,10},{9,11},{14,12},{15,13},{16,18},{17,... | collective-permute-start | bytes 1572872 | tf_op jit(solution)/shard_map/ppermute | solution.py:455
  90.0 22.4 %collective-permute-start.20 = (bf16[512,512]{1,0:T(8,128)(2,1)S(1)}, bf16[512,512]{1,0:T(8,128)(2,1)S(1)}, u32[]{:S(2)}, u32[]{:S(2)}) collective-permute-start(bf16[512,512]{1,0:T(8,128)(2,1)S(1)} %get-tuple-element.105), channel_id=1, source_target_pairs={{4,6},{5,7},{2,0},{3,1},{12,14},{13,15},{10,8},{11,9},{20,22},{21,... | collective-permute-start | bytes 1572872 | tf_op jit(solution)/shard_map/ppermute | solution.py:455
  91.3 21.1 %collective-permute-start.19 = (bf16[512,512]{1,0:T(8,128)(2,1)S(1)}, bf16[512,512]{1,0:T(8,128)(2,1)S(1)}, u32[]{:S(2)}, u32[]{:S(2)}) collective-permute-start(bf16[512,512]{1,0:T(8,128)(2,1)S(1)} %get-tuple-element.106), channel_id=1, source_target_pairs={{2,4},{3,5},{4,2},{5,3},{10,12},{11,13},{12,10},{13,11},{18,20},{1... | collective-permute-start | bytes 1572872 | tf_op jit(solution)/shard_map/ppermute | solution.py:455
  92.0 29.5 %collective-permute-start.22 = (bf16[512,512]{1,0:T(8,128)(2,1)S(1)}, bf16[512,512]{1,0:T(8,128)(2,1)S(1)}, u32[]{:S(2)}, u32[]{:S(2)}) collective-permute-start(bf16[512,512]{1,0:T(8,128)(2,1)S(1)} %project.10), channel_id=1, source_target_pairs={{0,2},{1,3},{6,4},{7,5},{8,10},{9,11},{14,12},{15,13},{16,18},{17,... | collective-permute-start | bytes 1572872 | tf_op jit(solution)/shard_map/ppermute | solution.py:455
  112.4 10.0 %collective-permute-start.24 = (bf16[512,512]{1,0:T(8,128)(2,1)S(1)}, bf16[512,512]{1,0:T(8,128)(2,1)S(1)}, u32[]{:S(2)}, u32[]{:S(2)}) collective-permute-start(bf16[512,512]{1,0:T(8,128)(2,1)S(1)} %add_convert_fusion.6), channel_id=1, source_target_pairs={{2,4},{3,5},{4,2},{5,3},{10,12},{11,13},{12,10},{13,11},{18,20},{1... | collective-permute-start | bytes 1572872 | tf_op jit(solution)/shard_map/ppermute | solution.py:455
  113.1 18.3 %collective-permute-start.21 = (bf16[512,512]{1,0:T(8,128)(2,1)S(1)}, bf16[512,512]{1,0:T(8,128)(2,1)S(1)}, u32[]{:S(2)}, u32[]{:S(2)}) collective-permute-start(bf16[512,512]{1,0:T(8,128)(2,1)S(1)} %project.11), channel_id=1, source_target_pairs={{0,2},{1,3},{6,4},{7,5},{8,10},{9,11},{14,12},{15,13},{16,18},{17,... | collective-permute-start | bytes 1572872 | tf_op jit(solution)/shard_map/ppermute | solution.py:455
  121.7 9.7 %collective-permute-start.23 = (bf16[512,512]{1,0:T(8,128)(2,1)S(1)}, bf16[512,512]{1,0:T(8,128)(2,1)S(1)}, u32[]{:S(2)}, u32[]{:S(2)}) collective-permute-start(bf16[512,512]{1,0:T(8,128)(2,1)S(1)} %add_convert_fusion.2), channel_id=1, source_target_pairs={{2,4},{3,5},{4,2},{5,3},{10,12},{11,13},{12,10},{13,11},{18,20},{1... | collective-permute-start | bytes 1572872 | tf_op jit(solution)/shard_map/ppermute | solution.py:455
  122.5 19.5 %collective-permute-start.25 = (bf16[512,512]{1,0:T(8,128)(2,1)S(1)}, bf16[512,512]{1,0:T(8,128)(2,1)S(1)}, u32[]{:S(2)}, u32[]{:S(2)}) collective-permute-start(bf16[512,512]{1,0:T(8,128)(2,1)S(1)} %add_convert_fusion.1), channel_id=1, source_target_pairs={{4,6},{5,7},{2,0},{3,1},{12,14},{13,15},{10,8},{11,9},{20,22},{21,... | collective-permute-start | bytes 1572872 | tf_op jit(solution)/shard_map/ppermute | solution.py:455

commit v6 on v5

--- a/solution.py
+++ b/solution.py
@@ -486,12 +486,13 @@
     near = range(1, group)
 
     low_out = pack(ctx_index, 0, queries, keys, values, docs)
+    low_out, later = tie(low_out, (queries, keys, values))
     low = [swap(low_out[distance - 1], "ctx", distance) for distance in near]
+    high_out = pack(ctx_index, 1, *later, None)
+    high_out, w_out = tie(high_out, w_out)
     w_mine, w_give = pack_projection(places, w_out, chips)
-    low, w_give = tie(low, w_give)
+    high_out, low, w_give = tie(high_out, low, w_give)
     w_sibling = swap(w_give, "head", 1)
-    high_out = pack(ctx_index, 1, queries, keys, values, None)
-    high_out, low = tie(high_out, low)
     high = [swap(high_out[0], "ctx", 1), swap(high_out[1], "ctx", 2)]
 
     def send_back(pieces):
@@ -501,8 +502,8 @@
         return project(mine, sibling, w_mine, w_sibling, turn, count, chips)
 
     pieces = attend(ctx_index, queries, keys, values, docs, low, None)
+    pieces, diagonal_out, w_sibling = tie(pieces, high_out[2], w_sibling)
     back = send_back(pieces)
-    pieces, diagonal_out = tie(pieces, high_out[2])
     back, high = tie(back, high)
     high.append(swap(diagonal_out, "ctx", 3))
     mine = assemble(ctx_index, [pieces[0], *back])
@@ -511,6 +512,7 @@
     shares = share_of(mine, sibling, 1, 2)
     kept = share_of(mine, sibling, 3)
     end = between_chips(share, TO_MIDDLE)
+    shares, high[2] = tie(shares, high[2])
     ends = between_chips(shares, TO_MIDDLE)
 
     high, share, shares, kept = tie(high, share, shares, kept)
@@ -518,24 +520,27 @@
     back = send_back(pieces)
     passed = add(share, end)
     back, passed = tie(back, passed)
-    across = [between_chips(passed, ACROSS)]
+    across = between_chips(passed, ACROSS)
     mine = assemble(ctx_index, [pieces[0], *back])
     sibling = swap(mine, "head", 1)
     late = [share_of(mine, sibling, turn) for turn in range(chips)]
     end_high = [between_chips(late[0], TO_MIDDLE)]
-    late[1], ends, across[0] = tie(late[1], ends, across[0])
+    late[1], ends, across = tie(late[1], ends, across)
     end_high.append(between_chips(late[1], TO_MIDDLE))
-    across.append(between_chips(add(shares[:, :columns], ends[:, :columns]), ACROSS))
-    outer = between_chips(add(shares[:, columns:], across[0]), TO_ENDS)
+    across_second = between_chips(add(shares[:, :columns], ends[:, :columns]), ACROSS)
     passed = add(late[0], end_high[0])
-    late[2], passed, across[1], outer = tie(late[2], passed, across[1], outer)
-    across_high = [between_chips(passed, ACROSS)]
+    late[2], passed = tie(late[2], passed)
+    across_high = between_chips(passed, ACROSS)
+    outer = between_chips(add(shares[:, columns:], across), TO_ENDS)
     end_high.append(between_chips(late[2], TO_MIDDLE))
-    first = add(kept, ends[:, columns:], across[1], outer)
     passed = add(late[1], end_high[1])
-    across_high.append(between_chips(passed, ACROSS))
-    outer_high = between_chips(add(late[2], across_high[0]), TO_ENDS)
-    second = add(late[3], end_high[2], across_high[1], outer_high)
+    passed, across_second = tie(passed, across_second)
+    across_high_second = between_chips(passed, ACROSS)
+    passed = add(late[2], across_high)
+    passed, outer = tie(passed, outer)
+    outer_high = between_chips(passed, TO_ENDS)
+    first = add(kept, ends[:, columns:], across_second, outer)
+    second = add(late[3], end_high[2], across_high_second, outer_high)
     return jnp.concatenate([first, second], axis=0)
 
 

time: 146 us -> 140 us (0.959)
  starting transfers between devices: 51.7 us -> 45.4 us
    ppermute x11, starting transfers between devices: 36.4 us -> 29.7 us  [between_chips(): return lax.ppermute(value, 'head', both)]
    ppermute x11, waiting for transfers between devices: 22.4 us -> 26.4 us  [between_chips(): return lax.ppermute(value, 'head', both)]
    ppermute x15, waiting for transfers between devices: 34.9 us -> 31.7 us  [swap(): lax.ppermute(value, axis, [(source, source ^ distance) for source in rang...]
  transfers between devices with their start and end apart: 26 -> 26, of which waited for: 12 -> 15; matrix products, arithmetic and copies ran while one was open for 2% -> 2% of each run, Pallas kernels for 19% -> 20%
where the time goes in v6:
time: 140 us; the launch traced here: 138 us
  waiting for transfers between devices  58 us (41%)
  starting transfers between devices  45.4 us (32%)
  Pallas kernels  30.4 us (22%)
  other arithmetic  3.18 us (2%)
    ppermute x15, waiting for transfers between devices, swap(): lax.ppermute(value, axis, [(source, source ^ distance) for source in rang...  31.7 us
    ppermute x11, starting transfers between devices, between_chips(): return lax.ppermute(value, 'head', both)  29.7 us
    ppermute x11, waiting for transfers between devices, between_chips(): return lax.ppermute(value, 'head', both)  26.4 us
    ppermute x15, starting transfers between devices, swap(): lax.ppermute(value, axis, [(source, source ^ distance) for source in rang...  15.7 us
    pallas_call x2, Pallas kernels, attend(): pl.pallas_call(kernel, grid_spec=pltpu.PrefetchScalarGridSpec(num_scalar_...  13.4 us
    pallas_call x7, Pallas kernels, project(): pl.pallas_call(kernel, grid=(count,), in_specs=[attended, attended, weigh...  5.92 us
    pallas_call x1, Pallas kernels, pack_projection(): pl.pallas_call(kernel, grid_spec=pltpu.PrefetchScalarGridSpec(num_scalar_...  5.92 us
    pallas_call x2, Pallas kernels, pack(): pl.pallas_call(kernel, grid_spec=pltpu.PrefetchScalarGridSpec(num_scalar_...  5.04 us
  transfers between devices with their start and end apart: 26, of which 15 were waited for; matrix products, arithmetic and copies ran while one was open for 2% of the time, Pallas kernels for 20%

profile of v6, /device:TPU:0, one launch (start us, length us, event | category | flops | bytes accessed | tf_op | source)
XLA Modules:
  0.0 138.0 jit_solution(10490876396340061792)
XLA Ops:
  0.0 2.5 %pack.2 = (bf16[1552,128]{1,0:T(8,128)(2,1)}, bf16[1552,128]{1,0:T(8,128)(2,1)}, bf16[1552,128]{1,0:T(8,128)(2,1)}) custom-call(s32[1]{0:T(128)} %bitcast.ctx_ref, bf16[1024,512]{1,0:T(8,128)(2,1)} %refs_3_.4, bf16[1024,512]{1,0:T(8,128)(2,1)} %refs_4_.4, bf16[1024,512]{1,0:T(8,128)(2,1)} %refs_5_.4, bf16[1024,512]{1,0:T(8,128)(2,1)} %refs_3_.4, ...), custom_call_target="tpu_custom_call" | custom-call | flops 1024 | bytes 1024 | tf_op jit(solution)/shard_map/pack/pallas_call | solution.py:201
  2.5 2.9 %collective-permute-start = (bf16[1552,128]{1,0:T(8,128)(2,1)}, bf16[1552,128]{1,0:T(8,128)(2,1)S(1)}, u32[]{:S(2)}, u32[]{:S(2)}) collective-permute-start(bf16[1552,128]{1,0:T(8,128)(2,1)} %get-tuple-element.82), channel_id=1, source_target_pairs={{0,8},{8,0},{16,24},{24,16},{1,9},{9,1},{17,25},{25,17},{2,10},{10... | collective-permute-start | bytes 1191944 | tf_op jit(solution)/shard_map/ppermute | solution.py:450
  5.5 1.5 %collective-permute-start.1 = (bf16[1552,128]{1,0:T(8,128)(2,1)}, bf16[1552,128]{1,0:T(8,128)(2,1)S(1)}, u32[]{:S(2)}, u32[]{:S(2)}) collective-permute-start(bf16[1552,128]{1,0:T(8,128)(2,1)} %get-tuple-element.83), channel_id=1, source_target_pairs={{0,16},{8,24},{16,0},{24,8},{1,17},{9,25},{17,1},{25,9},{2,18},{10... | collective-permute-start | bytes 1191944 | tf_op jit(solution)/shard_map/ppermute | solution.py:450
  7.0 2.5 %pack.3 = (bf16[1536,128]{1,0:T(8,128)(2,1)}, bf16[1536,128]{1,0:T(8,128)(2,1)}, bf16[1536,128]{1,0:T(8,128)(2,1)}) custom-call(s32[1]{0:T(128)} %bitcast.ctx_ref, bf16[1024,512]{1,0:T(8,128)(2,1)} %refs_3_.4, bf16[1024,512]{1,0:T(8,128)(2,1)} %refs_4_.4, bf16[1024,512]{1,0:T(8,128)(2,1)} %refs_5_.4, bf16[1024,512]{1,0:T(8,128)(2,1)} %refs_3_.4, ...), custom_call_target="tpu_custom_call" | custom-call | flops 1024 | bytes 1024 | tf_op jit(solution)/shard_map/pack/pallas_call | solution.py:201
  9.5 0.7 dynamic-slice_bitcast_fusion
  10.2 0.6 pad_add_fusion.places_ref
  10.8 0.0 copy-start.4
  10.8 5.9 %pack_projection.1 = (bf16[512,2048]{1,0:T(8,128)(2,1)}, bf16[512,2048]{1,0:T(8,128)(2,1)}) custom-call(s32[5]{0:T(128)} %pad_add_fusion.places_ref, bf16[512,4096]{1,0:T(8,128)(2,1)} %give_in, bf16[512,4096]{1,0:T(8,128)(2,1)} %give_in), custom_call_target="tpu_custom_call" | custom-call | flops 1024 | bytes 1024 | tf_op jit(solution)/shard_map/pack_projection/pallas_call | solution.py:232
  16.7 8.1 %collective-permute-done.1.refs_5_.refs_8_ = bf16[1552,128]{1,0:T(8,128)(2,1)S(1)} collective-permute-done((bf16[1552,128]{1,0:T(8,128)(2,1)}, bf16[1552,128]{1,0:T(8,128)(2,1)S(1)}, u32[]{:S(2)}, u32[]{:S(2)}) %collective-permute-start.1) | collective-permute-done | bytes 397344 | tf_op jit(solution)/shard_map/ppermute | solution.py:450
  24.9 1.3 collective-permute-start.7
  26.2 0.8 collective-permute-start.8
  27.0 5.1 %attend_low.1 = (bf16[512,128]{1,0:T(8,128)(2,1)S(1)}, bf16[512,128]{1,0:T(8,128)(2,1)S(1)}, bf16[512,128]{1,0:T(8,128)(2,1)S(1)}, bf16[512,128]{1,0:T(8,128)(2,1)S(1)}) custom-call(s32[1]{0:T(128)} %bitcast.ctx_ref, bf16[1024,512]{1,0:T(8,128)(2,1)S(1)} %copy-done.1, bf16[1024,512]{1,0:T(8,128)(2,1)S(1)} %copy-done.2, bf16[1024,512]{1,0:T(8,128)(2,1)S(1)} %copy-done.3, ...), custom_call_target="tpu_custom_call" | custom-call | flops 1024 | bytes 1024 | tf_op jit(solution)/shard_map/attend_low/pallas_call | solution.py:380
  32.2 1.5 %collective-permute-start.4 = (bf16[512,128]{1,0:T(8,128)(2,1)S(1)}, bf16[512,128]{1,0:T(8,128)(2,1)S(1)}, u32[]{:S(2)}, u32[]{:S(2)}) collective-permute-start(bf16[512,128]{1,0:T(8,128)(2,1)S(1)} %get-tuple-element.96), channel_id=1, source_target_pairs={{0,8},{8,0},{16,24},{24,16},{1,9},{9,1},{17,25},{25,17},{2,10},{10... | collective-permute-start | bytes 393224 | tf_op jit(solution)/shard_map/ppermute | solution.py:450
  33.7 0.5 collective-permute-start.5
  34.2 1.5 %collective-permute-start.6 = (bf16[512,128]{1,0:T(8,128)(2,1)S(1)}, bf16[512,128]{1,0:T(8,128)(2,1)S(1)}, u32[]{:S(2)}, u32[]{:S(2)}) collective-permute-start(bf16[512,128]{1,0:T(8,128)(2,1)S(1)} %get-tuple-element.98), channel_id=1, source_target_pairs={{0,24},{8,16},{16,8},{24,0},{1,25},{9,17},{17,9},{25,1},{2,26},{10... | collective-permute-start | bytes 393224 | tf_op jit(solution)/shard_map/ppermute | solution.py:450
  35.7 1.1 collective-permute-done.7.refs_10_
  36.8 1.3 collective-permute-done.8.refs_11_
  38.1 1.5 %collective-permute-done.4.refs_1_ = bf16[512,128]{1,0:T(8,128)(2,1)S(1)} collective-permute-done((bf16[512,128]{1,0:T(8,128)(2,1)S(1)}, bf16[512,128]{1,0:T(8,128)(2,1)S(1)}, u32[]{:S(2)}, u32[]{:S(2)}) %collective-permute-start.4) | collective-permute-done | bytes 131104 | tf_op jit(solution)/shard_map/ppermute | solution.py:450
  39.7 1.7 %collective-permute-done.5.refs_2_ = bf16[512,128]{1,0:T(8,128)(2,1)S(1)} collective-permute-done((bf16[512,128]{1,0:T(8,128)(2,1)S(1)}, bf16[512,128]{1,0:T(8,128)(2,1)S(1)}, u32[]{:S(2)}, u32[]{:S(2)}) %collective-permute-start.5) | collective-permute-done | bytes 131104 | tf_op jit(solution)/shard_map/ppermute | solution.py:450
  41.3 1.6 %collective-permute-done.6.refs_3_ = bf16[512,128]{1,0:T(8,128)(2,1)S(1)} collective-permute-done((bf16[512,128]{1,0:T(8,128)(2,1)S(1)}, bf16[512,128]{1,0:T(8,128)(2,1)S(1)}, u32[]{:S(2)}, u32[]{:S(2)}) %collective-permute-start.6) | collective-permute-done | bytes 131104 | tf_op jit(solution)/shard_map/ppermute | solution.py:450
  43.0 0.1 assemble.2.mine_ref
  43.1 0.1 collective-permute-start.9
  43.1 1.9 %collective-permute-done.9.sibling_ref = bf16[512,512]{1,0:T(8,128)(2,1)S(1)} collective-permute-done((bf16[512,512]{1,0:T(8,128)(2,1)S(1)}, bf16[512,512]{1,0:T(8,128)(2,1)S(1)}, u32[]{:S(2)}, u32[]{:S(2)}) %collective-permute-start.9) | collective-permute-done | bytes 524320 | tf_op jit(solution)/shard_map/ppermute | solution.py:450
  45.0 0.7 project.8
  45.8 3.5 %collective-permute-start.14 = (bf16[512,512]{1,0:T(8,128)(2,1)S(1)}, bf16[512,512]{1,0:T(8,128)(2,1)S(1)}, u32[]{:S(2)}, u32[]{:S(2)}) collective-permute-start(bf16[512,512]{1,0:T(8,128)(2,1)S(1)} %project.8), channel_id=1, source_target_pairs={{0,2},{1,3},{6,4},{7,5},{8,10},{9,11},{14,12},{15,13},{16,18},{17,... | collective-permute-start | bytes 1572872 | tf_op jit(solution)/shard_map/ppermute | solution.py:455
  49.3 1.8 %collective-permute-start.10 = (bf16[1536,128]{1,0:T(8,128)(2,1)S(1)}, bf16[1536,128]{1,0:T(8,128)(2,1)S(1)}, u32[]{:S(2)}, u32[]{:S(2)}) collective-permute-start(bf16[1536,128]{1,0:T(8,128)(2,1)S(1)} %copy-done.5), channel_id=1, source_target_pairs={{0,24},{8,16},{16,8},{24,0},{1,25},{9,17},{17,9},{25,1},{2,26},{10... | collective-permute-start | bytes 1179656 | tf_op jit(solution)/shard_map/ppermute | solution.py:450
  51.1 1.7 %project.7 = bf16[512,1024]{1,0:T(8,128)(2,1)S(1)} custom-call(bf16[512,512]{1,0:T(8,128)(2,1)S(1)} %assemble.2.mine_ref, bf16[512,512]{1,0:T(8,128)(2,1)S(1)} %collective-permute-done.9.sibling_ref, bf16[512,2048]{1,0:T(8,128)(2,1)S(1)} %copy-done, bf16[512,2048]{1,0:T(8,128)(2,1)S(1)} %collective-permute-done.3.w_sibling_ref), custom_call_target="tpu_custom_call" | custom-call | flops 1024 | bytes 1024 | tf_op jit(solution)/shard_map/project/pallas_call | solution.py:436
  52.8 8.3 %collective-permute-done.10.refs_12_ = bf16[1536,128]{1,0:T(8,128)(2,1)S(1)} collective-permute-done((bf16[1536,128]{1,0:T(8,128)(2,1)S(1)}, bf16[1536,128]{1,0:T(8,128)(2,1)S(1)}, u32[]{:S(2)}, u32[]{:S(2)}) %collective-permute-start.10) | collective-permute-done | bytes 393248 | tf_op jit(solution)/shard_map/ppermute | solution.py:450
  61.1 1.6 %collective-permute-start.16 = (bf16[512,1024]{1,0:T(8,128)(2,1)S(1)}, bf16[512,1024]{1,0:T(8,128)(2,1)S(1)}, u32[]{:S(2)}, u32[]{:S(2)}) collective-permute-start(bf16[512,1024]{1,0:T(8,128)(2,1)S(1)} %project.7), channel_id=1, source_target_pairs={{0,2},{1,3},{6,4},{7,5},{8,10},{9,11},{14,12},{15,13},{16,18},{17,... | collective-permute-start | bytes 3145736 | tf_op jit(solution)/shard_map/ppermute | solution.py:455
  62.7 0.7 project.9
  63.5 8.2 %attend_high.1 = (bf16[512,128]{1,0:T(8,128)(2,1)S(1)}, bf16[512,128]{1,0:T(8,128)(2,1)S(1)}, bf16[512,128]{1,0:T(8,128)(2,1)S(1)}, bf16[512,128]{1,0:T(8,128)(2,1)S(1)}) custom-call(s32[1]{0:T(128)} %bitcast.ctx_ref, bf16[1024,512]{1,0:T(8,128)(2,1)S(1)} %copy-done.1, bf16[1024,512]{1,0:T(8,128)(2,1)S(1)} %copy-done.2, bf16[1024,512]{1,0:T(8,128)(2,1)S(1)} %copy-done.3, ...), custom_call_target="tpu_custom_call" | custom-call | flops 1024 | bytes 1024 | tf_op jit(solution)/shard_map/attend_high/pallas_call | solution.py:380
  71.7 0.9 collective-permute-start.11
  72.6 1.5 %collective-permute-start.12 = (bf16[512,128]{1,0:T(8,128)(2,1)S(1)}, bf16[512,128]{1,0:T(8,128)(2,1)S(1)}, u32[]{:S(2)}, u32[]{:S(2)}) collective-permute-start(bf16[512,128]{1,0:T(8,128)(2,1)S(1)} %get-tuple-element.118), channel_id=1, source_target_pairs={{0,16},{8,24},{16,0},{24,8},{1,17},{9,25},{17,1},{25,9},{2,18},{10... | collective-permute-start | bytes 393224 | tf_op jit(solution)/shard_map/ppermute | solution.py:450
  74.1 1.2 collective-permute-start.13
  75.2 0.1 add_convert_fusion.7
  75.4 2.5 %collective-permute-done.11.refs_1_ = bf16[512,128]{1,0:T(8,128)(2,1)S(1)} collective-permute-done((bf16[512,128]{1,0:T(8,128)(2,1)S(1)}, bf16[512,128]{1,0:T(8,128)(2,1)S(1)}, u32[]{:S(2)}, u32[]{:S(2)}) %collective-permute-start.11) | collective-permute-done | bytes 131104 | tf_op jit(solution)/shard_map/ppermute | solution.py:450
  77.9 2.4 %collective-permute-done.12.refs_2_ = bf16[512,128]{1,0:T(8,128)(2,1)S(1)} collective-permute-done((bf16[512,128]{1,0:T(8,128)(2,1)S(1)}, bf16[512,128]{1,0:T(8,128)(2,1)S(1)}, u32[]{:S(2)}, u32[]{:S(2)}) %collective-permute-start.12) | collective-permute-done | bytes 131104 | tf_op jit(solution)/shard_map/ppermute | solution.py:450
  80.3 0.1 assemble.3.mine_ref
  80.4 0.1 collective-permute-start.15
  80.4 0.7 collective-permute-start.17
  81.1 1.2 collective-permute-done.15.sibling_ref
  82.3 0.7 project.12
  83.0 2.9 %collective-permute-start.20 = (bf16[512,512]{1,0:T(8,128)(2,1)S(1)}, bf16[512,512]{1,0:T(8,128)(2,1)S(1)}, u32[]{:S(2)}, u32[]{:S(2)}) collective-permute-start(bf16[512,512]{1,0:T(8,128)(2,1)S(1)} %project.12), channel_id=1, source_target_pairs={{0,2},{1,3},{6,4},{7,5},{8,10},{9,11},{14,12},{15,13},{16,18},{17,... | collective-permute-start | bytes 1572872 | tf_op jit(solution)/shard_map/ppermute | solution.py:455
  86.0 0.7 project.11
  86.7 0.7 project.10
  87.4 10.5 %collective-permute-start.18 = (bf16[512,512]{1,0:T(8,128)(2,1)S(1)}, bf16[512,512]{1,0:T(8,128)(2,1)S(1)}, u32[]{:S(2)}, u32[]{:S(2)}) collective-permute-start(bf16[512,512]{1,0:T(8,128)(2,1)S(1)} %project.10), channel_id=1, source_target_pairs={{0,2},{1,3},{6,4},{7,5},{8,10},{9,11},{14,12},{15,13},{16,18},{17,... | collective-permute-start | bytes 1572872 | tf_op jit(solution)/shard_map/ppermute | solution.py:455
  98.0 0.4 add_convert_fusion.5
  98.3 0.7 collective-permute-start.19
  99.1 0.1 add_convert_fusion.4
  99.2 0.7 collective-permute-start.21
  99.9 1.3 collective-permute-start.22
  101.2 5.8 %collective-permute-start.23 = (bf16[512,512]{1,0:T(8,128)(2,1)S(1)}, bf16[512,512]{1,0:T(8,128)(2,1)S(1)}, u32[]{:S(2)}, u32[]{:S(2)}) collective-permute-start(bf16[512,512]{1,0:T(8,128)(2,1)S(1)} %project.11), channel_id=1, source_target_pairs={{0,2},{1,3},{6,4},{7,5},{8,10},{9,11},{14,12},{15,13},{16,18},{17,... | collective-permute-start | bytes 1572872 | tf_op jit(solution)/shard_map/ppermute | solution.py:455
  107.0 3.3 %collective-permute-done.18 = bf16[512,512]{1,0:T(8,128)(2,1)S(1)} collective-permute-done((bf16[512,512]{1,0:T(8,128)(2,1)S(1)}, bf16[512,512]{1,0:T(8,128)(2,1)S(1)}, u32[]{:S(2)}, u32[]{:S(2)}) %collective-permute-start.18) | collective-permute-done | bytes 524320 | tf_op jit(solution)/shard_map/ppermute | solution.py:455
  110.3 0.1 add_convert_fusion.6
  110.4 0.7 collective-permute-start.24
  111.1 0.1 add_convert_fusion.3
  111.3 4.9 %collective-permute-done.22 = bf16[512,512]{1,0:T(8,128)(2,1)S(1)} collective-permute-done((bf16[512,512]{1,0:T(8,128)(2,1)S(1)}, bf16[512,512]{1,0:T(8,128)(2,1)S(1)}, u32[]{:S(2)}, u32[]{:S(2)}) %collective-permute-start.22) | collective-permute-done | bytes 524320 | tf_op jit(solution)/shard_map/ppermute | solution.py:455
  116.2 1.3 collective-permute-start.25
  117.5 0.7 project.13
  118.2 0.3 add_convert_fusion.1
  118.6 1.7 %collective-permute-done.23 = bf16[512,512]{1,0:T(8,128)(2,1)S(1)} collective-permute-done((bf16[512,512]{1,0:T(8,128)(2,1)S(1)}, bf16[512,512]{1,0:T(8,128)(2,1)S(1)}, u32[]{:S(2)}, u32[]{:S(2)}) %collective-permute-start.23) | collective-permute-done | bytes 524320 | tf_op jit(solution)/shard_map/ppermute | solution.py:455
  120.2 16.5 %collective-permute-done.25 = bf16[512,512]{1,0:T(8,128)(2,1)S(1)} collective-permute-done((bf16[512,512]{1,0:T(8,128)(2,1)S(1)}, bf16[512,512]{1,0:T(8,128)(2,1)S(1)}, u32[]{:S(2)}, u32[]{:S(2)}) %collective-permute-start.25) | collective-permute-done | bytes 524320 | tf_op jit(solution)/shard_map/ppermute | solution.py:455
  136.7 0.3 add_convert_fusion
  137.0 1.0 pad_maximum_fusion
  (28 shorter events, 0.1 us)
Async XLA Ops:
  2.5 14.2 %collective-permute-start = (bf16[1552,128]{1,0:T(8,128)(2,1)}, bf16[1552,128]{1,0:T(8,128)(2,1)S(1)}, u32[]{:S(2)}, u32[]{:S(2)}) collective-permute-start(bf16[1552,128]{1,0:T(8,128)(2,1)} %get-tuple-element.82), channel_id=1, source_target_pairs={{0,8},{8,0},{16,24},{24,16},{1,9},{9,1},{17,25},{25,17},{2,10},{10... | collective-permute-start | bytes 1191944 | tf_op jit(solution)/shard_map/ppermute | solution.py:450
  5.5 19.4 %collective-permute-start.1 = (bf16[1552,128]{1,0:T(8,128)(2,1)}, bf16[1552,128]{1,0:T(8,128)(2,1)S(1)}, u32[]{:S(2)}, u32[]{:S(2)}) collective-permute-start(bf16[1552,128]{1,0:T(8,128)(2,1)} %get-tuple-element.83), channel_id=1, source_target_pairs={{0,16},{8,24},{16,0},{24,8},{1,17},{9,25},{17,1},{25,9},{2,18},{10... | collective-permute-start | bytes 1191944 | tf_op jit(solution)/shard_map/ppermute | solution.py:450
  7.0 17.9 %collective-permute-start.2 = (bf16[1552,128]{1,0:T(8,128)(2,1)}, bf16[1552,128]{1,0:T(8,128)(2,1)S(1)}, u32[]{:S(2)}, u32[]{:S(2)}) collective-permute-start(bf16[1552,128]{1,0:T(8,128)(2,1)} %get-tuple-element.84), channel_id=1, source_target_pairs={{0,24},{8,16},{16,8},{24,0},{1,25},{9,17},{17,9},{25,1},{2,26},{10... | collective-permute-start | bytes 1191944 | tf_op jit(solution)/shard_map/ppermute | solution.py:450
  10.8 14.1 %copy-start.7 = (bf16[1536,128]{1,0:T(8,128)(2,1)S(1)}, bf16[1536,128]{1,0:T(8,128)(2,1)}, u32[]{:S(2)}) copy-start(bf16[1536,128]{1,0:T(8,128)(2,1)} %get-tuple-element.99) | copy-start | bytes 1179652
  10.8 15.4 %copy-start.6 = (bf16[1536,128]{1,0:T(8,128)(2,1)S(1)}, bf16[1536,128]{1,0:T(8,128)(2,1)}, u32[]{:S(2)}) copy-start(bf16[1536,128]{1,0:T(8,128)(2,1)} %get-tuple-element.100) | copy-start | bytes 1179652
  10.8 16.2 %copy-start.1 = (bf16[1024,512]{1,0:T(8,128)(2,1)S(1)}, bf16[1024,512]{1,0:T(8,128)(2,1)}, u32[]{:S(2)}) copy-start(bf16[1024,512]{1,0:T(8,128)(2,1)} %refs_3_.4) | copy-start | bytes 3145732
  10.8 16.2 %copy-start.2 = (bf16[1024,512]{1,0:T(8,128)(2,1)S(1)}, bf16[1024,512]{1,0:T(8,128)(2,1)}, u32[]{:S(2)}) copy-start(bf16[1024,512]{1,0:T(8,128)(2,1)} %refs_4_.4) | copy-start | bytes 3145732
  10.8 16.2 %copy-start.3 = (bf16[1024,512]{1,0:T(8,128)(2,1)S(1)}, bf16[1024,512]{1,0:T(8,128)(2,1)}, u32[]{:S(2)}) copy-start(bf16[1024,512]{1,0:T(8,128)(2,1)} %refs_5_.4) | copy-start | bytes 3145732
  10.8 16.2 %copy-start.4 = (s32[1024]{0:T(1024)S(1)}, s32[1024]{0:T(1024)}, u32[]{:S(2)}) copy-start(s32[1024]{0:T(1024)} %param.9) | copy-start | bytes 12292
  24.8 20.2 %copy-start = (bf16[512,2048]{1,0:T(8,128)(2,1)S(1)}, bf16[512,2048]{1,0:T(8,128)(2,1)}, u32[]{:S(2)}) copy-start(bf16[512,2048]{1,0:T(8,128)(2,1)} %get-tuple-element.107.w_mine_ref) | copy-start | bytes 6291460
  24.8 7.3 %collective-permute-start.3 = (bf16[512,2048]{1,0:T(8,128)(2,1)}, bf16[512,2048]{1,0:T(8,128)(2,1)S(1)}, u32[]{:S(2)}, u32[]{:S(2)}) collective-permute-start(bf16[512,2048]{1,0:T(8,128)(2,1)} %get-tuple-element.95), channel_id=1, source_target_pairs={{0,1},{1,0},{2,3},{3,2},{4,5},{5,4},{6,7},{7,6},{8,9},{9,8},{10,11... | collective-permute-start | bytes 6291464 | tf_op jit(solution)/shard_map/ppermute | solution.py:450
  24.9 12.0 %collective-permute-start.7 = (bf16[1536,128]{1,0:T(8,128)(2,1)S(1)}, bf16[1536,128]{1,0:T(8,128)(2,1)S(1)}, u32[]{:S(2)}, u32[]{:S(2)}) collective-permute-start(bf16[1536,128]{1,0:T(8,128)(2,1)S(1)} %copy-done.7), channel_id=1, source_target_pairs={{0,8},{8,0},{16,24},{24,16},{1,9},{9,1},{17,25},{25,17},{2,10},{10... | collective-permute-start | bytes 1179656 | tf_op jit(solution)/shard_map/ppermute | solution.py:450
  26.2 12.0 %collective-permute-start.8 = (bf16[1536,128]{1,0:T(8,128)(2,1)S(1)}, bf16[1536,128]{1,0:T(8,128)(2,1)S(1)}, u32[]{:S(2)}, u32[]{:S(2)}) collective-permute-start(bf16[1536,128]{1,0:T(8,128)(2,1)S(1)} %copy-done.6), channel_id=1, source_target_pairs={{0,16},{8,24},{16,0},{24,8},{1,17},{9,25},{17,1},{25,9},{2,18},{10... | collective-permute-start | bytes 1179656 | tf_op jit(solution)/shard_map/ppermute | solution.py:450
  32.2 7.5 %collective-permute-start.4 = (bf16[512,128]{1,0:T(8,128)(2,1)S(1)}, bf16[512,128]{1,0:T(8,128)(2,1)S(1)}, u32[]{:S(2)}, u32[]{:S(2)}) collective-permute-start(bf16[512,128]{1,0:T(8,128)(2,1)S(1)} %get-tuple-element.96), channel_id=1, source_target_pairs={{0,8},{8,0},{16,24},{24,16},{1,9},{9,1},{17,25},{25,17},{2,10},{10... | collective-permute-start | bytes 393224 | tf_op jit(solution)/shard_map/ppermute | solution.py:450
  33.7 7.7 %collective-permute-start.5 = (bf16[512,128]{1,0:T(8,128)(2,1)S(1)}, bf16[512,128]{1,0:T(8,128)(2,1)S(1)}, u32[]{:S(2)}, u32[]{:S(2)}) collective-permute-start(bf16[512,128]{1,0:T(8,128)(2,1)S(1)} %get-tuple-element.97), channel_id=1, source_target_pairs={{0,16},{8,24},{16,0},{24,8},{1,17},{9,25},{17,1},{25,9},{2,18},{10... | collective-permute-start | bytes 393224 | tf_op jit(solution)/shard_map/ppermute | solution.py:450
  34.2 8.8 %collective-permute-start.6 = (bf16[512,128]{1,0:T(8,128)(2,1)S(1)}, bf16[512,128]{1,0:T(8,128)(2,1)S(1)}, u32[]{:S(2)}, u32[]{:S(2)}) collective-permute-start(bf16[512,128]{1,0:T(8,128)(2,1)S(1)} %get-tuple-element.98), channel_id=1, source_target_pairs={{0,24},{8,16},{16,8},{24,0},{1,25},{9,17},{17,9},{25,1},{2,26},{10... | collective-permute-start | bytes 393224 | tf_op jit(solution)/shard_map/ppermute | solution.py:450
  43.1 2.0 %collective-permute-start.9 = (bf16[512,512]{1,0:T(8,128)(2,1)S(1)}, bf16[512,512]{1,0:T(8,128)(2,1)S(1)}, u32[]{:S(2)}, u32[]{:S(2)}) collective-permute-start(bf16[512,512]{1,0:T(8,128)(2,1)S(1)} %assemble.2.mine_ref), channel_id=1, source_target_pairs={{0,1},{1,0},{2,3},{3,2},{4,5},{5,4},{6,7},{7,6},{8,9},{9,8},{10,11... | collective-permute-start | bytes 1572872 | tf_op jit(solution)/shard_map/ppermute | solution.py:450
  45.0 4.2 %copy-start.5 = (bf16[1536,128]{1,0:T(8,128)(2,1)S(1)}, bf16[1536,128]{1,0:T(8,128)(2,1)}, u32[]{:S(2)}) copy-start(bf16[1536,128]{1,0:T(8,128)(2,1)} %get-tuple-element.109) | copy-start | bytes 1179652
  45.8 29.5 %collective-permute-start.14 = (bf16[512,512]{1,0:T(8,128)(2,1)S(1)}, bf16[512,512]{1,0:T(8,128)(2,1)S(1)}, u32[]{:S(2)}, u32[]{:S(2)}) collective-permute-start(bf16[512,512]{1,0:T(8,128)(2,1)S(1)} %project.8), channel_id=1, source_target_pairs={{0,2},{1,3},{6,4},{7,5},{8,10},{9,11},{14,12},{15,13},{16,18},{17,... | collective-permute-start | bytes 1572872 | tf_op jit(solution)/shard_map/ppermute | solution.py:455
  49.3 11.8 %collective-permute-start.10 = (bf16[1536,128]{1,0:T(8,128)(2,1)S(1)}, bf16[1536,128]{1,0:T(8,128)(2,1)S(1)}, u32[]{:S(2)}, u32[]{:S(2)}) collective-permute-start(bf16[1536,128]{1,0:T(8,128)(2,1)S(1)} %copy-done.5), channel_id=1, source_target_pairs={{0,24},{8,16},{16,8},{24,0},{1,25},{9,17},{17,9},{25,1},{2,26},{10... | collective-permute-start | bytes 1179656 | tf_op jit(solution)/shard_map/ppermute | solution.py:450
  61.1 26.3 %collective-permute-start.16 = (bf16[512,1024]{1,0:T(8,128)(2,1)S(1)}, bf16[512,1024]{1,0:T(8,128)(2,1)S(1)}, u32[]{:S(2)}, u32[]{:S(2)}) collective-permute-start(bf16[512,1024]{1,0:T(8,128)(2,1)S(1)} %project.7), channel_id=1, source_target_pairs={{0,2},{1,3},{6,4},{7,5},{8,10},{9,11},{14,12},{15,13},{16,18},{17,... | collective-permute-start | bytes 3145736 | tf_op jit(solution)/shard_map/ppermute | solution.py:455
  71.7 6.2 %collective-permute-start.11 = (bf16[512,128]{1,0:T(8,128)(2,1)S(1)}, bf16[512,128]{1,0:T(8,128)(2,1)S(1)}, u32[]{:S(2)}, u32[]{:S(2)}) collective-permute-start(bf16[512,128]{1,0:T(8,128)(2,1)S(1)} %get-tuple-element.117), channel_id=1, source_target_pairs={{0,8},{8,0},{16,24},{24,16},{1,9},{9,1},{17,25},{25,17},{2,10},{10... | collective-permute-start | bytes 393224 | tf_op jit(solution)/shard_map/ppermute | solution.py:450
  72.6 7.7 %collective-permute-start.12 = (bf16[512,128]{1,0:T(8,128)(2,1)S(1)}, bf16[512,128]{1,0:T(8,128)(2,1)S(1)}, u32[]{:S(2)}, u32[]{:S(2)}) collective-permute-start(bf16[512,128]{1,0:T(8,128)(2,1)S(1)} %get-tuple-element.118), channel_id=1, source_target_pairs={{0,16},{8,24},{16,0},{24,8},{1,17},{9,25},{17,1},{25,9},{2,18},{10... | collective-permute-start | bytes 393224 | tf_op jit(solution)/shard_map/ppermute | solution.py:450
  74.1 6.2 %collective-permute-start.13 = (bf16[512,128]{1,0:T(8,128)(2,1)S(1)}, bf16[512,128]{1,0:T(8,128)(2,1)S(1)}, u32[]{:S(2)}, u32[]{:S(2)}) collective-permute-start(bf16[512,128]{1,0:T(8,128)(2,1)S(1)} %get-tuple-element.119), channel_id=1, source_target_pairs={{0,24},{8,16},{16,8},{24,0},{1,25},{9,17},{17,9},{25,1},{2,26},{10... | collective-permute-start | bytes 393224 | tf_op jit(solution)/shard_map/ppermute | solution.py:450
  80.4 2.0 %collective-permute-start.15 = (bf16[512,512]{1,0:T(8,128)(2,1)S(1)}, bf16[512,512]{1,0:T(8,128)(2,1)S(1)}, u32[]{:S(2)}, u32[]{:S(2)}) collective-permute-start(bf16[512,512]{1,0:T(8,128)(2,1)S(1)} %assemble.3.mine_ref), channel_id=1, source_target_pairs={{0,1},{1,0},{2,3},{3,2},{4,5},{5,4},{6,7},{7,6},{8,9},{9,8},{10,11... | collective-permute-start | bytes 1572872 | tf_op jit(solution)/shard_map/ppermute | solution.py:450
  80.4 7.0 %collective-permute-start.17 = (bf16[512,512]{1,0:T(8,128)(2,1)S(1)}, bf16[512,512]{1,0:T(8,128)(2,1)S(1)}, u32[]{:S(2)}, u32[]{:S(2)}) collective-permute-start(bf16[512,512]{1,0:T(8,128)(2,1)S(1)} %add_convert_fusion.7), channel_id=1, source_target_pairs={{2,4},{3,5},{4,2},{5,3},{10,12},{11,13},{12,10},{13,11},{18,20},{1... | collective-permute-start | bytes 1572872 | tf_op jit(solution)/shard_map/ppermute | solution.py:455
  83.0 16.0 %collective-permute-start.20 = (bf16[512,512]{1,0:T(8,128)(2,1)S(1)}, bf16[512,512]{1,0:T(8,128)(2,1)S(1)}, u32[]{:S(2)}, u32[]{:S(2)}) collective-permute-start(bf16[512,512]{1,0:T(8,128)(2,1)S(1)} %project.12), channel_id=1, source_target_pairs={{0,2},{1,3},{6,4},{7,5},{8,10},{9,11},{14,12},{15,13},{16,18},{17,... | collective-permute-start | bytes 1572872 | tf_op jit(solution)/shard_map/ppermute | solution.py:455
  87.4 22.8 %collective-permute-start.18 = (bf16[512,512]{1,0:T(8,128)(2,1)S(1)}, bf16[512,512]{1,0:T(8,128)(2,1)S(1)}, u32[]{:S(2)}, u32[]{:S(2)}) collective-permute-start(bf16[512,512]{1,0:T(8,128)(2,1)S(1)} %project.10), channel_id=1, source_target_pairs={{0,2},{1,3},{6,4},{7,5},{8,10},{9,11},{14,12},{15,13},{16,18},{17,... | collective-permute-start | bytes 1572872 | tf_op jit(solution)/shard_map/ppermute | solution.py:455
  98.3 12.1 %collective-permute-start.19 = (bf16[512,512]{1,0:T(8,128)(2,1)S(1)}, bf16[512,512]{1,0:T(8,128)(2,1)S(1)}, u32[]{:S(2)}, u32[]{:S(2)}) collective-permute-start(bf16[512,512]{1,0:T(8,128)(2,1)S(1)} %get-tuple-element.135), channel_id=1, source_target_pairs={{2,4},{3,5},{4,2},{5,3},{10,12},{11,13},{12,10},{13,11},{18,20},{1... | collective-permute-start | bytes 1572872 | tf_op jit(solution)/shard_map/ppermute | solution.py:455
  99.2 11.9 %collective-permute-start.21 = (bf16[512,512]{1,0:T(8,128)(2,1)S(1)}, bf16[512,512]{1,0:T(8,128)(2,1)S(1)}, u32[]{:S(2)}, u32[]{:S(2)}) collective-permute-start(bf16[512,512]{1,0:T(8,128)(2,1)S(1)} %add_convert_fusion.4), channel_id=1, source_target_pairs={{2,4},{3,5},{4,2},{5,3},{10,12},{11,13},{12,10},{13,11},{18,20},{1... | collective-permute-start | bytes 1572872 | tf_op jit(solution)/shard_map/ppermute | solution.py:455
  99.9 16.3 %collective-permute-start.22 = (bf16[512,512]{1,0:T(8,128)(2,1)S(1)}, bf16[512,512]{1,0:T(8,128)(2,1)S(1)}, u32[]{:S(2)}, u32[]{:S(2)}) collective-permute-start(bf16[512,512]{1,0:T(8,128)(2,1)S(1)} %get-tuple-element.136), channel_id=1, source_target_pairs={{4,6},{5,7},{2,0},{3,1},{12,14},{13,15},{10,8},{11,9},{20,22},{21,... | collective-permute-start | bytes 1572872 | tf_op jit(solution)/shard_map/ppermute | solution.py:455
  101.2 19.0 %collective-permute-start.23 = (bf16[512,512]{1,0:T(8,128)(2,1)S(1)}, bf16[512,512]{1,0:T(8,128)(2,1)S(1)}, u32[]{:S(2)}, u32[]{:S(2)}) collective-permute-start(bf16[512,512]{1,0:T(8,128)(2,1)S(1)} %project.11), channel_id=1, source_target_pairs={{0,2},{1,3},{6,4},{7,5},{8,10},{9,11},{14,12},{15,13},{16,18},{17,... | collective-permute-start | bytes 1572872 | tf_op jit(solution)/shard_map/ppermute | solution.py:455
  110.4 9.8 %collective-permute-start.24 = (bf16[512,512]{1,0:T(8,128)(2,1)S(1)}, bf16[512,512]{1,0:T(8,128)(2,1)S(1)}, u32[]{:S(2)}, u32[]{:S(2)}) collective-permute-start(bf16[512,512]{1,0:T(8,128)(2,1)S(1)} %add_convert_fusion.6), channel_id=1, source_target_pairs={{2,4},{3,5},{4,2},{5,3},{10,12},{11,13},{12,10},{13,11},{18,20},{1... | collective-permute-start | bytes 1572872 | tf_op jit(solution)/shard_map/ppermute | solution.py:455
  116.2 20.5 %collective-permute-start.25 = (bf16[512,512]{1,0:T(8,128)(2,1)S(1)}, bf16[512,512]{1,0:T(8,128)(2,1)S(1)}, u32[]{:S(2)}, u32[]{:S(2)}) collective-permute-start(bf16[512,512]{1,0:T(8,128)(2,1)S(1)} %add_convert_fusion.3), channel_id=1, source_target_pairs={{4,6},{5,7},{2,0},{3,1},{12,14},{13,15},{10,8},{11,9},{20,22},{21,... | collective-permute-start | bytes 1572872 | tf_op jit(solution)/shard_map/ppermute | solution.py:455

commit v7 on v6

--- a/solution.py
+++ b/solution.py
@@ -450,11 +450,6 @@
     return lax.ppermute(value, axis, [(source, source ^ distance) for source in range(count)])
 
 
-def between_chips(value, pairs):
-    both = [(2 * source + core, 2 * target + core) for source, target in pairs for core in (0, 1)]
-    return lax.ppermute(value, "head", both)
-
-
 def add(*terms):
     total = terms[0].astype(jnp.float32)
     for term in terms[1:]:
@@ -462,10 +457,7 @@
     return total.astype(jnp.bfloat16)
 
 
-SENDING = ((3, 2, 1, 0), (3, 2, 0, 1), (0, 1, 3, 2), (0, 1, 2, 3))
-TO_MIDDLE = ((0, 1), (3, 2))
-ACROSS = ((1, 2), (2, 1))
-TO_ENDS = ((2, 3), (1, 0))
+TURNS = (3, 1, 2, 0)
 
 
 def tie(*values):
@@ -481,7 +473,7 @@
     head_index = lax.axis_index("head").astype(jnp.int32)
     chip = head_index // 2
     core = (head_index % 2).reshape(1)
-    places = jnp.concatenate([jnp.array(SENDING, jnp.int32)[chip], core])
+    places = jnp.concatenate([chip ^ jnp.array(TURNS, jnp.int32), core])
     docs = doc_ids.reshape(shard_rows // HD, HD)
     near = range(1, group)
 
@@ -508,39 +500,25 @@
     high.append(swap(diagonal_out, "ctx", 3))
     mine = assemble(ctx_index, [pieces[0], *back])
     sibling = swap(mine, "head", 1)
-    share = share_of(mine, sibling, 0)
-    shares = share_of(mine, sibling, 1, 2)
-    kept = share_of(mine, sibling, 3)
-    end = between_chips(share, TO_MIDDLE)
-    shares, high[2] = tie(shares, high[2])
-    ends = between_chips(shares, TO_MIDDLE)
-
-    high, share, shares, kept = tie(high, share, shares, kept)
+    shares = [share_of(mine, sibling, turn) for turn in range(chips)]
+    far = swap(shares[0], "head", 2)
+    near_sum = swap(shares[1], "head", 2)
+
+    high, shares = tie(high, shares)
     pieces = attend(ctx_index, queries, keys, values, docs, low, high)
     back = send_back(pieces)
-    passed = add(share, end)
-    back, passed = tie(back, passed)
-    across = between_chips(passed, ACROSS)
+    passed = add(shares[2], far)
+    back, passed, near_sum = tie(back, passed, near_sum)
+    across = swap(passed, "head", 4)
     mine = assemble(ctx_index, [pieces[0], *back])
     sibling = swap(mine, "head", 1)
     late = [share_of(mine, sibling, turn) for turn in range(chips)]
-    end_high = [between_chips(late[0], TO_MIDDLE)]
-    late[1], ends, across = tie(late[1], ends, across)
-    end_high.append(between_chips(late[1], TO_MIDDLE))
-    across_second = between_chips(add(shares[:, :columns], ends[:, :columns]), ACROSS)
-    passed = add(late[0], end_high[0])
-    late[2], passed = tie(late[2], passed)
-    across_high = between_chips(passed, ACROSS)
-    outer = between_chips(add(shares[:, columns:], across), TO_ENDS)
-    end_high.append(between_chips(late[2], TO_MIDDLE))
-    passed = add(late[1], end_high[1])
-    passed, across_second = tie(passed, across_second)
-    across_high_second = between_chips(passed, ACROSS)
-    passed = add(late[2], across_high)
-    passed, outer = tie(passed, outer)
-    outer_high = between_chips(passed, TO_ENDS)
-    first = add(kept, ends[:, columns:], across_second, outer)
-    second = add(late[3], end_high[2], across_high_second, outer_high)
+    far = swap(late[0], "head", 2)
+    late[1], across = tie(late[1], across)
+    first = add(shares[3], near_sum, across)
+    near_sum = swap(late[1], "head", 2)
+    across = swap(add(late[2], far), "head", 4)
+    second = add(late[3], near_sum, across)
     return jnp.concatenate([first, second], axis=0)
 
 
@@ -552,7 +530,7 @@
 
     def local(queries, keys, values, doc_ids, w_out):
         heads = queries.shape[1] // HD
-        exchange = heads == ctx_count and heads == 4 and head_count == 2 * len(SENDING)
+        exchange = heads == ctx_count and heads == 4 and head_count == 2 * len(TURNS)
         exchange = exchange and queries.shape[0] % (4 * TILE) == 0
         body = exchange_local if exchange else ring_local
         return body(queries, keys, values, doc_ids, w_out)

time: 140 us -> 130 us (0.929); the launches traced: 138 us -> 132 us
  starting transfers between devices: 45.4 us -> 22.9 us
  waiting for transfers between devices: 58 us -> 74.4 us
  Pallas kernels: 30.4 us -> 31.8 us
    ppermute x15 -> x21, waiting for transfers between devices: 31.7 us -> 74.4 us  [swap(): lax.ppermute(value, axis, [(source, source ^ distance) for source in rang...]
    ppermute x11 -> x0, starting transfers between devices: 29.7 us -> none  [between_chips(): return lax.ppermute(value, 'head', both)]
    ppermute x11 -> x0, waiting for transfers between devices: 26.4 us -> none  [between_chips(): return lax.ppermute(value, 'head', both)]
    ppermute x15 -> x21, starting transfers between devices: 15.7 us -> 22.9 us  [swap(): lax.ppermute(value, axis, [(source, source ^ distance) for source in rang...]
    pallas_call x2, Pallas kernels: 13.4 us -> 15 us  [attend(): pl.pallas_call(kernel, grid_spec=pltpu.PrefetchScalarGridSpec(num_scalar_...]
    pallas_call x7 -> x8, Pallas kernels: 5.92 us -> 5.68 us  [project(): pl.pallas_call(kernel, grid=(count,), in_specs=[attended, attended, weigh...]
  transfers between devices with their start and end apart: 26 -> 21, of which waited for: 15 -> 13; matrix products, arithmetic and copies ran while one was open for 2% -> 1% of each run, Pallas kernels for 20% -> 22%
where the time goes in v7:
time: 130 us; the launch traced here: 132 us
  waiting for transfers between devices  74.4 us (57%)
  Pallas kernels  31.8 us (24%)
  starting transfers between devices  22.9 us (18%)
  other arithmetic  2.35 us (2%)
    ppermute x21, waiting for transfers between devices, swap(): lax.ppermute(value, axis, [(source, source ^ distance) for source in rang...  74.4 us
    ppermute x21, starting transfers between devices, swap(): lax.ppermute(value, axis, [(source, source ^ distance) for source in rang...  22.9 us
    pallas_call x2, Pallas kernels, attend(): pl.pallas_call(kernel, grid_spec=pltpu.PrefetchScalarGridSpec(num_scalar_...  15 us
    pallas_call x1, Pallas kernels, pack_projection(): pl.pallas_call(kernel, grid_spec=pltpu.PrefetchScalarGridSpec(num_scalar_...  5.89 us
    pallas_call x8, Pallas kernels, project(): pl.pallas_call(kernel, grid=(count,), in_specs=[attended, attended, weigh...  5.68 us
    pallas_call x2, Pallas kernels, pack(): pl.pallas_call(kernel, grid_spec=pltpu.PrefetchScalarGridSpec(num_scalar_...  5.05 us
  transfers between devices with their start and end apart: 21, of which 13 were waited for; matrix products, arithmetic and copies ran while one was open for 1% of the time, Pallas kernels for 22%

profile of v7, /device:TPU:0, one launch (start us, length us, event | category | flops | bytes accessed | tf_op | source)
XLA Modules:
  0.0 131.7 jit_solution(16831424015622925824)
XLA Ops:
  0.0 2.5 %pack.2 = (bf16[1552,128]{1,0:T(8,128)(2,1)}, bf16[1552,128]{1,0:T(8,128)(2,1)}, bf16[1552,128]{1,0:T(8,128)(2,1)}) custom-call(s32[1]{0:T(128)} %bitcast.ctx_ref, bf16[1024,512]{1,0:T(8,128)(2,1)} %refs_3_.4, bf16[1024,512]{1,0:T(8,128)(2,1)} %refs_4_.4, bf16[1024,512]{1,0:T(8,128)(2,1)} %refs_5_.4, bf16[1024,512]{1,0:T(8,128)(2,1)} %refs_3_.4, ...), custom_call_target="tpu_custom_call" | custom-call | flops 1024 | bytes 1024 | tf_op jit(solution)/shard_map/pack/pallas_call | solution.py:201
  2.5 2.9 %collective-permute-start = (bf16[1552,128]{1,0:T(8,128)(2,1)}, bf16[1552,128]{1,0:T(8,128)(2,1)S(1)}, u32[]{:S(2)}, u32[]{:S(2)}) collective-permute-start(bf16[1552,128]{1,0:T(8,128)(2,1)} %get-tuple-element.73), channel_id=1, source_target_pairs={{0,8},{8,0},{16,24},{24,16},{1,9},{9,1},{17,25},{25,17},{2,10},{10... | collective-permute-start | bytes 1191944 | tf_op jit(solution)/shard_map/ppermute | solution.py:450
  5.4 1.5 %collective-permute-start.1 = (bf16[1552,128]{1,0:T(8,128)(2,1)}, bf16[1552,128]{1,0:T(8,128)(2,1)S(1)}, u32[]{:S(2)}, u32[]{:S(2)}) collective-permute-start(bf16[1552,128]{1,0:T(8,128)(2,1)} %get-tuple-element.74), channel_id=1, source_target_pairs={{0,16},{8,24},{16,0},{24,8},{1,17},{9,25},{17,1},{25,9},{2,18},{10... | collective-permute-start | bytes 1191944 | tf_op jit(solution)/shard_map/ppermute | solution.py:450
  7.0 0.0 collective-permute-start.2
  7.0 2.5 %pack.3 = (bf16[1536,128]{1,0:T(8,128)(2,1)}, bf16[1536,128]{1,0:T(8,128)(2,1)}, bf16[1536,128]{1,0:T(8,128)(2,1)}) custom-call(s32[1]{0:T(128)} %bitcast.ctx_ref, bf16[1024,512]{1,0:T(8,128)(2,1)} %refs_3_.4, bf16[1024,512]{1,0:T(8,128)(2,1)} %refs_4_.4, bf16[1024,512]{1,0:T(8,128)(2,1)} %refs_5_.4, bf16[1024,512]{1,0:T(8,128)(2,1)} %refs_3_.4, ...), custom_call_target="tpu_custom_call" | custom-call | flops 1024 | bytes 1024 | tf_op jit(solution)/shard_map/pack/pallas_call | solution.py:201
  9.5 0.6 pad_add_fusion.places_ref
  10.2 0.0 copy-start.3
  10.2 0.0 copy-start.4
  10.2 5.9 %pack_projection.1 = (bf16[512,2048]{1,0:T(8,128)(2,1)}, bf16[512,2048]{1,0:T(8,128)(2,1)}) custom-call(s32[5]{0:T(128)} %pad_add_fusion.places_ref, bf16[512,4096]{1,0:T(8,128)(2,1)} %give_in, bf16[512,4096]{1,0:T(8,128)(2,1)} %give_in), custom_call_target="tpu_custom_call" | custom-call | flops 1024 | bytes 1024 | tf_op jit(solution)/shard_map/pack_projection/pallas_call | solution.py:232
  16.1 0.0 collective-permute-done.refs_4_.refs_7_
  16.1 8.7 %collective-permute-done.1.refs_5_.refs_8_ = bf16[1552,128]{1,0:T(8,128)(2,1)S(1)} collective-permute-done((bf16[1552,128]{1,0:T(8,128)(2,1)}, bf16[1552,128]{1,0:T(8,128)(2,1)S(1)}, u32[]{:S(2)}, u32[]{:S(2)}) %collective-permute-start.1) | collective-permute-done | bytes 397344 | tf_op jit(solution)/shard_map/ppermute | solution.py:450
  24.8 0.0 collective-permute-done.2.refs_6_.refs_9_
  24.8 0.0 collective-permute-start.3
  24.8 1.3 collective-permute-start.7
  26.1 0.8 collective-permute-start.8
  27.0 6.6 %attend_low.1 = (bf16[512,128]{1,0:T(8,128)(2,1)S(1)}, bf16[512,128]{1,0:T(8,128)(2,1)S(1)}, bf16[512,128]{1,0:T(8,128)(2,1)S(1)}, bf16[512,128]{1,0:T(8,128)(2,1)S(1)}) custom-call(s32[1]{0:T(128)} %bitcast.ctx_ref, bf16[1024,512]{1,0:T(8,128)(2,1)S(1)} %copy-done.1, bf16[1024,512]{1,0:T(8,128)(2,1)S(1)} %copy-done.2, bf16[1024,512]{1,0:T(8,128)(2,1)S(1)} %copy-done.3, ...), custom_call_target="tpu_custom_call" | custom-call | flops 1024 | bytes 1024 | tf_op jit(solution)/shard_map/attend_low/pallas_call | solution.py:380
  33.6 0.0 collective-permute-done.3.w_sibling_ref
  33.6 1.5 %collective-permute-start.4 = (bf16[512,128]{1,0:T(8,128)(2,1)S(1)}, bf16[512,128]{1,0:T(8,128)(2,1)S(1)}, u32[]{:S(2)}, u32[]{:S(2)}) collective-permute-start(bf16[512,128]{1,0:T(8,128)(2,1)S(1)} %get-tuple-element.87), channel_id=1, source_target_pairs={{0,8},{8,0},{16,24},{24,16},{1,9},{9,1},{17,25},{25,17},{2,10},{10... | collective-permute-start | bytes 393224 | tf_op jit(solution)/shard_map/ppermute | solution.py:450
  35.1 0.5 collective-permute-start.5
  35.6 1.5 %collective-permute-start.6 = (bf16[512,128]{1,0:T(8,128)(2,1)S(1)}, bf16[512,128]{1,0:T(8,128)(2,1)S(1)}, u32[]{:S(2)}, u32[]{:S(2)}) collective-permute-start(bf16[512,128]{1,0:T(8,128)(2,1)S(1)} %get-tuple-element.89), channel_id=1, source_target_pairs={{0,24},{8,16},{16,8},{24,0},{1,25},{9,17},{17,9},{25,1},{2,26},{10... | collective-permute-start | bytes 393224 | tf_op jit(solution)/shard_map/ppermute | solution.py:450
  37.2 0.2 collective-permute-done.8.refs_11_
  37.3 2.5 %collective-permute-done.4.refs_1_ = bf16[512,128]{1,0:T(8,128)(2,1)S(1)} collective-permute-done((bf16[512,128]{1,0:T(8,128)(2,1)S(1)}, bf16[512,128]{1,0:T(8,128)(2,1)S(1)}, u32[]{:S(2)}, u32[]{:S(2)}) %collective-permute-start.4) | collective-permute-done | bytes 131104 | tf_op jit(solution)/shard_map/ppermute | solution.py:450
  39.8 1.5 %collective-permute-done.5.refs_2_ = bf16[512,128]{1,0:T(8,128)(2,1)S(1)} collective-permute-done((bf16[512,128]{1,0:T(8,128)(2,1)S(1)}, bf16[512,128]{1,0:T(8,128)(2,1)S(1)}, u32[]{:S(2)}, u32[]{:S(2)}) %collective-permute-start.5) | collective-permute-done | bytes 131104 | tf_op jit(solution)/shard_map/ppermute | solution.py:450
  41.3 1.6 %collective-permute-done.6.refs_3_ = bf16[512,128]{1,0:T(8,128)(2,1)S(1)} collective-permute-done((bf16[512,128]{1,0:T(8,128)(2,1)S(1)}, bf16[512,128]{1,0:T(8,128)(2,1)S(1)}, u32[]{:S(2)}, u32[]{:S(2)}) %collective-permute-start.6) | collective-permute-done | bytes 131104 | tf_op jit(solution)/shard_map/ppermute | solution.py:450
  43.0 0.1 assemble.2.mine_ref
  43.1 0.1 collective-permute-start.10
  43.1 1.9 %collective-permute-done.10.sibling_ref = bf16[512,512]{1,0:T(8,128)(2,1)S(1)} collective-permute-done((bf16[512,512]{1,0:T(8,128)(2,1)S(1)}, bf16[512,512]{1,0:T(8,128)(2,1)S(1)}, u32[]{:S(2)}, u32[]{:S(2)}) %collective-permute-start.10) | collective-permute-done | bytes 524320 | tf_op jit(solution)/shard_map/ppermute | solution.py:450
  45.0 0.7 project.8
  45.7 1.6 %collective-permute-start.14 = (bf16[512,512]{1,0:T(8,128)(2,1)S(1)}, bf16[512,512]{1,0:T(8,128)(2,1)S(1)}, u32[]{:S(2)}, u32[]{:S(2)}) collective-permute-start(bf16[512,512]{1,0:T(8,128)(2,1)S(1)} %project.8), channel_id=1, source_target_pairs={{0,2},{1,3},{2,0},{3,1},{4,6},{5,7},{6,4},{7,5},{8,10},{9,11},{10,... | collective-permute-start | bytes 1572872 | tf_op jit(solution)/shard_map/ppermute | solution.py:450
  47.4 1.8 %collective-permute-start.9 = (bf16[1536,128]{1,0:T(8,128)(2,1)S(1)}, bf16[1536,128]{1,0:T(8,128)(2,1)S(1)}, u32[]{:S(2)}, u32[]{:S(2)}) collective-permute-start(bf16[1536,128]{1,0:T(8,128)(2,1)S(1)} %copy-done.5), channel_id=1, source_target_pairs={{0,24},{8,16},{16,8},{24,0},{1,25},{9,17},{17,9},{25,1},{2,26},{10... | collective-permute-start | bytes 1179656 | tf_op jit(solution)/shard_map/ppermute | solution.py:450
  49.1 0.7 project.9
  49.9 0.5 collective-permute-start.15
  50.4 0.7 project.11
  51.1 0.7 project.10
  51.8 7.4 %collective-permute-done.9.refs_12_ = bf16[1536,128]{1,0:T(8,128)(2,1)S(1)} collective-permute-done((bf16[1536,128]{1,0:T(8,128)(2,1)S(1)}, bf16[1536,128]{1,0:T(8,128)(2,1)S(1)}, u32[]{:S(2)}, u32[]{:S(2)}) %collective-permute-start.9) | collective-permute-done | bytes 393248 | tf_op jit(solution)/shard_map/ppermute | solution.py:450
  59.2 8.4 %attend_high.1 = (bf16[512,128]{1,0:T(8,128)(2,1)S(1)}, bf16[512,128]{1,0:T(8,128)(2,1)S(1)}, bf16[512,128]{1,0:T(8,128)(2,1)S(1)}, bf16[512,128]{1,0:T(8,128)(2,1)S(1)}) custom-call(s32[1]{0:T(128)} %bitcast.ctx_ref, bf16[1024,512]{1,0:T(8,128)(2,1)S(1)} %copy-done.1, bf16[1024,512]{1,0:T(8,128)(2,1)S(1)} %copy-done.2, bf16[1024,512]{1,0:T(8,128)(2,1)S(1)} %copy-done.3, ...), custom_call_target="tpu_custom_call" | custom-call | flops 1024 | bytes 1024 | tf_op jit(solution)/shard_map/attend_high/pallas_call | solution.py:380
  67.5 0.9 collective-permute-start.11
  68.4 1.5 %collective-permute-start.12 = (bf16[512,128]{1,0:T(8,128)(2,1)S(1)}, bf16[512,128]{1,0:T(8,128)(2,1)S(1)}, u32[]{:S(2)}, u32[]{:S(2)}) collective-permute-start(bf16[512,128]{1,0:T(8,128)(2,1)S(1)} %get-tuple-element.106), channel_id=1, source_target_pairs={{0,16},{8,24},{16,0},{24,8},{1,17},{9,25},{17,1},{25,9},{2,18},{10... | collective-permute-start | bytes 393224 | tf_op jit(solution)/shard_map/ppermute | solution.py:450
  70.0 1.1 collective-permute-start.13
  71.1 0.0 collective-permute-done.14
  71.1 0.1 add_convert_fusion.3
  71.2 2.5 %collective-permute-done.11.refs_1_ = bf16[512,128]{1,0:T(8,128)(2,1)S(1)} collective-permute-done((bf16[512,128]{1,0:T(8,128)(2,1)S(1)}, bf16[512,128]{1,0:T(8,128)(2,1)S(1)}, u32[]{:S(2)}, u32[]{:S(2)}) %collective-permute-start.11) | collective-permute-done | bytes 131104 | tf_op jit(solution)/shard_map/ppermute | solution.py:450
  73.7 2.4 %collective-permute-done.12.refs_2_ = bf16[512,128]{1,0:T(8,128)(2,1)S(1)} collective-permute-done((bf16[512,128]{1,0:T(8,128)(2,1)S(1)}, bf16[512,128]{1,0:T(8,128)(2,1)S(1)}, u32[]{:S(2)}, u32[]{:S(2)}) %collective-permute-start.12) | collective-permute-done | bytes 131104 | tf_op jit(solution)/shard_map/ppermute | solution.py:450
  76.1 0.0 collective-permute-done.13.refs_3_
  76.1 0.0 collective-permute-done.15
  76.1 0.1 assemble.3.mine_ref
  76.2 0.1 collective-permute-start.16
  76.3 2.6 %collective-permute-start.17 = (bf16[512,512]{1,0:T(8,128)(2,1)S(1)}, bf16[512,512]{1,0:T(8,128)(2,1)S(1)}, u32[]{:S(2)}, u32[]{:S(2)}) collective-permute-start(bf16[512,512]{1,0:T(8,128)(2,1)S(1)} %add_convert_fusion.3), channel_id=1, source_target_pairs={{0,4},{1,5},{2,6},{3,7},{4,0},{5,1},{6,2},{7,3},{8,12},{9,13},{10,... | collective-permute-start | bytes 1572872 | tf_op jit(solution)/shard_map/ppermute | solution.py:450
  78.9 0.0 collective-permute-done.16.sibling_ref
  78.9 0.7 project.15
  79.7 0.6 collective-permute-start.19
  80.3 0.7 project.12
  81.0 21.9 %collective-permute-done.17 = bf16[512,512]{1,0:T(8,128)(2,1)S(1)} collective-permute-done((bf16[512,512]{1,0:T(8,128)(2,1)S(1)}, bf16[512,512]{1,0:T(8,128)(2,1)S(1)}, u32[]{:S(2)}, u32[]{:S(2)}) %collective-permute-start.17) | collective-permute-done | bytes 524320 | tf_op jit(solution)/shard_map/ppermute | solution.py:450
  102.8 0.0 collective-permute-start.18
  102.8 0.7 project.14
  103.5 1.3 collective-permute-done.19
  104.9 0.1 add_convert_fusion.1
  105.0 1.9 %collective-permute-start.20 = (bf16[512,512]{1,0:T(8,128)(2,1)S(1)}, bf16[512,512]{1,0:T(8,128)(2,1)S(1)}, u32[]{:S(2)}, u32[]{:S(2)}) collective-permute-start(bf16[512,512]{1,0:T(8,128)(2,1)S(1)} %add_convert_fusion.1), channel_id=1, source_target_pairs={{0,4},{1,5},{2,6},{3,7},{4,0},{5,1},{6,2},{7,3},{8,12},{9,13},{10,... | collective-permute-start | bytes 1572872 | tf_op jit(solution)/shard_map/ppermute | solution.py:450
  106.9 0.7 project.13
  107.6 0.2 add_convert_fusion.2
  107.8 18.1 %collective-permute-done.18 = bf16[512,512]{1,0:T(8,128)(2,1)S(1)} collective-permute-done((bf16[512,512]{1,0:T(8,128)(2,1)S(1)}, bf16[512,512]{1,0:T(8,128)(2,1)S(1)}, u32[]{:S(2)}, u32[]{:S(2)}) %collective-permute-start.18) | collective-permute-done | bytes 524320 | tf_op jit(solution)/shard_map/ppermute | solution.py:450
  125.9 4.5 %collective-permute-done.20 = bf16[512,512]{1,0:T(8,128)(2,1)S(1)} collective-permute-done((bf16[512,512]{1,0:T(8,128)(2,1)S(1)}, bf16[512,512]{1,0:T(8,128)(2,1)S(1)}, u32[]{:S(2)}, u32[]{:S(2)}) %collective-permute-start.20) | collective-permute-done | bytes 524320 | tf_op jit(solution)/shard_map/ppermute | solution.py:450
  130.4 0.2 add_convert_fusion
  130.6 1.0 pad_maximum_fusion
  (18 shorter events, 0.0 us)
Async XLA Ops:
  2.5 7.0 %copy-start.8 = (s32[4]{0:T(128)S(1)}, s32[4]{0:T(128)}, u32[]{:S(2)}) copy-start(s32[4]{0:T(128)} %constant.34.clone) | copy-start | bytes 52
  2.5 13.6 %collective-permute-start = (bf16[1552,128]{1,0:T(8,128)(2,1)}, bf16[1552,128]{1,0:T(8,128)(2,1)S(1)}, u32[]{:S(2)}, u32[]{:S(2)}) collective-permute-start(bf16[1552,128]{1,0:T(8,128)(2,1)} %get-tuple-element.73), channel_id=1, source_target_pairs={{0,8},{8,0},{16,24},{24,16},{1,9},{9,1},{17,25},{25,17},{2,10},{10... | collective-permute-start | bytes 1191944 | tf_op jit(solution)/shard_map/ppermute | solution.py:450
  5.4 19.4 %collective-permute-start.1 = (bf16[1552,128]{1,0:T(8,128)(2,1)}, bf16[1552,128]{1,0:T(8,128)(2,1)S(1)}, u32[]{:S(2)}, u32[]{:S(2)}) collective-permute-start(bf16[1552,128]{1,0:T(8,128)(2,1)} %get-tuple-element.74), channel_id=1, source_target_pairs={{0,16},{8,24},{16,0},{24,8},{1,17},{9,25},{17,1},{25,9},{2,18},{10... | collective-permute-start | bytes 1191944 | tf_op jit(solution)/shard_map/ppermute | solution.py:450
  7.0 17.9 %collective-permute-start.2 = (bf16[1552,128]{1,0:T(8,128)(2,1)}, bf16[1552,128]{1,0:T(8,128)(2,1)S(1)}, u32[]{:S(2)}, u32[]{:S(2)}) collective-permute-start(bf16[1552,128]{1,0:T(8,128)(2,1)} %get-tuple-element.75), channel_id=1, source_target_pairs={{0,24},{8,16},{16,8},{24,0},{1,25},{9,17},{17,9},{25,1},{2,26},{10... | collective-permute-start | bytes 1191944 | tf_op jit(solution)/shard_map/ppermute | solution.py:450
  10.2 14.7 %copy-start.7 = (bf16[1536,128]{1,0:T(8,128)(2,1)S(1)}, bf16[1536,128]{1,0:T(8,128)(2,1)}, u32[]{:S(2)}) copy-start(bf16[1536,128]{1,0:T(8,128)(2,1)} %get-tuple-element.90) | copy-start | bytes 1179652
  10.2 16.0 %copy-start.6 = (bf16[1536,128]{1,0:T(8,128)(2,1)S(1)}, bf16[1536,128]{1,0:T(8,128)(2,1)}, u32[]{:S(2)}) copy-start(bf16[1536,128]{1,0:T(8,128)(2,1)} %get-tuple-element.91) | copy-start | bytes 1179652
  10.2 16.8 %copy-start.1 = (bf16[1024,512]{1,0:T(8,128)(2,1)S(1)}, bf16[1024,512]{1,0:T(8,128)(2,1)}, u32[]{:S(2)}) copy-start(bf16[1024,512]{1,0:T(8,128)(2,1)} %refs_3_.4) | copy-start | bytes 3145732
  10.2 16.8 %copy-start.2 = (bf16[1024,512]{1,0:T(8,128)(2,1)S(1)}, bf16[1024,512]{1,0:T(8,128)(2,1)}, u32[]{:S(2)}) copy-start(bf16[1024,512]{1,0:T(8,128)(2,1)} %refs_4_.4) | copy-start | bytes 3145732
  10.2 16.8 %copy-start.3 = (bf16[1024,512]{1,0:T(8,128)(2,1)S(1)}, bf16[1024,512]{1,0:T(8,128)(2,1)}, u32[]{:S(2)}) copy-start(bf16[1024,512]{1,0:T(8,128)(2,1)} %refs_5_.4) | copy-start | bytes 3145732
  10.2 16.8 %copy-start.4 = (s32[1024]{0:T(1024)S(1)}, s32[1024]{0:T(1024)}, u32[]{:S(2)}) copy-start(s32[1024]{0:T(1024)} %param.9) | copy-start | bytes 12292
  24.8 20.2 %copy-start = (bf16[512,2048]{1,0:T(8,128)(2,1)S(1)}, bf16[512,2048]{1,0:T(8,128)(2,1)}, u32[]{:S(2)}) copy-start(bf16[512,2048]{1,0:T(8,128)(2,1)} %get-tuple-element.99.w_mine_ref) | copy-start | bytes 6291460
  24.8 8.8 %collective-permute-start.3 = (bf16[512,2048]{1,0:T(8,128)(2,1)}, bf16[512,2048]{1,0:T(8,128)(2,1)S(1)}, u32[]{:S(2)}, u32[]{:S(2)}) collective-permute-start(bf16[512,2048]{1,0:T(8,128)(2,1)} %get-tuple-element.86), channel_id=1, source_target_pairs={{0,1},{1,0},{2,3},{3,2},{4,5},{5,4},{6,7},{7,6},{8,9},{9,8},{10,11... | collective-permute-start | bytes 6291464 | tf_op jit(solution)/shard_map/ppermute | solution.py:450
  24.8 12.3 %collective-permute-start.7 = (bf16[1536,128]{1,0:T(8,128)(2,1)S(1)}, bf16[1536,128]{1,0:T(8,128)(2,1)S(1)}, u32[]{:S(2)}, u32[]{:S(2)}) collective-permute-start(bf16[1536,128]{1,0:T(8,128)(2,1)S(1)} %copy-done.7), channel_id=1, source_target_pairs={{0,8},{8,0},{16,24},{24,16},{1,9},{9,1},{17,25},{25,17},{2,10},{10... | collective-permute-start | bytes 1179656 | tf_op jit(solution)/shard_map/ppermute | solution.py:450
  26.1 11.2 %collective-permute-start.8 = (bf16[1536,128]{1,0:T(8,128)(2,1)S(1)}, bf16[1536,128]{1,0:T(8,128)(2,1)S(1)}, u32[]{:S(2)}, u32[]{:S(2)}) collective-permute-start(bf16[1536,128]{1,0:T(8,128)(2,1)S(1)} %copy-done.6), channel_id=1, source_target_pairs={{0,16},{8,24},{16,0},{24,8},{1,17},{9,25},{17,1},{25,9},{2,18},{10... | collective-permute-start | bytes 1179656 | tf_op jit(solution)/shard_map/ppermute | solution.py:450
  33.6 6.2 %collective-permute-start.4 = (bf16[512,128]{1,0:T(8,128)(2,1)S(1)}, bf16[512,128]{1,0:T(8,128)(2,1)S(1)}, u32[]{:S(2)}, u32[]{:S(2)}) collective-permute-start(bf16[512,128]{1,0:T(8,128)(2,1)S(1)} %get-tuple-element.87), channel_id=1, source_target_pairs={{0,8},{8,0},{16,24},{24,16},{1,9},{9,1},{17,25},{25,17},{2,10},{10... | collective-permute-start | bytes 393224 | tf_op jit(solution)/shard_map/ppermute | solution.py:450
  35.1 6.2 %collective-permute-start.5 = (bf16[512,128]{1,0:T(8,128)(2,1)S(1)}, bf16[512,128]{1,0:T(8,128)(2,1)S(1)}, u32[]{:S(2)}, u32[]{:S(2)}) collective-permute-start(bf16[512,128]{1,0:T(8,128)(2,1)S(1)} %get-tuple-element.88), channel_id=1, source_target_pairs={{0,16},{8,24},{16,0},{24,8},{1,17},{9,25},{17,1},{25,9},{2,18},{10... | collective-permute-start | bytes 393224 | tf_op jit(solution)/shard_map/ppermute | solution.py:450
  35.6 7.3 %collective-permute-start.6 = (bf16[512,128]{1,0:T(8,128)(2,1)S(1)}, bf16[512,128]{1,0:T(8,128)(2,1)S(1)}, u32[]{:S(2)}, u32[]{:S(2)}) collective-permute-start(bf16[512,128]{1,0:T(8,128)(2,1)S(1)} %get-tuple-element.89), channel_id=1, source_target_pairs={{0,24},{8,16},{16,8},{24,0},{1,25},{9,17},{17,9},{25,1},{2,26},{10... | collective-permute-start | bytes 393224 | tf_op jit(solution)/shard_map/ppermute | solution.py:450
  43.1 2.0 %collective-permute-start.10 = (bf16[512,512]{1,0:T(8,128)(2,1)S(1)}, bf16[512,512]{1,0:T(8,128)(2,1)S(1)}, u32[]{:S(2)}, u32[]{:S(2)}) collective-permute-start(bf16[512,512]{1,0:T(8,128)(2,1)S(1)} %assemble.2.mine_ref), channel_id=1, source_target_pairs={{0,1},{1,0},{2,3},{3,2},{4,5},{5,4},{6,7},{7,6},{8,9},{9,8},{10,11... | collective-permute-start | bytes 1572872 | tf_op jit(solution)/shard_map/ppermute | solution.py:450
  45.0 2.4 %copy-start.5 = (bf16[1536,128]{1,0:T(8,128)(2,1)S(1)}, bf16[1536,128]{1,0:T(8,128)(2,1)}, u32[]{:S(2)}) copy-start(bf16[1536,128]{1,0:T(8,128)(2,1)} %get-tuple-element.94) | copy-start | bytes 1179652
  45.7 25.4 %collective-permute-start.14 = (bf16[512,512]{1,0:T(8,128)(2,1)S(1)}, bf16[512,512]{1,0:T(8,128)(2,1)S(1)}, u32[]{:S(2)}, u32[]{:S(2)}) collective-permute-start(bf16[512,512]{1,0:T(8,128)(2,1)S(1)} %project.8), channel_id=1, source_target_pairs={{0,2},{1,3},{2,0},{3,1},{4,6},{5,7},{6,4},{7,5},{8,10},{9,11},{10,... | collective-permute-start | bytes 1572872 | tf_op jit(solution)/shard_map/ppermute | solution.py:450
  47.4 11.8 %collective-permute-start.9 = (bf16[1536,128]{1,0:T(8,128)(2,1)S(1)}, bf16[1536,128]{1,0:T(8,128)(2,1)S(1)}, u32[]{:S(2)}, u32[]{:S(2)}) collective-permute-start(bf16[1536,128]{1,0:T(8,128)(2,1)S(1)} %copy-done.5), channel_id=1, source_target_pairs={{0,24},{8,16},{16,8},{24,0},{1,25},{9,17},{17,9},{25,1},{2,26},{10... | collective-permute-start | bytes 1179656 | tf_op jit(solution)/shard_map/ppermute | solution.py:450
  49.9 26.3 %collective-permute-start.15 = (bf16[512,512]{1,0:T(8,128)(2,1)S(1)}, bf16[512,512]{1,0:T(8,128)(2,1)S(1)}, u32[]{:S(2)}, u32[]{:S(2)}) collective-permute-start(bf16[512,512]{1,0:T(8,128)(2,1)S(1)} %project.9), channel_id=1, source_target_pairs={{0,2},{1,3},{2,0},{3,1},{4,6},{5,7},{6,4},{7,5},{8,10},{9,11},{10,... | collective-permute-start | bytes 1572872 | tf_op jit(solution)/shard_map/ppermute | solution.py:450
  67.5 6.2 %collective-permute-start.11 = (bf16[512,128]{1,0:T(8,128)(2,1)S(1)}, bf16[512,128]{1,0:T(8,128)(2,1)S(1)}, u32[]{:S(2)}, u32[]{:S(2)}) collective-permute-start(bf16[512,128]{1,0:T(8,128)(2,1)S(1)} %get-tuple-element.105), channel_id=1, source_target_pairs={{0,8},{8,0},{16,24},{24,16},{1,9},{9,1},{17,25},{25,17},{2,10},{10... | collective-permute-start | bytes 393224 | tf_op jit(solution)/shard_map/ppermute | solution.py:450
  68.4 7.7 %collective-permute-start.12 = (bf16[512,128]{1,0:T(8,128)(2,1)S(1)}, bf16[512,128]{1,0:T(8,128)(2,1)S(1)}, u32[]{:S(2)}, u32[]{:S(2)}) collective-permute-start(bf16[512,128]{1,0:T(8,128)(2,1)S(1)} %get-tuple-element.106), channel_id=1, source_target_pairs={{0,16},{8,24},{16,0},{24,8},{1,17},{9,25},{17,1},{25,9},{2,18},{10... | collective-permute-start | bytes 393224 | tf_op jit(solution)/shard_map/ppermute | solution.py:450
  70.0 6.2 %collective-permute-start.13 = (bf16[512,128]{1,0:T(8,128)(2,1)S(1)}, bf16[512,128]{1,0:T(8,128)(2,1)S(1)}, u32[]{:S(2)}, u32[]{:S(2)}) collective-permute-start(bf16[512,128]{1,0:T(8,128)(2,1)S(1)} %get-tuple-element.107), channel_id=1, source_target_pairs={{0,24},{8,16},{16,8},{24,0},{1,25},{9,17},{17,9},{25,1},{2,26},{10... | collective-permute-start | bytes 393224 | tf_op jit(solution)/shard_map/ppermute | solution.py:450
  76.2 2.7 %collective-permute-start.16 = (bf16[512,512]{1,0:T(8,128)(2,1)S(1)}, bf16[512,512]{1,0:T(8,128)(2,1)S(1)}, u32[]{:S(2)}, u32[]{:S(2)}) collective-permute-start(bf16[512,512]{1,0:T(8,128)(2,1)S(1)} %assemble.3.mine_ref), channel_id=1, source_target_pairs={{0,1},{1,0},{2,3},{3,2},{4,5},{5,4},{6,7},{7,6},{8,9},{9,8},{10,11... | collective-permute-start | bytes 1572872 | tf_op jit(solution)/shard_map/ppermute | solution.py:450
  76.3 26.5 %collective-permute-start.17 = (bf16[512,512]{1,0:T(8,128)(2,1)S(1)}, bf16[512,512]{1,0:T(8,128)(2,1)S(1)}, u32[]{:S(2)}, u32[]{:S(2)}) collective-permute-start(bf16[512,512]{1,0:T(8,128)(2,1)S(1)} %add_convert_fusion.3), channel_id=1, source_target_pairs={{0,4},{1,5},{2,6},{3,7},{4,0},{5,1},{6,2},{7,3},{8,12},{9,13},{10,... | collective-permute-start | bytes 1572872 | tf_op jit(solution)/shard_map/ppermute | solution.py:450
  79.7 25.2 %collective-permute-start.19 = (bf16[512,512]{1,0:T(8,128)(2,1)S(1)}, bf16[512,512]{1,0:T(8,128)(2,1)S(1)}, u32[]{:S(2)}, u32[]{:S(2)}) collective-permute-start(bf16[512,512]{1,0:T(8,128)(2,1)S(1)} %project.15), channel_id=1, source_target_pairs={{0,2},{1,3},{2,0},{3,1},{4,6},{5,7},{6,4},{7,5},{8,10},{9,11},{10,... | collective-permute-start | bytes 1572872 | tf_op jit(solution)/shard_map/ppermute | solution.py:450
  102.8 23.1 %collective-permute-start.18 = (bf16[512,512]{1,0:T(8,128)(2,1)S(1)}, bf16[512,512]{1,0:T(8,128)(2,1)S(1)}, u32[]{:S(2)}, u32[]{:S(2)}) collective-permute-start(bf16[512,512]{1,0:T(8,128)(2,1)S(1)} %project.12), channel_id=1, source_target_pairs={{0,2},{1,3},{2,0},{3,1},{4,6},{5,7},{6,4},{7,5},{8,10},{9,11},{10,... | collective-permute-start | bytes 1572872 | tf_op jit(solution)/shard_map/ppermute | solution.py:450
  105.0 25.4 %collective-permute-start.20 = (bf16[512,512]{1,0:T(8,128)(2,1)S(1)}, bf16[512,512]{1,0:T(8,128)(2,1)S(1)}, u32[]{:S(2)}, u32[]{:S(2)}) collective-permute-start(bf16[512,512]{1,0:T(8,128)(2,1)S(1)} %add_convert_fusion.1), channel_id=1, source_target_pairs={{0,4},{1,5},{2,6},{3,7},{4,0},{5,1},{6,2},{7,3},{8,12},{9,13},{10,... | collective-permute-start | bytes 1572872 | tf_op jit(solution)/shard_map/ppermute | solution.py:450

commit v8 on v7

--- a/solution.py
+++ b/solution.py
@@ -251,6 +251,7 @@
     per_block = rows // TILE
     lines = rows // HD
     key_rows = (2 * group if with_high else group) * rows
+    key_tiles = key_rows // TILE
     scaling = LOG2E / math.sqrt(HD)
 
     def kernel(ctx_ref, *refs):
@@ -261,7 +262,7 @@
         low_refs = [refs.pop(0) for _ in range(group - 1)]
         high_refs = [refs.pop(0) for _ in range(group - 1)] if with_high else None
         outs = [refs.pop(0) for _ in range(group)]
-        key_buf, value_buf, doc_buf, summed = refs
+        key_buf, value_buf, doc_buf, query_buf, start_buf, largest_buf, summed = refs
         ctx = ctx_ref[0]
 
         def part(upper, distance, index, lower=0, count=rows):
@@ -305,66 +306,84 @@
                 reached = doc_rows[with_high, distance] >= number
                 starts[distance] = jnp.where(reached, count, starts[distance])
 
-        def scores_of(distance, offset, count):
+        def scores_of(query, offset):
             raw = lax.dot_general(
-                key_buf[pl.ds(offset, count), :],
-                part(with_high, distance, 0),
+                key_buf[pl.ds(offset, TILE), :],
+                query,
                 (((1,), (1,)), ((), ())),
                 preferred_element_type=jnp.float32,
             )
             return raw * scaling
 
-        def weighted(weights, offset, count):
+        def weighted(weights, offset):
             return jnp.dot(
-                value_buf[:, pl.ds(offset, count)],
+                value_buf[:, pl.ds(offset, TILE)],
                 weights.astype(jnp.bfloat16),
                 preferred_element_type=jnp.float32,
             )
 
-        key_row = lax.broadcasted_iota(jnp.int32, (rows, rows), 0)
-        causal = key_row <= lax.broadcasted_iota(jnp.int32, (rows, rows), 1)
+        key_row = lax.broadcasted_iota(jnp.int32, (TILE, TILE), 0)
+        causal = key_row <= lax.broadcasted_iota(jnp.int32, (TILE, TILE), 1)
         key_row = key_row.astype(jnp.float32)
-        largest = []
         first_tiles = []
         ends = []
-        for distance in range(group):
-            block = place[with_high, distance]
-            offset = pl.multiple_of(block * rows, rows)
-            least = starts[distance] - offset.astype(jnp.float32)
-            scores = scores_of(distance, offset, rows)
-            scores = jnp.where((key_row >= least) & causal, scores, MASKED_SCORE)
-            largest.append(jnp.max(scores, axis=0, keepdims=True))
-            summed[distance] = weighted(jnp.exp2(scores - largest[-1]), offset, rows)
-            first_tiles.append(jnp.min(starts[distance]).astype(jnp.int32) // TILE)
-            ends.append(block * per_block)
-
-        longest = ends[0] - first_tiles[0]
-        for distance in range(1, group):
-            longest = jnp.maximum(longest, ends[distance] - first_tiles[distance])
-        tile_row = lax.broadcasted_iota(jnp.int32, (TILE, rows), 0).astype(jnp.float32)
-
-        def visit(step, running):
-            renewed = []
+        for tile in range(per_block):
             for distance in range(group):
-                wanted = first_tiles[distance] + step
-                index = jnp.maximum(jnp.minimum(wanted, ends[distance] - 1), 0)
-                offset = pl.multiple_of(index * TILE, TILE)
-                least = jnp.where(
-                    wanted < ends[distance], starts[distance] - offset.astype(jnp.float32), 1e9
-                )
-                scores = scores_of(distance, offset, TILE)
-                scores = jnp.where(tile_row >= least, scores, MASKED_SCORE)
-                new_max = jnp.maximum(running[distance], jnp.max(scores, axis=0, keepdims=True))
-                factor = jnp.exp2(running[distance] - new_max)
-                product = weighted(jnp.exp2(scores - new_max), offset, TILE)
-                summed[distance] = summed[distance] * factor + product
-                renewed.append(new_max)
-            return tuple(renewed)
-
-        lax.fori_loop(0, longest, visit, tuple(largest))
-        for distance in range(group):
-            attended = summed[distance, :HD, :] / summed[distance, HD : HD + 1, :]
-            outs[distance][...] = jnp.transpose(attended).astype(jnp.bfloat16)
+                slot = tile * group + distance
+                query = part(with_high, distance, 0, tile * TILE, TILE)
+                query_buf[slot] = query
+                start = starts[distance][:, tile * TILE : (tile + 1) * TILE]
+                start_buf[slot, 0:1, :] = start
+                end = place[with_high, distance] * per_block + tile
+                offset = pl.multiple_of(end * TILE, TILE)
+                least = start - offset.astype(jnp.float32)
+                scores = scores_of(query, offset)
+                scores = jnp.where((key_row >= least) & causal, scores, MASKED_SCORE)
+                largest = jnp.max(scores, axis=0, keepdims=True)
+                largest_buf[slot, 0:1, :] = largest
+                summed[slot] = weighted(jnp.exp2(scores - largest), offset)
+                first_tiles.append(jnp.min(start).astype(jnp.int32) // TILE)
+                ends.append(end)
+
+        counts = [end - first for end, first in zip(ends, first_tiles)]
+        lanes = [
+            [tile * group + (lane ^ (tile * (group - 1))) for tile in range(per_block)]
+            for lane in range(group)
+        ]
+        longest = jnp.int32(0)
+        for lane in lanes:
+            longest = jnp.maximum(longest, sum(counts[slot] for slot in lane))
+
+        def visit(step, carry):
+            for lane in lanes:
+                slot = jnp.int32(lane[0])
+                index = first_tiles[lane[0]] + step
+                before = counts[lane[0]]
+                for later in lane[1:]:
+                    reached = step >= before
+                    slot = jnp.where(reached, later, slot)
+                    index = jnp.where(reached, first_tiles[later] + step - before, index)
+                    before = before + counts[later]
+                offset = pl.multiple_of(jnp.minimum(index, key_tiles - 1) * TILE, TILE)
+                beyond = jnp.where(step < before, -offset.astype(jnp.float32), 1e9)
+                scores = scores_of(query_buf[slot], offset)
+                least = start_buf[slot, 0:1, :] + beyond
+                scores = jnp.where(key_row >= least, scores, MASKED_SCORE)
+                largest = largest_buf[slot, 0:1, :]
+                new_max = jnp.maximum(largest, jnp.max(scores, axis=0, keepdims=True))
+                product = weighted(jnp.exp2(scores - new_max), offset)
+                summed[slot] = summed[slot] * jnp.exp2(largest - new_max) + product
+                largest_buf[slot, 0:1, :] = new_max
+            return carry
+
+        lax.fori_loop(0, longest, visit, jnp.int32(0))
+        for tile in range(per_block):
+            for distance in range(group):
+                slot = tile * group + distance
+                attended = summed[slot, :HD, :] / summed[slot, HD : HD + 1, :]
+                outs[distance][tile * TILE : (tile + 1) * TILE, :] = jnp.transpose(
+                    attended
+                ).astype(jnp.bfloat16)
 
     def own(upper):
         return pl.BlockSpec((rows, HD), lambda step, ctx: (int(upper), ctx[0]))
@@ -388,7 +407,10 @@
                 pltpu.VMEM((key_rows, HD), jnp.bfloat16),
                 pltpu.VMEM((HD + 16, key_rows), jnp.bfloat16),
                 pltpu.VMEM((key_rows // HD, HD), jnp.float32),
-                pltpu.VMEM((group, HD + 16, rows), jnp.float32),
+                pltpu.VMEM((group * per_block, TILE, HD), jnp.bfloat16),
+                pltpu.VMEM((group * per_block, 8, TILE), jnp.float32),
+                pltpu.VMEM((group * per_block, 8, TILE), jnp.float32),
+                pltpu.VMEM((group * per_block, HD + 16, TILE), jnp.float32),
             ],
         ),
         out_shape=[jax.ShapeDtypeStruct((rows, HD), jnp.bfloat16)] * group,
@@ -502,6 +524,7 @@
     sibling = swap(mine, "head", 1)
     shares = [share_of(mine, sibling, turn) for turn in range(chips)]
     far = swap(shares[0], "head", 2)
+    shares[1], high[2] = tie(shares[1], high[2])
     near_sum = swap(shares[1], "head", 2)
 
     high, shares = tie(high, shares)

time: 130 us -> 135 us (1.038)
  Pallas kernels: 31.8 us -> 38 us
    pallas_call x2, Pallas kernels: 15 us -> 21.2 us  [attend(): pl.pallas_call(kernel, grid_spec=pltpu.PrefetchScalarGridSpec(num_scalar_...]
  transfers between devices with their start and end apart: 21 -> 21, of which waited for: 13 -> 11; matrix products, arithmetic and copies ran while one was open for 1% -> 1% of each run, Pallas kernels for 22% -> 26%
where the time goes in v8:
time: 135 us; the launch traced here: 137 us
  waiting for transfers between devices  73.2 us (54%)
  Pallas kernels  38 us (28%)
  starting transfers between devices  23.4 us (17%)
  other arithmetic  2.36 us (2%)
    ppermute x21, waiting for transfers between devices, swap(): lax.ppermute(value, axis, [(source, source ^ distance) for source in rang...  73.2 us
    ppermute x21, starting transfers between devices, swap(): lax.ppermute(value, axis, [(source, source ^ distance) for source in rang...  23.4 us
    pallas_call x2, Pallas kernels, attend(): pl.pallas_call(kernel, grid_spec=pltpu.PrefetchScalarGridSpec(num_scalar_...  21.2 us
    pallas_call x1, Pallas kernels, pack_projection(): pl.pallas_call(kernel, grid_spec=pltpu.PrefetchScalarGridSpec(num_scalar_...  5.89 us
    pallas_call x8, Pallas kernels, project(): pl.pallas_call(kernel, grid=(count,), in_specs=[attended, attended, weigh...  5.7 us
    pallas_call x2, Pallas kernels, pack(): pl.pallas_call(kernel, grid_spec=pltpu.PrefetchScalarGridSpec(num_scalar_...  5.05 us
  transfers between devices with their start and end apart: 21, of which 11 were waited for; matrix products, arithmetic and copies ran while one was open for 1% of the time, Pallas kernels for 26%

profile of v8, /device:TPU:0, one launch (start us, length us, event | category | flops | bytes accessed | tf_op | source)
XLA Modules:
  0.0 137.2 jit_solution(1515693439667947820)
XLA Ops:
  0.0 2.5 %pack.2 = (bf16[1552,128]{1,0:T(8,128)(2,1)}, bf16[1552,128]{1,0:T(8,128)(2,1)}, bf16[1552,128]{1,0:T(8,128)(2,1)}) custom-call(s32[1]{0:T(128)} %bitcast.ctx_ref, bf16[1024,512]{1,0:T(8,128)(2,1)} %refs_3_.4, bf16[1024,512]{1,0:T(8,128)(2,1)} %refs_4_.4, bf16[1024,512]{1,0:T(8,128)(2,1)} %refs_5_.4, bf16[1024,512]{1,0:T(8,128)(2,1)} %refs_3_.4, ...), custom_call_target="tpu_custom_call" | custom-call | flops 1024 | bytes 1024 | tf_op jit(solution)/shard_map/pack/pallas_call | solution.py:201
  2.5 2.9 %collective-permute-start = (bf16[1552,128]{1,0:T(8,128)(2,1)}, bf16[1552,128]{1,0:T(8,128)(2,1)S(1)}, u32[]{:S(2)}, u32[]{:S(2)}) collective-permute-start(bf16[1552,128]{1,0:T(8,128)(2,1)} %get-tuple-element.75), channel_id=1, source_target_pairs={{0,8},{8,0},{16,24},{24,16},{1,9},{9,1},{17,25},{25,17},{2,10},{10... | collective-permute-start | bytes 1191944 | tf_op jit(solution)/shard_map/ppermute | solution.py:472
  5.4 1.5 %collective-permute-start.1 = (bf16[1552,128]{1,0:T(8,128)(2,1)}, bf16[1552,128]{1,0:T(8,128)(2,1)S(1)}, u32[]{:S(2)}, u32[]{:S(2)}) collective-permute-start(bf16[1552,128]{1,0:T(8,128)(2,1)} %get-tuple-element.76), channel_id=1, source_target_pairs={{0,16},{8,24},{16,0},{24,8},{1,17},{9,25},{17,1},{25,9},{2,18},{10... | collective-permute-start | bytes 1191944 | tf_op jit(solution)/shard_map/ppermute | solution.py:472
  7.0 0.0 collective-permute-start.2
  7.0 2.5 %pack.3 = (bf16[1536,128]{1,0:T(8,128)(2,1)}, bf16[1536,128]{1,0:T(8,128)(2,1)}, bf16[1536,128]{1,0:T(8,128)(2,1)}) custom-call(s32[1]{0:T(128)} %bitcast.ctx_ref, bf16[1024,512]{1,0:T(8,128)(2,1)} %refs_3_.4, bf16[1024,512]{1,0:T(8,128)(2,1)} %refs_4_.4, bf16[1024,512]{1,0:T(8,128)(2,1)} %refs_5_.4, bf16[1024,512]{1,0:T(8,128)(2,1)} %refs_3_.4, ...), custom_call_target="tpu_custom_call" | custom-call | flops 1024 | bytes 1024 | tf_op jit(solution)/shard_map/pack/pallas_call | solution.py:201
  9.5 0.6 pad_add_fusion.places_ref
  10.2 0.0 copy-start.3
  10.2 0.0 copy-start.4
  10.2 5.9 %pack_projection.1 = (bf16[512,2048]{1,0:T(8,128)(2,1)}, bf16[512,2048]{1,0:T(8,128)(2,1)}) custom-call(s32[5]{0:T(128)} %pad_add_fusion.places_ref, bf16[512,4096]{1,0:T(8,128)(2,1)} %give_in, bf16[512,4096]{1,0:T(8,128)(2,1)} %give_in), custom_call_target="tpu_custom_call" | custom-call | flops 1024 | bytes 1024 | tf_op jit(solution)/shard_map/pack_projection/pallas_call | solution.py:232
  16.1 0.0 collective-permute-done.refs_4_.refs_7_
  16.1 8.7 %collective-permute-done.1.refs_5_.refs_8_ = bf16[1552,128]{1,0:T(8,128)(2,1)S(1)} collective-permute-done((bf16[1552,128]{1,0:T(8,128)(2,1)}, bf16[1552,128]{1,0:T(8,128)(2,1)S(1)}, u32[]{:S(2)}, u32[]{:S(2)}) %collective-permute-start.1) | collective-permute-done | bytes 397344 | tf_op jit(solution)/shard_map/ppermute | solution.py:472
  24.8 0.0 collective-permute-done.2.refs_6_.refs_9_
  24.8 0.1 collective-permute-start.3
  24.9 1.2 collective-permute-start.7
  26.1 0.9 collective-permute-start.8
  27.1 11.7 %attend_low.1 = (bf16[512,128]{1,0:T(8,128)(2,1)S(1)}, bf16[512,128]{1,0:T(8,128)(2,1)S(1)}, bf16[512,128]{1,0:T(8,128)(2,1)S(1)}, bf16[512,128]{1,0:T(8,128)(2,1)S(1)}) custom-call(s32[1]{0:T(128)} %bitcast.ctx_ref, bf16[1024,512]{1,0:T(8,128)(2,1)S(1)} %copy-done.1, bf16[1024,512]{1,0:T(8,128)(2,1)S(1)} %copy-done.2, bf16[1024,512]{1,0:T(8,128)(2,1)S(1)} %copy-done.3, ...), custom_call_target="tpu_custom_call" | custom-call | flops 1024 | bytes 1024 | tf_op jit(solution)/shard_map/attend_low/pallas_call | solution.py:399
  38.7 0.0 collective-permute-done.3.w_sibling_ref
  38.8 1.6 %collective-permute-start.4 = (bf16[512,128]{1,0:T(8,128)(2,1)S(1)}, bf16[512,128]{1,0:T(8,128)(2,1)S(1)}, u32[]{:S(2)}, u32[]{:S(2)}) collective-permute-start(bf16[512,128]{1,0:T(8,128)(2,1)S(1)} %get-tuple-element.89), channel_id=1, source_target_pairs={{0,8},{8,0},{16,24},{24,16},{1,9},{9,1},{17,25},{25,17},{2,10},{10... | collective-permute-start | bytes 393224 | tf_op jit(solution)/shard_map/ppermute | solution.py:472
  40.3 0.5 collective-permute-start.5
  40.8 1.5 %collective-permute-start.6 = (bf16[512,128]{1,0:T(8,128)(2,1)S(1)}, bf16[512,128]{1,0:T(8,128)(2,1)S(1)}, u32[]{:S(2)}, u32[]{:S(2)}) collective-permute-start(bf16[512,128]{1,0:T(8,128)(2,1)S(1)} %get-tuple-element.91), channel_id=1, source_target_pairs={{0,24},{8,16},{16,8},{24,0},{1,25},{9,17},{17,9},{25,1},{2,26},{10... | collective-permute-start | bytes 393224 | tf_op jit(solution)/shard_map/ppermute | solution.py:472
  42.3 0.0 collective-permute-done.7.refs_10_
  42.3 0.0 collective-permute-done.8.refs_11_
  42.3 2.1 %collective-permute-done.4.refs_1_ = bf16[512,128]{1,0:T(8,128)(2,1)S(1)} collective-permute-done((bf16[512,128]{1,0:T(8,128)(2,1)S(1)}, bf16[512,128]{1,0:T(8,128)(2,1)S(1)}, u32[]{:S(2)}, u32[]{:S(2)}) %collective-permute-start.4) | collective-permute-done | bytes 131104 | tf_op jit(solution)/shard_map/ppermute | solution.py:472
  44.5 3.7 %collective-permute-done.5.refs_2_ = bf16[512,128]{1,0:T(8,128)(2,1)S(1)} collective-permute-done((bf16[512,128]{1,0:T(8,128)(2,1)S(1)}, bf16[512,128]{1,0:T(8,128)(2,1)S(1)}, u32[]{:S(2)}, u32[]{:S(2)}) %collective-permute-start.5) | collective-permute-done | bytes 131104 | tf_op jit(solution)/shard_map/ppermute | solution.py:472
  48.1 0.0 collective-permute-done.6.refs_3_
  48.1 0.1 assemble.2.mine_ref
  48.2 0.1 collective-permute-start.9
  48.3 1.2 collective-permute-start.10
  49.6 0.6 collective-permute-done.9.sibling_ref
  50.2 0.7 project.9
  50.9 1.6 %collective-permute-start.14 = (bf16[512,512]{1,0:T(8,128)(2,1)S(1)}, bf16[512,512]{1,0:T(8,128)(2,1)S(1)}, u32[]{:S(2)}, u32[]{:S(2)}) collective-permute-start(bf16[512,512]{1,0:T(8,128)(2,1)S(1)} %project.9), channel_id=1, source_target_pairs={{0,2},{1,3},{2,0},{3,1},{4,6},{5,7},{6,4},{7,5},{8,10},{9,11},{10,... | collective-permute-start | bytes 1572872 | tf_op jit(solution)/shard_map/ppermute | solution.py:472
  52.6 0.7 project.8
  53.3 7.5 %collective-permute-done.10.refs_12_ = bf16[1536,128]{1,0:T(8,128)(2,1)S(1)} collective-permute-done((bf16[1536,128]{1,0:T(8,128)(2,1)S(1)}, bf16[1536,128]{1,0:T(8,128)(2,1)S(1)}, u32[]{:S(2)}, u32[]{:S(2)}) %collective-permute-start.10) | collective-permute-done | bytes 393248 | tf_op jit(solution)/shard_map/ppermute | solution.py:472
  60.7 1.6 %collective-permute-start.15 = (bf16[512,512]{1,0:T(8,128)(2,1)S(1)}, bf16[512,512]{1,0:T(8,128)(2,1)S(1)}, u32[]{:S(2)}, u32[]{:S(2)}) collective-permute-start(bf16[512,512]{1,0:T(8,128)(2,1)S(1)} %project.8), channel_id=1, source_target_pairs={{0,2},{1,3},{2,0},{3,1},{4,6},{5,7},{6,4},{7,5},{8,10},{9,11},{10,... | collective-permute-start | bytes 1572872 | tf_op jit(solution)/shard_map/ppermute | solution.py:472
  62.3 0.7 project.11
  63.0 0.7 project.10
  63.8 9.5 %attend_high.1 = (bf16[512,128]{1,0:T(8,128)(2,1)S(1)}, bf16[512,128]{1,0:T(8,128)(2,1)S(1)}, bf16[512,128]{1,0:T(8,128)(2,1)S(1)}, bf16[512,128]{1,0:T(8,128)(2,1)S(1)}) custom-call(s32[1]{0:T(128)} %bitcast.ctx_ref, bf16[1024,512]{1,0:T(8,128)(2,1)S(1)} %copy-done.1, bf16[1024,512]{1,0:T(8,128)(2,1)S(1)} %copy-done.2, bf16[1024,512]{1,0:T(8,128)(2,1)S(1)} %copy-done.3, ...), custom_call_target="tpu_custom_call" | custom-call | flops 1024 | bytes 1024 | tf_op jit(solution)/shard_map/attend_high/pallas_call | solution.py:399
  73.3 0.6 collective-permute-start.11
  73.9 1.2 collective-permute-start.12
  75.1 1.7 %collective-permute-start.13 = (bf16[512,128]{1,0:T(8,128)(2,1)S(1)}, bf16[512,128]{1,0:T(8,128)(2,1)S(1)}, u32[]{:S(2)}, u32[]{:S(2)}) collective-permute-start(bf16[512,128]{1,0:T(8,128)(2,1)S(1)} %get-tuple-element.111), channel_id=1, source_target_pairs={{0,24},{8,16},{16,8},{24,0},{1,25},{9,17},{17,9},{25,1},{2,26},{10... | collective-permute-start | bytes 393224 | tf_op jit(solution)/shard_map/ppermute | solution.py:472
  76.8 0.0 collective-permute-done.14
  76.8 0.1 add_convert_fusion.3
  77.0 2.6 %collective-permute-done.11.refs_1_ = bf16[512,128]{1,0:T(8,128)(2,1)S(1)} collective-permute-done((bf16[512,128]{1,0:T(8,128)(2,1)S(1)}, bf16[512,128]{1,0:T(8,128)(2,1)S(1)}, u32[]{:S(2)}, u32[]{:S(2)}) %collective-permute-start.11) | collective-permute-done | bytes 131104 | tf_op jit(solution)/shard_map/ppermute | solution.py:472
  79.5 2.1 %collective-permute-done.12.refs_2_ = bf16[512,128]{1,0:T(8,128)(2,1)S(1)} collective-permute-done((bf16[512,128]{1,0:T(8,128)(2,1)S(1)}, bf16[512,128]{1,0:T(8,128)(2,1)S(1)}, u32[]{:S(2)}, u32[]{:S(2)}) %collective-permute-start.12) | collective-permute-done | bytes 131104 | tf_op jit(solution)/shard_map/ppermute | solution.py:472
  81.6 0.0 collective-permute-done.13.refs_3_
  81.6 0.1 assemble.3.mine_ref
  81.7 0.1 collective-permute-start.16
  81.8 2.6 %collective-permute-start.17 = (bf16[512,512]{1,0:T(8,128)(2,1)S(1)}, bf16[512,512]{1,0:T(8,128)(2,1)S(1)}, u32[]{:S(2)}, u32[]{:S(2)}) collective-permute-start(bf16[512,512]{1,0:T(8,128)(2,1)S(1)} %add_convert_fusion.3), channel_id=1, source_target_pairs={{0,4},{1,5},{2,6},{3,7},{4,0},{5,1},{6,2},{7,3},{8,12},{9,13},{10,... | collective-permute-start | bytes 1572872 | tf_op jit(solution)/shard_map/ppermute | solution.py:472
  84.4 0.0 collective-permute-done.16.sibling_ref
  84.4 0.7 project.15
  85.2 0.5 collective-permute-start.19
  85.7 0.7 project.12
  86.4 21.9 %collective-permute-done.17 = bf16[512,512]{1,0:T(8,128)(2,1)S(1)} collective-permute-done((bf16[512,512]{1,0:T(8,128)(2,1)S(1)}, bf16[512,512]{1,0:T(8,128)(2,1)S(1)}, u32[]{:S(2)}, u32[]{:S(2)}) %collective-permute-start.17) | collective-permute-done | bytes 524320 | tf_op jit(solution)/shard_map/ppermute | solution.py:472
  108.3 0.0 collective-permute-start.18
  108.3 0.7 project.14
  109.0 1.4 %collective-permute-done.19 = bf16[512,512]{1,0:T(8,128)(2,1)S(1)} collective-permute-done((bf16[512,512]{1,0:T(8,128)(2,1)S(1)}, bf16[512,512]{1,0:T(8,128)(2,1)S(1)}, u32[]{:S(2)}, u32[]{:S(2)}) %collective-permute-start.19) | collective-permute-done | bytes 524320 | tf_op jit(solution)/shard_map/ppermute | solution.py:472
  110.4 0.1 add_convert_fusion.1
  110.5 1.9 %collective-permute-start.20 = (bf16[512,512]{1,0:T(8,128)(2,1)S(1)}, bf16[512,512]{1,0:T(8,128)(2,1)S(1)}, u32[]{:S(2)}, u32[]{:S(2)}) collective-permute-start(bf16[512,512]{1,0:T(8,128)(2,1)S(1)} %add_convert_fusion.1), channel_id=1, source_target_pairs={{0,4},{1,5},{2,6},{3,7},{4,0},{5,1},{6,2},{7,3},{8,12},{9,13},{10,... | collective-permute-start | bytes 1572872 | tf_op jit(solution)/shard_map/ppermute | solution.py:472
  112.4 0.7 project.13
  113.1 0.2 add_convert_fusion.2
  113.3 18.0 %collective-permute-done.18 = bf16[512,512]{1,0:T(8,128)(2,1)S(1)} collective-permute-done((bf16[512,512]{1,0:T(8,128)(2,1)S(1)}, bf16[512,512]{1,0:T(8,128)(2,1)S(1)}, u32[]{:S(2)}, u32[]{:S(2)}) %collective-permute-start.18) | collective-permute-done | bytes 524320 | tf_op jit(solution)/shard_map/ppermute | solution.py:472
  131.3 4.6 %collective-permute-done.20 = bf16[512,512]{1,0:T(8,128)(2,1)S(1)} collective-permute-done((bf16[512,512]{1,0:T(8,128)(2,1)S(1)}, bf16[512,512]{1,0:T(8,128)(2,1)S(1)}, u32[]{:S(2)}, u32[]{:S(2)}) %collective-permute-start.20) | collective-permute-done | bytes 524320 | tf_op jit(solution)/shard_map/ppermute | solution.py:472
  135.9 0.2 add_convert_fusion
  136.1 1.0 pad_maximum_fusion
  (18 shorter events, 0.0 us)
Async XLA Ops:
  2.5 7.0 %copy-start.8 = (s32[4]{0:T(128)S(1)}, s32[4]{0:T(128)}, u32[]{:S(2)}) copy-start(s32[4]{0:T(128)} %constant.34.clone) | copy-start | bytes 52
  2.5 13.6 %collective-permute-start = (bf16[1552,128]{1,0:T(8,128)(2,1)}, bf16[1552,128]{1,0:T(8,128)(2,1)S(1)}, u32[]{:S(2)}, u32[]{:S(2)}) collective-permute-start(bf16[1552,128]{1,0:T(8,128)(2,1)} %get-tuple-element.75), channel_id=1, source_target_pairs={{0,8},{8,0},{16,24},{24,16},{1,9},{9,1},{17,25},{25,17},{2,10},{10... | collective-permute-start | bytes 1191944 | tf_op jit(solution)/shard_map/ppermute | solution.py:472
  5.4 19.4 %collective-permute-start.1 = (bf16[1552,128]{1,0:T(8,128)(2,1)}, bf16[1552,128]{1,0:T(8,128)(2,1)S(1)}, u32[]{:S(2)}, u32[]{:S(2)}) collective-permute-start(bf16[1552,128]{1,0:T(8,128)(2,1)} %get-tuple-element.76), channel_id=1, source_target_pairs={{0,16},{8,24},{16,0},{24,8},{1,17},{9,25},{17,1},{25,9},{2,18},{10... | collective-permute-start | bytes 1191944 | tf_op jit(solution)/shard_map/ppermute | solution.py:472
  7.0 17.9 %collective-permute-start.2 = (bf16[1552,128]{1,0:T(8,128)(2,1)}, bf16[1552,128]{1,0:T(8,128)(2,1)S(1)}, u32[]{:S(2)}, u32[]{:S(2)}) collective-permute-start(bf16[1552,128]{1,0:T(8,128)(2,1)} %get-tuple-element.77), channel_id=1, source_target_pairs={{0,24},{8,16},{16,8},{24,0},{1,25},{9,17},{17,9},{25,1},{2,26},{10... | collective-permute-start | bytes 1191944 | tf_op jit(solution)/shard_map/ppermute | solution.py:472
  10.2 14.8 %copy-start.7 = (bf16[1536,128]{1,0:T(8,128)(2,1)S(1)}, bf16[1536,128]{1,0:T(8,128)(2,1)}, u32[]{:S(2)}) copy-start(bf16[1536,128]{1,0:T(8,128)(2,1)} %get-tuple-element.92) | copy-start | bytes 1179652
  10.2 16.0 %copy-start.6 = (bf16[1536,128]{1,0:T(8,128)(2,1)S(1)}, bf16[1536,128]{1,0:T(8,128)(2,1)}, u32[]{:S(2)}) copy-start(bf16[1536,128]{1,0:T(8,128)(2,1)} %get-tuple-element.93) | copy-start | bytes 1179652
  10.2 16.9 %copy-start.1 = (bf16[1024,512]{1,0:T(8,128)(2,1)S(1)}, bf16[1024,512]{1,0:T(8,128)(2,1)}, u32[]{:S(2)}) copy-start(bf16[1024,512]{1,0:T(8,128)(2,1)} %refs_3_.4) | copy-start | bytes 3145732
  10.2 16.9 %copy-start.2 = (bf16[1024,512]{1,0:T(8,128)(2,1)S(1)}, bf16[1024,512]{1,0:T(8,128)(2,1)}, u32[]{:S(2)}) copy-start(bf16[1024,512]{1,0:T(8,128)(2,1)} %refs_4_.4) | copy-start | bytes 3145732
  10.2 16.9 %copy-start.3 = (bf16[1024,512]{1,0:T(8,128)(2,1)S(1)}, bf16[1024,512]{1,0:T(8,128)(2,1)}, u32[]{:S(2)}) copy-start(bf16[1024,512]{1,0:T(8,128)(2,1)} %refs_5_.4) | copy-start | bytes 3145732
  10.2 16.9 %copy-start.4 = (s32[1024]{0:T(1024)S(1)}, s32[1024]{0:T(1024)}, u32[]{:S(2)}) copy-start(s32[1024]{0:T(1024)} %param.9) | copy-start | bytes 12292
  24.8 23.5 %copy-start.5 = (bf16[1536,128]{1,0:T(8,128)(2,1)S(1)}, bf16[1536,128]{1,0:T(8,128)(2,1)}, u32[]{:S(2)}) copy-start(bf16[1536,128]{1,0:T(8,128)(2,1)} %get-tuple-element.102) | copy-start | bytes 1179652
  24.8 25.4 %copy-start = (bf16[512,2048]{1,0:T(8,128)(2,1)S(1)}, bf16[512,2048]{1,0:T(8,128)(2,1)}, u32[]{:S(2)}) copy-start(bf16[512,2048]{1,0:T(8,128)(2,1)} %get-tuple-element.100.w_mine_ref) | copy-start | bytes 6291460
  24.8 13.9 %collective-permute-start.3 = (bf16[512,2048]{1,0:T(8,128)(2,1)}, bf16[512,2048]{1,0:T(8,128)(2,1)S(1)}, u32[]{:S(2)}, u32[]{:S(2)}) collective-permute-start(bf16[512,2048]{1,0:T(8,128)(2,1)} %get-tuple-element.88), channel_id=1, source_target_pairs={{0,1},{1,0},{2,3},{3,2},{4,5},{5,4},{6,7},{7,6},{8,9},{9,8},{10,11... | collective-permute-start | bytes 6291464 | tf_op jit(solution)/shard_map/ppermute | solution.py:472
  24.9 17.4 %collective-permute-start.7 = (bf16[1536,128]{1,0:T(8,128)(2,1)S(1)}, bf16[1536,128]{1,0:T(8,128)(2,1)S(1)}, u32[]{:S(2)}, u32[]{:S(2)}) collective-permute-start(bf16[1536,128]{1,0:T(8,128)(2,1)S(1)} %copy-done.7), channel_id=1, source_target_pairs={{0,8},{8,0},{16,24},{24,16},{1,9},{9,1},{17,25},{25,17},{2,10},{10... | collective-permute-start | bytes 1179656 | tf_op jit(solution)/shard_map/ppermute | solution.py:472
  26.1 16.2 %collective-permute-start.8 = (bf16[1536,128]{1,0:T(8,128)(2,1)S(1)}, bf16[1536,128]{1,0:T(8,128)(2,1)S(1)}, u32[]{:S(2)}, u32[]{:S(2)}) collective-permute-start(bf16[1536,128]{1,0:T(8,128)(2,1)S(1)} %copy-done.6), channel_id=1, source_target_pairs={{0,16},{8,24},{16,0},{24,8},{1,17},{9,25},{17,1},{25,9},{2,18},{10... | collective-permute-start | bytes 1179656 | tf_op jit(solution)/shard_map/ppermute | solution.py:472
  38.8 5.7 %collective-permute-start.4 = (bf16[512,128]{1,0:T(8,128)(2,1)S(1)}, bf16[512,128]{1,0:T(8,128)(2,1)S(1)}, u32[]{:S(2)}, u32[]{:S(2)}) collective-permute-start(bf16[512,128]{1,0:T(8,128)(2,1)S(1)} %get-tuple-element.89), channel_id=1, source_target_pairs={{0,8},{8,0},{16,24},{24,16},{1,9},{9,1},{17,25},{25,17},{2,10},{10... | collective-permute-start | bytes 393224 | tf_op jit(solution)/shard_map/ppermute | solution.py:472
  40.3 7.8 %collective-permute-start.5 = (bf16[512,128]{1,0:T(8,128)(2,1)S(1)}, bf16[512,128]{1,0:T(8,128)(2,1)S(1)}, u32[]{:S(2)}, u32[]{:S(2)}) collective-permute-start(bf16[512,128]{1,0:T(8,128)(2,1)S(1)} %get-tuple-element.90), channel_id=1, source_target_pairs={{0,16},{8,24},{16,0},{24,8},{1,17},{9,25},{17,1},{25,9},{2,18},{10... | collective-permute-start | bytes 393224 | tf_op jit(solution)/shard_map/ppermute | solution.py:472
  40.8 7.3 %collective-permute-start.6 = (bf16[512,128]{1,0:T(8,128)(2,1)S(1)}, bf16[512,128]{1,0:T(8,128)(2,1)S(1)}, u32[]{:S(2)}, u32[]{:S(2)}) collective-permute-start(bf16[512,128]{1,0:T(8,128)(2,1)S(1)} %get-tuple-element.91), channel_id=1, source_target_pairs={{0,24},{8,16},{16,8},{24,0},{1,25},{9,17},{17,9},{25,1},{2,26},{10... | collective-permute-start | bytes 393224 | tf_op jit(solution)/shard_map/ppermute | solution.py:472
  48.2 2.0 %collective-permute-start.9 = (bf16[512,512]{1,0:T(8,128)(2,1)S(1)}, bf16[512,512]{1,0:T(8,128)(2,1)S(1)}, u32[]{:S(2)}, u32[]{:S(2)}) collective-permute-start(bf16[512,512]{1,0:T(8,128)(2,1)S(1)} %assemble.2.mine_ref), channel_id=1, source_target_pairs={{0,1},{1,0},{2,3},{3,2},{4,5},{5,4},{6,7},{7,6},{8,9},{9,8},{10,11... | collective-permute-start | bytes 1572872 | tf_op jit(solution)/shard_map/ppermute | solution.py:472
  48.3 12.4 %collective-permute-start.10 = (bf16[1536,128]{1,0:T(8,128)(2,1)S(1)}, bf16[1536,128]{1,0:T(8,128)(2,1)S(1)}, u32[]{:S(2)}, u32[]{:S(2)}) collective-permute-start(bf16[1536,128]{1,0:T(8,128)(2,1)S(1)} %copy-done.5), channel_id=1, source_target_pairs={{0,24},{8,16},{16,8},{24,0},{1,25},{9,17},{17,9},{25,1},{2,26},{10... | collective-permute-start | bytes 1179656 | tf_op jit(solution)/shard_map/ppermute | solution.py:472
  50.9 25.9 %collective-permute-start.14 = (bf16[512,512]{1,0:T(8,128)(2,1)S(1)}, bf16[512,512]{1,0:T(8,128)(2,1)S(1)}, u32[]{:S(2)}, u32[]{:S(2)}) collective-permute-start(bf16[512,512]{1,0:T(8,128)(2,1)S(1)} %project.9), channel_id=1, source_target_pairs={{0,2},{1,3},{2,0},{3,1},{4,6},{5,7},{6,4},{7,5},{8,10},{9,11},{10,... | collective-permute-start | bytes 1572872 | tf_op jit(solution)/shard_map/ppermute | solution.py:472
  60.7 20.9 %collective-permute-start.15 = (bf16[512,512]{1,0:T(8,128)(2,1)S(1)}, bf16[512,512]{1,0:T(8,128)(2,1)S(1)}, u32[]{:S(2)}, u32[]{:S(2)}) collective-permute-start(bf16[512,512]{1,0:T(8,128)(2,1)S(1)} %project.8), channel_id=1, source_target_pairs={{0,2},{1,3},{2,0},{3,1},{4,6},{5,7},{6,4},{7,5},{8,10},{9,11},{10,... | collective-permute-start | bytes 1572872 | tf_op jit(solution)/shard_map/ppermute | solution.py:472
  73.3 6.3 %collective-permute-start.11 = (bf16[512,128]{1,0:T(8,128)(2,1)S(1)}, bf16[512,128]{1,0:T(8,128)(2,1)S(1)}, u32[]{:S(2)}, u32[]{:S(2)}) collective-permute-start(bf16[512,128]{1,0:T(8,128)(2,1)S(1)} %get-tuple-element.109), channel_id=1, source_target_pairs={{0,8},{8,0},{16,24},{24,16},{1,9},{9,1},{17,25},{25,17},{2,10},{10... | collective-permute-start | bytes 393224 | tf_op jit(solution)/shard_map/ppermute | solution.py:472
  73.9 7.7 %collective-permute-start.12 = (bf16[512,128]{1,0:T(8,128)(2,1)S(1)}, bf16[512,128]{1,0:T(8,128)(2,1)S(1)}, u32[]{:S(2)}, u32[]{:S(2)}) collective-permute-start(bf16[512,128]{1,0:T(8,128)(2,1)S(1)} %get-tuple-element.110), channel_id=1, source_target_pairs={{0,16},{8,24},{16,0},{24,8},{1,17},{9,25},{17,1},{25,9},{2,18},{10... | collective-permute-start | bytes 393224 | tf_op jit(solution)/shard_map/ppermute | solution.py:472
  75.1 6.5 %collective-permute-start.13 = (bf16[512,128]{1,0:T(8,128)(2,1)S(1)}, bf16[512,128]{1,0:T(8,128)(2,1)S(1)}, u32[]{:S(2)}, u32[]{:S(2)}) collective-permute-start(bf16[512,128]{1,0:T(8,128)(2,1)S(1)} %get-tuple-element.111), channel_id=1, source_target_pairs={{0,24},{8,16},{16,8},{24,0},{1,25},{9,17},{17,9},{25,1},{2,26},{10... | collective-permute-start | bytes 393224 | tf_op jit(solution)/shard_map/ppermute | solution.py:472
  81.7 2.7 %collective-permute-start.16 = (bf16[512,512]{1,0:T(8,128)(2,1)S(1)}, bf16[512,512]{1,0:T(8,128)(2,1)S(1)}, u32[]{:S(2)}, u32[]{:S(2)}) collective-permute-start(bf16[512,512]{1,0:T(8,128)(2,1)S(1)} %assemble.3.mine_ref), channel_id=1, source_target_pairs={{0,1},{1,0},{2,3},{3,2},{4,5},{5,4},{6,7},{7,6},{8,9},{9,8},{10,11... | collective-permute-start | bytes 1572872 | tf_op jit(solution)/shard_map/ppermute | solution.py:472
  81.8 26.5 %collective-permute-start.17 = (bf16[512,512]{1,0:T(8,128)(2,1)S(1)}, bf16[512,512]{1,0:T(8,128)(2,1)S(1)}, u32[]{:S(2)}, u32[]{:S(2)}) collective-permute-start(bf16[512,512]{1,0:T(8,128)(2,1)S(1)} %add_convert_fusion.3), channel_id=1, source_target_pairs={{0,4},{1,5},{2,6},{3,7},{4,0},{5,1},{6,2},{7,3},{8,12},{9,13},{10,... | collective-permute-start | bytes 1572872 | tf_op jit(solution)/shard_map/ppermute | solution.py:472
  85.2 25.2 %collective-permute-start.19 = (bf16[512,512]{1,0:T(8,128)(2,1)S(1)}, bf16[512,512]{1,0:T(8,128)(2,1)S(1)}, u32[]{:S(2)}, u32[]{:S(2)}) collective-permute-start(bf16[512,512]{1,0:T(8,128)(2,1)S(1)} %project.15), channel_id=1, source_target_pairs={{0,2},{1,3},{2,0},{3,1},{4,6},{5,7},{6,4},{7,5},{8,10},{9,11},{10,... | collective-permute-start | bytes 1572872 | tf_op jit(solution)/shard_map/ppermute | solution.py:472
  108.3 23.0 %collective-permute-start.18 = (bf16[512,512]{1,0:T(8,128)(2,1)S(1)}, bf16[512,512]{1,0:T(8,128)(2,1)S(1)}, u32[]{:S(2)}, u32[]{:S(2)}) collective-permute-start(bf16[512,512]{1,0:T(8,128)(2,1)S(1)} %project.12), channel_id=1, source_target_pairs={{0,2},{1,3},{2,0},{3,1},{4,6},{5,7},{6,4},{7,5},{8,10},{9,11},{10,... | collective-permute-start | bytes 1572872 | tf_op jit(solution)/shard_map/ppermute | solution.py:472
  110.5 25.4 %collective-permute-start.20 = (bf16[512,512]{1,0:T(8,128)(2,1)S(1)}, bf16[512,512]{1,0:T(8,128)(2,1)S(1)}, u32[]{:S(2)}, u32[]{:S(2)}) collective-permute-start(bf16[512,512]{1,0:T(8,128)(2,1)S(1)} %add_convert_fusion.1), channel_id=1, source_target_pairs={{0,4},{1,5},{2,6},{3,7},{4,0},{5,1},{6,2},{7,3},{8,12},{9,13},{10,... | collective-permute-start | bytes 1572872 | tf_op jit(solution)/shard_map/ppermute | solution.py:472

commit v9 on v8

--- a/solution.py
+++ b/solution.py
@@ -262,7 +262,10 @@
         low_refs = [refs.pop(0) for _ in range(group - 1)]
         high_refs = [refs.pop(0) for _ in range(group - 1)] if with_high else None
         outs = [refs.pop(0) for _ in range(group)]
-        key_buf, value_buf, doc_buf, query_buf, start_buf, largest_buf, summed = refs
+        key_buf, value_buf, doc_buf = refs[:3]
+        query_buf, start_buf, largest_buf, summed = (
+            refs[3 + kind * group : 3 + (kind + 1) * group] for kind in range(4)
+        )
         ctx = ctx_ref[0]
 
         def part(upper, distance, index, lower=0, count=rows):
@@ -325,65 +328,77 @@
         key_row = lax.broadcasted_iota(jnp.int32, (TILE, TILE), 0)
         causal = key_row <= lax.broadcasted_iota(jnp.int32, (TILE, TILE), 1)
         key_row = key_row.astype(jnp.float32)
-        first_tiles = []
-        ends = []
-        for tile in range(per_block):
-            for distance in range(group):
-                slot = tile * group + distance
-                query = part(with_high, distance, 0, tile * TILE, TILE)
-                query_buf[slot] = query
-                start = starts[distance][:, tile * TILE : (tile + 1) * TILE]
-                start_buf[slot, 0:1, :] = start
-                end = place[with_high, distance] * per_block + tile
+        firsts = []
+        counts = []
+        for lane in range(group):
+            for slot in range(per_block):
+                distance = lane ^ (slot * (group - 1))
+                query = part(with_high, distance, 0, slot * TILE, TILE)
+                query_buf[lane][slot] = query
+                start = starts[distance][:, slot * TILE : (slot + 1) * TILE]
+                start_buf[lane][slot, 0:1, :] = start
+                end = place[with_high, distance] * per_block + slot
                 offset = pl.multiple_of(end * TILE, TILE)
                 least = start - offset.astype(jnp.float32)
                 scores = scores_of(query, offset)
                 scores = jnp.where((key_row >= least) & causal, scores, MASKED_SCORE)
                 largest = jnp.max(scores, axis=0, keepdims=True)
-                largest_buf[slot, 0:1, :] = largest
-                summed[slot] = weighted(jnp.exp2(scores - largest), offset)
-                first_tiles.append(jnp.min(start).astype(jnp.int32) // TILE)
-                ends.append(end)
-
-        counts = [end - first for end, first in zip(ends, first_tiles)]
-        lanes = [
-            [tile * group + (lane ^ (tile * (group - 1))) for tile in range(per_block)]
-            for lane in range(group)
-        ]
+                largest_buf[lane][slot, 0:1, :] = largest
+                summed[lane][slot] = weighted(jnp.exp2(scores - largest), offset)
+                first = jnp.min(start).astype(jnp.int32) // TILE
+                firsts.append(first)
+                counts.append(end - first)
+
         longest = jnp.int32(0)
-        for lane in lanes:
-            longest = jnp.maximum(longest, sum(counts[slot] for slot in lane))
+        for lane in range(group):
+            of_lane = counts[lane * per_block : (lane + 1) * per_block]
+            longest = jnp.maximum(longest, sum(of_lane))
 
         def visit(step, carry):
-            for lane in lanes:
-                slot = jnp.int32(lane[0])
-                index = first_tiles[lane[0]] + step
-                before = counts[lane[0]]
-                for later in lane[1:]:
+            slots = []
+            offsets = []
+            beyonds = []
+            for lane in range(group):
+                slot = jnp.int32(0)
+                index = firsts[lane * per_block] + step
+                before = counts[lane * per_block]
+                for later in range(1, per_block):
                     reached = step >= before
                     slot = jnp.where(reached, later, slot)
-                    index = jnp.where(reached, first_tiles[later] + step - before, index)
-                    before = before + counts[later]
+                    place_later = lane * per_block + later
+                    index = jnp.where(reached, firsts[place_later] + step - before, index)
+                    before = before + counts[place_later]
                 offset = pl.multiple_of(jnp.minimum(index, key_tiles - 1) * TILE, TILE)
-                beyond = jnp.where(step < before, -offset.astype(jnp.float32), 1e9)
-                scores = scores_of(query_buf[slot], offset)
-                least = start_buf[slot, 0:1, :] + beyond
-                scores = jnp.where(key_row >= least, scores, MASKED_SCORE)
-                largest = largest_buf[slot, 0:1, :]
-                new_max = jnp.maximum(largest, jnp.max(scores, axis=0, keepdims=True))
-                product = weighted(jnp.exp2(scores - new_max), offset)
-                summed[slot] = summed[slot] * jnp.exp2(largest - new_max) + product
-                largest_buf[slot, 0:1, :] = new_max
+                slots.append(slot)
+                offsets.append(offset)
+                beyonds.append(jnp.where(step < before, -offset.astype(jnp.float32), 1e9))
+            each = range(group)
+            scores = [scores_of(query_buf[lane][slots[lane]], offsets[lane]) for lane in each]
+            old_max = [largest_buf[lane][slots[lane], 0:1, :] for lane in each]
+            new_max = []
+            for lane in each:
+                least = start_buf[lane][slots[lane], 0:1, :] + beyonds[lane]
+                scores[lane] = jnp.where(key_row >= least, scores[lane], MASKED_SCORE)
+                tile_max = jnp.max(scores[lane], axis=0, keepdims=True)
+                new_max.append(jnp.maximum(old_max[lane], tile_max))
+            products = [
+                weighted(jnp.exp2(scores[lane] - new_max[lane]), offsets[lane]) for lane in each
+            ]
+            for lane in each:
+                factor = jnp.exp2(old_max[lane] - new_max[lane])
+                summed[lane][slots[lane]] = summed[lane][slots[lane]] * factor + products[lane]
+                largest_buf[lane][slots[lane], 0:1, :] = new_max[lane]
             return carry
 
         lax.fori_loop(0, longest, visit, jnp.int32(0))
-        for tile in range(per_block):
-            for distance in range(group):
-                slot = tile * group + distance
-                attended = summed[slot, :HD, :] / summed[slot, HD : HD + 1, :]
-                outs[distance][tile * TILE : (tile + 1) * TILE, :] = jnp.transpose(
-                    attended
-                ).astype(jnp.bfloat16)
+        for lane in range(group):
+            for slot in range(per_block):
+                state = summed[lane]
+                attended = state[slot, :HD, :] / state[slot, HD : HD + 1, :]
+                out = outs[lane ^ (slot * (group - 1))]
+                out[slot * TILE : (slot + 1) * TILE, :] = jnp.transpose(attended).astype(
+                    jnp.bfloat16
+                )
 
     def own(upper):
         return pl.BlockSpec((rows, HD), lambda step, ctx: (int(upper), ctx[0]))
@@ -407,10 +422,9 @@
                 pltpu.VMEM((key_rows, HD), jnp.bfloat16),
                 pltpu.VMEM((HD + 16, key_rows), jnp.bfloat16),
                 pltpu.VMEM((key_rows // HD, HD), jnp.float32),
-                pltpu.VMEM((group * per_block, TILE, HD), jnp.bfloat16),
-                pltpu.VMEM((group * per_block, 8, TILE), jnp.float32),
-                pltpu.VMEM((group * per_block, 8, TILE), jnp.float32),
-                pltpu.VMEM((group * per_block, HD + 16, TILE), jnp.float32),
+                *[pltpu.VMEM((per_block, TILE, HD), jnp.bfloat16)] * group,
+                *[pltpu.VMEM((per_block, 8, TILE), jnp.float32)] * (2 * group),
+                *[pltpu.VMEM((per_block, HD + 16, TILE), jnp.float32)] * group,
             ],
         ),
         out_shape=[jax.ShapeDtypeStruct((rows, HD), jnp.bfloat16)] * group,

time: 135 us -> 129 us (0.956); the launches traced: 137 us -> 129 us
  Pallas kernels: 38 us -> 30.3 us
    pallas_call x2, Pallas kernels: 21.2 us -> 13.5 us  [attend(): pl.pallas_call(kernel, grid_spec=pltpu.PrefetchScalarGridSpec(num_scalar_...]
  transfers between devices with their start and end apart: 21 -> 21, of which waited for: 11 -> 11; matrix products, arithmetic and copies ran while one was open for 1% -> 1% of each run, Pallas kernels for 26% -> 21%
where the time goes in v9:
time: 129 us
  waiting for transfers between devices  73.2 us (57%)
  Pallas kernels  30.3 us (23%)
  starting transfers between devices  23.4 us (18%)
  other arithmetic  2.36 us (2%)
    ppermute x21, waiting for transfers between devices, swap(): lax.ppermute(value, axis, [(source, source ^ distance) for source in rang...  73.2 us
    ppermute x21, starting transfers between devices, swap(): lax.ppermute(value, axis, [(source, source ^ distance) for source in rang...  23.4 us
    pallas_call x2, Pallas kernels, attend(): pl.pallas_call(kernel, grid_spec=pltpu.PrefetchScalarGridSpec(num_scalar_...  13.5 us
    pallas_call x1, Pallas kernels, pack_projection(): pl.pallas_call(kernel, grid_spec=pltpu.PrefetchScalarGridSpec(num_scalar_...  5.89 us
    pallas_call x8, Pallas kernels, project(): pl.pallas_call(kernel, grid=(count,), in_specs=[attended, attended, weigh...  5.7 us
    pallas_call x2, Pallas kernels, pack(): pl.pallas_call(kernel, grid_spec=pltpu.PrefetchScalarGridSpec(num_scalar_...  5.05 us
  transfers between devices with their start and end apart: 21, of which 11 were waited for; matrix products, arithmetic and copies ran while one was open for 1% of the time, Pallas kernels for 21%

profile of v9, /device:TPU:0, one launch (start us, length us, event | category | flops | bytes accessed | tf_op | source)
XLA Modules:
  0.0 129.4 jit_solution(4070309627733391483)
XLA Ops:
  0.0 2.5 %pack.2 = (bf16[1552,128]{1,0:T(8,128)(2,1)}, bf16[1552,128]{1,0:T(8,128)(2,1)}, bf16[1552,128]{1,0:T(8,128)(2,1)}) custom-call(s32[1]{0:T(128)} %bitcast.ctx_ref, bf16[1024,512]{1,0:T(8,128)(2,1)} %refs_3_.4, bf16[1024,512]{1,0:T(8,128)(2,1)} %refs_4_.4, bf16[1024,512]{1,0:T(8,128)(2,1)} %refs_5_.4, bf16[1024,512]{1,0:T(8,128)(2,1)} %refs_3_.4, ...), custom_call_target="tpu_custom_call" | custom-call | flops 1024 | bytes 1024 | tf_op jit(solution)/shard_map/pack/pallas_call | solution.py:201
  2.5 2.9 %collective-permute-start = (bf16[1552,128]{1,0:T(8,128)(2,1)}, bf16[1552,128]{1,0:T(8,128)(2,1)S(1)}, u32[]{:S(2)}, u32[]{:S(2)}) collective-permute-start(bf16[1552,128]{1,0:T(8,128)(2,1)} %get-tuple-element.75), channel_id=1, source_target_pairs={{0,8},{8,0},{16,24},{24,16},{1,9},{9,1},{17,25},{25,17},{2,10},{10... | collective-permute-start | bytes 1191944 | tf_op jit(solution)/shard_map/ppermute | solution.py:486
  5.4 1.5 %collective-permute-start.1 = (bf16[1552,128]{1,0:T(8,128)(2,1)}, bf16[1552,128]{1,0:T(8,128)(2,1)S(1)}, u32[]{:S(2)}, u32[]{:S(2)}) collective-permute-start(bf16[1552,128]{1,0:T(8,128)(2,1)} %get-tuple-element.76), channel_id=1, source_target_pairs={{0,16},{8,24},{16,0},{24,8},{1,17},{9,25},{17,1},{25,9},{2,18},{10... | collective-permute-start | bytes 1191944 | tf_op jit(solution)/shard_map/ppermute | solution.py:486
  7.0 0.0 collective-permute-start.2
  7.0 2.5 %pack.3 = (bf16[1536,128]{1,0:T(8,128)(2,1)}, bf16[1536,128]{1,0:T(8,128)(2,1)}, bf16[1536,128]{1,0:T(8,128)(2,1)}) custom-call(s32[1]{0:T(128)} %bitcast.ctx_ref, bf16[1024,512]{1,0:T(8,128)(2,1)} %refs_3_.4, bf16[1024,512]{1,0:T(8,128)(2,1)} %refs_4_.4, bf16[1024,512]{1,0:T(8,128)(2,1)} %refs_5_.4, bf16[1024,512]{1,0:T(8,128)(2,1)} %refs_3_.4, ...), custom_call_target="tpu_custom_call" | custom-call | flops 1024 | bytes 1024 | tf_op jit(solution)/shard_map/pack/pallas_call | solution.py:201
  9.5 0.6 pad_add_fusion.places_ref
  10.2 0.0 copy-start.3
  10.2 0.0 copy-start.4
  10.2 5.9 %pack_projection.1 = (bf16[512,2048]{1,0:T(8,128)(2,1)}, bf16[512,2048]{1,0:T(8,128)(2,1)}) custom-call(s32[5]{0:T(128)} %pad_add_fusion.places_ref, bf16[512,4096]{1,0:T(8,128)(2,1)} %give_in, bf16[512,4096]{1,0:T(8,128)(2,1)} %give_in), custom_call_target="tpu_custom_call" | custom-call | flops 1024 | bytes 1024 | tf_op jit(solution)/shard_map/pack_projection/pallas_call | solution.py:232
  16.1 0.0 collective-permute-done.refs_4_.refs_7_
  16.1 8.7 %collective-permute-done.1.refs_5_.refs_8_ = bf16[1552,128]{1,0:T(8,128)(2,1)S(1)} collective-permute-done((bf16[1552,128]{1,0:T(8,128)(2,1)}, bf16[1552,128]{1,0:T(8,128)(2,1)S(1)}, u32[]{:S(2)}, u32[]{:S(2)}) %collective-permute-start.1) | collective-permute-done | bytes 397344 | tf_op jit(solution)/shard_map/ppermute | solution.py:486
  24.8 0.0 collective-permute-done.2.refs_6_.refs_9_
  24.8 0.1 collective-permute-start.3
  24.9 1.2 collective-permute-start.7
  26.1 0.9 collective-permute-start.8
  27.1 7.3 %attend_low.1 = (bf16[512,128]{1,0:T(8,128)(2,1)S(1)}, bf16[512,128]{1,0:T(8,128)(2,1)S(1)}, bf16[512,128]{1,0:T(8,128)(2,1)S(1)}, bf16[512,128]{1,0:T(8,128)(2,1)S(1)}) custom-call(s32[1]{0:T(128)} %bitcast.ctx_ref, bf16[1024,512]{1,0:T(8,128)(2,1)S(1)} %copy-done.1, bf16[1024,512]{1,0:T(8,128)(2,1)S(1)} %copy-done.2, bf16[1024,512]{1,0:T(8,128)(2,1)S(1)} %copy-done.3, ...), custom_call_target="tpu_custom_call" | custom-call | flops 1024 | bytes 1024 | tf_op jit(solution)/shard_map/attend_low/pallas_call | solution.py:414
  34.4 0.0 collective-permute-done.3.w_sibling_ref
  34.4 1.6 %collective-permute-start.4 = (bf16[512,128]{1,0:T(8,128)(2,1)S(1)}, bf16[512,128]{1,0:T(8,128)(2,1)S(1)}, u32[]{:S(2)}, u32[]{:S(2)}) collective-permute-start(bf16[512,128]{1,0:T(8,128)(2,1)S(1)} %get-tuple-element.89), channel_id=1, source_target_pairs={{0,8},{8,0},{16,24},{24,16},{1,9},{9,1},{17,25},{25,17},{2,10},{10... | collective-permute-start | bytes 393224 | tf_op jit(solution)/shard_map/ppermute | solution.py:486
  35.9 0.5 collective-permute-start.5
  36.4 1.5 %collective-permute-start.6 = (bf16[512,128]{1,0:T(8,128)(2,1)S(1)}, bf16[512,128]{1,0:T(8,128)(2,1)S(1)}, u32[]{:S(2)}, u32[]{:S(2)}) collective-permute-start(bf16[512,128]{1,0:T(8,128)(2,1)S(1)} %get-tuple-element.91), channel_id=1, source_target_pairs={{0,24},{8,16},{16,8},{24,0},{1,25},{9,17},{17,9},{25,1},{2,26},{10... | collective-permute-start | bytes 393224 | tf_op jit(solution)/shard_map/ppermute | solution.py:486
  37.9 0.0 collective-permute-done.7.refs_10_
  37.9 0.0 collective-permute-done.8.refs_11_
  37.9 2.1 %collective-permute-done.4.refs_1_ = bf16[512,128]{1,0:T(8,128)(2,1)S(1)} collective-permute-done((bf16[512,128]{1,0:T(8,128)(2,1)S(1)}, bf16[512,128]{1,0:T(8,128)(2,1)S(1)}, u32[]{:S(2)}, u32[]{:S(2)}) %collective-permute-start.4) | collective-permute-done | bytes 131104 | tf_op jit(solution)/shard_map/ppermute | solution.py:486
  40.1 3.7 %collective-permute-done.5.refs_2_ = bf16[512,128]{1,0:T(8,128)(2,1)S(1)} collective-permute-done((bf16[512,128]{1,0:T(8,128)(2,1)S(1)}, bf16[512,128]{1,0:T(8,128)(2,1)S(1)}, u32[]{:S(2)}, u32[]{:S(2)}) %collective-permute-start.5) | collective-permute-done | bytes 131104 | tf_op jit(solution)/shard_map/ppermute | solution.py:486
  43.7 0.0 collective-permute-done.6.refs_3_
  43.7 0.1 assemble.2.mine_ref
  43.8 0.1 collective-permute-start.9
  43.9 1.2 collective-permute-start.10
  45.2 0.6 collective-permute-done.9.sibling_ref
  45.8 0.7 project.9
  46.5 1.6 %collective-permute-start.14 = (bf16[512,512]{1,0:T(8,128)(2,1)S(1)}, bf16[512,512]{1,0:T(8,128)(2,1)S(1)}, u32[]{:S(2)}, u32[]{:S(2)}) collective-permute-start(bf16[512,512]{1,0:T(8,128)(2,1)S(1)} %project.9), channel_id=1, source_target_pairs={{0,2},{1,3},{2,0},{3,1},{4,6},{5,7},{6,4},{7,5},{8,10},{9,11},{10,... | collective-permute-start | bytes 1572872 | tf_op jit(solution)/shard_map/ppermute | solution.py:486
  48.2 0.7 project.8
  48.9 7.5 %collective-permute-done.10.refs_12_ = bf16[1536,128]{1,0:T(8,128)(2,1)S(1)} collective-permute-done((bf16[1536,128]{1,0:T(8,128)(2,1)S(1)}, bf16[1536,128]{1,0:T(8,128)(2,1)S(1)}, u32[]{:S(2)}, u32[]{:S(2)}) %collective-permute-start.10) | collective-permute-done | bytes 393248 | tf_op jit(solution)/shard_map/ppermute | solution.py:486
  56.4 1.6 %collective-permute-start.15 = (bf16[512,512]{1,0:T(8,128)(2,1)S(1)}, bf16[512,512]{1,0:T(8,128)(2,1)S(1)}, u32[]{:S(2)}, u32[]{:S(2)}) collective-permute-start(bf16[512,512]{1,0:T(8,128)(2,1)S(1)} %project.8), channel_id=1, source_target_pairs={{0,2},{1,3},{2,0},{3,1},{4,6},{5,7},{6,4},{7,5},{8,10},{9,11},{10,... | collective-permute-start | bytes 1572872 | tf_op jit(solution)/shard_map/ppermute | solution.py:486
  57.9 0.7 project.11
  58.7 0.7 project.10
  59.4 6.2 %attend_high.1 = (bf16[512,128]{1,0:T(8,128)(2,1)S(1)}, bf16[512,128]{1,0:T(8,128)(2,1)S(1)}, bf16[512,128]{1,0:T(8,128)(2,1)S(1)}, bf16[512,128]{1,0:T(8,128)(2,1)S(1)}) custom-call(s32[1]{0:T(128)} %bitcast.ctx_ref, bf16[1024,512]{1,0:T(8,128)(2,1)S(1)} %copy-done.1, bf16[1024,512]{1,0:T(8,128)(2,1)S(1)} %copy-done.2, bf16[1024,512]{1,0:T(8,128)(2,1)S(1)} %copy-done.3, ...), custom_call_target="tpu_custom_call" | custom-call | flops 1024 | bytes 1024 | tf_op jit(solution)/shard_map/attend_high/pallas_call | solution.py:414
  65.6 0.6 collective-permute-start.11
  66.1 1.2 collective-permute-start.12
  67.4 1.8 %collective-permute-start.13 = (bf16[512,128]{1,0:T(8,128)(2,1)S(1)}, bf16[512,128]{1,0:T(8,128)(2,1)S(1)}, u32[]{:S(2)}, u32[]{:S(2)}) collective-permute-start(bf16[512,128]{1,0:T(8,128)(2,1)S(1)} %get-tuple-element.111), channel_id=1, source_target_pairs={{0,24},{8,16},{16,8},{24,0},{1,25},{9,17},{17,9},{25,1},{2,26},{10... | collective-permute-start | bytes 393224 | tf_op jit(solution)/shard_map/ppermute | solution.py:486
  69.1 0.0 collective-permute-done.14
  69.1 0.1 add_convert_fusion.3
  69.3 2.6 %collective-permute-done.11.refs_1_ = bf16[512,128]{1,0:T(8,128)(2,1)S(1)} collective-permute-done((bf16[512,128]{1,0:T(8,128)(2,1)S(1)}, bf16[512,128]{1,0:T(8,128)(2,1)S(1)}, u32[]{:S(2)}, u32[]{:S(2)}) %collective-permute-start.11) | collective-permute-done | bytes 131104 | tf_op jit(solution)/shard_map/ppermute | solution.py:486
  71.8 2.1 %collective-permute-done.12.refs_2_ = bf16[512,128]{1,0:T(8,128)(2,1)S(1)} collective-permute-done((bf16[512,128]{1,0:T(8,128)(2,1)S(1)}, bf16[512,128]{1,0:T(8,128)(2,1)S(1)}, u32[]{:S(2)}, u32[]{:S(2)}) %collective-permute-start.12) | collective-permute-done | bytes 131104 | tf_op jit(solution)/shard_map/ppermute | solution.py:486
  73.9 0.0 collective-permute-done.13.refs_3_
  73.9 0.0 collective-permute-done.15
  73.9 0.1 assemble.3.mine_ref
  74.0 0.1 collective-permute-start.16
  74.1 2.7 %collective-permute-start.17 = (bf16[512,512]{1,0:T(8,128)(2,1)S(1)}, bf16[512,512]{1,0:T(8,128)(2,1)S(1)}, u32[]{:S(2)}, u32[]{:S(2)}) collective-permute-start(bf16[512,512]{1,0:T(8,128)(2,1)S(1)} %add_convert_fusion.3), channel_id=1, source_target_pairs={{0,4},{1,5},{2,6},{3,7},{4,0},{5,1},{6,2},{7,3},{8,12},{9,13},{10,... | collective-permute-start | bytes 1572872 | tf_op jit(solution)/shard_map/ppermute | solution.py:486
  76.7 0.0 collective-permute-done.16.sibling_ref
  76.7 0.7 project.15
  77.4 0.5 collective-permute-start.19
  78.0 0.7 project.12
  78.7 21.9 %collective-permute-done.17 = bf16[512,512]{1,0:T(8,128)(2,1)S(1)} collective-permute-done((bf16[512,512]{1,0:T(8,128)(2,1)S(1)}, bf16[512,512]{1,0:T(8,128)(2,1)S(1)}, u32[]{:S(2)}, u32[]{:S(2)}) %collective-permute-start.17) | collective-permute-done | bytes 524320 | tf_op jit(solution)/shard_map/ppermute | solution.py:486
  100.5 0.7 project.14
  101.3 1.4 %collective-permute-done.19 = bf16[512,512]{1,0:T(8,128)(2,1)S(1)} collective-permute-done((bf16[512,512]{1,0:T(8,128)(2,1)S(1)}, bf16[512,512]{1,0:T(8,128)(2,1)S(1)}, u32[]{:S(2)}, u32[]{:S(2)}) %collective-permute-start.19) | collective-permute-done | bytes 524320 | tf_op jit(solution)/shard_map/ppermute | solution.py:486
  102.6 0.1 add_convert_fusion.1
  102.8 1.8 %collective-permute-start.20 = (bf16[512,512]{1,0:T(8,128)(2,1)S(1)}, bf16[512,512]{1,0:T(8,128)(2,1)S(1)}, u32[]{:S(2)}, u32[]{:S(2)}) collective-permute-start(bf16[512,512]{1,0:T(8,128)(2,1)S(1)} %add_convert_fusion.1), channel_id=1, source_target_pairs={{0,4},{1,5},{2,6},{3,7},{4,0},{5,1},{6,2},{7,3},{8,12},{9,13},{10,... | collective-permute-start | bytes 1572872 | tf_op jit(solution)/shard_map/ppermute | solution.py:486
  104.6 0.7 project.13
  105.3 0.2 add_convert_fusion.2
  105.6 18.0 %collective-permute-done.18 = bf16[512,512]{1,0:T(8,128)(2,1)S(1)} collective-permute-done((bf16[512,512]{1,0:T(8,128)(2,1)S(1)}, bf16[512,512]{1,0:T(8,128)(2,1)S(1)}, u32[]{:S(2)}, u32[]{:S(2)}) %collective-permute-start.18) | collective-permute-done | bytes 524320 | tf_op jit(solution)/shard_map/ppermute | solution.py:486
  123.6 4.6 %collective-permute-done.20 = bf16[512,512]{1,0:T(8,128)(2,1)S(1)} collective-permute-done((bf16[512,512]{1,0:T(8,128)(2,1)S(1)}, bf16[512,512]{1,0:T(8,128)(2,1)S(1)}, u32[]{:S(2)}, u32[]{:S(2)}) %collective-permute-start.20) | collective-permute-done | bytes 524320 | tf_op jit(solution)/shard_map/ppermute | solution.py:486
  128.2 0.2 add_convert_fusion
  128.4 1.0 pad_maximum_fusion
  (18 shorter events, 0.0 us)
Async XLA Ops:
  2.5 7.0 %copy-start.8 = (s32[4]{0:T(128)S(1)}, s32[4]{0:T(128)}, u32[]{:S(2)}) copy-start(s32[4]{0:T(128)} %constant.34.clone) | copy-start | bytes 52
  2.5 13.6 %collective-permute-start = (bf16[1552,128]{1,0:T(8,128)(2,1)}, bf16[1552,128]{1,0:T(8,128)(2,1)S(1)}, u32[]{:S(2)}, u32[]{:S(2)}) collective-permute-start(bf16[1552,128]{1,0:T(8,128)(2,1)} %get-tuple-element.75), channel_id=1, source_target_pairs={{0,8},{8,0},{16,24},{24,16},{1,9},{9,1},{17,25},{25,17},{2,10},{10... | collective-permute-start | bytes 1191944 | tf_op jit(solution)/shard_map/ppermute | solution.py:486
  5.4 19.4 %collective-permute-start.1 = (bf16[1552,128]{1,0:T(8,128)(2,1)}, bf16[1552,128]{1,0:T(8,128)(2,1)S(1)}, u32[]{:S(2)}, u32[]{:S(2)}) collective-permute-start(bf16[1552,128]{1,0:T(8,128)(2,1)} %get-tuple-element.76), channel_id=1, source_target_pairs={{0,16},{8,24},{16,0},{24,8},{1,17},{9,25},{17,1},{25,9},{2,18},{10... | collective-permute-start | bytes 1191944 | tf_op jit(solution)/shard_map/ppermute | solution.py:486
  7.0 17.9 %collective-permute-start.2 = (bf16[1552,128]{1,0:T(8,128)(2,1)}, bf16[1552,128]{1,0:T(8,128)(2,1)S(1)}, u32[]{:S(2)}, u32[]{:S(2)}) collective-permute-start(bf16[1552,128]{1,0:T(8,128)(2,1)} %get-tuple-element.77), channel_id=1, source_target_pairs={{0,24},{8,16},{16,8},{24,0},{1,25},{9,17},{17,9},{25,1},{2,26},{10... | collective-permute-start | bytes 1191944 | tf_op jit(solution)/shard_map/ppermute | solution.py:486
  10.2 14.8 %copy-start.7 = (bf16[1536,128]{1,0:T(8,128)(2,1)S(1)}, bf16[1536,128]{1,0:T(8,128)(2,1)}, u32[]{:S(2)}) copy-start(bf16[1536,128]{1,0:T(8,128)(2,1)} %get-tuple-element.92) | copy-start | bytes 1179652
  10.2 16.0 %copy-start.6 = (bf16[1536,128]{1,0:T(8,128)(2,1)S(1)}, bf16[1536,128]{1,0:T(8,128)(2,1)}, u32[]{:S(2)}) copy-start(bf16[1536,128]{1,0:T(8,128)(2,1)} %get-tuple-element.93) | copy-start | bytes 1179652
  10.2 16.9 %copy-start.1 = (bf16[1024,512]{1,0:T(8,128)(2,1)S(1)}, bf16[1024,512]{1,0:T(8,128)(2,1)}, u32[]{:S(2)}) copy-start(bf16[1024,512]{1,0:T(8,128)(2,1)} %refs_3_.4) | copy-start | bytes 3145732
  10.2 16.9 %copy-start.2 = (bf16[1024,512]{1,0:T(8,128)(2,1)S(1)}, bf16[1024,512]{1,0:T(8,128)(2,1)}, u32[]{:S(2)}) copy-start(bf16[1024,512]{1,0:T(8,128)(2,1)} %refs_4_.4) | copy-start | bytes 3145732
  10.2 16.9 %copy-start.3 = (bf16[1024,512]{1,0:T(8,128)(2,1)S(1)}, bf16[1024,512]{1,0:T(8,128)(2,1)}, u32[]{:S(2)}) copy-start(bf16[1024,512]{1,0:T(8,128)(2,1)} %refs_5_.4) | copy-start | bytes 3145732
  10.2 16.9 %copy-start.4 = (s32[1024]{0:T(1024)S(1)}, s32[1024]{0:T(1024)}, u32[]{:S(2)}) copy-start(s32[1024]{0:T(1024)} %param.9) | copy-start | bytes 12292
  24.8 19.1 %copy-start.5 = (bf16[1536,128]{1,0:T(8,128)(2,1)S(1)}, bf16[1536,128]{1,0:T(8,128)(2,1)}, u32[]{:S(2)}) copy-start(bf16[1536,128]{1,0:T(8,128)(2,1)} %get-tuple-element.102) | copy-start | bytes 1179652
  24.8 21.0 %copy-start = (bf16[512,2048]{1,0:T(8,128)(2,1)S(1)}, bf16[512,2048]{1,0:T(8,128)(2,1)}, u32[]{:S(2)}) copy-start(bf16[512,2048]{1,0:T(8,128)(2,1)} %get-tuple-element.100.w_mine_ref) | copy-start | bytes 6291460
  24.8 9.5 %collective-permute-start.3 = (bf16[512,2048]{1,0:T(8,128)(2,1)}, bf16[512,2048]{1,0:T(8,128)(2,1)S(1)}, u32[]{:S(2)}, u32[]{:S(2)}) collective-permute-start(bf16[512,2048]{1,0:T(8,128)(2,1)} %get-tuple-element.88), channel_id=1, source_target_pairs={{0,1},{1,0},{2,3},{3,2},{4,5},{5,4},{6,7},{7,6},{8,9},{9,8},{10,11... | collective-permute-start | bytes 6291464 | tf_op jit(solution)/shard_map/ppermute | solution.py:486
  24.9 13.0 %collective-permute-start.7 = (bf16[1536,128]{1,0:T(8,128)(2,1)S(1)}, bf16[1536,128]{1,0:T(8,128)(2,1)S(1)}, u32[]{:S(2)}, u32[]{:S(2)}) collective-permute-start(bf16[1536,128]{1,0:T(8,128)(2,1)S(1)} %copy-done.7), channel_id=1, source_target_pairs={{0,8},{8,0},{16,24},{24,16},{1,9},{9,1},{17,25},{25,17},{2,10},{10... | collective-permute-start | bytes 1179656 | tf_op jit(solution)/shard_map/ppermute | solution.py:486
  26.1 11.8 %collective-permute-start.8 = (bf16[1536,128]{1,0:T(8,128)(2,1)S(1)}, bf16[1536,128]{1,0:T(8,128)(2,1)S(1)}, u32[]{:S(2)}, u32[]{:S(2)}) collective-permute-start(bf16[1536,128]{1,0:T(8,128)(2,1)S(1)} %copy-done.6), channel_id=1, source_target_pairs={{0,16},{8,24},{16,0},{24,8},{1,17},{9,25},{17,1},{25,9},{2,18},{10... | collective-permute-start | bytes 1179656 | tf_op jit(solution)/shard_map/ppermute | solution.py:486
  34.4 5.7 %collective-permute-start.4 = (bf16[512,128]{1,0:T(8,128)(2,1)S(1)}, bf16[512,128]{1,0:T(8,128)(2,1)S(1)}, u32[]{:S(2)}, u32[]{:S(2)}) collective-permute-start(bf16[512,128]{1,0:T(8,128)(2,1)S(1)} %get-tuple-element.89), channel_id=1, source_target_pairs={{0,8},{8,0},{16,24},{24,16},{1,9},{9,1},{17,25},{25,17},{2,10},{10... | collective-permute-start | bytes 393224 | tf_op jit(solution)/shard_map/ppermute | solution.py:486
  35.9 7.8 %collective-permute-start.5 = (bf16[512,128]{1,0:T(8,128)(2,1)S(1)}, bf16[512,128]{1,0:T(8,128)(2,1)S(1)}, u32[]{:S(2)}, u32[]{:S(2)}) collective-permute-start(bf16[512,128]{1,0:T(8,128)(2,1)S(1)} %get-tuple-element.90), channel_id=1, source_target_pairs={{0,16},{8,24},{16,0},{24,8},{1,17},{9,25},{17,1},{25,9},{2,18},{10... | collective-permute-start | bytes 393224 | tf_op jit(solution)/shard_map/ppermute | solution.py:486
  36.4 7.3 %collective-permute-start.6 = (bf16[512,128]{1,0:T(8,128)(2,1)S(1)}, bf16[512,128]{1,0:T(8,128)(2,1)S(1)}, u32[]{:S(2)}, u32[]{:S(2)}) collective-permute-start(bf16[512,128]{1,0:T(8,128)(2,1)S(1)} %get-tuple-element.91), channel_id=1, source_target_pairs={{0,24},{8,16},{16,8},{24,0},{1,25},{9,17},{17,9},{25,1},{2,26},{10... | collective-permute-start | bytes 393224 | tf_op jit(solution)/shard_map/ppermute | solution.py:486
  43.8 2.0 %collective-permute-start.9 = (bf16[512,512]{1,0:T(8,128)(2,1)S(1)}, bf16[512,512]{1,0:T(8,128)(2,1)S(1)}, u32[]{:S(2)}, u32[]{:S(2)}) collective-permute-start(bf16[512,512]{1,0:T(8,128)(2,1)S(1)} %assemble.2.mine_ref), channel_id=1, source_target_pairs={{0,1},{1,0},{2,3},{3,2},{4,5},{5,4},{6,7},{7,6},{8,9},{9,8},{10,11... | collective-permute-start | bytes 1572872 | tf_op jit(solution)/shard_map/ppermute | solution.py:486
  43.9 12.4 %collective-permute-start.10 = (bf16[1536,128]{1,0:T(8,128)(2,1)S(1)}, bf16[1536,128]{1,0:T(8,128)(2,1)S(1)}, u32[]{:S(2)}, u32[]{:S(2)}) collective-permute-start(bf16[1536,128]{1,0:T(8,128)(2,1)S(1)} %copy-done.5), channel_id=1, source_target_pairs={{0,24},{8,16},{16,8},{24,0},{1,25},{9,17},{17,9},{25,1},{2,26},{10... | collective-permute-start | bytes 1179656 | tf_op jit(solution)/shard_map/ppermute | solution.py:486
  46.5 22.6 %collective-permute-start.14 = (bf16[512,512]{1,0:T(8,128)(2,1)S(1)}, bf16[512,512]{1,0:T(8,128)(2,1)S(1)}, u32[]{:S(2)}, u32[]{:S(2)}) collective-permute-start(bf16[512,512]{1,0:T(8,128)(2,1)S(1)} %project.9), channel_id=1, source_target_pairs={{0,2},{1,3},{2,0},{3,1},{4,6},{5,7},{6,4},{7,5},{8,10},{9,11},{10,... | collective-permute-start | bytes 1572872 | tf_op jit(solution)/shard_map/ppermute | solution.py:486
  56.4 17.5 %collective-permute-start.15 = (bf16[512,512]{1,0:T(8,128)(2,1)S(1)}, bf16[512,512]{1,0:T(8,128)(2,1)S(1)}, u32[]{:S(2)}, u32[]{:S(2)}) collective-permute-start(bf16[512,512]{1,0:T(8,128)(2,1)S(1)} %project.8), channel_id=1, source_target_pairs={{0,2},{1,3},{2,0},{3,1},{4,6},{5,7},{6,4},{7,5},{8,10},{9,11},{10,... | collective-permute-start | bytes 1572872 | tf_op jit(solution)/shard_map/ppermute | solution.py:486
  65.6 6.3 %collective-permute-start.11 = (bf16[512,128]{1,0:T(8,128)(2,1)S(1)}, bf16[512,128]{1,0:T(8,128)(2,1)S(1)}, u32[]{:S(2)}, u32[]{:S(2)}) collective-permute-start(bf16[512,128]{1,0:T(8,128)(2,1)S(1)} %get-tuple-element.109), channel_id=1, source_target_pairs={{0,8},{8,0},{16,24},{24,16},{1,9},{9,1},{17,25},{25,17},{2,10},{10... | collective-permute-start | bytes 393224 | tf_op jit(solution)/shard_map/ppermute | solution.py:486
  66.1 7.7 %collective-permute-start.12 = (bf16[512,128]{1,0:T(8,128)(2,1)S(1)}, bf16[512,128]{1,0:T(8,128)(2,1)S(1)}, u32[]{:S(2)}, u32[]{:S(2)}) collective-permute-start(bf16[512,128]{1,0:T(8,128)(2,1)S(1)} %get-tuple-element.110), channel_id=1, source_target_pairs={{0,16},{8,24},{16,0},{24,8},{1,17},{9,25},{17,1},{25,9},{2,18},{10... | collective-permute-start | bytes 393224 | tf_op jit(solution)/shard_map/ppermute | solution.py:486
  67.4 6.5 %collective-permute-start.13 = (bf16[512,128]{1,0:T(8,128)(2,1)S(1)}, bf16[512,128]{1,0:T(8,128)(2,1)S(1)}, u32[]{:S(2)}, u32[]{:S(2)}) collective-permute-start(bf16[512,128]{1,0:T(8,128)(2,1)S(1)} %get-tuple-element.111), channel_id=1, source_target_pairs={{0,24},{8,16},{16,8},{24,0},{1,25},{9,17},{17,9},{25,1},{2,26},{10... | collective-permute-start | bytes 393224 | tf_op jit(solution)/shard_map/ppermute | solution.py:486
  74.0 2.7 %collective-permute-start.16 = (bf16[512,512]{1,0:T(8,128)(2,1)S(1)}, bf16[512,512]{1,0:T(8,128)(2,1)S(1)}, u32[]{:S(2)}, u32[]{:S(2)}) collective-permute-start(bf16[512,512]{1,0:T(8,128)(2,1)S(1)} %assemble.3.mine_ref), channel_id=1, source_target_pairs={{0,1},{1,0},{2,3},{3,2},{4,5},{5,4},{6,7},{7,6},{8,9},{9,8},{10,11... | collective-permute-start | bytes 1572872 | tf_op jit(solution)/shard_map/ppermute | solution.py:486
  74.1 26.5 %collective-permute-start.17 = (bf16[512,512]{1,0:T(8,128)(2,1)S(1)}, bf16[512,512]{1,0:T(8,128)(2,1)S(1)}, u32[]{:S(2)}, u32[]{:S(2)}) collective-permute-start(bf16[512,512]{1,0:T(8,128)(2,1)S(1)} %add_convert_fusion.3), channel_id=1, source_target_pairs={{0,4},{1,5},{2,6},{3,7},{4,0},{5,1},{6,2},{7,3},{8,12},{9,13},{10,... | collective-permute-start | bytes 1572872 | tf_op jit(solution)/shard_map/ppermute | solution.py:486
  77.4 25.2 %collective-permute-start.19 = (bf16[512,512]{1,0:T(8,128)(2,1)S(1)}, bf16[512,512]{1,0:T(8,128)(2,1)S(1)}, u32[]{:S(2)}, u32[]{:S(2)}) collective-permute-start(bf16[512,512]{1,0:T(8,128)(2,1)S(1)} %project.15), channel_id=1, source_target_pairs={{0,2},{1,3},{2,0},{3,1},{4,6},{5,7},{6,4},{7,5},{8,10},{9,11},{10,... | collective-permute-start | bytes 1572872 | tf_op jit(solution)/shard_map/ppermute | solution.py:486
  100.5 23.0 %collective-permute-start.18 = (bf16[512,512]{1,0:T(8,128)(2,1)S(1)}, bf16[512,512]{1,0:T(8,128)(2,1)S(1)}, u32[]{:S(2)}, u32[]{:S(2)}) collective-permute-start(bf16[512,512]{1,0:T(8,128)(2,1)S(1)} %project.12), channel_id=1, source_target_pairs={{0,2},{1,3},{2,0},{3,1},{4,6},{5,7},{6,4},{7,5},{8,10},{9,11},{10,... | collective-permute-start | bytes 1572872 | tf_op jit(solution)/shard_map/ppermute | solution.py:486
  102.8 25.4 %collective-permute-start.20 = (bf16[512,512]{1,0:T(8,128)(2,1)S(1)}, bf16[512,512]{1,0:T(8,128)(2,1)S(1)}, u32[]{:S(2)}, u32[]{:S(2)}) collective-permute-start(bf16[512,512]{1,0:T(8,128)(2,1)S(1)} %add_convert_fusion.1), channel_id=1, source_target_pairs={{0,4},{1,5},{2,6},{3,7},{4,0},{5,1},{6,2},{7,3},{8,12},{9,13},{10,... | collective-permute-start | bytes 1572872 | tf_op jit(solution)/shard_map/ppermute | solution.py:486

commit v10 on v9

--- a/solution.py
+++ b/solution.py
@@ -213,37 +213,6 @@
     )(ctx_index, *operands)
 
 
-def pack_projection(places, w_out, chips):
-    depth, width = w_out.shape
-    columns = width // (2 * chips)
-
-    def kernel(places_ref, keep_in, give_in, keep_out, give_out):
-        keep_out[...] = keep_in[...]
-        give_out[...] = give_in[...]
-
-    def block(other):
-        def index_map(turn, at):
-            parity = 1 - at[chips] if other else at[chips]
-            return (0, 2 * at[turn] + parity)
-
-        return pl.BlockSpec((depth, columns), index_map)
-
-    out_spec = pl.BlockSpec((depth, columns), lambda turn, at: (0, turn))
-    return pl.pallas_call(
-        kernel,
-        grid_spec=pltpu.PrefetchScalarGridSpec(
-            num_scalar_prefetch=1,
-            grid=(chips,),
-            in_specs=[block(False), block(True)],
-            out_specs=[out_spec] * 2,
-        ),
-        out_shape=[jax.ShapeDtypeStruct((depth, chips * columns), w_out.dtype)] * 2,
-        compiler_params=params(56),
-        cost_estimate=SMALL,
-        name="pack_projection",
-    )(places, w_out, w_out)
-
-
 def attend(ctx_index, queries, keys, values, docs, low, high):
     rows = queries.shape[0] // 2
     group = queries.shape[1] // HD
@@ -458,27 +427,29 @@
     )(ctx_index, *pieces)
 
 
-def project(mine, sibling, w_mine, w_sibling, first, count, chips):
+def project(places, turn, mine, sibling, w_mine, w_sibling):
     rows, depth = mine.shape
-    columns = w_mine.shape[1] // chips
-
-    def kernel(mine_ref, sibling_ref, w_mine_ref, w_sibling_ref, out_ref):
+    columns = w_mine.shape[1] // (2 * len(TURNS))
+
+    def kernel(places_ref, mine_ref, sibling_ref, w_mine_ref, w_sibling_ref, out_ref):
         total = jnp.dot(mine_ref[...], w_mine_ref[...], preferred_element_type=jnp.float32)
         total += jnp.dot(sibling_ref[...], w_sibling_ref[...], preferred_element_type=jnp.float32)
         out_ref[...] = total.astype(jnp.bfloat16)
 
-    weights = pl.BlockSpec((depth, columns), lambda turn: (0, first + turn))
-    attended = pl.BlockSpec((rows, depth), lambda turn: (0, 0))
+    weights = pl.BlockSpec((depth, columns), lambda step, at: (0, at[turn]))
     return pl.pallas_call(
         kernel,
-        grid=(count,),
-        in_specs=[attended, attended, weights, weights],
-        out_specs=pl.BlockSpec((rows, columns), lambda turn: (0, turn)),
-        out_shape=jax.ShapeDtypeStruct((rows, count * columns), jnp.bfloat16),
+        grid_spec=pltpu.PrefetchScalarGridSpec(
+            num_scalar_prefetch=1,
+            grid=(1,),
+            in_specs=[whole((rows, depth)), whole((rows, depth)), weights, weights],
+            out_specs=whole((rows, columns)),
+        ),
+        out_shape=jax.ShapeDtypeStruct((rows, columns), jnp.bfloat16),
         compiler_params=params(16),
         cost_estimate=SMALL,
         name="project",
-    )(mine, sibling, w_mine, w_sibling)
+    )(places, mine, sibling, w_mine, w_sibling)
 
 
 def swap(value, axis, distance):
@@ -503,31 +474,25 @@
 def exchange_local(queries, keys, values, doc_ids, w_out):
     shard_rows = queries.shape[0]
     group = queries.shape[1] // HD
-    chips = lax.axis_size("head") // 2
-    columns = w_out.shape[1] // (2 * chips)
     ctx_index = lax.axis_index("ctx").astype(jnp.int32).reshape(1)
     head_index = lax.axis_index("head").astype(jnp.int32)
-    chip = head_index // 2
-    core = (head_index % 2).reshape(1)
-    places = jnp.concatenate([chip ^ jnp.array(TURNS, jnp.int32), core])
+    places = head_index ^ (2 * jnp.array(TURNS, jnp.int32))
     docs = doc_ids.reshape(shard_rows // HD, HD)
     near = range(1, group)
 
+    w_sibling = swap(w_out, "head", 1)
     low_out = pack(ctx_index, 0, queries, keys, values, docs)
     low_out, later = tie(low_out, (queries, keys, values))
     low = [swap(low_out[distance - 1], "ctx", distance) for distance in near]
     high_out = pack(ctx_index, 1, *later, None)
-    high_out, w_out = tie(high_out, w_out)
-    w_mine, w_give = pack_projection(places, w_out, chips)
-    high_out, low, w_give = tie(high_out, low, w_give)
-    w_sibling = swap(w_give, "head", 1)
+    high_out, low = tie(high_out, low)
     high = [swap(high_out[0], "ctx", 1), swap(high_out[1], "ctx", 2)]
 
     def send_back(pieces):
         return [swap(pieces[distance], "ctx", distance) for distance in near]
 
-    def share_of(mine, sibling, turn, count=1):
-        return project(mine, sibling, w_mine, w_sibling, turn, count, chips)
+    def share_of(mine, sibling, turn):
+        return project(places, turn, mine, sibling, w_out, w_sibling)
 
     pieces = attend(ctx_index, queries, keys, values, docs, low, None)
     pieces, diagonal_out, w_sibling = tie(pieces, high_out[2], w_sibling)
@@ -536,23 +501,22 @@
     high.append(swap(diagonal_out, "ctx", 3))
     mine = assemble(ctx_index, [pieces[0], *back])
     sibling = swap(mine, "head", 1)
-    shares = [share_of(mine, sibling, turn) for turn in range(chips)]
+    shares = [share_of(mine, sibling, turn) for turn in range(len(TURNS))]
     far = swap(shares[0], "head", 2)
     shares[1], high[2] = tie(shares[1], high[2])
     near_sum = swap(shares[1], "head", 2)
 
-    high, shares = tie(high, shares)
+    passed = add(shares[2], far)
+    high, shares, passed = tie(high, shares, passed)
+    across = swap(passed, "head", 4)
     pieces = attend(ctx_index, queries, keys, values, docs, low, high)
     back = send_back(pieces)
-    passed = add(shares[2], far)
-    back, passed, near_sum = tie(back, passed, near_sum)
-    across = swap(passed, "head", 4)
     mine = assemble(ctx_index, [pieces[0], *back])
+    mine, across, near_sum = tie(mine, across, near_sum)
+    first = add(shares[3], near_sum, across)
     sibling = swap(mine, "head", 1)
-    late = [share_of(mine, sibling, turn) for turn in range(chips)]
+    late = [share_of(mine, sibling, turn) for turn in range(len(TURNS))]
     far = swap(late[0], "head", 2)
-    late[1], across = tie(late[1], across)
-    first = add(shares[3], near_sum, across)
     near_sum = swap(late[1], "head", 2)
     across = swap(add(late[2], far), "head", 4)
     second = add(late[3], near_sum, across)

time: 129 us -> 141 us (1.093)
  Pallas kernels: 30.3 us -> 39.9 us
  local copies, waits for them, and re-layouts: 0.04 us -> 3.76 us
  waiting for transfers between devices: 73.2 us -> 70.4 us
    pallas_call x9 -> x8, Pallas kernels: 11.6 us -> 19.7 us  [project(): pl.pallas_call(kernel, grid_spec=pltpu.PrefetchScalarGridSpec(num_scalar_...]
    unnamed x18 -> x32, local copies, waits for them, and re-layouts: 0.04 us -> 3.76 us
    ppermute x21, waiting for transfers between devices: 73.2 us -> 70.4 us  [swap(): lax.ppermute(value, axis, [(source, source ^ distance) for source in rang...]
  transfers between devices with their start and end apart: 21 -> 21, of which waited for: 11 -> 16; matrix products, arithmetic and copies ran while one was open for 1% -> 0% of each run, Pallas kernels for 21% -> 24%
where the time goes in v10:
time: 141 us; the launch traced here: 140 us
  waiting for transfers between devices  70.4 us (50%)
  Pallas kernels  39.9 us (28%)
  starting transfers between devices  24.4 us (17%)
  local copies, waits for them, and re-layouts  3.76 us (3%)
  other arithmetic  1.74 us (1%)
    ppermute x21, waiting for transfers between devices, swap(): lax.ppermute(value, axis, [(source, source ^ distance) for source in rang...  70.4 us
    ppermute x21, starting transfers between devices, swap(): lax.ppermute(value, axis, [(source, source ^ distance) for source in rang...  24.4 us
    pallas_call x8, Pallas kernels, project(): pl.pallas_call(kernel, grid_spec=pltpu.PrefetchScalarGridSpec(num_scalar_...  19.7 us
    pallas_call x2, Pallas kernels, attend(): pl.pallas_call(kernel, grid_spec=pltpu.PrefetchScalarGridSpec(num_scalar_...  14.1 us
    pallas_call x2, Pallas kernels, pack(): pl.pallas_call(kernel, grid_spec=pltpu.PrefetchScalarGridSpec(num_scalar_...  5.06 us
    unnamed x32, local copies, waits for them, and re-layouts  3.76 us
  transfers between devices with their start and end apart: 21, of which 16 were waited for; matrix products, arithmetic and copies ran while one was open for 0% of the time, Pallas kernels for 24%

profile of v10, /device:TPU:0, one launch (start us, length us, event | category | flops | bytes accessed | tf_op | source)
XLA Modules:
  0.0 140.3 jit_solution(17512459974383479640)
XLA Ops:
  0.0 0.5 collective-permute-start.3
  0.5 2.5 %pack.2 = (bf16[1552,128]{1,0:T(8,128)(2,1)}, bf16[1552,128]{1,0:T(8,128)(2,1)}, bf16[1552,128]{1,0:T(8,128)(2,1)}) custom-call(s32[1]{0:T(128)} %bitcast.ctx_ref, bf16[1024,512]{1,0:T(8,128)(2,1)} %refs_3_.4, bf16[1024,512]{1,0:T(8,128)(2,1)} %refs_4_.4, bf16[1024,512]{1,0:T(8,128)(2,1)} %refs_5_.4, bf16[1024,512]{1,0:T(8,128)(2,1)} %refs_3_.4, ...), custom_call_target="tpu_custom_call" | custom-call | flops 1024 | bytes 1024 | tf_op jit(solution)/shard_map/pack/pallas_call | solution.py:201
  3.0 0.0 copy-start.13
  3.0 2.6 %collective-permute-start = (bf16[1552,128]{1,0:T(8,128)(2,1)}, bf16[1552,128]{1,0:T(8,128)(2,1)S(1)}, u32[]{:S(2)}, u32[]{:S(2)}) collective-permute-start(bf16[1552,128]{1,0:T(8,128)(2,1)} %get-tuple-element.61), channel_id=1, source_target_pairs={{0,8},{8,0},{16,24},{24,16},{1,9},{9,1},{17,25},{25,17},{2,10},{10... | collective-permute-start | bytes 1191944 | tf_op jit(solution)/shard_map/ppermute | solution.py:457
  5.6 1.5 %collective-permute-start.1 = (bf16[1552,128]{1,0:T(8,128)(2,1)}, bf16[1552,128]{1,0:T(8,128)(2,1)S(1)}, u32[]{:S(2)}, u32[]{:S(2)}) collective-permute-start(bf16[1552,128]{1,0:T(8,128)(2,1)} %get-tuple-element.62), channel_id=1, source_target_pairs={{0,16},{8,24},{16,0},{24,8},{1,17},{9,25},{17,1},{25,9},{2,18},{10... | collective-permute-start | bytes 1191944 | tf_op jit(solution)/shard_map/ppermute | solution.py:457
  7.1 0.0 collective-permute-start.2
  7.1 2.5 %pack.3 = (bf16[1536,128]{1,0:T(8,128)(2,1)}, bf16[1536,128]{1,0:T(8,128)(2,1)}, bf16[1536,128]{1,0:T(8,128)(2,1)}) custom-call(s32[1]{0:T(128)} %bitcast.ctx_ref, bf16[1024,512]{1,0:T(8,128)(2,1)} %refs_3_.4, bf16[1024,512]{1,0:T(8,128)(2,1)} %refs_4_.4, bf16[1024,512]{1,0:T(8,128)(2,1)} %refs_5_.4, bf16[1024,512]{1,0:T(8,128)(2,1)} %refs_3_.4, ...), custom_call_target="tpu_custom_call" | custom-call | flops 1024 | bytes 1024 | tf_op jit(solution)/shard_map/pack/pallas_call | solution.py:201
  9.6 6.2 %collective-permute-done.refs_4_.refs_7_ = bf16[1552,128]{1,0:T(8,128)(2,1)S(1)} collective-permute-done((bf16[1552,128]{1,0:T(8,128)(2,1)}, bf16[1552,128]{1,0:T(8,128)(2,1)S(1)}, u32[]{:S(2)}, u32[]{:S(2)}) %collective-permute-start) | collective-permute-done | bytes 397344 | tf_op jit(solution)/shard_map/ppermute | solution.py:457
  15.8 9.8 %collective-permute-done.1.refs_5_.refs_8_ = bf16[1552,128]{1,0:T(8,128)(2,1)S(1)} collective-permute-done((bf16[1552,128]{1,0:T(8,128)(2,1)}, bf16[1552,128]{1,0:T(8,128)(2,1)S(1)}, u32[]{:S(2)}, u32[]{:S(2)}) %collective-permute-start.1) | collective-permute-done | bytes 397344 | tf_op jit(solution)/shard_map/ppermute | solution.py:457
  25.6 0.0 collective-permute-done.2.refs_6_.refs_9_
  25.6 1.2 collective-permute-start.7
  26.9 0.9 collective-permute-start.8
  27.8 5.4 %attend_low.1 = (bf16[512,128]{1,0:T(8,128)(2,1)S(1)}, bf16[512,128]{1,0:T(8,128)(2,1)S(1)}, bf16[512,128]{1,0:T(8,128)(2,1)S(1)}, bf16[512,128]{1,0:T(8,128)(2,1)S(1)}) custom-call(s32[1]{0:T(128)} %bitcast.ctx_ref, bf16[1024,512]{1,0:T(8,128)(2,1)S(1)} %copy-done.2, bf16[1024,512]{1,0:T(8,128)(2,1)S(1)} %copy-done.3, bf16[1024,512]{1,0:T(8,128)(2,1)S(1)} %copy-done.4, ...), custom_call_target="tpu_custom_call" | custom-call | flops 1024 | bytes 1024 | tf_op jit(solution)/shard_map/attend_low/pallas_call | solution.py:383
  33.2 0.0 collective-permute-done.3.w_sibling_ref
  33.2 1.6 %collective-permute-start.4 = (bf16[512,128]{1,0:T(8,128)(2,1)S(1)}, bf16[512,128]{1,0:T(8,128)(2,1)S(1)}, u32[]{:S(2)}, u32[]{:S(2)}) collective-permute-start(bf16[512,128]{1,0:T(8,128)(2,1)S(1)} %get-tuple-element.72), channel_id=1, source_target_pairs={{0,8},{8,0},{16,24},{24,16},{1,9},{9,1},{17,25},{25,17},{2,10},{10... | collective-permute-start | bytes 393224 | tf_op jit(solution)/shard_map/ppermute | solution.py:457
  34.7 0.5 collective-permute-start.5
  35.2 1.5 %collective-permute-start.6 = (bf16[512,128]{1,0:T(8,128)(2,1)S(1)}, bf16[512,128]{1,0:T(8,128)(2,1)S(1)}, u32[]{:S(2)}, u32[]{:S(2)}) collective-permute-start(bf16[512,128]{1,0:T(8,128)(2,1)S(1)} %get-tuple-element.74), channel_id=1, source_target_pairs={{0,24},{8,16},{16,8},{24,0},{1,25},{9,17},{17,9},{25,1},{2,26},{10... | collective-permute-start | bytes 393224 | tf_op jit(solution)/shard_map/ppermute | solution.py:457
  36.7 1.2 collective-permute-done.7.refs_10_
  38.0 0.8 copy-done.9
  38.7 0.7 collective-permute-done.8.refs_11_
  39.4 0.8 copy-done.11
  40.2 0.4 collective-permute-done.4.refs_1_
  40.6 2.6 %collective-permute-done.5.refs_2_ = bf16[512,128]{1,0:T(8,128)(2,1)S(1)} collective-permute-done((bf16[512,128]{1,0:T(8,128)(2,1)S(1)}, bf16[512,128]{1,0:T(8,128)(2,1)S(1)}, u32[]{:S(2)}, u32[]{:S(2)}) %collective-permute-start.5) | collective-permute-done | bytes 131104 | tf_op jit(solution)/shard_map/ppermute | solution.py:457
  43.1 0.0 collective-permute-done.6.refs_3_
  43.2 0.9 assemble.2.mine_ref
  44.0 0.0 collective-permute-start.9
  44.0 2.2 %collective-permute-done.9.sibling_ref = bf16[512,512]{1,0:T(8,128)(2,1)} collective-permute-done((bf16[512,512]{1,0:T(8,128)(2,1)}, bf16[512,512]{1,0:T(8,128)(2,1)}, u32[]{:S(2)}, u32[]{:S(2)}) %collective-permute-start.9) | collective-permute-done | bytes 524320 | tf_op jit(solution)/shard_map/ppermute | solution.py:457
  46.3 2.2 %copy-done = bf16[512,4096]{1,0:T(8,128)(2,1)S(1)} copy-done((bf16[512,4096]{1,0:T(8,128)(2,1)S(1)}, bf16[512,4096]{1,0:T(8,128)(2,1)}, u32[]{:S(2)}) %copy-start) | copy-done | bytes 4194328
  48.5 2.6 %project.9 = bf16[512,512]{1,0:T(8,128)(2,1)S(1)} custom-call(s32[4]{0:T(128)S(1)} %broadcast_xor_fusion.places_ref, bf16[512,512]{1,0:T(8,128)(2,1)} %assemble.2.mine_ref, bf16[512,512]{1,0:T(8,128)(2,1)} %collective-permute-done.9.sibling_ref, bf16[512,4096]{1,0:T(8,128)(2,1)S(1)} %copy-done, bf16[512,4096]{1,0:T(8,128)(2,1)} %collective-permute-done.3.w_sibling_ref), custom_call_target="tpu_custom_call" | custom-call | flops 1024 | bytes 1024 | tf_op jit(solution)/shard_map/project/pallas_call | solution.py:440
  51.1 1.6 %collective-permute-start.11 = (bf16[512,512]{1,0:T(8,128)(2,1)S(1)}, bf16[512,512]{1,0:T(8,128)(2,1)S(1)}, u32[]{:S(2)}, u32[]{:S(2)}) collective-permute-start(bf16[512,512]{1,0:T(8,128)(2,1)S(1)} %project.9), channel_id=1, source_target_pairs={{0,2},{1,3},{2,0},{3,1},{4,6},{5,7},{6,4},{7,5},{8,10},{9,11},{10,... | collective-permute-start | bytes 1572872 | tf_op jit(solution)/shard_map/ppermute | solution.py:457
  52.7 1.5 %collective-permute-start.10 = (bf16[1536,128]{1,0:T(8,128)(2,1)S(1)}, bf16[1536,128]{1,0:T(8,128)(2,1)S(1)}, u32[]{:S(2)}, u32[]{:S(2)}) collective-permute-start(bf16[1536,128]{1,0:T(8,128)(2,1)S(1)} %copy-done.14), channel_id=1, source_target_pairs={{0,24},{8,16},{16,8},{24,0},{1,25},{9,17},{17,9},{25,1},{2,26},{10... | collective-permute-start | bytes 1179656 | tf_op jit(solution)/shard_map/ppermute | solution.py:457
  54.2 2.6 %project.8 = bf16[512,512]{1,0:T(8,128)(2,1)S(1)} custom-call(s32[4]{0:T(128)S(1)} %broadcast_xor_fusion.places_ref, bf16[512,512]{1,0:T(8,128)(2,1)} %assemble.2.mine_ref, bf16[512,512]{1,0:T(8,128)(2,1)} %collective-permute-done.9.sibling_ref, bf16[512,4096]{1,0:T(8,128)(2,1)S(1)} %copy-done, bf16[512,4096]{1,0:T(8,128)(2,1)} %collective-permute-done.3.w_sibling_ref), custom_call_target="tpu_custom_call" | custom-call | flops 1024 | bytes 1024 | tf_op jit(solution)/shard_map/project/pallas_call | solution.py:440
  56.9 7.7 %collective-permute-done.10.refs_12_ = bf16[1536,128]{1,0:T(8,128)(2,1)S(1)} collective-permute-done((bf16[1536,128]{1,0:T(8,128)(2,1)S(1)}, bf16[1536,128]{1,0:T(8,128)(2,1)S(1)}, u32[]{:S(2)}, u32[]{:S(2)}) %collective-permute-start.10) | collective-permute-done | bytes 393248 | tf_op jit(solution)/shard_map/ppermute | solution.py:457
  64.5 0.5 collective-permute-start.16
  65.0 2.6 %project.10 = bf16[512,512]{1,0:T(8,128)(2,1)S(1)} custom-call(s32[4]{0:T(128)S(1)} %broadcast_xor_fusion.places_ref, bf16[512,512]{1,0:T(8,128)(2,1)} %assemble.2.mine_ref, bf16[512,512]{1,0:T(8,128)(2,1)} %collective-permute-done.9.sibling_ref, bf16[512,4096]{1,0:T(8,128)(2,1)S(1)} %copy-done, bf16[512,4096]{1,0:T(8,128)(2,1)} %collective-permute-done.3.w_sibling_ref), custom_call_target="tpu_custom_call" | custom-call | flops 1024 | bytes 1024 | tf_op jit(solution)/shard_map/project/pallas_call | solution.py:440
  67.6 2.6 %project.11 = bf16[512,512]{1,0:T(8,128)(2,1)S(1)} custom-call(s32[4]{0:T(128)S(1)} %broadcast_xor_fusion.places_ref, bf16[512,512]{1,0:T(8,128)(2,1)} %assemble.2.mine_ref, bf16[512,512]{1,0:T(8,128)(2,1)} %collective-permute-done.9.sibling_ref, bf16[512,4096]{1,0:T(8,128)(2,1)S(1)} %copy-done, bf16[512,4096]{1,0:T(8,128)(2,1)} %collective-permute-done.3.w_sibling_ref), custom_call_target="tpu_custom_call" | custom-call | flops 1024 | bytes 1024 | tf_op jit(solution)/shard_map/project/pallas_call | solution.py:440
  70.2 0.0 collective-permute-done.11
  70.2 0.1 add_convert_fusion.3
  70.4 2.7 %collective-permute-start.15 = (bf16[512,512]{1,0:T(8,128)(2,1)S(1)}, bf16[512,512]{1,0:T(8,128)(2,1)S(1)}, u32[]{:S(2)}, u32[]{:S(2)}) collective-permute-start(bf16[512,512]{1,0:T(8,128)(2,1)S(1)} %add_convert_fusion.3), channel_id=1, source_target_pairs={{0,4},{1,5},{2,6},{3,7},{4,0},{5,1},{6,2},{7,3},{8,12},{9,13},{10,... | collective-permute-start | bytes 1572872 | tf_op jit(solution)/shard_map/ppermute | solution.py:457
  73.1 0.0 copy-start.1
  73.1 8.7 %attend_high.1 = (bf16[512,128]{1,0:T(8,128)(2,1)S(1)}, bf16[512,128]{1,0:T(8,128)(2,1)S(1)}, bf16[512,128]{1,0:T(8,128)(2,1)S(1)}, bf16[512,128]{1,0:T(8,128)(2,1)S(1)}) custom-call(s32[1]{0:T(128)} %bitcast.ctx_ref, bf16[1024,512]{1,0:T(8,128)(2,1)S(1)} %copy-done.2, bf16[1024,512]{1,0:T(8,128)(2,1)S(1)} %copy-done.3, bf16[1024,512]{1,0:T(8,128)(2,1)S(1)} %copy-done.4, ...), custom_call_target="tpu_custom_call" | custom-call | flops 1024 | bytes 1024 | tf_op jit(solution)/shard_map/attend_high/pallas_call | solution.py:383
  81.8 0.6 collective-permute-start.12
  82.5 1.5 %collective-permute-start.13 = (bf16[512,128]{1,0:T(8,128)(2,1)S(1)}, bf16[512,128]{1,0:T(8,128)(2,1)S(1)}, u32[]{:S(2)}, u32[]{:S(2)}) collective-permute-start(bf16[512,128]{1,0:T(8,128)(2,1)S(1)} %get-tuple-element.93), channel_id=1, source_target_pairs={{0,16},{8,24},{16,0},{24,8},{1,17},{9,25},{17,1},{25,9},{2,18},{10... | collective-permute-start | bytes 393224 | tf_op jit(solution)/shard_map/ppermute | solution.py:457
  84.0 1.4 %collective-permute-start.14 = (bf16[512,128]{1,0:T(8,128)(2,1)S(1)}, bf16[512,128]{1,0:T(8,128)(2,1)S(1)}, u32[]{:S(2)}, u32[]{:S(2)}) collective-permute-start(bf16[512,128]{1,0:T(8,128)(2,1)S(1)} %get-tuple-element.94), channel_id=1, source_target_pairs={{0,24},{8,16},{16,8},{24,0},{1,25},{9,17},{17,9},{25,1},{2,26},{10... | collective-permute-start | bytes 393224 | tf_op jit(solution)/shard_map/ppermute | solution.py:457
  85.4 1.9 %collective-permute-done.12.refs_1_ = bf16[512,128]{1,0:T(8,128)(2,1)S(1)} collective-permute-done((bf16[512,128]{1,0:T(8,128)(2,1)S(1)}, bf16[512,128]{1,0:T(8,128)(2,1)S(1)}, u32[]{:S(2)}, u32[]{:S(2)}) %collective-permute-start.12) | collective-permute-done | bytes 131104 | tf_op jit(solution)/shard_map/ppermute | solution.py:457
  87.2 1.2 collective-permute-done.13.refs_2_
  88.4 1.4 collective-permute-done.14.refs_3_
  89.8 0.1 assemble.3.mine_ref
  89.9 5.2 %collective-permute-done.15 = bf16[512,512]{1,0:T(8,128)(2,1)S(1)} collective-permute-done((bf16[512,512]{1,0:T(8,128)(2,1)S(1)}, bf16[512,512]{1,0:T(8,128)(2,1)S(1)}, u32[]{:S(2)}, u32[]{:S(2)}) %collective-permute-start.15) | collective-permute-done | bytes 524320 | tf_op jit(solution)/shard_map/ppermute | solution.py:457
  95.2 1.9 %collective-permute-done.17.sibling_ref = bf16[512,512]{1,0:T(8,128)(2,1)S(1)} collective-permute-done((bf16[512,512]{1,0:T(8,128)(2,1)S(1)}, bf16[512,512]{1,0:T(8,128)(2,1)S(1)}, u32[]{:S(2)}, u32[]{:S(2)}) %collective-permute-start.17) | collective-permute-done | bytes 524320 | tf_op jit(solution)/shard_map/ppermute | solution.py:457
  97.1 2.3 %project.15 = bf16[512,512]{1,0:T(8,128)(2,1)S(1)} custom-call(s32[4]{0:T(128)S(1)} %broadcast_xor_fusion.places_ref, bf16[512,512]{1,0:T(8,128)(2,1)S(1)} %assemble.3.mine_ref, bf16[512,512]{1,0:T(8,128)(2,1)S(1)} %collective-permute-done.17.sibling_ref, bf16[512,4096]{1,0:T(8,128)(2,1)S(1)} %copy-done.1, bf16[512,4096]{1,0:T(8,128)(2,1)} %collective-permute-done.3.w_sibling_ref), custom_call_target="tpu_custom_call" | custom-call | flops 1024 | bytes 1024 | tf_op jit(solution)/shard_map/project/pallas_call | solution.py:440
  99.4 0.9 collective-permute-start.19
  100.3 2.3 %project.13 = bf16[512,512]{1,0:T(8,128)(2,1)S(1)} custom-call(s32[4]{0:T(128)S(1)} %broadcast_xor_fusion.places_ref, bf16[512,512]{1,0:T(8,128)(2,1)S(1)} %assemble.3.mine_ref, bf16[512,512]{1,0:T(8,128)(2,1)S(1)} %collective-permute-done.17.sibling_ref, bf16[512,4096]{1,0:T(8,128)(2,1)S(1)} %copy-done.1, bf16[512,4096]{1,0:T(8,128)(2,1)} %collective-permute-done.3.w_sibling_ref), custom_call_target="tpu_custom_call" | custom-call | flops 1024 | bytes 1024 | tf_op jit(solution)/shard_map/project/pallas_call | solution.py:440
  102.6 1.3 collective-permute-start.18
  103.9 2.3 %project.14 = bf16[512,512]{1,0:T(8,128)(2,1)S(1)} custom-call(s32[4]{0:T(128)S(1)} %broadcast_xor_fusion.places_ref, bf16[512,512]{1,0:T(8,128)(2,1)S(1)} %assemble.3.mine_ref, bf16[512,512]{1,0:T(8,128)(2,1)S(1)} %collective-permute-done.17.sibling_ref, bf16[512,4096]{1,0:T(8,128)(2,1)S(1)} %copy-done.1, bf16[512,4096]{1,0:T(8,128)(2,1)} %collective-permute-done.3.w_sibling_ref), custom_call_target="tpu_custom_call" | custom-call | flops 1024 | bytes 1024 | tf_op jit(solution)/shard_map/project/pallas_call | solution.py:440
  106.2 8.0 %collective-permute-done.19 = bf16[512,512]{1,0:T(8,128)(2,1)S(1)} collective-permute-done((bf16[512,512]{1,0:T(8,128)(2,1)S(1)}, bf16[512,512]{1,0:T(8,128)(2,1)S(1)}, u32[]{:S(2)}, u32[]{:S(2)}) %collective-permute-start.19) | collective-permute-done | bytes 524320 | tf_op jit(solution)/shard_map/ppermute | solution.py:457
  114.2 0.1 add_convert_fusion.1
  114.4 2.2 %collective-permute-start.20 = (bf16[512,512]{1,0:T(8,128)(2,1)S(1)}, bf16[512,512]{1,0:T(8,128)(2,1)S(1)}, u32[]{:S(2)}, u32[]{:S(2)}) collective-permute-start(bf16[512,512]{1,0:T(8,128)(2,1)S(1)} %add_convert_fusion.1), channel_id=1, source_target_pairs={{0,4},{1,5},{2,6},{3,7},{4,0},{5,1},{6,2},{7,3},{8,12},{9,13},{10,... | collective-permute-start | bytes 1572872 | tf_op jit(solution)/shard_map/ppermute | solution.py:457
  116.6 0.2 add_convert_fusion.2
  116.8 2.3 %project.12 = bf16[512,512]{1,0:T(8,128)(2,1)S(1)} custom-call(s32[4]{0:T(128)S(1)} %broadcast_xor_fusion.places_ref, bf16[512,512]{1,0:T(8,128)(2,1)S(1)} %assemble.3.mine_ref, bf16[512,512]{1,0:T(8,128)(2,1)S(1)} %collective-permute-done.17.sibling_ref, bf16[512,4096]{1,0:T(8,128)(2,1)S(1)} %copy-done.1, bf16[512,4096]{1,0:T(8,128)(2,1)} %collective-permute-done.3.w_sibling_ref), custom_call_target="tpu_custom_call" | custom-call | flops 1024 | bytes 1024 | tf_op jit(solution)/shard_map/project/pallas_call | solution.py:440
  119.1 15.6 %collective-permute-done.18 = bf16[512,512]{1,0:T(8,128)(2,1)S(1)} collective-permute-done((bf16[512,512]{1,0:T(8,128)(2,1)S(1)}, bf16[512,512]{1,0:T(8,128)(2,1)S(1)}, u32[]{:S(2)}, u32[]{:S(2)}) %collective-permute-start.18) | collective-permute-done | bytes 524320 | tf_op jit(solution)/shard_map/ppermute | solution.py:457
  134.7 4.4 %collective-permute-done.20 = bf16[512,512]{1,0:T(8,128)(2,1)S(1)} collective-permute-done((bf16[512,512]{1,0:T(8,128)(2,1)S(1)}, bf16[512,512]{1,0:T(8,128)(2,1)S(1)}, u32[]{:S(2)}, u32[]{:S(2)}) %collective-permute-start.20) | collective-permute-done | bytes 524320 | tf_op jit(solution)/shard_map/ppermute | solution.py:457
  139.1 0.2 add_convert_fusion
  139.3 1.0 pad_maximum_fusion
  (30 shorter events, 0.1 us)
Async XLA Ops:
  0.0 33.2 %collective-permute-start.3 = (bf16[512,4096]{1,0:T(8,128)(2,1)}, bf16[512,4096]{1,0:T(8,128)(2,1)}, u32[]{:S(2)}, u32[]{:S(2)}) collective-permute-start(bf16[512,4096]{1,0:T(8,128)(2,1)} %w_mine_ref.15), channel_id=1, source_target_pairs={{0,1},{1,0},{2,3},{3,2},{4,5},{5,4},{6,7},{7,6},{8,9},{9,8},{10,11... | collective-permute-start | bytes 12582920 | tf_op jit(solution)/shard_map/ppermute | solution.py:457
  3.0 24.8 %copy-start.2 = (bf16[1024,512]{1,0:T(8,128)(2,1)S(1)}, bf16[1024,512]{1,0:T(8,128)(2,1)}, u32[]{:S(2)}) copy-start(bf16[1024,512]{1,0:T(8,128)(2,1)} %refs_3_.4) | copy-start | bytes 3145732
  3.0 24.8 %copy-start.3 = (bf16[1024,512]{1,0:T(8,128)(2,1)S(1)}, bf16[1024,512]{1,0:T(8,128)(2,1)}, u32[]{:S(2)}) copy-start(bf16[1024,512]{1,0:T(8,128)(2,1)} %refs_4_.4) | copy-start | bytes 3145732
  3.0 24.8 %copy-start.4 = (bf16[1024,512]{1,0:T(8,128)(2,1)S(1)}, bf16[1024,512]{1,0:T(8,128)(2,1)}, u32[]{:S(2)}) copy-start(bf16[1024,512]{1,0:T(8,128)(2,1)} %refs_5_.4) | copy-start | bytes 3145732
  3.0 24.8 %copy-start.13 = (s32[1024]{0:T(1024)S(1)}, s32[1024]{0:T(1024)}, u32[]{:S(2)}) copy-start(s32[1024]{0:T(1024)} %param.9) | copy-start | bytes 12292
  3.0 12.8 %collective-permute-start = (bf16[1552,128]{1,0:T(8,128)(2,1)}, bf16[1552,128]{1,0:T(8,128)(2,1)S(1)}, u32[]{:S(2)}, u32[]{:S(2)}) collective-permute-start(bf16[1552,128]{1,0:T(8,128)(2,1)} %get-tuple-element.61), channel_id=1, source_target_pairs={{0,8},{8,0},{16,24},{24,16},{1,9},{9,1},{17,25},{25,17},{2,10},{10... | collective-permute-start | bytes 1191944 | tf_op jit(solution)/shard_map/ppermute | solution.py:457
  5.6 20.1 %collective-permute-start.1 = (bf16[1552,128]{1,0:T(8,128)(2,1)}, bf16[1552,128]{1,0:T(8,128)(2,1)S(1)}, u32[]{:S(2)}, u32[]{:S(2)}) collective-permute-start(bf16[1552,128]{1,0:T(8,128)(2,1)} %get-tuple-element.62), channel_id=1, source_target_pairs={{0,16},{8,24},{16,0},{24,8},{1,17},{9,25},{17,1},{25,9},{2,18},{10... | collective-permute-start | bytes 1191944 | tf_op jit(solution)/shard_map/ppermute | solution.py:457
  7.1 18.5 %collective-permute-start.2 = (bf16[1552,128]{1,0:T(8,128)(2,1)}, bf16[1552,128]{1,0:T(8,128)(2,1)S(1)}, u32[]{:S(2)}, u32[]{:S(2)}) collective-permute-start(bf16[1552,128]{1,0:T(8,128)(2,1)} %get-tuple-element.63), channel_id=1, source_target_pairs={{0,24},{8,16},{16,8},{24,0},{1,25},{9,17},{17,9},{25,1},{2,26},{10... | collective-permute-start | bytes 1191944 | tf_op jit(solution)/shard_map/ppermute | solution.py:457
  25.6 7.5 %copy-start.5 = (bf16[1552,128]{1,0:T(8,128)(2,1)}, bf16[1552,128]{1,0:T(8,128)(2,1)S(1)}, u32[]{:S(2)}) copy-start(bf16[1552,128]{1,0:T(8,128)(2,1)S(1)} %collective-permute-done.1.refs_5_.refs_8_) | copy-start | bytes 1191940
  25.6 7.5 %copy-start.7 = (bf16[1552,128]{1,0:T(8,128)(2,1)}, bf16[1552,128]{1,0:T(8,128)(2,1)S(1)}, u32[]{:S(2)}) copy-start(bf16[1552,128]{1,0:T(8,128)(2,1)S(1)} %collective-permute-done.2.refs_6_.refs_9_) | copy-start | bytes 1191940
  25.6 18.4 %copy-start.15 = (s32[4]{0:T(128)S(1)}, s32[4]{0:T(128)}, u32[]{:S(2)}) copy-start(s32[4]{0:T(128)} %constant.13) | copy-start | bytes 52
  25.6 12.3 %collective-permute-start.7 = (bf16[1536,128]{1,0:T(8,128)(2,1)}, bf16[1536,128]{1,0:T(8,128)(2,1)S(1)}, u32[]{:S(2)}, u32[]{:S(2)}) collective-permute-start(bf16[1536,128]{1,0:T(8,128)(2,1)} %get-tuple-element.75), channel_id=1, source_target_pairs={{0,8},{8,0},{16,24},{24,16},{1,9},{9,1},{17,25},{25,17},{2,10},{10... | collective-permute-start | bytes 1179656 | tf_op jit(solution)/shard_map/ppermute | solution.py:457
  26.9 12.5 %collective-permute-start.8 = (bf16[1536,128]{1,0:T(8,128)(2,1)}, bf16[1536,128]{1,0:T(8,128)(2,1)S(1)}, u32[]{:S(2)}, u32[]{:S(2)}) collective-permute-start(bf16[1536,128]{1,0:T(8,128)(2,1)} %get-tuple-element.76), channel_id=1, source_target_pairs={{0,16},{8,24},{16,0},{24,8},{1,17},{9,25},{17,1},{25,9},{2,18},{10... | collective-permute-start | bytes 1179656 | tf_op jit(solution)/shard_map/ppermute | solution.py:457
  33.2 7.4 %collective-permute-start.4 = (bf16[512,128]{1,0:T(8,128)(2,1)S(1)}, bf16[512,128]{1,0:T(8,128)(2,1)S(1)}, u32[]{:S(2)}, u32[]{:S(2)}) collective-permute-start(bf16[512,128]{1,0:T(8,128)(2,1)S(1)} %get-tuple-element.72), channel_id=1, source_target_pairs={{0,8},{8,0},{16,24},{24,16},{1,9},{9,1},{17,25},{25,17},{2,10},{10... | collective-permute-start | bytes 393224 | tf_op jit(solution)/shard_map/ppermute | solution.py:457
  34.7 8.4 %collective-permute-start.5 = (bf16[512,128]{1,0:T(8,128)(2,1)S(1)}, bf16[512,128]{1,0:T(8,128)(2,1)S(1)}, u32[]{:S(2)}, u32[]{:S(2)}) collective-permute-start(bf16[512,128]{1,0:T(8,128)(2,1)S(1)} %get-tuple-element.73), channel_id=1, source_target_pairs={{0,16},{8,24},{16,0},{24,8},{1,17},{9,25},{17,1},{25,9},{2,18},{10... | collective-permute-start | bytes 393224 | tf_op jit(solution)/shard_map/ppermute | solution.py:457
  35.2 7.9 %collective-permute-start.6 = (bf16[512,128]{1,0:T(8,128)(2,1)S(1)}, bf16[512,128]{1,0:T(8,128)(2,1)S(1)}, u32[]{:S(2)}, u32[]{:S(2)}) collective-permute-start(bf16[512,128]{1,0:T(8,128)(2,1)S(1)} %get-tuple-element.74), channel_id=1, source_target_pairs={{0,24},{8,16},{16,8},{24,0},{1,25},{9,17},{17,9},{25,1},{2,26},{10... | collective-permute-start | bytes 393224 | tf_op jit(solution)/shard_map/ppermute | solution.py:457
  38.0 0.8 copy-start.9
  39.4 0.8 copy-start.11
  44.0 2.3 %collective-permute-start.9 = (bf16[512,512]{1,0:T(8,128)(2,1)}, bf16[512,512]{1,0:T(8,128)(2,1)}, u32[]{:S(2)}, u32[]{:S(2)}) collective-permute-start(bf16[512,512]{1,0:T(8,128)(2,1)} %assemble.2.mine_ref), channel_id=1, source_target_pairs={{0,1},{1,0},{2,3},{3,2},{4,5},{5,4},{6,7},{7,6},{8,9},{9,8},{10,11... | collective-permute-start | bytes 1572872 | tf_op jit(solution)/shard_map/ppermute | solution.py:457
  46.3 2.2 %copy-start = (bf16[512,4096]{1,0:T(8,128)(2,1)S(1)}, bf16[512,4096]{1,0:T(8,128)(2,1)}, u32[]{:S(2)}) copy-start(bf16[512,4096]{1,0:T(8,128)(2,1)} %w_mine_ref.15) | copy-start | bytes 12582916
  48.5 4.3 %copy-start.14 = (bf16[1536,128]{1,0:T(8,128)(2,1)S(1)}, bf16[1536,128]{1,0:T(8,128)(2,1)}, u32[]{:S(2)}) copy-start(bf16[1536,128]{1,0:T(8,128)(2,1)} %get-tuple-element.84) | copy-start | bytes 1179652
  51.1 19.1 %collective-permute-start.11 = (bf16[512,512]{1,0:T(8,128)(2,1)S(1)}, bf16[512,512]{1,0:T(8,128)(2,1)S(1)}, u32[]{:S(2)}, u32[]{:S(2)}) collective-permute-start(bf16[512,512]{1,0:T(8,128)(2,1)S(1)} %project.9), channel_id=1, source_target_pairs={{0,2},{1,3},{2,0},{3,1},{4,6},{5,7},{6,4},{7,5},{8,10},{9,11},{10,... | collective-permute-start | bytes 1572872 | tf_op jit(solution)/shard_map/ppermute | solution.py:457
  52.7 11.8 %collective-permute-start.10 = (bf16[1536,128]{1,0:T(8,128)(2,1)S(1)}, bf16[1536,128]{1,0:T(8,128)(2,1)S(1)}, u32[]{:S(2)}, u32[]{:S(2)}) collective-permute-start(bf16[1536,128]{1,0:T(8,128)(2,1)S(1)} %copy-done.14), channel_id=1, source_target_pairs={{0,24},{8,16},{16,8},{24,0},{1,25},{9,17},{17,9},{25,1},{2,26},{10... | collective-permute-start | bytes 1179656 | tf_op jit(solution)/shard_map/ppermute | solution.py:457
  64.5 25.4 %collective-permute-start.16 = (bf16[512,512]{1,0:T(8,128)(2,1)S(1)}, bf16[512,512]{1,0:T(8,128)(2,1)S(1)}, u32[]{:S(2)}, u32[]{:S(2)}) collective-permute-start(bf16[512,512]{1,0:T(8,128)(2,1)S(1)} %project.8), channel_id=1, source_target_pairs={{0,2},{1,3},{2,0},{3,1},{4,6},{5,7},{6,4},{7,5},{8,10},{9,11},{10,... | collective-permute-start | bytes 1572872 | tf_op jit(solution)/shard_map/ppermute | solution.py:457
  67.6 5.5 %copy-start.6 = (bf16[1552,128]{1,0:T(8,128)(2,1)S(1)}, bf16[1552,128]{1,0:T(8,128)(2,1)}, u32[]{:S(2)}) copy-start(bf16[1552,128]{1,0:T(8,128)(2,1)} %copy-done.5) | copy-start | bytes 1191940
  67.6 5.5 %copy-start.8 = (bf16[1552,128]{1,0:T(8,128)(2,1)S(1)}, bf16[1552,128]{1,0:T(8,128)(2,1)}, u32[]{:S(2)}) copy-start(bf16[1552,128]{1,0:T(8,128)(2,1)} %copy-done.7) | copy-start | bytes 1191940
  67.6 5.5 %copy-start.10 = (bf16[1536,128]{1,0:T(8,128)(2,1)S(1)}, bf16[1536,128]{1,0:T(8,128)(2,1)}, u32[]{:S(2)}) copy-start(bf16[1536,128]{1,0:T(8,128)(2,1)} %copy-done.9) | copy-start | bytes 1179652
  67.6 5.4 %copy-start.12 = (bf16[1536,128]{1,0:T(8,128)(2,1)S(1)}, bf16[1536,128]{1,0:T(8,128)(2,1)}, u32[]{:S(2)}) copy-start(bf16[1536,128]{1,0:T(8,128)(2,1)} %copy-done.11) | copy-start | bytes 1179652
  70.4 24.8 %collective-permute-start.15 = (bf16[512,512]{1,0:T(8,128)(2,1)S(1)}, bf16[512,512]{1,0:T(8,128)(2,1)S(1)}, u32[]{:S(2)}, u32[]{:S(2)}) collective-permute-start(bf16[512,512]{1,0:T(8,128)(2,1)S(1)} %add_convert_fusion.3), channel_id=1, source_target_pairs={{0,4},{1,5},{2,6},{3,7},{4,0},{5,1},{6,2},{7,3},{8,12},{9,13},{10,... | collective-permute-start | bytes 1572872 | tf_op jit(solution)/shard_map/ppermute | solution.py:457
  73.1 24.0 %copy-start.1 = (bf16[512,4096]{1,0:T(8,128)(2,1)S(1)}, bf16[512,4096]{1,0:T(8,128)(2,1)}, u32[]{:S(2)}) copy-start(bf16[512,4096]{1,0:T(8,128)(2,1)} %w_mine_ref.15) | copy-start | bytes 12582916
  81.8 5.4 %collective-permute-start.12 = (bf16[512,128]{1,0:T(8,128)(2,1)S(1)}, bf16[512,128]{1,0:T(8,128)(2,1)S(1)}, u32[]{:S(2)}, u32[]{:S(2)}) collective-permute-start(bf16[512,128]{1,0:T(8,128)(2,1)S(1)} %get-tuple-element.92), channel_id=1, source_target_pairs={{0,8},{8,0},{16,24},{24,16},{1,9},{9,1},{17,25},{25,17},{2,10},{10... | collective-permute-start | bytes 393224 | tf_op jit(solution)/shard_map/ppermute | solution.py:457
  82.5 6.0 %collective-permute-start.13 = (bf16[512,128]{1,0:T(8,128)(2,1)S(1)}, bf16[512,128]{1,0:T(8,128)(2,1)S(1)}, u32[]{:S(2)}, u32[]{:S(2)}) collective-permute-start(bf16[512,128]{1,0:T(8,128)(2,1)S(1)} %get-tuple-element.93), channel_id=1, source_target_pairs={{0,16},{8,24},{16,0},{24,8},{1,17},{9,25},{17,1},{25,9},{2,18},{10... | collective-permute-start | bytes 393224 | tf_op jit(solution)/shard_map/ppermute | solution.py:457
  84.0 5.9 %collective-permute-start.14 = (bf16[512,128]{1,0:T(8,128)(2,1)S(1)}, bf16[512,128]{1,0:T(8,128)(2,1)S(1)}, u32[]{:S(2)}, u32[]{:S(2)}) collective-permute-start(bf16[512,128]{1,0:T(8,128)(2,1)S(1)} %get-tuple-element.94), channel_id=1, source_target_pairs={{0,24},{8,16},{16,8},{24,0},{1,25},{9,17},{17,9},{25,1},{2,26},{10... | collective-permute-start | bytes 393224 | tf_op jit(solution)/shard_map/ppermute | solution.py:457
  95.2 1.9 %collective-permute-start.17 = (bf16[512,512]{1,0:T(8,128)(2,1)S(1)}, bf16[512,512]{1,0:T(8,128)(2,1)S(1)}, u32[]{:S(2)}, u32[]{:S(2)}) collective-permute-start(bf16[512,512]{1,0:T(8,128)(2,1)S(1)} %assemble.3.mine_ref), channel_id=1, source_target_pairs={{0,1},{1,0},{2,3},{3,2},{4,5},{5,4},{6,7},{7,6},{8,9},{9,8},{10,11... | collective-permute-start | bytes 1572872 | tf_op jit(solution)/shard_map/ppermute | solution.py:457
  99.4 14.8 %collective-permute-start.19 = (bf16[512,512]{1,0:T(8,128)(2,1)S(1)}, bf16[512,512]{1,0:T(8,128)(2,1)S(1)}, u32[]{:S(2)}, u32[]{:S(2)}) collective-permute-start(bf16[512,512]{1,0:T(8,128)(2,1)S(1)} %project.15), channel_id=1, source_target_pairs={{0,2},{1,3},{2,0},{3,1},{4,6},{5,7},{6,4},{7,5},{8,10},{9,11},{10,... | collective-permute-start | bytes 1572872 | tf_op jit(solution)/shard_map/ppermute | solution.py:457
  102.6 32.1 %collective-permute-start.18 = (bf16[512,512]{1,0:T(8,128)(2,1)S(1)}, bf16[512,512]{1,0:T(8,128)(2,1)S(1)}, u32[]{:S(2)}, u32[]{:S(2)}) collective-permute-start(bf16[512,512]{1,0:T(8,128)(2,1)S(1)} %project.13), channel_id=1, source_target_pairs={{0,2},{1,3},{2,0},{3,1},{4,6},{5,7},{6,4},{7,5},{8,10},{9,11},{10,... | collective-permute-start | bytes 1572872 | tf_op jit(solution)/shard_map/ppermute | solution.py:457
  114.4 24.7 %collective-permute-start.20 = (bf16[512,512]{1,0:T(8,128)(2,1)S(1)}, bf16[512,512]{1,0:T(8,128)(2,1)S(1)}, u32[]{:S(2)}, u32[]{:S(2)}) collective-permute-start(bf16[512,512]{1,0:T(8,128)(2,1)S(1)} %add_convert_fusion.1), channel_id=1, source_target_pairs={{0,4},{1,5},{2,6},{3,7},{4,0},{5,1},{6,2},{7,3},{8,12},{9,13},{10,... | collective-permute-start | bytes 1572872 | tf_op jit(solution)/shard_map/ppermute | solution.py:457

commit v11 on v10

--- a/solution.py
+++ b/solution.py
@@ -213,6 +213,32 @@
     )(ctx_index, *operands)
 
 
+def pack_projection(places, w_mine, w_sibling):
+    depth, width = w_mine.shape
+    turns = len(TURNS)
+    columns = width // (2 * turns)
+
+    def kernel(places_ref, mine_in, sibling_in, mine_out, sibling_out):
+        mine_out[...] = mine_in[...]
+        sibling_out[...] = sibling_in[...]
+
+    in_spec = pl.BlockSpec((depth, columns), lambda turn, at: (0, at[turn]))
+    out_spec = pl.BlockSpec((depth, columns), lambda turn, at: (0, turn))
+    return pl.pallas_call(
+        kernel,
+        grid_spec=pltpu.PrefetchScalarGridSpec(
+            num_scalar_prefetch=1,
+            grid=(turns,),
+            in_specs=[in_spec] * 2,
+            out_specs=[out_spec] * 2,
+        ),
+        out_shape=[jax.ShapeDtypeStruct((depth, turns * columns), w_mine.dtype)] * 2,
+        compiler_params=params(56),
+        cost_estimate=SMALL,
+        name="pack_projection",
+    )(places, w_mine, w_sibling)
+
+
 def attend(ctx_index, queries, keys, values, docs, low, high):
     rows = queries.shape[0] // 2
     group = queries.shape[1] // HD
@@ -427,29 +453,27 @@
     )(ctx_index, *pieces)
 
 
-def project(places, turn, mine, sibling, w_mine, w_sibling):
+def project(turn, mine, sibling, w_mine, w_sibling):
     rows, depth = mine.shape
-    columns = w_mine.shape[1] // (2 * len(TURNS))
-
-    def kernel(places_ref, mine_ref, sibling_ref, w_mine_ref, w_sibling_ref, out_ref):
+    columns = w_mine.shape[1] // len(TURNS)
+
+    def kernel(mine_ref, sibling_ref, w_mine_ref, w_sibling_ref, out_ref):
         total = jnp.dot(mine_ref[...], w_mine_ref[...], preferred_element_type=jnp.float32)
         total += jnp.dot(sibling_ref[...], w_sibling_ref[...], preferred_element_type=jnp.float32)
         out_ref[...] = total.astype(jnp.bfloat16)
 
-    weights = pl.BlockSpec((depth, columns), lambda step, at: (0, at[turn]))
+    weights = pl.BlockSpec((depth, columns), lambda step: (0, turn))
+    attended = pl.BlockSpec((rows, depth), lambda step: (0, 0))
     return pl.pallas_call(
         kernel,
-        grid_spec=pltpu.PrefetchScalarGridSpec(
-            num_scalar_prefetch=1,
-            grid=(1,),
-            in_specs=[whole((rows, depth)), whole((rows, depth)), weights, weights],
-            out_specs=whole((rows, columns)),
-        ),
+        grid=(1,),
+        in_specs=[attended, attended, weights, weights],
+        out_specs=pl.BlockSpec((rows, columns), lambda step: (0, 0)),
         out_shape=jax.ShapeDtypeStruct((rows, columns), jnp.bfloat16),
         compiler_params=params(16),
         cost_estimate=SMALL,
         name="project",
-    )(places, mine, sibling, w_mine, w_sibling)
+    )(mine, sibling, w_mine, w_sibling)
 
 
 def swap(value, axis, distance):
@@ -485,17 +509,18 @@
     low_out, later = tie(low_out, (queries, keys, values))
     low = [swap(low_out[distance - 1], "ctx", distance) for distance in near]
     high_out = pack(ctx_index, 1, *later, None)
-    high_out, low = tie(high_out, low)
+    w_packed = pack_projection(places, w_out, w_sibling)
+    high_out, low, w_packed = tie(high_out, low, w_packed)
     high = [swap(high_out[0], "ctx", 1), swap(high_out[1], "ctx", 2)]
 
     def send_back(pieces):
         return [swap(pieces[distance], "ctx", distance) for distance in near]
 
     def share_of(mine, sibling, turn):
-        return project(places, turn, mine, sibling, w_out, w_sibling)
+        return project(turn, mine, sibling, *w_packed)
 
     pieces = attend(ctx_index, queries, keys, values, docs, low, None)
-    pieces, diagonal_out, w_sibling = tie(pieces, high_out[2], w_sibling)
+    pieces, diagonal_out = tie(pieces, high_out[2])
     back = send_back(pieces)
     back, high = tie(back, high)
     high.append(swap(diagonal_out, "ctx", 3))

time: 141 us -> 130 us (0.922)
  Pallas kernels: 39.9 us -> 30.3 us
  local copies, waits for them, and re-layouts: 3.76 us -> 0.04 us
  waiting for transfers between devices: 70.4 us -> 73.3 us
    pallas_call x8 -> x9, Pallas kernels: 19.7 us -> 11.6 us  [the longest x1 5.89 us: pack_projection(): pl.pallas_call(kernel, grid_spec=pltpu.PrefetchScalarGridSpec(num_scalar_...]
    unnamed x32 -> x20, local copies, waits for them, and re-layouts: 3.76 us -> 0.04 us
    ppermute x21, waiting for transfers between devices: 70.4 us -> 73.3 us  [swap(): lax.ppermute(value, axis, [(source, source ^ distance) for source in rang...]
  transfers between devices with their start and end apart: 21 -> 21, of which waited for: 16 -> 14; matrix products, arithmetic and copies ran while one was open for 0% -> 1% of each run, Pallas kernels for 24% -> 22%
where the time goes in v11:
time: 130 us
  waiting for transfers between devices  73.3 us (56%)
  Pallas kernels  30.3 us (23%)
  starting transfers between devices  24.1 us (19%)
  other arithmetic  2.24 us (2%)
    ppermute x21, waiting for transfers between devices, swap(): lax.ppermute(value, axis, [(source, source ^ distance) for source in rang...  73.3 us
    ppermute x21, starting transfers between devices, swap(): lax.ppermute(value, axis, [(source, source ^ distance) for source in rang...  24.1 us
    pallas_call x2, Pallas kernels, attend(): pl.pallas_call(kernel, grid_spec=pltpu.PrefetchScalarGridSpec(num_scalar_...  13.5 us
    pallas_call x1, Pallas kernels, pack_projection(): pl.pallas_call(kernel, grid_spec=pltpu.PrefetchScalarGridSpec(num_scalar_...  5.89 us
    pallas_call x8, Pallas kernels, project(): pl.pallas_call(kernel, grid=(1,), in_specs=[attended, attended, weights,...  5.69 us
    pallas_call x2, Pallas kernels, pack(): pl.pallas_call(kernel, grid_spec=pltpu.PrefetchScalarGridSpec(num_scalar_...  5.03 us
  transfers between devices with their start and end apart: 21, of which 14 were waited for; matrix products, arithmetic and copies ran while one was open for 1% of the time, Pallas kernels for 22%

profile of v11, /device:TPU:0, one launch (start us, length us, event | category | flops | bytes accessed | tf_op | source)
XLA Modules:
  0.0 130.1 jit_solution(16854619653852734488)
XLA Ops:
  0.0 0.5 collective-permute-start.3
  0.5 2.5 %pack.2 = (bf16[1552,128]{1,0:T(8,128)(2,1)}, bf16[1552,128]{1,0:T(8,128)(2,1)}, bf16[1552,128]{1,0:T(8,128)(2,1)}) custom-call(s32[1]{0:T(128)} %bitcast.ctx_ref, bf16[1024,512]{1,0:T(8,128)(2,1)} %refs_3_.4, bf16[1024,512]{1,0:T(8,128)(2,1)} %refs_4_.4, bf16[1024,512]{1,0:T(8,128)(2,1)} %refs_5_.4, bf16[1024,512]{1,0:T(8,128)(2,1)} %refs_3_.4, ...), custom_call_target="tpu_custom_call" | custom-call | flops 1024 | bytes 1024 | tf_op jit(solution)/shard_map/pack/pallas_call | solution.py:201
  3.0 2.5 %collective-permute-start = (bf16[1552,128]{1,0:T(8,128)(2,1)}, bf16[1552,128]{1,0:T(8,128)(2,1)S(1)}, u32[]{:S(2)}, u32[]{:S(2)}) collective-permute-start(bf16[1552,128]{1,0:T(8,128)(2,1)} %get-tuple-element.64), channel_id=1, source_target_pairs={{0,8},{8,0},{16,24},{24,16},{1,9},{9,1},{17,25},{25,17},{2,10},{10... | collective-permute-start | bytes 1191944 | tf_op jit(solution)/shard_map/ppermute | solution.py:481
  5.4 1.5 %collective-permute-start.1 = (bf16[1552,128]{1,0:T(8,128)(2,1)}, bf16[1552,128]{1,0:T(8,128)(2,1)S(1)}, u32[]{:S(2)}, u32[]{:S(2)}) collective-permute-start(bf16[1552,128]{1,0:T(8,128)(2,1)} %get-tuple-element.65), channel_id=1, source_target_pairs={{0,16},{8,24},{16,0},{24,8},{1,17},{9,25},{17,1},{25,9},{2,18},{10... | collective-permute-start | bytes 1191944 | tf_op jit(solution)/shard_map/ppermute | solution.py:481
  7.0 0.0 collective-permute-start.2
  7.0 2.5 %pack.3 = (bf16[1536,128]{1,0:T(8,128)(2,1)}, bf16[1536,128]{1,0:T(8,128)(2,1)}, bf16[1536,128]{1,0:T(8,128)(2,1)}) custom-call(s32[1]{0:T(128)} %bitcast.ctx_ref, bf16[1024,512]{1,0:T(8,128)(2,1)} %refs_3_.4, bf16[1024,512]{1,0:T(8,128)(2,1)} %refs_4_.4, bf16[1024,512]{1,0:T(8,128)(2,1)} %refs_5_.4, bf16[1024,512]{1,0:T(8,128)(2,1)} %refs_3_.4, ...), custom_call_target="tpu_custom_call" | custom-call | flops 1024 | bytes 1024 | tf_op jit(solution)/shard_map/pack/pallas_call | solution.py:201
  9.5 0.5 broadcast_xor_fusion.places_ref
  10.0 0.0 copy-start.4
  10.0 0.0 copy-start.5
  10.1 0.0 collective-permute-done.3.sibling_in
  10.1 5.9 %pack_projection.1 = (bf16[512,2048]{1,0:T(8,128)(2,1)}, bf16[512,2048]{1,0:T(8,128)(2,1)}) custom-call(s32[4]{0:T(128)} %broadcast_xor_fusion.places_ref, bf16[512,4096]{1,0:T(8,128)(2,1)} %mine_in.1, bf16[512,4096]{1,0:T(8,128)(2,1)} %collective-permute-done.3.sibling_in), custom_call_target="tpu_custom_call" | custom-call | flops 1024 | bytes 1024 | tf_op jit(solution)/shard_map/pack_projection/pallas_call | solution.py:227
  16.0 0.0 collective-permute-done.refs_4_.refs_7_
  16.0 9.5 %collective-permute-done.1.refs_5_.refs_8_ = bf16[1552,128]{1,0:T(8,128)(2,1)S(1)} collective-permute-done((bf16[1552,128]{1,0:T(8,128)(2,1)}, bf16[1552,128]{1,0:T(8,128)(2,1)S(1)}, u32[]{:S(2)}, u32[]{:S(2)}) %collective-permute-start.1) | collective-permute-done | bytes 397344 | tf_op jit(solution)/shard_map/ppermute | solution.py:481
  25.5 0.0 collective-permute-done.2.refs_6_.refs_9_
  25.5 1.2 collective-permute-start.7
  26.8 0.9 collective-permute-start.8
  27.7 7.3 %attend_low.1 = (bf16[512,128]{1,0:T(8,128)(2,1)S(1)}, bf16[512,128]{1,0:T(8,128)(2,1)S(1)}, bf16[512,128]{1,0:T(8,128)(2,1)S(1)}, bf16[512,128]{1,0:T(8,128)(2,1)S(1)}) custom-call(s32[1]{0:T(128)} %bitcast.ctx_ref, bf16[1024,512]{1,0:T(8,128)(2,1)S(1)} %copy-done.2, bf16[1024,512]{1,0:T(8,128)(2,1)S(1)} %copy-done.3, bf16[1024,512]{1,0:T(8,128)(2,1)S(1)} %copy-done.4, ...), custom_call_target="tpu_custom_call" | custom-call | flops 1024 | bytes 1024 | tf_op jit(solution)/shard_map/attend_low/pallas_call | solution.py:409
  35.0 1.6 %collective-permute-start.4 = (bf16[512,128]{1,0:T(8,128)(2,1)S(1)}, bf16[512,128]{1,0:T(8,128)(2,1)S(1)}, u32[]{:S(2)}, u32[]{:S(2)}) collective-permute-start(bf16[512,128]{1,0:T(8,128)(2,1)S(1)} %get-tuple-element.77), channel_id=1, source_target_pairs={{0,8},{8,0},{16,24},{24,16},{1,9},{9,1},{17,25},{25,17},{2,10},{10... | collective-permute-start | bytes 393224 | tf_op jit(solution)/shard_map/ppermute | solution.py:481
  36.5 0.5 collective-permute-start.5
  37.0 1.5 %collective-permute-start.6 = (bf16[512,128]{1,0:T(8,128)(2,1)S(1)}, bf16[512,128]{1,0:T(8,128)(2,1)S(1)}, u32[]{:S(2)}, u32[]{:S(2)}) collective-permute-start(bf16[512,128]{1,0:T(8,128)(2,1)S(1)} %get-tuple-element.79), channel_id=1, source_target_pairs={{0,24},{8,16},{16,8},{24,0},{1,25},{9,17},{17,9},{25,1},{2,26},{10... | collective-permute-start | bytes 393224 | tf_op jit(solution)/shard_map/ppermute | solution.py:481
  38.5 2.6 %collective-permute-done.4.refs_1_ = bf16[512,128]{1,0:T(8,128)(2,1)S(1)} collective-permute-done((bf16[512,128]{1,0:T(8,128)(2,1)S(1)}, bf16[512,128]{1,0:T(8,128)(2,1)S(1)}, u32[]{:S(2)}, u32[]{:S(2)}) %collective-permute-start.4) | collective-permute-done | bytes 131104 | tf_op jit(solution)/shard_map/ppermute | solution.py:481
  41.1 2.4 %collective-permute-done.5.refs_2_ = bf16[512,128]{1,0:T(8,128)(2,1)S(1)} collective-permute-done((bf16[512,128]{1,0:T(8,128)(2,1)S(1)}, bf16[512,128]{1,0:T(8,128)(2,1)S(1)}, u32[]{:S(2)}, u32[]{:S(2)}) %collective-permute-start.5) | collective-permute-done | bytes 131104 | tf_op jit(solution)/shard_map/ppermute | solution.py:481
  43.5 0.0 collective-permute-done.6.refs_3_
  43.5 0.0 collective-permute-done.7.refs_10_
  43.5 0.0 collective-permute-done.8.refs_11_
  43.5 0.1 assemble.2.mine_ref
  43.7 0.1 collective-permute-start.9
  43.7 1.9 %collective-permute-done.9.sibling_ref = bf16[512,512]{1,0:T(8,128)(2,1)S(1)} collective-permute-done((bf16[512,512]{1,0:T(8,128)(2,1)S(1)}, bf16[512,512]{1,0:T(8,128)(2,1)S(1)}, u32[]{:S(2)}, u32[]{:S(2)}) %collective-permute-start.9) | collective-permute-done | bytes 524320 | tf_op jit(solution)/shard_map/ppermute | solution.py:481
  45.6 0.7 project.9
  46.4 1.6 %collective-permute-start.11 = (bf16[512,512]{1,0:T(8,128)(2,1)S(1)}, bf16[512,512]{1,0:T(8,128)(2,1)S(1)}, u32[]{:S(2)}, u32[]{:S(2)}) collective-permute-start(bf16[512,512]{1,0:T(8,128)(2,1)S(1)} %project.9), channel_id=1, source_target_pairs={{0,2},{1,3},{2,0},{3,1},{4,6},{5,7},{6,4},{7,5},{8,10},{9,11},{10,... | collective-permute-start | bytes 1572872 | tf_op jit(solution)/shard_map/ppermute | solution.py:481
  48.0 1.2 collective-permute-start.10
  49.2 0.7 project.8
  49.9 9.9 %collective-permute-done.10.refs_12_ = bf16[1536,128]{1,0:T(8,128)(2,1)S(1)} collective-permute-done((bf16[1536,128]{1,0:T(8,128)(2,1)S(1)}, bf16[1536,128]{1,0:T(8,128)(2,1)S(1)}, u32[]{:S(2)}, u32[]{:S(2)}) %collective-permute-start.10) | collective-permute-done | bytes 393248 | tf_op jit(solution)/shard_map/ppermute | solution.py:481
  59.8 0.4 collective-permute-start.16
  60.2 0.7 project.10
  60.9 0.7 project.11
  61.7 0.1 add_convert_fusion.3
  61.8 2.7 %collective-permute-start.15 = (bf16[512,512]{1,0:T(8,128)(2,1)S(1)}, bf16[512,512]{1,0:T(8,128)(2,1)S(1)}, u32[]{:S(2)}, u32[]{:S(2)}) collective-permute-start(bf16[512,512]{1,0:T(8,128)(2,1)S(1)} %add_convert_fusion.3), channel_id=1, source_target_pairs={{0,4},{1,5},{2,6},{3,7},{4,0},{5,1},{6,2},{7,3},{8,12},{9,13},{10,... | collective-permute-start | bytes 1572872 | tf_op jit(solution)/shard_map/ppermute | solution.py:481
  64.5 6.2 %attend_high.1 = (bf16[512,128]{1,0:T(8,128)(2,1)S(1)}, bf16[512,128]{1,0:T(8,128)(2,1)S(1)}, bf16[512,128]{1,0:T(8,128)(2,1)S(1)}, bf16[512,128]{1,0:T(8,128)(2,1)S(1)}) custom-call(s32[1]{0:T(128)} %bitcast.ctx_ref, bf16[1024,512]{1,0:T(8,128)(2,1)S(1)} %copy-done.2, bf16[1024,512]{1,0:T(8,128)(2,1)S(1)} %copy-done.3, bf16[1024,512]{1,0:T(8,128)(2,1)S(1)} %copy-done.4, ...), custom_call_target="tpu_custom_call" | custom-call | flops 1024 | bytes 1024 | tf_op jit(solution)/shard_map/attend_high/pallas_call | solution.py:409
  70.7 1.2 collective-permute-start.12
  71.8 0.6 collective-permute-start.13
  72.5 1.7 %collective-permute-start.14 = (bf16[512,128]{1,0:T(8,128)(2,1)S(1)}, bf16[512,128]{1,0:T(8,128)(2,1)S(1)}, u32[]{:S(2)}, u32[]{:S(2)}) collective-permute-start(bf16[512,128]{1,0:T(8,128)(2,1)S(1)} %get-tuple-element.100), channel_id=1, source_target_pairs={{0,24},{8,16},{16,8},{24,0},{1,25},{9,17},{17,9},{25,1},{2,26},{10... | collective-permute-start | bytes 393224 | tf_op jit(solution)/shard_map/ppermute | solution.py:481
  74.2 2.4 %collective-permute-done.12.refs_1_ = bf16[512,128]{1,0:T(8,128)(2,1)S(1)} collective-permute-done((bf16[512,128]{1,0:T(8,128)(2,1)S(1)}, bf16[512,128]{1,0:T(8,128)(2,1)S(1)}, u32[]{:S(2)}, u32[]{:S(2)}) %collective-permute-start.12) | collective-permute-done | bytes 131104 | tf_op jit(solution)/shard_map/ppermute | solution.py:481
  76.6 0.4 collective-permute-done.13.refs_2_
  77.0 1.4 %collective-permute-done.14.refs_3_ = bf16[512,128]{1,0:T(8,128)(2,1)S(1)} collective-permute-done((bf16[512,128]{1,0:T(8,128)(2,1)S(1)}, bf16[512,128]{1,0:T(8,128)(2,1)S(1)}, u32[]{:S(2)}, u32[]{:S(2)}) %collective-permute-start.14) | collective-permute-done | bytes 131104 | tf_op jit(solution)/shard_map/ppermute | solution.py:481
  78.4 0.1 assemble.3.mine_ref
  78.5 4.8 %collective-permute-done.16 = bf16[512,512]{1,0:T(8,128)(2,1)S(1)} collective-permute-done((bf16[512,512]{1,0:T(8,128)(2,1)S(1)}, bf16[512,512]{1,0:T(8,128)(2,1)S(1)}, u32[]{:S(2)}, u32[]{:S(2)}) %collective-permute-start.16) | collective-permute-done | bytes 524320 | tf_op jit(solution)/shard_map/ppermute | solution.py:481
  83.2 3.4 %collective-permute-done.15 = bf16[512,512]{1,0:T(8,128)(2,1)S(1)} collective-permute-done((bf16[512,512]{1,0:T(8,128)(2,1)S(1)}, bf16[512,512]{1,0:T(8,128)(2,1)S(1)}, u32[]{:S(2)}, u32[]{:S(2)}) %collective-permute-start.15) | collective-permute-done | bytes 524320 | tf_op jit(solution)/shard_map/ppermute | solution.py:481
  86.6 0.0 collective-permute-start.17
  86.6 1.9 %collective-permute-done.17.sibling_ref = bf16[512,512]{1,0:T(8,128)(2,1)S(1)} collective-permute-done((bf16[512,512]{1,0:T(8,128)(2,1)S(1)}, bf16[512,512]{1,0:T(8,128)(2,1)S(1)}, u32[]{:S(2)}, u32[]{:S(2)}) %collective-permute-start.17) | collective-permute-done | bytes 524320 | tf_op jit(solution)/shard_map/ppermute | solution.py:481
  88.5 0.7 project.15
  89.2 0.9 collective-permute-start.19
  90.1 0.7 project.13
  90.8 1.3 collective-permute-start.18
  92.1 0.7 project.14
  92.8 11.2 %collective-permute-done.19 = bf16[512,512]{1,0:T(8,128)(2,1)S(1)} collective-permute-done((bf16[512,512]{1,0:T(8,128)(2,1)S(1)}, bf16[512,512]{1,0:T(8,128)(2,1)S(1)}, u32[]{:S(2)}, u32[]{:S(2)}) %collective-permute-start.19) | collective-permute-done | bytes 524320 | tf_op jit(solution)/shard_map/ppermute | solution.py:481
  104.1 0.1 add_convert_fusion.1
  104.2 2.2 %collective-permute-start.20 = (bf16[512,512]{1,0:T(8,128)(2,1)S(1)}, bf16[512,512]{1,0:T(8,128)(2,1)S(1)}, u32[]{:S(2)}, u32[]{:S(2)}) collective-permute-start(bf16[512,512]{1,0:T(8,128)(2,1)S(1)} %add_convert_fusion.1), channel_id=1, source_target_pairs={{0,4},{1,5},{2,6},{3,7},{4,0},{5,1},{6,2},{7,3},{8,12},{9,13},{10,... | collective-permute-start | bytes 1572872 | tf_op jit(solution)/shard_map/ppermute | solution.py:481
  106.4 0.2 add_convert_fusion.2
  106.6 0.7 project.12
  107.3 17.2 %collective-permute-done.18 = bf16[512,512]{1,0:T(8,128)(2,1)S(1)} collective-permute-done((bf16[512,512]{1,0:T(8,128)(2,1)S(1)}, bf16[512,512]{1,0:T(8,128)(2,1)S(1)}, u32[]{:S(2)}, u32[]{:S(2)}) %collective-permute-start.18) | collective-permute-done | bytes 524320 | tf_op jit(solution)/shard_map/ppermute | solution.py:481
  124.5 4.4 %collective-permute-done.20 = bf16[512,512]{1,0:T(8,128)(2,1)S(1)} collective-permute-done((bf16[512,512]{1,0:T(8,128)(2,1)S(1)}, bf16[512,512]{1,0:T(8,128)(2,1)S(1)}, u32[]{:S(2)}, u32[]{:S(2)}) %collective-permute-start.20) | collective-permute-done | bytes 524320 | tf_op jit(solution)/shard_map/ppermute | solution.py:481
  128.9 0.2 add_convert_fusion
  129.1 1.0 pad_maximum_fusion
  (19 shorter events, 0.0 us)
Async XLA Ops:
  0.0 10.1 %collective-permute-start.3 = (bf16[512,4096]{1,0:T(8,128)(2,1)}, bf16[512,4096]{1,0:T(8,128)(2,1)}, u32[]{:S(2)}, u32[]{:S(2)}) collective-permute-start(bf16[512,4096]{1,0:T(8,128)(2,1)} %mine_in.1), channel_id=1, source_target_pairs={{0,1},{1,0},{2,3},{3,2},{4,5},{5,4},{6,7},{7,6},{8,9},{9,8},{10,11... | collective-permute-start | bytes 12582920 | tf_op jit(solution)/shard_map/ppermute | solution.py:481
  3.0 6.6 %copy-start.9 = (s32[4]{0:T(128)S(1)}, s32[4]{0:T(128)}, u32[]{:S(2)}) copy-start(s32[4]{0:T(128)} %constant.13) | copy-start | bytes 52
  3.0 13.0 %collective-permute-start = (bf16[1552,128]{1,0:T(8,128)(2,1)}, bf16[1552,128]{1,0:T(8,128)(2,1)S(1)}, u32[]{:S(2)}, u32[]{:S(2)}) collective-permute-start(bf16[1552,128]{1,0:T(8,128)(2,1)} %get-tuple-element.64), channel_id=1, source_target_pairs={{0,8},{8,0},{16,24},{24,16},{1,9},{9,1},{17,25},{25,17},{2,10},{10... | collective-permute-start | bytes 1191944 | tf_op jit(solution)/shard_map/ppermute | solution.py:481
  5.4 20.1 %collective-permute-start.1 = (bf16[1552,128]{1,0:T(8,128)(2,1)}, bf16[1552,128]{1,0:T(8,128)(2,1)S(1)}, u32[]{:S(2)}, u32[]{:S(2)}) collective-permute-start(bf16[1552,128]{1,0:T(8,128)(2,1)} %get-tuple-element.65), channel_id=1, source_target_pairs={{0,16},{8,24},{16,0},{24,8},{1,17},{9,25},{17,1},{25,9},{2,18},{10... | collective-permute-start | bytes 1191944 | tf_op jit(solution)/shard_map/ppermute | solution.py:481
  7.0 18.5 %collective-permute-start.2 = (bf16[1552,128]{1,0:T(8,128)(2,1)}, bf16[1552,128]{1,0:T(8,128)(2,1)S(1)}, u32[]{:S(2)}, u32[]{:S(2)}) collective-permute-start(bf16[1552,128]{1,0:T(8,128)(2,1)} %get-tuple-element.66), channel_id=1, source_target_pairs={{0,24},{8,16},{16,8},{24,0},{1,25},{9,17},{17,9},{25,1},{2,26},{10... | collective-permute-start | bytes 1191944 | tf_op jit(solution)/shard_map/ppermute | solution.py:481
  10.0 15.5 %copy-start.8 = (bf16[1536,128]{1,0:T(8,128)(2,1)S(1)}, bf16[1536,128]{1,0:T(8,128)(2,1)}, u32[]{:S(2)}) copy-start(bf16[1536,128]{1,0:T(8,128)(2,1)} %get-tuple-element.80) | copy-start | bytes 1179652
  10.0 16.7 %copy-start.7 = (bf16[1536,128]{1,0:T(8,128)(2,1)S(1)}, bf16[1536,128]{1,0:T(8,128)(2,1)}, u32[]{:S(2)}) copy-start(bf16[1536,128]{1,0:T(8,128)(2,1)} %get-tuple-element.81) | copy-start | bytes 1179652
  10.0 17.6 %copy-start.2 = (bf16[1024,512]{1,0:T(8,128)(2,1)S(1)}, bf16[1024,512]{1,0:T(8,128)(2,1)}, u32[]{:S(2)}) copy-start(bf16[1024,512]{1,0:T(8,128)(2,1)} %refs_3_.4) | copy-start | bytes 3145732
  10.0 17.6 %copy-start.3 = (bf16[1024,512]{1,0:T(8,128)(2,1)S(1)}, bf16[1024,512]{1,0:T(8,128)(2,1)}, u32[]{:S(2)}) copy-start(bf16[1024,512]{1,0:T(8,128)(2,1)} %refs_4_.4) | copy-start | bytes 3145732
  10.0 17.6 %copy-start.4 = (bf16[1024,512]{1,0:T(8,128)(2,1)S(1)}, bf16[1024,512]{1,0:T(8,128)(2,1)}, u32[]{:S(2)}) copy-start(bf16[1024,512]{1,0:T(8,128)(2,1)} %refs_5_.4) | copy-start | bytes 3145732
  10.0 17.6 %copy-start.5 = (s32[1024]{0:T(1024)S(1)}, s32[1024]{0:T(1024)}, u32[]{:S(2)}) copy-start(s32[1024]{0:T(1024)} %param.9) | copy-start | bytes 12292
  25.5 20.1 %copy-start = (bf16[512,2048]{1,0:T(8,128)(2,1)S(1)}, bf16[512,2048]{1,0:T(8,128)(2,1)}, u32[]{:S(2)}) copy-start(bf16[512,2048]{1,0:T(8,128)(2,1)} %get-tuple-element.88.w_mine_ref) | copy-start | bytes 6291460
  25.5 20.1 %copy-start.1 = (bf16[512,2048]{1,0:T(8,128)(2,1)S(1)}, bf16[512,2048]{1,0:T(8,128)(2,1)}, u32[]{:S(2)}) copy-start(bf16[512,2048]{1,0:T(8,128)(2,1)} %get-tuple-element.89.w_sibling_ref) | copy-start | bytes 6291460
  25.5 18.0 %collective-permute-start.7 = (bf16[1536,128]{1,0:T(8,128)(2,1)S(1)}, bf16[1536,128]{1,0:T(8,128)(2,1)S(1)}, u32[]{:S(2)}, u32[]{:S(2)}) collective-permute-start(bf16[1536,128]{1,0:T(8,128)(2,1)S(1)} %copy-done.8), channel_id=1, source_target_pairs={{0,8},{8,0},{16,24},{24,16},{1,9},{9,1},{17,25},{25,17},{2,10},{10... | collective-permute-start | bytes 1179656 | tf_op jit(solution)/shard_map/ppermute | solution.py:481
  26.8 16.8 %collective-permute-start.8 = (bf16[1536,128]{1,0:T(8,128)(2,1)S(1)}, bf16[1536,128]{1,0:T(8,128)(2,1)S(1)}, u32[]{:S(2)}, u32[]{:S(2)}) collective-permute-start(bf16[1536,128]{1,0:T(8,128)(2,1)S(1)} %copy-done.7), channel_id=1, source_target_pairs={{0,16},{8,24},{16,0},{24,8},{1,17},{9,25},{17,1},{25,9},{2,18},{10... | collective-permute-start | bytes 1179656 | tf_op jit(solution)/shard_map/ppermute | solution.py:481
  35.0 6.1 %collective-permute-start.4 = (bf16[512,128]{1,0:T(8,128)(2,1)S(1)}, bf16[512,128]{1,0:T(8,128)(2,1)S(1)}, u32[]{:S(2)}, u32[]{:S(2)}) collective-permute-start(bf16[512,128]{1,0:T(8,128)(2,1)S(1)} %get-tuple-element.77), channel_id=1, source_target_pairs={{0,8},{8,0},{16,24},{24,16},{1,9},{9,1},{17,25},{25,17},{2,10},{10... | collective-permute-start | bytes 393224 | tf_op jit(solution)/shard_map/ppermute | solution.py:481
  36.5 7.0 %collective-permute-start.5 = (bf16[512,128]{1,0:T(8,128)(2,1)S(1)}, bf16[512,128]{1,0:T(8,128)(2,1)S(1)}, u32[]{:S(2)}, u32[]{:S(2)}) collective-permute-start(bf16[512,128]{1,0:T(8,128)(2,1)S(1)} %get-tuple-element.78), channel_id=1, source_target_pairs={{0,16},{8,24},{16,0},{24,8},{1,17},{9,25},{17,1},{25,9},{2,18},{10... | collective-permute-start | bytes 393224 | tf_op jit(solution)/shard_map/ppermute | solution.py:481
  37.0 6.5 %collective-permute-start.6 = (bf16[512,128]{1,0:T(8,128)(2,1)S(1)}, bf16[512,128]{1,0:T(8,128)(2,1)S(1)}, u32[]{:S(2)}, u32[]{:S(2)}) collective-permute-start(bf16[512,128]{1,0:T(8,128)(2,1)S(1)} %get-tuple-element.79), channel_id=1, source_target_pairs={{0,24},{8,16},{16,8},{24,0},{1,25},{9,17},{17,9},{25,1},{2,26},{10... | collective-permute-start | bytes 393224 | tf_op jit(solution)/shard_map/ppermute | solution.py:481
  43.6 4.4 %copy-start.6 = (bf16[1536,128]{1,0:T(8,128)(2,1)S(1)}, bf16[1536,128]{1,0:T(8,128)(2,1)}, u32[]{:S(2)}) copy-start(bf16[1536,128]{1,0:T(8,128)(2,1)} %get-tuple-element.90) | copy-start | bytes 1179652
  43.7 2.0 %collective-permute-start.9 = (bf16[512,512]{1,0:T(8,128)(2,1)S(1)}, bf16[512,512]{1,0:T(8,128)(2,1)S(1)}, u32[]{:S(2)}, u32[]{:S(2)}) collective-permute-start(bf16[512,512]{1,0:T(8,128)(2,1)S(1)} %assemble.2.mine_ref), channel_id=1, source_target_pairs={{0,1},{1,0},{2,3},{3,2},{4,5},{5,4},{6,7},{7,6},{8,9},{9,8},{10,11... | collective-permute-start | bytes 1572872 | tf_op jit(solution)/shard_map/ppermute | solution.py:481
  46.4 15.3 %collective-permute-start.11 = (bf16[512,512]{1,0:T(8,128)(2,1)S(1)}, bf16[512,512]{1,0:T(8,128)(2,1)S(1)}, u32[]{:S(2)}, u32[]{:S(2)}) collective-permute-start(bf16[512,512]{1,0:T(8,128)(2,1)S(1)} %project.9), channel_id=1, source_target_pairs={{0,2},{1,3},{2,0},{3,1},{4,6},{5,7},{6,4},{7,5},{8,10},{9,11},{10,... | collective-permute-start | bytes 1572872 | tf_op jit(solution)/shard_map/ppermute | solution.py:481
  48.0 11.8 %collective-permute-start.10 = (bf16[1536,128]{1,0:T(8,128)(2,1)S(1)}, bf16[1536,128]{1,0:T(8,128)(2,1)S(1)}, u32[]{:S(2)}, u32[]{:S(2)}) collective-permute-start(bf16[1536,128]{1,0:T(8,128)(2,1)S(1)} %copy-done.6), channel_id=1, source_target_pairs={{0,24},{8,16},{16,8},{24,0},{1,25},{9,17},{17,9},{25,1},{2,26},{10... | collective-permute-start | bytes 1179656 | tf_op jit(solution)/shard_map/ppermute | solution.py:481
  59.8 23.4 %collective-permute-start.16 = (bf16[512,512]{1,0:T(8,128)(2,1)S(1)}, bf16[512,512]{1,0:T(8,128)(2,1)S(1)}, u32[]{:S(2)}, u32[]{:S(2)}) collective-permute-start(bf16[512,512]{1,0:T(8,128)(2,1)S(1)} %project.8), channel_id=1, source_target_pairs={{0,2},{1,3},{2,0},{3,1},{4,6},{5,7},{6,4},{7,5},{8,10},{9,11},{10,... | collective-permute-start | bytes 1572872 | tf_op jit(solution)/shard_map/ppermute | solution.py:481
  61.8 24.8 %collective-permute-start.15 = (bf16[512,512]{1,0:T(8,128)(2,1)S(1)}, bf16[512,512]{1,0:T(8,128)(2,1)S(1)}, u32[]{:S(2)}, u32[]{:S(2)}) collective-permute-start(bf16[512,512]{1,0:T(8,128)(2,1)S(1)} %add_convert_fusion.3), channel_id=1, source_target_pairs={{0,4},{1,5},{2,6},{3,7},{4,0},{5,1},{6,2},{7,3},{8,12},{9,13},{10,... | collective-permute-start | bytes 1572872 | tf_op jit(solution)/shard_map/ppermute | solution.py:481
  70.7 5.9 %collective-permute-start.12 = (bf16[512,128]{1,0:T(8,128)(2,1)S(1)}, bf16[512,128]{1,0:T(8,128)(2,1)S(1)}, u32[]{:S(2)}, u32[]{:S(2)}) collective-permute-start(bf16[512,128]{1,0:T(8,128)(2,1)S(1)} %get-tuple-element.98), channel_id=1, source_target_pairs={{0,8},{8,0},{16,24},{24,16},{1,9},{9,1},{17,25},{25,17},{2,10},{10... | collective-permute-start | bytes 393224 | tf_op jit(solution)/shard_map/ppermute | solution.py:481
  71.8 5.1 %collective-permute-start.13 = (bf16[512,128]{1,0:T(8,128)(2,1)S(1)}, bf16[512,128]{1,0:T(8,128)(2,1)S(1)}, u32[]{:S(2)}, u32[]{:S(2)}) collective-permute-start(bf16[512,128]{1,0:T(8,128)(2,1)S(1)} %get-tuple-element.99), channel_id=1, source_target_pairs={{0,16},{8,24},{16,0},{24,8},{1,17},{9,25},{17,1},{25,9},{2,18},{10... | collective-permute-start | bytes 393224 | tf_op jit(solution)/shard_map/ppermute | solution.py:481
  72.5 5.9 %collective-permute-start.14 = (bf16[512,128]{1,0:T(8,128)(2,1)S(1)}, bf16[512,128]{1,0:T(8,128)(2,1)S(1)}, u32[]{:S(2)}, u32[]{:S(2)}) collective-permute-start(bf16[512,128]{1,0:T(8,128)(2,1)S(1)} %get-tuple-element.100), channel_id=1, source_target_pairs={{0,24},{8,16},{16,8},{24,0},{1,25},{9,17},{17,9},{25,1},{2,26},{10... | collective-permute-start | bytes 393224 | tf_op jit(solution)/shard_map/ppermute | solution.py:481
  86.6 1.9 %collective-permute-start.17 = (bf16[512,512]{1,0:T(8,128)(2,1)S(1)}, bf16[512,512]{1,0:T(8,128)(2,1)S(1)}, u32[]{:S(2)}, u32[]{:S(2)}) collective-permute-start(bf16[512,512]{1,0:T(8,128)(2,1)S(1)} %assemble.3.mine_ref), channel_id=1, source_target_pairs={{0,1},{1,0},{2,3},{3,2},{4,5},{5,4},{6,7},{7,6},{8,9},{9,8},{10,11... | collective-permute-start | bytes 1572872 | tf_op jit(solution)/shard_map/ppermute | solution.py:481
  89.2 14.8 %collective-permute-start.19 = (bf16[512,512]{1,0:T(8,128)(2,1)S(1)}, bf16[512,512]{1,0:T(8,128)(2,1)S(1)}, u32[]{:S(2)}, u32[]{:S(2)}) collective-permute-start(bf16[512,512]{1,0:T(8,128)(2,1)S(1)} %project.15), channel_id=1, source_target_pairs={{0,2},{1,3},{2,0},{3,1},{4,6},{5,7},{6,4},{7,5},{8,10},{9,11},{10,... | collective-permute-start | bytes 1572872 | tf_op jit(solution)/shard_map/ppermute | solution.py:481
  90.8 33.7 %collective-permute-start.18 = (bf16[512,512]{1,0:T(8,128)(2,1)S(1)}, bf16[512,512]{1,0:T(8,128)(2,1)S(1)}, u32[]{:S(2)}, u32[]{:S(2)}) collective-permute-start(bf16[512,512]{1,0:T(8,128)(2,1)S(1)} %project.13), channel_id=1, source_target_pairs={{0,2},{1,3},{2,0},{3,1},{4,6},{5,7},{6,4},{7,5},{8,10},{9,11},{10,... | collective-permute-start | bytes 1572872 | tf_op jit(solution)/shard_map/ppermute | solution.py:481
  104.2 24.7 %collective-permute-start.20 = (bf16[512,512]{1,0:T(8,128)(2,1)S(1)}, bf16[512,512]{1,0:T(8,128)(2,1)S(1)}, u32[]{:S(2)}, u32[]{:S(2)}) collective-permute-start(bf16[512,512]{1,0:T(8,128)(2,1)S(1)} %add_convert_fusion.1), channel_id=1, source_target_pairs={{0,4},{1,5},{2,6},{3,7},{4,0},{5,1},{6,2},{7,3},{8,12},{9,13},{10,... | collective-permute-start | bytes 1572872 | tf_op jit(solution)/shard_map/ppermute | solution.py:481

commit v12 on v11

--- a/solution.py
+++ b/solution.py
@@ -164,37 +164,27 @@
     return pl.BlockSpec(shape, lambda step, scalars: (0,) * len(shape))
 
 
-def pack(ctx_index, half, queries, keys, values, docs):
+def pack(ctx_index, distance, half, queries, keys, values, docs):
     rows = queries.shape[0] // 2
-    group = queries.shape[1] // HD
     doc_rows = 0 if docs is None else 16 * pl.cdiv(docs.shape[0], 16)
     total = 3 * rows + doc_rows
 
     def kernel(ctx_ref, *refs):
-        outs = refs[len(refs) - (group - 1) :]
+        out = refs[-1]
+        for part in range(2):
+            out[part * rows : (part + 1) * rows, :] = refs[part][...]
+        for block in range(rows // HD):
+            taken = refs[2][block * HD : (block + 1) * HD, :]
+            lower = 2 * rows + block * HD
+            out[lower : lower + HD, :] = jnp.transpose(taken)
         if docs is not None:
-            mine = refs[3 * (group - 1)][...].astype(jnp.float32)
+            mine = refs[3][...].astype(jnp.float32)
             empty = jnp.zeros((doc_rows - mine.shape[0], HD), jnp.float32)
-            mine = jnp.concatenate([mine, empty], axis=0).astype(jnp.bfloat16)
-        for place in range(group - 1):
-            for part in range(2):
-                outs[place][part * rows : (part + 1) * rows, :] = refs[place * 3 + part][...]
-            for block in range(rows // HD):
-                taken = refs[place * 3 + 2][block * HD : (block + 1) * HD, :]
-                lower = 2 * rows + block * HD
-                outs[place][lower : lower + HD, :] = jnp.transpose(taken)
-            if docs is not None:
-                outs[place][3 * rows :, :] = mine
-
-    def piece(distance):
-        return pl.BlockSpec((rows, HD), lambda step, ctx: (half, ctx[0] ^ distance))
-
-    in_specs = []
-    operands = []
-    for distance in range(1, group):
-        for array in (queries, keys, values):
-            in_specs.append(piece(distance))
-            operands.append(array)
+            out[3 * rows :, :] = jnp.concatenate([mine, empty], axis=0).astype(jnp.bfloat16)
+
+    piece = pl.BlockSpec((rows, HD), lambda step, ctx: (half, ctx[0] ^ distance))
+    in_specs = [piece] * 3
+    operands = [queries, keys, values]
     if docs is not None:
         in_specs.append(whole(docs.shape))
         operands.append(docs)
@@ -204,9 +194,9 @@
             num_scalar_prefetch=1,
             grid=(1,),
             in_specs=in_specs,
-            out_specs=[whole((total, HD))] * (group - 1),
+            out_specs=whole((total, HD)),
         ),
-        out_shape=[jax.ShapeDtypeStruct((total, HD), jnp.bfloat16)] * (group - 1),
+        out_shape=jax.ShapeDtypeStruct((total, HD), jnp.bfloat16),
         compiler_params=params(56),
         cost_estimate=SMALL,
         name="pack",
@@ -429,14 +419,17 @@
     )(ctx_index, *operands)
 
 
-def assemble(ctx_index, pieces):
+def assemble(ctx_index, pieces, parts):
     rows = pieces[0].shape[0]
     group = len(pieces)
+    part_rows = rows // parts
 
     def kernel(ctx_ref, *refs):
-        for distance in range(group):
-            column = pl.multiple_of((ctx_ref[0] ^ distance) * HD, HD)
-            refs[-1][:, pl.ds(column, HD)] = refs[distance][...]
+        for part in range(parts):
+            for distance in range(group):
+                column = pl.multiple_of((ctx_ref[0] ^ distance) * HD, HD)
+                taken = refs[distance][part * part_rows : (part + 1) * part_rows, :]
+                refs[group + part][:, pl.ds(column, HD)] = taken
 
     return pl.pallas_call(
         kernel,
@@ -444,9 +437,9 @@
             num_scalar_prefetch=1,
             grid=(1,),
             in_specs=[whole((rows, HD))] * group,
-            out_specs=whole((rows, group * HD)),
+            out_specs=[whole((part_rows, group * HD))] * parts,
         ),
-        out_shape=jax.ShapeDtypeStruct((rows, group * HD), jnp.bfloat16),
+        out_shape=[jax.ShapeDtypeStruct((part_rows, group * HD), jnp.bfloat16)] * parts,
         compiler_params=params(16),
         cost_estimate=SMALL,
         name="assemble",
@@ -454,26 +447,60 @@
 
 
 def project(turn, mine, sibling, w_mine, w_sibling):
-    rows, depth = mine.shape
+    parts = len(mine)
+    rows, depth = mine[0].shape
     columns = w_mine.shape[1] // len(TURNS)
 
-    def kernel(mine_ref, sibling_ref, w_mine_ref, w_sibling_ref, out_ref):
-        total = jnp.dot(mine_ref[...], w_mine_ref[...], preferred_element_type=jnp.float32)
-        total += jnp.dot(sibling_ref[...], w_sibling_ref[...], preferred_element_type=jnp.float32)
-        out_ref[...] = total.astype(jnp.bfloat16)
+    def kernel(*refs):
+        w_mine_ref, w_sibling_ref, out_ref = refs[2 * parts :]
+        for part in range(parts):
+            total = jnp.dot(refs[part][...], w_mine_ref[...], preferred_element_type=jnp.float32)
+            total += jnp.dot(
+                refs[parts + part][...], w_sibling_ref[...], preferred_element_type=jnp.float32
+            )
+            out_ref[part * rows : (part + 1) * rows, :] = total.astype(jnp.bfloat16)
 
     weights = pl.BlockSpec((depth, columns), lambda step: (0, turn))
     attended = pl.BlockSpec((rows, depth), lambda step: (0, 0))
     return pl.pallas_call(
         kernel,
         grid=(1,),
-        in_specs=[attended, attended, weights, weights],
-        out_specs=pl.BlockSpec((rows, columns), lambda step: (0, 0)),
-        out_shape=jax.ShapeDtypeStruct((rows, columns), jnp.bfloat16),
+        in_specs=[attended] * (2 * parts) + [weights] * 2,
+        out_specs=pl.BlockSpec((parts * rows, columns), lambda step: (0, 0)),
+        out_shape=jax.ShapeDtypeStruct((parts * rows, columns), jnp.bfloat16),
         compiler_params=params(16),
         cost_estimate=SMALL,
         name="project",
-    )(mine, sibling, w_mine, w_sibling)
+    )(*mine, *sibling, w_mine, w_sibling)
+
+
+def finish(half, terms, result):
+    rows, columns = terms[0].shape
+
+    def kernel(*refs):
+        total = refs[0][...].astype(jnp.float32)
+        for ref in refs[1 : len(terms)]:
+            total += ref[...].astype(jnp.float32)
+        refs[-1][...] = total.astype(jnp.bfloat16)
+
+    in_specs = [pl.BlockSpec((rows, columns), lambda step: (0, 0))] * len(terms)
+    operands = list(terms)
+    aliases = {}
+    if result is not None:
+        in_specs.append(pl.BlockSpec(memory_space=pl.ANY))
+        operands.append(result)
+        aliases = {len(terms): 0}
+    return pl.pallas_call(
+        kernel,
+        grid=(1,),
+        in_specs=in_specs,
+        out_specs=pl.BlockSpec((rows, columns), lambda step: (half, 0)),
+        out_shape=jax.ShapeDtypeStruct((2 * rows, columns), jnp.bfloat16),
+        input_output_aliases=aliases,
+        compiler_params=params(16),
+        cost_estimate=SMALL,
+        name="finish",
+    )(*operands)
 
 
 def swap(value, axis, distance):
@@ -505,47 +532,55 @@
     near = range(1, group)
 
     w_sibling = swap(w_out, "head", 1)
-    low_out = pack(ctx_index, 0, queries, keys, values, docs)
-    low_out, later = tie(low_out, (queries, keys, values))
-    low = [swap(low_out[distance - 1], "ctx", distance) for distance in near]
-    high_out = pack(ctx_index, 1, *later, None)
+
+    def exchange(half, distance, arrays):
+        packed = pack(ctx_index, distance, half, *arrays, None if half else docs)
+        return packed, swap(packed, "ctx", distance)
+
+    low = {}
+    arrays = (queries, keys, values)
+    for distance in (3, 1, 2):
+        packed, low[distance] = exchange(0, distance, arrays)
+        packed, arrays = tie(packed, arrays)
+    high_out = {}
+    high = {}
+    for distance in (1, 2):
+        high_out[distance], high[distance] = exchange(1, distance, arrays)
+    low = [low[distance] for distance in near]
+    diagonal_out = pack(ctx_index, 3, 1, *arrays, None)
     w_packed = pack_projection(places, w_out, w_sibling)
-    high_out, low, w_packed = tie(high_out, low, w_packed)
-    high = [swap(high_out[0], "ctx", 1), swap(high_out[1], "ctx", 2)]
+    low, w_packed, diagonal_out = tie(low, w_packed, diagonal_out)
 
     def send_back(pieces):
         return [swap(pieces[distance], "ctx", distance) for distance in near]
 
-    def share_of(mine, sibling, turn):
-        return project(turn, mine, sibling, *w_packed)
+    def shares_of(mine, sibling):
+        return [project(turn, mine, sibling, *w_packed) for turn in range(len(TURNS))]
 
     pieces = attend(ctx_index, queries, keys, values, docs, low, None)
-    pieces, diagonal_out = tie(pieces, high_out[2])
+    pieces, diagonal_out = tie(pieces, diagonal_out)
     back = send_back(pieces)
     back, high = tie(back, high)
-    high.append(swap(diagonal_out, "ctx", 3))
-    mine = assemble(ctx_index, [pieces[0], *back])
-    sibling = swap(mine, "head", 1)
-    shares = [share_of(mine, sibling, turn) for turn in range(len(TURNS))]
+    high = [high[1], high[2], swap(diagonal_out, "ctx", 3)]
+    mine = assemble(ctx_index, [pieces[0], *back], 1)
+    shares = shares_of(mine, [swap(mine[0], "head", 1)])
     far = swap(shares[0], "head", 2)
-    shares[1], high[2] = tie(shares[1], high[2])
     near_sum = swap(shares[1], "head", 2)
 
-    passed = add(shares[2], far)
-    high, shares, passed = tie(high, shares, passed)
-    across = swap(passed, "head", 4)
+    high, shares = tie(high, shares)
     pieces = attend(ctx_index, queries, keys, values, docs, low, high)
     back = send_back(pieces)
-    mine = assemble(ctx_index, [pieces[0], *back])
-    mine, across, near_sum = tie(mine, across, near_sum)
-    first = add(shares[3], near_sum, across)
-    sibling = swap(mine, "head", 1)
-    late = [share_of(mine, sibling, turn) for turn in range(len(TURNS))]
+    pieces, passed = tie(pieces, add(shares[2], far))
+    across = swap(passed, "head", 4)
+    back, near_sum = tie(back, near_sum)
+    mine = assemble(ctx_index, [pieces[0], *back], 2)
+    late = shares_of(mine, [swap(part, "head", 1) for part in mine])
+    late[0], across = tie(late[0], across)
+    result = finish(0, [shares[3], near_sum, across], None)
     far = swap(late[0], "head", 2)
     near_sum = swap(late[1], "head", 2)
     across = swap(add(late[2], far), "head", 4)
-    second = add(late[3], near_sum, across)
-    return jnp.concatenate([first, second], axis=0)
+    return finish(1, [late[3], near_sum, across], result)
 
 
 def solution(mesh):

time: 130 us -> 133 us (1.023)
  Pallas kernels: 30.3 us -> 38.4 us
  waiting for transfers between devices: 73.3 us -> 68.8 us
  other arithmetic: 2.24 us -> 0.79 us
    pallas_call x2 -> x6, Pallas kernels: 5.03 us -> 11.3 us  [pack(): pl.pallas_call(kernel, grid_spec=pltpu.PrefetchScalarGridSpec(num_scalar_...]
    ppermute x21 -> x22, waiting for transfers between devices: 73.3 us -> 68.8 us  [swap(): lax.ppermute(value, axis, [(source, source ^ distance) for source in rang...]
    pallas_call x8 -> x10, Pallas kernels: 5.69 us -> 7.66 us  [the longest x8 5.69 us: project(): pl.pallas_call(kernel, grid=(1,), in_specs=[attended] * (2 * parts) + [we...]
    ppermute x21 -> x22, starting transfers between devices: 24.1 us -> 25.2 us  [swap(): lax.ppermute(value, axis, [(source, source ^ distance) for source in rang...]
  transfers between devices with their start and end apart: 21 -> 22, of which waited for: 14 -> 14; matrix products, arithmetic and copies ran while one was open for 1% -> 1% of each run, Pallas kernels for 22% -> 27%
where the time goes in v12:
time: 133 us
  waiting for transfers between devices  68.8 us (52%)
  Pallas kernels  38.4 us (29%)
  starting transfers between devices  25.2 us (19%)
    ppermute x22, waiting for transfers between devices, swap(): lax.ppermute(value, axis, [(source, source ^ distance) for source in rang...  68.8 us
    ppermute x22, starting transfers between devices, swap(): lax.ppermute(value, axis, [(source, source ^ distance) for source in rang...  25.2 us
    pallas_call x2, Pallas kernels, attend(): pl.pallas_call(kernel, grid_spec=pltpu.PrefetchScalarGridSpec(num_scalar_...  13.5 us
    pallas_call x6, Pallas kernels, pack(): pl.pallas_call(kernel, grid_spec=pltpu.PrefetchScalarGridSpec(num_scalar_...  11.3 us
    pallas_call x1, Pallas kernels, pack_projection(): pl.pallas_call(kernel, grid_spec=pltpu.PrefetchScalarGridSpec(num_scalar_...  5.71 us
    pallas_call x8, Pallas kernels, project(): pl.pallas_call(kernel, grid=(1,), in_specs=[attended] * (2 * parts) + [we...  5.69 us
  transfers between devices with their start and end apart: 22, of which 14 were waited for; matrix products, arithmetic and copies ran while one was open for 1% of the time, Pallas kernels for 27%

profile of v12, /device:TPU:0, one launch (start us, length us, event | category | flops | bytes accessed | tf_op | source)
XLA Modules:
  0.0 133.4 jit_solution(18362233186549808469)
XLA Ops:
  0.0 0.5 collective-permute-start.3
  0.5 1.9 %pack.6 = bf16[1552,128]{1,0:T(8,128)(2,1)} custom-call(s32[1]{0:T(128)} %bitcast.ctx_ref, bf16[1024,512]{1,0:T(8,128)(2,1)} %refs_3_.1, bf16[1024,512]{1,0:T(8,128)(2,1)} %refs_4_.1, bf16[1024,512]{1,0:T(8,128)(2,1)} %refs_5_.1, s32[8,128]{1,0:T(8,128)} %bitcast.2), custom_call_target="tpu_custom_call" | custom-call | flops 1024 | bytes 1024 | tf_op jit(solution)/shard_map/pack/pallas_call | solution.py:191
  2.3 1.9 %pack.7 = bf16[1552,128]{1,0:T(8,128)(2,1)} custom-call(s32[1]{0:T(128)} %bitcast.ctx_ref, bf16[1024,512]{1,0:T(8,128)(2,1)} %refs_3_.1, bf16[1024,512]{1,0:T(8,128)(2,1)} %refs_4_.1, bf16[1024,512]{1,0:T(8,128)(2,1)} %refs_5_.1, s32[8,128]{1,0:T(8,128)} %bitcast.3), custom_call_target="tpu_custom_call" | custom-call | flops 1024 | bytes 1024 | tf_op jit(solution)/shard_map/pack/pallas_call | solution.py:191
  4.3 2.5 %collective-permute-start = (bf16[1552,128]{1,0:T(8,128)(2,1)}, bf16[1552,128]{1,0:T(8,128)(2,1)S(1)}, u32[]{:S(2)}, u32[]{:S(2)}) collective-permute-start(bf16[1552,128]{1,0:T(8,128)(2,1)} %pack.7), channel_id=1, source_target_pairs={{0,8},{8,0},{16,24},{24,16},{1,9},{9,1},{17,25},{25,17},{2,10},{10... | collective-permute-start | bytes 1191944 | tf_op jit(solution)/shard_map/ppermute | solution.py:508
  6.8 1.9 %pack.8 = bf16[1552,128]{1,0:T(8,128)(2,1)} custom-call(s32[1]{0:T(128)} %bitcast.ctx_ref, bf16[1024,512]{1,0:T(8,128)(2,1)} %refs_3_.1, bf16[1024,512]{1,0:T(8,128)(2,1)} %refs_4_.1, bf16[1024,512]{1,0:T(8,128)(2,1)} %refs_5_.1, s32[8,128]{1,0:T(8,128)} %bitcast.4), custom_call_target="tpu_custom_call" | custom-call | flops 1024 | bytes 1024 | tf_op jit(solution)/shard_map/pack/pallas_call | solution.py:191
  8.7 1.5 %collective-permute-start.1 = (bf16[1552,128]{1,0:T(8,128)(2,1)}, bf16[1552,128]{1,0:T(8,128)(2,1)S(1)}, u32[]{:S(2)}, u32[]{:S(2)}) collective-permute-start(bf16[1552,128]{1,0:T(8,128)(2,1)} %pack.8), channel_id=1, source_target_pairs={{0,16},{8,24},{16,0},{24,8},{1,17},{9,25},{17,1},{25,9},{2,18},{10... | collective-permute-start | bytes 1191944 | tf_op jit(solution)/shard_map/ppermute | solution.py:508
  10.2 0.0 collective-permute-start.2
  10.2 1.9 %pack.10 = bf16[1536,128]{1,0:T(8,128)(2,1)} custom-call(s32[1]{0:T(128)} %bitcast.ctx_ref, bf16[1024,512]{1,0:T(8,128)(2,1)} %refs_3_.1, bf16[1024,512]{1,0:T(8,128)(2,1)} %refs_4_.1, bf16[1024,512]{1,0:T(8,128)(2,1)} %refs_5_.1), custom_call_target="tpu_custom_call" | custom-call | flops 1024 | bytes 1024 | tf_op jit(solution)/shard_map/pack/pallas_call | solution.py:191
  12.1 1.9 %collective-permute-start.7 = (bf16[1536,128]{1,0:T(8,128)(2,1)}, bf16[1536,128]{1,0:T(8,128)(2,1)S(1)}, u32[]{:S(2)}, u32[]{:S(2)}) collective-permute-start(bf16[1536,128]{1,0:T(8,128)(2,1)} %pack.10), channel_id=1, source_target_pairs={{0,8},{8,0},{16,24},{24,16},{1,9},{9,1},{17,25},{25,17},{2,10},{10... | collective-permute-start | bytes 1179656 | tf_op jit(solution)/shard_map/ppermute | solution.py:508
  14.0 1.9 %pack.11 = bf16[1536,128]{1,0:T(8,128)(2,1)} custom-call(s32[1]{0:T(128)} %bitcast.ctx_ref, bf16[1024,512]{1,0:T(8,128)(2,1)} %refs_3_.1, bf16[1024,512]{1,0:T(8,128)(2,1)} %refs_4_.1, bf16[1024,512]{1,0:T(8,128)(2,1)} %refs_5_.1), custom_call_target="tpu_custom_call" | custom-call | flops 1024 | bytes 1024 | tf_op jit(solution)/shard_map/pack/pallas_call | solution.py:191
  15.9 0.0 collective-permute-done.3.sibling_in
  15.9 1.5 %collective-permute-start.8 = (bf16[1536,128]{1,0:T(8,128)(2,1)}, bf16[1536,128]{1,0:T(8,128)(2,1)S(1)}, u32[]{:S(2)}, u32[]{:S(2)}) collective-permute-start(bf16[1536,128]{1,0:T(8,128)(2,1)} %pack.11), channel_id=1, source_target_pairs={{0,16},{8,24},{16,0},{24,8},{1,17},{9,25},{17,1},{25,9},{2,18},{10... | collective-permute-start | bytes 1179656 | tf_op jit(solution)/shard_map/ppermute | solution.py:508
  17.4 0.5 broadcast_xor_fusion.places_ref
  17.9 1.9 %pack.9 = bf16[1536,128]{1,0:T(8,128)(2,1)} custom-call(s32[1]{0:T(128)} %bitcast.ctx_ref, bf16[1024,512]{1,0:T(8,128)(2,1)} %refs_3_.1, bf16[1024,512]{1,0:T(8,128)(2,1)} %refs_4_.1, bf16[1024,512]{1,0:T(8,128)(2,1)} %refs_5_.1), custom_call_target="tpu_custom_call" | custom-call | flops 1024 | bytes 1024 | tf_op jit(solution)/shard_map/pack/pallas_call | solution.py:191
  19.8 5.7 %pack_projection.1 = (bf16[512,2048]{1,0:T(8,128)(2,1)}, bf16[512,2048]{1,0:T(8,128)(2,1)}) custom-call(s32[4]{0:T(128)} %broadcast_xor_fusion.places_ref, bf16[512,4096]{1,0:T(8,128)(2,1)} %mine_in.1, bf16[512,4096]{1,0:T(8,128)(2,1)} %collective-permute-done.3.sibling_in), custom_call_target="tpu_custom_call" | custom-call | flops 1024 | bytes 1024 | tf_op jit(solution)/shard_map/pack_projection/pallas_call | solution.py:217
  25.6 3.9 %collective-permute-done.1.refs_5_.refs_8_ = bf16[1552,128]{1,0:T(8,128)(2,1)S(1)} collective-permute-done((bf16[1552,128]{1,0:T(8,128)(2,1)}, bf16[1552,128]{1,0:T(8,128)(2,1)S(1)}, u32[]{:S(2)}, u32[]{:S(2)}) %collective-permute-start.1) | collective-permute-done | bytes 397344 | tf_op jit(solution)/shard_map/ppermute | solution.py:508
  29.4 0.0 collective-permute-done.2.refs_6_.refs_9_
  29.5 7.3 %attend_low.1 = (bf16[512,128]{1,0:T(8,128)(2,1)S(1)}, bf16[512,128]{1,0:T(8,128)(2,1)S(1)}, bf16[512,128]{1,0:T(8,128)(2,1)S(1)}, bf16[512,128]{1,0:T(8,128)(2,1)S(1)}) custom-call(s32[1]{0:T(128)} %bitcast.ctx_ref, bf16[1024,512]{1,0:T(8,128)(2,1)S(1)} %copy-done.2, bf16[1024,512]{1,0:T(8,128)(2,1)S(1)} %copy-done.3, bf16[1024,512]{1,0:T(8,128)(2,1)S(1)} %copy-done.4, ...), custom_call_target="tpu_custom_call" | custom-call | flops 1024 | bytes 1024 | tf_op jit(solution)/shard_map/attend_low/pallas_call | solution.py:399
  36.8 0.1 collective-permute-start.4
  36.8 2.1 %collective-permute-start.5 = (bf16[512,128]{1,0:T(8,128)(2,1)S(1)}, bf16[512,128]{1,0:T(8,128)(2,1)S(1)}, u32[]{:S(2)}, u32[]{:S(2)}) collective-permute-start(bf16[512,128]{1,0:T(8,128)(2,1)S(1)} %get-tuple-element.75), channel_id=1, source_target_pairs={{0,16},{8,24},{16,0},{24,8},{1,17},{9,25},{17,1},{25,9},{2,18},{10... | collective-permute-start | bytes 393224 | tf_op jit(solution)/shard_map/ppermute | solution.py:508
  38.9 1.4 %collective-permute-start.6 = (bf16[512,128]{1,0:T(8,128)(2,1)S(1)}, bf16[512,128]{1,0:T(8,128)(2,1)S(1)}, u32[]{:S(2)}, u32[]{:S(2)}) collective-permute-start(bf16[512,128]{1,0:T(8,128)(2,1)S(1)} %get-tuple-element.76), channel_id=1, source_target_pairs={{0,24},{8,16},{16,8},{24,0},{1,25},{9,17},{17,9},{25,1},{2,26},{10... | collective-permute-start | bytes 393224 | tf_op jit(solution)/shard_map/ppermute | solution.py:508
  40.3 0.0 collective-permute-done.7.refs_10_
  40.3 0.0 collective-permute-done.8.refs_11_
  40.3 2.2 %collective-permute-done.4.refs_1_ = bf16[512,128]{1,0:T(8,128)(2,1)S(1)} collective-permute-done((bf16[512,128]{1,0:T(8,128)(2,1)S(1)}, bf16[512,128]{1,0:T(8,128)(2,1)S(1)}, u32[]{:S(2)}, u32[]{:S(2)}) %collective-permute-start.4) | collective-permute-done | bytes 131104 | tf_op jit(solution)/shard_map/ppermute | solution.py:508
  42.5 0.8 collective-permute-done.5.refs_2_
  43.3 1.5 %collective-permute-done.6.refs_3_ = bf16[512,128]{1,0:T(8,128)(2,1)S(1)} collective-permute-done((bf16[512,128]{1,0:T(8,128)(2,1)S(1)}, bf16[512,128]{1,0:T(8,128)(2,1)S(1)}, u32[]{:S(2)}, u32[]{:S(2)}) %collective-permute-start.6) | collective-permute-done | bytes 131104 | tf_op jit(solution)/shard_map/ppermute | solution.py:508
  44.8 0.1 assemble.2.refs_0_
  44.9 0.1 collective-permute-start.10
  44.9 1.9 %collective-permute-done.10.refs_1_ = bf16[512,512]{1,0:T(8,128)(2,1)S(1)} collective-permute-done((bf16[512,512]{1,0:T(8,128)(2,1)S(1)}, bf16[512,512]{1,0:T(8,128)(2,1)S(1)}, u32[]{:S(2)}, u32[]{:S(2)}) %collective-permute-start.10) | collective-permute-done | bytes 524320 | tf_op jit(solution)/shard_map/ppermute | solution.py:508
  46.8 0.7 project.8
  47.6 1.6 %collective-permute-start.11 = (bf16[512,512]{1,0:T(8,128)(2,1)S(1)}, bf16[512,512]{1,0:T(8,128)(2,1)S(1)}, u32[]{:S(2)}, u32[]{:S(2)}) collective-permute-start(bf16[512,512]{1,0:T(8,128)(2,1)S(1)} %project.8), channel_id=1, source_target_pairs={{0,2},{1,3},{2,0},{3,1},{4,6},{5,7},{6,4},{7,5},{8,10},{9,11},{10,... | collective-permute-start | bytes 1572872 | tf_op jit(solution)/shard_map/ppermute | solution.py:508
  49.2 2.1 %collective-permute-start.9 = (bf16[1536,128]{1,0:T(8,128)(2,1)S(1)}, bf16[1536,128]{1,0:T(8,128)(2,1)S(1)}, u32[]{:S(2)}, u32[]{:S(2)}) collective-permute-start(bf16[1536,128]{1,0:T(8,128)(2,1)S(1)} %copy-done.7), channel_id=1, source_target_pairs={{0,24},{8,16},{16,8},{24,0},{1,25},{9,17},{17,9},{25,1},{2,26},{10... | collective-permute-start | bytes 1179656 | tf_op jit(solution)/shard_map/ppermute | solution.py:508
  51.3 0.7 project.9
  52.1 0.5 collective-permute-start.15
  52.5 0.7 project.10
  53.3 0.7 project.11.refs_0_
  54.0 7.0 %collective-permute-done.9.refs_12_ = bf16[1536,128]{1,0:T(8,128)(2,1)S(1)} collective-permute-done((bf16[1536,128]{1,0:T(8,128)(2,1)S(1)}, bf16[1536,128]{1,0:T(8,128)(2,1)S(1)}, u32[]{:S(2)}, u32[]{:S(2)}) %collective-permute-start.9) | collective-permute-done | bytes 393248 | tf_op jit(solution)/shard_map/ppermute | solution.py:508
  61.0 6.2 %attend_high.1 = (bf16[512,128]{1,0:T(8,128)(2,1)S(1)}, bf16[512,128]{1,0:T(8,128)(2,1)S(1)}, bf16[512,128]{1,0:T(8,128)(2,1)S(1)}, bf16[512,128]{1,0:T(8,128)(2,1)S(1)}) custom-call(s32[1]{0:T(128)} %bitcast.ctx_ref, bf16[1024,512]{1,0:T(8,128)(2,1)S(1)} %copy-done.2, bf16[1024,512]{1,0:T(8,128)(2,1)S(1)} %copy-done.3, bf16[1024,512]{1,0:T(8,128)(2,1)S(1)} %copy-done.4, ...), custom_call_target="tpu_custom_call" | custom-call | flops 1024 | bytes 1024 | tf_op jit(solution)/shard_map/attend_high/pallas_call | solution.py:399
  67.2 0.1 add_convert_fusion.1
  67.3 2.7 %collective-permute-start.19 = (bf16[512,512]{1,0:T(8,128)(2,1)S(1)}, bf16[512,512]{1,0:T(8,128)(2,1)S(1)}, u32[]{:S(2)}, u32[]{:S(2)}) collective-permute-start(bf16[512,512]{1,0:T(8,128)(2,1)S(1)} %add_convert_fusion.1), channel_id=1, source_target_pairs={{0,4},{1,5},{2,6},{3,7},{4,0},{5,1},{6,2},{7,3},{8,12},{9,13},{10,... | collective-permute-start | bytes 1572872 | tf_op jit(solution)/shard_map/ppermute | solution.py:508
  70.0 1.7 %collective-permute-start.12 = (bf16[512,128]{1,0:T(8,128)(2,1)S(1)}, bf16[512,128]{1,0:T(8,128)(2,1)S(1)}, u32[]{:S(2)}, u32[]{:S(2)}) collective-permute-start(bf16[512,128]{1,0:T(8,128)(2,1)S(1)} %get-tuple-element.90), channel_id=1, source_target_pairs={{0,8},{8,0},{16,24},{24,16},{1,9},{9,1},{17,25},{25,17},{2,10},{10... | collective-permute-start | bytes 393224 | tf_op jit(solution)/shard_map/ppermute | solution.py:508
  71.6 1.0 collective-permute-start.13
  72.7 0.8 collective-permute-start.14
  73.5 2.6 %collective-permute-done.12.refs_1_ = bf16[512,128]{1,0:T(8,128)(2,1)S(1)} collective-permute-done((bf16[512,128]{1,0:T(8,128)(2,1)S(1)}, bf16[512,128]{1,0:T(8,128)(2,1)S(1)}, u32[]{:S(2)}, u32[]{:S(2)}) %collective-permute-start.12) | collective-permute-done | bytes 131104 | tf_op jit(solution)/shard_map/ppermute | solution.py:508
  76.0 2.9 %collective-permute-done.13.refs_2_ = bf16[512,128]{1,0:T(8,128)(2,1)S(1)} collective-permute-done((bf16[512,128]{1,0:T(8,128)(2,1)S(1)}, bf16[512,128]{1,0:T(8,128)(2,1)S(1)}, u32[]{:S(2)}, u32[]{:S(2)}) %collective-permute-start.13) | collective-permute-done | bytes 131104 | tf_op jit(solution)/shard_map/ppermute | solution.py:508
  78.9 0.1 assemble.3
  79.0 0.1 collective-permute-start.16
  79.1 0.5 collective-permute-start.17
  79.6 1.0 collective-permute-done.16.refs_2_
  80.6 0.4 collective-permute-done.17.refs_3_
  81.0 0.7 project.15
  81.7 10.6 %collective-permute-done.19.refs_2_ = bf16[512,512]{1,0:T(8,128)(2,1)S(1)} collective-permute-done((bf16[512,512]{1,0:T(8,128)(2,1)S(1)}, bf16[512,512]{1,0:T(8,128)(2,1)S(1)}, u32[]{:S(2)}, u32[]{:S(2)}) %collective-permute-start.19) | collective-permute-done | bytes 524320 | tf_op jit(solution)/shard_map/ppermute | solution.py:508
  92.4 0.0 collective-permute-start.20
  92.4 0.7 project.13
  93.1 2.1 %collective-permute-start.18 = (bf16[512,512]{1,0:T(8,128)(2,1)S(1)}, bf16[512,512]{1,0:T(8,128)(2,1)S(1)}, u32[]{:S(2)}, u32[]{:S(2)}) collective-permute-start(bf16[512,512]{1,0:T(8,128)(2,1)S(1)} %project.13), channel_id=1, source_target_pairs={{0,2},{1,3},{2,0},{3,1},{4,6},{5,7},{6,4},{7,5},{8,10},{9,11},{10,... | collective-permute-start | bytes 1572872 | tf_op jit(solution)/shard_map/ppermute | solution.py:508
  95.2 0.7 project.14
  95.9 16.9 %collective-permute-done.20 = bf16[512,512]{1,0:T(8,128)(2,1)S(1)} collective-permute-done((bf16[512,512]{1,0:T(8,128)(2,1)S(1)}, bf16[512,512]{1,0:T(8,128)(2,1)S(1)}, u32[]{:S(2)}, u32[]{:S(2)}) %collective-permute-start.20) | collective-permute-done | bytes 524320 | tf_op jit(solution)/shard_map/ppermute | solution.py:508
  112.8 0.1 add_convert_fusion
  113.0 0.6 collective-permute-start.21
  113.6 0.7 project.12.refs_0_
  114.3 1.0 finish.2.refs_3_
  115.3 6.6 %collective-permute-done.18.refs_1_ = bf16[512,512]{1,0:T(8,128)(2,1)S(1)} collective-permute-done((bf16[512,512]{1,0:T(8,128)(2,1)S(1)}, bf16[512,512]{1,0:T(8,128)(2,1)S(1)}, u32[]{:S(2)}, u32[]{:S(2)}) %collective-permute-start.18) | collective-permute-done | bytes 524320 | tf_op jit(solution)/shard_map/ppermute | solution.py:508
  122.0 10.5 %collective-permute-done.21.refs_2_ = bf16[512,512]{1,0:T(8,128)(2,1)S(1)} collective-permute-done((bf16[512,512]{1,0:T(8,128)(2,1)S(1)}, bf16[512,512]{1,0:T(8,128)(2,1)S(1)}, u32[]{:S(2)}, u32[]{:S(2)}) %collective-permute-start.21) | collective-permute-done | bytes 524320 | tf_op jit(solution)/shard_map/ppermute | solution.py:508
  132.4 1.0 finish.3
  (22 shorter events, 0.0 us)
Async XLA Ops:
  0.0 15.9 %collective-permute-start.3 = (bf16[512,4096]{1,0:T(8,128)(2,1)}, bf16[512,4096]{1,0:T(8,128)(2,1)}, u32[]{:S(2)}, u32[]{:S(2)}) collective-permute-start(bf16[512,4096]{1,0:T(8,128)(2,1)} %mine_in.1), channel_id=1, source_target_pairs={{0,1},{1,0},{2,3},{3,2},{4,5},{5,4},{6,7},{7,6},{8,9},{9,8},{10,11... | collective-permute-start | bytes 12582920 | tf_op jit(solution)/shard_map/ppermute | solution.py:508
  2.3 7.8 %copy-start.6 = (bf16[1552,128]{1,0:T(8,128)(2,1)S(1)}, bf16[1552,128]{1,0:T(8,128)(2,1)}, u32[]{:S(2)}) copy-start(bf16[1552,128]{1,0:T(8,128)(2,1)} %pack.6) | copy-start | bytes 1191940
  4.3 21.3 %collective-permute-start = (bf16[1552,128]{1,0:T(8,128)(2,1)}, bf16[1552,128]{1,0:T(8,128)(2,1)S(1)}, u32[]{:S(2)}, u32[]{:S(2)}) collective-permute-start(bf16[1552,128]{1,0:T(8,128)(2,1)} %pack.7), channel_id=1, source_target_pairs={{0,8},{8,0},{16,24},{24,16},{1,9},{9,1},{17,25},{25,17},{2,10},{10... | collective-permute-start | bytes 1191944 | tf_op jit(solution)/shard_map/ppermute | solution.py:508
  8.7 8.8 %copy-start.8 = (s32[4]{0:T(128)S(1)}, s32[4]{0:T(128)}, u32[]{:S(2)}) copy-start(s32[4]{0:T(128)} %constant.13) | copy-start | bytes 52
  8.7 20.8 %collective-permute-start.1 = (bf16[1552,128]{1,0:T(8,128)(2,1)}, bf16[1552,128]{1,0:T(8,128)(2,1)S(1)}, u32[]{:S(2)}, u32[]{:S(2)}) collective-permute-start(bf16[1552,128]{1,0:T(8,128)(2,1)} %pack.8), channel_id=1, source_target_pairs={{0,16},{8,24},{16,0},{24,8},{1,17},{9,25},{17,1},{25,9},{2,18},{10... | collective-permute-start | bytes 1191944 | tf_op jit(solution)/shard_map/ppermute | solution.py:508
  10.2 19.2 %collective-permute-start.2 = (bf16[1552,128]{1,0:T(8,128)(2,1)S(1)}, bf16[1552,128]{1,0:T(8,128)(2,1)S(1)}, u32[]{:S(2)}, u32[]{:S(2)}) collective-permute-start(bf16[1552,128]{1,0:T(8,128)(2,1)S(1)} %copy-done.6), channel_id=1, source_target_pairs={{0,24},{8,16},{16,8},{24,0},{1,25},{9,17},{17,9},{25,1},{2,26},{10... | collective-permute-start | bytes 1191944 | tf_op jit(solution)/shard_map/ppermute | solution.py:508
  12.1 28.2 %collective-permute-start.7 = (bf16[1536,128]{1,0:T(8,128)(2,1)}, bf16[1536,128]{1,0:T(8,128)(2,1)S(1)}, u32[]{:S(2)}, u32[]{:S(2)}) collective-permute-start(bf16[1536,128]{1,0:T(8,128)(2,1)} %pack.10), channel_id=1, source_target_pairs={{0,8},{8,0},{16,24},{24,16},{1,9},{9,1},{17,25},{25,17},{2,10},{10... | collective-permute-start | bytes 1179656 | tf_op jit(solution)/shard_map/ppermute | solution.py:508
  15.9 24.4 %collective-permute-start.8 = (bf16[1536,128]{1,0:T(8,128)(2,1)}, bf16[1536,128]{1,0:T(8,128)(2,1)S(1)}, u32[]{:S(2)}, u32[]{:S(2)}) collective-permute-start(bf16[1536,128]{1,0:T(8,128)(2,1)} %pack.11), channel_id=1, source_target_pairs={{0,16},{8,24},{16,0},{24,8},{1,17},{9,25},{17,1},{25,9},{2,18},{10... | collective-permute-start | bytes 1179656 | tf_op jit(solution)/shard_map/ppermute | solution.py:508
  19.8 9.6 %copy-start.2 = (bf16[1024,512]{1,0:T(8,128)(2,1)S(1)}, bf16[1024,512]{1,0:T(8,128)(2,1)}, u32[]{:S(2)}) copy-start(bf16[1024,512]{1,0:T(8,128)(2,1)} %refs_3_.1) | copy-start | bytes 3145732
  19.8 9.6 %copy-start.3 = (bf16[1024,512]{1,0:T(8,128)(2,1)S(1)}, bf16[1024,512]{1,0:T(8,128)(2,1)}, u32[]{:S(2)}) copy-start(bf16[1024,512]{1,0:T(8,128)(2,1)} %refs_4_.1) | copy-start | bytes 3145732
  19.8 9.6 %copy-start.4 = (bf16[1024,512]{1,0:T(8,128)(2,1)S(1)}, bf16[1024,512]{1,0:T(8,128)(2,1)}, u32[]{:S(2)}) copy-start(bf16[1024,512]{1,0:T(8,128)(2,1)} %refs_5_.1) | copy-start | bytes 3145732
  19.8 9.6 %copy-start.5 = (s32[1024]{0:T(1024)S(1)}, s32[1024]{0:T(1024)}, u32[]{:S(2)}) copy-start(s32[1024]{0:T(1024)} %param.9) | copy-start | bytes 12292
  25.5 21.3 %copy-start = (bf16[512,2048]{1,0:T(8,128)(2,1)S(1)}, bf16[512,2048]{1,0:T(8,128)(2,1)}, u32[]{:S(2)}) copy-start(bf16[512,2048]{1,0:T(8,128)(2,1)} %get-tuple-element.84.refs_2_.refs_4_) | copy-start | bytes 6291460
  25.5 21.3 %copy-start.1 = (bf16[512,2048]{1,0:T(8,128)(2,1)S(1)}, bf16[512,2048]{1,0:T(8,128)(2,1)}, u32[]{:S(2)}) copy-start(bf16[512,2048]{1,0:T(8,128)(2,1)} %get-tuple-element.85.refs_3_.refs_5_) | copy-start | bytes 6291460
  36.8 12.5 %copy-start.7 = (bf16[1536,128]{1,0:T(8,128)(2,1)S(1)}, bf16[1536,128]{1,0:T(8,128)(2,1)}, u32[]{:S(2)}) copy-start(bf16[1536,128]{1,0:T(8,128)(2,1)} %pack.9) | copy-start | bytes 1179652
  36.8 5.7 %collective-permute-start.4 = (bf16[512,128]{1,0:T(8,128)(2,1)S(1)}, bf16[512,128]{1,0:T(8,128)(2,1)S(1)}, u32[]{:S(2)}, u32[]{:S(2)}) collective-permute-start(bf16[512,128]{1,0:T(8,128)(2,1)S(1)} %get-tuple-element.74), channel_id=1, source_target_pairs={{0,8},{8,0},{16,24},{24,16},{1,9},{9,1},{17,25},{25,17},{2,10},{10... | collective-permute-start | bytes 393224 | tf_op jit(solution)/shard_map/ppermute | solution.py:508
  36.8 6.4 %collective-permute-start.5 = (bf16[512,128]{1,0:T(8,128)(2,1)S(1)}, bf16[512,128]{1,0:T(8,128)(2,1)S(1)}, u32[]{:S(2)}, u32[]{:S(2)}) collective-permute-start(bf16[512,128]{1,0:T(8,128)(2,1)S(1)} %get-tuple-element.75), channel_id=1, source_target_pairs={{0,16},{8,24},{16,0},{24,8},{1,17},{9,25},{17,1},{25,9},{2,18},{10... | collective-permute-start | bytes 393224 | tf_op jit(solution)/shard_map/ppermute | solution.py:508
  38.9 5.9 %collective-permute-start.6 = (bf16[512,128]{1,0:T(8,128)(2,1)S(1)}, bf16[512,128]{1,0:T(8,128)(2,1)S(1)}, u32[]{:S(2)}, u32[]{:S(2)}) collective-permute-start(bf16[512,128]{1,0:T(8,128)(2,1)S(1)} %get-tuple-element.76), channel_id=1, source_target_pairs={{0,24},{8,16},{16,8},{24,0},{1,25},{9,17},{17,9},{25,1},{2,26},{10... | collective-permute-start | bytes 393224 | tf_op jit(solution)/shard_map/ppermute | solution.py:508
  44.9 2.0 %collective-permute-start.10 = (bf16[512,512]{1,0:T(8,128)(2,1)S(1)}, bf16[512,512]{1,0:T(8,128)(2,1)S(1)}, u32[]{:S(2)}, u32[]{:S(2)}) collective-permute-start(bf16[512,512]{1,0:T(8,128)(2,1)S(1)} %assemble.2.refs_0_), channel_id=1, source_target_pairs={{0,1},{1,0},{2,3},{3,2},{4,5},{5,4},{6,7},{7,6},{8,9},{9,8},{10,11... | collective-permute-start | bytes 1572872 | tf_op jit(solution)/shard_map/ppermute | solution.py:508
  47.6 19.6 %collective-permute-start.11 = (bf16[512,512]{1,0:T(8,128)(2,1)S(1)}, bf16[512,512]{1,0:T(8,128)(2,1)S(1)}, u32[]{:S(2)}, u32[]{:S(2)}) collective-permute-start(bf16[512,512]{1,0:T(8,128)(2,1)S(1)} %project.8), channel_id=1, source_target_pairs={{0,2},{1,3},{2,0},{3,1},{4,6},{5,7},{6,4},{7,5},{8,10},{9,11},{10,... | collective-permute-start | bytes 1572872 | tf_op jit(solution)/shard_map/ppermute | solution.py:508
  49.2 11.8 %collective-permute-start.9 = (bf16[1536,128]{1,0:T(8,128)(2,1)S(1)}, bf16[1536,128]{1,0:T(8,128)(2,1)S(1)}, u32[]{:S(2)}, u32[]{:S(2)}) collective-permute-start(bf16[1536,128]{1,0:T(8,128)(2,1)S(1)} %copy-done.7), channel_id=1, source_target_pairs={{0,24},{8,16},{16,8},{24,0},{1,25},{9,17},{17,9},{25,1},{2,26},{10... | collective-permute-start | bytes 1179656 | tf_op jit(solution)/shard_map/ppermute | solution.py:508
  52.1 26.9 %collective-permute-start.15 = (bf16[512,512]{1,0:T(8,128)(2,1)S(1)}, bf16[512,512]{1,0:T(8,128)(2,1)S(1)}, u32[]{:S(2)}, u32[]{:S(2)}) collective-permute-start(bf16[512,512]{1,0:T(8,128)(2,1)S(1)} %project.9), channel_id=1, source_target_pairs={{0,2},{1,3},{2,0},{3,1},{4,6},{5,7},{6,4},{7,5},{8,10},{9,11},{10,... | collective-permute-start | bytes 1572872 | tf_op jit(solution)/shard_map/ppermute | solution.py:508
  67.3 25.1 %collective-permute-start.19 = (bf16[512,512]{1,0:T(8,128)(2,1)S(1)}, bf16[512,512]{1,0:T(8,128)(2,1)S(1)}, u32[]{:S(2)}, u32[]{:S(2)}) collective-permute-start(bf16[512,512]{1,0:T(8,128)(2,1)S(1)} %add_convert_fusion.1), channel_id=1, source_target_pairs={{0,4},{1,5},{2,6},{3,7},{4,0},{5,1},{6,2},{7,3},{8,12},{9,13},{10,... | collective-permute-start | bytes 1572872 | tf_op jit(solution)/shard_map/ppermute | solution.py:508
  70.0 6.1 %collective-permute-start.12 = (bf16[512,128]{1,0:T(8,128)(2,1)S(1)}, bf16[512,128]{1,0:T(8,128)(2,1)S(1)}, u32[]{:S(2)}, u32[]{:S(2)}) collective-permute-start(bf16[512,128]{1,0:T(8,128)(2,1)S(1)} %get-tuple-element.90), channel_id=1, source_target_pairs={{0,8},{8,0},{16,24},{24,16},{1,9},{9,1},{17,25},{25,17},{2,10},{10... | collective-permute-start | bytes 393224 | tf_op jit(solution)/shard_map/ppermute | solution.py:508
  71.6 7.3 %collective-permute-start.13 = (bf16[512,128]{1,0:T(8,128)(2,1)S(1)}, bf16[512,128]{1,0:T(8,128)(2,1)S(1)}, u32[]{:S(2)}, u32[]{:S(2)}) collective-permute-start(bf16[512,128]{1,0:T(8,128)(2,1)S(1)} %get-tuple-element.91), channel_id=1, source_target_pairs={{0,16},{8,24},{16,0},{24,8},{1,17},{9,25},{17,1},{25,9},{2,18},{10... | collective-permute-start | bytes 393224 | tf_op jit(solution)/shard_map/ppermute | solution.py:508
  72.7 6.3 %collective-permute-start.14 = (bf16[512,128]{1,0:T(8,128)(2,1)S(1)}, bf16[512,128]{1,0:T(8,128)(2,1)S(1)}, u32[]{:S(2)}, u32[]{:S(2)}) collective-permute-start(bf16[512,128]{1,0:T(8,128)(2,1)S(1)} %get-tuple-element.92), channel_id=1, source_target_pairs={{0,24},{8,16},{16,8},{24,0},{1,25},{9,17},{17,9},{25,1},{2,26},{10... | collective-permute-start | bytes 393224 | tf_op jit(solution)/shard_map/ppermute | solution.py:508
  79.0 1.6 %collective-permute-start.16 = (bf16[256,512]{1,0:T(8,128)(2,1)S(1)}, bf16[256,512]{1,0:T(8,128)(2,1)S(1)}, u32[]{:S(2)}, u32[]{:S(2)}) collective-permute-start(bf16[256,512]{1,0:T(8,128)(2,1)S(1)} %get-tuple-element.98.refs_0_), channel_id=1, source_target_pairs={{0,1},{1,0},{2,3},{3,2},{4,5},{5,4},{6,7},{7,6},{8,9},{9,8},{10,11... | collective-permute-start | bytes 786440 | tf_op jit(solution)/shard_map/ppermute | solution.py:508
  79.1 1.9 %collective-permute-start.17 = (bf16[256,512]{1,0:T(8,128)(2,1)S(1)}, bf16[256,512]{1,0:T(8,128)(2,1)S(1)}, u32[]{:S(2)}, u32[]{:S(2)}) collective-permute-start(bf16[256,512]{1,0:T(8,128)(2,1)S(1)} %get-tuple-element.99.refs_1_), channel_id=1, source_target_pairs={{0,1},{1,0},{2,3},{3,2},{4,5},{5,4},{6,7},{7,6},{8,9},{9,8},{10,11... | collective-permute-start | bytes 786440 | tf_op jit(solution)/shard_map/ppermute | solution.py:508
  92.4 20.5 %collective-permute-start.20 = (bf16[512,512]{1,0:T(8,128)(2,1)S(1)}, bf16[512,512]{1,0:T(8,128)(2,1)S(1)}, u32[]{:S(2)}, u32[]{:S(2)}) collective-permute-start(bf16[512,512]{1,0:T(8,128)(2,1)S(1)} %project.15), channel_id=1, source_target_pairs={{0,2},{1,3},{2,0},{3,1},{4,6},{5,7},{6,4},{7,5},{8,10},{9,11},{10,... | collective-permute-start | bytes 1572872 | tf_op jit(solution)/shard_map/ppermute | solution.py:508
  93.1 28.9 %collective-permute-start.18 = (bf16[512,512]{1,0:T(8,128)(2,1)S(1)}, bf16[512,512]{1,0:T(8,128)(2,1)S(1)}, u32[]{:S(2)}, u32[]{:S(2)}) collective-permute-start(bf16[512,512]{1,0:T(8,128)(2,1)S(1)} %project.13), channel_id=1, source_target_pairs={{0,2},{1,3},{2,0},{3,1},{4,6},{5,7},{6,4},{7,5},{8,10},{9,11},{10,... | collective-permute-start | bytes 1572872 | tf_op jit(solution)/shard_map/ppermute | solution.py:508
  113.0 19.4 %collective-permute-start.21 = (bf16[512,512]{1,0:T(8,128)(2,1)S(1)}, bf16[512,512]{1,0:T(8,128)(2,1)S(1)}, u32[]{:S(2)}, u32[]{:S(2)}) collective-permute-start(bf16[512,512]{1,0:T(8,128)(2,1)S(1)} %add_convert_fusion), channel_id=1, source_target_pairs={{0,4},{1,5},{2,6},{3,7},{4,0},{5,1},{6,2},{7,3},{8,12},{9,13},{10,... | collective-permute-start | bytes 1572872 | tf_op jit(solution)/shard_map/ppermute | solution.py:508

commit v13 on v11

--- a/solution.py
+++ b/solution.py
@@ -429,14 +429,17 @@
     )(ctx_index, *operands)
 
 
-def assemble(ctx_index, pieces):
+def assemble(ctx_index, pieces, parts):
     rows = pieces[0].shape[0]
     group = len(pieces)
+    part_rows = rows // parts
 
     def kernel(ctx_ref, *refs):
-        for distance in range(group):
-            column = pl.multiple_of((ctx_ref[0] ^ distance) * HD, HD)
-            refs[-1][:, pl.ds(column, HD)] = refs[distance][...]
+        for part in range(parts):
+            for distance in range(group):
+                column = pl.multiple_of((ctx_ref[0] ^ distance) * HD, HD)
+                taken = refs[distance][part * part_rows : (part + 1) * part_rows, :]
+                refs[group + part][:, pl.ds(column, HD)] = taken
 
     return pl.pallas_call(
         kernel,
@@ -444,9 +447,9 @@
             num_scalar_prefetch=1,
             grid=(1,),
             in_specs=[whole((rows, HD))] * group,
-            out_specs=whole((rows, group * HD)),
+            out_specs=[whole((part_rows, group * HD))] * parts,
         ),
-        out_shape=jax.ShapeDtypeStruct((rows, group * HD), jnp.bfloat16),
+        out_shape=[jax.ShapeDtypeStruct((part_rows, group * HD), jnp.bfloat16)] * parts,
         compiler_params=params(16),
         cost_estimate=SMALL,
         name="assemble",
@@ -454,26 +457,63 @@
 
 
 def project(turn, mine, sibling, w_mine, w_sibling):
-    rows, depth = mine.shape
+    parts = len(mine)
+    rows, depth = mine[0].shape
     columns = w_mine.shape[1] // len(TURNS)
 
-    def kernel(mine_ref, sibling_ref, w_mine_ref, w_sibling_ref, out_ref):
-        total = jnp.dot(mine_ref[...], w_mine_ref[...], preferred_element_type=jnp.float32)
-        total += jnp.dot(sibling_ref[...], w_sibling_ref[...], preferred_element_type=jnp.float32)
-        out_ref[...] = total.astype(jnp.bfloat16)
+    def kernel(*refs):
+        w_mine_ref, w_sibling_ref = refs[2 * parts : 2 * parts + 2]
+        for part in range(parts):
+            total = jnp.dot(refs[part][...], w_mine_ref[...], preferred_element_type=jnp.float32)
+            total += jnp.dot(
+                refs[parts + part][...], w_sibling_ref[...], preferred_element_type=jnp.float32
+            )
+            refs[2 * parts + 2 + part][...] = total.astype(jnp.bfloat16)
 
     weights = pl.BlockSpec((depth, columns), lambda step: (0, turn))
     attended = pl.BlockSpec((rows, depth), lambda step: (0, 0))
     return pl.pallas_call(
         kernel,
         grid=(1,),
-        in_specs=[attended, attended, weights, weights],
-        out_specs=pl.BlockSpec((rows, columns), lambda step: (0, 0)),
-        out_shape=jax.ShapeDtypeStruct((rows, columns), jnp.bfloat16),
+        in_specs=[attended] * (2 * parts) + [weights] * 2,
+        out_specs=[pl.BlockSpec((rows, columns), lambda step: (0, 0))] * parts,
+        out_shape=[jax.ShapeDtypeStruct((rows, columns), jnp.bfloat16)] * parts,
         compiler_params=params(16),
         cost_estimate=SMALL,
         name="project",
-    )(mine, sibling, w_mine, w_sibling)
+    )(*mine, *sibling, w_mine, w_sibling)
+
+
+def finish(half, terms, result):
+    parts = len(terms[0])
+    rows, columns = terms[0][0].shape
+    flat = [part for term in terms for part in term]
+
+    def kernel(*refs):
+        for part in range(parts):
+            total = refs[part][...].astype(jnp.float32)
+            for term in range(1, len(terms)):
+                total += refs[term * parts + part][...].astype(jnp.float32)
+            refs[-1][part * rows : (part + 1) * rows, :] = total.astype(jnp.bfloat16)
+
+    in_specs = [pl.BlockSpec((rows, columns), lambda step: (0, 0))] * len(flat)
+    operands = list(flat)
+    aliases = {}
+    if result is not None:
+        in_specs.append(pl.BlockSpec(memory_space=pl.ANY))
+        operands.append(result)
+        aliases = {len(flat): 0}
+    return pl.pallas_call(
+        kernel,
+        grid=(1,),
+        in_specs=in_specs,
+        out_specs=pl.BlockSpec((parts * rows, columns), lambda step: (half, 0)),
+        out_shape=jax.ShapeDtypeStruct((2 * parts * rows, columns), jnp.bfloat16),
+        input_output_aliases=aliases,
+        compiler_params=params(16),
+        cost_estimate=SMALL,
+        name="finish",
+    )(*operands)
 
 
 def swap(value, axis, distance):
@@ -509,43 +549,42 @@
     low_out, later = tie(low_out, (queries, keys, values))
     low = [swap(low_out[distance - 1], "ctx", distance) for distance in near]
     high_out = pack(ctx_index, 1, *later, None)
+    high = [swap(high_out[distance - 1], "ctx", distance) for distance in near[:-1]]
     w_packed = pack_projection(places, w_out, w_sibling)
-    high_out, low, w_packed = tie(high_out, low, w_packed)
-    high = [swap(high_out[0], "ctx", 1), swap(high_out[1], "ctx", 2)]
+    low, w_packed = tie(low, w_packed)
 
     def send_back(pieces):
         return [swap(pieces[distance], "ctx", distance) for distance in near]
 
-    def share_of(mine, sibling, turn):
-        return project(turn, mine, sibling, *w_packed)
+    def shares_of(mine):
+        sibling = [swap(part, "head", 1) for part in mine]
+        return [project(turn, mine, sibling, *w_packed) for turn in range(len(TURNS))]
+
+    def to_next(parts, distance):
+        return [swap(part, "head", 2 * distance) for part in parts]
 
     pieces = attend(ctx_index, queries, keys, values, docs, low, None)
-    pieces, diagonal_out = tie(pieces, high_out[2])
+    pieces, diagonal_out = tie(pieces, high_out[-1])
     back = send_back(pieces)
     back, high = tie(back, high)
-    high.append(swap(diagonal_out, "ctx", 3))
-    mine = assemble(ctx_index, [pieces[0], *back])
-    sibling = swap(mine, "head", 1)
-    shares = [share_of(mine, sibling, turn) for turn in range(len(TURNS))]
-    far = swap(shares[0], "head", 2)
-    shares[1], high[2] = tie(shares[1], high[2])
-    near_sum = swap(shares[1], "head", 2)
-
-    passed = add(shares[2], far)
+    high = [*high, swap(diagonal_out, "ctx", near[-1])]
+    shares = shares_of(assemble(ctx_index, [pieces[0], *back], 1))
+    far = to_next(shares[0], 1)
+    near_sum = to_next(shares[1], 1)
+
+    passed = [add(*both) for both in zip(shares[2], far)]
     high, shares, passed = tie(high, shares, passed)
-    across = swap(passed, "head", 4)
+    across = to_next(passed, 2)
     pieces = attend(ctx_index, queries, keys, values, docs, low, high)
     back = send_back(pieces)
-    mine = assemble(ctx_index, [pieces[0], *back])
-    mine, across, near_sum = tie(mine, across, near_sum)
-    first = add(shares[3], near_sum, across)
-    sibling = swap(mine, "head", 1)
-    late = [share_of(mine, sibling, turn) for turn in range(len(TURNS))]
-    far = swap(late[0], "head", 2)
-    near_sum = swap(late[1], "head", 2)
-    across = swap(add(late[2], far), "head", 4)
-    second = add(late[3], near_sum, across)
-    return jnp.concatenate([first, second], axis=0)
+    back, near_sum = tie(back, near_sum)
+    late = shares_of(assemble(ctx_index, [pieces[0], *back], 2))
+    late[0], across = tie(late[0], across)
+    result = finish(0, [shares[3], near_sum, across], None)
+    far = to_next(late[0], 1)
+    near_sum = to_next(late[1], 1)
+    across = to_next([add(*both) for both in zip(late[2], far)], 2)
+    return finish(1, [late[3], near_sum, across], result)
 
 
 def solution(mesh):

time: 130 us -> 122 us (0.938)
  waiting for transfers between devices: 73.3 us -> 60.8 us
  starting transfers between devices: 24.1 us -> 29.9 us
  other arithmetic: 2.24 us -> 0.79 us
    ppermute x21 -> x25, waiting for transfers between devices: 73.3 us -> 60.8 us  [swap(): lax.ppermute(value, axis, [(source, source ^ distance) for source in rang...]
    ppermute x21 -> x25, starting transfers between devices: 24.1 us -> 29.9 us  [swap(): lax.ppermute(value, axis, [(source, source ^ distance) for source in rang...]
    pallas_call x8 -> x10, Pallas kernels: 5.69 us -> 7.67 us  [the longest x8 5.68 us: project(): pl.pallas_call(kernel, grid=(1,), in_specs=[attended] * (2 * parts) + [we...]
    pallas_call x2, Pallas kernels: 13.5 us -> 11.5 us  [attend(): pl.pallas_call(kernel, grid_spec=pltpu.PrefetchScalarGridSpec(num_scalar_...]
  transfers between devices with their start and end apart: 21 -> 25, of which waited for: 14 -> 14; matrix products, arithmetic and copies ran while one was open for 1% -> 1% of each run, Pallas kernels for 22% -> 23%
where the time goes in v13:
time: 122 us
  waiting for transfers between devices  60.8 us (50%)
  Pallas kernels  30.2 us (25%)
  starting transfers between devices  29.9 us (25%)
    ppermute x25, waiting for transfers between devices, swap(): lax.ppermute(value, axis, [(source, source ^ distance) for source in rang...  60.8 us
    ppermute x25, starting transfers between devices, swap(): lax.ppermute(value, axis, [(source, source ^ distance) for source in rang...  29.9 us
    pallas_call x2, Pallas kernels, attend(): pl.pallas_call(kernel, grid_spec=pltpu.PrefetchScalarGridSpec(num_scalar_...  11.5 us
    pallas_call x1, Pallas kernels, pack_projection(): pl.pallas_call(kernel, grid_spec=pltpu.PrefetchScalarGridSpec(num_scalar_...  5.74 us
    pallas_call x8, Pallas kernels, project(): pl.pallas_call(kernel, grid=(1,), in_specs=[attended] * (2 * parts) + [we...  5.68 us
    pallas_call x2, Pallas kernels, pack(): pl.pallas_call(kernel, grid_spec=pltpu.PrefetchScalarGridSpec(num_scalar_...  5.02 us
  transfers between devices with their start and end apart: 25, of which 14 were waited for; matrix products, arithmetic and copies ran while one was open for 1% of the time, Pallas kernels for 23%

profile of v13, /device:TPU:0, one launch (start us, length us, event | category | flops | bytes accessed | tf_op | source)
XLA Modules:
  0.0 121.9 jit_solution(8736726673245405285)
XLA Ops:
  0.0 0.5 collective-permute-start.3
  0.5 2.5 %pack.2 = (bf16[1552,128]{1,0:T(8,128)(2,1)}, bf16[1552,128]{1,0:T(8,128)(2,1)}, bf16[1552,128]{1,0:T(8,128)(2,1)}) custom-call(s32[1]{0:T(128)} %bitcast.ctx_ref, bf16[1024,512]{1,0:T(8,128)(2,1)} %refs_3_.4, bf16[1024,512]{1,0:T(8,128)(2,1)} %refs_4_.4, bf16[1024,512]{1,0:T(8,128)(2,1)} %refs_5_.4, bf16[1024,512]{1,0:T(8,128)(2,1)} %refs_3_.4, ...), custom_call_target="tpu_custom_call" | custom-call | flops 1024 | bytes 1024 | tf_op jit(solution)/shard_map/pack/pallas_call | solution.py:201
  2.9 2.5 %collective-permute-start = (bf16[1552,128]{1,0:T(8,128)(2,1)}, bf16[1552,128]{1,0:T(8,128)(2,1)S(1)}, u32[]{:S(2)}, u32[]{:S(2)}) collective-permute-start(bf16[1552,128]{1,0:T(8,128)(2,1)} %get-tuple-element.67), channel_id=1, source_target_pairs={{0,8},{8,0},{16,24},{24,16},{1,9},{9,1},{17,25},{25,17},{2,10},{10... | collective-permute-start | bytes 1191944 | tf_op jit(solution)/shard_map/ppermute | solution.py:521
  5.4 1.5 %collective-permute-start.1 = (bf16[1552,128]{1,0:T(8,128)(2,1)}, bf16[1552,128]{1,0:T(8,128)(2,1)S(1)}, u32[]{:S(2)}, u32[]{:S(2)}) collective-permute-start(bf16[1552,128]{1,0:T(8,128)(2,1)} %get-tuple-element.68), channel_id=1, source_target_pairs={{0,16},{8,24},{16,0},{24,8},{1,17},{9,25},{17,1},{25,9},{2,18},{10... | collective-permute-start | bytes 1191944 | tf_op jit(solution)/shard_map/ppermute | solution.py:521
  7.0 0.0 collective-permute-start.2
  7.0 2.5 %pack.3 = (bf16[1536,128]{1,0:T(8,128)(2,1)}, bf16[1536,128]{1,0:T(8,128)(2,1)}, bf16[1536,128]{1,0:T(8,128)(2,1)}) custom-call(s32[1]{0:T(128)} %bitcast.ctx_ref, bf16[1024,512]{1,0:T(8,128)(2,1)} %refs_3_.4, bf16[1024,512]{1,0:T(8,128)(2,1)} %refs_4_.4, bf16[1024,512]{1,0:T(8,128)(2,1)} %refs_5_.4, bf16[1024,512]{1,0:T(8,128)(2,1)} %refs_3_.4, ...), custom_call_target="tpu_custom_call" | custom-call | flops 1024 | bytes 1024 | tf_op jit(solution)/shard_map/pack/pallas_call | solution.py:201
  9.5 2.0 %collective-permute-start.7 = (bf16[1536,128]{1,0:T(8,128)(2,1)}, bf16[1536,128]{1,0:T(8,128)(2,1)S(1)}, u32[]{:S(2)}, u32[]{:S(2)}) collective-permute-start(bf16[1536,128]{1,0:T(8,128)(2,1)} %get-tuple-element.86), channel_id=1, source_target_pairs={{0,8},{8,0},{16,24},{24,16},{1,9},{9,1},{17,25},{25,17},{2,10},{10... | collective-permute-start | bytes 1179656 | tf_op jit(solution)/shard_map/ppermute | solution.py:521
  11.5 0.0 collective-permute-done.3.sibling_in
  11.5 1.5 %collective-permute-start.8 = (bf16[1536,128]{1,0:T(8,128)(2,1)}, bf16[1536,128]{1,0:T(8,128)(2,1)S(1)}, u32[]{:S(2)}, u32[]{:S(2)}) collective-permute-start(bf16[1536,128]{1,0:T(8,128)(2,1)} %get-tuple-element.87), channel_id=1, source_target_pairs={{0,16},{8,24},{16,0},{24,8},{1,17},{9,25},{17,1},{25,9},{2,18},{10... | collective-permute-start | bytes 1179656 | tf_op jit(solution)/shard_map/ppermute | solution.py:521
  13.0 0.5 broadcast_xor_fusion.places_ref
  13.5 5.7 %pack_projection.1 = (bf16[512,2048]{1,0:T(8,128)(2,1)}, bf16[512,2048]{1,0:T(8,128)(2,1)}) custom-call(s32[4]{0:T(128)} %broadcast_xor_fusion.places_ref, bf16[512,4096]{1,0:T(8,128)(2,1)} %mine_in.1, bf16[512,4096]{1,0:T(8,128)(2,1)} %collective-permute-done.3.sibling_in), custom_call_target="tpu_custom_call" | custom-call | flops 1024 | bytes 1024 | tf_op jit(solution)/shard_map/pack_projection/pallas_call | solution.py:227
  19.3 0.0 collective-permute-done.refs_4_.refs_7_
  19.3 6.9 %collective-permute-done.1.refs_5_.refs_8_ = bf16[1552,128]{1,0:T(8,128)(2,1)S(1)} collective-permute-done((bf16[1552,128]{1,0:T(8,128)(2,1)}, bf16[1552,128]{1,0:T(8,128)(2,1)S(1)}, u32[]{:S(2)}, u32[]{:S(2)}) %collective-permute-start.1) | collective-permute-done | bytes 397344 | tf_op jit(solution)/shard_map/ppermute | solution.py:521
  26.2 0.0 collective-permute-done.2.refs_6_.refs_9_
  26.2 5.4 %attend_low.1 = (bf16[512,128]{1,0:T(8,128)(2,1)S(1)}, bf16[512,128]{1,0:T(8,128)(2,1)S(1)}, bf16[512,128]{1,0:T(8,128)(2,1)S(1)}, bf16[512,128]{1,0:T(8,128)(2,1)S(1)}) custom-call(s32[1]{0:T(128)} %bitcast.ctx_ref, bf16[1024,512]{1,0:T(8,128)(2,1)S(1)} %copy-done.2, bf16[1024,512]{1,0:T(8,128)(2,1)S(1)} %copy-done.3, bf16[1024,512]{1,0:T(8,128)(2,1)S(1)} %copy-done.4, ...), custom_call_target="tpu_custom_call" | custom-call | flops 1024 | bytes 1024 | tf_op jit(solution)/shard_map/attend_low/pallas_call | solution.py:409
  31.6 1.0 collective-permute-start.4
  32.6 1.1 collective-permute-start.5
  33.7 1.4 %collective-permute-start.6 = (bf16[512,128]{1,0:T(8,128)(2,1)S(1)}, bf16[512,128]{1,0:T(8,128)(2,1)S(1)}, u32[]{:S(2)}, u32[]{:S(2)}) collective-permute-start(bf16[512,128]{1,0:T(8,128)(2,1)S(1)} %get-tuple-element.85), channel_id=1, source_target_pairs={{0,24},{8,16},{16,8},{24,0},{1,25},{9,17},{17,9},{25,1},{2,26},{10... | collective-permute-start | bytes 393224 | tf_op jit(solution)/shard_map/ppermute | solution.py:521
  35.2 0.0 collective-permute-done.7.refs_10_
  35.2 2.6 %collective-permute-done.4.refs_1_ = bf16[512,128]{1,0:T(8,128)(2,1)S(1)} collective-permute-done((bf16[512,128]{1,0:T(8,128)(2,1)S(1)}, bf16[512,128]{1,0:T(8,128)(2,1)S(1)}, u32[]{:S(2)}, u32[]{:S(2)}) %collective-permute-start.4) | collective-permute-done | bytes 131104 | tf_op jit(solution)/shard_map/ppermute | solution.py:521
  37.8 2.1 %collective-permute-done.5.refs_2_ = bf16[512,128]{1,0:T(8,128)(2,1)S(1)} collective-permute-done((bf16[512,128]{1,0:T(8,128)(2,1)S(1)}, bf16[512,128]{1,0:T(8,128)(2,1)S(1)}, u32[]{:S(2)}, u32[]{:S(2)}) %collective-permute-start.5) | collective-permute-done | bytes 131104 | tf_op jit(solution)/shard_map/ppermute | solution.py:521
  39.9 0.1 assemble.2.refs_0_
  40.0 0.1 collective-permute-start.10
  40.1 1.9 %collective-permute-done.10.refs_1_ = bf16[512,512]{1,0:T(8,128)(2,1)S(1)} collective-permute-done((bf16[512,512]{1,0:T(8,128)(2,1)S(1)}, bf16[512,512]{1,0:T(8,128)(2,1)S(1)}, u32[]{:S(2)}, u32[]{:S(2)}) %collective-permute-start.10) | collective-permute-done | bytes 524320 | tf_op jit(solution)/shard_map/ppermute | solution.py:521
  42.0 0.7 project.8
  42.7 1.6 %collective-permute-start.11 = (bf16[512,512]{1,0:T(8,128)(2,1)S(1)}, bf16[512,512]{1,0:T(8,128)(2,1)S(1)}, u32[]{:S(2)}, u32[]{:S(2)}) collective-permute-start(bf16[512,512]{1,0:T(8,128)(2,1)S(1)} %project.8), channel_id=1, source_target_pairs={{0,2},{1,3},{2,0},{3,1},{4,6},{5,7},{6,4},{7,5},{8,10},{9,11},{10,... | collective-permute-start | bytes 1572872 | tf_op jit(solution)/shard_map/ppermute | solution.py:521
  44.4 1.8 %collective-permute-start.9 = (bf16[1536,128]{1,0:T(8,128)(2,1)S(1)}, bf16[1536,128]{1,0:T(8,128)(2,1)S(1)}, u32[]{:S(2)}, u32[]{:S(2)}) collective-permute-start(bf16[1536,128]{1,0:T(8,128)(2,1)S(1)} %copy-done.6), channel_id=1, source_target_pairs={{0,24},{8,16},{16,8},{24,0},{1,25},{9,17},{17,9},{25,1},{2,26},{10... | collective-permute-start | bytes 1179656 | tf_op jit(solution)/shard_map/ppermute | solution.py:521
  46.1 0.7 project.9
  46.8 0.5 collective-permute-start.15
  47.4 0.7 project.10
  48.1 0.7 project.11.refs_0_
  48.8 8.7 %collective-permute-done.11 = bf16[512,512]{1,0:T(8,128)(2,1)S(1)} collective-permute-done((bf16[512,512]{1,0:T(8,128)(2,1)S(1)}, bf16[512,512]{1,0:T(8,128)(2,1)S(1)}, u32[]{:S(2)}, u32[]{:S(2)}) %collective-permute-start.11) | collective-permute-done | bytes 524320 | tf_op jit(solution)/shard_map/ppermute | solution.py:521
  57.5 0.1 add_convert_fusion
  57.7 2.7 %collective-permute-start.20 = (bf16[512,512]{1,0:T(8,128)(2,1)S(1)}, bf16[512,512]{1,0:T(8,128)(2,1)S(1)}, u32[]{:S(2)}, u32[]{:S(2)}) collective-permute-start(bf16[512,512]{1,0:T(8,128)(2,1)S(1)} %add_convert_fusion), channel_id=1, source_target_pairs={{0,4},{1,5},{2,6},{3,7},{4,0},{5,1},{6,2},{7,3},{8,12},{9,13},{10,... | collective-permute-start | bytes 1572872 | tf_op jit(solution)/shard_map/ppermute | solution.py:521
  60.4 6.2 %attend_high.1 = (bf16[512,128]{1,0:T(8,128)(2,1)S(1)}, bf16[512,128]{1,0:T(8,128)(2,1)S(1)}, bf16[512,128]{1,0:T(8,128)(2,1)S(1)}, bf16[512,128]{1,0:T(8,128)(2,1)S(1)}) custom-call(s32[1]{0:T(128)} %bitcast.ctx_ref, bf16[1024,512]{1,0:T(8,128)(2,1)S(1)} %copy-done.2, bf16[1024,512]{1,0:T(8,128)(2,1)S(1)} %copy-done.3, bf16[1024,512]{1,0:T(8,128)(2,1)S(1)} %copy-done.4, ...), custom_call_target="tpu_custom_call" | custom-call | flops 1024 | bytes 1024 | tf_op jit(solution)/shard_map/attend_high/pallas_call | solution.py:409
  66.5 1.4 %collective-permute-start.12 = (bf16[512,128]{1,0:T(8,128)(2,1)S(1)}, bf16[512,128]{1,0:T(8,128)(2,1)S(1)}, u32[]{:S(2)}, u32[]{:S(2)}) collective-permute-start(bf16[512,128]{1,0:T(8,128)(2,1)S(1)} %get-tuple-element.101), channel_id=1, source_target_pairs={{0,8},{8,0},{16,24},{24,16},{1,9},{9,1},{17,25},{25,17},{2,10},{10... | collective-permute-start | bytes 393224 | tf_op jit(solution)/shard_map/ppermute | solution.py:521
  68.0 1.0 collective-permute-start.13
  68.9 1.2 collective-permute-start.14
  70.1 8.2 %collective-permute-done.15.refs_1_ = bf16[512,512]{1,0:T(8,128)(2,1)S(1)} collective-permute-done((bf16[512,512]{1,0:T(8,128)(2,1)S(1)}, bf16[512,512]{1,0:T(8,128)(2,1)S(1)}, u32[]{:S(2)}, u32[]{:S(2)}) %collective-permute-start.15) | collective-permute-done | bytes 524320 | tf_op jit(solution)/shard_map/ppermute | solution.py:521
  78.3 0.1 assemble.3
  78.4 0.1 collective-permute-start.16
  78.5 0.5 collective-permute-start.17
  79.0 1.0 collective-permute-done.16.refs_2_
  80.0 0.4 collective-permute-done.17.refs_3_
  80.4 0.7 project.15
  81.1 1.2 collective-permute-done.20.refs_2_
  82.3 0.8 collective-permute-start.21
  83.1 1.2 %collective-permute-start.23 = (bf16[256,512]{1,0:T(8,128)(2,1)S(1)}, bf16[256,512]{1,0:T(8,128)(2,1)S(1)}, u32[]{:S(2)}, u32[]{:S(2)}) collective-permute-start(bf16[256,512]{1,0:T(8,128)(2,1)S(1)} %get-tuple-element.119), channel_id=1, source_target_pairs={{0,2},{1,3},{2,0},{3,1},{4,6},{5,7},{6,4},{7,5},{8,10},{9,11},{10,... | collective-permute-start | bytes 786440 | tf_op jit(solution)/shard_map/ppermute | solution.py:521
  84.3 0.7 project.13
  85.0 0.9 collective-permute-start.18
  85.9 1.2 %collective-permute-start.19 = (bf16[256,512]{1,0:T(8,128)(2,1)S(1)}, bf16[256,512]{1,0:T(8,128)(2,1)S(1)}, u32[]{:S(2)}, u32[]{:S(2)}) collective-permute-start(bf16[256,512]{1,0:T(8,128)(2,1)S(1)} %get-tuple-element.112), channel_id=1, source_target_pairs={{0,2},{1,3},{2,0},{3,1},{4,6},{5,7},{6,4},{7,5},{8,10},{9,11},{10,... | collective-permute-start | bytes 786440 | tf_op jit(solution)/shard_map/ppermute | solution.py:521
  87.1 0.7 project.14
  87.8 6.5 %collective-permute-done.21 = bf16[256,512]{1,0:T(8,128)(2,1)S(1)} collective-permute-done((bf16[256,512]{1,0:T(8,128)(2,1)S(1)}, bf16[256,512]{1,0:T(8,128)(2,1)S(1)}, u32[]{:S(2)}, u32[]{:S(2)}) %collective-permute-start.21) | collective-permute-done | bytes 262176 | tf_op jit(solution)/shard_map/ppermute | solution.py:521
  94.3 0.1 add_convert_fusion.2
  94.4 1.7 %collective-permute-start.22 = (bf16[256,512]{1,0:T(8,128)(2,1)S(1)}, bf16[256,512]{1,0:T(8,128)(2,1)S(1)}, u32[]{:S(2)}, u32[]{:S(2)}) collective-permute-start(bf16[256,512]{1,0:T(8,128)(2,1)S(1)} %add_convert_fusion.2), channel_id=1, source_target_pairs={{0,4},{1,5},{2,6},{3,7},{4,0},{5,1},{6,2},{7,3},{8,12},{9,13},{10,... | collective-permute-start | bytes 786440 | tf_op jit(solution)/shard_map/ppermute | solution.py:521
  96.2 9.4 %collective-permute-done.23 = bf16[256,512]{1,0:T(8,128)(2,1)S(1)} collective-permute-done((bf16[256,512]{1,0:T(8,128)(2,1)S(1)}, bf16[256,512]{1,0:T(8,128)(2,1)S(1)}, u32[]{:S(2)}, u32[]{:S(2)}) %collective-permute-start.23) | collective-permute-done | bytes 262176 | tf_op jit(solution)/shard_map/ppermute | solution.py:521
  105.6 0.1 add_convert_fusion.1
  105.6 1.7 %collective-permute-start.24 = (bf16[256,512]{1,0:T(8,128)(2,1)S(1)}, bf16[256,512]{1,0:T(8,128)(2,1)S(1)}, u32[]{:S(2)}, u32[]{:S(2)}) collective-permute-start(bf16[256,512]{1,0:T(8,128)(2,1)S(1)} %add_convert_fusion.1), channel_id=1, source_target_pairs={{0,4},{1,5},{2,6},{3,7},{4,0},{5,1},{6,2},{7,3},{8,12},{9,13},{10,... | collective-permute-start | bytes 786440 | tf_op jit(solution)/shard_map/ppermute | solution.py:521
  107.4 0.7 project.12
  108.1 1.0 finish.2.refs_6_
  109.1 2.2 %collective-permute-done.18.refs_2_ = bf16[256,512]{1,0:T(8,128)(2,1)S(1)} collective-permute-done((bf16[256,512]{1,0:T(8,128)(2,1)S(1)}, bf16[256,512]{1,0:T(8,128)(2,1)S(1)}, u32[]{:S(2)}, u32[]{:S(2)}) %collective-permute-start.18) | collective-permute-done | bytes 262176 | tf_op jit(solution)/shard_map/ppermute | solution.py:521
  111.3 3.6 %collective-permute-done.19.refs_3_ = bf16[256,512]{1,0:T(8,128)(2,1)S(1)} collective-permute-done((bf16[256,512]{1,0:T(8,128)(2,1)S(1)}, bf16[256,512]{1,0:T(8,128)(2,1)S(1)}, u32[]{:S(2)}, u32[]{:S(2)}) %collective-permute-start.19) | collective-permute-done | bytes 262176 | tf_op jit(solution)/shard_map/ppermute | solution.py:521
  114.9 6.0 %collective-permute-done.24.refs_5_ = bf16[256,512]{1,0:T(8,128)(2,1)S(1)} collective-permute-done((bf16[256,512]{1,0:T(8,128)(2,1)S(1)}, bf16[256,512]{1,0:T(8,128)(2,1)S(1)}, u32[]{:S(2)}, u32[]{:S(2)}) %collective-permute-start.24) | collective-permute-done | bytes 262176 | tf_op jit(solution)/shard_map/ppermute | solution.py:521
  120.9 1.0 finish.3
  (23 shorter events, 0.0 us)
Async XLA Ops:
  0.0 11.5 %collective-permute-start.3 = (bf16[512,4096]{1,0:T(8,128)(2,1)}, bf16[512,4096]{1,0:T(8,128)(2,1)}, u32[]{:S(2)}, u32[]{:S(2)}) collective-permute-start(bf16[512,4096]{1,0:T(8,128)(2,1)} %mine_in.1), channel_id=1, source_target_pairs={{0,1},{1,0},{2,3},{3,2},{4,5},{5,4},{6,7},{7,6},{8,9},{9,8},{10,11... | collective-permute-start | bytes 12582920 | tf_op jit(solution)/shard_map/ppermute | solution.py:521
  2.9 10.0 %copy-start.7 = (s32[4]{0:T(128)S(1)}, s32[4]{0:T(128)}, u32[]{:S(2)}) copy-start(s32[4]{0:T(128)} %constant.13) | copy-start | bytes 52
  2.9 16.3 %collective-permute-start = (bf16[1552,128]{1,0:T(8,128)(2,1)}, bf16[1552,128]{1,0:T(8,128)(2,1)S(1)}, u32[]{:S(2)}, u32[]{:S(2)}) collective-permute-start(bf16[1552,128]{1,0:T(8,128)(2,1)} %get-tuple-element.67), channel_id=1, source_target_pairs={{0,8},{8,0},{16,24},{24,16},{1,9},{9,1},{17,25},{25,17},{2,10},{10... | collective-permute-start | bytes 1191944 | tf_op jit(solution)/shard_map/ppermute | solution.py:521
  5.4 20.8 %collective-permute-start.1 = (bf16[1552,128]{1,0:T(8,128)(2,1)}, bf16[1552,128]{1,0:T(8,128)(2,1)S(1)}, u32[]{:S(2)}, u32[]{:S(2)}) collective-permute-start(bf16[1552,128]{1,0:T(8,128)(2,1)} %get-tuple-element.68), channel_id=1, source_target_pairs={{0,16},{8,24},{16,0},{24,8},{1,17},{9,25},{17,1},{25,9},{2,18},{10... | collective-permute-start | bytes 1191944 | tf_op jit(solution)/shard_map/ppermute | solution.py:521
  7.0 19.2 %collective-permute-start.2 = (bf16[1552,128]{1,0:T(8,128)(2,1)}, bf16[1552,128]{1,0:T(8,128)(2,1)S(1)}, u32[]{:S(2)}, u32[]{:S(2)}) collective-permute-start(bf16[1552,128]{1,0:T(8,128)(2,1)} %get-tuple-element.69), channel_id=1, source_target_pairs={{0,24},{8,16},{16,8},{24,0},{1,25},{9,17},{17,9},{25,1},{2,26},{10... | collective-permute-start | bytes 1191944 | tf_op jit(solution)/shard_map/ppermute | solution.py:521
  9.5 25.7 %collective-permute-start.7 = (bf16[1536,128]{1,0:T(8,128)(2,1)}, bf16[1536,128]{1,0:T(8,128)(2,1)S(1)}, u32[]{:S(2)}, u32[]{:S(2)}) collective-permute-start(bf16[1536,128]{1,0:T(8,128)(2,1)} %get-tuple-element.86), channel_id=1, source_target_pairs={{0,8},{8,0},{16,24},{24,16},{1,9},{9,1},{17,25},{25,17},{2,10},{10... | collective-permute-start | bytes 1179656 | tf_op jit(solution)/shard_map/ppermute | solution.py:521
  11.5 23.7 %collective-permute-start.8 = (bf16[1536,128]{1,0:T(8,128)(2,1)}, bf16[1536,128]{1,0:T(8,128)(2,1)S(1)}, u32[]{:S(2)}, u32[]{:S(2)}) collective-permute-start(bf16[1536,128]{1,0:T(8,128)(2,1)} %get-tuple-element.87), channel_id=1, source_target_pairs={{0,16},{8,24},{16,0},{24,8},{1,17},{9,25},{17,1},{25,9},{2,18},{10... | collective-permute-start | bytes 1179656 | tf_op jit(solution)/shard_map/ppermute | solution.py:521
  13.5 12.7 %copy-start.2 = (bf16[1024,512]{1,0:T(8,128)(2,1)S(1)}, bf16[1024,512]{1,0:T(8,128)(2,1)}, u32[]{:S(2)}) copy-start(bf16[1024,512]{1,0:T(8,128)(2,1)} %refs_3_.4) | copy-start | bytes 3145732
  13.5 12.7 %copy-start.3 = (bf16[1024,512]{1,0:T(8,128)(2,1)S(1)}, bf16[1024,512]{1,0:T(8,128)(2,1)}, u32[]{:S(2)}) copy-start(bf16[1024,512]{1,0:T(8,128)(2,1)} %refs_4_.4) | copy-start | bytes 3145732
  13.5 12.7 %copy-start.4 = (bf16[1024,512]{1,0:T(8,128)(2,1)S(1)}, bf16[1024,512]{1,0:T(8,128)(2,1)}, u32[]{:S(2)}) copy-start(bf16[1024,512]{1,0:T(8,128)(2,1)} %refs_5_.4) | copy-start | bytes 3145732
  13.5 12.7 %copy-start.5 = (s32[1024]{0:T(1024)S(1)}, s32[1024]{0:T(1024)}, u32[]{:S(2)}) copy-start(s32[1024]{0:T(1024)} %param.9) | copy-start | bytes 12292
  19.3 22.7 %copy-start = (bf16[512,2048]{1,0:T(8,128)(2,1)S(1)}, bf16[512,2048]{1,0:T(8,128)(2,1)}, u32[]{:S(2)}) copy-start(bf16[512,2048]{1,0:T(8,128)(2,1)} %get-tuple-element.95.refs_2_.refs_4_) | copy-start | bytes 6291460
  19.3 22.7 %copy-start.1 = (bf16[512,2048]{1,0:T(8,128)(2,1)S(1)}, bf16[512,2048]{1,0:T(8,128)(2,1)}, u32[]{:S(2)}) copy-start(bf16[512,2048]{1,0:T(8,128)(2,1)} %get-tuple-element.96.refs_3_.refs_5_) | copy-start | bytes 6291460
  31.6 12.8 %copy-start.6 = (bf16[1536,128]{1,0:T(8,128)(2,1)S(1)}, bf16[1536,128]{1,0:T(8,128)(2,1)}, u32[]{:S(2)}) copy-start(bf16[1536,128]{1,0:T(8,128)(2,1)} %get-tuple-element.90) | copy-start | bytes 1179652
  31.6 6.2 %collective-permute-start.4 = (bf16[512,128]{1,0:T(8,128)(2,1)S(1)}, bf16[512,128]{1,0:T(8,128)(2,1)S(1)}, u32[]{:S(2)}, u32[]{:S(2)}) collective-permute-start(bf16[512,128]{1,0:T(8,128)(2,1)S(1)} %get-tuple-element.83), channel_id=1, source_target_pairs={{0,8},{8,0},{16,24},{24,16},{1,9},{9,1},{17,25},{25,17},{2,10},{10... | collective-permute-start | bytes 393224 | tf_op jit(solution)/shard_map/ppermute | solution.py:521
  32.6 7.3 %collective-permute-start.5 = (bf16[512,128]{1,0:T(8,128)(2,1)S(1)}, bf16[512,128]{1,0:T(8,128)(2,1)S(1)}, u32[]{:S(2)}, u32[]{:S(2)}) collective-permute-start(bf16[512,128]{1,0:T(8,128)(2,1)S(1)} %get-tuple-element.84), channel_id=1, source_target_pairs={{0,16},{8,24},{16,0},{24,8},{1,17},{9,25},{17,1},{25,9},{2,18},{10... | collective-permute-start | bytes 393224 | tf_op jit(solution)/shard_map/ppermute | solution.py:521
  33.7 6.2 %collective-permute-start.6 = (bf16[512,128]{1,0:T(8,128)(2,1)S(1)}, bf16[512,128]{1,0:T(8,128)(2,1)S(1)}, u32[]{:S(2)}, u32[]{:S(2)}) collective-permute-start(bf16[512,128]{1,0:T(8,128)(2,1)S(1)} %get-tuple-element.85), channel_id=1, source_target_pairs={{0,24},{8,16},{16,8},{24,0},{1,25},{9,17},{17,9},{25,1},{2,26},{10... | collective-permute-start | bytes 393224 | tf_op jit(solution)/shard_map/ppermute | solution.py:521
  40.0 2.0 %collective-permute-start.10 = (bf16[512,512]{1,0:T(8,128)(2,1)S(1)}, bf16[512,512]{1,0:T(8,128)(2,1)S(1)}, u32[]{:S(2)}, u32[]{:S(2)}) collective-permute-start(bf16[512,512]{1,0:T(8,128)(2,1)S(1)} %assemble.2.refs_0_), channel_id=1, source_target_pairs={{0,1},{1,0},{2,3},{3,2},{4,5},{5,4},{6,7},{7,6},{8,9},{9,8},{10,11... | collective-permute-start | bytes 1572872 | tf_op jit(solution)/shard_map/ppermute | solution.py:521
  42.7 14.8 %collective-permute-start.11 = (bf16[512,512]{1,0:T(8,128)(2,1)S(1)}, bf16[512,512]{1,0:T(8,128)(2,1)S(1)}, u32[]{:S(2)}, u32[]{:S(2)}) collective-permute-start(bf16[512,512]{1,0:T(8,128)(2,1)S(1)} %project.8), channel_id=1, source_target_pairs={{0,2},{1,3},{2,0},{3,1},{4,6},{5,7},{6,4},{7,5},{8,10},{9,11},{10,... | collective-permute-start | bytes 1572872 | tf_op jit(solution)/shard_map/ppermute | solution.py:521
  44.4 13.3 %collective-permute-start.9 = (bf16[1536,128]{1,0:T(8,128)(2,1)S(1)}, bf16[1536,128]{1,0:T(8,128)(2,1)S(1)}, u32[]{:S(2)}, u32[]{:S(2)}) collective-permute-start(bf16[1536,128]{1,0:T(8,128)(2,1)S(1)} %copy-done.6), channel_id=1, source_target_pairs={{0,24},{8,16},{16,8},{24,0},{1,25},{9,17},{17,9},{25,1},{2,26},{10... | collective-permute-start | bytes 1179656 | tf_op jit(solution)/shard_map/ppermute | solution.py:521
  46.8 31.4 %collective-permute-start.15 = (bf16[512,512]{1,0:T(8,128)(2,1)S(1)}, bf16[512,512]{1,0:T(8,128)(2,1)S(1)}, u32[]{:S(2)}, u32[]{:S(2)}) collective-permute-start(bf16[512,512]{1,0:T(8,128)(2,1)S(1)} %project.9), channel_id=1, source_target_pairs={{0,2},{1,3},{2,0},{3,1},{4,6},{5,7},{6,4},{7,5},{8,10},{9,11},{10,... | collective-permute-start | bytes 1572872 | tf_op jit(solution)/shard_map/ppermute | solution.py:521
  57.7 24.6 %collective-permute-start.20 = (bf16[512,512]{1,0:T(8,128)(2,1)S(1)}, bf16[512,512]{1,0:T(8,128)(2,1)S(1)}, u32[]{:S(2)}, u32[]{:S(2)}) collective-permute-start(bf16[512,512]{1,0:T(8,128)(2,1)S(1)} %add_convert_fusion), channel_id=1, source_target_pairs={{0,4},{1,5},{2,6},{3,7},{4,0},{5,1},{6,2},{7,3},{8,12},{9,13},{10,... | collective-permute-start | bytes 1572872 | tf_op jit(solution)/shard_map/ppermute | solution.py:521
  66.5 11.8 %collective-permute-start.12 = (bf16[512,128]{1,0:T(8,128)(2,1)S(1)}, bf16[512,128]{1,0:T(8,128)(2,1)S(1)}, u32[]{:S(2)}, u32[]{:S(2)}) collective-permute-start(bf16[512,128]{1,0:T(8,128)(2,1)S(1)} %get-tuple-element.101), channel_id=1, source_target_pairs={{0,8},{8,0},{16,24},{24,16},{1,9},{9,1},{17,25},{25,17},{2,10},{10... | collective-permute-start | bytes 393224 | tf_op jit(solution)/shard_map/ppermute | solution.py:521
  68.0 10.3 %collective-permute-start.13 = (bf16[512,128]{1,0:T(8,128)(2,1)S(1)}, bf16[512,128]{1,0:T(8,128)(2,1)S(1)}, u32[]{:S(2)}, u32[]{:S(2)}) collective-permute-start(bf16[512,128]{1,0:T(8,128)(2,1)S(1)} %get-tuple-element.102), channel_id=1, source_target_pairs={{0,16},{8,24},{16,0},{24,8},{1,17},{9,25},{17,1},{25,9},{2,18},{10... | collective-permute-start | bytes 393224 | tf_op jit(solution)/shard_map/ppermute | solution.py:521
  68.9 9.4 %collective-permute-start.14 = (bf16[512,128]{1,0:T(8,128)(2,1)S(1)}, bf16[512,128]{1,0:T(8,128)(2,1)S(1)}, u32[]{:S(2)}, u32[]{:S(2)}) collective-permute-start(bf16[512,128]{1,0:T(8,128)(2,1)S(1)} %get-tuple-element.103), channel_id=1, source_target_pairs={{0,24},{8,16},{16,8},{24,0},{1,25},{9,17},{17,9},{25,1},{2,26},{10... | collective-permute-start | bytes 393224 | tf_op jit(solution)/shard_map/ppermute | solution.py:521
  78.4 1.6 %collective-permute-start.16 = (bf16[256,512]{1,0:T(8,128)(2,1)S(1)}, bf16[256,512]{1,0:T(8,128)(2,1)S(1)}, u32[]{:S(2)}, u32[]{:S(2)}) collective-permute-start(bf16[256,512]{1,0:T(8,128)(2,1)S(1)} %get-tuple-element.107.refs_0_), channel_id=1, source_target_pairs={{0,1},{1,0},{2,3},{3,2},{4,5},{5,4},{6,7},{7,6},{8,9},{9,8},{10,11... | collective-permute-start | bytes 786440 | tf_op jit(solution)/shard_map/ppermute | solution.py:521
  78.5 1.9 %collective-permute-start.17 = (bf16[256,512]{1,0:T(8,128)(2,1)S(1)}, bf16[256,512]{1,0:T(8,128)(2,1)S(1)}, u32[]{:S(2)}, u32[]{:S(2)}) collective-permute-start(bf16[256,512]{1,0:T(8,128)(2,1)S(1)} %get-tuple-element.108.refs_1_), channel_id=1, source_target_pairs={{0,1},{1,0},{2,3},{3,2},{4,5},{5,4},{6,7},{7,6},{8,9},{9,8},{10,11... | collective-permute-start | bytes 786440 | tf_op jit(solution)/shard_map/ppermute | solution.py:521
  82.3 12.1 %collective-permute-start.21 = (bf16[256,512]{1,0:T(8,128)(2,1)S(1)}, bf16[256,512]{1,0:T(8,128)(2,1)S(1)}, u32[]{:S(2)}, u32[]{:S(2)}) collective-permute-start(bf16[256,512]{1,0:T(8,128)(2,1)S(1)} %get-tuple-element.117), channel_id=1, source_target_pairs={{0,2},{1,3},{2,0},{3,1},{4,6},{5,7},{6,4},{7,5},{8,10},{9,11},{10,... | collective-permute-start | bytes 786440 | tf_op jit(solution)/shard_map/ppermute | solution.py:521
  83.1 22.5 %collective-permute-start.23 = (bf16[256,512]{1,0:T(8,128)(2,1)S(1)}, bf16[256,512]{1,0:T(8,128)(2,1)S(1)}, u32[]{:S(2)}, u32[]{:S(2)}) collective-permute-start(bf16[256,512]{1,0:T(8,128)(2,1)S(1)} %get-tuple-element.119), channel_id=1, source_target_pairs={{0,2},{1,3},{2,0},{3,1},{4,6},{5,7},{6,4},{7,5},{8,10},{9,11},{10,... | collective-permute-start | bytes 786440 | tf_op jit(solution)/shard_map/ppermute | solution.py:521
  85.0 26.3 %collective-permute-start.18 = (bf16[256,512]{1,0:T(8,128)(2,1)S(1)}, bf16[256,512]{1,0:T(8,128)(2,1)S(1)}, u32[]{:S(2)}, u32[]{:S(2)}) collective-permute-start(bf16[256,512]{1,0:T(8,128)(2,1)S(1)} %get-tuple-element.111), channel_id=1, source_target_pairs={{0,2},{1,3},{2,0},{3,1},{4,6},{5,7},{6,4},{7,5},{8,10},{9,11},{10,... | collective-permute-start | bytes 786440 | tf_op jit(solution)/shard_map/ppermute | solution.py:521
  85.9 29.0 %collective-permute-start.19 = (bf16[256,512]{1,0:T(8,128)(2,1)S(1)}, bf16[256,512]{1,0:T(8,128)(2,1)S(1)}, u32[]{:S(2)}, u32[]{:S(2)}) collective-permute-start(bf16[256,512]{1,0:T(8,128)(2,1)S(1)} %get-tuple-element.112), channel_id=1, source_target_pairs={{0,2},{1,3},{2,0},{3,1},{4,6},{5,7},{6,4},{7,5},{8,10},{9,11},{10,... | collective-permute-start | bytes 786440 | tf_op jit(solution)/shard_map/ppermute | solution.py:521
  94.4 20.5 %collective-permute-start.22 = (bf16[256,512]{1,0:T(8,128)(2,1)S(1)}, bf16[256,512]{1,0:T(8,128)(2,1)S(1)}, u32[]{:S(2)}, u32[]{:S(2)}) collective-permute-start(bf16[256,512]{1,0:T(8,128)(2,1)S(1)} %add_convert_fusion.2), channel_id=1, source_target_pairs={{0,4},{1,5},{2,6},{3,7},{4,0},{5,1},{6,2},{7,3},{8,12},{9,13},{10,... | collective-permute-start | bytes 786440 | tf_op jit(solution)/shard_map/ppermute | solution.py:521
  105.6 15.2 %collective-permute-start.24 = (bf16[256,512]{1,0:T(8,128)(2,1)S(1)}, bf16[256,512]{1,0:T(8,128)(2,1)S(1)}, u32[]{:S(2)}, u32[]{:S(2)}) collective-permute-start(bf16[256,512]{1,0:T(8,128)(2,1)S(1)} %add_convert_fusion.1), channel_id=1, source_target_pairs={{0,4},{1,5},{2,6},{3,7},{4,0},{5,1},{6,2},{7,3},{8,12},{9,13},{10,... | collective-permute-start | bytes 786440 | tf_op jit(solution)/shard_map/ppermute | solution.py:521

commit v14 on v13

--- a/solution.py
+++ b/solution.py
@@ -340,7 +340,7 @@
                 largest = jnp.max(scores, axis=0, keepdims=True)
                 largest_buf[lane][slot, 0:1, :] = largest
                 summed[lane][slot] = weighted(jnp.exp2(scores - largest), offset)
-                first = jnp.min(start).astype(jnp.int32) // TILE
+                first = start[0, 0].astype(jnp.int32) // TILE
                 firsts.append(first)
                 counts.append(end - first)
 
@@ -389,10 +389,10 @@
         for lane in range(group):
             for slot in range(per_block):
                 state = summed[lane]
-                attended = state[slot, :HD, :] / state[slot, HD : HD + 1, :]
+                attended = state[slot, :HD, :] * (1.0 / state[slot, HD : HD + 1, :])
                 out = outs[lane ^ (slot * (group - 1))]
-                out[slot * TILE : (slot + 1) * TILE, :] = jnp.transpose(attended).astype(
-                    jnp.bfloat16
+                out[slot * TILE : (slot + 1) * TILE, :] = jnp.transpose(
+                    attended.astype(jnp.bfloat16)
                 )
 
     def own(upper):
@@ -577,13 +577,14 @@
     across = to_next(passed, 2)
     pieces = attend(ctx_index, queries, keys, values, docs, low, high)
     back = send_back(pieces)
-    back, near_sum = tie(back, near_sum)
     late = shares_of(assemble(ctx_index, [pieces[0], *back], 2))
-    late[0], across = tie(late[0], across)
+    late[0], near_sum, across = tie(late[0], near_sum, across)
     result = finish(0, [shares[3], near_sum, across], None)
     far = to_next(late[0], 1)
+    passed = [add(*both) for both in zip(late[2], far)]
+    across = to_next(passed, 2)
+    late[1], passed = tie(late[1], passed)
     near_sum = to_next(late[1], 1)
-    across = to_next([add(*both) for both in zip(late[2], far)], 2)
     return finish(1, [late[3], near_sum, across], result)
 
 

time: 122 us -> 118 us (0.967)
  waiting for transfers between devices: 60.8 us -> 57.8 us
  Pallas kernels: 30.2 us -> 28.9 us
    ppermute x25, waiting for transfers between devices: 60.8 us -> 57.8 us  [swap(): lax.ppermute(value, axis, [(source, source ^ distance) for source in rang...]
    pallas_call x2, Pallas kernels: 11.5 us -> 10.2 us  [attend(): pl.pallas_call(kernel, grid_spec=pltpu.PrefetchScalarGridSpec(num_scalar_...]
  transfers between devices with their start and end apart: 25 -> 25, of which waited for: 14 -> 16; matrix products, arithmetic and copies ran while one was open for 1% -> 1% of each run, Pallas kernels for 23% -> 23%
where the time goes in v14:
time: 118 us; the launch traced here: 117 us
  waiting for transfers between devices  57.8 us (49%)
  starting transfers between devices  29.3 us (25%)
  Pallas kernels  28.9 us (24%)
    ppermute x25, waiting for transfers between devices, swap(): lax.ppermute(value, axis, [(source, source ^ distance) for source in rang...  57.8 us
    ppermute x25, starting transfers between devices, swap(): lax.ppermute(value, axis, [(source, source ^ distance) for source in rang...  29.3 us
    pallas_call x2, Pallas kernels, attend(): pl.pallas_call(kernel, grid_spec=pltpu.PrefetchScalarGridSpec(num_scalar_...  10.2 us
    pallas_call x1, Pallas kernels, pack_projection(): pl.pallas_call(kernel, grid_spec=pltpu.PrefetchScalarGridSpec(num_scalar_...  5.74 us
    pallas_call x8, Pallas kernels, project(): pl.pallas_call(kernel, grid=(1,), in_specs=[attended] * (2 * parts) + [we...  5.69 us
    pallas_call x2, Pallas kernels, pack(): pl.pallas_call(kernel, grid_spec=pltpu.PrefetchScalarGridSpec(num_scalar_...  5.02 us
  transfers between devices with their start and end apart: 25, of which 16 were waited for; matrix products, arithmetic and copies ran while one was open for 1% of the time, Pallas kernels for 23%

profile of v14, /device:TPU:0, one launch (start us, length us, event | category | flops | bytes accessed | tf_op | source)
XLA Modules:
  0.0 116.9 jit_solution(10090678463759983434)
XLA Ops:
  0.0 0.5 collective-permute-start.3
  0.5 2.5 %pack.2 = (bf16[1552,128]{1,0:T(8,128)(2,1)}, bf16[1552,128]{1,0:T(8,128)(2,1)}, bf16[1552,128]{1,0:T(8,128)(2,1)}) custom-call(s32[1]{0:T(128)} %bitcast.ctx_ref, bf16[1024,512]{1,0:T(8,128)(2,1)} %refs_3_.4, bf16[1024,512]{1,0:T(8,128)(2,1)} %refs_4_.4, bf16[1024,512]{1,0:T(8,128)(2,1)} %refs_5_.4, bf16[1024,512]{1,0:T(8,128)(2,1)} %refs_3_.4, ...), custom_call_target="tpu_custom_call" | custom-call | flops 1024 | bytes 1024 | tf_op jit(solution)/shard_map/pack/pallas_call | solution.py:201
  2.9 2.5 %collective-permute-start = (bf16[1552,128]{1,0:T(8,128)(2,1)}, bf16[1552,128]{1,0:T(8,128)(2,1)S(1)}, u32[]{:S(2)}, u32[]{:S(2)}) collective-permute-start(bf16[1552,128]{1,0:T(8,128)(2,1)} %get-tuple-element.66), channel_id=1, source_target_pairs={{0,8},{8,0},{16,24},{24,16},{1,9},{9,1},{17,25},{25,17},{2,10},{10... | collective-permute-start | bytes 1191944 | tf_op jit(solution)/shard_map/ppermute | solution.py:521
  5.4 1.5 %collective-permute-start.1 = (bf16[1552,128]{1,0:T(8,128)(2,1)}, bf16[1552,128]{1,0:T(8,128)(2,1)S(1)}, u32[]{:S(2)}, u32[]{:S(2)}) collective-permute-start(bf16[1552,128]{1,0:T(8,128)(2,1)} %get-tuple-element.67), channel_id=1, source_target_pairs={{0,16},{8,24},{16,0},{24,8},{1,17},{9,25},{17,1},{25,9},{2,18},{10... | collective-permute-start | bytes 1191944 | tf_op jit(solution)/shard_map/ppermute | solution.py:521
  7.0 0.0 collective-permute-start.2
  7.0 2.5 %pack.3 = (bf16[1536,128]{1,0:T(8,128)(2,1)}, bf16[1536,128]{1,0:T(8,128)(2,1)}, bf16[1536,128]{1,0:T(8,128)(2,1)}) custom-call(s32[1]{0:T(128)} %bitcast.ctx_ref, bf16[1024,512]{1,0:T(8,128)(2,1)} %refs_3_.4, bf16[1024,512]{1,0:T(8,128)(2,1)} %refs_4_.4, bf16[1024,512]{1,0:T(8,128)(2,1)} %refs_5_.4, bf16[1024,512]{1,0:T(8,128)(2,1)} %refs_3_.4, ...), custom_call_target="tpu_custom_call" | custom-call | flops 1024 | bytes 1024 | tf_op jit(solution)/shard_map/pack/pallas_call | solution.py:201
  9.5 2.0 %collective-permute-start.7 = (bf16[1536,128]{1,0:T(8,128)(2,1)}, bf16[1536,128]{1,0:T(8,128)(2,1)S(1)}, u32[]{:S(2)}, u32[]{:S(2)}) collective-permute-start(bf16[1536,128]{1,0:T(8,128)(2,1)} %get-tuple-element.85), channel_id=1, source_target_pairs={{0,8},{8,0},{16,24},{24,16},{1,9},{9,1},{17,25},{25,17},{2,10},{10... | collective-permute-start | bytes 1179656 | tf_op jit(solution)/shard_map/ppermute | solution.py:521
  11.5 0.0 collective-permute-done.3.sibling_in
  11.5 1.5 %collective-permute-start.8 = (bf16[1536,128]{1,0:T(8,128)(2,1)}, bf16[1536,128]{1,0:T(8,128)(2,1)S(1)}, u32[]{:S(2)}, u32[]{:S(2)}) collective-permute-start(bf16[1536,128]{1,0:T(8,128)(2,1)} %get-tuple-element.86), channel_id=1, source_target_pairs={{0,16},{8,24},{16,0},{24,8},{1,17},{9,25},{17,1},{25,9},{2,18},{10... | collective-permute-start | bytes 1179656 | tf_op jit(solution)/shard_map/ppermute | solution.py:521
  13.0 0.5 broadcast_xor_fusion.places_ref
  13.5 5.7 %pack_projection.1 = (bf16[512,2048]{1,0:T(8,128)(2,1)}, bf16[512,2048]{1,0:T(8,128)(2,1)}) custom-call(s32[4]{0:T(128)} %broadcast_xor_fusion.places_ref, bf16[512,4096]{1,0:T(8,128)(2,1)} %mine_in.1, bf16[512,4096]{1,0:T(8,128)(2,1)} %collective-permute-done.3.sibling_in), custom_call_target="tpu_custom_call" | custom-call | flops 1024 | bytes 1024 | tf_op jit(solution)/shard_map/pack_projection/pallas_call | solution.py:227
  19.3 0.0 collective-permute-done.refs_4_.refs_7_
  19.3 6.9 %collective-permute-done.1.refs_5_.refs_8_ = bf16[1552,128]{1,0:T(8,128)(2,1)S(1)} collective-permute-done((bf16[1552,128]{1,0:T(8,128)(2,1)}, bf16[1552,128]{1,0:T(8,128)(2,1)S(1)}, u32[]{:S(2)}, u32[]{:S(2)}) %collective-permute-start.1) | collective-permute-done | bytes 397344 | tf_op jit(solution)/shard_map/ppermute | solution.py:521
  26.2 5.4 %attend_low.1 = (bf16[512,128]{1,0:T(8,128)(2,1)S(1)}, bf16[512,128]{1,0:T(8,128)(2,1)S(1)}, bf16[512,128]{1,0:T(8,128)(2,1)S(1)}, bf16[512,128]{1,0:T(8,128)(2,1)S(1)}) custom-call(s32[1]{0:T(128)} %bitcast.ctx_ref, bf16[1024,512]{1,0:T(8,128)(2,1)S(1)} %copy-done.2, bf16[1024,512]{1,0:T(8,128)(2,1)S(1)} %copy-done.3, bf16[1024,512]{1,0:T(8,128)(2,1)S(1)} %copy-done.4, ...), custom_call_target="tpu_custom_call" | custom-call | flops 1024 | bytes 1024 | tf_op jit(solution)/shard_map/attend_low/pallas_call | solution.py:409
  31.6 1.0 collective-permute-start.4
  32.6 1.1 collective-permute-start.5
  33.7 1.4 %collective-permute-start.6 = (bf16[512,128]{1,0:T(8,128)(2,1)S(1)}, bf16[512,128]{1,0:T(8,128)(2,1)S(1)}, u32[]{:S(2)}, u32[]{:S(2)}) collective-permute-start(bf16[512,128]{1,0:T(8,128)(2,1)S(1)} %get-tuple-element.84), channel_id=1, source_target_pairs={{0,24},{8,16},{16,8},{24,0},{1,25},{9,17},{17,9},{25,1},{2,26},{10... | collective-permute-start | bytes 393224 | tf_op jit(solution)/shard_map/ppermute | solution.py:521
  35.2 2.6 %collective-permute-done.4.refs_1_ = bf16[512,128]{1,0:T(8,128)(2,1)S(1)} collective-permute-done((bf16[512,128]{1,0:T(8,128)(2,1)S(1)}, bf16[512,128]{1,0:T(8,128)(2,1)S(1)}, u32[]{:S(2)}, u32[]{:S(2)}) %collective-permute-start.4) | collective-permute-done | bytes 131104 | tf_op jit(solution)/shard_map/ppermute | solution.py:521
  37.8 2.1 %collective-permute-done.5.refs_2_ = bf16[512,128]{1,0:T(8,128)(2,1)S(1)} collective-permute-done((bf16[512,128]{1,0:T(8,128)(2,1)S(1)}, bf16[512,128]{1,0:T(8,128)(2,1)S(1)}, u32[]{:S(2)}, u32[]{:S(2)}) %collective-permute-start.5) | collective-permute-done | bytes 131104 | tf_op jit(solution)/shard_map/ppermute | solution.py:521
  39.9 0.1 assemble.2.refs_0_
  40.0 0.1 collective-permute-start.10
  40.1 1.9 %collective-permute-done.10.refs_1_ = bf16[512,512]{1,0:T(8,128)(2,1)S(1)} collective-permute-done((bf16[512,512]{1,0:T(8,128)(2,1)S(1)}, bf16[512,512]{1,0:T(8,128)(2,1)S(1)}, u32[]{:S(2)}, u32[]{:S(2)}) %collective-permute-start.10) | collective-permute-done | bytes 524320 | tf_op jit(solution)/shard_map/ppermute | solution.py:521
  42.0 0.7 project.8
  42.7 1.6 %collective-permute-start.11 = (bf16[512,512]{1,0:T(8,128)(2,1)S(1)}, bf16[512,512]{1,0:T(8,128)(2,1)S(1)}, u32[]{:S(2)}, u32[]{:S(2)}) collective-permute-start(bf16[512,512]{1,0:T(8,128)(2,1)S(1)} %project.8), channel_id=1, source_target_pairs={{0,2},{1,3},{2,0},{3,1},{4,6},{5,7},{6,4},{7,5},{8,10},{9,11},{10,... | collective-permute-start | bytes 1572872 | tf_op jit(solution)/shard_map/ppermute | solution.py:521
  44.3 1.8 %collective-permute-start.9 = (bf16[1536,128]{1,0:T(8,128)(2,1)S(1)}, bf16[1536,128]{1,0:T(8,128)(2,1)S(1)}, u32[]{:S(2)}, u32[]{:S(2)}) collective-permute-start(bf16[1536,128]{1,0:T(8,128)(2,1)S(1)} %copy-done.6), channel_id=1, source_target_pairs={{0,24},{8,16},{16,8},{24,0},{1,25},{9,17},{17,9},{25,1},{2,26},{10... | collective-permute-start | bytes 1179656 | tf_op jit(solution)/shard_map/ppermute | solution.py:521
  46.1 0.7 project.9
  46.8 0.5 collective-permute-start.17
  47.3 0.7 project.10
  48.1 0.7 project.11.refs_0_
  48.8 8.8 %collective-permute-done.11 = bf16[512,512]{1,0:T(8,128)(2,1)S(1)} collective-permute-done((bf16[512,512]{1,0:T(8,128)(2,1)S(1)}, bf16[512,512]{1,0:T(8,128)(2,1)S(1)}, u32[]{:S(2)}, u32[]{:S(2)}) %collective-permute-start.11) | collective-permute-done | bytes 524320 | tf_op jit(solution)/shard_map/ppermute | solution.py:521
  57.5 0.1 add_convert_fusion
  57.7 2.7 %collective-permute-start.18 = (bf16[512,512]{1,0:T(8,128)(2,1)S(1)}, bf16[512,512]{1,0:T(8,128)(2,1)S(1)}, u32[]{:S(2)}, u32[]{:S(2)}) collective-permute-start(bf16[512,512]{1,0:T(8,128)(2,1)S(1)} %add_convert_fusion), channel_id=1, source_target_pairs={{0,4},{1,5},{2,6},{3,7},{4,0},{5,1},{6,2},{7,3},{8,12},{9,13},{10,... | collective-permute-start | bytes 1572872 | tf_op jit(solution)/shard_map/ppermute | solution.py:521
  60.3 4.9 %attend_high.1 = (bf16[512,128]{1,0:T(8,128)(2,1)S(1)}, bf16[512,128]{1,0:T(8,128)(2,1)S(1)}, bf16[512,128]{1,0:T(8,128)(2,1)S(1)}, bf16[512,128]{1,0:T(8,128)(2,1)S(1)}) custom-call(s32[1]{0:T(128)} %bitcast.ctx_ref, bf16[1024,512]{1,0:T(8,128)(2,1)S(1)} %copy-done.2, bf16[1024,512]{1,0:T(8,128)(2,1)S(1)} %copy-done.3, bf16[1024,512]{1,0:T(8,128)(2,1)S(1)} %copy-done.4, ...), custom_call_target="tpu_custom_call" | custom-call | flops 1024 | bytes 1024 | tf_op jit(solution)/shard_map/attend_high/pallas_call | solution.py:409
  65.2 1.4 %collective-permute-start.12 = (bf16[512,128]{1,0:T(8,128)(2,1)S(1)}, bf16[512,128]{1,0:T(8,128)(2,1)S(1)}, u32[]{:S(2)}, u32[]{:S(2)}) collective-permute-start(bf16[512,128]{1,0:T(8,128)(2,1)S(1)} %get-tuple-element.100), channel_id=1, source_target_pairs={{0,8},{8,0},{16,24},{24,16},{1,9},{9,1},{17,25},{25,17},{2,10},{10... | collective-permute-start | bytes 393224 | tf_op jit(solution)/shard_map/ppermute | solution.py:521
  66.6 1.0 collective-permute-start.13
  67.6 1.1 collective-permute-start.14
  68.8 2.4 %collective-permute-done.12.refs_1_ = bf16[512,128]{1,0:T(8,128)(2,1)S(1)} collective-permute-done((bf16[512,128]{1,0:T(8,128)(2,1)S(1)}, bf16[512,128]{1,0:T(8,128)(2,1)S(1)}, u32[]{:S(2)}, u32[]{:S(2)}) %collective-permute-start.12) | collective-permute-done | bytes 131104 | tf_op jit(solution)/shard_map/ppermute | solution.py:521
  71.2 0.7 collective-permute-done.13.refs_2_
  71.8 1.6 %collective-permute-done.14.refs_3_ = bf16[512,128]{1,0:T(8,128)(2,1)S(1)} collective-permute-done((bf16[512,128]{1,0:T(8,128)(2,1)S(1)}, bf16[512,128]{1,0:T(8,128)(2,1)S(1)}, u32[]{:S(2)}, u32[]{:S(2)}) %collective-permute-start.14) | collective-permute-done | bytes 131104 | tf_op jit(solution)/shard_map/ppermute | solution.py:521
  73.5 0.1 assemble.3
  73.6 0.1 collective-permute-start.15
  73.7 0.5 collective-permute-start.16
  74.2 1.0 collective-permute-done.15.refs_2_
  75.2 0.4 collective-permute-done.16.refs_3_
  75.6 0.7 project.15
  76.3 2.0 %collective-permute-done.17.refs_1_ = bf16[512,512]{1,0:T(8,128)(2,1)S(1)} collective-permute-done((bf16[512,512]{1,0:T(8,128)(2,1)S(1)}, bf16[512,512]{1,0:T(8,128)(2,1)S(1)}, u32[]{:S(2)}, u32[]{:S(2)}) %collective-permute-start.17) | collective-permute-done | bytes 524320 | tf_op jit(solution)/shard_map/ppermute | solution.py:521
  78.3 4.0 %collective-permute-done.18.refs_2_ = bf16[512,512]{1,0:T(8,128)(2,1)S(1)} collective-permute-done((bf16[512,512]{1,0:T(8,128)(2,1)S(1)}, bf16[512,512]{1,0:T(8,128)(2,1)S(1)}, u32[]{:S(2)}, u32[]{:S(2)}) %collective-permute-start.18) | collective-permute-done | bytes 524320 | tf_op jit(solution)/shard_map/ppermute | solution.py:521
  82.3 0.8 collective-permute-start.19
  83.0 1.3 %collective-permute-start.20 = (bf16[256,512]{1,0:T(8,128)(2,1)S(1)}, bf16[256,512]{1,0:T(8,128)(2,1)S(1)}, u32[]{:S(2)}, u32[]{:S(2)}) collective-permute-start(bf16[256,512]{1,0:T(8,128)(2,1)S(1)} %get-tuple-element.115), channel_id=1, source_target_pairs={{0,2},{1,3},{2,0},{3,1},{4,6},{5,7},{6,4},{7,5},{8,10},{9,11},{10,... | collective-permute-start | bytes 786440 | tf_op jit(solution)/shard_map/ppermute | solution.py:521
  84.3 0.7 project.13
  85.0 0.7 project.14
  85.7 4.9 %collective-permute-done.19 = bf16[256,512]{1,0:T(8,128)(2,1)S(1)} collective-permute-done((bf16[256,512]{1,0:T(8,128)(2,1)S(1)}, bf16[256,512]{1,0:T(8,128)(2,1)S(1)}, u32[]{:S(2)}, u32[]{:S(2)}) %collective-permute-start.19) | collective-permute-done | bytes 262176 | tf_op jit(solution)/shard_map/ppermute | solution.py:521
  90.7 0.1 add_convert_fusion.2
  90.7 3.0 %collective-permute-done.20 = bf16[256,512]{1,0:T(8,128)(2,1)S(1)} collective-permute-done((bf16[256,512]{1,0:T(8,128)(2,1)S(1)}, bf16[256,512]{1,0:T(8,128)(2,1)S(1)}, u32[]{:S(2)}, u32[]{:S(2)}) %collective-permute-start.20) | collective-permute-done | bytes 262176 | tf_op jit(solution)/shard_map/ppermute | solution.py:521
  93.8 0.1 add_convert_fusion.1
  93.8 1.3 %collective-permute-start.21 = (bf16[256,512]{1,0:T(8,128)(2,1)S(1)}, bf16[256,512]{1,0:T(8,128)(2,1)S(1)}, u32[]{:S(2)}, u32[]{:S(2)}) collective-permute-start(bf16[256,512]{1,0:T(8,128)(2,1)S(1)} %get-tuple-element.116), channel_id=1, source_target_pairs={{0,2},{1,3},{2,0},{3,1},{4,6},{5,7},{6,4},{7,5},{8,10},{9,11},{10,... | collective-permute-start | bytes 786440 | tf_op jit(solution)/shard_map/ppermute | solution.py:521
  95.1 0.8 collective-permute-start.22
  95.9 2.6 %collective-permute-start.23 = (bf16[256,512]{1,0:T(8,128)(2,1)S(1)}, bf16[256,512]{1,0:T(8,128)(2,1)S(1)}, u32[]{:S(2)}, u32[]{:S(2)}) collective-permute-start(bf16[256,512]{1,0:T(8,128)(2,1)S(1)} %add_convert_fusion.2), channel_id=1, source_target_pairs={{0,4},{1,5},{2,6},{3,7},{4,0},{5,1},{6,2},{7,3},{8,12},{9,13},{10,... | collective-permute-start | bytes 786440 | tf_op jit(solution)/shard_map/ppermute | solution.py:521
  98.6 0.3 collective-permute-start.24
  98.9 0.7 project.12
  99.6 1.0 finish.2.refs_6_
  100.6 12.0 %collective-permute-done.21.refs_2_ = bf16[256,512]{1,0:T(8,128)(2,1)S(1)} collective-permute-done((bf16[256,512]{1,0:T(8,128)(2,1)S(1)}, bf16[256,512]{1,0:T(8,128)(2,1)S(1)}, u32[]{:S(2)}, u32[]{:S(2)}) %collective-permute-start.21) | collective-permute-done | bytes 262176 | tf_op jit(solution)/shard_map/ppermute | solution.py:521
  112.6 3.4 %collective-permute-done.22.refs_3_ = bf16[256,512]{1,0:T(8,128)(2,1)S(1)} collective-permute-done((bf16[256,512]{1,0:T(8,128)(2,1)S(1)}, bf16[256,512]{1,0:T(8,128)(2,1)S(1)}, u32[]{:S(2)}, u32[]{:S(2)}) %collective-permute-start.22) | collective-permute-done | bytes 262176 | tf_op jit(solution)/shard_map/ppermute | solution.py:521
  116.0 1.0 finish.3
  (23 shorter events, 0.0 us)
Async XLA Ops:
  0.0 11.5 %collective-permute-start.3 = (bf16[512,4096]{1,0:T(8,128)(2,1)}, bf16[512,4096]{1,0:T(8,128)(2,1)}, u32[]{:S(2)}, u32[]{:S(2)}) collective-permute-start(bf16[512,4096]{1,0:T(8,128)(2,1)} %mine_in.1), channel_id=1, source_target_pairs={{0,1},{1,0},{2,3},{3,2},{4,5},{5,4},{6,7},{7,6},{8,9},{9,8},{10,11... | collective-permute-start | bytes 12582920 | tf_op jit(solution)/shard_map/ppermute | solution.py:521
  2.9 10.0 %copy-start.7 = (s32[4]{0:T(128)S(1)}, s32[4]{0:T(128)}, u32[]{:S(2)}) copy-start(s32[4]{0:T(128)} %constant.13) | copy-start | bytes 52
  2.9 16.3 %collective-permute-start = (bf16[1552,128]{1,0:T(8,128)(2,1)}, bf16[1552,128]{1,0:T(8,128)(2,1)S(1)}, u32[]{:S(2)}, u32[]{:S(2)}) collective-permute-start(bf16[1552,128]{1,0:T(8,128)(2,1)} %get-tuple-element.66), channel_id=1, source_target_pairs={{0,8},{8,0},{16,24},{24,16},{1,9},{9,1},{17,25},{25,17},{2,10},{10... | collective-permute-start | bytes 1191944 | tf_op jit(solution)/shard_map/ppermute | solution.py:521
  5.4 20.8 %collective-permute-start.1 = (bf16[1552,128]{1,0:T(8,128)(2,1)}, bf16[1552,128]{1,0:T(8,128)(2,1)S(1)}, u32[]{:S(2)}, u32[]{:S(2)}) collective-permute-start(bf16[1552,128]{1,0:T(8,128)(2,1)} %get-tuple-element.67), channel_id=1, source_target_pairs={{0,16},{8,24},{16,0},{24,8},{1,17},{9,25},{17,1},{25,9},{2,18},{10... | collective-permute-start | bytes 1191944 | tf_op jit(solution)/shard_map/ppermute | solution.py:521
  7.0 19.2 %collective-permute-start.2 = (bf16[1552,128]{1,0:T(8,128)(2,1)}, bf16[1552,128]{1,0:T(8,128)(2,1)S(1)}, u32[]{:S(2)}, u32[]{:S(2)}) collective-permute-start(bf16[1552,128]{1,0:T(8,128)(2,1)} %get-tuple-element.68), channel_id=1, source_target_pairs={{0,24},{8,16},{16,8},{24,0},{1,25},{9,17},{17,9},{25,1},{2,26},{10... | collective-permute-start | bytes 1191944 | tf_op jit(solution)/shard_map/ppermute | solution.py:521
  9.5 25.6 %collective-permute-start.7 = (bf16[1536,128]{1,0:T(8,128)(2,1)}, bf16[1536,128]{1,0:T(8,128)(2,1)S(1)}, u32[]{:S(2)}, u32[]{:S(2)}) collective-permute-start(bf16[1536,128]{1,0:T(8,128)(2,1)} %get-tuple-element.85), channel_id=1, source_target_pairs={{0,8},{8,0},{16,24},{24,16},{1,9},{9,1},{17,25},{25,17},{2,10},{10... | collective-permute-start | bytes 1179656 | tf_op jit(solution)/shard_map/ppermute | solution.py:521
  11.5 23.7 %collective-permute-start.8 = (bf16[1536,128]{1,0:T(8,128)(2,1)}, bf16[1536,128]{1,0:T(8,128)(2,1)S(1)}, u32[]{:S(2)}, u32[]{:S(2)}) collective-permute-start(bf16[1536,128]{1,0:T(8,128)(2,1)} %get-tuple-element.86), channel_id=1, source_target_pairs={{0,16},{8,24},{16,0},{24,8},{1,17},{9,25},{17,1},{25,9},{2,18},{10... | collective-permute-start | bytes 1179656 | tf_op jit(solution)/shard_map/ppermute | solution.py:521
  13.5 12.7 %copy-start.2 = (bf16[1024,512]{1,0:T(8,128)(2,1)S(1)}, bf16[1024,512]{1,0:T(8,128)(2,1)}, u32[]{:S(2)}) copy-start(bf16[1024,512]{1,0:T(8,128)(2,1)} %refs_3_.4) | copy-start | bytes 3145732
  13.5 12.7 %copy-start.3 = (bf16[1024,512]{1,0:T(8,128)(2,1)S(1)}, bf16[1024,512]{1,0:T(8,128)(2,1)}, u32[]{:S(2)}) copy-start(bf16[1024,512]{1,0:T(8,128)(2,1)} %refs_4_.4) | copy-start | bytes 3145732
  13.5 12.7 %copy-start.4 = (bf16[1024,512]{1,0:T(8,128)(2,1)S(1)}, bf16[1024,512]{1,0:T(8,128)(2,1)}, u32[]{:S(2)}) copy-start(bf16[1024,512]{1,0:T(8,128)(2,1)} %refs_5_.4) | copy-start | bytes 3145732
  13.5 12.7 %copy-start.5 = (s32[1024]{0:T(1024)S(1)}, s32[1024]{0:T(1024)}, u32[]{:S(2)}) copy-start(s32[1024]{0:T(1024)} %param.9) | copy-start | bytes 12292
  19.3 22.7 %copy-start = (bf16[512,2048]{1,0:T(8,128)(2,1)S(1)}, bf16[512,2048]{1,0:T(8,128)(2,1)}, u32[]{:S(2)}) copy-start(bf16[512,2048]{1,0:T(8,128)(2,1)} %get-tuple-element.94.refs_2_.refs_4_) | copy-start | bytes 6291460
  19.3 22.7 %copy-start.1 = (bf16[512,2048]{1,0:T(8,128)(2,1)S(1)}, bf16[512,2048]{1,0:T(8,128)(2,1)}, u32[]{:S(2)}) copy-start(bf16[512,2048]{1,0:T(8,128)(2,1)} %get-tuple-element.95.refs_3_.refs_5_) | copy-start | bytes 6291460
  31.6 12.7 %copy-start.6 = (bf16[1536,128]{1,0:T(8,128)(2,1)S(1)}, bf16[1536,128]{1,0:T(8,128)(2,1)}, u32[]{:S(2)}) copy-start(bf16[1536,128]{1,0:T(8,128)(2,1)} %get-tuple-element.89) | copy-start | bytes 1179652
  31.6 6.2 %collective-permute-start.4 = (bf16[512,128]{1,0:T(8,128)(2,1)S(1)}, bf16[512,128]{1,0:T(8,128)(2,1)S(1)}, u32[]{:S(2)}, u32[]{:S(2)}) collective-permute-start(bf16[512,128]{1,0:T(8,128)(2,1)S(1)} %get-tuple-element.82), channel_id=1, source_target_pairs={{0,8},{8,0},{16,24},{24,16},{1,9},{9,1},{17,25},{25,17},{2,10},{10... | collective-permute-start | bytes 393224 | tf_op jit(solution)/shard_map/ppermute | solution.py:521
  32.6 7.3 %collective-permute-start.5 = (bf16[512,128]{1,0:T(8,128)(2,1)S(1)}, bf16[512,128]{1,0:T(8,128)(2,1)S(1)}, u32[]{:S(2)}, u32[]{:S(2)}) collective-permute-start(bf16[512,128]{1,0:T(8,128)(2,1)S(1)} %get-tuple-element.83), channel_id=1, source_target_pairs={{0,16},{8,24},{16,0},{24,8},{1,17},{9,25},{17,1},{25,9},{2,18},{10... | collective-permute-start | bytes 393224 | tf_op jit(solution)/shard_map/ppermute | solution.py:521
  33.7 6.2 %collective-permute-start.6 = (bf16[512,128]{1,0:T(8,128)(2,1)S(1)}, bf16[512,128]{1,0:T(8,128)(2,1)S(1)}, u32[]{:S(2)}, u32[]{:S(2)}) collective-permute-start(bf16[512,128]{1,0:T(8,128)(2,1)S(1)} %get-tuple-element.84), channel_id=1, source_target_pairs={{0,24},{8,16},{16,8},{24,0},{1,25},{9,17},{17,9},{25,1},{2,26},{10... | collective-permute-start | bytes 393224 | tf_op jit(solution)/shard_map/ppermute | solution.py:521
  40.0 2.0 %collective-permute-start.10 = (bf16[512,512]{1,0:T(8,128)(2,1)S(1)}, bf16[512,512]{1,0:T(8,128)(2,1)S(1)}, u32[]{:S(2)}, u32[]{:S(2)}) collective-permute-start(bf16[512,512]{1,0:T(8,128)(2,1)S(1)} %assemble.2.refs_0_), channel_id=1, source_target_pairs={{0,1},{1,0},{2,3},{3,2},{4,5},{5,4},{6,7},{7,6},{8,9},{9,8},{10,11... | collective-permute-start | bytes 1572872 | tf_op jit(solution)/shard_map/ppermute | solution.py:521
  42.7 14.8 %collective-permute-start.11 = (bf16[512,512]{1,0:T(8,128)(2,1)S(1)}, bf16[512,512]{1,0:T(8,128)(2,1)S(1)}, u32[]{:S(2)}, u32[]{:S(2)}) collective-permute-start(bf16[512,512]{1,0:T(8,128)(2,1)S(1)} %project.8), channel_id=1, source_target_pairs={{0,2},{1,3},{2,0},{3,1},{4,6},{5,7},{6,4},{7,5},{8,10},{9,11},{10,... | collective-permute-start | bytes 1572872 | tf_op jit(solution)/shard_map/ppermute | solution.py:521
  44.3 13.3 %collective-permute-start.9 = (bf16[1536,128]{1,0:T(8,128)(2,1)S(1)}, bf16[1536,128]{1,0:T(8,128)(2,1)S(1)}, u32[]{:S(2)}, u32[]{:S(2)}) collective-permute-start(bf16[1536,128]{1,0:T(8,128)(2,1)S(1)} %copy-done.6), channel_id=1, source_target_pairs={{0,24},{8,16},{16,8},{24,0},{1,25},{9,17},{17,9},{25,1},{2,26},{10... | collective-permute-start | bytes 1179656 | tf_op jit(solution)/shard_map/ppermute | solution.py:521
  46.8 31.4 %collective-permute-start.17 = (bf16[512,512]{1,0:T(8,128)(2,1)S(1)}, bf16[512,512]{1,0:T(8,128)(2,1)S(1)}, u32[]{:S(2)}, u32[]{:S(2)}) collective-permute-start(bf16[512,512]{1,0:T(8,128)(2,1)S(1)} %project.9), channel_id=1, source_target_pairs={{0,2},{1,3},{2,0},{3,1},{4,6},{5,7},{6,4},{7,5},{8,10},{9,11},{10,... | collective-permute-start | bytes 1572872 | tf_op jit(solution)/shard_map/ppermute | solution.py:521
  57.7 24.6 %collective-permute-start.18 = (bf16[512,512]{1,0:T(8,128)(2,1)S(1)}, bf16[512,512]{1,0:T(8,128)(2,1)S(1)}, u32[]{:S(2)}, u32[]{:S(2)}) collective-permute-start(bf16[512,512]{1,0:T(8,128)(2,1)S(1)} %add_convert_fusion), channel_id=1, source_target_pairs={{0,4},{1,5},{2,6},{3,7},{4,0},{5,1},{6,2},{7,3},{8,12},{9,13},{10,... | collective-permute-start | bytes 1572872 | tf_op jit(solution)/shard_map/ppermute | solution.py:521
  65.2 6.0 %collective-permute-start.12 = (bf16[512,128]{1,0:T(8,128)(2,1)S(1)}, bf16[512,128]{1,0:T(8,128)(2,1)S(1)}, u32[]{:S(2)}, u32[]{:S(2)}) collective-permute-start(bf16[512,128]{1,0:T(8,128)(2,1)S(1)} %get-tuple-element.100), channel_id=1, source_target_pairs={{0,8},{8,0},{16,24},{24,16},{1,9},{9,1},{17,25},{25,17},{2,10},{10... | collective-permute-start | bytes 393224 | tf_op jit(solution)/shard_map/ppermute | solution.py:521
  66.6 5.2 %collective-permute-start.13 = (bf16[512,128]{1,0:T(8,128)(2,1)S(1)}, bf16[512,128]{1,0:T(8,128)(2,1)S(1)}, u32[]{:S(2)}, u32[]{:S(2)}) collective-permute-start(bf16[512,128]{1,0:T(8,128)(2,1)S(1)} %get-tuple-element.101), channel_id=1, source_target_pairs={{0,16},{8,24},{16,0},{24,8},{1,17},{9,25},{17,1},{25,9},{2,18},{10... | collective-permute-start | bytes 393224 | tf_op jit(solution)/shard_map/ppermute | solution.py:521
  67.6 5.9 %collective-permute-start.14 = (bf16[512,128]{1,0:T(8,128)(2,1)S(1)}, bf16[512,128]{1,0:T(8,128)(2,1)S(1)}, u32[]{:S(2)}, u32[]{:S(2)}) collective-permute-start(bf16[512,128]{1,0:T(8,128)(2,1)S(1)} %get-tuple-element.102), channel_id=1, source_target_pairs={{0,24},{8,16},{16,8},{24,0},{1,25},{9,17},{17,9},{25,1},{2,26},{10... | collective-permute-start | bytes 393224 | tf_op jit(solution)/shard_map/ppermute | solution.py:521
  73.6 1.6 %collective-permute-start.15 = (bf16[256,512]{1,0:T(8,128)(2,1)S(1)}, bf16[256,512]{1,0:T(8,128)(2,1)S(1)}, u32[]{:S(2)}, u32[]{:S(2)}) collective-permute-start(bf16[256,512]{1,0:T(8,128)(2,1)S(1)} %get-tuple-element.103.refs_0_), channel_id=1, source_target_pairs={{0,1},{1,0},{2,3},{3,2},{4,5},{5,4},{6,7},{7,6},{8,9},{9,8},{10,11... | collective-permute-start | bytes 786440 | tf_op jit(solution)/shard_map/ppermute | solution.py:521
  73.7 1.9 %collective-permute-start.16 = (bf16[256,512]{1,0:T(8,128)(2,1)S(1)}, bf16[256,512]{1,0:T(8,128)(2,1)S(1)}, u32[]{:S(2)}, u32[]{:S(2)}) collective-permute-start(bf16[256,512]{1,0:T(8,128)(2,1)S(1)} %get-tuple-element.104.refs_1_), channel_id=1, source_target_pairs={{0,1},{1,0},{2,3},{3,2},{4,5},{5,4},{6,7},{7,6},{8,9},{9,8},{10,11... | collective-permute-start | bytes 786440 | tf_op jit(solution)/shard_map/ppermute | solution.py:521
  82.3 8.4 %collective-permute-start.19 = (bf16[256,512]{1,0:T(8,128)(2,1)S(1)}, bf16[256,512]{1,0:T(8,128)(2,1)S(1)}, u32[]{:S(2)}, u32[]{:S(2)}) collective-permute-start(bf16[256,512]{1,0:T(8,128)(2,1)S(1)} %get-tuple-element.113), channel_id=1, source_target_pairs={{0,2},{1,3},{2,0},{3,1},{4,6},{5,7},{6,4},{7,5},{8,10},{9,11},{10,... | collective-permute-start | bytes 786440 | tf_op jit(solution)/shard_map/ppermute | solution.py:521
  83.0 10.7 %collective-permute-start.20 = (bf16[256,512]{1,0:T(8,128)(2,1)S(1)}, bf16[256,512]{1,0:T(8,128)(2,1)S(1)}, u32[]{:S(2)}, u32[]{:S(2)}) collective-permute-start(bf16[256,512]{1,0:T(8,128)(2,1)S(1)} %get-tuple-element.115), channel_id=1, source_target_pairs={{0,2},{1,3},{2,0},{3,1},{4,6},{5,7},{6,4},{7,5},{8,10},{9,11},{10,... | collective-permute-start | bytes 786440 | tf_op jit(solution)/shard_map/ppermute | solution.py:521
  93.8 18.7 %collective-permute-start.21 = (bf16[256,512]{1,0:T(8,128)(2,1)S(1)}, bf16[256,512]{1,0:T(8,128)(2,1)S(1)}, u32[]{:S(2)}, u32[]{:S(2)}) collective-permute-start(bf16[256,512]{1,0:T(8,128)(2,1)S(1)} %get-tuple-element.116), channel_id=1, source_target_pairs={{0,2},{1,3},{2,0},{3,1},{4,6},{5,7},{6,4},{7,5},{8,10},{9,11},{10,... | collective-permute-start | bytes 786440 | tf_op jit(solution)/shard_map/ppermute | solution.py:521
  95.1 20.8 %collective-permute-start.22 = (bf16[256,512]{1,0:T(8,128)(2,1)S(1)}, bf16[256,512]{1,0:T(8,128)(2,1)S(1)}, u32[]{:S(2)}, u32[]{:S(2)}) collective-permute-start(bf16[256,512]{1,0:T(8,128)(2,1)S(1)} %get-tuple-element.117), channel_id=1, source_target_pairs={{0,2},{1,3},{2,0},{3,1},{4,6},{5,7},{6,4},{7,5},{8,10},{9,11},{10,... | collective-permute-start | bytes 786440 | tf_op jit(solution)/shard_map/ppermute | solution.py:521
  95.9 20.0 %collective-permute-start.23 = (bf16[256,512]{1,0:T(8,128)(2,1)S(1)}, bf16[256,512]{1,0:T(8,128)(2,1)S(1)}, u32[]{:S(2)}, u32[]{:S(2)}) collective-permute-start(bf16[256,512]{1,0:T(8,128)(2,1)S(1)} %add_convert_fusion.2), channel_id=1, source_target_pairs={{0,4},{1,5},{2,6},{3,7},{4,0},{5,1},{6,2},{7,3},{8,12},{9,13},{10,... | collective-permute-start | bytes 786440 | tf_op jit(solution)/shard_map/ppermute | solution.py:521
  98.6 17.4 %collective-permute-start.24 = (bf16[256,512]{1,0:T(8,128)(2,1)S(1)}, bf16[256,512]{1,0:T(8,128)(2,1)S(1)}, u32[]{:S(2)}, u32[]{:S(2)}) collective-permute-start(bf16[256,512]{1,0:T(8,128)(2,1)S(1)} %add_convert_fusion.1), channel_id=1, source_target_pairs={{0,4},{1,5},{2,6},{3,7},{4,0},{5,1},{6,2},{7,3},{8,12},{9,13},{10,... | collective-permute-start | bytes 786440 | tf_op jit(solution)/shard_map/ppermute | solution.py:521

commit v15 on v14

--- a/solution.py
+++ b/solution.py
@@ -429,74 +429,99 @@
     )(ctx_index, *operands)
 
 
-def assemble(ctx_index, pieces, parts):
+def assemble(ctx_index, pieces, cuts):
     rows = pieces[0].shape[0]
     group = len(pieces)
-    part_rows = rows // parts
+    spans = list(zip(cuts[:-1], cuts[1:]))
 
     def kernel(ctx_ref, *refs):
-        for part in range(parts):
+        for part, (lower, upper) in enumerate(spans):
             for distance in range(group):
                 column = pl.multiple_of((ctx_ref[0] ^ distance) * HD, HD)
-                taken = refs[distance][part * part_rows : (part + 1) * part_rows, :]
-                refs[group + part][:, pl.ds(column, HD)] = taken
-
+                refs[group + part][:, pl.ds(column, HD)] = refs[distance][lower:upper, :]
+
+    shapes = [(upper - lower, group * HD) for lower, upper in spans]
     return pl.pallas_call(
         kernel,
         grid_spec=pltpu.PrefetchScalarGridSpec(
             num_scalar_prefetch=1,
             grid=(1,),
             in_specs=[whole((rows, HD))] * group,
-            out_specs=[whole((part_rows, group * HD))] * parts,
+            out_specs=[whole(shape) for shape in shapes],
         ),
-        out_shape=[jax.ShapeDtypeStruct((part_rows, group * HD), jnp.bfloat16)] * parts,
+        out_shape=[jax.ShapeDtypeStruct(shape, jnp.bfloat16) for shape in shapes],
         compiler_params=params(16),
         cost_estimate=SMALL,
         name="assemble",
     )(ctx_index, *pieces)
 
 
-def project(turn, mine, sibling, w_mine, w_sibling):
+def plain(shape):
+    return pl.BlockSpec(shape, lambda step: (0,) * len(shape))
+
+
+def stacked(refs):
+    values = [ref[...] for ref in refs]
+    return values[0] if len(values) == 1 else jnp.concatenate(values, axis=0)
+
+
+def project(wanted, mine, sibling, w_mine, w_sibling):
     parts = len(mine)
-    rows, depth = mine[0].shape
+    depth = mine[0].shape[1]
     columns = w_mine.shape[1] // len(TURNS)
+    turns = sorted({turn for output in wanted for turn, _, _ in output})
 
     def kernel(*refs):
-        w_mine_ref, w_sibling_ref = refs[2 * parts : 2 * parts + 2]
-        for part in range(parts):
-            total = jnp.dot(refs[part][...], w_mine_ref[...], preferred_element_type=jnp.float32)
-            total += jnp.dot(
-                refs[parts + part][...], w_sibling_ref[...], preferred_element_type=jnp.float32
-            )
-            refs[2 * parts + 2 + part][...] = total.astype(jnp.bfloat16)
-
-    weights = pl.BlockSpec((depth, columns), lambda step: (0, turn))
-    attended = pl.BlockSpec((rows, depth), lambda step: (0, 0))
+        own_rows = stacked(refs[:parts])
+        other_rows = stacked(refs[parts : 2 * parts])
+        weights = refs[2 * parts : 2 * parts + 2 * len(turns)]
+        outs = refs[2 * parts + 2 * len(turns) :]
+        for out, output in zip(outs, wanted):
+            place = 0
+            for turn, lower, upper in output:
+                at = turns.index(turn)
+                total = jnp.dot(
+                    own_rows[lower:upper, :], weights[at][...], preferred_element_type=jnp.float32
+                )
+                total += jnp.dot(
+                    other_rows[lower:upper, :],
+                    weights[len(turns) + at][...],
+                    preferred_element_type=jnp.float32,
+                )
+                out[place : place + upper - lower, :] = total.astype(jnp.bfloat16)
+                place += upper - lower
+
+    def columns_of(turn):
+        return pl.BlockSpec((depth, columns), lambda step: (0, turn))
+
+    shapes = [(sum(upper - lower for _, lower, upper in output), columns) for output in wanted]
     return pl.pallas_call(
         kernel,
         grid=(1,),
-        in_specs=[attended] * (2 * parts) + [weights] * 2,
-        out_specs=[pl.BlockSpec((rows, columns), lambda step: (0, 0))] * parts,
-        out_shape=[jax.ShapeDtypeStruct((rows, columns), jnp.bfloat16)] * parts,
-        compiler_params=params(16),
+        in_specs=[plain(part.shape) for part in (*mine, *sibling)]
+        + [columns_of(turn) for turn in turns] * 2,
+        out_specs=[plain(shape) for shape in shapes],
+        out_shape=[jax.ShapeDtypeStruct(shape, jnp.bfloat16) for shape in shapes],
+        compiler_params=params(24),
         cost_estimate=SMALL,
         name="project",
-    )(*mine, *sibling, w_mine, w_sibling)
-
-
-def finish(half, terms, result):
-    parts = len(terms[0])
-    rows, columns = terms[0][0].shape
-    flat = [part for term in terms for part in term]
+    )(*mine, *sibling, *([w_mine] * len(turns)), *([w_sibling] * len(turns)))
+
+
+def finish(half, rows, terms, result):
+    flat = [array for term in terms for array, _ in term]
+    columns = flat[0].shape[1]
 
     def kernel(*refs):
-        for part in range(parts):
-            total = refs[part][...].astype(jnp.float32)
-            for term in range(1, len(terms)):
-                total += refs[term * parts + part][...].astype(jnp.float32)
-            refs[-1][part * rows : (part + 1) * rows, :] = total.astype(jnp.bfloat16)
-
-    in_specs = [pl.BlockSpec((rows, columns), lambda step: (0, 0))] * len(flat)
+        refs = list(refs)
+        total = None
+        for term in terms:
+            values = [refs.pop(0)[first:, :].astype(jnp.float32) for _, first in term]
+            value = values[0] if len(values) == 1 else jnp.concatenate(values, axis=0)
+            total = value if total is None else total + value
+        refs[-1][...] = total.astype(jnp.bfloat16)
+
+    in_specs = [plain(array.shape) for array in flat]
     operands = list(flat)
     aliases = {}
     if result is not None:
@@ -507,8 +532,8 @@
         kernel,
         grid=(1,),
         in_specs=in_specs,
-        out_specs=pl.BlockSpec((parts * rows, columns), lambda step: (half, 0)),
-        out_shape=jax.ShapeDtypeStruct((2 * parts * rows, columns), jnp.bfloat16),
+        out_specs=pl.BlockSpec((rows, columns), lambda step: (half, 0)),
+        out_shape=jax.ShapeDtypeStruct((2 * rows, columns), jnp.bfloat16),
         input_output_aliases=aliases,
         compiler_params=params(16),
         cost_estimate=SMALL,
@@ -556,36 +581,54 @@
     def send_back(pieces):
         return [swap(pieces[distance], "ctx", distance) for distance in near]
 
-    def shares_of(mine):
-        sibling = [swap(part, "head", 1) for part in mine]
-        return [project(turn, mine, sibling, *w_packed) for turn in range(len(TURNS))]
-
-    def to_next(parts, distance):
-        return [swap(part, "head", 2 * distance) for part in parts]
+    rows = shard_rows // 2
+    cut = rows * 21 // 32 // 16 * 16
+    middle = rows // 2
+
+    def projected(mine, sibling, *wanted):
+        return list(project(wanted, mine, sibling, *w_packed))
+
+    def to_next(part, distance):
+        return swap(part, "head", 2 * distance)
 
     pieces = attend(ctx_index, queries, keys, values, docs, low, None)
     pieces, diagonal_out = tie(pieces, high_out[-1])
     back = send_back(pieces)
     back, high = tie(back, high)
     high = [*high, swap(diagonal_out, "ctx", near[-1])]
-    shares = shares_of(assemble(ctx_index, [pieces[0], *back], 1))
-    far = to_next(shares[0], 1)
-    near_sum = to_next(shares[1], 1)
-
-    passed = [add(*both) for both in zip(shares[2], far)]
-    high, shares, passed = tie(high, shares, passed)
+    mine = assemble(ctx_index, [pieces[0], *back], (0, rows))
+    sibling = [swap(part, "head", 1) for part in mine]
+    (share,) = projected(mine, sibling, [(0, 0, cut)])
+    far = to_next(share, 1)
+    (behind,) = projected(mine, sibling, [(0, cut, rows), (1, 0, rows)])
+    shares = projected(mine, sibling, [(2, 0, cut)], [(2, cut, rows)])
+    (kept,) = projected(mine, sibling, [(3, 0, rows)])
+
+    passed = add(shares[0], far)
+    high, passed, _, shares[1], kept = tie(high, passed, behind, shares[1], kept)
+    behind = to_next(behind, 1)
     across = to_next(passed, 2)
     pieces = attend(ctx_index, queries, keys, values, docs, low, high)
     back = send_back(pieces)
-    late = shares_of(assemble(ctx_index, [pieces[0], *back], 2))
-    late[0], near_sum, across = tie(late[0], near_sum, across)
-    result = finish(0, [shares[3], near_sum, across], None)
-    far = to_next(late[0], 1)
-    passed = [add(*both) for both in zip(late[2], far)]
-    across = to_next(passed, 2)
-    late[1], passed = tie(late[1], passed)
-    near_sum = to_next(late[1], 1)
-    return finish(1, [late[3], near_sum, across], result)
+    mine = assemble(ctx_index, [pieces[0], *back], (0, cut, rows))
+    mine, across = tie(mine, across)
+    sibling = [swap(part, "head", 1) for part in mine]
+    late = projected(mine, sibling, [(0, 0, cut)], [(0, cut, rows)])
+    late, behind = tie(late, behind)
+    far = [to_next(part, 1) for part in late]
+    across = [across, to_next(add(shares[1], behind[: rows - cut]), 2)]
+    late = projected(mine, sibling, [(2, 0, cut)], [(2, cut, rows)])
+    passed = [add(*both) for both in zip(late, far)]
+    passed[0], across[1] = tie(passed[0], across[1])
+    terms = [[(kept, 0)], [(behind, rows - cut)], [(part, 0) for part in across]]
+    result = finish(0, rows, terms, None)
+    across = [to_next(part, 2) for part in passed]
+    late = projected(mine, sibling, [(1, 0, middle)], [(1, middle, rows)])
+    late, passed = tie(late, passed)
+    near_sum = [to_next(part, 1) for part in late]
+    (kept,) = projected(mine, sibling, [(3, 0, rows)])
+    terms = [[(kept, 0)], [(part, 0) for part in near_sum], [(part, 0) for part in across]]
+    return finish(1, rows, terms, result)
 
 
 def solution(mesh):

time: 118 us -> 123 us (1.042)
  starting transfers between devices: 29.3 us -> 33.7 us
  Pallas kernels: 28.9 us -> 32.7 us
  waiting for transfers between devices: 57.8 us -> 55.2 us
    ppermute x25 -> x26, starting transfers between devices: 29.3 us -> 33.7 us  [swap(): lax.ppermute(value, axis, [(source, source ^ distance) for source in rang...]
    pallas_call x2, Pallas kernels: 10.2 us -> 14.1 us  [attend(): pl.pallas_call(kernel, grid_spec=pltpu.PrefetchScalarGridSpec(num_scalar_...]
    ppermute x25 -> x26, waiting for transfers between devices: 57.8 us -> 55.2 us  [swap(): lax.ppermute(value, axis, [(source, source ^ distance) for source in rang...]
  transfers between devices with their start and end apart: 25 -> 26, of which waited for: 16 -> 14; matrix products, arithmetic and copies ran while one was open for 1% -> 1% of each run, Pallas kernels for 23% -> 25%
where the time goes in v15:
time: 123 us
  waiting for transfers between devices  55.2 us (45%)
  starting transfers between devices  33.7 us (27%)
  Pallas kernels  32.7 us (27%)
    ppermute x26, waiting for transfers between devices, swap(): lax.ppermute(value, axis, [(source, source ^ distance) for source in rang...  55.2 us
    ppermute x26, starting transfers between devices, swap(): lax.ppermute(value, axis, [(source, source ^ distance) for source in rang...  33.7 us
    pallas_call x2, Pallas kernels, attend(): pl.pallas_call(kernel, grid_spec=pltpu.PrefetchScalarGridSpec(num_scalar_...  14.1 us
    pallas_call x8, Pallas kernels, project(): pl.pallas_call(kernel, grid=(1,), in_specs=[plain(part.shape) for part in...  5.72 us
    pallas_call x1, Pallas kernels, pack_projection(): pl.pallas_call(kernel, grid_spec=pltpu.PrefetchScalarGridSpec(num_scalar_...  5.72 us
    pallas_call x2, Pallas kernels, pack(): pl.pallas_call(kernel, grid_spec=pltpu.PrefetchScalarGridSpec(num_scalar_...  5.02 us
  transfers between devices with their start and end apart: 26, of which 14 were waited for; matrix products, arithmetic and copies ran while one was open for 1% of the time, Pallas kernels for 25%

profile of v15, /device:TPU:0, one launch (start us, length us, event | category | flops | bytes accessed | tf_op | source)
XLA Modules:
  0.0 122.5 jit_solution(13542726885070553955)
XLA Ops:
  0.0 0.5 collective-permute-start.3
  0.5 2.5 %pack.2 = (bf16[1552,128]{1,0:T(8,128)(2,1)}, bf16[1552,128]{1,0:T(8,128)(2,1)}, bf16[1552,128]{1,0:T(8,128)(2,1)}) custom-call(s32[1]{0:T(128)} %bitcast.ctx_ref, bf16[1024,512]{1,0:T(8,128)(2,1)} %refs_3_.4, bf16[1024,512]{1,0:T(8,128)(2,1)} %refs_4_.4, bf16[1024,512]{1,0:T(8,128)(2,1)} %refs_5_.4, bf16[1024,512]{1,0:T(8,128)(2,1)} %refs_3_.4, ...), custom_call_target="tpu_custom_call" | custom-call | flops 1024 | bytes 1024 | tf_op jit(solution)/shard_map/pack/pallas_call | solution.py:201
  3.0 2.5 %collective-permute-start = (bf16[1552,128]{1,0:T(8,128)(2,1)}, bf16[1552,128]{1,0:T(8,128)(2,1)S(1)}, u32[]{:S(2)}, u32[]{:S(2)}) collective-permute-start(bf16[1552,128]{1,0:T(8,128)(2,1)} %get-tuple-element.71), channel_id=1, source_target_pairs={{0,8},{8,0},{16,24},{24,16},{1,9},{9,1},{17,25},{25,17},{2,10},{10... | collective-permute-start | bytes 1191944 | tf_op jit(solution)/shard_map/ppermute | solution.py:546
  5.4 1.5 %collective-permute-start.1 = (bf16[1552,128]{1,0:T(8,128)(2,1)}, bf16[1552,128]{1,0:T(8,128)(2,1)S(1)}, u32[]{:S(2)}, u32[]{:S(2)}) collective-permute-start(bf16[1552,128]{1,0:T(8,128)(2,1)} %get-tuple-element.72), channel_id=1, source_target_pairs={{0,16},{8,24},{16,0},{24,8},{1,17},{9,25},{17,1},{25,9},{2,18},{10... | collective-permute-start | bytes 1191944 | tf_op jit(solution)/shard_map/ppermute | solution.py:546
  7.0 0.0 collective-permute-start.2
  7.0 2.5 %pack.3 = (bf16[1536,128]{1,0:T(8,128)(2,1)}, bf16[1536,128]{1,0:T(8,128)(2,1)}, bf16[1536,128]{1,0:T(8,128)(2,1)}) custom-call(s32[1]{0:T(128)} %bitcast.ctx_ref, bf16[1024,512]{1,0:T(8,128)(2,1)} %refs_3_.4, bf16[1024,512]{1,0:T(8,128)(2,1)} %refs_4_.4, bf16[1024,512]{1,0:T(8,128)(2,1)} %refs_5_.4, bf16[1024,512]{1,0:T(8,128)(2,1)} %refs_3_.4, ...), custom_call_target="tpu_custom_call" | custom-call | flops 1024 | bytes 1024 | tf_op jit(solution)/shard_map/pack/pallas_call | solution.py:201
  9.5 2.0 %collective-permute-start.7 = (bf16[1536,128]{1,0:T(8,128)(2,1)}, bf16[1536,128]{1,0:T(8,128)(2,1)S(1)}, u32[]{:S(2)}, u32[]{:S(2)}) collective-permute-start(bf16[1536,128]{1,0:T(8,128)(2,1)} %get-tuple-element.90), channel_id=1, source_target_pairs={{0,8},{8,0},{16,24},{24,16},{1,9},{9,1},{17,25},{25,17},{2,10},{10... | collective-permute-start | bytes 1179656 | tf_op jit(solution)/shard_map/ppermute | solution.py:546
  11.5 1.5 %collective-permute-start.8 = (bf16[1536,128]{1,0:T(8,128)(2,1)}, bf16[1536,128]{1,0:T(8,128)(2,1)S(1)}, u32[]{:S(2)}, u32[]{:S(2)}) collective-permute-start(bf16[1536,128]{1,0:T(8,128)(2,1)} %get-tuple-element.91), channel_id=1, source_target_pairs={{0,16},{8,24},{16,0},{24,8},{1,17},{9,25},{17,1},{25,9},{2,18},{10... | collective-permute-start | bytes 1179656 | tf_op jit(solution)/shard_map/ppermute | solution.py:546
  13.0 0.5 broadcast_xor_fusion.places_ref
  13.5 5.7 %pack_projection.1 = (bf16[512,2048]{1,0:T(8,128)(2,1)}, bf16[512,2048]{1,0:T(8,128)(2,1)}) custom-call(s32[4]{0:T(128)} %broadcast_xor_fusion.places_ref, bf16[512,4096]{1,0:T(8,128)(2,1)} %mine_in.1, bf16[512,4096]{1,0:T(8,128)(2,1)} %collective-permute-done.3.sibling_in), custom_call_target="tpu_custom_call" | custom-call | flops 1024 | bytes 1024 | tf_op jit(solution)/shard_map/pack_projection/pallas_call | solution.py:227
  19.3 0.0 collective-permute-done.refs_4_.refs_7_
  19.3 6.9 %collective-permute-done.1.refs_5_.refs_8_ = bf16[1552,128]{1,0:T(8,128)(2,1)S(1)} collective-permute-done((bf16[1552,128]{1,0:T(8,128)(2,1)}, bf16[1552,128]{1,0:T(8,128)(2,1)S(1)}, u32[]{:S(2)}, u32[]{:S(2)}) %collective-permute-start.1) | collective-permute-done | bytes 397344 | tf_op jit(solution)/shard_map/ppermute | solution.py:546
  26.2 0.0 collective-permute-done.2.refs_6_.refs_9_
  26.2 7.3 %attend_low.1 = (bf16[512,128]{1,0:T(8,128)(2,1)S(1)}, bf16[512,128]{1,0:T(8,128)(2,1)S(1)}, bf16[512,128]{1,0:T(8,128)(2,1)S(1)}, bf16[512,128]{1,0:T(8,128)(2,1)S(1)}) custom-call(s32[1]{0:T(128)} %bitcast.ctx_ref, bf16[1024,512]{1,0:T(8,128)(2,1)S(1)} %copy-done.2, bf16[1024,512]{1,0:T(8,128)(2,1)S(1)} %copy-done.3, bf16[1024,512]{1,0:T(8,128)(2,1)S(1)} %copy-done.4, ...), custom_call_target="tpu_custom_call" | custom-call | flops 1024 | bytes 1024 | tf_op jit(solution)/shard_map/attend_low/pallas_call | solution.py:409
  33.5 1.0 collective-permute-start.4
  34.5 1.1 collective-permute-start.5
  35.6 1.4 %collective-permute-start.6 = (bf16[512,128]{1,0:T(8,128)(2,1)S(1)}, bf16[512,128]{1,0:T(8,128)(2,1)S(1)}, u32[]{:S(2)}, u32[]{:S(2)}) collective-permute-start(bf16[512,128]{1,0:T(8,128)(2,1)S(1)} %get-tuple-element.89), channel_id=1, source_target_pairs={{0,24},{8,16},{16,8},{24,0},{1,25},{9,17},{17,9},{25,1},{2,26},{10... | collective-permute-start | bytes 393224 | tf_op jit(solution)/shard_map/ppermute | solution.py:546
  37.1 0.0 collective-permute-done.7.refs_10_
  37.1 0.0 collective-permute-done.8.refs_11_
  37.1 2.6 %collective-permute-done.4.refs_1_ = bf16[512,128]{1,0:T(8,128)(2,1)S(1)} collective-permute-done((bf16[512,128]{1,0:T(8,128)(2,1)S(1)}, bf16[512,128]{1,0:T(8,128)(2,1)S(1)}, u32[]{:S(2)}, u32[]{:S(2)}) %collective-permute-start.4) | collective-permute-done | bytes 131104 | tf_op jit(solution)/shard_map/ppermute | solution.py:546
  39.7 2.1 %collective-permute-done.5.refs_2_ = bf16[512,128]{1,0:T(8,128)(2,1)S(1)} collective-permute-done((bf16[512,128]{1,0:T(8,128)(2,1)S(1)}, bf16[512,128]{1,0:T(8,128)(2,1)S(1)}, u32[]{:S(2)}, u32[]{:S(2)}) %collective-permute-start.5) | collective-permute-done | bytes 131104 | tf_op jit(solution)/shard_map/ppermute | solution.py:546
  41.8 0.0 collective-permute-done.6.refs_3_
  41.8 0.1 assemble.2.refs_0_
  41.9 0.1 collective-permute-start.10
  42.0 1.9 %collective-permute-done.10.refs_1_ = bf16[512,512]{1,0:T(8,128)(2,1)S(1)} collective-permute-done((bf16[512,512]{1,0:T(8,128)(2,1)S(1)}, bf16[512,512]{1,0:T(8,128)(2,1)S(1)}, u32[]{:S(2)}, u32[]{:S(2)}) %collective-permute-start.10) | collective-permute-done | bytes 524320 | tf_op jit(solution)/shard_map/ppermute | solution.py:546
  43.9 0.5 project.9
  44.4 1.6 %collective-permute-start.11 = (bf16[336,512]{1,0:T(8,128)(2,1)S(1)}, bf16[336,512]{1,0:T(8,128)(2,1)S(1)}, u32[]{:S(2)}, u32[]{:S(2)}) collective-permute-start(bf16[336,512]{1,0:T(8,128)(2,1)S(1)} %project.9), channel_id=1, source_target_pairs={{0,2},{1,3},{2,0},{3,1},{4,6},{5,7},{6,4},{7,5},{8,10},{9,11},{10,... | collective-permute-start | bytes 1032200 | tf_op jit(solution)/shard_map/ppermute | solution.py:546
  46.1 1.8 %collective-permute-start.9 = (bf16[1536,128]{1,0:T(8,128)(2,1)S(1)}, bf16[1536,128]{1,0:T(8,128)(2,1)S(1)}, u32[]{:S(2)}, u32[]{:S(2)}) collective-permute-start(bf16[1536,128]{1,0:T(8,128)(2,1)S(1)} %copy-done.6), channel_id=1, source_target_pairs={{0,24},{8,16},{16,8},{24,0},{1,25},{9,17},{17,9},{25,1},{2,26},{10... | collective-permute-start | bytes 1179656 | tf_op jit(solution)/shard_map/ppermute | solution.py:546
  47.8 0.9 project.10
  48.8 0.5 collective-permute-start.18
  49.3 0.7 project.8
  50.0 0.7 project.11.refs_0_
  50.7 4.7 %collective-permute-done.11 = bf16[336,512]{1,0:T(8,128)(2,1)S(1)} collective-permute-done((bf16[336,512]{1,0:T(8,128)(2,1)S(1)}, bf16[336,512]{1,0:T(8,128)(2,1)S(1)}, u32[]{:S(2)}, u32[]{:S(2)}) %collective-permute-start.11) | collective-permute-done | bytes 344096 | tf_op jit(solution)/shard_map/ppermute | solution.py:546
  55.4 0.1 add_convert_fusion.1
  55.5 2.4 %collective-permute-done.9.refs_12_ = bf16[1536,128]{1,0:T(8,128)(2,1)S(1)} collective-permute-done((bf16[1536,128]{1,0:T(8,128)(2,1)S(1)}, bf16[1536,128]{1,0:T(8,128)(2,1)S(1)}, u32[]{:S(2)}, u32[]{:S(2)}) %collective-permute-start.9) | collective-permute-done | bytes 393248 | tf_op jit(solution)/shard_map/ppermute | solution.py:546
  57.9 2.6 %collective-permute-start.15 = (bf16[336,512]{1,0:T(8,128)(2,1)S(1)}, bf16[336,512]{1,0:T(8,128)(2,1)S(1)}, u32[]{:S(2)}, u32[]{:S(2)}) collective-permute-start(bf16[336,512]{1,0:T(8,128)(2,1)S(1)} %add_convert_fusion.1), channel_id=1, source_target_pairs={{0,4},{1,5},{2,6},{3,7},{4,0},{5,1},{6,2},{7,3},{8,12},{9,13},{10,... | collective-permute-start | bytes 1032200 | tf_op jit(solution)/shard_map/ppermute | solution.py:546
  60.4 6.8 %attend_high.1 = (bf16[512,128]{1,0:T(8,128)(2,1)S(1)}, bf16[512,128]{1,0:T(8,128)(2,1)S(1)}, bf16[512,128]{1,0:T(8,128)(2,1)S(1)}, bf16[512,128]{1,0:T(8,128)(2,1)S(1)}) custom-call(s32[1]{0:T(128)} %bitcast.ctx_ref, bf16[1024,512]{1,0:T(8,128)(2,1)S(1)} %copy-done.2, bf16[1024,512]{1,0:T(8,128)(2,1)S(1)} %copy-done.3, bf16[1024,512]{1,0:T(8,128)(2,1)S(1)} %copy-done.4, ...), custom_call_target="tpu_custom_call" | custom-call | flops 1024 | bytes 1024 | tf_op jit(solution)/shard_map/attend_high/pallas_call | solution.py:409
  67.2 1.4 %collective-permute-start.12 = (bf16[512,128]{1,0:T(8,128)(2,1)S(1)}, bf16[512,128]{1,0:T(8,128)(2,1)S(1)}, u32[]{:S(2)}, u32[]{:S(2)}) collective-permute-start(bf16[512,128]{1,0:T(8,128)(2,1)S(1)} %get-tuple-element.107), channel_id=1, source_target_pairs={{0,8},{8,0},{16,24},{24,16},{1,9},{9,1},{17,25},{25,17},{2,10},{10... | collective-permute-start | bytes 393224 | tf_op jit(solution)/shard_map/ppermute | solution.py:546
  68.7 1.0 collective-permute-start.13
  69.6 1.1 collective-permute-start.14
  70.8 2.9 %collective-permute-done.12.refs_1_ = bf16[512,128]{1,0:T(8,128)(2,1)S(1)} collective-permute-done((bf16[512,128]{1,0:T(8,128)(2,1)S(1)}, bf16[512,128]{1,0:T(8,128)(2,1)S(1)}, u32[]{:S(2)}, u32[]{:S(2)}) %collective-permute-start.12) | collective-permute-done | bytes 131104 | tf_op jit(solution)/shard_map/ppermute | solution.py:546
  73.7 2.1 %collective-permute-done.13.refs_2_ = bf16[512,128]{1,0:T(8,128)(2,1)S(1)} collective-permute-done((bf16[512,128]{1,0:T(8,128)(2,1)S(1)}, bf16[512,128]{1,0:T(8,128)(2,1)S(1)}, u32[]{:S(2)}, u32[]{:S(2)}) %collective-permute-start.13) | collective-permute-done | bytes 131104 | tf_op jit(solution)/shard_map/ppermute | solution.py:546
  75.8 0.1 assemble.3
  75.9 0.3 collective-permute-done.15.refs_2_
  76.2 0.5 collective-permute-start.17
  76.7 1.4 %collective-permute-done.17.refs_3_ = bf16[176,512]{1,0:T(8,128)(2,1)S(1)} collective-permute-done((bf16[176,512]{1,0:T(8,128)(2,1)S(1)}, bf16[176,512]{1,0:T(8,128)(2,1)S(1)}, u32[]{:S(2)}, u32[]{:S(2)}) %collective-permute-start.17) | collective-permute-done | bytes 180256 | tf_op jit(solution)/shard_map/ppermute | solution.py:546
  78.1 0.7 project.15
  78.8 3.6 %collective-permute-start.19 = (bf16[336,512]{1,0:T(8,128)(2,1)S(1)}, bf16[336,512]{1,0:T(8,128)(2,1)S(1)}, u32[]{:S(2)}, u32[]{:S(2)}) collective-permute-start(bf16[336,512]{1,0:T(8,128)(2,1)S(1)} %get-tuple-element.120), channel_id=1, source_target_pairs={{0,2},{1,3},{2,0},{3,1},{4,6},{5,7},{6,4},{7,5},{8,10},{9,11},{10,... | collective-permute-start | bytes 1032200 | tf_op jit(solution)/shard_map/ppermute | solution.py:546
  82.4 0.1 collective-permute-start.20
  82.5 1.9 %collective-permute-start.21 = (bf16[176,512]{1,0:T(8,128)(2,1)S(1)}, bf16[176,512]{1,0:T(8,128)(2,1)S(1)}, u32[]{:S(2)}, u32[]{:S(2)}) collective-permute-start(bf16[176,512]{1,0:T(8,128)(2,1)S(1)} %get-tuple-element.125), channel_id=1, source_target_pairs={{0,2},{1,3},{2,0},{3,1},{4,6},{5,7},{6,4},{7,5},{8,10},{9,11},{10,... | collective-permute-start | bytes 540680 | tf_op jit(solution)/shard_map/ppermute | solution.py:546
  84.4 0.7 project.13
  85.1 0.7 project.14
  85.8 9.2 %collective-permute-done.19 = bf16[336,512]{1,0:T(8,128)(2,1)S(1)} collective-permute-done((bf16[336,512]{1,0:T(8,128)(2,1)S(1)}, bf16[336,512]{1,0:T(8,128)(2,1)S(1)}, u32[]{:S(2)}, u32[]{:S(2)}) %collective-permute-start.19) | collective-permute-done | bytes 344096 | tf_op jit(solution)/shard_map/ppermute | solution.py:546
  95.1 0.1 add_convert_fusion
  95.2 2.9 %collective-permute-start.24 = (bf16[336,512]{1,0:T(8,128)(2,1)S(1)}, bf16[336,512]{1,0:T(8,128)(2,1)S(1)}, u32[]{:S(2)}, u32[]{:S(2)}) collective-permute-start(bf16[336,512]{1,0:T(8,128)(2,1)S(1)} %add_convert_fusion), channel_id=1, source_target_pairs={{0,4},{1,5},{2,6},{3,7},{4,0},{5,1},{6,2},{7,3},{8,12},{9,13},{10,... | collective-permute-start | bytes 1032200 | tf_op jit(solution)/shard_map/ppermute | solution.py:546
  98.0 1.8 %collective-permute-done.21 = bf16[176,512]{1,0:T(8,128)(2,1)S(1)} collective-permute-done((bf16[176,512]{1,0:T(8,128)(2,1)S(1)}, bf16[176,512]{1,0:T(8,128)(2,1)S(1)}, u32[]{:S(2)}, u32[]{:S(2)}) %collective-permute-start.21) | collective-permute-done | bytes 180256 | tf_op jit(solution)/shard_map/ppermute | solution.py:546
  99.9 1.2 collective-permute-start.22
  101.1 0.9 collective-permute-start.23
  102.0 1.0 collective-permute-start.25
  103.0 0.7 project.12.refs_0_
  103.7 1.0 finish.2.refs_5_
  104.7 15.5 %collective-permute-done.25.refs_4_ = bf16[176,512]{1,0:T(8,128)(2,1)S(1)} collective-permute-done((bf16[176,512]{1,0:T(8,128)(2,1)S(1)}, bf16[176,512]{1,0:T(8,128)(2,1)S(1)}, u32[]{:S(2)}, u32[]{:S(2)}) %collective-permute-start.25) | collective-permute-done | bytes 180256 | tf_op jit(solution)/shard_map/ppermute | solution.py:546
  120.2 1.3 %collective-permute-done.23.refs_2_ = bf16[256,512]{1,0:T(8,128)(2,1)S(1)} collective-permute-done((bf16[256,512]{1,0:T(8,128)(2,1)S(1)}, bf16[256,512]{1,0:T(8,128)(2,1)S(1)}, u32[]{:S(2)}, u32[]{:S(2)}) %collective-permute-start.23) | collective-permute-done | bytes 262176 | tf_op jit(solution)/shard_map/ppermute | solution.py:546
  121.5 1.0 finish.3
  (26 shorter events, 0.1 us)
Async XLA Ops:
  0.0 11.5 %collective-permute-start.3 = (bf16[512,4096]{1,0:T(8,128)(2,1)}, bf16[512,4096]{1,0:T(8,128)(2,1)}, u32[]{:S(2)}, u32[]{:S(2)}) collective-permute-start(bf16[512,4096]{1,0:T(8,128)(2,1)} %mine_in.1), channel_id=1, source_target_pairs={{0,1},{1,0},{2,3},{3,2},{4,5},{5,4},{6,7},{7,6},{8,9},{9,8},{10,11... | collective-permute-start | bytes 12582920 | tf_op jit(solution)/shard_map/ppermute | solution.py:546
  2.9 10.0 %copy-start.7 = (s32[4]{0:T(128)S(1)}, s32[4]{0:T(128)}, u32[]{:S(2)}) copy-start(s32[4]{0:T(128)} %constant.13) | copy-start | bytes 52
  3.0 16.3 %collective-permute-start = (bf16[1552,128]{1,0:T(8,128)(2,1)}, bf16[1552,128]{1,0:T(8,128)(2,1)S(1)}, u32[]{:S(2)}, u32[]{:S(2)}) collective-permute-start(bf16[1552,128]{1,0:T(8,128)(2,1)} %get-tuple-element.71), channel_id=1, source_target_pairs={{0,8},{8,0},{16,24},{24,16},{1,9},{9,1},{17,25},{25,17},{2,10},{10... | collective-permute-start | bytes 1191944 | tf_op jit(solution)/shard_map/ppermute | solution.py:546
  5.4 20.8 %collective-permute-start.1 = (bf16[1552,128]{1,0:T(8,128)(2,1)}, bf16[1552,128]{1,0:T(8,128)(2,1)S(1)}, u32[]{:S(2)}, u32[]{:S(2)}) collective-permute-start(bf16[1552,128]{1,0:T(8,128)(2,1)} %get-tuple-element.72), channel_id=1, source_target_pairs={{0,16},{8,24},{16,0},{24,8},{1,17},{9,25},{17,1},{25,9},{2,18},{10... | collective-permute-start | bytes 1191944 | tf_op jit(solution)/shard_map/ppermute | solution.py:546
  7.0 19.2 %collective-permute-start.2 = (bf16[1552,128]{1,0:T(8,128)(2,1)}, bf16[1552,128]{1,0:T(8,128)(2,1)S(1)}, u32[]{:S(2)}, u32[]{:S(2)}) collective-permute-start(bf16[1552,128]{1,0:T(8,128)(2,1)} %get-tuple-element.73), channel_id=1, source_target_pairs={{0,24},{8,16},{16,8},{24,0},{1,25},{9,17},{17,9},{25,1},{2,26},{10... | collective-permute-start | bytes 1191944 | tf_op jit(solution)/shard_map/ppermute | solution.py:546
  9.5 27.6 %collective-permute-start.7 = (bf16[1536,128]{1,0:T(8,128)(2,1)}, bf16[1536,128]{1,0:T(8,128)(2,1)S(1)}, u32[]{:S(2)}, u32[]{:S(2)}) collective-permute-start(bf16[1536,128]{1,0:T(8,128)(2,1)} %get-tuple-element.90), channel_id=1, source_target_pairs={{0,8},{8,0},{16,24},{24,16},{1,9},{9,1},{17,25},{25,17},{2,10},{10... | collective-permute-start | bytes 1179656 | tf_op jit(solution)/shard_map/ppermute | solution.py:546
  11.5 25.6 %collective-permute-start.8 = (bf16[1536,128]{1,0:T(8,128)(2,1)}, bf16[1536,128]{1,0:T(8,128)(2,1)S(1)}, u32[]{:S(2)}, u32[]{:S(2)}) collective-permute-start(bf16[1536,128]{1,0:T(8,128)(2,1)} %get-tuple-element.91), channel_id=1, source_target_pairs={{0,16},{8,24},{16,0},{24,8},{1,17},{9,25},{17,1},{25,9},{2,18},{10... | collective-permute-start | bytes 1179656 | tf_op jit(solution)/shard_map/ppermute | solution.py:546
  13.5 12.7 %copy-start.2 = (bf16[1024,512]{1,0:T(8,128)(2,1)S(1)}, bf16[1024,512]{1,0:T(8,128)(2,1)}, u32[]{:S(2)}) copy-start(bf16[1024,512]{1,0:T(8,128)(2,1)} %refs_3_.4) | copy-start | bytes 3145732
  13.5 12.7 %copy-start.3 = (bf16[1024,512]{1,0:T(8,128)(2,1)S(1)}, bf16[1024,512]{1,0:T(8,128)(2,1)}, u32[]{:S(2)}) copy-start(bf16[1024,512]{1,0:T(8,128)(2,1)} %refs_4_.4) | copy-start | bytes 3145732
  13.5 12.7 %copy-start.4 = (bf16[1024,512]{1,0:T(8,128)(2,1)S(1)}, bf16[1024,512]{1,0:T(8,128)(2,1)}, u32[]{:S(2)}) copy-start(bf16[1024,512]{1,0:T(8,128)(2,1)} %refs_5_.4) | copy-start | bytes 3145732
  13.5 12.7 %copy-start.5 = (s32[1024]{0:T(1024)S(1)}, s32[1024]{0:T(1024)}, u32[]{:S(2)}) copy-start(s32[1024]{0:T(1024)} %param.9) | copy-start | bytes 12292
  19.3 24.6 %copy-start = (bf16[512,2048]{1,0:T(8,128)(2,1)S(1)}, bf16[512,2048]{1,0:T(8,128)(2,1)}, u32[]{:S(2)}) copy-start(bf16[512,2048]{1,0:T(8,128)(2,1)} %get-tuple-element.99.refs_2_.refs_3_.refs_4_) | copy-start | bytes 6291460
  19.3 24.6 %copy-start.1 = (bf16[512,2048]{1,0:T(8,128)(2,1)S(1)}, bf16[512,2048]{1,0:T(8,128)(2,1)}, u32[]{:S(2)}) copy-start(bf16[512,2048]{1,0:T(8,128)(2,1)} %get-tuple-element.100.refs_3_.refs_4_.refs_5_) | copy-start | bytes 6291460
  33.5 12.6 %copy-start.6 = (bf16[1536,128]{1,0:T(8,128)(2,1)S(1)}, bf16[1536,128]{1,0:T(8,128)(2,1)}, u32[]{:S(2)}) copy-start(bf16[1536,128]{1,0:T(8,128)(2,1)} %get-tuple-element.94) | copy-start | bytes 1179652
  33.5 6.2 %collective-permute-start.4 = (bf16[512,128]{1,0:T(8,128)(2,1)S(1)}, bf16[512,128]{1,0:T(8,128)(2,1)S(1)}, u32[]{:S(2)}, u32[]{:S(2)}) collective-permute-start(bf16[512,128]{1,0:T(8,128)(2,1)S(1)} %get-tuple-element.87), channel_id=1, source_target_pairs={{0,8},{8,0},{16,24},{24,16},{1,9},{9,1},{17,25},{25,17},{2,10},{10... | collective-permute-start | bytes 393224 | tf_op jit(solution)/shard_map/ppermute | solution.py:546
  34.5 7.3 %collective-permute-start.5 = (bf16[512,128]{1,0:T(8,128)(2,1)S(1)}, bf16[512,128]{1,0:T(8,128)(2,1)S(1)}, u32[]{:S(2)}, u32[]{:S(2)}) collective-permute-start(bf16[512,128]{1,0:T(8,128)(2,1)S(1)} %get-tuple-element.88), channel_id=1, source_target_pairs={{0,16},{8,24},{16,0},{24,8},{1,17},{9,25},{17,1},{25,9},{2,18},{10... | collective-permute-start | bytes 393224 | tf_op jit(solution)/shard_map/ppermute | solution.py:546
  35.6 6.2 %collective-permute-start.6 = (bf16[512,128]{1,0:T(8,128)(2,1)S(1)}, bf16[512,128]{1,0:T(8,128)(2,1)S(1)}, u32[]{:S(2)}, u32[]{:S(2)}) collective-permute-start(bf16[512,128]{1,0:T(8,128)(2,1)S(1)} %get-tuple-element.89), channel_id=1, source_target_pairs={{0,24},{8,16},{16,8},{24,0},{1,25},{9,17},{17,9},{25,1},{2,26},{10... | collective-permute-start | bytes 393224 | tf_op jit(solution)/shard_map/ppermute | solution.py:546
  41.9 2.0 %collective-permute-start.10 = (bf16[512,512]{1,0:T(8,128)(2,1)S(1)}, bf16[512,512]{1,0:T(8,128)(2,1)S(1)}, u32[]{:S(2)}, u32[]{:S(2)}) collective-permute-start(bf16[512,512]{1,0:T(8,128)(2,1)S(1)} %assemble.2.refs_0_), channel_id=1, source_target_pairs={{0,1},{1,0},{2,3},{3,2},{4,5},{5,4},{6,7},{7,6},{8,9},{9,8},{10,11... | collective-permute-start | bytes 1572872 | tf_op jit(solution)/shard_map/ppermute | solution.py:546
  44.4 11.0 %collective-permute-start.11 = (bf16[336,512]{1,0:T(8,128)(2,1)S(1)}, bf16[336,512]{1,0:T(8,128)(2,1)S(1)}, u32[]{:S(2)}, u32[]{:S(2)}) collective-permute-start(bf16[336,512]{1,0:T(8,128)(2,1)S(1)} %project.9), channel_id=1, source_target_pairs={{0,2},{1,3},{2,0},{3,1},{4,6},{5,7},{6,4},{7,5},{8,10},{9,11},{10,... | collective-permute-start | bytes 1032200 | tf_op jit(solution)/shard_map/ppermute | solution.py:546
  46.1 11.8 %collective-permute-start.9 = (bf16[1536,128]{1,0:T(8,128)(2,1)S(1)}, bf16[1536,128]{1,0:T(8,128)(2,1)S(1)}, u32[]{:S(2)}, u32[]{:S(2)}) collective-permute-start(bf16[1536,128]{1,0:T(8,128)(2,1)S(1)} %copy-done.6), channel_id=1, source_target_pairs={{0,24},{8,16},{16,8},{24,0},{1,25},{9,17},{17,9},{25,1},{2,26},{10... | collective-permute-start | bytes 1179656 | tf_op jit(solution)/shard_map/ppermute | solution.py:546
  48.8 30.0 %collective-permute-start.18 = (bf16[688,512]{1,0:T(8,128)(2,1)S(1)}, bf16[688,512]{1,0:T(8,128)(2,1)S(1)}, u32[]{:S(2)}, u32[]{:S(2)}) collective-permute-start(bf16[688,512]{1,0:T(8,128)(2,1)S(1)} %project.10), channel_id=1, source_target_pairs={{0,2},{1,3},{2,0},{3,1},{4,6},{5,7},{6,4},{7,5},{8,10},{9,11},{10,... | collective-permute-start | bytes 2113544 | tf_op jit(solution)/shard_map/ppermute | solution.py:546
  57.9 18.3 %collective-permute-start.15 = (bf16[336,512]{1,0:T(8,128)(2,1)S(1)}, bf16[336,512]{1,0:T(8,128)(2,1)S(1)}, u32[]{:S(2)}, u32[]{:S(2)}) collective-permute-start(bf16[336,512]{1,0:T(8,128)(2,1)S(1)} %add_convert_fusion.1), channel_id=1, source_target_pairs={{0,4},{1,5},{2,6},{3,7},{4,0},{5,1},{6,2},{7,3},{8,12},{9,13},{10,... | collective-permute-start | bytes 1032200 | tf_op jit(solution)/shard_map/ppermute | solution.py:546
  67.2 6.4 %collective-permute-start.12 = (bf16[512,128]{1,0:T(8,128)(2,1)S(1)}, bf16[512,128]{1,0:T(8,128)(2,1)S(1)}, u32[]{:S(2)}, u32[]{:S(2)}) collective-permute-start(bf16[512,128]{1,0:T(8,128)(2,1)S(1)} %get-tuple-element.107), channel_id=1, source_target_pairs={{0,8},{8,0},{16,24},{24,16},{1,9},{9,1},{17,25},{25,17},{2,10},{10... | collective-permute-start | bytes 393224 | tf_op jit(solution)/shard_map/ppermute | solution.py:546
  68.7 7.1 %collective-permute-start.13 = (bf16[512,128]{1,0:T(8,128)(2,1)S(1)}, bf16[512,128]{1,0:T(8,128)(2,1)S(1)}, u32[]{:S(2)}, u32[]{:S(2)}) collective-permute-start(bf16[512,128]{1,0:T(8,128)(2,1)S(1)} %get-tuple-element.108), channel_id=1, source_target_pairs={{0,16},{8,24},{16,0},{24,8},{1,17},{9,25},{17,1},{25,9},{2,18},{10... | collective-permute-start | bytes 393224 | tf_op jit(solution)/shard_map/ppermute | solution.py:546
  69.6 6.1 %collective-permute-start.14 = (bf16[512,128]{1,0:T(8,128)(2,1)S(1)}, bf16[512,128]{1,0:T(8,128)(2,1)S(1)}, u32[]{:S(2)}, u32[]{:S(2)}) collective-permute-start(bf16[512,128]{1,0:T(8,128)(2,1)S(1)} %get-tuple-element.109), channel_id=1, source_target_pairs={{0,24},{8,16},{16,8},{24,0},{1,25},{9,17},{17,9},{25,1},{2,26},{10... | collective-permute-start | bytes 393224 | tf_op jit(solution)/shard_map/ppermute | solution.py:546
  76.2 1.9 %collective-permute-start.16 = (bf16[336,512]{1,0:T(8,128)(2,1)S(1)}, bf16[336,512]{1,0:T(8,128)(2,1)S(1)}, u32[]{:S(2)}, u32[]{:S(2)}) collective-permute-start(bf16[336,512]{1,0:T(8,128)(2,1)S(1)} %get-tuple-element.113.refs_0_), channel_id=1, source_target_pairs={{0,1},{1,0},{2,3},{3,2},{4,5},{5,4},{6,7},{7,6},{8,9},{9,8},{10,11... | collective-permute-start | bytes 1032200 | tf_op jit(solution)/shard_map/ppermute | solution.py:546
  76.2 1.9 %collective-permute-start.17 = (bf16[176,512]{1,0:T(8,128)(2,1)S(1)}, bf16[176,512]{1,0:T(8,128)(2,1)S(1)}, u32[]{:S(2)}, u32[]{:S(2)}) collective-permute-start(bf16[176,512]{1,0:T(8,128)(2,1)S(1)} %get-tuple-element.114.refs_1_), channel_id=1, source_target_pairs={{0,1},{1,0},{2,3},{3,2},{4,5},{5,4},{6,7},{7,6},{8,9},{9,8},{10,11... | collective-permute-start | bytes 540680 | tf_op jit(solution)/shard_map/ppermute | solution.py:546
  78.8 16.3 %collective-permute-start.19 = (bf16[336,512]{1,0:T(8,128)(2,1)S(1)}, bf16[336,512]{1,0:T(8,128)(2,1)S(1)}, u32[]{:S(2)}, u32[]{:S(2)}) collective-permute-start(bf16[336,512]{1,0:T(8,128)(2,1)S(1)} %get-tuple-element.120), channel_id=1, source_target_pairs={{0,2},{1,3},{2,0},{3,1},{4,6},{5,7},{6,4},{7,5},{8,10},{9,11},{10,... | collective-permute-start | bytes 1032200 | tf_op jit(solution)/shard_map/ppermute | solution.py:546
  82.4 12.8 %collective-permute-start.20 = (bf16[176,512]{1,0:T(8,128)(2,1)S(1)}, bf16[176,512]{1,0:T(8,128)(2,1)S(1)}, u32[]{:S(2)}, u32[]{:S(2)}) collective-permute-start(bf16[176,512]{1,0:T(8,128)(2,1)S(1)} %add_convert_fusion.3), channel_id=1, source_target_pairs={{0,4},{1,5},{2,6},{3,7},{4,0},{5,1},{6,2},{7,3},{8,12},{9,13},{10,... | collective-permute-start | bytes 540680 | tf_op jit(solution)/shard_map/ppermute | solution.py:546
  82.5 17.4 %collective-permute-start.21 = (bf16[176,512]{1,0:T(8,128)(2,1)S(1)}, bf16[176,512]{1,0:T(8,128)(2,1)S(1)}, u32[]{:S(2)}, u32[]{:S(2)}) collective-permute-start(bf16[176,512]{1,0:T(8,128)(2,1)S(1)} %get-tuple-element.125), channel_id=1, source_target_pairs={{0,2},{1,3},{2,0},{3,1},{4,6},{5,7},{6,4},{7,5},{8,10},{9,11},{10,... | collective-permute-start | bytes 540680 | tf_op jit(solution)/shard_map/ppermute | solution.py:546
  95.2 26.4 %collective-permute-start.24 = (bf16[336,512]{1,0:T(8,128)(2,1)S(1)}, bf16[336,512]{1,0:T(8,128)(2,1)S(1)}, u32[]{:S(2)}, u32[]{:S(2)}) collective-permute-start(bf16[336,512]{1,0:T(8,128)(2,1)S(1)} %add_convert_fusion), channel_id=1, source_target_pairs={{0,4},{1,5},{2,6},{3,7},{4,0},{5,1},{6,2},{7,3},{8,12},{9,13},{10,... | collective-permute-start | bytes 1032200 | tf_op jit(solution)/shard_map/ppermute | solution.py:546
  99.9 20.3 %collective-permute-start.22 = (bf16[256,512]{1,0:T(8,128)(2,1)S(1)}, bf16[256,512]{1,0:T(8,128)(2,1)S(1)}, u32[]{:S(2)}, u32[]{:S(2)}) collective-permute-start(bf16[256,512]{1,0:T(8,128)(2,1)S(1)} %get-tuple-element.126), channel_id=1, source_target_pairs={{0,2},{1,3},{2,0},{3,1},{4,6},{5,7},{6,4},{7,5},{8,10},{9,11},{10,... | collective-permute-start | bytes 786440 | tf_op jit(solution)/shard_map/ppermute | solution.py:546
  101.1 20.4 %collective-permute-start.23 = (bf16[256,512]{1,0:T(8,128)(2,1)S(1)}, bf16[256,512]{1,0:T(8,128)(2,1)S(1)}, u32[]{:S(2)}, u32[]{:S(2)}) collective-permute-start(bf16[256,512]{1,0:T(8,128)(2,1)S(1)} %get-tuple-element.127), channel_id=1, source_target_pairs={{0,2},{1,3},{2,0},{3,1},{4,6},{5,7},{6,4},{7,5},{8,10},{9,11},{10,... | collective-permute-start | bytes 786440 | tf_op jit(solution)/shard_map/ppermute | solution.py:546
  102.0 18.2 %collective-permute-start.25 = (bf16[176,512]{1,0:T(8,128)(2,1)S(1)}, bf16[176,512]{1,0:T(8,128)(2,1)S(1)}, u32[]{:S(2)}, u32[]{:S(2)}) collective-permute-start(bf16[176,512]{1,0:T(8,128)(2,1)S(1)} %add_convert_fusion.2), channel_id=1, source_target_pairs={{0,4},{1,5},{2,6},{3,7},{4,0},{5,1},{6,2},{7,3},{8,12},{9,13},{10,... | collective-permute-start | bytes 540680 | tf_op jit(solution)/shard_map/ppermute | solution.py:546

commit v16 on v15

--- a/solution.py
+++ b/solution.py
@@ -582,8 +582,7 @@
         return [swap(pieces[distance], "ctx", distance) for distance in near]
 
     rows = shard_rows // 2
-    cut = rows * 21 // 32 // 16 * 16
-    middle = rows // 2
+    cuts = (0, rows // 2, rows)
 
     def projected(mine, sibling, *wanted):
         return list(project(wanted, mine, sibling, *w_packed))
@@ -598,36 +597,28 @@
     high = [*high, swap(diagonal_out, "ctx", near[-1])]
     mine = assemble(ctx_index, [pieces[0], *back], (0, rows))
     sibling = [swap(part, "head", 1) for part in mine]
-    (share,) = projected(mine, sibling, [(0, 0, cut)])
-    far = to_next(share, 1)
-    (behind,) = projected(mine, sibling, [(0, cut, rows), (1, 0, rows)])
-    shares = projected(mine, sibling, [(2, 0, cut)], [(2, cut, rows)])
-    (kept,) = projected(mine, sibling, [(3, 0, rows)])
-
-    passed = add(shares[0], far)
-    high, passed, _, shares[1], kept = tie(high, passed, behind, shares[1], kept)
-    behind = to_next(behind, 1)
+    shares = [projected(mine, sibling, [(turn, 0, rows)])[0] for turn in range(len(TURNS))]
+    far = to_next(shares[0], 1)
+    passed = add(shares[2], far)
+    shares, passed = tie(shares, passed)
     across = to_next(passed, 2)
+    near_sum = to_next(shares[1], 1)
+
+    high, kept, passed = tie(high, shares[3], passed)
     pieces = attend(ctx_index, queries, keys, values, docs, low, high)
     back = send_back(pieces)
-    mine = assemble(ctx_index, [pieces[0], *back], (0, cut, rows))
-    mine, across = tie(mine, across)
+    mine = assemble(ctx_index, [pieces[0], *back], cuts)
     sibling = [swap(part, "head", 1) for part in mine]
-    late = projected(mine, sibling, [(0, 0, cut)], [(0, cut, rows)])
-    late, behind = tie(late, behind)
-    far = [to_next(part, 1) for part in late]
-    across = [across, to_next(add(shares[1], behind[: rows - cut]), 2)]
-    late = projected(mine, sibling, [(2, 0, cut)], [(2, cut, rows)])
-    passed = [add(*both) for both in zip(late, far)]
-    passed[0], across[1] = tie(passed[0], across[1])
-    terms = [[(kept, 0)], [(behind, rows - cut)], [(part, 0) for part in across]]
-    result = finish(0, rows, terms, None)
-    across = [to_next(part, 2) for part in passed]
-    late = projected(mine, sibling, [(1, 0, middle)], [(1, middle, rows)])
-    late, passed = tie(late, passed)
-    near_sum = [to_next(part, 1) for part in late]
-    (kept,) = projected(mine, sibling, [(3, 0, rows)])
-    terms = [[(kept, 0)], [(part, 0) for part in near_sum], [(part, 0) for part in across]]
+    late = [projected(mine, sibling, [(turn, 0, rows)])[0] for turn in (0, 2, 3)]
+    late[0], near_sum, across = tie(late[0], near_sum, across)
+    result = finish(0, rows, [[(kept, 0)], [(near_sum, 0)], [(across, 0)]], None)
+    far = to_next(late[0], 1)
+    passed = add(late[1], far)
+    across = to_next(passed, 2)
+    last = projected(mine, sibling, *[[(1, *span)] for span in zip(cuts[:-1], cuts[1:])])
+    last, passed = tie(last, passed)
+    near_sum = [to_next(part, 1) for part in last]
+    terms = [[(late[2], 0)], [(part, 0) for part in near_sum], [(across, 0)]]
     return finish(1, rows, terms, result)
 
 

time: 123 us -> 120 us (0.976)
  starting transfers between devices: 33.7 us -> 26.8 us
  waiting for transfers between devices: 55.2 us -> 59 us
    ppermute x26 -> x23, starting transfers between devices: 33.7 us -> 26.8 us  [swap(): lax.ppermute(value, axis, [(source, source ^ distance) for source in rang...]
    ppermute x26 -> x23, waiting for transfers between devices: 55.2 us -> 59 us  [swap(): lax.ppermute(value, axis, [(source, source ^ distance) for source in rang...]
  transfers between devices with their start and end apart: 26 -> 23, of which waited for: 14 -> 15; matrix products, arithmetic and copies ran while one was open for 1% -> 1% of each run, Pallas kernels for 25% -> 25%
where the time goes in v16:
time: 120 us; the launch traced here: 119 us
  waiting for transfers between devices  59 us (49%)
  Pallas kernels  32 us (27%)
  starting transfers between devices  26.8 us (22%)
    ppermute x23, waiting for transfers between devices, swap(): lax.ppermute(value, axis, [(source, source ^ distance) for source in rang...  59 us
    ppermute x23, starting transfers between devices, swap(): lax.ppermute(value, axis, [(source, source ^ distance) for source in rang...  26.8 us
    pallas_call x2, Pallas kernels, attend(): pl.pallas_call(kernel, grid_spec=pltpu.PrefetchScalarGridSpec(num_scalar_...  13.4 us
    pallas_call x1, Pallas kernels, pack_projection(): pl.pallas_call(kernel, grid_spec=pltpu.PrefetchScalarGridSpec(num_scalar_...  5.7 us
    pallas_call x8, Pallas kernels, project(): pl.pallas_call(kernel, grid=(1,), in_specs=[plain(part.shape) for part in...  5.7 us
    pallas_call x2, Pallas kernels, pack(): pl.pallas_call(kernel, grid_spec=pltpu.PrefetchScalarGridSpec(num_scalar_...  5.03 us
  transfers between devices with their start and end apart: 23, of which 15 were waited for; matrix products, arithmetic and copies ran while one was open for 1% of the time, Pallas kernels for 25%

profile of v16, /device:TPU:0, one launch (start us, length us, event | category | flops | bytes accessed | tf_op | source)
XLA Modules:
  0.0 118.8 jit_solution(13213331966823128194)
XLA Ops:
  0.0 0.5 collective-permute-start.3
  0.5 2.5 %pack.2 = (bf16[1552,128]{1,0:T(8,128)(2,1)}, bf16[1552,128]{1,0:T(8,128)(2,1)}, bf16[1552,128]{1,0:T(8,128)(2,1)}) custom-call(s32[1]{0:T(128)} %bitcast.ctx_ref, bf16[1024,512]{1,0:T(8,128)(2,1)} %refs_3_.4, bf16[1024,512]{1,0:T(8,128)(2,1)} %refs_4_.4, bf16[1024,512]{1,0:T(8,128)(2,1)} %refs_5_.4, bf16[1024,512]{1,0:T(8,128)(2,1)} %refs_3_.4, ...), custom_call_target="tpu_custom_call" | custom-call | flops 1024 | bytes 1024 | tf_op jit(solution)/shard_map/pack/pallas_call | solution.py:201
  2.9 2.5 %collective-permute-start = (bf16[1552,128]{1,0:T(8,128)(2,1)}, bf16[1552,128]{1,0:T(8,128)(2,1)S(1)}, u32[]{:S(2)}, u32[]{:S(2)}) collective-permute-start(bf16[1552,128]{1,0:T(8,128)(2,1)} %get-tuple-element.61), channel_id=1, source_target_pairs={{0,8},{8,0},{16,24},{24,16},{1,9},{9,1},{17,25},{25,17},{2,10},{10... | collective-permute-start | bytes 1191944 | tf_op jit(solution)/shard_map/ppermute | solution.py:546
  5.4 1.5 %collective-permute-start.1 = (bf16[1552,128]{1,0:T(8,128)(2,1)}, bf16[1552,128]{1,0:T(8,128)(2,1)S(1)}, u32[]{:S(2)}, u32[]{:S(2)}) collective-permute-start(bf16[1552,128]{1,0:T(8,128)(2,1)} %get-tuple-element.62), channel_id=1, source_target_pairs={{0,16},{8,24},{16,0},{24,8},{1,17},{9,25},{17,1},{25,9},{2,18},{10... | collective-permute-start | bytes 1191944 | tf_op jit(solution)/shard_map/ppermute | solution.py:546
  7.0 0.0 collective-permute-start.2
  7.0 2.5 %pack.3 = (bf16[1536,128]{1,0:T(8,128)(2,1)}, bf16[1536,128]{1,0:T(8,128)(2,1)}, bf16[1536,128]{1,0:T(8,128)(2,1)}) custom-call(s32[1]{0:T(128)} %bitcast.ctx_ref, bf16[1024,512]{1,0:T(8,128)(2,1)} %refs_3_.4, bf16[1024,512]{1,0:T(8,128)(2,1)} %refs_4_.4, bf16[1024,512]{1,0:T(8,128)(2,1)} %refs_5_.4, bf16[1024,512]{1,0:T(8,128)(2,1)} %refs_3_.4, ...), custom_call_target="tpu_custom_call" | custom-call | flops 1024 | bytes 1024 | tf_op jit(solution)/shard_map/pack/pallas_call | solution.py:201
  9.5 2.0 %collective-permute-start.7 = (bf16[1536,128]{1,0:T(8,128)(2,1)}, bf16[1536,128]{1,0:T(8,128)(2,1)S(1)}, u32[]{:S(2)}, u32[]{:S(2)}) collective-permute-start(bf16[1536,128]{1,0:T(8,128)(2,1)} %get-tuple-element.80), channel_id=1, source_target_pairs={{0,8},{8,0},{16,24},{24,16},{1,9},{9,1},{17,25},{25,17},{2,10},{10... | collective-permute-start | bytes 1179656 | tf_op jit(solution)/shard_map/ppermute | solution.py:546
  11.5 0.0 collective-permute-done.3.sibling_in
  11.5 1.5 %collective-permute-start.8 = (bf16[1536,128]{1,0:T(8,128)(2,1)}, bf16[1536,128]{1,0:T(8,128)(2,1)S(1)}, u32[]{:S(2)}, u32[]{:S(2)}) collective-permute-start(bf16[1536,128]{1,0:T(8,128)(2,1)} %get-tuple-element.81), channel_id=1, source_target_pairs={{0,16},{8,24},{16,0},{24,8},{1,17},{9,25},{17,1},{25,9},{2,18},{10... | collective-permute-start | bytes 1179656 | tf_op jit(solution)/shard_map/ppermute | solution.py:546
  13.0 0.5 broadcast_xor_fusion.places_ref
  13.5 5.7 %pack_projection.1 = (bf16[512,2048]{1,0:T(8,128)(2,1)}, bf16[512,2048]{1,0:T(8,128)(2,1)}) custom-call(s32[4]{0:T(128)} %broadcast_xor_fusion.places_ref, bf16[512,4096]{1,0:T(8,128)(2,1)} %mine_in.1, bf16[512,4096]{1,0:T(8,128)(2,1)} %collective-permute-done.3.sibling_in), custom_call_target="tpu_custom_call" | custom-call | flops 1024 | bytes 1024 | tf_op jit(solution)/shard_map/pack_projection/pallas_call | solution.py:227
  19.2 0.0 collective-permute-done.refs_4_.refs_7_
  19.2 7.0 %collective-permute-done.1.refs_5_.refs_8_ = bf16[1552,128]{1,0:T(8,128)(2,1)S(1)} collective-permute-done((bf16[1552,128]{1,0:T(8,128)(2,1)}, bf16[1552,128]{1,0:T(8,128)(2,1)S(1)}, u32[]{:S(2)}, u32[]{:S(2)}) %collective-permute-start.1) | collective-permute-done | bytes 397344 | tf_op jit(solution)/shard_map/ppermute | solution.py:546
  26.2 0.0 collective-permute-done.2.refs_6_.refs_9_
  26.2 4.7 %attend_low.1 = (bf16[512,128]{1,0:T(8,128)(2,1)S(1)}, bf16[512,128]{1,0:T(8,128)(2,1)S(1)}, bf16[512,128]{1,0:T(8,128)(2,1)S(1)}, bf16[512,128]{1,0:T(8,128)(2,1)S(1)}) custom-call(s32[1]{0:T(128)} %bitcast.ctx_ref, bf16[1024,512]{1,0:T(8,128)(2,1)S(1)} %copy-done.2, bf16[1024,512]{1,0:T(8,128)(2,1)S(1)} %copy-done.3, bf16[1024,512]{1,0:T(8,128)(2,1)S(1)} %copy-done.4, ...), custom_call_target="tpu_custom_call" | custom-call | flops 1024 | bytes 1024 | tf_op jit(solution)/shard_map/attend_low/pallas_call | solution.py:409
  31.0 1.0 collective-permute-start.4
  32.0 1.1 collective-permute-start.5
  33.1 1.4 %collective-permute-start.6 = (bf16[512,128]{1,0:T(8,128)(2,1)S(1)}, bf16[512,128]{1,0:T(8,128)(2,1)S(1)}, u32[]{:S(2)}, u32[]{:S(2)}) collective-permute-start(bf16[512,128]{1,0:T(8,128)(2,1)S(1)} %get-tuple-element.79), channel_id=1, source_target_pairs={{0,24},{8,16},{16,8},{24,0},{1,25},{9,17},{17,9},{25,1},{2,26},{10... | collective-permute-start | bytes 393224 | tf_op jit(solution)/shard_map/ppermute | solution.py:546
  34.5 0.0 collective-permute-done.7.refs_10_
  34.5 0.0 collective-permute-done.8.refs_11_
  34.5 2.6 %collective-permute-done.4.refs_1_ = bf16[512,128]{1,0:T(8,128)(2,1)S(1)} collective-permute-done((bf16[512,128]{1,0:T(8,128)(2,1)S(1)}, bf16[512,128]{1,0:T(8,128)(2,1)S(1)}, u32[]{:S(2)}, u32[]{:S(2)}) %collective-permute-start.4) | collective-permute-done | bytes 131104 | tf_op jit(solution)/shard_map/ppermute | solution.py:546
  37.2 2.4 %collective-permute-done.5.refs_2_ = bf16[512,128]{1,0:T(8,128)(2,1)S(1)} collective-permute-done((bf16[512,128]{1,0:T(8,128)(2,1)S(1)}, bf16[512,128]{1,0:T(8,128)(2,1)S(1)}, u32[]{:S(2)}, u32[]{:S(2)}) %collective-permute-start.5) | collective-permute-done | bytes 131104 | tf_op jit(solution)/shard_map/ppermute | solution.py:546
  39.5 0.0 collective-permute-done.6.refs_3_
  39.5 0.1 assemble.2.refs_0_
  39.6 0.1 collective-permute-start.10
  39.7 1.9 %collective-permute-done.10.refs_1_ = bf16[512,512]{1,0:T(8,128)(2,1)S(1)} collective-permute-done((bf16[512,512]{1,0:T(8,128)(2,1)S(1)}, bf16[512,512]{1,0:T(8,128)(2,1)S(1)}, u32[]{:S(2)}, u32[]{:S(2)}) %collective-permute-start.10) | collective-permute-done | bytes 524320 | tf_op jit(solution)/shard_map/ppermute | solution.py:546
  41.6 0.7 project.8
  42.3 1.6 %collective-permute-start.11 = (bf16[512,512]{1,0:T(8,128)(2,1)S(1)}, bf16[512,512]{1,0:T(8,128)(2,1)S(1)}, u32[]{:S(2)}, u32[]{:S(2)}) collective-permute-start(bf16[512,512]{1,0:T(8,128)(2,1)S(1)} %project.8), channel_id=1, source_target_pairs={{0,2},{1,3},{2,0},{3,1},{4,6},{5,7},{6,4},{7,5},{8,10},{9,11},{10,... | collective-permute-start | bytes 1572872 | tf_op jit(solution)/shard_map/ppermute | solution.py:546
  44.0 1.8 %collective-permute-start.9 = (bf16[1536,128]{1,0:T(8,128)(2,1)S(1)}, bf16[1536,128]{1,0:T(8,128)(2,1)S(1)}, u32[]{:S(2)}, u32[]{:S(2)}) collective-permute-start(bf16[1536,128]{1,0:T(8,128)(2,1)S(1)} %copy-done.6), channel_id=1, source_target_pairs={{0,24},{8,16},{16,8},{24,0},{1,25},{9,17},{17,9},{25,1},{2,26},{10... | collective-permute-start | bytes 1179656 | tf_op jit(solution)/shard_map/ppermute | solution.py:546
  45.7 0.7 project.9
  46.5 0.7 project.10
  47.2 0.7 project.11.refs_0_
  47.9 8.5 %collective-permute-done.11 = bf16[512,512]{1,0:T(8,128)(2,1)S(1)} collective-permute-done((bf16[512,512]{1,0:T(8,128)(2,1)S(1)}, bf16[512,512]{1,0:T(8,128)(2,1)S(1)}, u32[]{:S(2)}, u32[]{:S(2)}) %collective-permute-start.11) | collective-permute-done | bytes 524320 | tf_op jit(solution)/shard_map/ppermute | solution.py:546
  56.4 0.1 add_convert_fusion.1
  56.5 1.6 %collective-permute-start.17 = (bf16[512,512]{1,0:T(8,128)(2,1)S(1)}, bf16[512,512]{1,0:T(8,128)(2,1)S(1)}, u32[]{:S(2)}, u32[]{:S(2)}) collective-permute-start(bf16[512,512]{1,0:T(8,128)(2,1)S(1)} %project.9), channel_id=1, source_target_pairs={{0,2},{1,3},{2,0},{3,1},{4,6},{5,7},{6,4},{7,5},{8,10},{9,11},{10,... | collective-permute-start | bytes 1572872 | tf_op jit(solution)/shard_map/ppermute | solution.py:546
  58.1 2.6 %collective-permute-start.18 = (bf16[512,512]{1,0:T(8,128)(2,1)S(1)}, bf16[512,512]{1,0:T(8,128)(2,1)S(1)}, u32[]{:S(2)}, u32[]{:S(2)}) collective-permute-start(bf16[512,512]{1,0:T(8,128)(2,1)S(1)} %add_convert_fusion.1), channel_id=1, source_target_pairs={{0,4},{1,5},{2,6},{3,7},{4,0},{5,1},{6,2},{7,3},{8,12},{9,13},{10,... | collective-permute-start | bytes 1572872 | tf_op jit(solution)/shard_map/ppermute | solution.py:546
  60.7 8.7 %attend_high.1 = (bf16[512,128]{1,0:T(8,128)(2,1)S(1)}, bf16[512,128]{1,0:T(8,128)(2,1)S(1)}, bf16[512,128]{1,0:T(8,128)(2,1)S(1)}, bf16[512,128]{1,0:T(8,128)(2,1)S(1)}) custom-call(s32[1]{0:T(128)} %bitcast.ctx_ref, bf16[1024,512]{1,0:T(8,128)(2,1)S(1)} %copy-done.2, bf16[1024,512]{1,0:T(8,128)(2,1)S(1)} %copy-done.3, bf16[1024,512]{1,0:T(8,128)(2,1)S(1)} %copy-done.4, ...), custom_call_target="tpu_custom_call" | custom-call | flops 1024 | bytes 1024 | tf_op jit(solution)/shard_map/attend_high/pallas_call | solution.py:409
  69.5 1.3 %collective-permute-start.12 = (bf16[512,128]{1,0:T(8,128)(2,1)S(1)}, bf16[512,128]{1,0:T(8,128)(2,1)S(1)}, u32[]{:S(2)}, u32[]{:S(2)}) collective-permute-start(bf16[512,128]{1,0:T(8,128)(2,1)S(1)} %get-tuple-element.97), channel_id=1, source_target_pairs={{0,8},{8,0},{16,24},{24,16},{1,9},{9,1},{17,25},{25,17},{2,10},{10... | collective-permute-start | bytes 393224 | tf_op jit(solution)/shard_map/ppermute | solution.py:546
  70.8 1.1 collective-permute-start.13
  71.9 1.2 collective-permute-start.14
  73.0 2.8 %collective-permute-done.12.refs_1_ = bf16[512,128]{1,0:T(8,128)(2,1)S(1)} collective-permute-done((bf16[512,128]{1,0:T(8,128)(2,1)S(1)}, bf16[512,128]{1,0:T(8,128)(2,1)S(1)}, u32[]{:S(2)}, u32[]{:S(2)}) %collective-permute-start.12) | collective-permute-done | bytes 131104 | tf_op jit(solution)/shard_map/ppermute | solution.py:546
  75.8 2.1 %collective-permute-done.13.refs_2_ = bf16[512,128]{1,0:T(8,128)(2,1)S(1)} collective-permute-done((bf16[512,128]{1,0:T(8,128)(2,1)S(1)}, bf16[512,128]{1,0:T(8,128)(2,1)S(1)}, u32[]{:S(2)}, u32[]{:S(2)}) %collective-permute-start.13) | collective-permute-done | bytes 131104 | tf_op jit(solution)/shard_map/ppermute | solution.py:546
  77.9 0.1 assemble.3
  78.0 0.1 collective-permute-start.15
  78.1 0.5 collective-permute-start.16
  78.6 1.0 collective-permute-done.15.refs_2_
  79.6 0.4 collective-permute-done.16.refs_3_
  80.0 0.7 project.15
  80.7 0.1 collective-permute-done.17.refs_1_
  80.8 2.4 %collective-permute-done.18.refs_2_ = bf16[512,512]{1,0:T(8,128)(2,1)S(1)} collective-permute-done((bf16[512,512]{1,0:T(8,128)(2,1)S(1)}, bf16[512,512]{1,0:T(8,128)(2,1)S(1)}, u32[]{:S(2)}, u32[]{:S(2)}) %collective-permute-start.18) | collective-permute-done | bytes 524320 | tf_op jit(solution)/shard_map/ppermute | solution.py:546
  83.2 0.4 collective-permute-start.19
  83.6 0.7 project.14
  84.4 10.4 %collective-permute-done.19 = bf16[512,512]{1,0:T(8,128)(2,1)S(1)} collective-permute-done((bf16[512,512]{1,0:T(8,128)(2,1)S(1)}, bf16[512,512]{1,0:T(8,128)(2,1)S(1)}, u32[]{:S(2)}, u32[]{:S(2)}) %collective-permute-start.19) | collective-permute-done | bytes 524320 | tf_op jit(solution)/shard_map/ppermute | solution.py:546
  94.8 0.1 add_convert_fusion
  94.9 1.0 collective-permute-start.22
  95.9 0.7 project.13
  96.6 1.8 %collective-permute-start.20 = (bf16[256,512]{1,0:T(8,128)(2,1)S(1)}, bf16[256,512]{1,0:T(8,128)(2,1)S(1)}, u32[]{:S(2)}, u32[]{:S(2)}) collective-permute-start(bf16[256,512]{1,0:T(8,128)(2,1)S(1)} %get-tuple-element.106), channel_id=1, source_target_pairs={{0,2},{1,3},{2,0},{3,1},{4,6},{5,7},{6,4},{7,5},{8,10},{9,11},{10,... | collective-permute-start | bytes 786440 | tf_op jit(solution)/shard_map/ppermute | solution.py:546
  98.4 0.2 collective-permute-start.21
  98.7 0.7 project.12.refs_0_
  99.4 1.0 finish.2.refs_4_
  100.4 12.6 %collective-permute-done.20.refs_1_ = bf16[256,512]{1,0:T(8,128)(2,1)S(1)} collective-permute-done((bf16[256,512]{1,0:T(8,128)(2,1)S(1)}, bf16[256,512]{1,0:T(8,128)(2,1)S(1)}, u32[]{:S(2)}, u32[]{:S(2)}) %collective-permute-start.20) | collective-permute-done | bytes 262176 | tf_op jit(solution)/shard_map/ppermute | solution.py:546
  113.0 2.8 %collective-permute-done.21.refs_2_ = bf16[256,512]{1,0:T(8,128)(2,1)S(1)} collective-permute-done((bf16[256,512]{1,0:T(8,128)(2,1)S(1)}, bf16[256,512]{1,0:T(8,128)(2,1)S(1)}, u32[]{:S(2)}, u32[]{:S(2)}) %collective-permute-start.21) | collective-permute-done | bytes 262176 | tf_op jit(solution)/shard_map/ppermute | solution.py:546
  115.8 2.0 %collective-permute-done.22.refs_3_ = bf16[512,512]{1,0:T(8,128)(2,1)S(1)} collective-permute-done((bf16[512,512]{1,0:T(8,128)(2,1)S(1)}, bf16[512,512]{1,0:T(8,128)(2,1)S(1)}, u32[]{:S(2)}, u32[]{:S(2)}) %collective-permute-start.22) | collective-permute-done | bytes 524320 | tf_op jit(solution)/shard_map/ppermute | solution.py:546
  117.8 1.0 finish.3
  (18 shorter events, 0.0 us)
Async XLA Ops:
  0.0 11.5 %collective-permute-start.3 = (bf16[512,4096]{1,0:T(8,128)(2,1)}, bf16[512,4096]{1,0:T(8,128)(2,1)}, u32[]{:S(2)}, u32[]{:S(2)}) collective-permute-start(bf16[512,4096]{1,0:T(8,128)(2,1)} %mine_in.1), channel_id=1, source_target_pairs={{0,1},{1,0},{2,3},{3,2},{4,5},{5,4},{6,7},{7,6},{8,9},{9,8},{10,11... | collective-permute-start | bytes 12582920 | tf_op jit(solution)/shard_map/ppermute | solution.py:546
  2.9 10.0 %copy-start.7 = (s32[4]{0:T(128)S(1)}, s32[4]{0:T(128)}, u32[]{:S(2)}) copy-start(s32[4]{0:T(128)} %constant.13) | copy-start | bytes 52
  2.9 16.3 %collective-permute-start = (bf16[1552,128]{1,0:T(8,128)(2,1)}, bf16[1552,128]{1,0:T(8,128)(2,1)S(1)}, u32[]{:S(2)}, u32[]{:S(2)}) collective-permute-start(bf16[1552,128]{1,0:T(8,128)(2,1)} %get-tuple-element.61), channel_id=1, source_target_pairs={{0,8},{8,0},{16,24},{24,16},{1,9},{9,1},{17,25},{25,17},{2,10},{10... | collective-permute-start | bytes 1191944 | tf_op jit(solution)/shard_map/ppermute | solution.py:546
  5.4 20.8 %collective-permute-start.1 = (bf16[1552,128]{1,0:T(8,128)(2,1)}, bf16[1552,128]{1,0:T(8,128)(2,1)S(1)}, u32[]{:S(2)}, u32[]{:S(2)}) collective-permute-start(bf16[1552,128]{1,0:T(8,128)(2,1)} %get-tuple-element.62), channel_id=1, source_target_pairs={{0,16},{8,24},{16,0},{24,8},{1,17},{9,25},{17,1},{25,9},{2,18},{10... | collective-permute-start | bytes 1191944 | tf_op jit(solution)/shard_map/ppermute | solution.py:546
  7.0 19.2 %collective-permute-start.2 = (bf16[1552,128]{1,0:T(8,128)(2,1)}, bf16[1552,128]{1,0:T(8,128)(2,1)S(1)}, u32[]{:S(2)}, u32[]{:S(2)}) collective-permute-start(bf16[1552,128]{1,0:T(8,128)(2,1)} %get-tuple-element.63), channel_id=1, source_target_pairs={{0,24},{8,16},{16,8},{24,0},{1,25},{9,17},{17,9},{25,1},{2,26},{10... | collective-permute-start | bytes 1191944 | tf_op jit(solution)/shard_map/ppermute | solution.py:546
  9.5 25.0 %collective-permute-start.7 = (bf16[1536,128]{1,0:T(8,128)(2,1)}, bf16[1536,128]{1,0:T(8,128)(2,1)S(1)}, u32[]{:S(2)}, u32[]{:S(2)}) collective-permute-start(bf16[1536,128]{1,0:T(8,128)(2,1)} %get-tuple-element.80), channel_id=1, source_target_pairs={{0,8},{8,0},{16,24},{24,16},{1,9},{9,1},{17,25},{25,17},{2,10},{10... | collective-permute-start | bytes 1179656 | tf_op jit(solution)/shard_map/ppermute | solution.py:546
  11.5 23.0 %collective-permute-start.8 = (bf16[1536,128]{1,0:T(8,128)(2,1)}, bf16[1536,128]{1,0:T(8,128)(2,1)S(1)}, u32[]{:S(2)}, u32[]{:S(2)}) collective-permute-start(bf16[1536,128]{1,0:T(8,128)(2,1)} %get-tuple-element.81), channel_id=1, source_target_pairs={{0,16},{8,24},{16,0},{24,8},{1,17},{9,25},{17,1},{25,9},{2,18},{10... | collective-permute-start | bytes 1179656 | tf_op jit(solution)/shard_map/ppermute | solution.py:546
  13.5 12.7 %copy-start.2 = (bf16[1024,512]{1,0:T(8,128)(2,1)S(1)}, bf16[1024,512]{1,0:T(8,128)(2,1)}, u32[]{:S(2)}) copy-start(bf16[1024,512]{1,0:T(8,128)(2,1)} %refs_3_.4) | copy-start | bytes 3145732
  13.5 12.7 %copy-start.3 = (bf16[1024,512]{1,0:T(8,128)(2,1)S(1)}, bf16[1024,512]{1,0:T(8,128)(2,1)}, u32[]{:S(2)}) copy-start(bf16[1024,512]{1,0:T(8,128)(2,1)} %refs_4_.4) | copy-start | bytes 3145732
  13.5 12.7 %copy-start.4 = (bf16[1024,512]{1,0:T(8,128)(2,1)S(1)}, bf16[1024,512]{1,0:T(8,128)(2,1)}, u32[]{:S(2)}) copy-start(bf16[1024,512]{1,0:T(8,128)(2,1)} %refs_5_.4) | copy-start | bytes 3145732
  13.5 12.7 %copy-start.5 = (s32[1024]{0:T(1024)S(1)}, s32[1024]{0:T(1024)}, u32[]{:S(2)}) copy-start(s32[1024]{0:T(1024)} %param.9) | copy-start | bytes 12292
  19.2 22.4 %copy-start = (bf16[512,2048]{1,0:T(8,128)(2,1)S(1)}, bf16[512,2048]{1,0:T(8,128)(2,1)}, u32[]{:S(2)}) copy-start(bf16[512,2048]{1,0:T(8,128)(2,1)} %get-tuple-element.89.refs_2_.refs_4_) | copy-start | bytes 6291460
  19.2 22.4 %copy-start.1 = (bf16[512,2048]{1,0:T(8,128)(2,1)S(1)}, bf16[512,2048]{1,0:T(8,128)(2,1)}, u32[]{:S(2)}) copy-start(bf16[512,2048]{1,0:T(8,128)(2,1)} %get-tuple-element.90.refs_3_.refs_5_) | copy-start | bytes 6291460
  30.9 13.0 %copy-start.6 = (bf16[1536,128]{1,0:T(8,128)(2,1)S(1)}, bf16[1536,128]{1,0:T(8,128)(2,1)}, u32[]{:S(2)}) copy-start(bf16[1536,128]{1,0:T(8,128)(2,1)} %get-tuple-element.84) | copy-start | bytes 1179652
  31.0 6.2 %collective-permute-start.4 = (bf16[512,128]{1,0:T(8,128)(2,1)S(1)}, bf16[512,128]{1,0:T(8,128)(2,1)S(1)}, u32[]{:S(2)}, u32[]{:S(2)}) collective-permute-start(bf16[512,128]{1,0:T(8,128)(2,1)S(1)} %get-tuple-element.77), channel_id=1, source_target_pairs={{0,8},{8,0},{16,24},{24,16},{1,9},{9,1},{17,25},{25,17},{2,10},{10... | collective-permute-start | bytes 393224 | tf_op jit(solution)/shard_map/ppermute | solution.py:546
  32.0 7.6 %collective-permute-start.5 = (bf16[512,128]{1,0:T(8,128)(2,1)S(1)}, bf16[512,128]{1,0:T(8,128)(2,1)S(1)}, u32[]{:S(2)}, u32[]{:S(2)}) collective-permute-start(bf16[512,128]{1,0:T(8,128)(2,1)S(1)} %get-tuple-element.78), channel_id=1, source_target_pairs={{0,16},{8,24},{16,0},{24,8},{1,17},{9,25},{17,1},{25,9},{2,18},{10... | collective-permute-start | bytes 393224 | tf_op jit(solution)/shard_map/ppermute | solution.py:546
  33.1 6.5 %collective-permute-start.6 = (bf16[512,128]{1,0:T(8,128)(2,1)S(1)}, bf16[512,128]{1,0:T(8,128)(2,1)S(1)}, u32[]{:S(2)}, u32[]{:S(2)}) collective-permute-start(bf16[512,128]{1,0:T(8,128)(2,1)S(1)} %get-tuple-element.79), channel_id=1, source_target_pairs={{0,24},{8,16},{16,8},{24,0},{1,25},{9,17},{17,9},{25,1},{2,26},{10... | collective-permute-start | bytes 393224 | tf_op jit(solution)/shard_map/ppermute | solution.py:546
  39.6 2.0 %collective-permute-start.10 = (bf16[512,512]{1,0:T(8,128)(2,1)S(1)}, bf16[512,512]{1,0:T(8,128)(2,1)S(1)}, u32[]{:S(2)}, u32[]{:S(2)}) collective-permute-start(bf16[512,512]{1,0:T(8,128)(2,1)S(1)} %assemble.2.refs_0_), channel_id=1, source_target_pairs={{0,1},{1,0},{2,3},{3,2},{4,5},{5,4},{6,7},{7,6},{8,9},{9,8},{10,11... | collective-permute-start | bytes 1572872 | tf_op jit(solution)/shard_map/ppermute | solution.py:546
  42.3 14.0 %collective-permute-start.11 = (bf16[512,512]{1,0:T(8,128)(2,1)S(1)}, bf16[512,512]{1,0:T(8,128)(2,1)S(1)}, u32[]{:S(2)}, u32[]{:S(2)}) collective-permute-start(bf16[512,512]{1,0:T(8,128)(2,1)S(1)} %project.8), channel_id=1, source_target_pairs={{0,2},{1,3},{2,0},{3,1},{4,6},{5,7},{6,4},{7,5},{8,10},{9,11},{10,... | collective-permute-start | bytes 1572872 | tf_op jit(solution)/shard_map/ppermute | solution.py:546
  44.0 16.8 %collective-permute-start.9 = (bf16[1536,128]{1,0:T(8,128)(2,1)S(1)}, bf16[1536,128]{1,0:T(8,128)(2,1)S(1)}, u32[]{:S(2)}, u32[]{:S(2)}) collective-permute-start(bf16[1536,128]{1,0:T(8,128)(2,1)S(1)} %copy-done.6), channel_id=1, source_target_pairs={{0,24},{8,16},{16,8},{24,0},{1,25},{9,17},{17,9},{25,1},{2,26},{10... | collective-permute-start | bytes 1179656 | tf_op jit(solution)/shard_map/ppermute | solution.py:546
  56.5 24.3 %collective-permute-start.17 = (bf16[512,512]{1,0:T(8,128)(2,1)S(1)}, bf16[512,512]{1,0:T(8,128)(2,1)S(1)}, u32[]{:S(2)}, u32[]{:S(2)}) collective-permute-start(bf16[512,512]{1,0:T(8,128)(2,1)S(1)} %project.9), channel_id=1, source_target_pairs={{0,2},{1,3},{2,0},{3,1},{4,6},{5,7},{6,4},{7,5},{8,10},{9,11},{10,... | collective-permute-start | bytes 1572872 | tf_op jit(solution)/shard_map/ppermute | solution.py:546
  58.1 25.0 %collective-permute-start.18 = (bf16[512,512]{1,0:T(8,128)(2,1)S(1)}, bf16[512,512]{1,0:T(8,128)(2,1)S(1)}, u32[]{:S(2)}, u32[]{:S(2)}) collective-permute-start(bf16[512,512]{1,0:T(8,128)(2,1)S(1)} %add_convert_fusion.1), channel_id=1, source_target_pairs={{0,4},{1,5},{2,6},{3,7},{4,0},{5,1},{6,2},{7,3},{8,12},{9,13},{10,... | collective-permute-start | bytes 1572872 | tf_op jit(solution)/shard_map/ppermute | solution.py:546
  69.5 6.4 %collective-permute-start.12 = (bf16[512,128]{1,0:T(8,128)(2,1)S(1)}, bf16[512,128]{1,0:T(8,128)(2,1)S(1)}, u32[]{:S(2)}, u32[]{:S(2)}) collective-permute-start(bf16[512,128]{1,0:T(8,128)(2,1)S(1)} %get-tuple-element.97), channel_id=1, source_target_pairs={{0,8},{8,0},{16,24},{24,16},{1,9},{9,1},{17,25},{25,17},{2,10},{10... | collective-permute-start | bytes 393224 | tf_op jit(solution)/shard_map/ppermute | solution.py:546
  70.8 7.1 %collective-permute-start.13 = (bf16[512,128]{1,0:T(8,128)(2,1)S(1)}, bf16[512,128]{1,0:T(8,128)(2,1)S(1)}, u32[]{:S(2)}, u32[]{:S(2)}) collective-permute-start(bf16[512,128]{1,0:T(8,128)(2,1)S(1)} %get-tuple-element.98), channel_id=1, source_target_pairs={{0,16},{8,24},{16,0},{24,8},{1,17},{9,25},{17,1},{25,9},{2,18},{10... | collective-permute-start | bytes 393224 | tf_op jit(solution)/shard_map/ppermute | solution.py:546
  71.9 6.1 %collective-permute-start.14 = (bf16[512,128]{1,0:T(8,128)(2,1)S(1)}, bf16[512,128]{1,0:T(8,128)(2,1)S(1)}, u32[]{:S(2)}, u32[]{:S(2)}) collective-permute-start(bf16[512,128]{1,0:T(8,128)(2,1)S(1)} %get-tuple-element.99), channel_id=1, source_target_pairs={{0,24},{8,16},{16,8},{24,0},{1,25},{9,17},{17,9},{25,1},{2,26},{10... | collective-permute-start | bytes 393224 | tf_op jit(solution)/shard_map/ppermute | solution.py:546
  78.0 1.6 %collective-permute-start.15 = (bf16[256,512]{1,0:T(8,128)(2,1)S(1)}, bf16[256,512]{1,0:T(8,128)(2,1)S(1)}, u32[]{:S(2)}, u32[]{:S(2)}) collective-permute-start(bf16[256,512]{1,0:T(8,128)(2,1)S(1)} %get-tuple-element.100.refs_0_), channel_id=1, source_target_pairs={{0,1},{1,0},{2,3},{3,2},{4,5},{5,4},{6,7},{7,6},{8,9},{9,8},{10,11... | collective-permute-start | bytes 786440 | tf_op jit(solution)/shard_map/ppermute | solution.py:546
  78.1 1.9 %collective-permute-start.16 = (bf16[256,512]{1,0:T(8,128)(2,1)S(1)}, bf16[256,512]{1,0:T(8,128)(2,1)S(1)}, u32[]{:S(2)}, u32[]{:S(2)}) collective-permute-start(bf16[256,512]{1,0:T(8,128)(2,1)S(1)} %get-tuple-element.101.refs_1_), channel_id=1, source_target_pairs={{0,1},{1,0},{2,3},{3,2},{4,5},{5,4},{6,7},{7,6},{8,9},{9,8},{10,11... | collective-permute-start | bytes 786440 | tf_op jit(solution)/shard_map/ppermute | solution.py:546
  83.2 11.6 %collective-permute-start.19 = (bf16[512,512]{1,0:T(8,128)(2,1)S(1)}, bf16[512,512]{1,0:T(8,128)(2,1)S(1)}, u32[]{:S(2)}, u32[]{:S(2)}) collective-permute-start(bf16[512,512]{1,0:T(8,128)(2,1)S(1)} %project.15), channel_id=1, source_target_pairs={{0,2},{1,3},{2,0},{3,1},{4,6},{5,7},{6,4},{7,5},{8,10},{9,11},{10,... | collective-permute-start | bytes 1572872 | tf_op jit(solution)/shard_map/ppermute | solution.py:546
  94.9 22.9 %collective-permute-start.22 = (bf16[512,512]{1,0:T(8,128)(2,1)S(1)}, bf16[512,512]{1,0:T(8,128)(2,1)S(1)}, u32[]{:S(2)}, u32[]{:S(2)}) collective-permute-start(bf16[512,512]{1,0:T(8,128)(2,1)S(1)} %add_convert_fusion), channel_id=1, source_target_pairs={{0,4},{1,5},{2,6},{3,7},{4,0},{5,1},{6,2},{7,3},{8,12},{9,13},{10,... | collective-permute-start | bytes 1572872 | tf_op jit(solution)/shard_map/ppermute | solution.py:546
  96.6 16.4 %collective-permute-start.20 = (bf16[256,512]{1,0:T(8,128)(2,1)S(1)}, bf16[256,512]{1,0:T(8,128)(2,1)S(1)}, u32[]{:S(2)}, u32[]{:S(2)}) collective-permute-start(bf16[256,512]{1,0:T(8,128)(2,1)S(1)} %get-tuple-element.106), channel_id=1, source_target_pairs={{0,2},{1,3},{2,0},{3,1},{4,6},{5,7},{6,4},{7,5},{8,10},{9,11},{10,... | collective-permute-start | bytes 786440 | tf_op jit(solution)/shard_map/ppermute | solution.py:546
  98.4 17.4 %collective-permute-start.21 = (bf16[256,512]{1,0:T(8,128)(2,1)S(1)}, bf16[256,512]{1,0:T(8,128)(2,1)S(1)}, u32[]{:S(2)}, u32[]{:S(2)}) collective-permute-start(bf16[256,512]{1,0:T(8,128)(2,1)S(1)} %get-tuple-element.107), channel_id=1, source_target_pairs={{0,2},{1,3},{2,0},{3,1},{4,6},{5,7},{6,4},{7,5},{8,10},{9,11},{10,... | collective-permute-start | bytes 786440 | tf_op jit(solution)/shard_map/ppermute | solution.py:546

commit v17 on v16

--- a/solution.py
+++ b/solution.py
@@ -239,11 +239,12 @@
     )(places, w_mine, w_sibling)
 
 
-def attend(ctx_index, queries, keys, values, docs, low, high):
+def attend(ctx_index, queries, keys, values, docs, low, high, tiles):
     rows = queries.shape[0] // 2
     group = queries.shape[1] // HD
     with_high = high is not None
     per_block = rows // TILE
+    slots_each = len(tiles)
     lines = rows // HD
     key_rows = (2 * group if with_high else group) * rows
     key_tiles = key_rows // TILE
@@ -326,13 +327,13 @@
         firsts = []
         counts = []
         for lane in range(group):
-            for slot in range(per_block):
+            for slot, tile in enumerate(tiles):
                 distance = lane ^ (slot * (group - 1))
-                query = part(with_high, distance, 0, slot * TILE, TILE)
+                query = part(with_high, distance, 0, tile * TILE, TILE)
                 query_buf[lane][slot] = query
-                start = starts[distance][:, slot * TILE : (slot + 1) * TILE]
+                start = starts[distance][:, tile * TILE : (tile + 1) * TILE]
                 start_buf[lane][slot, 0:1, :] = start
-                end = place[with_high, distance] * per_block + slot
+                end = place[with_high, distance] * per_block + tile
                 offset = pl.multiple_of(end * TILE, TILE)
                 least = start - offset.astype(jnp.float32)
                 scores = scores_of(query, offset)
@@ -346,7 +347,7 @@
 
         longest = jnp.int32(0)
         for lane in range(group):
-            of_lane = counts[lane * per_block : (lane + 1) * per_block]
+            of_lane = counts[lane * slots_each : (lane + 1) * slots_each]
             longest = jnp.maximum(longest, sum(of_lane))
 
         def visit(step, carry):
@@ -355,12 +356,12 @@
             beyonds = []
             for lane in range(group):
                 slot = jnp.int32(0)
-                index = firsts[lane * per_block] + step
-                before = counts[lane * per_block]
-                for later in range(1, per_block):
+                index = firsts[lane * slots_each] + step
+                before = counts[lane * slots_each]
+                for later in range(1, slots_each):
                     reached = step >= before
                     slot = jnp.where(reached, later, slot)
-                    place_later = lane * per_block + later
+                    place_later = lane * slots_each + later
                     index = jnp.where(reached, firsts[place_later] + step - before, index)
                     before = before + counts[place_later]
                 offset = pl.multiple_of(jnp.minimum(index, key_tiles - 1) * TILE, TILE)
@@ -387,7 +388,7 @@
 
         lax.fori_loop(0, longest, visit, jnp.int32(0))
         for lane in range(group):
-            for slot in range(per_block):
+            for slot in range(slots_each):
                 state = summed[lane]
                 attended = state[slot, :HD, :] * (1.0 / state[slot, HD : HD + 1, :])
                 out = outs[lane ^ (slot * (group - 1))]
@@ -412,17 +413,17 @@
             num_scalar_prefetch=1,
             grid=(1,),
             in_specs=in_specs,
-            out_specs=[whole((rows, HD))] * group,
+            out_specs=[whole((slots_each * TILE, HD))] * group,
             scratch_shapes=[
                 pltpu.VMEM((key_rows, HD), jnp.bfloat16),
                 pltpu.VMEM((HD + 16, key_rows), jnp.bfloat16),
                 pltpu.VMEM((key_rows // HD, HD), jnp.float32),
-                *[pltpu.VMEM((per_block, TILE, HD), jnp.bfloat16)] * group,
-                *[pltpu.VMEM((per_block, 8, TILE), jnp.float32)] * (2 * group),
-                *[pltpu.VMEM((per_block, HD + 16, TILE), jnp.float32)] * group,
+                *[pltpu.VMEM((slots_each, TILE, HD), jnp.bfloat16)] * group,
+                *[pltpu.VMEM((slots_each, 8, TILE), jnp.float32)] * (2 * group),
+                *[pltpu.VMEM((slots_each, HD + 16, TILE), jnp.float32)] * group,
             ],
         ),
-        out_shape=[jax.ShapeDtypeStruct((rows, HD), jnp.bfloat16)] * group,
+        out_shape=[jax.ShapeDtypeStruct((slots_each * TILE, HD), jnp.bfloat16)] * group,
         compiler_params=params(40),
         cost_estimate=SMALL,
         name="attend_high" if with_high else "attend_low",
@@ -582,7 +583,6 @@
         return [swap(pieces[distance], "ctx", distance) for distance in near]
 
     rows = shard_rows // 2
-    cuts = (0, rows // 2, rows)
 
     def projected(mine, sibling, *wanted):
         return list(project(wanted, mine, sibling, *w_packed))
@@ -590,7 +590,8 @@
     def to_next(part, distance):
         return swap(part, "head", 2 * distance)
 
-    pieces = attend(ctx_index, queries, keys, values, docs, low, None)
+    tiles = tuple(range(rows // TILE))
+    pieces = attend(ctx_index, queries, keys, values, docs, low, None, tiles)
     pieces, diagonal_out = tie(pieces, high_out[-1])
     back = send_back(pieces)
     back, high = tie(back, high)
@@ -599,26 +600,37 @@
     sibling = [swap(part, "head", 1) for part in mine]
     shares = [projected(mine, sibling, [(turn, 0, rows)])[0] for turn in range(len(TURNS))]
     far = to_next(shares[0], 1)
+    near_sum = to_next(shares[1], 1)
     passed = add(shares[2], far)
-    shares, passed = tie(shares, passed)
-    across = to_next(passed, 2)
-    near_sum = to_next(shares[1], 1)
-
-    high, kept, passed = tie(high, shares[3], passed)
-    pieces = attend(ctx_index, queries, keys, values, docs, low, high)
-    back = send_back(pieces)
-    mine = assemble(ctx_index, [pieces[0], *back], cuts)
-    sibling = [swap(part, "head", 1) for part in mine]
-    late = [projected(mine, sibling, [(turn, 0, rows)])[0] for turn in (0, 2, 3)]
-    late[0], near_sum, across = tie(late[0], near_sum, across)
-    result = finish(0, rows, [[(kept, 0)], [(near_sum, 0)], [(across, 0)]], None)
-    far = to_next(late[0], 1)
-    passed = add(late[1], far)
-    across = to_next(passed, 2)
-    last = projected(mine, sibling, *[[(1, *span)] for span in zip(cuts[:-1], cuts[1:])])
-    last, passed = tie(last, passed)
-    near_sum = [to_next(part, 1) for part in last]
-    terms = [[(late[2], 0)], [(part, 0) for part in near_sum], [(across, 0)]]
+    high, shares = tie(high, shares)
+
+    mine = []
+    for tile in tiles:
+        pieces = attend(ctx_index, queries, keys, values, docs, low, high, (tile,))
+        back = send_back(pieces)
+        if tile == 0:
+            pieces, passed = tie(pieces, passed)
+            across = to_next(passed, 2)
+            high, passed = tie(high, passed)
+        mine += assemble(ctx_index, [pieces[0], *back], (0, TILE))
+    far = []
+    sibling = []
+    for part in mine:
+        sibling.append(swap(part, "head", 1))
+        (share,) = projected([part], [sibling[-1]], [(0, 0, TILE)])
+        if far:
+            share, near_sum, across = tie(share, near_sum, across)
+        far.append(to_next(share, 1))
+    result = finish(0, rows, [[(shares[3], 0)], [(near_sum, 0)], [(across, 0)]], None)
+    spans = [(tile * TILE, (tile + 1) * TILE) for tile in tiles]
+    late = projected(mine, sibling, *[[(2, *span)] for span in spans])
+    passed = [add(*both) for both in zip(late, far)]
+    across = [to_next(part, 2) for part in passed]
+    late = projected(mine, sibling, *[[(1, *span)] for span in spans])
+    late, passed = tie(late, passed)
+    near_sum = [to_next(part, 1) for part in late]
+    (kept,) = projected(mine, sibling, [(3, 0, rows)])
+    terms = [[(kept, 0)], [(part, 0) for part in near_sum], [(part, 0) for part in across]]
     return finish(1, rows, terms, result)
 
 

time: 120 us -> 128 us (1.067)
  waiting for transfers between devices: 59 us -> 64.4 us
  Pallas kernels: 32 us -> 33.5 us
  starting transfers between devices: 26.8 us -> 28.1 us
    ppermute x23 -> x28, waiting for transfers between devices: 59 us -> 64.4 us  [swap(): lax.ppermute(value, axis, [(source, source ^ distance) for source in rang...]
    pallas_call x2 -> x3, Pallas kernels: 13.4 us -> 14.7 us  [attend(): pl.pallas_call(kernel, grid_spec=pltpu.PrefetchScalarGridSpec(num_scalar_...]
    ppermute x23 -> x28, starting transfers between devices: 26.8 us -> 28.1 us  [swap(): lax.ppermute(value, axis, [(source, source ^ distance) for source in rang...]
    pallas_call x8 -> x9, Pallas kernels: 5.7 us -> 5.84 us  [project(): pl.pallas_call(kernel, grid=(1,), in_specs=[plain(part.shape) for part in...]
  transfers between devices with their start and end apart: 23 -> 28, of which waited for: 15 -> 15; matrix products, arithmetic and copies ran while one was open for 1% -> 1% of each run, Pallas kernels for 25% -> 25%
where the time goes in v17:
time: 128 us; the launch traced here: 127 us
  waiting for transfers between devices  64.4 us (50%)
  Pallas kernels  33.5 us (26%)
  starting transfers between devices  28.1 us (22%)
    ppermute x28, waiting for transfers between devices, swap(): lax.ppermute(value, axis, [(source, source ^ distance) for source in rang...  64.4 us
    ppermute x28, starting transfers between devices, swap(): lax.ppermute(value, axis, [(source, source ^ distance) for source in rang...  28.1 us
    pallas_call x3, Pallas kernels, attend(): pl.pallas_call(kernel, grid_spec=pltpu.PrefetchScalarGridSpec(num_scalar_...  14.7 us
    pallas_call x9, Pallas kernels, project(): pl.pallas_call(kernel, grid=(1,), in_specs=[plain(part.shape) for part in...  5.84 us
    pallas_call x1, Pallas kernels, pack_projection(): pl.pallas_call(kernel, grid_spec=pltpu.PrefetchScalarGridSpec(num_scalar_...  5.72 us
    pallas_call x2, Pallas kernels, pack(): pl.pallas_call(kernel, grid_spec=pltpu.PrefetchScalarGridSpec(num_scalar_...  5.02 us
  transfers between devices with their start and end apart: 28, of which 15 were waited for; matrix products, arithmetic and copies ran while one was open for 1% of the time, Pallas kernels for 25%

profile of v17, /device:TPU:0, one launch (start us, length us, event | category | flops | bytes accessed | tf_op | source)
XLA Modules:
  0.0 127.1 jit_solution(4234642700817647769)
XLA Ops:
  0.0 0.5 collective-permute-start.3
  0.5 2.5 %pack.2 = (bf16[1552,128]{1,0:T(8,128)(2,1)}, bf16[1552,128]{1,0:T(8,128)(2,1)}, bf16[1552,128]{1,0:T(8,128)(2,1)}) custom-call(s32[1]{0:T(128)} %bitcast.ctx_ref, bf16[1024,512]{1,0:T(8,128)(2,1)} %refs_3_.6, bf16[1024,512]{1,0:T(8,128)(2,1)} %refs_4_.6, bf16[1024,512]{1,0:T(8,128)(2,1)} %refs_5_.6, bf16[1024,512]{1,0:T(8,128)(2,1)} %refs_3_.6, ...), custom_call_target="tpu_custom_call" | custom-call | flops 1024 | bytes 1024 | tf_op jit(solution)/shard_map/pack/pallas_call | solution.py:201
  3.0 2.5 %collective-permute-start = (bf16[1552,128]{1,0:T(8,128)(2,1)}, bf16[1552,128]{1,0:T(8,128)(2,1)S(1)}, u32[]{:S(2)}, u32[]{:S(2)}) collective-permute-start(bf16[1552,128]{1,0:T(8,128)(2,1)} %get-tuple-element.67), channel_id=1, source_target_pairs={{0,8},{8,0},{16,24},{24,16},{1,9},{9,1},{17,25},{25,17},{2,10},{10... | collective-permute-start | bytes 1191944 | tf_op jit(solution)/shard_map/ppermute | solution.py:547
  5.4 1.5 %collective-permute-start.1 = (bf16[1552,128]{1,0:T(8,128)(2,1)}, bf16[1552,128]{1,0:T(8,128)(2,1)S(1)}, u32[]{:S(2)}, u32[]{:S(2)}) collective-permute-start(bf16[1552,128]{1,0:T(8,128)(2,1)} %get-tuple-element.68), channel_id=1, source_target_pairs={{0,16},{8,24},{16,0},{24,8},{1,17},{9,25},{17,1},{25,9},{2,18},{10... | collective-permute-start | bytes 1191944 | tf_op jit(solution)/shard_map/ppermute | solution.py:547
  7.0 0.0 collective-permute-start.2
  7.0 2.5 %pack.3 = (bf16[1536,128]{1,0:T(8,128)(2,1)}, bf16[1536,128]{1,0:T(8,128)(2,1)}, bf16[1536,128]{1,0:T(8,128)(2,1)}) custom-call(s32[1]{0:T(128)} %bitcast.ctx_ref, bf16[1024,512]{1,0:T(8,128)(2,1)} %refs_3_.6, bf16[1024,512]{1,0:T(8,128)(2,1)} %refs_4_.6, bf16[1024,512]{1,0:T(8,128)(2,1)} %refs_5_.6, bf16[1024,512]{1,0:T(8,128)(2,1)} %refs_3_.6, ...), custom_call_target="tpu_custom_call" | custom-call | flops 1024 | bytes 1024 | tf_op jit(solution)/shard_map/pack/pallas_call | solution.py:201
  9.5 2.0 %collective-permute-start.7 = (bf16[1536,128]{1,0:T(8,128)(2,1)}, bf16[1536,128]{1,0:T(8,128)(2,1)S(1)}, u32[]{:S(2)}, u32[]{:S(2)}) collective-permute-start(bf16[1536,128]{1,0:T(8,128)(2,1)} %get-tuple-element.86), channel_id=1, source_target_pairs={{0,8},{8,0},{16,24},{24,16},{1,9},{9,1},{17,25},{25,17},{2,10},{10... | collective-permute-start | bytes 1179656 | tf_op jit(solution)/shard_map/ppermute | solution.py:547
  11.5 1.5 %collective-permute-start.8 = (bf16[1536,128]{1,0:T(8,128)(2,1)}, bf16[1536,128]{1,0:T(8,128)(2,1)S(1)}, u32[]{:S(2)}, u32[]{:S(2)}) collective-permute-start(bf16[1536,128]{1,0:T(8,128)(2,1)} %get-tuple-element.87), channel_id=1, source_target_pairs={{0,16},{8,24},{16,0},{24,8},{1,17},{9,25},{17,1},{25,9},{2,18},{10... | collective-permute-start | bytes 1179656 | tf_op jit(solution)/shard_map/ppermute | solution.py:547
  13.0 0.5 broadcast_xor_fusion.places_ref
  13.5 5.7 %pack_projection.1 = (bf16[512,2048]{1,0:T(8,128)(2,1)}, bf16[512,2048]{1,0:T(8,128)(2,1)}) custom-call(s32[4]{0:T(128)} %broadcast_xor_fusion.places_ref, bf16[512,4096]{1,0:T(8,128)(2,1)} %mine_in.1, bf16[512,4096]{1,0:T(8,128)(2,1)} %collective-permute-done.3.sibling_in), custom_call_target="tpu_custom_call" | custom-call | flops 1024 | bytes 1024 | tf_op jit(solution)/shard_map/pack_projection/pallas_call | solution.py:227
  19.3 6.9 %collective-permute-done.1.refs_5_.refs_8_ = bf16[1552,128]{1,0:T(8,128)(2,1)S(1)} collective-permute-done((bf16[1552,128]{1,0:T(8,128)(2,1)}, bf16[1552,128]{1,0:T(8,128)(2,1)S(1)}, u32[]{:S(2)}, u32[]{:S(2)}) %collective-permute-start.1) | collective-permute-done | bytes 397344 | tf_op jit(solution)/shard_map/ppermute | solution.py:547
  26.2 7.3 %attend_low.1 = (bf16[512,128]{1,0:T(8,128)(2,1)S(1)}, bf16[512,128]{1,0:T(8,128)(2,1)S(1)}, bf16[512,128]{1,0:T(8,128)(2,1)S(1)}, bf16[512,128]{1,0:T(8,128)(2,1)S(1)}) custom-call(s32[1]{0:T(128)} %bitcast.ctx_ref, bf16[1024,512]{1,0:T(8,128)(2,1)S(1)} %copy-done.2, bf16[1024,512]{1,0:T(8,128)(2,1)S(1)} %copy-done.3, bf16[1024,512]{1,0:T(8,128)(2,1)S(1)} %copy-done.4, ...), custom_call_target="tpu_custom_call" | custom-call | flops 1024 | bytes 1024 | tf_op jit(solution)/shard_map/attend_low/pallas_call | solution.py:410
  33.5 1.0 collective-permute-start.4
  34.5 1.1 collective-permute-start.5
  35.7 1.4 %collective-permute-start.6 = (bf16[512,128]{1,0:T(8,128)(2,1)S(1)}, bf16[512,128]{1,0:T(8,128)(2,1)S(1)}, u32[]{:S(2)}, u32[]{:S(2)}) collective-permute-start(bf16[512,128]{1,0:T(8,128)(2,1)S(1)} %get-tuple-element.85), channel_id=1, source_target_pairs={{0,24},{8,16},{16,8},{24,0},{1,25},{9,17},{17,9},{25,1},{2,26},{10... | collective-permute-start | bytes 393224 | tf_op jit(solution)/shard_map/ppermute | solution.py:547
  37.1 2.6 %collective-permute-done.4.refs_1_ = bf16[512,128]{1,0:T(8,128)(2,1)S(1)} collective-permute-done((bf16[512,128]{1,0:T(8,128)(2,1)S(1)}, bf16[512,128]{1,0:T(8,128)(2,1)S(1)}, u32[]{:S(2)}, u32[]{:S(2)}) %collective-permute-start.4) | collective-permute-done | bytes 131104 | tf_op jit(solution)/shard_map/ppermute | solution.py:547
  39.7 2.1 %collective-permute-done.5.refs_2_ = bf16[512,128]{1,0:T(8,128)(2,1)S(1)} collective-permute-done((bf16[512,128]{1,0:T(8,128)(2,1)S(1)}, bf16[512,128]{1,0:T(8,128)(2,1)S(1)}, u32[]{:S(2)}, u32[]{:S(2)}) %collective-permute-start.5) | collective-permute-done | bytes 131104 | tf_op jit(solution)/shard_map/ppermute | solution.py:547
  41.8 0.1 assemble.3.refs_0_
  41.9 0.1 collective-permute-start.10
  42.0 1.9 %collective-permute-done.10.refs_1_ = bf16[512,512]{1,0:T(8,128)(2,1)S(1)} collective-permute-done((bf16[512,512]{1,0:T(8,128)(2,1)S(1)}, bf16[512,512]{1,0:T(8,128)(2,1)S(1)}, u32[]{:S(2)}, u32[]{:S(2)}) %collective-permute-start.10) | collective-permute-done | bytes 524320 | tf_op jit(solution)/shard_map/ppermute | solution.py:547
  43.9 0.7 project.9
  44.6 1.6 %collective-permute-start.11 = (bf16[512,512]{1,0:T(8,128)(2,1)S(1)}, bf16[512,512]{1,0:T(8,128)(2,1)S(1)}, u32[]{:S(2)}, u32[]{:S(2)}) collective-permute-start(bf16[512,512]{1,0:T(8,128)(2,1)S(1)} %project.9), channel_id=1, source_target_pairs={{0,2},{1,3},{2,0},{3,1},{4,6},{5,7},{6,4},{7,5},{8,10},{9,11},{10,... | collective-permute-start | bytes 1572872 | tf_op jit(solution)/shard_map/ppermute | solution.py:547
  46.3 1.8 %collective-permute-start.9 = (bf16[1536,128]{1,0:T(8,128)(2,1)S(1)}, bf16[1536,128]{1,0:T(8,128)(2,1)S(1)}, u32[]{:S(2)}, u32[]{:S(2)}) collective-permute-start(bf16[1536,128]{1,0:T(8,128)(2,1)S(1)} %copy-done.6), channel_id=1, source_target_pairs={{0,24},{8,16},{16,8},{24,0},{1,25},{9,17},{17,9},{25,1},{2,26},{10... | collective-permute-start | bytes 1179656 | tf_op jit(solution)/shard_map/ppermute | solution.py:547
  48.0 0.7 project.10
  48.7 0.5 collective-permute-start.21
  49.3 0.7 project.11
  50.0 0.7 project.12.refs_0_
  50.7 7.3 %collective-permute-done.9.refs_12_ = bf16[1536,128]{1,0:T(8,128)(2,1)S(1)} collective-permute-done((bf16[1536,128]{1,0:T(8,128)(2,1)S(1)}, bf16[1536,128]{1,0:T(8,128)(2,1)S(1)}, u32[]{:S(2)}, u32[]{:S(2)}) %collective-permute-start.9) | collective-permute-done | bytes 393248 | tf_op jit(solution)/shard_map/ppermute | solution.py:547
  58.0 3.6 %attend_high.2 = (bf16[256,128]{1,0:T(8,128)(2,1)S(1)}, bf16[256,128]{1,0:T(8,128)(2,1)S(1)}, bf16[256,128]{1,0:T(8,128)(2,1)S(1)}, bf16[256,128]{1,0:T(8,128)(2,1)S(1)}) custom-call(s32[1]{0:T(128)} %bitcast.ctx_ref, bf16[1024,512]{1,0:T(8,128)(2,1)S(1)} %copy-done.2, bf16[1024,512]{1,0:T(8,128)(2,1)S(1)} %copy-done.3, bf16[1024,512]{1,0:T(8,128)(2,1)S(1)} %copy-done.4, ...), custom_call_target="tpu_custom_call" | custom-call | flops 1024 | bytes 1024 | tf_op jit(solution)/shard_map/attend_high/pallas_call | solution.py:410
  61.7 1.4 %collective-permute-start.12 = (bf16[256,128]{1,0:T(8,128)(2,1)S(1)}, bf16[256,128]{1,0:T(8,128)(2,1)S(1)}, u32[]{:S(2)}, u32[]{:S(2)}) collective-permute-start(bf16[256,128]{1,0:T(8,128)(2,1)S(1)} %get-tuple-element.101), channel_id=1, source_target_pairs={{0,8},{8,0},{16,24},{24,16},{1,9},{9,1},{17,25},{25,17},{2,10},{10... | collective-permute-start | bytes 196616 | tf_op jit(solution)/shard_map/ppermute | solution.py:547
  63.1 1.0 collective-permute-start.13
  64.1 1.2 collective-permute-start.14
  65.2 0.1 add_convert_fusion
  65.4 2.7 %collective-permute-start.22 = (bf16[512,512]{1,0:T(8,128)(2,1)S(1)}, bf16[512,512]{1,0:T(8,128)(2,1)S(1)}, u32[]{:S(2)}, u32[]{:S(2)}) collective-permute-start(bf16[512,512]{1,0:T(8,128)(2,1)S(1)} %add_convert_fusion), channel_id=1, source_target_pairs={{0,4},{1,5},{2,6},{3,7},{4,0},{5,1},{6,2},{7,3},{8,12},{9,13},{10,... | collective-permute-start | bytes 1572872 | tf_op jit(solution)/shard_map/ppermute | solution.py:547
  68.0 1.2 collective-permute-done.14.refs_3_
  69.3 0.1 collective-permute-start.18
  69.4 3.8 %attend_high.3 = (bf16[256,128]{1,0:T(8,128)(2,1)S(1)}, bf16[256,128]{1,0:T(8,128)(2,1)S(1)}, bf16[256,128]{1,0:T(8,128)(2,1)S(1)}, bf16[256,128]{1,0:T(8,128)(2,1)S(1)}) custom-call(s32[1]{0:T(128)} %bitcast.ctx_ref, bf16[1024,512]{1,0:T(8,128)(2,1)S(1)} %copy-done.2, bf16[1024,512]{1,0:T(8,128)(2,1)S(1)} %copy-done.3, bf16[1024,512]{1,0:T(8,128)(2,1)S(1)} %copy-done.4, ...), custom_call_target="tpu_custom_call" | custom-call | flops 1024 | bytes 1024 | tf_op jit(solution)/shard_map/attend_high/pallas_call | solution.py:410
  73.2 1.2 collective-permute-start.15
  74.4 0.6 collective-permute-start.16
  75.0 2.8 %collective-permute-done.15.refs_1_ = bf16[256,128]{1,0:T(8,128)(2,1)S(1)} collective-permute-done((bf16[256,128]{1,0:T(8,128)(2,1)S(1)}, bf16[256,128]{1,0:T(8,128)(2,1)S(1)}, u32[]{:S(2)}, u32[]{:S(2)}) %collective-permute-start.15) | collective-permute-done | bytes 65568 | tf_op jit(solution)/shard_map/ppermute | solution.py:547
  77.7 1.2 collective-permute-start.17
  78.9 4.0 %collective-permute-done.17.refs_3_ = bf16[256,128]{1,0:T(8,128)(2,1)S(1)} collective-permute-done((bf16[256,128]{1,0:T(8,128)(2,1)S(1)}, bf16[256,128]{1,0:T(8,128)(2,1)S(1)}, u32[]{:S(2)}, u32[]{:S(2)}) %collective-permute-start.17) | collective-permute-done | bytes 65568 | tf_op jit(solution)/shard_map/ppermute | solution.py:547
  83.0 0.1 collective-permute-start.19
  83.0 0.4 project.16
  83.5 0.5 collective-permute-start.20
  84.0 0.6 collective-permute-done.19.refs_3_.refs_1_
  84.6 0.4 project.17
  85.0 4.7 %collective-permute-done.22.refs_2_ = bf16[512,512]{1,0:T(8,128)(2,1)S(1)} collective-permute-done((bf16[512,512]{1,0:T(8,128)(2,1)S(1)}, bf16[512,512]{1,0:T(8,128)(2,1)S(1)}, u32[]{:S(2)}, u32[]{:S(2)}) %collective-permute-start.22) | collective-permute-done | bytes 524320 | tf_op jit(solution)/shard_map/ppermute | solution.py:547
  89.7 0.7 project.14
  90.4 0.7 project.15
  91.1 4.1 %collective-permute-done.20 = bf16[256,512]{1,0:T(8,128)(2,1)S(1)} collective-permute-done((bf16[256,512]{1,0:T(8,128)(2,1)S(1)}, bf16[256,512]{1,0:T(8,128)(2,1)S(1)}, u32[]{:S(2)}, u32[]{:S(2)}) %collective-permute-start.20) | collective-permute-done | bytes 262176 | tf_op jit(solution)/shard_map/ppermute | solution.py:547
  95.3 0.1 add_convert_fusion.2
  95.3 0.6 collective-permute-start.26
  95.9 6.0 %collective-permute-done.23 = bf16[256,512]{1,0:T(8,128)(2,1)S(1)} collective-permute-done((bf16[256,512]{1,0:T(8,128)(2,1)S(1)}, bf16[256,512]{1,0:T(8,128)(2,1)S(1)}, u32[]{:S(2)}, u32[]{:S(2)}) %collective-permute-start.23) | collective-permute-done | bytes 262176 | tf_op jit(solution)/shard_map/ppermute | solution.py:547
  101.9 0.1 add_convert_fusion.1
  102.0 0.1 collective-permute-start.24
  102.1 2.0 %collective-permute-start.25 = (bf16[256,512]{1,0:T(8,128)(2,1)S(1)}, bf16[256,512]{1,0:T(8,128)(2,1)S(1)}, u32[]{:S(2)}, u32[]{:S(2)}) collective-permute-start(bf16[256,512]{1,0:T(8,128)(2,1)S(1)} %get-tuple-element.119), channel_id=1, source_target_pairs={{0,2},{1,3},{2,0},{3,1},{4,6},{5,7},{6,4},{7,5},{8,10},{9,11},{10,... | collective-permute-start | bytes 786440 | tf_op jit(solution)/shard_map/ppermute | solution.py:547
  104.1 0.1 collective-permute-start.27
  104.2 0.7 project.13.refs_0_
  104.9 1.0 finish.2.refs_5_
  105.9 5.1 %collective-permute-done.26.refs_3_ = bf16[256,512]{1,0:T(8,128)(2,1)S(1)} collective-permute-done((bf16[256,512]{1,0:T(8,128)(2,1)S(1)}, bf16[256,512]{1,0:T(8,128)(2,1)S(1)}, u32[]{:S(2)}, u32[]{:S(2)}) %collective-permute-start.26) | collective-permute-done | bytes 262176 | tf_op jit(solution)/shard_map/ppermute | solution.py:547
  111.0 10.2 %collective-permute-done.24.refs_1_ = bf16[256,512]{1,0:T(8,128)(2,1)S(1)} collective-permute-done((bf16[256,512]{1,0:T(8,128)(2,1)S(1)}, bf16[256,512]{1,0:T(8,128)(2,1)S(1)}, u32[]{:S(2)}, u32[]{:S(2)}) %collective-permute-start.24) | collective-permute-done | bytes 262176 | tf_op jit(solution)/shard_map/ppermute | solution.py:547
  121.2 4.9 %collective-permute-done.25.refs_2_ = bf16[256,512]{1,0:T(8,128)(2,1)S(1)} collective-permute-done((bf16[256,512]{1,0:T(8,128)(2,1)S(1)}, bf16[256,512]{1,0:T(8,128)(2,1)S(1)}, u32[]{:S(2)}, u32[]{:S(2)}) %collective-permute-start.25) | collective-permute-done | bytes 262176 | tf_op jit(solution)/shard_map/ppermute | solution.py:547
  126.1 1.0 finish.3
  (32 shorter events, 0.2 us)
Async XLA Ops:
  0.0 11.5 %collective-permute-start.3 = (bf16[512,4096]{1,0:T(8,128)(2,1)}, bf16[512,4096]{1,0:T(8,128)(2,1)}, u32[]{:S(2)}, u32[]{:S(2)}) collective-permute-start(bf16[512,4096]{1,0:T(8,128)(2,1)} %mine_in.1), channel_id=1, source_target_pairs={{0,1},{1,0},{2,3},{3,2},{4,5},{5,4},{6,7},{7,6},{8,9},{9,8},{10,11... | collective-permute-start | bytes 12582920 | tf_op jit(solution)/shard_map/ppermute | solution.py:547
  2.9 10.0 %copy-start.7 = (s32[4]{0:T(128)S(1)}, s32[4]{0:T(128)}, u32[]{:S(2)}) copy-start(s32[4]{0:T(128)} %constant.13) | copy-start | bytes 52
  3.0 16.3 %collective-permute-start = (bf16[1552,128]{1,0:T(8,128)(2,1)}, bf16[1552,128]{1,0:T(8,128)(2,1)S(1)}, u32[]{:S(2)}, u32[]{:S(2)}) collective-permute-start(bf16[1552,128]{1,0:T(8,128)(2,1)} %get-tuple-element.67), channel_id=1, source_target_pairs={{0,8},{8,0},{16,24},{24,16},{1,9},{9,1},{17,25},{25,17},{2,10},{10... | collective-permute-start | bytes 1191944 | tf_op jit(solution)/shard_map/ppermute | solution.py:547
  5.4 20.8 %collective-permute-start.1 = (bf16[1552,128]{1,0:T(8,128)(2,1)}, bf16[1552,128]{1,0:T(8,128)(2,1)S(1)}, u32[]{:S(2)}, u32[]{:S(2)}) collective-permute-start(bf16[1552,128]{1,0:T(8,128)(2,1)} %get-tuple-element.68), channel_id=1, source_target_pairs={{0,16},{8,24},{16,0},{24,8},{1,17},{9,25},{17,1},{25,9},{2,18},{10... | collective-permute-start | bytes 1191944 | tf_op jit(solution)/shard_map/ppermute | solution.py:547
  7.0 19.2 %collective-permute-start.2 = (bf16[1552,128]{1,0:T(8,128)(2,1)}, bf16[1552,128]{1,0:T(8,128)(2,1)S(1)}, u32[]{:S(2)}, u32[]{:S(2)}) collective-permute-start(bf16[1552,128]{1,0:T(8,128)(2,1)} %get-tuple-element.69), channel_id=1, source_target_pairs={{0,24},{8,16},{16,8},{24,0},{1,25},{9,17},{17,9},{25,1},{2,26},{10... | collective-permute-start | bytes 1191944 | tf_op jit(solution)/shard_map/ppermute | solution.py:547
  9.5 27.6 %collective-permute-start.7 = (bf16[1536,128]{1,0:T(8,128)(2,1)}, bf16[1536,128]{1,0:T(8,128)(2,1)S(1)}, u32[]{:S(2)}, u32[]{:S(2)}) collective-permute-start(bf16[1536,128]{1,0:T(8,128)(2,1)} %get-tuple-element.86), channel_id=1, source_target_pairs={{0,8},{8,0},{16,24},{24,16},{1,9},{9,1},{17,25},{25,17},{2,10},{10... | collective-permute-start | bytes 1179656 | tf_op jit(solution)/shard_map/ppermute | solution.py:547
  11.5 25.6 %collective-permute-start.8 = (bf16[1536,128]{1,0:T(8,128)(2,1)}, bf16[1536,128]{1,0:T(8,128)(2,1)S(1)}, u32[]{:S(2)}, u32[]{:S(2)}) collective-permute-start(bf16[1536,128]{1,0:T(8,128)(2,1)} %get-tuple-element.87), channel_id=1, source_target_pairs={{0,16},{8,24},{16,0},{24,8},{1,17},{9,25},{17,1},{25,9},{2,18},{10... | collective-permute-start | bytes 1179656 | tf_op jit(solution)/shard_map/ppermute | solution.py:547
  13.5 12.7 %copy-start.2 = (bf16[1024,512]{1,0:T(8,128)(2,1)S(1)}, bf16[1024,512]{1,0:T(8,128)(2,1)}, u32[]{:S(2)}) copy-start(bf16[1024,512]{1,0:T(8,128)(2,1)} %refs_3_.6) | copy-start | bytes 3145732
  13.5 12.7 %copy-start.3 = (bf16[1024,512]{1,0:T(8,128)(2,1)S(1)}, bf16[1024,512]{1,0:T(8,128)(2,1)}, u32[]{:S(2)}) copy-start(bf16[1024,512]{1,0:T(8,128)(2,1)} %refs_4_.6) | copy-start | bytes 3145732
  13.5 12.7 %copy-start.4 = (bf16[1024,512]{1,0:T(8,128)(2,1)S(1)}, bf16[1024,512]{1,0:T(8,128)(2,1)}, u32[]{:S(2)}) copy-start(bf16[1024,512]{1,0:T(8,128)(2,1)} %refs_5_.6) | copy-start | bytes 3145732
  13.5 12.7 %copy-start.5 = (s32[1024]{0:T(1024)S(1)}, s32[1024]{0:T(1024)}, u32[]{:S(2)}) copy-start(s32[1024]{0:T(1024)} %param.9) | copy-start | bytes 12292
  19.3 24.6 %copy-start = (bf16[512,2048]{1,0:T(8,128)(2,1)S(1)}, bf16[512,2048]{1,0:T(8,128)(2,1)}, u32[]{:S(2)}) copy-start(bf16[512,2048]{1,0:T(8,128)(2,1)} %get-tuple-element.95.refs_2_.refs_4_) | copy-start | bytes 6291460
  19.3 24.6 %copy-start.1 = (bf16[512,2048]{1,0:T(8,128)(2,1)S(1)}, bf16[512,2048]{1,0:T(8,128)(2,1)}, u32[]{:S(2)}) copy-start(bf16[512,2048]{1,0:T(8,128)(2,1)} %get-tuple-element.96.refs_3_.refs_5_) | copy-start | bytes 6291460
  33.5 12.7 %copy-start.6 = (bf16[1536,128]{1,0:T(8,128)(2,1)S(1)}, bf16[1536,128]{1,0:T(8,128)(2,1)}, u32[]{:S(2)}) copy-start(bf16[1536,128]{1,0:T(8,128)(2,1)} %get-tuple-element.90) | copy-start | bytes 1179652
  33.5 6.2 %collective-permute-start.4 = (bf16[512,128]{1,0:T(8,128)(2,1)S(1)}, bf16[512,128]{1,0:T(8,128)(2,1)S(1)}, u32[]{:S(2)}, u32[]{:S(2)}) collective-permute-start(bf16[512,128]{1,0:T(8,128)(2,1)S(1)} %get-tuple-element.83), channel_id=1, source_target_pairs={{0,8},{8,0},{16,24},{24,16},{1,9},{9,1},{17,25},{25,17},{2,10},{10... | collective-permute-start | bytes 393224 | tf_op jit(solution)/shard_map/ppermute | solution.py:547
  34.5 7.3 %collective-permute-start.5 = (bf16[512,128]{1,0:T(8,128)(2,1)S(1)}, bf16[512,128]{1,0:T(8,128)(2,1)S(1)}, u32[]{:S(2)}, u32[]{:S(2)}) collective-permute-start(bf16[512,128]{1,0:T(8,128)(2,1)S(1)} %get-tuple-element.84), channel_id=1, source_target_pairs={{0,16},{8,24},{16,0},{24,8},{1,17},{9,25},{17,1},{25,9},{2,18},{10... | collective-permute-start | bytes 393224 | tf_op jit(solution)/shard_map/ppermute | solution.py:547
  35.7 6.2 %collective-permute-start.6 = (bf16[512,128]{1,0:T(8,128)(2,1)S(1)}, bf16[512,128]{1,0:T(8,128)(2,1)S(1)}, u32[]{:S(2)}, u32[]{:S(2)}) collective-permute-start(bf16[512,128]{1,0:T(8,128)(2,1)S(1)} %get-tuple-element.85), channel_id=1, source_target_pairs={{0,24},{8,16},{16,8},{24,0},{1,25},{9,17},{17,9},{25,1},{2,26},{10... | collective-permute-start | bytes 393224 | tf_op jit(solution)/shard_map/ppermute | solution.py:547
  41.9 2.0 %collective-permute-start.10 = (bf16[512,512]{1,0:T(8,128)(2,1)S(1)}, bf16[512,512]{1,0:T(8,128)(2,1)S(1)}, u32[]{:S(2)}, u32[]{:S(2)}) collective-permute-start(bf16[512,512]{1,0:T(8,128)(2,1)S(1)} %assemble.3.refs_0_), channel_id=1, source_target_pairs={{0,1},{1,0},{2,3},{3,2},{4,5},{5,4},{6,7},{7,6},{8,9},{9,8},{10,11... | collective-permute-start | bytes 1572872 | tf_op jit(solution)/shard_map/ppermute | solution.py:547
  44.6 20.6 %collective-permute-start.11 = (bf16[512,512]{1,0:T(8,128)(2,1)S(1)}, bf16[512,512]{1,0:T(8,128)(2,1)S(1)}, u32[]{:S(2)}, u32[]{:S(2)}) collective-permute-start(bf16[512,512]{1,0:T(8,128)(2,1)S(1)} %project.9), channel_id=1, source_target_pairs={{0,2},{1,3},{2,0},{3,1},{4,6},{5,7},{6,4},{7,5},{8,10},{9,11},{10,... | collective-permute-start | bytes 1572872 | tf_op jit(solution)/shard_map/ppermute | solution.py:547
  46.3 11.8 %collective-permute-start.9 = (bf16[1536,128]{1,0:T(8,128)(2,1)S(1)}, bf16[1536,128]{1,0:T(8,128)(2,1)S(1)}, u32[]{:S(2)}, u32[]{:S(2)}) collective-permute-start(bf16[1536,128]{1,0:T(8,128)(2,1)S(1)} %copy-done.6), channel_id=1, source_target_pairs={{0,24},{8,16},{16,8},{24,0},{1,25},{9,17},{17,9},{25,1},{2,26},{10... | collective-permute-start | bytes 1179656 | tf_op jit(solution)/shard_map/ppermute | solution.py:547
  48.7 36.3 %collective-permute-start.21 = (bf16[512,512]{1,0:T(8,128)(2,1)S(1)}, bf16[512,512]{1,0:T(8,128)(2,1)S(1)}, u32[]{:S(2)}, u32[]{:S(2)}) collective-permute-start(bf16[512,512]{1,0:T(8,128)(2,1)S(1)} %project.10), channel_id=1, source_target_pairs={{0,2},{1,3},{2,0},{3,1},{4,6},{5,7},{6,4},{7,5},{8,10},{9,11},{10,... | collective-permute-start | bytes 1572872 | tf_op jit(solution)/shard_map/ppermute | solution.py:547
  61.7 6.4 %collective-permute-start.12 = (bf16[256,128]{1,0:T(8,128)(2,1)S(1)}, bf16[256,128]{1,0:T(8,128)(2,1)S(1)}, u32[]{:S(2)}, u32[]{:S(2)}) collective-permute-start(bf16[256,128]{1,0:T(8,128)(2,1)S(1)} %get-tuple-element.101), channel_id=1, source_target_pairs={{0,8},{8,0},{16,24},{24,16},{1,9},{9,1},{17,25},{25,17},{2,10},{10... | collective-permute-start | bytes 196616 | tf_op jit(solution)/shard_map/ppermute | solution.py:547
  63.1 4.9 %collective-permute-start.13 = (bf16[256,128]{1,0:T(8,128)(2,1)S(1)}, bf16[256,128]{1,0:T(8,128)(2,1)S(1)}, u32[]{:S(2)}, u32[]{:S(2)}) collective-permute-start(bf16[256,128]{1,0:T(8,128)(2,1)S(1)} %get-tuple-element.102), channel_id=1, source_target_pairs={{0,16},{8,24},{16,0},{24,8},{1,17},{9,25},{17,1},{25,9},{2,18},{10... | collective-permute-start | bytes 196616 | tf_op jit(solution)/shard_map/ppermute | solution.py:547
  64.1 5.2 %collective-permute-start.14 = (bf16[256,128]{1,0:T(8,128)(2,1)S(1)}, bf16[256,128]{1,0:T(8,128)(2,1)S(1)}, u32[]{:S(2)}, u32[]{:S(2)}) collective-permute-start(bf16[256,128]{1,0:T(8,128)(2,1)S(1)} %get-tuple-element.103), channel_id=1, source_target_pairs={{0,24},{8,16},{16,8},{24,0},{1,25},{9,17},{17,9},{25,1},{2,26},{10... | collective-permute-start | bytes 196616 | tf_op jit(solution)/shard_map/ppermute | solution.py:547
  65.4 24.3 %collective-permute-start.22 = (bf16[512,512]{1,0:T(8,128)(2,1)S(1)}, bf16[512,512]{1,0:T(8,128)(2,1)S(1)}, u32[]{:S(2)}, u32[]{:S(2)}) collective-permute-start(bf16[512,512]{1,0:T(8,128)(2,1)S(1)} %add_convert_fusion), channel_id=1, source_target_pairs={{0,4},{1,5},{2,6},{3,7},{4,0},{5,1},{6,2},{7,3},{8,12},{9,13},{10,... | collective-permute-start | bytes 1572872 | tf_op jit(solution)/shard_map/ppermute | solution.py:547
  69.3 13.7 %collective-permute-start.18 = (bf16[256,512]{1,0:T(8,128)(2,1)S(1)}, bf16[256,512]{1,0:T(8,128)(2,1)S(1)}, u32[]{:S(2)}, u32[]{:S(2)}) collective-permute-start(bf16[256,512]{1,0:T(8,128)(2,1)S(1)} %assemble.4.refs_0_), channel_id=1, source_target_pairs={{0,1},{1,0},{2,3},{3,2},{4,5},{5,4},{6,7},{7,6},{8,9},{9,8},{10,11... | collective-permute-start | bytes 786440 | tf_op jit(solution)/shard_map/ppermute | solution.py:547
  73.2 4.5 %collective-permute-start.15 = (bf16[256,128]{1,0:T(8,128)(2,1)S(1)}, bf16[256,128]{1,0:T(8,128)(2,1)S(1)}, u32[]{:S(2)}, u32[]{:S(2)}) collective-permute-start(bf16[256,128]{1,0:T(8,128)(2,1)S(1)} %get-tuple-element.110), channel_id=1, source_target_pairs={{0,8},{8,0},{16,24},{24,16},{1,9},{9,1},{17,25},{25,17},{2,10},{10... | collective-permute-start | bytes 196616 | tf_op jit(solution)/shard_map/ppermute | solution.py:547
  74.4 4.5 %collective-permute-start.16 = (bf16[256,128]{1,0:T(8,128)(2,1)S(1)}, bf16[256,128]{1,0:T(8,128)(2,1)S(1)}, u32[]{:S(2)}, u32[]{:S(2)}) collective-permute-start(bf16[256,128]{1,0:T(8,128)(2,1)S(1)} %get-tuple-element.111), channel_id=1, source_target_pairs={{0,16},{8,24},{16,0},{24,8},{1,17},{9,25},{17,1},{25,9},{2,18},{10... | collective-permute-start | bytes 196616 | tf_op jit(solution)/shard_map/ppermute | solution.py:547
  77.7 5.2 %collective-permute-start.17 = (bf16[256,128]{1,0:T(8,128)(2,1)S(1)}, bf16[256,128]{1,0:T(8,128)(2,1)S(1)}, u32[]{:S(2)}, u32[]{:S(2)}) collective-permute-start(bf16[256,128]{1,0:T(8,128)(2,1)S(1)} %get-tuple-element.112), channel_id=1, source_target_pairs={{0,24},{8,16},{16,8},{24,0},{1,25},{9,17},{17,9},{25,1},{2,26},{10... | collective-permute-start | bytes 196616 | tf_op jit(solution)/shard_map/ppermute | solution.py:547
  83.0 1.6 %collective-permute-start.19 = (bf16[256,512]{1,0:T(8,128)(2,1)S(1)}, bf16[256,512]{1,0:T(8,128)(2,1)S(1)}, u32[]{:S(2)}, u32[]{:S(2)}) collective-permute-start(bf16[256,512]{1,0:T(8,128)(2,1)S(1)} %assemble.5.refs_1_.refs_0_), channel_id=1, source_target_pairs={{0,1},{1,0},{2,3},{3,2},{4,5},{5,4},{6,7},{7,6},{8,9},{9,8},{10,11... | collective-permute-start | bytes 786440 | tf_op jit(solution)/shard_map/ppermute | solution.py:547
  83.5 11.8 %collective-permute-start.20 = (bf16[256,512]{1,0:T(8,128)(2,1)S(1)}, bf16[256,512]{1,0:T(8,128)(2,1)S(1)}, u32[]{:S(2)}, u32[]{:S(2)}) collective-permute-start(bf16[256,512]{1,0:T(8,128)(2,1)S(1)} %project.16), channel_id=1, source_target_pairs={{0,2},{1,3},{2,0},{3,1},{4,6},{5,7},{6,4},{7,5},{8,10},{9,11},{10,... | collective-permute-start | bytes 786440 | tf_op jit(solution)/shard_map/ppermute | solution.py:547
  89.7 12.2 %collective-permute-start.23 = (bf16[256,512]{1,0:T(8,128)(2,1)S(1)}, bf16[256,512]{1,0:T(8,128)(2,1)S(1)}, u32[]{:S(2)}, u32[]{:S(2)}) collective-permute-start(bf16[256,512]{1,0:T(8,128)(2,1)S(1)} %project.17), channel_id=1, source_target_pairs={{0,2},{1,3},{2,0},{3,1},{4,6},{5,7},{6,4},{7,5},{8,10},{9,11},{10,... | collective-permute-start | bytes 786440 | tf_op jit(solution)/shard_map/ppermute | solution.py:547
  95.3 15.7 %collective-permute-start.26 = (bf16[256,512]{1,0:T(8,128)(2,1)S(1)}, bf16[256,512]{1,0:T(8,128)(2,1)S(1)}, u32[]{:S(2)}, u32[]{:S(2)}) collective-permute-start(bf16[256,512]{1,0:T(8,128)(2,1)S(1)} %add_convert_fusion.2), channel_id=1, source_target_pairs={{0,4},{1,5},{2,6},{3,7},{4,0},{5,1},{6,2},{7,3},{8,12},{9,13},{10,... | collective-permute-start | bytes 786440 | tf_op jit(solution)/shard_map/ppermute | solution.py:547
  102.0 19.2 %collective-permute-start.24 = (bf16[256,512]{1,0:T(8,128)(2,1)S(1)}, bf16[256,512]{1,0:T(8,128)(2,1)S(1)}, u32[]{:S(2)}, u32[]{:S(2)}) collective-permute-start(bf16[256,512]{1,0:T(8,128)(2,1)S(1)} %get-tuple-element.118), channel_id=1, source_target_pairs={{0,2},{1,3},{2,0},{3,1},{4,6},{5,7},{6,4},{7,5},{8,10},{9,11},{10,... | collective-permute-start | bytes 786440 | tf_op jit(solution)/shard_map/ppermute | solution.py:547
  102.1 24.0 %collective-permute-start.25 = (bf16[256,512]{1,0:T(8,128)(2,1)S(1)}, bf16[256,512]{1,0:T(8,128)(2,1)S(1)}, u32[]{:S(2)}, u32[]{:S(2)}) collective-permute-start(bf16[256,512]{1,0:T(8,128)(2,1)S(1)} %get-tuple-element.119), channel_id=1, source_target_pairs={{0,2},{1,3},{2,0},{3,1},{4,6},{5,7},{6,4},{7,5},{8,10},{9,11},{10,... | collective-permute-start | bytes 786440 | tf_op jit(solution)/shard_map/ppermute | solution.py:547
  104.1 22.0 %collective-permute-start.27 = (bf16[256,512]{1,0:T(8,128)(2,1)S(1)}, bf16[256,512]{1,0:T(8,128)(2,1)S(1)}, u32[]{:S(2)}, u32[]{:S(2)}) collective-permute-start(bf16[256,512]{1,0:T(8,128)(2,1)S(1)} %add_convert_fusion.1), channel_id=1, source_target_pairs={{0,4},{1,5},{2,6},{3,7},{4,0},{5,1},{6,2},{7,3},{8,12},{9,13},{10,... | collective-permute-start | bytes 786440 | tf_op jit(solution)/shard_map/ppermute | solution.py:547

commit v18 on v16

--- a/solution.py
+++ b/solution.py
@@ -599,19 +599,18 @@
     sibling = [swap(part, "head", 1) for part in mine]
     shares = [projected(mine, sibling, [(turn, 0, rows)])[0] for turn in range(len(TURNS))]
     far = to_next(shares[0], 1)
+    near_sum = to_next(shares[1], 1)
     passed = add(shares[2], far)
-    shares, passed = tie(shares, passed)
+
+    high, shares, passed = tie(high, shares, passed)
     across = to_next(passed, 2)
-    near_sum = to_next(shares[1], 1)
-
-    high, kept, passed = tie(high, shares[3], passed)
     pieces = attend(ctx_index, queries, keys, values, docs, low, high)
     back = send_back(pieces)
     mine = assemble(ctx_index, [pieces[0], *back], cuts)
     sibling = [swap(part, "head", 1) for part in mine]
     late = [projected(mine, sibling, [(turn, 0, rows)])[0] for turn in (0, 2, 3)]
     late[0], near_sum, across = tie(late[0], near_sum, across)
-    result = finish(0, rows, [[(kept, 0)], [(near_sum, 0)], [(across, 0)]], None)
+    result = finish(0, rows, [[(shares[3], 0)], [(near_sum, 0)], [(across, 0)]], None)
     far = to_next(late[0], 1)
     passed = add(late[1], far)
     across = to_next(passed, 2)

time: 120 us -> 119 us (level); the launches traced: 119 us -> 119 us
  starting transfers between devices: 26.8 us -> 28.1 us
    ppermute x23, starting transfers between devices: 26.8 us -> 28.1 us  [swap(): lax.ppermute(value, axis, [(source, source ^ distance) for source in rang...]
where the time goes in v18:
time: 119 us
  waiting for transfers between devices  58.6 us (49%)
  Pallas kernels  31.4 us (26%)
  starting transfers between devices  28.1 us (24%)
    ppermute x23, waiting for transfers between devices, swap(): lax.ppermute(value, axis, [(source, source ^ distance) for source in rang...  58.6 us
    ppermute x23, starting transfers between devices, swap(): lax.ppermute(value, axis, [(source, source ^ distance) for source in rang...  28.1 us
    pallas_call x2, Pallas kernels, attend(): pl.pallas_call(kernel, grid_spec=pltpu.PrefetchScalarGridSpec(num_scalar_...  12.8 us
    pallas_call x1, Pallas kernels, pack_projection(): pl.pallas_call(kernel, grid_spec=pltpu.PrefetchScalarGridSpec(num_scalar_...  5.7 us
    pallas_call x8, Pallas kernels, project(): pl.pallas_call(kernel, grid=(1,), in_specs=[plain(part.shape) for part in...  5.7 us
    pallas_call x2, Pallas kernels, pack(): pl.pallas_call(kernel, grid_spec=pltpu.PrefetchScalarGridSpec(num_scalar_...  5.03 us
  transfers between devices with their start and end apart: 23, of which 15 were waited for; matrix products, arithmetic and copies ran while one was open for 1% of the time, Pallas kernels for 25%

profile of v18, /device:TPU:0, one launch (start us, length us, event | category | flops | bytes accessed | tf_op | source)
XLA Modules:
  0.0 119.0 jit_solution(3796030443779209727)
XLA Ops:
  0.0 0.5 collective-permute-start.3
  0.5 2.5 %pack.2 = (bf16[1552,128]{1,0:T(8,128)(2,1)}, bf16[1552,128]{1,0:T(8,128)(2,1)}, bf16[1552,128]{1,0:T(8,128)(2,1)}) custom-call(s32[1]{0:T(128)} %bitcast.ctx_ref, bf16[1024,512]{1,0:T(8,128)(2,1)} %refs_3_.4, bf16[1024,512]{1,0:T(8,128)(2,1)} %refs_4_.4, bf16[1024,512]{1,0:T(8,128)(2,1)} %refs_5_.4, bf16[1024,512]{1,0:T(8,128)(2,1)} %refs_3_.4, ...), custom_call_target="tpu_custom_call" | custom-call | flops 1024 | bytes 1024 | tf_op jit(solution)/shard_map/pack/pallas_call | solution.py:201
  2.9 2.5 %collective-permute-start = (bf16[1552,128]{1,0:T(8,128)(2,1)}, bf16[1552,128]{1,0:T(8,128)(2,1)S(1)}, u32[]{:S(2)}, u32[]{:S(2)}) collective-permute-start(bf16[1552,128]{1,0:T(8,128)(2,1)} %get-tuple-element.59), channel_id=1, source_target_pairs={{0,8},{8,0},{16,24},{24,16},{1,9},{9,1},{17,25},{25,17},{2,10},{10... | collective-permute-start | bytes 1191944 | tf_op jit(solution)/shard_map/ppermute | solution.py:546
  5.4 1.5 %collective-permute-start.1 = (bf16[1552,128]{1,0:T(8,128)(2,1)}, bf16[1552,128]{1,0:T(8,128)(2,1)S(1)}, u32[]{:S(2)}, u32[]{:S(2)}) collective-permute-start(bf16[1552,128]{1,0:T(8,128)(2,1)} %get-tuple-element.60), channel_id=1, source_target_pairs={{0,16},{8,24},{16,0},{24,8},{1,17},{9,25},{17,1},{25,9},{2,18},{10... | collective-permute-start | bytes 1191944 | tf_op jit(solution)/shard_map/ppermute | solution.py:546
  7.0 0.0 collective-permute-start.2
  7.0 2.5 %pack.3 = (bf16[1536,128]{1,0:T(8,128)(2,1)}, bf16[1536,128]{1,0:T(8,128)(2,1)}, bf16[1536,128]{1,0:T(8,128)(2,1)}) custom-call(s32[1]{0:T(128)} %bitcast.ctx_ref, bf16[1024,512]{1,0:T(8,128)(2,1)} %refs_3_.4, bf16[1024,512]{1,0:T(8,128)(2,1)} %refs_4_.4, bf16[1024,512]{1,0:T(8,128)(2,1)} %refs_5_.4, bf16[1024,512]{1,0:T(8,128)(2,1)} %refs_3_.4, ...), custom_call_target="tpu_custom_call" | custom-call | flops 1024 | bytes 1024 | tf_op jit(solution)/shard_map/pack/pallas_call | solution.py:201
  9.5 2.0 %collective-permute-start.7 = (bf16[1536,128]{1,0:T(8,128)(2,1)}, bf16[1536,128]{1,0:T(8,128)(2,1)S(1)}, u32[]{:S(2)}, u32[]{:S(2)}) collective-permute-start(bf16[1536,128]{1,0:T(8,128)(2,1)} %get-tuple-element.78), channel_id=1, source_target_pairs={{0,8},{8,0},{16,24},{24,16},{1,9},{9,1},{17,25},{25,17},{2,10},{10... | collective-permute-start | bytes 1179656 | tf_op jit(solution)/shard_map/ppermute | solution.py:546
  11.5 1.5 %collective-permute-start.8 = (bf16[1536,128]{1,0:T(8,128)(2,1)}, bf16[1536,128]{1,0:T(8,128)(2,1)S(1)}, u32[]{:S(2)}, u32[]{:S(2)}) collective-permute-start(bf16[1536,128]{1,0:T(8,128)(2,1)} %get-tuple-element.79), channel_id=1, source_target_pairs={{0,16},{8,24},{16,0},{24,8},{1,17},{9,25},{17,1},{25,9},{2,18},{10... | collective-permute-start | bytes 1179656 | tf_op jit(solution)/shard_map/ppermute | solution.py:546
  13.0 0.5 broadcast_xor_fusion.places_ref
  13.5 5.7 %pack_projection.1 = (bf16[512,2048]{1,0:T(8,128)(2,1)}, bf16[512,2048]{1,0:T(8,128)(2,1)}) custom-call(s32[4]{0:T(128)} %broadcast_xor_fusion.places_ref, bf16[512,4096]{1,0:T(8,128)(2,1)} %mine_in.1, bf16[512,4096]{1,0:T(8,128)(2,1)} %collective-permute-done.3.sibling_in), custom_call_target="tpu_custom_call" | custom-call | flops 1024 | bytes 1024 | tf_op jit(solution)/shard_map/pack_projection/pallas_call | solution.py:227
  19.2 7.0 %collective-permute-done.1.refs_5_.refs_8_ = bf16[1552,128]{1,0:T(8,128)(2,1)S(1)} collective-permute-done((bf16[1552,128]{1,0:T(8,128)(2,1)}, bf16[1552,128]{1,0:T(8,128)(2,1)S(1)}, u32[]{:S(2)}, u32[]{:S(2)}) %collective-permute-start.1) | collective-permute-done | bytes 397344 | tf_op jit(solution)/shard_map/ppermute | solution.py:546
  26.2 0.0 collective-permute-done.2.refs_6_.refs_9_
  26.2 6.0 %attend_low.1 = (bf16[512,128]{1,0:T(8,128)(2,1)S(1)}, bf16[512,128]{1,0:T(8,128)(2,1)S(1)}, bf16[512,128]{1,0:T(8,128)(2,1)S(1)}, bf16[512,128]{1,0:T(8,128)(2,1)S(1)}) custom-call(s32[1]{0:T(128)} %bitcast.ctx_ref, bf16[1024,512]{1,0:T(8,128)(2,1)S(1)} %copy-done.2, bf16[1024,512]{1,0:T(8,128)(2,1)S(1)} %copy-done.3, bf16[1024,512]{1,0:T(8,128)(2,1)S(1)} %copy-done.4, ...), custom_call_target="tpu_custom_call" | custom-call | flops 1024 | bytes 1024 | tf_op jit(solution)/shard_map/attend_low/pallas_call | solution.py:409
  32.2 1.0 collective-permute-start.4
  33.3 1.1 collective-permute-start.5
  34.4 1.4 %collective-permute-start.6 = (bf16[512,128]{1,0:T(8,128)(2,1)S(1)}, bf16[512,128]{1,0:T(8,128)(2,1)S(1)}, u32[]{:S(2)}, u32[]{:S(2)}) collective-permute-start(bf16[512,128]{1,0:T(8,128)(2,1)S(1)} %get-tuple-element.77), channel_id=1, source_target_pairs={{0,24},{8,16},{16,8},{24,0},{1,25},{9,17},{17,9},{25,1},{2,26},{10... | collective-permute-start | bytes 393224 | tf_op jit(solution)/shard_map/ppermute | solution.py:546
  35.8 0.0 collective-permute-done.7.refs_10_
  35.8 0.0 collective-permute-done.8.refs_11_
  35.8 2.6 %collective-permute-done.4.refs_1_ = bf16[512,128]{1,0:T(8,128)(2,1)S(1)} collective-permute-done((bf16[512,128]{1,0:T(8,128)(2,1)S(1)}, bf16[512,128]{1,0:T(8,128)(2,1)S(1)}, u32[]{:S(2)}, u32[]{:S(2)}) %collective-permute-start.4) | collective-permute-done | bytes 131104 | tf_op jit(solution)/shard_map/ppermute | solution.py:546
  38.4 2.1 %collective-permute-done.5.refs_2_ = bf16[512,128]{1,0:T(8,128)(2,1)S(1)} collective-permute-done((bf16[512,128]{1,0:T(8,128)(2,1)S(1)}, bf16[512,128]{1,0:T(8,128)(2,1)S(1)}, u32[]{:S(2)}, u32[]{:S(2)}) %collective-permute-start.5) | collective-permute-done | bytes 131104 | tf_op jit(solution)/shard_map/ppermute | solution.py:546
  40.5 0.0 collective-permute-done.6.refs_3_
  40.5 0.1 assemble.2.refs_0_
  40.6 0.1 collective-permute-start.10
  40.7 1.9 %collective-permute-done.10.refs_1_ = bf16[512,512]{1,0:T(8,128)(2,1)S(1)} collective-permute-done((bf16[512,512]{1,0:T(8,128)(2,1)S(1)}, bf16[512,512]{1,0:T(8,128)(2,1)S(1)}, u32[]{:S(2)}, u32[]{:S(2)}) %collective-permute-start.10) | collective-permute-done | bytes 524320 | tf_op jit(solution)/shard_map/ppermute | solution.py:546
  42.6 0.7 project.8
  43.3 1.6 %collective-permute-start.11 = (bf16[512,512]{1,0:T(8,128)(2,1)S(1)}, bf16[512,512]{1,0:T(8,128)(2,1)S(1)}, u32[]{:S(2)}, u32[]{:S(2)}) collective-permute-start(bf16[512,512]{1,0:T(8,128)(2,1)S(1)} %project.8), channel_id=1, source_target_pairs={{0,2},{1,3},{2,0},{3,1},{4,6},{5,7},{6,4},{7,5},{8,10},{9,11},{10,... | collective-permute-start | bytes 1572872 | tf_op jit(solution)/shard_map/ppermute | solution.py:546
  45.0 1.8 %collective-permute-start.9 = (bf16[1536,128]{1,0:T(8,128)(2,1)S(1)}, bf16[1536,128]{1,0:T(8,128)(2,1)S(1)}, u32[]{:S(2)}, u32[]{:S(2)}) collective-permute-start(bf16[1536,128]{1,0:T(8,128)(2,1)S(1)} %copy-done.6), channel_id=1, source_target_pairs={{0,24},{8,16},{16,8},{24,0},{1,25},{9,17},{17,9},{25,1},{2,26},{10... | collective-permute-start | bytes 1179656 | tf_op jit(solution)/shard_map/ppermute | solution.py:546
  46.7 0.7 project.9
  47.5 0.5 collective-permute-start.17
  48.0 0.7 project.10
  48.7 0.7 project.11.refs_0_
  49.4 8.7 %collective-permute-done.11 = bf16[512,512]{1,0:T(8,128)(2,1)S(1)} collective-permute-done((bf16[512,512]{1,0:T(8,128)(2,1)S(1)}, bf16[512,512]{1,0:T(8,128)(2,1)S(1)}, u32[]{:S(2)}, u32[]{:S(2)}) %collective-permute-start.11) | collective-permute-done | bytes 524320 | tf_op jit(solution)/shard_map/ppermute | solution.py:546
  58.2 0.1 add_convert_fusion.1
  58.3 0.0 collective-permute-done.9.refs_12_
  58.3 2.7 %collective-permute-start.18 = (bf16[512,512]{1,0:T(8,128)(2,1)S(1)}, bf16[512,512]{1,0:T(8,128)(2,1)S(1)}, u32[]{:S(2)}, u32[]{:S(2)}) collective-permute-start(bf16[512,512]{1,0:T(8,128)(2,1)S(1)} %add_convert_fusion.1), channel_id=1, source_target_pairs={{0,4},{1,5},{2,6},{3,7},{4,0},{5,1},{6,2},{7,3},{8,12},{9,13},{10,... | collective-permute-start | bytes 1572872 | tf_op jit(solution)/shard_map/ppermute | solution.py:546
  61.0 6.8 %attend_high.1 = (bf16[512,128]{1,0:T(8,128)(2,1)S(1)}, bf16[512,128]{1,0:T(8,128)(2,1)S(1)}, bf16[512,128]{1,0:T(8,128)(2,1)S(1)}, bf16[512,128]{1,0:T(8,128)(2,1)S(1)}) custom-call(s32[1]{0:T(128)} %bitcast.ctx_ref, bf16[1024,512]{1,0:T(8,128)(2,1)S(1)} %copy-done.2, bf16[1024,512]{1,0:T(8,128)(2,1)S(1)} %copy-done.3, bf16[1024,512]{1,0:T(8,128)(2,1)S(1)} %copy-done.4, ...), custom_call_target="tpu_custom_call" | custom-call | flops 1024 | bytes 1024 | tf_op jit(solution)/shard_map/attend_high/pallas_call | solution.py:409
  67.8 1.4 %collective-permute-start.12 = (bf16[512,128]{1,0:T(8,128)(2,1)S(1)}, bf16[512,128]{1,0:T(8,128)(2,1)S(1)}, u32[]{:S(2)}, u32[]{:S(2)}) collective-permute-start(bf16[512,128]{1,0:T(8,128)(2,1)S(1)} %get-tuple-element.93), channel_id=1, source_target_pairs={{0,8},{8,0},{16,24},{24,16},{1,9},{9,1},{17,25},{25,17},{2,10},{10... | collective-permute-start | bytes 393224 | tf_op jit(solution)/shard_map/ppermute | solution.py:546
  69.2 1.0 collective-permute-start.13
  70.2 1.1 collective-permute-start.14
  71.3 2.4 %collective-permute-done.12.refs_1_ = bf16[512,128]{1,0:T(8,128)(2,1)S(1)} collective-permute-done((bf16[512,128]{1,0:T(8,128)(2,1)S(1)}, bf16[512,128]{1,0:T(8,128)(2,1)S(1)}, u32[]{:S(2)}, u32[]{:S(2)}) %collective-permute-start.12) | collective-permute-done | bytes 131104 | tf_op jit(solution)/shard_map/ppermute | solution.py:546
  73.7 0.7 collective-permute-done.13.refs_2_
  74.4 1.6 %collective-permute-done.14.refs_3_ = bf16[512,128]{1,0:T(8,128)(2,1)S(1)} collective-permute-done((bf16[512,128]{1,0:T(8,128)(2,1)S(1)}, bf16[512,128]{1,0:T(8,128)(2,1)S(1)}, u32[]{:S(2)}, u32[]{:S(2)}) %collective-permute-start.14) | collective-permute-done | bytes 131104 | tf_op jit(solution)/shard_map/ppermute | solution.py:546
  76.0 0.1 assemble.3
  76.1 0.1 collective-permute-start.15
  76.2 0.5 collective-permute-start.16
  76.7 1.0 collective-permute-done.15.refs_2_
  77.7 0.4 collective-permute-done.16.refs_3_
  78.1 0.7 project.15
  78.8 0.1 collective-permute-done.17.refs_1_
  78.9 4.0 %collective-permute-done.18.refs_2_ = bf16[512,512]{1,0:T(8,128)(2,1)S(1)} collective-permute-done((bf16[512,512]{1,0:T(8,128)(2,1)S(1)}, bf16[512,512]{1,0:T(8,128)(2,1)S(1)}, u32[]{:S(2)}, u32[]{:S(2)}) %collective-permute-start.18) | collective-permute-done | bytes 524320 | tf_op jit(solution)/shard_map/ppermute | solution.py:546
  82.9 0.8 collective-permute-start.19
  83.7 0.7 project.14
  84.4 9.7 %collective-permute-done.19 = bf16[512,512]{1,0:T(8,128)(2,1)S(1)} collective-permute-done((bf16[512,512]{1,0:T(8,128)(2,1)S(1)}, bf16[512,512]{1,0:T(8,128)(2,1)S(1)}, u32[]{:S(2)}, u32[]{:S(2)}) %collective-permute-start.19) | collective-permute-done | bytes 524320 | tf_op jit(solution)/shard_map/ppermute | solution.py:546
  94.1 0.1 add_convert_fusion
  94.3 2.9 %collective-permute-start.22 = (bf16[512,512]{1,0:T(8,128)(2,1)S(1)}, bf16[512,512]{1,0:T(8,128)(2,1)S(1)}, u32[]{:S(2)}, u32[]{:S(2)}) collective-permute-start(bf16[512,512]{1,0:T(8,128)(2,1)S(1)} %add_convert_fusion), channel_id=1, source_target_pairs={{0,4},{1,5},{2,6},{3,7},{4,0},{5,1},{6,2},{7,3},{8,12},{9,13},{10,... | collective-permute-start | bytes 1572872 | tf_op jit(solution)/shard_map/ppermute | solution.py:546
  97.2 0.7 project.13
  97.9 1.6 %collective-permute-start.20 = (bf16[256,512]{1,0:T(8,128)(2,1)S(1)}, bf16[256,512]{1,0:T(8,128)(2,1)S(1)}, u32[]{:S(2)}, u32[]{:S(2)}) collective-permute-start(bf16[256,512]{1,0:T(8,128)(2,1)S(1)} %get-tuple-element.102), channel_id=1, source_target_pairs={{0,2},{1,3},{2,0},{3,1},{4,6},{5,7},{6,4},{7,5},{8,10},{9,11},{10,... | collective-permute-start | bytes 786440 | tf_op jit(solution)/shard_map/ppermute | solution.py:546
  99.5 0.5 collective-permute-start.21
  100.0 0.7 project.12.refs_0_
  100.7 1.0 finish.2.refs_4_
  101.7 12.0 %collective-permute-done.20.refs_1_ = bf16[256,512]{1,0:T(8,128)(2,1)S(1)} collective-permute-done((bf16[256,512]{1,0:T(8,128)(2,1)S(1)}, bf16[256,512]{1,0:T(8,128)(2,1)S(1)}, u32[]{:S(2)}, u32[]{:S(2)}) %collective-permute-start.20) | collective-permute-done | bytes 262176 | tf_op jit(solution)/shard_map/ppermute | solution.py:546
  113.8 4.3 %collective-permute-done.21.refs_2_ = bf16[256,512]{1,0:T(8,128)(2,1)S(1)} collective-permute-done((bf16[256,512]{1,0:T(8,128)(2,1)S(1)}, bf16[256,512]{1,0:T(8,128)(2,1)S(1)}, u32[]{:S(2)}, u32[]{:S(2)}) %collective-permute-start.21) | collective-permute-done | bytes 262176 | tf_op jit(solution)/shard_map/ppermute | solution.py:546
  118.0 0.0 collective-permute-done.22.refs_3_
  118.0 1.0 finish.3
  (18 shorter events, 0.0 us)
Async XLA Ops:
  0.0 11.5 %collective-permute-start.3 = (bf16[512,4096]{1,0:T(8,128)(2,1)}, bf16[512,4096]{1,0:T(8,128)(2,1)}, u32[]{:S(2)}, u32[]{:S(2)}) collective-permute-start(bf16[512,4096]{1,0:T(8,128)(2,1)} %mine_in.1), channel_id=1, source_target_pairs={{0,1},{1,0},{2,3},{3,2},{4,5},{5,4},{6,7},{7,6},{8,9},{9,8},{10,11... | collective-permute-start | bytes 12582920 | tf_op jit(solution)/shard_map/ppermute | solution.py:546
  2.9 10.0 %copy-start.7 = (s32[4]{0:T(128)S(1)}, s32[4]{0:T(128)}, u32[]{:S(2)}) copy-start(s32[4]{0:T(128)} %constant.13) | copy-start | bytes 52
  2.9 16.3 %collective-permute-start = (bf16[1552,128]{1,0:T(8,128)(2,1)}, bf16[1552,128]{1,0:T(8,128)(2,1)S(1)}, u32[]{:S(2)}, u32[]{:S(2)}) collective-permute-start(bf16[1552,128]{1,0:T(8,128)(2,1)} %get-tuple-element.59), channel_id=1, source_target_pairs={{0,8},{8,0},{16,24},{24,16},{1,9},{9,1},{17,25},{25,17},{2,10},{10... | collective-permute-start | bytes 1191944 | tf_op jit(solution)/shard_map/ppermute | solution.py:546
  5.4 20.8 %collective-permute-start.1 = (bf16[1552,128]{1,0:T(8,128)(2,1)}, bf16[1552,128]{1,0:T(8,128)(2,1)S(1)}, u32[]{:S(2)}, u32[]{:S(2)}) collective-permute-start(bf16[1552,128]{1,0:T(8,128)(2,1)} %get-tuple-element.60), channel_id=1, source_target_pairs={{0,16},{8,24},{16,0},{24,8},{1,17},{9,25},{17,1},{25,9},{2,18},{10... | collective-permute-start | bytes 1191944 | tf_op jit(solution)/shard_map/ppermute | solution.py:546
  7.0 19.2 %collective-permute-start.2 = (bf16[1552,128]{1,0:T(8,128)(2,1)}, bf16[1552,128]{1,0:T(8,128)(2,1)S(1)}, u32[]{:S(2)}, u32[]{:S(2)}) collective-permute-start(bf16[1552,128]{1,0:T(8,128)(2,1)} %get-tuple-element.61), channel_id=1, source_target_pairs={{0,24},{8,16},{16,8},{24,0},{1,25},{9,17},{17,9},{25,1},{2,26},{10... | collective-permute-start | bytes 1191944 | tf_op jit(solution)/shard_map/ppermute | solution.py:546
  9.5 26.3 %collective-permute-start.7 = (bf16[1536,128]{1,0:T(8,128)(2,1)}, bf16[1536,128]{1,0:T(8,128)(2,1)S(1)}, u32[]{:S(2)}, u32[]{:S(2)}) collective-permute-start(bf16[1536,128]{1,0:T(8,128)(2,1)} %get-tuple-element.78), channel_id=1, source_target_pairs={{0,8},{8,0},{16,24},{24,16},{1,9},{9,1},{17,25},{25,17},{2,10},{10... | collective-permute-start | bytes 1179656 | tf_op jit(solution)/shard_map/ppermute | solution.py:546
  11.5 24.3 %collective-permute-start.8 = (bf16[1536,128]{1,0:T(8,128)(2,1)}, bf16[1536,128]{1,0:T(8,128)(2,1)S(1)}, u32[]{:S(2)}, u32[]{:S(2)}) collective-permute-start(bf16[1536,128]{1,0:T(8,128)(2,1)} %get-tuple-element.79), channel_id=1, source_target_pairs={{0,16},{8,24},{16,0},{24,8},{1,17},{9,25},{17,1},{25,9},{2,18},{10... | collective-permute-start | bytes 1179656 | tf_op jit(solution)/shard_map/ppermute | solution.py:546
  13.5 12.7 %copy-start.2 = (bf16[1024,512]{1,0:T(8,128)(2,1)S(1)}, bf16[1024,512]{1,0:T(8,128)(2,1)}, u32[]{:S(2)}) copy-start(bf16[1024,512]{1,0:T(8,128)(2,1)} %refs_3_.4) | copy-start | bytes 3145732
  13.5 12.7 %copy-start.3 = (bf16[1024,512]{1,0:T(8,128)(2,1)S(1)}, bf16[1024,512]{1,0:T(8,128)(2,1)}, u32[]{:S(2)}) copy-start(bf16[1024,512]{1,0:T(8,128)(2,1)} %refs_4_.4) | copy-start | bytes 3145732
  13.5 12.7 %copy-start.4 = (bf16[1024,512]{1,0:T(8,128)(2,1)S(1)}, bf16[1024,512]{1,0:T(8,128)(2,1)}, u32[]{:S(2)}) copy-start(bf16[1024,512]{1,0:T(8,128)(2,1)} %refs_5_.4) | copy-start | bytes 3145732
  13.5 12.7 %copy-start.5 = (s32[1024]{0:T(1024)S(1)}, s32[1024]{0:T(1024)}, u32[]{:S(2)}) copy-start(s32[1024]{0:T(1024)} %param.9) | copy-start | bytes 12292
  19.2 23.4 %copy-start = (bf16[512,2048]{1,0:T(8,128)(2,1)S(1)}, bf16[512,2048]{1,0:T(8,128)(2,1)}, u32[]{:S(2)}) copy-start(bf16[512,2048]{1,0:T(8,128)(2,1)} %get-tuple-element.87.refs_2_.refs_4_) | copy-start | bytes 6291460
  19.2 23.4 %copy-start.1 = (bf16[512,2048]{1,0:T(8,128)(2,1)S(1)}, bf16[512,2048]{1,0:T(8,128)(2,1)}, u32[]{:S(2)}) copy-start(bf16[512,2048]{1,0:T(8,128)(2,1)} %get-tuple-element.88.refs_3_.refs_5_) | copy-start | bytes 6291460
  32.2 12.7 %copy-start.6 = (bf16[1536,128]{1,0:T(8,128)(2,1)S(1)}, bf16[1536,128]{1,0:T(8,128)(2,1)}, u32[]{:S(2)}) copy-start(bf16[1536,128]{1,0:T(8,128)(2,1)} %get-tuple-element.82) | copy-start | bytes 1179652
  32.2 6.2 %collective-permute-start.4 = (bf16[512,128]{1,0:T(8,128)(2,1)S(1)}, bf16[512,128]{1,0:T(8,128)(2,1)S(1)}, u32[]{:S(2)}, u32[]{:S(2)}) collective-permute-start(bf16[512,128]{1,0:T(8,128)(2,1)S(1)} %get-tuple-element.75), channel_id=1, source_target_pairs={{0,8},{8,0},{16,24},{24,16},{1,9},{9,1},{17,25},{25,17},{2,10},{10... | collective-permute-start | bytes 393224 | tf_op jit(solution)/shard_map/ppermute | solution.py:546
  33.3 7.3 %collective-permute-start.5 = (bf16[512,128]{1,0:T(8,128)(2,1)S(1)}, bf16[512,128]{1,0:T(8,128)(2,1)S(1)}, u32[]{:S(2)}, u32[]{:S(2)}) collective-permute-start(bf16[512,128]{1,0:T(8,128)(2,1)S(1)} %get-tuple-element.76), channel_id=1, source_target_pairs={{0,16},{8,24},{16,0},{24,8},{1,17},{9,25},{17,1},{25,9},{2,18},{10... | collective-permute-start | bytes 393224 | tf_op jit(solution)/shard_map/ppermute | solution.py:546
  34.4 6.2 %collective-permute-start.6 = (bf16[512,128]{1,0:T(8,128)(2,1)S(1)}, bf16[512,128]{1,0:T(8,128)(2,1)S(1)}, u32[]{:S(2)}, u32[]{:S(2)}) collective-permute-start(bf16[512,128]{1,0:T(8,128)(2,1)S(1)} %get-tuple-element.77), channel_id=1, source_target_pairs={{0,24},{8,16},{16,8},{24,0},{1,25},{9,17},{17,9},{25,1},{2,26},{10... | collective-permute-start | bytes 393224 | tf_op jit(solution)/shard_map/ppermute | solution.py:546
  40.6 2.0 %collective-permute-start.10 = (bf16[512,512]{1,0:T(8,128)(2,1)S(1)}, bf16[512,512]{1,0:T(8,128)(2,1)S(1)}, u32[]{:S(2)}, u32[]{:S(2)}) collective-permute-start(bf16[512,512]{1,0:T(8,128)(2,1)S(1)} %assemble.2.refs_0_), channel_id=1, source_target_pairs={{0,1},{1,0},{2,3},{3,2},{4,5},{5,4},{6,7},{7,6},{8,9},{9,8},{10,11... | collective-permute-start | bytes 1572872 | tf_op jit(solution)/shard_map/ppermute | solution.py:546
  43.3 14.8 %collective-permute-start.11 = (bf16[512,512]{1,0:T(8,128)(2,1)S(1)}, bf16[512,512]{1,0:T(8,128)(2,1)S(1)}, u32[]{:S(2)}, u32[]{:S(2)}) collective-permute-start(bf16[512,512]{1,0:T(8,128)(2,1)S(1)} %project.8), channel_id=1, source_target_pairs={{0,2},{1,3},{2,0},{3,1},{4,6},{5,7},{6,4},{7,5},{8,10},{9,11},{10,... | collective-permute-start | bytes 1572872 | tf_op jit(solution)/shard_map/ppermute | solution.py:546
  45.0 13.3 %collective-permute-start.9 = (bf16[1536,128]{1,0:T(8,128)(2,1)S(1)}, bf16[1536,128]{1,0:T(8,128)(2,1)S(1)}, u32[]{:S(2)}, u32[]{:S(2)}) collective-permute-start(bf16[1536,128]{1,0:T(8,128)(2,1)S(1)} %copy-done.6), channel_id=1, source_target_pairs={{0,24},{8,16},{16,8},{24,0},{1,25},{9,17},{17,9},{25,1},{2,26},{10... | collective-permute-start | bytes 1179656 | tf_op jit(solution)/shard_map/ppermute | solution.py:546
  47.5 31.4 %collective-permute-start.17 = (bf16[512,512]{1,0:T(8,128)(2,1)S(1)}, bf16[512,512]{1,0:T(8,128)(2,1)S(1)}, u32[]{:S(2)}, u32[]{:S(2)}) collective-permute-start(bf16[512,512]{1,0:T(8,128)(2,1)S(1)} %project.9), channel_id=1, source_target_pairs={{0,2},{1,3},{2,0},{3,1},{4,6},{5,7},{6,4},{7,5},{8,10},{9,11},{10,... | collective-permute-start | bytes 1572872 | tf_op jit(solution)/shard_map/ppermute | solution.py:546
  58.3 24.6 %collective-permute-start.18 = (bf16[512,512]{1,0:T(8,128)(2,1)S(1)}, bf16[512,512]{1,0:T(8,128)(2,1)S(1)}, u32[]{:S(2)}, u32[]{:S(2)}) collective-permute-start(bf16[512,512]{1,0:T(8,128)(2,1)S(1)} %add_convert_fusion.1), channel_id=1, source_target_pairs={{0,4},{1,5},{2,6},{3,7},{4,0},{5,1},{6,2},{7,3},{8,12},{9,13},{10,... | collective-permute-start | bytes 1572872 | tf_op jit(solution)/shard_map/ppermute | solution.py:546
  67.8 6.0 %collective-permute-start.12 = (bf16[512,128]{1,0:T(8,128)(2,1)S(1)}, bf16[512,128]{1,0:T(8,128)(2,1)S(1)}, u32[]{:S(2)}, u32[]{:S(2)}) collective-permute-start(bf16[512,128]{1,0:T(8,128)(2,1)S(1)} %get-tuple-element.93), channel_id=1, source_target_pairs={{0,8},{8,0},{16,24},{24,16},{1,9},{9,1},{17,25},{25,17},{2,10},{10... | collective-permute-start | bytes 393224 | tf_op jit(solution)/shard_map/ppermute | solution.py:546
  69.2 5.2 %collective-permute-start.13 = (bf16[512,128]{1,0:T(8,128)(2,1)S(1)}, bf16[512,128]{1,0:T(8,128)(2,1)S(1)}, u32[]{:S(2)}, u32[]{:S(2)}) collective-permute-start(bf16[512,128]{1,0:T(8,128)(2,1)S(1)} %get-tuple-element.94), channel_id=1, source_target_pairs={{0,16},{8,24},{16,0},{24,8},{1,17},{9,25},{17,1},{25,9},{2,18},{10... | collective-permute-start | bytes 393224 | tf_op jit(solution)/shard_map/ppermute | solution.py:546
  70.2 5.9 %collective-permute-start.14 = (bf16[512,128]{1,0:T(8,128)(2,1)S(1)}, bf16[512,128]{1,0:T(8,128)(2,1)S(1)}, u32[]{:S(2)}, u32[]{:S(2)}) collective-permute-start(bf16[512,128]{1,0:T(8,128)(2,1)S(1)} %get-tuple-element.95), channel_id=1, source_target_pairs={{0,24},{8,16},{16,8},{24,0},{1,25},{9,17},{17,9},{25,1},{2,26},{10... | collective-permute-start | bytes 393224 | tf_op jit(solution)/shard_map/ppermute | solution.py:546
  76.1 1.6 %collective-permute-start.15 = (bf16[256,512]{1,0:T(8,128)(2,1)S(1)}, bf16[256,512]{1,0:T(8,128)(2,1)S(1)}, u32[]{:S(2)}, u32[]{:S(2)}) collective-permute-start(bf16[256,512]{1,0:T(8,128)(2,1)S(1)} %get-tuple-element.96.refs_0_), channel_id=1, source_target_pairs={{0,1},{1,0},{2,3},{3,2},{4,5},{5,4},{6,7},{7,6},{8,9},{9,8},{10,11... | collective-permute-start | bytes 786440 | tf_op jit(solution)/shard_map/ppermute | solution.py:546
  76.2 1.9 %collective-permute-start.16 = (bf16[256,512]{1,0:T(8,128)(2,1)S(1)}, bf16[256,512]{1,0:T(8,128)(2,1)S(1)}, u32[]{:S(2)}, u32[]{:S(2)}) collective-permute-start(bf16[256,512]{1,0:T(8,128)(2,1)S(1)} %get-tuple-element.97.refs_1_), channel_id=1, source_target_pairs={{0,1},{1,0},{2,3},{3,2},{4,5},{5,4},{6,7},{7,6},{8,9},{9,8},{10,11... | collective-permute-start | bytes 786440 | tf_op jit(solution)/shard_map/ppermute | solution.py:546
  82.9 11.2 %collective-permute-start.19 = (bf16[512,512]{1,0:T(8,128)(2,1)S(1)}, bf16[512,512]{1,0:T(8,128)(2,1)S(1)}, u32[]{:S(2)}, u32[]{:S(2)}) collective-permute-start(bf16[512,512]{1,0:T(8,128)(2,1)S(1)} %project.15), channel_id=1, source_target_pairs={{0,2},{1,3},{2,0},{3,1},{4,6},{5,7},{6,4},{7,5},{8,10},{9,11},{10,... | collective-permute-start | bytes 1572872 | tf_op jit(solution)/shard_map/ppermute | solution.py:546
  94.3 23.8 %collective-permute-start.22 = (bf16[512,512]{1,0:T(8,128)(2,1)S(1)}, bf16[512,512]{1,0:T(8,128)(2,1)S(1)}, u32[]{:S(2)}, u32[]{:S(2)}) collective-permute-start(bf16[512,512]{1,0:T(8,128)(2,1)S(1)} %add_convert_fusion), channel_id=1, source_target_pairs={{0,4},{1,5},{2,6},{3,7},{4,0},{5,1},{6,2},{7,3},{8,12},{9,13},{10,... | collective-permute-start | bytes 1572872 | tf_op jit(solution)/shard_map/ppermute | solution.py:546
  97.9 15.9 %collective-permute-start.20 = (bf16[256,512]{1,0:T(8,128)(2,1)S(1)}, bf16[256,512]{1,0:T(8,128)(2,1)S(1)}, u32[]{:S(2)}, u32[]{:S(2)}) collective-permute-start(bf16[256,512]{1,0:T(8,128)(2,1)S(1)} %get-tuple-element.102), channel_id=1, source_target_pairs={{0,2},{1,3},{2,0},{3,1},{4,6},{5,7},{6,4},{7,5},{8,10},{9,11},{10,... | collective-permute-start | bytes 786440 | tf_op jit(solution)/shard_map/ppermute | solution.py:546
  99.5 18.5 %collective-permute-start.21 = (bf16[256,512]{1,0:T(8,128)(2,1)S(1)}, bf16[256,512]{1,0:T(8,128)(2,1)S(1)}, u32[]{:S(2)}, u32[]{:S(2)}) collective-permute-start(bf16[256,512]{1,0:T(8,128)(2,1)S(1)} %get-tuple-element.103), channel_id=1, source_target_pairs={{0,2},{1,3},{2,0},{3,1},{4,6},{5,7},{6,4},{7,5},{8,10},{9,11},{10,... | collective-permute-start | bytes 786440 | tf_op jit(solution)/shard_map/ppermute | solution.py:546

commit v19 on v18

--- a/solution.py
+++ b/solution.py
@@ -582,7 +582,9 @@
         return [swap(pieces[distance], "ctx", distance) for distance in near]
 
     rows = shard_rows // 2
-    cuts = (0, rows // 2, rows)
+    cut = rows * 23 // 32 // 16 * 16
+    third = rows * 11 // 32 // 16 * 16
+    middle = rows // 2
 
     def projected(mine, sibling, *wanted):
         return list(project(wanted, mine, sibling, *w_packed))
@@ -597,24 +599,30 @@
     high = [*high, swap(diagonal_out, "ctx", near[-1])]
     mine = assemble(ctx_index, [pieces[0], *back], (0, rows))
     sibling = [swap(part, "head", 1) for part in mine]
-    shares = [projected(mine, sibling, [(turn, 0, rows)])[0] for turn in range(len(TURNS))]
-    far = to_next(shares[0], 1)
-    near_sum = to_next(shares[1], 1)
-    passed = add(shares[2], far)
-
-    high, shares, passed = tie(high, shares, passed)
+    (share,) = projected(mine, sibling, [(0, 0, cut)])
+    far = to_next(share, 1)
+    (behind,) = projected(mine, sibling, [(0, cut, rows), (1, 0, rows)])
+    shares = projected(mine, sibling, [(2, 0, cut)], [(2, cut, rows)])
+    (kept,) = projected(mine, sibling, [(3, 0, rows)])
+
+    passed = add(shares[0], far)
+    high, passed, _, shares[1], kept = tie(high, passed, behind, shares[1], kept)
+    behind = to_next(behind, 1)
     across = to_next(passed, 2)
     pieces = attend(ctx_index, queries, keys, values, docs, low, high)
     back = send_back(pieces)
-    mine = assemble(ctx_index, [pieces[0], *back], cuts)
+    mine = assemble(ctx_index, [pieces[0], *back], (0, third, 2 * third, rows))
     sibling = [swap(part, "head", 1) for part in mine]
     late = [projected(mine, sibling, [(turn, 0, rows)])[0] for turn in (0, 2, 3)]
-    late[0], near_sum, across = tie(late[0], near_sum, across)
-    result = finish(0, rows, [[(shares[3], 0)], [(near_sum, 0)], [(across, 0)]], None)
+    late[0], behind, across = tie(late[0], behind, across)
     far = to_next(late[0], 1)
+    across = [across, to_next(add(shares[1], behind[: rows - cut]), 2)]
     passed = add(late[1], far)
+    passed, across[1] = tie(passed, across[1])
+    terms = [[(kept, 0)], [(behind, rows - cut)], [(part, 0) for part in across]]
+    result = finish(0, rows, terms, None)
     across = to_next(passed, 2)
-    last = projected(mine, sibling, *[[(1, *span)] for span in zip(cuts[:-1], cuts[1:])])
+    last = projected(mine, sibling, [(1, 0, middle)], [(1, middle, rows)])
     last, passed = tie(last, passed)
     near_sum = [to_next(part, 1) for part in last]
     terms = [[(late[2], 0)], [(part, 0) for part in near_sum], [(across, 0)]]

time: 119 us -> 123 us (1.034)
  waiting for transfers between devices: 58.6 us -> 60.5 us
    ppermute x23 -> x25, waiting for transfers between devices: 58.6 us -> 60.5 us  [swap(): lax.ppermute(value, axis, [(source, source ^ distance) for source in rang...]
    ppermute x23 -> x25, starting transfers between devices: 28.1 us -> 28.4 us  [swap(): lax.ppermute(value, axis, [(source, source ^ distance) for source in rang...]
  transfers between devices with their start and end apart: 23 -> 25, of which waited for: 15 -> 12; matrix products, arithmetic and copies ran while one was open for 1% -> 1% of each run, Pallas kernels for 25% -> 25%
where the time goes in v19:
time: 123 us; the launch traced here: 122 us
  waiting for transfers between devices  60.5 us (49%)
  Pallas kernels  32.1 us (26%)
  starting transfers between devices  28.4 us (23%)
    ppermute x25, waiting for transfers between devices, swap(): lax.ppermute(value, axis, [(source, source ^ distance) for source in rang...  60.5 us
    ppermute x25, starting transfers between devices, swap(): lax.ppermute(value, axis, [(source, source ^ distance) for source in rang...  28.4 us
    pallas_call x2, Pallas kernels, attend(): pl.pallas_call(kernel, grid_spec=pltpu.PrefetchScalarGridSpec(num_scalar_...  13.4 us
    pallas_call x1, Pallas kernels, pack_projection(): pl.pallas_call(kernel, grid_spec=pltpu.PrefetchScalarGridSpec(num_scalar_...  5.73 us
    pallas_call x8, Pallas kernels, project(): pl.pallas_call(kernel, grid=(1,), in_specs=[plain(part.shape) for part in...  5.72 us
    pallas_call x2, Pallas kernels, pack(): pl.pallas_call(kernel, grid_spec=pltpu.PrefetchScalarGridSpec(num_scalar_...  5.05 us
  transfers between devices with their start and end apart: 25, of which 12 were waited for; matrix products, arithmetic and copies ran while one was open for 1% of the time, Pallas kernels for 25%

profile of v19, /device:TPU:0, one launch (start us, length us, event | category | flops | bytes accessed | tf_op | source)
XLA Modules:
  0.0 121.9 jit_solution(12422634589324492706)
XLA Ops:
  0.0 0.5 collective-permute-start.3
  0.5 2.5 %pack.2 = (bf16[1552,128]{1,0:T(8,128)(2,1)}, bf16[1552,128]{1,0:T(8,128)(2,1)}, bf16[1552,128]{1,0:T(8,128)(2,1)}) custom-call(s32[1]{0:T(128)} %bitcast.ctx_ref, bf16[1024,512]{1,0:T(8,128)(2,1)} %refs_3_.4, bf16[1024,512]{1,0:T(8,128)(2,1)} %refs_4_.4, bf16[1024,512]{1,0:T(8,128)(2,1)} %refs_5_.4, bf16[1024,512]{1,0:T(8,128)(2,1)} %refs_3_.4, ...), custom_call_target="tpu_custom_call" | custom-call | flops 1024 | bytes 1024 | tf_op jit(solution)/shard_map/pack/pallas_call | solution.py:201
  2.9 2.5 %collective-permute-start = (bf16[1552,128]{1,0:T(8,128)(2,1)}, bf16[1552,128]{1,0:T(8,128)(2,1)S(1)}, u32[]{:S(2)}, u32[]{:S(2)}) collective-permute-start(bf16[1552,128]{1,0:T(8,128)(2,1)} %get-tuple-element.65), channel_id=1, source_target_pairs={{0,8},{8,0},{16,24},{24,16},{1,9},{9,1},{17,25},{25,17},{2,10},{10... | collective-permute-start | bytes 1191944 | tf_op jit(solution)/shard_map/ppermute | solution.py:546
  5.4 1.5 %collective-permute-start.1 = (bf16[1552,128]{1,0:T(8,128)(2,1)}, bf16[1552,128]{1,0:T(8,128)(2,1)S(1)}, u32[]{:S(2)}, u32[]{:S(2)}) collective-permute-start(bf16[1552,128]{1,0:T(8,128)(2,1)} %get-tuple-element.66), channel_id=1, source_target_pairs={{0,16},{8,24},{16,0},{24,8},{1,17},{9,25},{17,1},{25,9},{2,18},{10... | collective-permute-start | bytes 1191944 | tf_op jit(solution)/shard_map/ppermute | solution.py:546
  7.0 0.0 collective-permute-start.2
  7.0 2.6 %pack.3 = (bf16[1536,128]{1,0:T(8,128)(2,1)}, bf16[1536,128]{1,0:T(8,128)(2,1)}, bf16[1536,128]{1,0:T(8,128)(2,1)}) custom-call(s32[1]{0:T(128)} %bitcast.ctx_ref, bf16[1024,512]{1,0:T(8,128)(2,1)} %refs_3_.4, bf16[1024,512]{1,0:T(8,128)(2,1)} %refs_4_.4, bf16[1024,512]{1,0:T(8,128)(2,1)} %refs_5_.4, bf16[1024,512]{1,0:T(8,128)(2,1)} %refs_3_.4, ...), custom_call_target="tpu_custom_call" | custom-call | flops 1024 | bytes 1024 | tf_op jit(solution)/shard_map/pack/pallas_call | solution.py:201
  9.5 2.0 %collective-permute-start.7 = (bf16[1536,128]{1,0:T(8,128)(2,1)}, bf16[1536,128]{1,0:T(8,128)(2,1)S(1)}, u32[]{:S(2)}, u32[]{:S(2)}) collective-permute-start(bf16[1536,128]{1,0:T(8,128)(2,1)} %get-tuple-element.84), channel_id=1, source_target_pairs={{0,8},{8,0},{16,24},{24,16},{1,9},{9,1},{17,25},{25,17},{2,10},{10... | collective-permute-start | bytes 1179656 | tf_op jit(solution)/shard_map/ppermute | solution.py:546
  11.5 1.5 %collective-permute-start.8 = (bf16[1536,128]{1,0:T(8,128)(2,1)}, bf16[1536,128]{1,0:T(8,128)(2,1)S(1)}, u32[]{:S(2)}, u32[]{:S(2)}) collective-permute-start(bf16[1536,128]{1,0:T(8,128)(2,1)} %get-tuple-element.85), channel_id=1, source_target_pairs={{0,16},{8,24},{16,0},{24,8},{1,17},{9,25},{17,1},{25,9},{2,18},{10... | collective-permute-start | bytes 1179656 | tf_op jit(solution)/shard_map/ppermute | solution.py:546
  13.0 0.5 broadcast_xor_fusion.places_ref
  13.6 5.7 %pack_projection.1 = (bf16[512,2048]{1,0:T(8,128)(2,1)}, bf16[512,2048]{1,0:T(8,128)(2,1)}) custom-call(s32[4]{0:T(128)} %broadcast_xor_fusion.places_ref, bf16[512,4096]{1,0:T(8,128)(2,1)} %mine_in.1, bf16[512,4096]{1,0:T(8,128)(2,1)} %collective-permute-done.3.sibling_in), custom_call_target="tpu_custom_call" | custom-call | flops 1024 | bytes 1024 | tf_op jit(solution)/shard_map/pack_projection/pallas_call | solution.py:227
  19.3 0.0 collective-permute-done.refs_4_.refs_7_
  19.3 6.9 %collective-permute-done.1.refs_5_.refs_8_ = bf16[1552,128]{1,0:T(8,128)(2,1)S(1)} collective-permute-done((bf16[1552,128]{1,0:T(8,128)(2,1)}, bf16[1552,128]{1,0:T(8,128)(2,1)S(1)}, u32[]{:S(2)}, u32[]{:S(2)}) %collective-permute-start.1) | collective-permute-done | bytes 397344 | tf_op jit(solution)/shard_map/ppermute | solution.py:546
  26.2 6.0 %attend_low.1 = (bf16[512,128]{1,0:T(8,128)(2,1)S(1)}, bf16[512,128]{1,0:T(8,128)(2,1)S(1)}, bf16[512,128]{1,0:T(8,128)(2,1)S(1)}, bf16[512,128]{1,0:T(8,128)(2,1)S(1)}) custom-call(s32[1]{0:T(128)} %bitcast.ctx_ref, bf16[1024,512]{1,0:T(8,128)(2,1)S(1)} %copy-done.2, bf16[1024,512]{1,0:T(8,128)(2,1)S(1)} %copy-done.3, bf16[1024,512]{1,0:T(8,128)(2,1)S(1)} %copy-done.4, ...), custom_call_target="tpu_custom_call" | custom-call | flops 1024 | bytes 1024 | tf_op jit(solution)/shard_map/attend_low/pallas_call | solution.py:409
  32.2 1.0 collective-permute-start.4
  33.3 1.1 collective-permute-start.5
  34.4 1.4 %collective-permute-start.6 = (bf16[512,128]{1,0:T(8,128)(2,1)S(1)}, bf16[512,128]{1,0:T(8,128)(2,1)S(1)}, u32[]{:S(2)}, u32[]{:S(2)}) collective-permute-start(bf16[512,128]{1,0:T(8,128)(2,1)S(1)} %get-tuple-element.83), channel_id=1, source_target_pairs={{0,24},{8,16},{16,8},{24,0},{1,25},{9,17},{17,9},{25,1},{2,26},{10... | collective-permute-start | bytes 393224 | tf_op jit(solution)/shard_map/ppermute | solution.py:546
  35.8 0.0 collective-permute-done.8.refs_11_
  35.8 2.6 %collective-permute-done.4.refs_1_ = bf16[512,128]{1,0:T(8,128)(2,1)S(1)} collective-permute-done((bf16[512,128]{1,0:T(8,128)(2,1)S(1)}, bf16[512,128]{1,0:T(8,128)(2,1)S(1)}, u32[]{:S(2)}, u32[]{:S(2)}) %collective-permute-start.4) | collective-permute-done | bytes 131104 | tf_op jit(solution)/shard_map/ppermute | solution.py:546
  38.4 2.1 %collective-permute-done.5.refs_2_ = bf16[512,128]{1,0:T(8,128)(2,1)S(1)} collective-permute-done((bf16[512,128]{1,0:T(8,128)(2,1)S(1)}, bf16[512,128]{1,0:T(8,128)(2,1)S(1)}, u32[]{:S(2)}, u32[]{:S(2)}) %collective-permute-start.5) | collective-permute-done | bytes 131104 | tf_op jit(solution)/shard_map/ppermute | solution.py:546
  40.5 0.0 collective-permute-done.6.refs_3_
  40.5 0.1 assemble.2.refs_0_
  40.6 0.1 collective-permute-start.10
  40.7 1.9 %collective-permute-done.10.refs_1_ = bf16[512,512]{1,0:T(8,128)(2,1)S(1)} collective-permute-done((bf16[512,512]{1,0:T(8,128)(2,1)S(1)}, bf16[512,512]{1,0:T(8,128)(2,1)S(1)}, u32[]{:S(2)}, u32[]{:S(2)}) %collective-permute-start.10) | collective-permute-done | bytes 524320 | tf_op jit(solution)/shard_map/ppermute | solution.py:546
  42.6 0.6 project.9
  43.2 1.6 %collective-permute-start.11 = (bf16[368,512]{1,0:T(8,128)(2,1)S(1)}, bf16[368,512]{1,0:T(8,128)(2,1)S(1)}, u32[]{:S(2)}, u32[]{:S(2)}) collective-permute-start(bf16[368,512]{1,0:T(8,128)(2,1)S(1)} %project.9), channel_id=1, source_target_pairs={{0,2},{1,3},{2,0},{3,1},{4,6},{5,7},{6,4},{7,5},{8,10},{9,11},{10,... | collective-permute-start | bytes 1130504 | tf_op jit(solution)/shard_map/ppermute | solution.py:546
  44.8 1.8 %collective-permute-start.9 = (bf16[1536,128]{1,0:T(8,128)(2,1)S(1)}, bf16[1536,128]{1,0:T(8,128)(2,1)S(1)}, u32[]{:S(2)}, u32[]{:S(2)}) collective-permute-start(bf16[1536,128]{1,0:T(8,128)(2,1)S(1)} %copy-done.6), channel_id=1, source_target_pairs={{0,24},{8,16},{16,8},{24,0},{1,25},{9,17},{17,9},{25,1},{2,26},{10... | collective-permute-start | bytes 1179656 | tf_op jit(solution)/shard_map/ppermute | solution.py:546
  46.6 0.9 project.10
  47.5 0.5 collective-permute-start.18
  48.0 0.7 project.8
  48.7 0.7 project.11.refs_0_
  49.4 5.4 %collective-permute-done.11 = bf16[368,512]{1,0:T(8,128)(2,1)S(1)} collective-permute-done((bf16[368,512]{1,0:T(8,128)(2,1)S(1)}, bf16[368,512]{1,0:T(8,128)(2,1)S(1)}, u32[]{:S(2)}, u32[]{:S(2)}) %collective-permute-start.11) | collective-permute-done | bytes 376864 | tf_op jit(solution)/shard_map/ppermute | solution.py:546
  54.9 0.1 add_convert_fusion.1
  55.0 1.6 %collective-permute-done.9.refs_12_ = bf16[1536,128]{1,0:T(8,128)(2,1)S(1)} collective-permute-done((bf16[1536,128]{1,0:T(8,128)(2,1)S(1)}, bf16[1536,128]{1,0:T(8,128)(2,1)S(1)}, u32[]{:S(2)}, u32[]{:S(2)}) %collective-permute-start.9) | collective-permute-done | bytes 393248 | tf_op jit(solution)/shard_map/ppermute | solution.py:546
  56.6 2.6 %collective-permute-start.19 = (bf16[368,512]{1,0:T(8,128)(2,1)S(1)}, bf16[368,512]{1,0:T(8,128)(2,1)S(1)}, u32[]{:S(2)}, u32[]{:S(2)}) collective-permute-start(bf16[368,512]{1,0:T(8,128)(2,1)S(1)} %add_convert_fusion.1), channel_id=1, source_target_pairs={{0,4},{1,5},{2,6},{3,7},{4,0},{5,1},{6,2},{7,3},{8,12},{9,13},{10,... | collective-permute-start | bytes 1130504 | tf_op jit(solution)/shard_map/ppermute | solution.py:546
  59.2 7.4 %attend_high.1 = (bf16[512,128]{1,0:T(8,128)(2,1)S(1)}, bf16[512,128]{1,0:T(8,128)(2,1)S(1)}, bf16[512,128]{1,0:T(8,128)(2,1)S(1)}, bf16[512,128]{1,0:T(8,128)(2,1)S(1)}) custom-call(s32[1]{0:T(128)} %bitcast.ctx_ref, bf16[1024,512]{1,0:T(8,128)(2,1)S(1)} %copy-done.2, bf16[1024,512]{1,0:T(8,128)(2,1)S(1)} %copy-done.3, bf16[1024,512]{1,0:T(8,128)(2,1)S(1)} %copy-done.4, ...), custom_call_target="tpu_custom_call" | custom-call | flops 1024 | bytes 1024 | tf_op jit(solution)/shard_map/attend_high/pallas_call | solution.py:409
  66.6 1.4 %collective-permute-start.12 = (bf16[512,128]{1,0:T(8,128)(2,1)S(1)}, bf16[512,128]{1,0:T(8,128)(2,1)S(1)}, u32[]{:S(2)}, u32[]{:S(2)}) collective-permute-start(bf16[512,128]{1,0:T(8,128)(2,1)S(1)} %get-tuple-element.101), channel_id=1, source_target_pairs={{0,8},{8,0},{16,24},{24,16},{1,9},{9,1},{17,25},{25,17},{2,10},{10... | collective-permute-start | bytes 393224 | tf_op jit(solution)/shard_map/ppermute | solution.py:546
  68.1 1.0 collective-permute-start.13
  69.0 1.2 collective-permute-start.14
  70.2 2.9 %collective-permute-done.12.refs_1_ = bf16[512,128]{1,0:T(8,128)(2,1)S(1)} collective-permute-done((bf16[512,128]{1,0:T(8,128)(2,1)S(1)}, bf16[512,128]{1,0:T(8,128)(2,1)S(1)}, u32[]{:S(2)}, u32[]{:S(2)}) %collective-permute-start.12) | collective-permute-done | bytes 131104 | tf_op jit(solution)/shard_map/ppermute | solution.py:546
  73.0 2.1 %collective-permute-done.13.refs_2_ = bf16[512,128]{1,0:T(8,128)(2,1)S(1)} collective-permute-done((bf16[512,128]{1,0:T(8,128)(2,1)S(1)}, bf16[512,128]{1,0:T(8,128)(2,1)S(1)}, u32[]{:S(2)}, u32[]{:S(2)}) %collective-permute-start.13) | collective-permute-done | bytes 131104 | tf_op jit(solution)/shard_map/ppermute | solution.py:546
  75.2 0.0 collective-permute-done.14.refs_3_
  75.2 0.1 assemble.3
  75.3 0.1 collective-permute-start.15
  75.3 0.5 collective-permute-start.16
  75.8 0.1 collective-permute-start.17
  75.9 1.3 %collective-permute-done.17.refs_5_ = bf16[160,512]{1,0:T(8,128)(2,1)S(1)} collective-permute-done((bf16[160,512]{1,0:T(8,128)(2,1)S(1)}, bf16[160,512]{1,0:T(8,128)(2,1)S(1)}, u32[]{:S(2)}, u32[]{:S(2)}) %collective-permute-start.17) | collective-permute-done | bytes 163872 | tf_op jit(solution)/shard_map/ppermute | solution.py:546
  77.2 0.0 collective-permute-done.15.refs_3_
  77.2 0.7 project.15
  78.0 0.0 collective-permute-done.18.refs_1_
  78.0 0.0 collective-permute-done.19.refs_2_
  78.0 1.1 collective-permute-start.20
  79.1 0.7 project.14
  79.9 1.6 %collective-permute-start.21 = (bf16[144,512]{1,0:T(8,128)(2,1)S(1)}, bf16[144,512]{1,0:T(8,128)(2,1)S(1)}, u32[]{:S(2)}, u32[]{:S(2)}) collective-permute-start(bf16[144,512]{1,0:T(8,128)(2,1)S(1)} %add_convert_fusion.2), channel_id=1, source_target_pairs={{0,4},{1,5},{2,6},{3,7},{4,0},{5,1},{6,2},{7,3},{8,12},{9,13},{10,... | collective-permute-start | bytes 442376 | tf_op jit(solution)/shard_map/ppermute | solution.py:546
  81.5 13.8 %collective-permute-done.20 = bf16[512,512]{1,0:T(8,128)(2,1)S(1)} collective-permute-done((bf16[512,512]{1,0:T(8,128)(2,1)S(1)}, bf16[512,512]{1,0:T(8,128)(2,1)S(1)}, u32[]{:S(2)}, u32[]{:S(2)}) %collective-permute-start.20) | collective-permute-done | bytes 524320 | tf_op jit(solution)/shard_map/ppermute | solution.py:546
  95.3 0.1 add_convert_fusion
  95.4 1.2 collective-permute-start.24
  96.6 0.7 project.13
  97.4 0.6 collective-permute-start.22
  98.0 1.5 %collective-permute-start.23 = (bf16[256,512]{1,0:T(8,128)(2,1)S(1)}, bf16[256,512]{1,0:T(8,128)(2,1)S(1)}, u32[]{:S(2)}, u32[]{:S(2)}) collective-permute-start(bf16[256,512]{1,0:T(8,128)(2,1)S(1)} %get-tuple-element.115), channel_id=1, source_target_pairs={{0,2},{1,3},{2,0},{3,1},{4,6},{5,7},{6,4},{7,5},{8,10},{9,11},{10,... | collective-permute-start | bytes 786440 | tf_op jit(solution)/shard_map/ppermute | solution.py:546
  99.4 0.7 project.12.refs_0_
  100.2 1.0 finish.2.refs_4_
  101.2 13.5 %collective-permute-done.22.refs_1_ = bf16[256,512]{1,0:T(8,128)(2,1)S(1)} collective-permute-done((bf16[256,512]{1,0:T(8,128)(2,1)S(1)}, bf16[256,512]{1,0:T(8,128)(2,1)S(1)}, u32[]{:S(2)}, u32[]{:S(2)}) %collective-permute-start.22) | collective-permute-done | bytes 262176 | tf_op jit(solution)/shard_map/ppermute | solution.py:546
  114.6 6.3 %collective-permute-done.23.refs_2_ = bf16[256,512]{1,0:T(8,128)(2,1)S(1)} collective-permute-done((bf16[256,512]{1,0:T(8,128)(2,1)S(1)}, bf16[256,512]{1,0:T(8,128)(2,1)S(1)}, u32[]{:S(2)}, u32[]{:S(2)}) %collective-permute-start.23) | collective-permute-done | bytes 262176 | tf_op jit(solution)/shard_map/ppermute | solution.py:546
  120.9 1.0 finish.3
  (23 shorter events, 0.1 us)
Async XLA Ops:
  0.0 11.5 %collective-permute-start.3 = (bf16[512,4096]{1,0:T(8,128)(2,1)}, bf16[512,4096]{1,0:T(8,128)(2,1)}, u32[]{:S(2)}, u32[]{:S(2)}) collective-permute-start(bf16[512,4096]{1,0:T(8,128)(2,1)} %mine_in.1), channel_id=1, source_target_pairs={{0,1},{1,0},{2,3},{3,2},{4,5},{5,4},{6,7},{7,6},{8,9},{9,8},{10,11... | collective-permute-start | bytes 12582920 | tf_op jit(solution)/shard_map/ppermute | solution.py:546
  2.9 10.1 %copy-start.7 = (s32[4]{0:T(128)S(1)}, s32[4]{0:T(128)}, u32[]{:S(2)}) copy-start(s32[4]{0:T(128)} %constant.13) | copy-start | bytes 52
  2.9 16.3 %collective-permute-start = (bf16[1552,128]{1,0:T(8,128)(2,1)}, bf16[1552,128]{1,0:T(8,128)(2,1)S(1)}, u32[]{:S(2)}, u32[]{:S(2)}) collective-permute-start(bf16[1552,128]{1,0:T(8,128)(2,1)} %get-tuple-element.65), channel_id=1, source_target_pairs={{0,8},{8,0},{16,24},{24,16},{1,9},{9,1},{17,25},{25,17},{2,10},{10... | collective-permute-start | bytes 1191944 | tf_op jit(solution)/shard_map/ppermute | solution.py:546
  5.4 20.8 %collective-permute-start.1 = (bf16[1552,128]{1,0:T(8,128)(2,1)}, bf16[1552,128]{1,0:T(8,128)(2,1)S(1)}, u32[]{:S(2)}, u32[]{:S(2)}) collective-permute-start(bf16[1552,128]{1,0:T(8,128)(2,1)} %get-tuple-element.66), channel_id=1, source_target_pairs={{0,16},{8,24},{16,0},{24,8},{1,17},{9,25},{17,1},{25,9},{2,18},{10... | collective-permute-start | bytes 1191944 | tf_op jit(solution)/shard_map/ppermute | solution.py:546
  7.0 19.2 %collective-permute-start.2 = (bf16[1552,128]{1,0:T(8,128)(2,1)}, bf16[1552,128]{1,0:T(8,128)(2,1)S(1)}, u32[]{:S(2)}, u32[]{:S(2)}) collective-permute-start(bf16[1552,128]{1,0:T(8,128)(2,1)} %get-tuple-element.67), channel_id=1, source_target_pairs={{0,24},{8,16},{16,8},{24,0},{1,25},{9,17},{17,9},{25,1},{2,26},{10... | collective-permute-start | bytes 1191944 | tf_op jit(solution)/shard_map/ppermute | solution.py:546
  9.5 26.3 %collective-permute-start.7 = (bf16[1536,128]{1,0:T(8,128)(2,1)}, bf16[1536,128]{1,0:T(8,128)(2,1)S(1)}, u32[]{:S(2)}, u32[]{:S(2)}) collective-permute-start(bf16[1536,128]{1,0:T(8,128)(2,1)} %get-tuple-element.84), channel_id=1, source_target_pairs={{0,8},{8,0},{16,24},{24,16},{1,9},{9,1},{17,25},{25,17},{2,10},{10... | collective-permute-start | bytes 1179656 | tf_op jit(solution)/shard_map/ppermute | solution.py:546
  11.5 24.3 %collective-permute-start.8 = (bf16[1536,128]{1,0:T(8,128)(2,1)}, bf16[1536,128]{1,0:T(8,128)(2,1)S(1)}, u32[]{:S(2)}, u32[]{:S(2)}) collective-permute-start(bf16[1536,128]{1,0:T(8,128)(2,1)} %get-tuple-element.85), channel_id=1, source_target_pairs={{0,16},{8,24},{16,0},{24,8},{1,17},{9,25},{17,1},{25,9},{2,18},{10... | collective-permute-start | bytes 1179656 | tf_op jit(solution)/shard_map/ppermute | solution.py:546
  13.5 12.7 %copy-start.2 = (bf16[1024,512]{1,0:T(8,128)(2,1)S(1)}, bf16[1024,512]{1,0:T(8,128)(2,1)}, u32[]{:S(2)}) copy-start(bf16[1024,512]{1,0:T(8,128)(2,1)} %refs_3_.4) | copy-start | bytes 3145732
  13.5 12.7 %copy-start.3 = (bf16[1024,512]{1,0:T(8,128)(2,1)S(1)}, bf16[1024,512]{1,0:T(8,128)(2,1)}, u32[]{:S(2)}) copy-start(bf16[1024,512]{1,0:T(8,128)(2,1)} %refs_4_.4) | copy-start | bytes 3145732
  13.5 12.7 %copy-start.4 = (bf16[1024,512]{1,0:T(8,128)(2,1)S(1)}, bf16[1024,512]{1,0:T(8,128)(2,1)}, u32[]{:S(2)}) copy-start(bf16[1024,512]{1,0:T(8,128)(2,1)} %refs_5_.4) | copy-start | bytes 3145732
  13.6 12.7 %copy-start.5 = (s32[1024]{0:T(1024)S(1)}, s32[1024]{0:T(1024)}, u32[]{:S(2)}) copy-start(s32[1024]{0:T(1024)} %param.9) | copy-start | bytes 12292
  19.3 23.3 %copy-start = (bf16[512,2048]{1,0:T(8,128)(2,1)S(1)}, bf16[512,2048]{1,0:T(8,128)(2,1)}, u32[]{:S(2)}) copy-start(bf16[512,2048]{1,0:T(8,128)(2,1)} %get-tuple-element.93.refs_2_.refs_3_.refs_6_) | copy-start | bytes 6291460
  19.3 23.3 %copy-start.1 = (bf16[512,2048]{1,0:T(8,128)(2,1)S(1)}, bf16[512,2048]{1,0:T(8,128)(2,1)}, u32[]{:S(2)}) copy-start(bf16[512,2048]{1,0:T(8,128)(2,1)} %get-tuple-element.94.refs_3_.refs_4_.refs_5_.refs_7_) | copy-start | bytes 6291460
  32.2 12.6 %copy-start.6 = (bf16[1536,128]{1,0:T(8,128)(2,1)S(1)}, bf16[1536,128]{1,0:T(8,128)(2,1)}, u32[]{:S(2)}) copy-start(bf16[1536,128]{1,0:T(8,128)(2,1)} %get-tuple-element.88) | copy-start | bytes 1179652
  32.2 6.2 %collective-permute-start.4 = (bf16[512,128]{1,0:T(8,128)(2,1)S(1)}, bf16[512,128]{1,0:T(8,128)(2,1)S(1)}, u32[]{:S(2)}, u32[]{:S(2)}) collective-permute-start(bf16[512,128]{1,0:T(8,128)(2,1)S(1)} %get-tuple-element.81), channel_id=1, source_target_pairs={{0,8},{8,0},{16,24},{24,16},{1,9},{9,1},{17,25},{25,17},{2,10},{10... | collective-permute-start | bytes 393224 | tf_op jit(solution)/shard_map/ppermute | solution.py:546
  33.3 7.3 %collective-permute-start.5 = (bf16[512,128]{1,0:T(8,128)(2,1)S(1)}, bf16[512,128]{1,0:T(8,128)(2,1)S(1)}, u32[]{:S(2)}, u32[]{:S(2)}) collective-permute-start(bf16[512,128]{1,0:T(8,128)(2,1)S(1)} %get-tuple-element.82), channel_id=1, source_target_pairs={{0,16},{8,24},{16,0},{24,8},{1,17},{9,25},{17,1},{25,9},{2,18},{10... | collective-permute-start | bytes 393224 | tf_op jit(solution)/shard_map/ppermute | solution.py:546
  34.4 6.2 %collective-permute-start.6 = (bf16[512,128]{1,0:T(8,128)(2,1)S(1)}, bf16[512,128]{1,0:T(8,128)(2,1)S(1)}, u32[]{:S(2)}, u32[]{:S(2)}) collective-permute-start(bf16[512,128]{1,0:T(8,128)(2,1)S(1)} %get-tuple-element.83), channel_id=1, source_target_pairs={{0,24},{8,16},{16,8},{24,0},{1,25},{9,17},{17,9},{25,1},{2,26},{10... | collective-permute-start | bytes 393224 | tf_op jit(solution)/shard_map/ppermute | solution.py:546
  40.6 2.0 %collective-permute-start.10 = (bf16[512,512]{1,0:T(8,128)(2,1)S(1)}, bf16[512,512]{1,0:T(8,128)(2,1)S(1)}, u32[]{:S(2)}, u32[]{:S(2)}) collective-permute-start(bf16[512,512]{1,0:T(8,128)(2,1)S(1)} %assemble.2.refs_0_), channel_id=1, source_target_pairs={{0,1},{1,0},{2,3},{3,2},{4,5},{5,4},{6,7},{7,6},{8,9},{9,8},{10,11... | collective-permute-start | bytes 1572872 | tf_op jit(solution)/shard_map/ppermute | solution.py:546
  43.2 11.7 %collective-permute-start.11 = (bf16[368,512]{1,0:T(8,128)(2,1)S(1)}, bf16[368,512]{1,0:T(8,128)(2,1)S(1)}, u32[]{:S(2)}, u32[]{:S(2)}) collective-permute-start(bf16[368,512]{1,0:T(8,128)(2,1)S(1)} %project.9), channel_id=1, source_target_pairs={{0,2},{1,3},{2,0},{3,1},{4,6},{5,7},{6,4},{7,5},{8,10},{9,11},{10,... | collective-permute-start | bytes 1130504 | tf_op jit(solution)/shard_map/ppermute | solution.py:546
  44.8 11.8 %collective-permute-start.9 = (bf16[1536,128]{1,0:T(8,128)(2,1)S(1)}, bf16[1536,128]{1,0:T(8,128)(2,1)S(1)}, u32[]{:S(2)}, u32[]{:S(2)}) collective-permute-start(bf16[1536,128]{1,0:T(8,128)(2,1)S(1)} %copy-done.6), channel_id=1, source_target_pairs={{0,24},{8,16},{16,8},{24,0},{1,25},{9,17},{17,9},{25,1},{2,26},{10... | collective-permute-start | bytes 1179656 | tf_op jit(solution)/shard_map/ppermute | solution.py:546
  47.5 30.5 %collective-permute-start.18 = (bf16[656,512]{1,0:T(8,128)(2,1)S(1)}, bf16[656,512]{1,0:T(8,128)(2,1)S(1)}, u32[]{:S(2)}, u32[]{:S(2)}) collective-permute-start(bf16[656,512]{1,0:T(8,128)(2,1)S(1)} %project.10), channel_id=1, source_target_pairs={{0,2},{1,3},{2,0},{3,1},{4,6},{5,7},{6,4},{7,5},{8,10},{9,11},{10,... | collective-permute-start | bytes 2015240 | tf_op jit(solution)/shard_map/ppermute | solution.py:546
  56.6 21.4 %collective-permute-start.19 = (bf16[368,512]{1,0:T(8,128)(2,1)S(1)}, bf16[368,512]{1,0:T(8,128)(2,1)S(1)}, u32[]{:S(2)}, u32[]{:S(2)}) collective-permute-start(bf16[368,512]{1,0:T(8,128)(2,1)S(1)} %add_convert_fusion.1), channel_id=1, source_target_pairs={{0,4},{1,5},{2,6},{3,7},{4,0},{5,1},{6,2},{7,3},{8,12},{9,13},{10,... | collective-permute-start | bytes 1130504 | tf_op jit(solution)/shard_map/ppermute | solution.py:546
  66.6 6.4 %collective-permute-start.12 = (bf16[512,128]{1,0:T(8,128)(2,1)S(1)}, bf16[512,128]{1,0:T(8,128)(2,1)S(1)}, u32[]{:S(2)}, u32[]{:S(2)}) collective-permute-start(bf16[512,128]{1,0:T(8,128)(2,1)S(1)} %get-tuple-element.101), channel_id=1, source_target_pairs={{0,8},{8,0},{16,24},{24,16},{1,9},{9,1},{17,25},{25,17},{2,10},{10... | collective-permute-start | bytes 393224 | tf_op jit(solution)/shard_map/ppermute | solution.py:546
  68.1 7.1 %collective-permute-start.13 = (bf16[512,128]{1,0:T(8,128)(2,1)S(1)}, bf16[512,128]{1,0:T(8,128)(2,1)S(1)}, u32[]{:S(2)}, u32[]{:S(2)}) collective-permute-start(bf16[512,128]{1,0:T(8,128)(2,1)S(1)} %get-tuple-element.102), channel_id=1, source_target_pairs={{0,16},{8,24},{16,0},{24,8},{1,17},{9,25},{17,1},{25,9},{2,18},{10... | collective-permute-start | bytes 393224 | tf_op jit(solution)/shard_map/ppermute | solution.py:546
  69.0 6.1 %collective-permute-start.14 = (bf16[512,128]{1,0:T(8,128)(2,1)S(1)}, bf16[512,128]{1,0:T(8,128)(2,1)S(1)}, u32[]{:S(2)}, u32[]{:S(2)}) collective-permute-start(bf16[512,128]{1,0:T(8,128)(2,1)S(1)} %get-tuple-element.103), channel_id=1, source_target_pairs={{0,24},{8,16},{16,8},{24,0},{1,25},{9,17},{17,9},{25,1},{2,26},{10... | collective-permute-start | bytes 393224 | tf_op jit(solution)/shard_map/ppermute | solution.py:546
  75.3 2.0 %collective-permute-start.15 = (bf16[176,512]{1,0:T(8,128)(2,1)S(1)}, bf16[176,512]{1,0:T(8,128)(2,1)S(1)}, u32[]{:S(2)}, u32[]{:S(2)}) collective-permute-start(bf16[176,512]{1,0:T(8,128)(2,1)S(1)} %get-tuple-element.104.refs_0_), channel_id=1, source_target_pairs={{0,1},{1,0},{2,3},{3,2},{4,5},{5,4},{6,7},{7,6},{8,9},{9,8},{10,11... | collective-permute-start | bytes 540680 | tf_op jit(solution)/shard_map/ppermute | solution.py:546
  75.3 1.9 %collective-permute-start.16 = (bf16[176,512]{1,0:T(8,128)(2,1)S(1)}, bf16[176,512]{1,0:T(8,128)(2,1)S(1)}, u32[]{:S(2)}, u32[]{:S(2)}) collective-permute-start(bf16[176,512]{1,0:T(8,128)(2,1)S(1)} %get-tuple-element.105.refs_1_), channel_id=1, source_target_pairs={{0,1},{1,0},{2,3},{3,2},{4,5},{5,4},{6,7},{7,6},{8,9},{9,8},{10,11... | collective-permute-start | bytes 540680 | tf_op jit(solution)/shard_map/ppermute | solution.py:546
  75.8 1.4 %collective-permute-start.17 = (bf16[160,512]{1,0:T(8,128)(2,1)S(1)}, bf16[160,512]{1,0:T(8,128)(2,1)S(1)}, u32[]{:S(2)}, u32[]{:S(2)}) collective-permute-start(bf16[160,512]{1,0:T(8,128)(2,1)S(1)} %get-tuple-element.106.refs_2_), channel_id=1, source_target_pairs={{0,1},{1,0},{2,3},{3,2},{4,5},{5,4},{6,7},{7,6},{8,9},{9,8},{10,11... | collective-permute-start | bytes 491528 | tf_op jit(solution)/shard_map/ppermute | solution.py:546
  78.0 17.3 %collective-permute-start.20 = (bf16[512,512]{1,0:T(8,128)(2,1)S(1)}, bf16[512,512]{1,0:T(8,128)(2,1)S(1)}, u32[]{:S(2)}, u32[]{:S(2)}) collective-permute-start(bf16[512,512]{1,0:T(8,128)(2,1)S(1)} %project.15), channel_id=1, source_target_pairs={{0,2},{1,3},{2,0},{3,1},{4,6},{5,7},{6,4},{7,5},{8,10},{9,11},{10,... | collective-permute-start | bytes 1572872 | tf_op jit(solution)/shard_map/ppermute | solution.py:546
  79.9 15.5 %collective-permute-start.21 = (bf16[144,512]{1,0:T(8,128)(2,1)S(1)}, bf16[144,512]{1,0:T(8,128)(2,1)S(1)}, u32[]{:S(2)}, u32[]{:S(2)}) collective-permute-start(bf16[144,512]{1,0:T(8,128)(2,1)S(1)} %add_convert_fusion.2), channel_id=1, source_target_pairs={{0,4},{1,5},{2,6},{3,7},{4,0},{5,1},{6,2},{7,3},{8,12},{9,13},{10,... | collective-permute-start | bytes 442376 | tf_op jit(solution)/shard_map/ppermute | solution.py:546
  95.4 25.5 %collective-permute-start.24 = (bf16[512,512]{1,0:T(8,128)(2,1)S(1)}, bf16[512,512]{1,0:T(8,128)(2,1)S(1)}, u32[]{:S(2)}, u32[]{:S(2)}) collective-permute-start(bf16[512,512]{1,0:T(8,128)(2,1)S(1)} %add_convert_fusion), channel_id=1, source_target_pairs={{0,4},{1,5},{2,6},{3,7},{4,0},{5,1},{6,2},{7,3},{8,12},{9,13},{10,... | collective-permute-start | bytes 1572872 | tf_op jit(solution)/shard_map/ppermute | solution.py:546
  97.4 17.3 %collective-permute-start.22 = (bf16[256,512]{1,0:T(8,128)(2,1)S(1)}, bf16[256,512]{1,0:T(8,128)(2,1)S(1)}, u32[]{:S(2)}, u32[]{:S(2)}) collective-permute-start(bf16[256,512]{1,0:T(8,128)(2,1)S(1)} %get-tuple-element.114), channel_id=1, source_target_pairs={{0,2},{1,3},{2,0},{3,1},{4,6},{5,7},{6,4},{7,5},{8,10},{9,11},{10,... | collective-permute-start | bytes 786440 | tf_op jit(solution)/shard_map/ppermute | solution.py:546
  98.0 22.9 %collective-permute-start.23 = (bf16[256,512]{1,0:T(8,128)(2,1)S(1)}, bf16[256,512]{1,0:T(8,128)(2,1)S(1)}, u32[]{:S(2)}, u32[]{:S(2)}) collective-permute-start(bf16[256,512]{1,0:T(8,128)(2,1)S(1)} %get-tuple-element.115), channel_id=1, source_target_pairs={{0,2},{1,3},{2,0},{3,1},{4,6},{5,7},{6,4},{7,5},{8,10},{9,11},{10,... | collective-permute-start | bytes 786440 | tf_op jit(solution)/shard_map/ppermute | solution.py:546

commit v20 on v18

--- a/solution.py
+++ b/solution.py
@@ -608,16 +608,21 @@
     back = send_back(pieces)
     mine = assemble(ctx_index, [pieces[0], *back], cuts)
     sibling = [swap(part, "head", 1) for part in mine]
-    late = [projected(mine, sibling, [(turn, 0, rows)])[0] for turn in (0, 2, 3)]
-    late[0], near_sum, across = tie(late[0], near_sum, across)
+    halves = list(zip(cuts[:-1], cuts[1:]))
+    late = projected(mine, sibling, *[[(0, *span)] for span in halves])
+    late, near_sum, across = tie(late, near_sum, across)
     result = finish(0, rows, [[(shares[3], 0)], [(near_sum, 0)], [(across, 0)]], None)
-    far = to_next(late[0], 1)
-    passed = add(late[1], far)
-    across = to_next(passed, 2)
-    last = projected(mine, sibling, *[[(1, *span)] for span in zip(cuts[:-1], cuts[1:])])
+    far = [to_next(part, 1) for part in late]
+    late = projected(mine, sibling, *[[(2, *span)] for span in halves])
+    passed = [add(*both) for both in zip(late, far)]
+    across = [to_next(part, 2) for part in passed]
+    third = rows * 11 // 32 // 16 * 16
+    thirds = ((0, third), (third, 2 * third), (2 * third, rows))
+    last = projected(mine, sibling, *[[(1, *span)] for span in thirds])
     last, passed = tie(last, passed)
     near_sum = [to_next(part, 1) for part in last]
-    terms = [[(late[2], 0)], [(part, 0) for part in near_sum], [(across, 0)]]
+    (kept,) = projected(mine, sibling, [(3, 0, rows)])
+    terms = [[(kept, 0)], [(part, 0) for part in near_sum], [(part, 0) for part in across]]
     return finish(1, rows, terms, result)
 
 

time: 119 us -> 119 us (level)
  waiting for transfers between devices: 58.6 us -> 52.5 us
  starting transfers between devices: 28.1 us -> 32.8 us
  Pallas kernels: 31.4 us -> 32.7 us
    ppermute x23 -> x26, waiting for transfers between devices: 58.6 us -> 52.5 us  [swap(): lax.ppermute(value, axis, [(source, source ^ distance) for source in rang...]
    ppermute x23 -> x26, starting transfers between devices: 28.1 us -> 32.8 us  [swap(): lax.ppermute(value, axis, [(source, source ^ distance) for source in rang...]
    pallas_call x2, Pallas kernels: 12.8 us -> 14.1 us  [attend(): pl.pallas_call(kernel, grid_spec=pltpu.PrefetchScalarGridSpec(num_scalar_...]
  transfers between devices with their start and end apart: 23 -> 26, of which waited for: 15 -> 14; matrix products, arithmetic and copies ran while one was open for 1% -> 1% of each run, Pallas kernels for 25% -> 26%
where the time goes in v20:
time: 119 us
  waiting for transfers between devices  52.5 us (44%)
  starting transfers between devices  32.8 us (28%)
  Pallas kernels  32.7 us (27%)
    ppermute x26, waiting for transfers between devices, swap(): lax.ppermute(value, axis, [(source, source ^ distance) for source in rang...  52.5 us
    ppermute x26, starting transfers between devices, swap(): lax.ppermute(value, axis, [(source, source ^ distance) for source in rang...  32.8 us
    pallas_call x2, Pallas kernels, attend(): pl.pallas_call(kernel, grid_spec=pltpu.PrefetchScalarGridSpec(num_scalar_...  14.1 us
    pallas_call x1, Pallas kernels, pack_projection(): pl.pallas_call(kernel, grid_spec=pltpu.PrefetchScalarGridSpec(num_scalar_...  5.74 us
    pallas_call x8, Pallas kernels, project(): pl.pallas_call(kernel, grid=(1,), in_specs=[plain(part.shape) for part in...  5.71 us
    pallas_call x2, Pallas kernels, pack(): pl.pallas_call(kernel, grid_spec=pltpu.PrefetchScalarGridSpec(num_scalar_...  5.02 us
  transfers between devices with their start and end apart: 26, of which 14 were waited for; matrix products, arithmetic and copies ran while one was open for 1% of the time, Pallas kernels for 26%

profile of v20, /device:TPU:0, one launch (start us, length us, event | category | flops | bytes accessed | tf_op | source)
XLA Modules:
  0.0 119.0 jit_solution(5191519693598846272)
XLA Ops:
  0.0 0.5 collective-permute-start.3
  0.5 2.5 %pack.2 = (bf16[1552,128]{1,0:T(8,128)(2,1)}, bf16[1552,128]{1,0:T(8,128)(2,1)}, bf16[1552,128]{1,0:T(8,128)(2,1)}) custom-call(s32[1]{0:T(128)} %bitcast.ctx_ref, bf16[1024,512]{1,0:T(8,128)(2,1)} %refs_3_.4, bf16[1024,512]{1,0:T(8,128)(2,1)} %refs_4_.4, bf16[1024,512]{1,0:T(8,128)(2,1)} %refs_5_.4, bf16[1024,512]{1,0:T(8,128)(2,1)} %refs_3_.4, ...), custom_call_target="tpu_custom_call" | custom-call | flops 1024 | bytes 1024 | tf_op jit(solution)/shard_map/pack/pallas_call | solution.py:201
  2.9 2.5 %collective-permute-start = (bf16[1552,128]{1,0:T(8,128)(2,1)}, bf16[1552,128]{1,0:T(8,128)(2,1)S(1)}, u32[]{:S(2)}, u32[]{:S(2)}) collective-permute-start(bf16[1552,128]{1,0:T(8,128)(2,1)} %get-tuple-element.66), channel_id=1, source_target_pairs={{0,8},{8,0},{16,24},{24,16},{1,9},{9,1},{17,25},{25,17},{2,10},{10... | collective-permute-start | bytes 1191944 | tf_op jit(solution)/shard_map/ppermute | solution.py:546
  5.4 1.5 %collective-permute-start.1 = (bf16[1552,128]{1,0:T(8,128)(2,1)}, bf16[1552,128]{1,0:T(8,128)(2,1)S(1)}, u32[]{:S(2)}, u32[]{:S(2)}) collective-permute-start(bf16[1552,128]{1,0:T(8,128)(2,1)} %get-tuple-element.67), channel_id=1, source_target_pairs={{0,16},{8,24},{16,0},{24,8},{1,17},{9,25},{17,1},{25,9},{2,18},{10... | collective-permute-start | bytes 1191944 | tf_op jit(solution)/shard_map/ppermute | solution.py:546
  7.0 0.0 collective-permute-start.2
  7.0 2.5 %pack.3 = (bf16[1536,128]{1,0:T(8,128)(2,1)}, bf16[1536,128]{1,0:T(8,128)(2,1)}, bf16[1536,128]{1,0:T(8,128)(2,1)}) custom-call(s32[1]{0:T(128)} %bitcast.ctx_ref, bf16[1024,512]{1,0:T(8,128)(2,1)} %refs_3_.4, bf16[1024,512]{1,0:T(8,128)(2,1)} %refs_4_.4, bf16[1024,512]{1,0:T(8,128)(2,1)} %refs_5_.4, bf16[1024,512]{1,0:T(8,128)(2,1)} %refs_3_.4, ...), custom_call_target="tpu_custom_call" | custom-call | flops 1024 | bytes 1024 | tf_op jit(solution)/shard_map/pack/pallas_call | solution.py:201
  9.5 2.0 %collective-permute-start.7 = (bf16[1536,128]{1,0:T(8,128)(2,1)}, bf16[1536,128]{1,0:T(8,128)(2,1)S(1)}, u32[]{:S(2)}, u32[]{:S(2)}) collective-permute-start(bf16[1536,128]{1,0:T(8,128)(2,1)} %get-tuple-element.85), channel_id=1, source_target_pairs={{0,8},{8,0},{16,24},{24,16},{1,9},{9,1},{17,25},{25,17},{2,10},{10... | collective-permute-start | bytes 1179656 | tf_op jit(solution)/shard_map/ppermute | solution.py:546
  11.5 0.0 collective-permute-done.3.sibling_in
  11.5 1.5 %collective-permute-start.8 = (bf16[1536,128]{1,0:T(8,128)(2,1)}, bf16[1536,128]{1,0:T(8,128)(2,1)S(1)}, u32[]{:S(2)}, u32[]{:S(2)}) collective-permute-start(bf16[1536,128]{1,0:T(8,128)(2,1)} %get-tuple-element.86), channel_id=1, source_target_pairs={{0,16},{8,24},{16,0},{24,8},{1,17},{9,25},{17,1},{25,9},{2,18},{10... | collective-permute-start | bytes 1179656 | tf_op jit(solution)/shard_map/ppermute | solution.py:546
  13.0 0.5 broadcast_xor_fusion.places_ref
  13.5 5.7 %pack_projection.1 = (bf16[512,2048]{1,0:T(8,128)(2,1)}, bf16[512,2048]{1,0:T(8,128)(2,1)}) custom-call(s32[4]{0:T(128)} %broadcast_xor_fusion.places_ref, bf16[512,4096]{1,0:T(8,128)(2,1)} %mine_in.1, bf16[512,4096]{1,0:T(8,128)(2,1)} %collective-permute-done.3.sibling_in), custom_call_target="tpu_custom_call" | custom-call | flops 1024 | bytes 1024 | tf_op jit(solution)/shard_map/pack_projection/pallas_call | solution.py:227
  19.3 0.0 collective-permute-done.refs_4_.refs_7_
  19.3 6.9 %collective-permute-done.1.refs_5_.refs_8_ = bf16[1552,128]{1,0:T(8,128)(2,1)S(1)} collective-permute-done((bf16[1552,128]{1,0:T(8,128)(2,1)}, bf16[1552,128]{1,0:T(8,128)(2,1)S(1)}, u32[]{:S(2)}, u32[]{:S(2)}) %collective-permute-start.1) | collective-permute-done | bytes 397344 | tf_op jit(solution)/shard_map/ppermute | solution.py:546
  26.2 0.0 collective-permute-done.2.refs_6_.refs_9_
  26.2 6.0 %attend_low.1 = (bf16[512,128]{1,0:T(8,128)(2,1)S(1)}, bf16[512,128]{1,0:T(8,128)(2,1)S(1)}, bf16[512,128]{1,0:T(8,128)(2,1)S(1)}, bf16[512,128]{1,0:T(8,128)(2,1)S(1)}) custom-call(s32[1]{0:T(128)} %bitcast.ctx_ref, bf16[1024,512]{1,0:T(8,128)(2,1)S(1)} %copy-done.2, bf16[1024,512]{1,0:T(8,128)(2,1)S(1)} %copy-done.3, bf16[1024,512]{1,0:T(8,128)(2,1)S(1)} %copy-done.4, ...), custom_call_target="tpu_custom_call" | custom-call | flops 1024 | bytes 1024 | tf_op jit(solution)/shard_map/attend_low/pallas_call | solution.py:409
  32.2 1.0 collective-permute-start.4
  33.3 1.1 collective-permute-start.5
  34.4 1.4 %collective-permute-start.6 = (bf16[512,128]{1,0:T(8,128)(2,1)S(1)}, bf16[512,128]{1,0:T(8,128)(2,1)S(1)}, u32[]{:S(2)}, u32[]{:S(2)}) collective-permute-start(bf16[512,128]{1,0:T(8,128)(2,1)S(1)} %get-tuple-element.84), channel_id=1, source_target_pairs={{0,24},{8,16},{16,8},{24,0},{1,25},{9,17},{17,9},{25,1},{2,26},{10... | collective-permute-start | bytes 393224 | tf_op jit(solution)/shard_map/ppermute | solution.py:546
  35.8 2.6 %collective-permute-done.4.refs_1_ = bf16[512,128]{1,0:T(8,128)(2,1)S(1)} collective-permute-done((bf16[512,128]{1,0:T(8,128)(2,1)S(1)}, bf16[512,128]{1,0:T(8,128)(2,1)S(1)}, u32[]{:S(2)}, u32[]{:S(2)}) %collective-permute-start.4) | collective-permute-done | bytes 131104 | tf_op jit(solution)/shard_map/ppermute | solution.py:546
  38.4 2.1 %collective-permute-done.5.refs_2_ = bf16[512,128]{1,0:T(8,128)(2,1)S(1)} collective-permute-done((bf16[512,128]{1,0:T(8,128)(2,1)S(1)}, bf16[512,128]{1,0:T(8,128)(2,1)S(1)}, u32[]{:S(2)}, u32[]{:S(2)}) %collective-permute-start.5) | collective-permute-done | bytes 131104 | tf_op jit(solution)/shard_map/ppermute | solution.py:546
  40.5 0.1 assemble.2.refs_0_
  40.6 0.1 collective-permute-start.10
  40.7 1.9 %collective-permute-done.10.refs_1_ = bf16[512,512]{1,0:T(8,128)(2,1)S(1)} collective-permute-done((bf16[512,512]{1,0:T(8,128)(2,1)S(1)}, bf16[512,512]{1,0:T(8,128)(2,1)S(1)}, u32[]{:S(2)}, u32[]{:S(2)}) %collective-permute-start.10) | collective-permute-done | bytes 524320 | tf_op jit(solution)/shard_map/ppermute | solution.py:546
  42.6 0.7 project.8
  43.3 1.6 %collective-permute-start.11 = (bf16[512,512]{1,0:T(8,128)(2,1)S(1)}, bf16[512,512]{1,0:T(8,128)(2,1)S(1)}, u32[]{:S(2)}, u32[]{:S(2)}) collective-permute-start(bf16[512,512]{1,0:T(8,128)(2,1)S(1)} %project.8), channel_id=1, source_target_pairs={{0,2},{1,3},{2,0},{3,1},{4,6},{5,7},{6,4},{7,5},{8,10},{9,11},{10,... | collective-permute-start | bytes 1572872 | tf_op jit(solution)/shard_map/ppermute | solution.py:546
  45.0 1.8 %collective-permute-start.9 = (bf16[1536,128]{1,0:T(8,128)(2,1)S(1)}, bf16[1536,128]{1,0:T(8,128)(2,1)S(1)}, u32[]{:S(2)}, u32[]{:S(2)}) collective-permute-start(bf16[1536,128]{1,0:T(8,128)(2,1)S(1)} %copy-done.6), channel_id=1, source_target_pairs={{0,24},{8,16},{16,8},{24,0},{1,25},{9,17},{17,9},{25,1},{2,26},{10... | collective-permute-start | bytes 1179656 | tf_op jit(solution)/shard_map/ppermute | solution.py:546
  46.7 0.7 project.9
  47.5 0.5 collective-permute-start.17
  48.0 0.7 project.10
  48.7 0.7 project.11.refs_0_
  49.4 8.8 %collective-permute-done.11 = bf16[512,512]{1,0:T(8,128)(2,1)S(1)} collective-permute-done((bf16[512,512]{1,0:T(8,128)(2,1)S(1)}, bf16[512,512]{1,0:T(8,128)(2,1)S(1)}, u32[]{:S(2)}, u32[]{:S(2)}) %collective-permute-start.11) | collective-permute-done | bytes 524320 | tf_op jit(solution)/shard_map/ppermute | solution.py:546
  58.2 0.1 add_convert_fusion
  58.3 2.7 %collective-permute-start.18 = (bf16[512,512]{1,0:T(8,128)(2,1)S(1)}, bf16[512,512]{1,0:T(8,128)(2,1)S(1)}, u32[]{:S(2)}, u32[]{:S(2)}) collective-permute-start(bf16[512,512]{1,0:T(8,128)(2,1)S(1)} %add_convert_fusion), channel_id=1, source_target_pairs={{0,4},{1,5},{2,6},{3,7},{4,0},{5,1},{6,2},{7,3},{8,12},{9,13},{10,... | collective-permute-start | bytes 1572872 | tf_op jit(solution)/shard_map/ppermute | solution.py:546
  61.0 8.1 %attend_high.1 = (bf16[512,128]{1,0:T(8,128)(2,1)S(1)}, bf16[512,128]{1,0:T(8,128)(2,1)S(1)}, bf16[512,128]{1,0:T(8,128)(2,1)S(1)}, bf16[512,128]{1,0:T(8,128)(2,1)S(1)}) custom-call(s32[1]{0:T(128)} %bitcast.ctx_ref, bf16[1024,512]{1,0:T(8,128)(2,1)S(1)} %copy-done.2, bf16[1024,512]{1,0:T(8,128)(2,1)S(1)} %copy-done.3, bf16[1024,512]{1,0:T(8,128)(2,1)S(1)} %copy-done.4, ...), custom_call_target="tpu_custom_call" | custom-call | flops 1024 | bytes 1024 | tf_op jit(solution)/shard_map/attend_high/pallas_call | solution.py:409
  69.0 1.4 %collective-permute-start.12 = (bf16[512,128]{1,0:T(8,128)(2,1)S(1)}, bf16[512,128]{1,0:T(8,128)(2,1)S(1)}, u32[]{:S(2)}, u32[]{:S(2)}) collective-permute-start(bf16[512,128]{1,0:T(8,128)(2,1)S(1)} %get-tuple-element.100), channel_id=1, source_target_pairs={{0,8},{8,0},{16,24},{24,16},{1,9},{9,1},{17,25},{25,17},{2,10},{10... | collective-permute-start | bytes 393224 | tf_op jit(solution)/shard_map/ppermute | solution.py:546
  70.5 1.0 collective-permute-start.13
  71.4 1.2 collective-permute-start.14
  72.6 2.4 %collective-permute-done.12.refs_1_ = bf16[512,128]{1,0:T(8,128)(2,1)S(1)} collective-permute-done((bf16[512,128]{1,0:T(8,128)(2,1)S(1)}, bf16[512,128]{1,0:T(8,128)(2,1)S(1)}, u32[]{:S(2)}, u32[]{:S(2)}) %collective-permute-start.12) | collective-permute-done | bytes 131104 | tf_op jit(solution)/shard_map/ppermute | solution.py:546
  75.0 0.7 collective-permute-done.13.refs_2_
  75.7 1.6 %collective-permute-done.14.refs_3_ = bf16[512,128]{1,0:T(8,128)(2,1)S(1)} collective-permute-done((bf16[512,128]{1,0:T(8,128)(2,1)S(1)}, bf16[512,128]{1,0:T(8,128)(2,1)S(1)}, u32[]{:S(2)}, u32[]{:S(2)}) %collective-permute-start.14) | collective-permute-done | bytes 131104 | tf_op jit(solution)/shard_map/ppermute | solution.py:546
  77.3 0.1 assemble.3
  77.4 0.1 collective-permute-start.15
  77.5 0.5 collective-permute-start.16
  78.0 1.0 collective-permute-done.15.refs_2_
  79.0 0.4 collective-permute-done.16.refs_3_
  79.4 0.7 project.15
  80.1 2.8 %collective-permute-done.18.refs_2_ = bf16[512,512]{1,0:T(8,128)(2,1)S(1)} collective-permute-done((bf16[512,512]{1,0:T(8,128)(2,1)S(1)}, bf16[512,512]{1,0:T(8,128)(2,1)S(1)}, u32[]{:S(2)}, u32[]{:S(2)}) %collective-permute-start.18) | collective-permute-done | bytes 524320 | tf_op jit(solution)/shard_map/ppermute | solution.py:546
  82.9 0.8 collective-permute-start.19
  83.7 1.2 %collective-permute-start.20 = (bf16[256,512]{1,0:T(8,128)(2,1)S(1)}, bf16[256,512]{1,0:T(8,128)(2,1)S(1)}, u32[]{:S(2)}, u32[]{:S(2)}) collective-permute-start(bf16[256,512]{1,0:T(8,128)(2,1)S(1)} %get-tuple-element.114), channel_id=1, source_target_pairs={{0,2},{1,3},{2,0},{3,1},{4,6},{5,7},{6,4},{7,5},{8,10},{9,11},{10,... | collective-permute-start | bytes 786440 | tf_op jit(solution)/shard_map/ppermute | solution.py:546
  84.9 0.7 project.14
  85.6 8.5 %collective-permute-done.19 = bf16[256,512]{1,0:T(8,128)(2,1)S(1)} collective-permute-done((bf16[256,512]{1,0:T(8,128)(2,1)S(1)}, bf16[256,512]{1,0:T(8,128)(2,1)S(1)}, u32[]{:S(2)}, u32[]{:S(2)}) %collective-permute-start.19) | collective-permute-done | bytes 262176 | tf_op jit(solution)/shard_map/ppermute | solution.py:546
  94.2 0.1 add_convert_fusion.2
  94.2 1.9 %collective-permute-start.24 = (bf16[256,512]{1,0:T(8,128)(2,1)S(1)}, bf16[256,512]{1,0:T(8,128)(2,1)S(1)}, u32[]{:S(2)}, u32[]{:S(2)}) collective-permute-start(bf16[256,512]{1,0:T(8,128)(2,1)S(1)} %add_convert_fusion.2), channel_id=1, source_target_pairs={{0,4},{1,5},{2,6},{3,7},{4,0},{5,1},{6,2},{7,3},{8,12},{9,13},{10,... | collective-permute-start | bytes 786440 | tf_op jit(solution)/shard_map/ppermute | solution.py:546
  96.2 0.8 collective-permute-done.20
  97.0 0.1 add_convert_fusion.1
  97.0 3.0 %collective-permute-start.25 = (bf16[256,512]{1,0:T(8,128)(2,1)S(1)}, bf16[256,512]{1,0:T(8,128)(2,1)S(1)}, u32[]{:S(2)}, u32[]{:S(2)}) collective-permute-start(bf16[256,512]{1,0:T(8,128)(2,1)S(1)} %add_convert_fusion.1), channel_id=1, source_target_pairs={{0,4},{1,5},{2,6},{3,7},{4,0},{5,1},{6,2},{7,3},{8,12},{9,13},{10,... | collective-permute-start | bytes 786440 | tf_op jit(solution)/shard_map/ppermute | solution.py:546
  100.0 0.7 project.13
  100.8 1.5 %collective-permute-start.21 = (bf16[176,512]{1,0:T(8,128)(2,1)S(1)}, bf16[176,512]{1,0:T(8,128)(2,1)S(1)}, u32[]{:S(2)}, u32[]{:S(2)}) collective-permute-start(bf16[176,512]{1,0:T(8,128)(2,1)S(1)} %get-tuple-element.115), channel_id=1, source_target_pairs={{0,2},{1,3},{2,0},{3,1},{4,6},{5,7},{6,4},{7,5},{8,10},{9,11},{10,... | collective-permute-start | bytes 540680 | tf_op jit(solution)/shard_map/ppermute | solution.py:546
  102.3 0.6 collective-permute-start.22
  102.9 1.4 %collective-permute-start.23 = (bf16[160,512]{1,0:T(8,128)(2,1)S(1)}, bf16[160,512]{1,0:T(8,128)(2,1)S(1)}, u32[]{:S(2)}, u32[]{:S(2)}) collective-permute-start(bf16[160,512]{1,0:T(8,128)(2,1)S(1)} %get-tuple-element.117), channel_id=1, source_target_pairs={{0,2},{1,3},{2,0},{3,1},{4,6},{5,7},{6,4},{7,5},{8,10},{9,11},{10,... | collective-permute-start | bytes 491528 | tf_op jit(solution)/shard_map/ppermute | solution.py:546
  104.3 0.7 project.12.refs_0_
  105.0 1.0 finish.2.refs_6_
  106.0 12.0 %collective-permute-done.23.refs_3_ = bf16[160,512]{1,0:T(8,128)(2,1)S(1)} collective-permute-done((bf16[160,512]{1,0:T(8,128)(2,1)S(1)}, bf16[160,512]{1,0:T(8,128)(2,1)S(1)}, u32[]{:S(2)}, u32[]{:S(2)}) %collective-permute-start.23) | collective-permute-done | bytes 163872 | tf_op jit(solution)/shard_map/ppermute | solution.py:546
  118.0 1.0 finish.3
  (25 shorter events, 0.1 us)
Async XLA Ops:
  0.0 11.5 %collective-permute-start.3 = (bf16[512,4096]{1,0:T(8,128)(2,1)}, bf16[512,4096]{1,0:T(8,128)(2,1)}, u32[]{:S(2)}, u32[]{:S(2)}) collective-permute-start(bf16[512,4096]{1,0:T(8,128)(2,1)} %mine_in.1), channel_id=1, source_target_pairs={{0,1},{1,0},{2,3},{3,2},{4,5},{5,4},{6,7},{7,6},{8,9},{9,8},{10,11... | collective-permute-start | bytes 12582920 | tf_op jit(solution)/shard_map/ppermute | solution.py:546
  2.9 10.0 %copy-start.7 = (s32[4]{0:T(128)S(1)}, s32[4]{0:T(128)}, u32[]{:S(2)}) copy-start(s32[4]{0:T(128)} %constant.13) | copy-start | bytes 52
  2.9 16.3 %collective-permute-start = (bf16[1552,128]{1,0:T(8,128)(2,1)}, bf16[1552,128]{1,0:T(8,128)(2,1)S(1)}, u32[]{:S(2)}, u32[]{:S(2)}) collective-permute-start(bf16[1552,128]{1,0:T(8,128)(2,1)} %get-tuple-element.66), channel_id=1, source_target_pairs={{0,8},{8,0},{16,24},{24,16},{1,9},{9,1},{17,25},{25,17},{2,10},{10... | collective-permute-start | bytes 1191944 | tf_op jit(solution)/shard_map/ppermute | solution.py:546
  5.4 20.8 %collective-permute-start.1 = (bf16[1552,128]{1,0:T(8,128)(2,1)}, bf16[1552,128]{1,0:T(8,128)(2,1)S(1)}, u32[]{:S(2)}, u32[]{:S(2)}) collective-permute-start(bf16[1552,128]{1,0:T(8,128)(2,1)} %get-tuple-element.67), channel_id=1, source_target_pairs={{0,16},{8,24},{16,0},{24,8},{1,17},{9,25},{17,1},{25,9},{2,18},{10... | collective-permute-start | bytes 1191944 | tf_op jit(solution)/shard_map/ppermute | solution.py:546
  7.0 19.2 %collective-permute-start.2 = (bf16[1552,128]{1,0:T(8,128)(2,1)}, bf16[1552,128]{1,0:T(8,128)(2,1)S(1)}, u32[]{:S(2)}, u32[]{:S(2)}) collective-permute-start(bf16[1552,128]{1,0:T(8,128)(2,1)} %get-tuple-element.68), channel_id=1, source_target_pairs={{0,24},{8,16},{16,8},{24,0},{1,25},{9,17},{17,9},{25,1},{2,26},{10... | collective-permute-start | bytes 1191944 | tf_op jit(solution)/shard_map/ppermute | solution.py:546
  9.5 26.3 %collective-permute-start.7 = (bf16[1536,128]{1,0:T(8,128)(2,1)}, bf16[1536,128]{1,0:T(8,128)(2,1)S(1)}, u32[]{:S(2)}, u32[]{:S(2)}) collective-permute-start(bf16[1536,128]{1,0:T(8,128)(2,1)} %get-tuple-element.85), channel_id=1, source_target_pairs={{0,8},{8,0},{16,24},{24,16},{1,9},{9,1},{17,25},{25,17},{2,10},{10... | collective-permute-start | bytes 1179656 | tf_op jit(solution)/shard_map/ppermute | solution.py:546
  11.5 24.3 %collective-permute-start.8 = (bf16[1536,128]{1,0:T(8,128)(2,1)}, bf16[1536,128]{1,0:T(8,128)(2,1)S(1)}, u32[]{:S(2)}, u32[]{:S(2)}) collective-permute-start(bf16[1536,128]{1,0:T(8,128)(2,1)} %get-tuple-element.86), channel_id=1, source_target_pairs={{0,16},{8,24},{16,0},{24,8},{1,17},{9,25},{17,1},{25,9},{2,18},{10... | collective-permute-start | bytes 1179656 | tf_op jit(solution)/shard_map/ppermute | solution.py:546
  13.5 12.7 %copy-start.2 = (bf16[1024,512]{1,0:T(8,128)(2,1)S(1)}, bf16[1024,512]{1,0:T(8,128)(2,1)}, u32[]{:S(2)}) copy-start(bf16[1024,512]{1,0:T(8,128)(2,1)} %refs_3_.4) | copy-start | bytes 3145732
  13.5 12.7 %copy-start.3 = (bf16[1024,512]{1,0:T(8,128)(2,1)S(1)}, bf16[1024,512]{1,0:T(8,128)(2,1)}, u32[]{:S(2)}) copy-start(bf16[1024,512]{1,0:T(8,128)(2,1)} %refs_4_.4) | copy-start | bytes 3145732
  13.5 12.7 %copy-start.4 = (bf16[1024,512]{1,0:T(8,128)(2,1)S(1)}, bf16[1024,512]{1,0:T(8,128)(2,1)}, u32[]{:S(2)}) copy-start(bf16[1024,512]{1,0:T(8,128)(2,1)} %refs_5_.4) | copy-start | bytes 3145732
  13.5 12.7 %copy-start.5 = (s32[1024]{0:T(1024)S(1)}, s32[1024]{0:T(1024)}, u32[]{:S(2)}) copy-start(s32[1024]{0:T(1024)} %param.9) | copy-start | bytes 12292
  19.3 23.4 %copy-start = (bf16[512,2048]{1,0:T(8,128)(2,1)S(1)}, bf16[512,2048]{1,0:T(8,128)(2,1)}, u32[]{:S(2)}) copy-start(bf16[512,2048]{1,0:T(8,128)(2,1)} %get-tuple-element.94.refs_2_.refs_4_) | copy-start | bytes 6291460
  19.3 23.4 %copy-start.1 = (bf16[512,2048]{1,0:T(8,128)(2,1)S(1)}, bf16[512,2048]{1,0:T(8,128)(2,1)}, u32[]{:S(2)}) copy-start(bf16[512,2048]{1,0:T(8,128)(2,1)} %get-tuple-element.95.refs_3_.refs_5_) | copy-start | bytes 6291460
  32.2 12.7 %copy-start.6 = (bf16[1536,128]{1,0:T(8,128)(2,1)S(1)}, bf16[1536,128]{1,0:T(8,128)(2,1)}, u32[]{:S(2)}) copy-start(bf16[1536,128]{1,0:T(8,128)(2,1)} %get-tuple-element.89) | copy-start | bytes 1179652
  32.2 6.2 %collective-permute-start.4 = (bf16[512,128]{1,0:T(8,128)(2,1)S(1)}, bf16[512,128]{1,0:T(8,128)(2,1)S(1)}, u32[]{:S(2)}, u32[]{:S(2)}) collective-permute-start(bf16[512,128]{1,0:T(8,128)(2,1)S(1)} %get-tuple-element.82), channel_id=1, source_target_pairs={{0,8},{8,0},{16,24},{24,16},{1,9},{9,1},{17,25},{25,17},{2,10},{10... | collective-permute-start | bytes 393224 | tf_op jit(solution)/shard_map/ppermute | solution.py:546
  33.3 7.3 %collective-permute-start.5 = (bf16[512,128]{1,0:T(8,128)(2,1)S(1)}, bf16[512,128]{1,0:T(8,128)(2,1)S(1)}, u32[]{:S(2)}, u32[]{:S(2)}) collective-permute-start(bf16[512,128]{1,0:T(8,128)(2,1)S(1)} %get-tuple-element.83), channel_id=1, source_target_pairs={{0,16},{8,24},{16,0},{24,8},{1,17},{9,25},{17,1},{25,9},{2,18},{10... | collective-permute-start | bytes 393224 | tf_op jit(solution)/shard_map/ppermute | solution.py:546
  34.4 6.2 %collective-permute-start.6 = (bf16[512,128]{1,0:T(8,128)(2,1)S(1)}, bf16[512,128]{1,0:T(8,128)(2,1)S(1)}, u32[]{:S(2)}, u32[]{:S(2)}) collective-permute-start(bf16[512,128]{1,0:T(8,128)(2,1)S(1)} %get-tuple-element.84), channel_id=1, source_target_pairs={{0,24},{8,16},{16,8},{24,0},{1,25},{9,17},{17,9},{25,1},{2,26},{10... | collective-permute-start | bytes 393224 | tf_op jit(solution)/shard_map/ppermute | solution.py:546
  40.6 2.0 %collective-permute-start.10 = (bf16[512,512]{1,0:T(8,128)(2,1)S(1)}, bf16[512,512]{1,0:T(8,128)(2,1)S(1)}, u32[]{:S(2)}, u32[]{:S(2)}) collective-permute-start(bf16[512,512]{1,0:T(8,128)(2,1)S(1)} %assemble.2.refs_0_), channel_id=1, source_target_pairs={{0,1},{1,0},{2,3},{3,2},{4,5},{5,4},{6,7},{7,6},{8,9},{9,8},{10,11... | collective-permute-start | bytes 1572872 | tf_op jit(solution)/shard_map/ppermute | solution.py:546
  43.3 14.8 %collective-permute-start.11 = (bf16[512,512]{1,0:T(8,128)(2,1)S(1)}, bf16[512,512]{1,0:T(8,128)(2,1)S(1)}, u32[]{:S(2)}, u32[]{:S(2)}) collective-permute-start(bf16[512,512]{1,0:T(8,128)(2,1)S(1)} %project.8), channel_id=1, source_target_pairs={{0,2},{1,3},{2,0},{3,1},{4,6},{5,7},{6,4},{7,5},{8,10},{9,11},{10,... | collective-permute-start | bytes 1572872 | tf_op jit(solution)/shard_map/ppermute | solution.py:546
  45.0 13.3 %collective-permute-start.9 = (bf16[1536,128]{1,0:T(8,128)(2,1)S(1)}, bf16[1536,128]{1,0:T(8,128)(2,1)S(1)}, u32[]{:S(2)}, u32[]{:S(2)}) collective-permute-start(bf16[1536,128]{1,0:T(8,128)(2,1)S(1)} %copy-done.6), channel_id=1, source_target_pairs={{0,24},{8,16},{16,8},{24,0},{1,25},{9,17},{17,9},{25,1},{2,26},{10... | collective-permute-start | bytes 1179656 | tf_op jit(solution)/shard_map/ppermute | solution.py:546
  47.5 32.6 %collective-permute-start.17 = (bf16[512,512]{1,0:T(8,128)(2,1)S(1)}, bf16[512,512]{1,0:T(8,128)(2,1)S(1)}, u32[]{:S(2)}, u32[]{:S(2)}) collective-permute-start(bf16[512,512]{1,0:T(8,128)(2,1)S(1)} %project.9), channel_id=1, source_target_pairs={{0,2},{1,3},{2,0},{3,1},{4,6},{5,7},{6,4},{7,5},{8,10},{9,11},{10,... | collective-permute-start | bytes 1572872 | tf_op jit(solution)/shard_map/ppermute | solution.py:546
  58.3 24.6 %collective-permute-start.18 = (bf16[512,512]{1,0:T(8,128)(2,1)S(1)}, bf16[512,512]{1,0:T(8,128)(2,1)S(1)}, u32[]{:S(2)}, u32[]{:S(2)}) collective-permute-start(bf16[512,512]{1,0:T(8,128)(2,1)S(1)} %add_convert_fusion), channel_id=1, source_target_pairs={{0,4},{1,5},{2,6},{3,7},{4,0},{5,1},{6,2},{7,3},{8,12},{9,13},{10,... | collective-permute-start | bytes 1572872 | tf_op jit(solution)/shard_map/ppermute | solution.py:546
  69.0 6.0 %collective-permute-start.12 = (bf16[512,128]{1,0:T(8,128)(2,1)S(1)}, bf16[512,128]{1,0:T(8,128)(2,1)S(1)}, u32[]{:S(2)}, u32[]{:S(2)}) collective-permute-start(bf16[512,128]{1,0:T(8,128)(2,1)S(1)} %get-tuple-element.100), channel_id=1, source_target_pairs={{0,8},{8,0},{16,24},{24,16},{1,9},{9,1},{17,25},{25,17},{2,10},{10... | collective-permute-start | bytes 393224 | tf_op jit(solution)/shard_map/ppermute | solution.py:546
  70.5 5.2 %collective-permute-start.13 = (bf16[512,128]{1,0:T(8,128)(2,1)S(1)}, bf16[512,128]{1,0:T(8,128)(2,1)S(1)}, u32[]{:S(2)}, u32[]{:S(2)}) collective-permute-start(bf16[512,128]{1,0:T(8,128)(2,1)S(1)} %get-tuple-element.101), channel_id=1, source_target_pairs={{0,16},{8,24},{16,0},{24,8},{1,17},{9,25},{17,1},{25,9},{2,18},{10... | collective-permute-start | bytes 393224 | tf_op jit(solution)/shard_map/ppermute | solution.py:546
  71.4 5.9 %collective-permute-start.14 = (bf16[512,128]{1,0:T(8,128)(2,1)S(1)}, bf16[512,128]{1,0:T(8,128)(2,1)S(1)}, u32[]{:S(2)}, u32[]{:S(2)}) collective-permute-start(bf16[512,128]{1,0:T(8,128)(2,1)S(1)} %get-tuple-element.102), channel_id=1, source_target_pairs={{0,24},{8,16},{16,8},{24,0},{1,25},{9,17},{17,9},{25,1},{2,26},{10... | collective-permute-start | bytes 393224 | tf_op jit(solution)/shard_map/ppermute | solution.py:546
  77.4 1.6 %collective-permute-start.15 = (bf16[256,512]{1,0:T(8,128)(2,1)S(1)}, bf16[256,512]{1,0:T(8,128)(2,1)S(1)}, u32[]{:S(2)}, u32[]{:S(2)}) collective-permute-start(bf16[256,512]{1,0:T(8,128)(2,1)S(1)} %get-tuple-element.103.refs_0_), channel_id=1, source_target_pairs={{0,1},{1,0},{2,3},{3,2},{4,5},{5,4},{6,7},{7,6},{8,9},{9,8},{10,11... | collective-permute-start | bytes 786440 | tf_op jit(solution)/shard_map/ppermute | solution.py:546
  77.5 1.9 %collective-permute-start.16 = (bf16[256,512]{1,0:T(8,128)(2,1)S(1)}, bf16[256,512]{1,0:T(8,128)(2,1)S(1)}, u32[]{:S(2)}, u32[]{:S(2)}) collective-permute-start(bf16[256,512]{1,0:T(8,128)(2,1)S(1)} %get-tuple-element.104.refs_1_), channel_id=1, source_target_pairs={{0,1},{1,0},{2,3},{3,2},{4,5},{5,4},{6,7},{7,6},{8,9},{9,8},{10,11... | collective-permute-start | bytes 786440 | tf_op jit(solution)/shard_map/ppermute | solution.py:546
  82.9 11.3 %collective-permute-start.19 = (bf16[256,512]{1,0:T(8,128)(2,1)S(1)}, bf16[256,512]{1,0:T(8,128)(2,1)S(1)}, u32[]{:S(2)}, u32[]{:S(2)}) collective-permute-start(bf16[256,512]{1,0:T(8,128)(2,1)S(1)} %get-tuple-element.112), channel_id=1, source_target_pairs={{0,2},{1,3},{2,0},{3,1},{4,6},{5,7},{6,4},{7,5},{8,10},{9,11},{10,... | collective-permute-start | bytes 786440 | tf_op jit(solution)/shard_map/ppermute | solution.py:546
  83.7 13.3 %collective-permute-start.20 = (bf16[256,512]{1,0:T(8,128)(2,1)S(1)}, bf16[256,512]{1,0:T(8,128)(2,1)S(1)}, u32[]{:S(2)}, u32[]{:S(2)}) collective-permute-start(bf16[256,512]{1,0:T(8,128)(2,1)S(1)} %get-tuple-element.114), channel_id=1, source_target_pairs={{0,2},{1,3},{2,0},{3,1},{4,6},{5,7},{6,4},{7,5},{8,10},{9,11},{10,... | collective-permute-start | bytes 786440 | tf_op jit(solution)/shard_map/ppermute | solution.py:546
  94.2 23.8 %collective-permute-start.24 = (bf16[256,512]{1,0:T(8,128)(2,1)S(1)}, bf16[256,512]{1,0:T(8,128)(2,1)S(1)}, u32[]{:S(2)}, u32[]{:S(2)}) collective-permute-start(bf16[256,512]{1,0:T(8,128)(2,1)S(1)} %add_convert_fusion.2), channel_id=1, source_target_pairs={{0,4},{1,5},{2,6},{3,7},{4,0},{5,1},{6,2},{7,3},{8,12},{9,13},{10,... | collective-permute-start | bytes 786440 | tf_op jit(solution)/shard_map/ppermute | solution.py:546
  97.0 21.0 %collective-permute-start.25 = (bf16[256,512]{1,0:T(8,128)(2,1)S(1)}, bf16[256,512]{1,0:T(8,128)(2,1)S(1)}, u32[]{:S(2)}, u32[]{:S(2)}) collective-permute-start(bf16[256,512]{1,0:T(8,128)(2,1)S(1)} %add_convert_fusion.1), channel_id=1, source_target_pairs={{0,4},{1,5},{2,6},{3,7},{4,0},{5,1},{6,2},{7,3},{8,12},{9,13},{10,... | collective-permute-start | bytes 786440 | tf_op jit(solution)/shard_map/ppermute | solution.py:546
  100.8 17.2 %collective-permute-start.21 = (bf16[176,512]{1,0:T(8,128)(2,1)S(1)}, bf16[176,512]{1,0:T(8,128)(2,1)S(1)}, u32[]{:S(2)}, u32[]{:S(2)}) collective-permute-start(bf16[176,512]{1,0:T(8,128)(2,1)S(1)} %get-tuple-element.115), channel_id=1, source_target_pairs={{0,2},{1,3},{2,0},{3,1},{4,6},{5,7},{6,4},{7,5},{8,10},{9,11},{10,... | collective-permute-start | bytes 540680 | tf_op jit(solution)/shard_map/ppermute | solution.py:546
  102.3 15.7 %collective-permute-start.22 = (bf16[176,512]{1,0:T(8,128)(2,1)S(1)}, bf16[176,512]{1,0:T(8,128)(2,1)S(1)}, u32[]{:S(2)}, u32[]{:S(2)}) collective-permute-start(bf16[176,512]{1,0:T(8,128)(2,1)S(1)} %get-tuple-element.116), channel_id=1, source_target_pairs={{0,2},{1,3},{2,0},{3,1},{4,6},{5,7},{6,4},{7,5},{8,10},{9,11},{10,... | collective-permute-start | bytes 540680 | tf_op jit(solution)/shard_map/ppermute | solution.py:546
  102.9 15.1 %collective-permute-start.23 = (bf16[160,512]{1,0:T(8,128)(2,1)S(1)}, bf16[160,512]{1,0:T(8,128)(2,1)S(1)}, u32[]{:S(2)}, u32[]{:S(2)}) collective-permute-start(bf16[160,512]{1,0:T(8,128)(2,1)S(1)} %get-tuple-element.117), channel_id=1, source_target_pairs={{0,2},{1,3},{2,0},{3,1},{4,6},{5,7},{6,4},{7,5},{8,10},{9,11},{10,... | collective-permute-start | bytes 491528 | tf_op jit(solution)/shard_map/ppermute | solution.py:546

commit v21 on v18

--- a/solution.py
+++ b/solution.py
@@ -169,48 +169,69 @@
     group = queries.shape[1] // HD
     doc_rows = 0 if docs is None else 16 * pl.cdiv(docs.shape[0], 16)
     total = 3 * rows + doc_rows
-
-    def kernel(ctx_ref, *refs):
-        outs = refs[len(refs) - (group - 1) :]
+    others = range(group - 1)
+
+    def kernel(ctx_ref, query_ref, key_ref, value_ref, *refs):
+        refs = list(refs)
+        docs_ref = None if docs is None else refs.pop(0)
+        outs = [refs.pop(0) for _ in others]
+        taken, turned, taken_sem, direct_sem, turned_sem = refs
+        taking = []
+        direct = []
+        for place in others:
+            column = pl.multiple_of((ctx_ref[0] ^ (place + 1)) * HD, HD)
+            piece = (pl.ds(half * rows, rows), pl.ds(column, HD))
+            taking.append(
+                pltpu.make_async_copy(value_ref.at[piece], taken.at[place], taken_sem.at[place])
+            )
+            taking[-1].start()
+            for part, ref in enumerate((query_ref, key_ref)):
+                target = outs[place].at[pl.ds(part * rows, rows), :]
+                direct.append(
+                    pltpu.make_async_copy(ref.at[piece], target, direct_sem.at[place, part])
+                )
+                direct[-1].start()
         if docs is not None:
-            mine = refs[3 * (group - 1)][...].astype(jnp.float32)
+            mine = docs_ref[...].astype(jnp.float32)
             empty = jnp.zeros((doc_rows - mine.shape[0], HD), jnp.float32)
             mine = jnp.concatenate([mine, empty], axis=0).astype(jnp.bfloat16)
-        for place in range(group - 1):
-            for part in range(2):
-                outs[place][part * rows : (part + 1) * rows, :] = refs[place * 3 + part][...]
+        giving = []
+        for place in others:
+            taking[place].wait()
             for block in range(rows // HD):
-                taken = refs[place * 3 + 2][block * HD : (block + 1) * HD, :]
-                lower = 2 * rows + block * HD
-                outs[place][lower : lower + HD, :] = jnp.transpose(taken)
+                span = slice(block * HD, (block + 1) * HD)
+                turned[place, span, :] = jnp.transpose(taken[place, span, :])
             if docs is not None:
-                outs[place][3 * rows :, :] = mine
-
-    def piece(distance):
-        return pl.BlockSpec((rows, HD), lambda step, ctx: (half, ctx[0] ^ distance))
-
-    in_specs = []
-    operands = []
-    for distance in range(1, group):
-        for array in (queries, keys, values):
-            in_specs.append(piece(distance))
-            operands.append(array)
-    if docs is not None:
-        in_specs.append(whole(docs.shape))
-        operands.append(docs)
+                turned[place, rows:, :] = mine
+            target = outs[place].at[pl.ds(2 * rows, rows + doc_rows), :]
+            giving.append(
+                pltpu.make_async_copy(turned.at[place], target, turned_sem.at[place])
+            )
+            giving[-1].start()
+        for copy in (*direct, *giving):
+            copy.wait()
+
+    anywhere = pl.BlockSpec(memory_space=pl.ANY)
     return pl.pallas_call(
         kernel,
         grid_spec=pltpu.PrefetchScalarGridSpec(
             num_scalar_prefetch=1,
             grid=(1,),
-            in_specs=in_specs,
-            out_specs=[whole((total, HD))] * (group - 1),
+            in_specs=[anywhere] * 3 + ([] if docs is None else [whole(docs.shape)]),
+            out_specs=[anywhere] * (group - 1),
+            scratch_shapes=[
+                pltpu.VMEM((group - 1, rows, HD), jnp.bfloat16),
+                pltpu.VMEM((group - 1, rows + doc_rows, HD), jnp.bfloat16),
+                pltpu.SemaphoreType.DMA((group - 1,)),
+                pltpu.SemaphoreType.DMA((group - 1, 2)),
+                pltpu.SemaphoreType.DMA((group - 1,)),
+            ],
         ),
         out_shape=[jax.ShapeDtypeStruct((total, HD), jnp.bfloat16)] * (group - 1),
         compiler_params=params(56),
         cost_estimate=SMALL,
         name="pack",
-    )(ctx_index, *operands)
+    )(ctx_index, queries, keys, values, *(() if docs is None else (docs,)))
 
 
 def pack_projection(places, w_mine, w_sibling):

time: 119 us -> 157 us (1.32)
  Pallas kernels: 31.4 us -> 75.8 us
  waiting for transfers between devices: 58.6 us -> 50.5 us
    pallas_call x2, Pallas kernels: 5.03 us -> 50.8 us  [pack(): pl.pallas_call(kernel, grid_spec=pltpu.PrefetchScalarGridSpec(num_scalar_...]
    ppermute x23, waiting for transfers between devices: 58.6 us -> 50.5 us  [swap(): lax.ppermute(value, axis, [(source, source ^ distance) for source in rang...]
  transfers between devices with their start and end apart: 23 -> 23, of which waited for: 15 -> 13; matrix products, arithmetic and copies ran while one was open for 1% -> 0% of each run, Pallas kernels for 25% -> 47%
where the time goes in v21:
time: 157 us; the launch traced here: 156 us
  Pallas kernels  75.8 us (48%)
  waiting for transfers between devices  50.5 us (32%)
  starting transfers between devices  28.8 us (18%)
    pallas_call x2, Pallas kernels, pack(): pl.pallas_call(kernel, grid_spec=pltpu.PrefetchScalarGridSpec(num_scalar_...  50.8 us
    ppermute x23, waiting for transfers between devices, swap(): lax.ppermute(value, axis, [(source, source ^ distance) for source in rang...  50.5 us
    ppermute x23, starting transfers between devices, swap(): lax.ppermute(value, axis, [(source, source ^ distance) for source in rang...  28.8 us
    pallas_call x2, Pallas kernels, attend(): pl.pallas_call(kernel, grid_spec=pltpu.PrefetchScalarGridSpec(num_scalar_...  11.5 us
    pallas_call x1, Pallas kernels, pack_projection(): pl.pallas_call(kernel, grid_spec=pltpu.PrefetchScalarGridSpec(num_scalar_...  5.7 us
    pallas_call x8, Pallas kernels, project(): pl.pallas_call(kernel, grid=(1,), in_specs=[plain(part.shape) for part in...  5.69 us
  transfers between devices with their start and end apart: 23, of which 13 were waited for; matrix products, arithmetic and copies ran while one was open for 0% of the time, Pallas kernels for 47%

profile of v21, /device:TPU:0, one launch (start us, length us, event | category | flops | bytes accessed | tf_op | source)
XLA Modules:
  0.0 156.1 jit_solution(8238005117131405735)
XLA Ops:
  0.0 0.5 collective-permute-start.3
  0.5 25.7 %pack.2 = (bf16[1552,128]{1,0:T(8,128)(2,1)}, bf16[1552,128]{1,0:T(8,128)(2,1)}, bf16[1552,128]{1,0:T(8,128)(2,1)}) custom-call(s32[1]{0:T(128)} %bitcast.ctx_ref, bf16[1024,512]{1,0:T(8,128)(2,1)} %refs_3_.1, bf16[1024,512]{1,0:T(8,128)(2,1)} %refs_4_.1, bf16[1024,512]{1,0:T(8,128)(2,1)} %refs_5_.1, s32[8,128]{1,0:T(8,128)} %bitcast.2), custom_call_target="tpu_custom_call" | custom-call | flops 1024 | bytes 1024 | tf_op jit(solution)/shard_map/pack/pallas_call | solution.py:215
  26.2 2.6 %collective-permute-start = (bf16[1552,128]{1,0:T(8,128)(2,1)}, bf16[1552,128]{1,0:T(8,128)(2,1)S(1)}, u32[]{:S(2)}, u32[]{:S(2)}) collective-permute-start(bf16[1552,128]{1,0:T(8,128)(2,1)} %get-tuple-element.59), channel_id=1, source_target_pairs={{0,8},{8,0},{16,24},{24,16},{1,9},{9,1},{17,25},{25,17},{2,10},{10... | collective-permute-start | bytes 1191944 | tf_op jit(solution)/shard_map/ppermute | solution.py:567
  28.7 1.5 collective-permute-start.1
  30.3 0.0 collective-permute-start.2
  30.3 25.0 %pack.3 = (bf16[1536,128]{1,0:T(8,128)(2,1)}, bf16[1536,128]{1,0:T(8,128)(2,1)}, bf16[1536,128]{1,0:T(8,128)(2,1)}) custom-call(s32[1]{0:T(128)} %bitcast.ctx_ref, bf16[1024,512]{1,0:T(8,128)(2,1)} %refs_3_.1, bf16[1024,512]{1,0:T(8,128)(2,1)} %refs_4_.1, bf16[1024,512]{1,0:T(8,128)(2,1)} %refs_5_.1), custom_call_target="tpu_custom_call" | custom-call | flops 1024 | bytes 1024 | tf_op jit(solution)/shard_map/pack/pallas_call | solution.py:215
  55.3 2.0 %collective-permute-start.7 = (bf16[1536,128]{1,0:T(8,128)(2,1)}, bf16[1536,128]{1,0:T(8,128)(2,1)S(1)}, u32[]{:S(2)}, u32[]{:S(2)}) collective-permute-start(bf16[1536,128]{1,0:T(8,128)(2,1)} %get-tuple-element.78), channel_id=1, source_target_pairs={{0,8},{8,0},{16,24},{24,16},{1,9},{9,1},{17,25},{25,17},{2,10},{10... | collective-permute-start | bytes 1179656 | tf_op jit(solution)/shard_map/ppermute | solution.py:567
  57.3 0.0 collective-permute-done.3.sibling_in
  57.3 1.5 collective-permute-start.8
  58.9 0.5 broadcast_xor_fusion.places_ref
  59.4 5.7 %pack_projection.1 = (bf16[512,2048]{1,0:T(8,128)(2,1)}, bf16[512,2048]{1,0:T(8,128)(2,1)}) custom-call(s32[4]{0:T(128)} %broadcast_xor_fusion.places_ref, bf16[512,4096]{1,0:T(8,128)(2,1)} %mine_in.1, bf16[512,4096]{1,0:T(8,128)(2,1)} %collective-permute-done.3.sibling_in), custom_call_target="tpu_custom_call" | custom-call | flops 1024 | bytes 1024 | tf_op jit(solution)/shard_map/pack_projection/pallas_call | solution.py:248
  65.1 0.0 collective-permute-done.refs_4_.refs_7_
  65.1 0.0 collective-permute-done.1.refs_5_.refs_8_
  65.1 0.0 collective-permute-done.2.refs_6_.refs_9_
  65.2 4.7 %attend_low.1 = (bf16[512,128]{1,0:T(8,128)(2,1)S(1)}, bf16[512,128]{1,0:T(8,128)(2,1)S(1)}, bf16[512,128]{1,0:T(8,128)(2,1)S(1)}, bf16[512,128]{1,0:T(8,128)(2,1)S(1)}) custom-call(s32[1]{0:T(128)} %bitcast.ctx_ref, bf16[1024,512]{1,0:T(8,128)(2,1)S(1)} %copy-done.2, bf16[1024,512]{1,0:T(8,128)(2,1)S(1)} %copy-done.3, bf16[1024,512]{1,0:T(8,128)(2,1)S(1)} %copy-done.4, ...), custom_call_target="tpu_custom_call" | custom-call | flops 1024 | bytes 1024 | tf_op jit(solution)/shard_map/attend_low/pallas_call | solution.py:430
  69.9 0.6 collective-permute-start.4
  70.5 0.1 collective-permute-start.5
  70.6 2.9 %collective-permute-start.6 = (bf16[512,128]{1,0:T(8,128)(2,1)S(1)}, bf16[512,128]{1,0:T(8,128)(2,1)S(1)}, u32[]{:S(2)}, u32[]{:S(2)}) collective-permute-start(bf16[512,128]{1,0:T(8,128)(2,1)S(1)} %get-tuple-element.77), channel_id=1, source_target_pairs={{0,24},{8,16},{16,8},{24,0},{1,25},{9,17},{17,9},{25,1},{2,26},{10... | collective-permute-start | bytes 393224 | tf_op jit(solution)/shard_map/ppermute | solution.py:567
  73.5 0.0 collective-permute-done.7.refs_10_
  73.5 0.0 collective-permute-done.8.refs_11_
  73.5 2.4 %collective-permute-done.4.refs_1_ = bf16[512,128]{1,0:T(8,128)(2,1)S(1)} collective-permute-done((bf16[512,128]{1,0:T(8,128)(2,1)S(1)}, bf16[512,128]{1,0:T(8,128)(2,1)S(1)}, u32[]{:S(2)}, u32[]{:S(2)}) %collective-permute-start.4) | collective-permute-done | bytes 131104 | tf_op jit(solution)/shard_map/ppermute | solution.py:567
  75.9 1.6 %collective-permute-done.5.refs_2_ = bf16[512,128]{1,0:T(8,128)(2,1)S(1)} collective-permute-done((bf16[512,128]{1,0:T(8,128)(2,1)S(1)}, bf16[512,128]{1,0:T(8,128)(2,1)S(1)}, u32[]{:S(2)}, u32[]{:S(2)}) %collective-permute-start.5) | collective-permute-done | bytes 131104 | tf_op jit(solution)/shard_map/ppermute | solution.py:567
  77.5 0.1 assemble.2.refs_0_
  77.6 0.1 collective-permute-start.10
  77.7 1.9 %collective-permute-done.10.refs_1_ = bf16[512,512]{1,0:T(8,128)(2,1)S(1)} collective-permute-done((bf16[512,512]{1,0:T(8,128)(2,1)S(1)}, bf16[512,512]{1,0:T(8,128)(2,1)S(1)}, u32[]{:S(2)}, u32[]{:S(2)}) %collective-permute-start.10) | collective-permute-done | bytes 524320 | tf_op jit(solution)/shard_map/ppermute | solution.py:567
  79.6 0.7 project.8
  80.3 1.7 %collective-permute-start.11 = (bf16[512,512]{1,0:T(8,128)(2,1)S(1)}, bf16[512,512]{1,0:T(8,128)(2,1)S(1)}, u32[]{:S(2)}, u32[]{:S(2)}) collective-permute-start(bf16[512,512]{1,0:T(8,128)(2,1)S(1)} %project.8), channel_id=1, source_target_pairs={{0,2},{1,3},{2,0},{3,1},{4,6},{5,7},{6,4},{7,5},{8,10},{9,11},{10,... | collective-permute-start | bytes 1572872 | tf_op jit(solution)/shard_map/ppermute | solution.py:567
  82.0 2.1 %collective-permute-start.9 = (bf16[1536,128]{1,0:T(8,128)(2,1)S(1)}, bf16[1536,128]{1,0:T(8,128)(2,1)S(1)}, u32[]{:S(2)}, u32[]{:S(2)}) collective-permute-start(bf16[1536,128]{1,0:T(8,128)(2,1)S(1)} %copy-done.6), channel_id=1, source_target_pairs={{0,24},{8,16},{16,8},{24,0},{1,25},{9,17},{17,9},{25,1},{2,26},{10... | collective-permute-start | bytes 1179656 | tf_op jit(solution)/shard_map/ppermute | solution.py:567
  84.2 0.7 project.9
  84.9 0.5 collective-permute-start.17
  85.4 0.7 project.10
  86.1 0.7 project.11.refs_0_
  86.8 8.3 %collective-permute-done.11 = bf16[512,512]{1,0:T(8,128)(2,1)S(1)} collective-permute-done((bf16[512,512]{1,0:T(8,128)(2,1)S(1)}, bf16[512,512]{1,0:T(8,128)(2,1)S(1)}, u32[]{:S(2)}, u32[]{:S(2)}) %collective-permute-start.11) | collective-permute-done | bytes 524320 | tf_op jit(solution)/shard_map/ppermute | solution.py:567
  95.2 0.1 add_convert_fusion.1
  95.3 2.7 %collective-permute-start.18 = (bf16[512,512]{1,0:T(8,128)(2,1)S(1)}, bf16[512,512]{1,0:T(8,128)(2,1)S(1)}, u32[]{:S(2)}, u32[]{:S(2)}) collective-permute-start(bf16[512,512]{1,0:T(8,128)(2,1)S(1)} %add_convert_fusion.1), channel_id=1, source_target_pairs={{0,4},{1,5},{2,6},{3,7},{4,0},{5,1},{6,2},{7,3},{8,12},{9,13},{10,... | collective-permute-start | bytes 1572872 | tf_op jit(solution)/shard_map/ppermute | solution.py:567
  98.0 6.8 %attend_high.1 = (bf16[512,128]{1,0:T(8,128)(2,1)S(1)}, bf16[512,128]{1,0:T(8,128)(2,1)S(1)}, bf16[512,128]{1,0:T(8,128)(2,1)S(1)}, bf16[512,128]{1,0:T(8,128)(2,1)S(1)}) custom-call(s32[1]{0:T(128)} %bitcast.ctx_ref, bf16[1024,512]{1,0:T(8,128)(2,1)S(1)} %copy-done.2, bf16[1024,512]{1,0:T(8,128)(2,1)S(1)} %copy-done.3, bf16[1024,512]{1,0:T(8,128)(2,1)S(1)} %copy-done.4, ...), custom_call_target="tpu_custom_call" | custom-call | flops 1024 | bytes 1024 | tf_op jit(solution)/shard_map/attend_high/pallas_call | solution.py:430
  104.8 1.7 %collective-permute-start.12 = (bf16[512,128]{1,0:T(8,128)(2,1)S(1)}, bf16[512,128]{1,0:T(8,128)(2,1)S(1)}, u32[]{:S(2)}, u32[]{:S(2)}) collective-permute-start(bf16[512,128]{1,0:T(8,128)(2,1)S(1)} %get-tuple-element.93), channel_id=1, source_target_pairs={{0,8},{8,0},{16,24},{24,16},{1,9},{9,1},{17,25},{25,17},{2,10},{10... | collective-permute-start | bytes 393224 | tf_op jit(solution)/shard_map/ppermute | solution.py:567
  106.5 1.0 collective-permute-start.13
  107.6 0.8 collective-permute-start.14
  108.4 2.7 %collective-permute-done.12.refs_1_ = bf16[512,128]{1,0:T(8,128)(2,1)S(1)} collective-permute-done((bf16[512,128]{1,0:T(8,128)(2,1)S(1)}, bf16[512,128]{1,0:T(8,128)(2,1)S(1)}, u32[]{:S(2)}, u32[]{:S(2)}) %collective-permute-start.12) | collective-permute-done | bytes 131104 | tf_op jit(solution)/shard_map/ppermute | solution.py:567
  111.1 1.0 collective-permute-done.13.refs_2_
  112.1 1.4 collective-permute-done.14.refs_3_
  113.5 0.1 assemble.3
  113.6 0.1 collective-permute-start.15
  113.7 0.5 collective-permute-start.16
  114.2 1.0 collective-permute-done.15.refs_2_
  115.2 0.4 collective-permute-done.16.refs_3_
  115.6 0.7 project.15
  116.3 0.0 collective-permute-done.17.refs_1_
  116.3 3.6 %collective-permute-done.18.refs_2_ = bf16[512,512]{1,0:T(8,128)(2,1)S(1)} collective-permute-done((bf16[512,512]{1,0:T(8,128)(2,1)S(1)}, bf16[512,512]{1,0:T(8,128)(2,1)S(1)}, u32[]{:S(2)}, u32[]{:S(2)}) %collective-permute-start.18) | collective-permute-done | bytes 524320 | tf_op jit(solution)/shard_map/ppermute | solution.py:567
  119.9 0.8 collective-permute-start.19
  120.8 0.7 project.14
  121.5 9.7 %collective-permute-done.19 = bf16[512,512]{1,0:T(8,128)(2,1)S(1)} collective-permute-done((bf16[512,512]{1,0:T(8,128)(2,1)S(1)}, bf16[512,512]{1,0:T(8,128)(2,1)S(1)}, u32[]{:S(2)}, u32[]{:S(2)}) %collective-permute-start.19) | collective-permute-done | bytes 524320 | tf_op jit(solution)/shard_map/ppermute | solution.py:567
  131.2 0.1 add_convert_fusion
  131.3 3.0 %collective-permute-start.22 = (bf16[512,512]{1,0:T(8,128)(2,1)S(1)}, bf16[512,512]{1,0:T(8,128)(2,1)S(1)}, u32[]{:S(2)}, u32[]{:S(2)}) collective-permute-start(bf16[512,512]{1,0:T(8,128)(2,1)S(1)} %add_convert_fusion), channel_id=1, source_target_pairs={{0,4},{1,5},{2,6},{3,7},{4,0},{5,1},{6,2},{7,3},{8,12},{9,13},{10,... | collective-permute-start | bytes 1572872 | tf_op jit(solution)/shard_map/ppermute | solution.py:567
  134.3 0.7 project.13
  135.0 1.6 %collective-permute-start.20 = (bf16[256,512]{1,0:T(8,128)(2,1)S(1)}, bf16[256,512]{1,0:T(8,128)(2,1)S(1)}, u32[]{:S(2)}, u32[]{:S(2)}) collective-permute-start(bf16[256,512]{1,0:T(8,128)(2,1)S(1)} %get-tuple-element.102), channel_id=1, source_target_pairs={{0,2},{1,3},{2,0},{3,1},{4,6},{5,7},{6,4},{7,5},{8,10},{9,11},{10,... | collective-permute-start | bytes 786440 | tf_op jit(solution)/shard_map/ppermute | solution.py:567
  136.6 0.5 collective-permute-start.21
  137.1 0.7 project.12.refs_0_
  137.8 1.0 finish.2.refs_4_
  138.8 12.0 %collective-permute-done.20.refs_1_ = bf16[256,512]{1,0:T(8,128)(2,1)S(1)} collective-permute-done((bf16[256,512]{1,0:T(8,128)(2,1)S(1)}, bf16[256,512]{1,0:T(8,128)(2,1)S(1)}, u32[]{:S(2)}, u32[]{:S(2)}) %collective-permute-start.20) | collective-permute-done | bytes 262176 | tf_op jit(solution)/shard_map/ppermute | solution.py:567
  150.8 4.3 %collective-permute-done.21.refs_2_ = bf16[256,512]{1,0:T(8,128)(2,1)S(1)} collective-permute-done((bf16[256,512]{1,0:T(8,128)(2,1)S(1)}, bf16[256,512]{1,0:T(8,128)(2,1)S(1)}, u32[]{:S(2)}, u32[]{:S(2)}) %collective-permute-start.21) | collective-permute-done | bytes 262176 | tf_op jit(solution)/shard_map/ppermute | solution.py:567
  155.1 0.0 collective-permute-done.22.refs_3_
  155.1 1.0 finish.3
  (18 shorter events, 0.0 us)
Async XLA Ops:
  0.0 58.9 %copy-start.7 = (s32[4]{0:T(128)S(1)}, s32[4]{0:T(128)}, u32[]{:S(2)}) copy-start(s32[4]{0:T(128)} %constant.13) | copy-start | bytes 52
  0.0 57.3 %collective-permute-start.3 = (bf16[512,4096]{1,0:T(8,128)(2,1)}, bf16[512,4096]{1,0:T(8,128)(2,1)}, u32[]{:S(2)}, u32[]{:S(2)}) collective-permute-start(bf16[512,4096]{1,0:T(8,128)(2,1)} %mine_in.1), channel_id=1, source_target_pairs={{0,1},{1,0},{2,3},{3,2},{4,5},{5,4},{6,7},{7,6},{8,9},{9,8},{10,11... | collective-permute-start | bytes 12582920 | tf_op jit(solution)/shard_map/ppermute | solution.py:567
  26.2 38.9 %collective-permute-start = (bf16[1552,128]{1,0:T(8,128)(2,1)}, bf16[1552,128]{1,0:T(8,128)(2,1)S(1)}, u32[]{:S(2)}, u32[]{:S(2)}) collective-permute-start(bf16[1552,128]{1,0:T(8,128)(2,1)} %get-tuple-element.59), channel_id=1, source_target_pairs={{0,8},{8,0},{16,24},{24,16},{1,9},{9,1},{17,25},{25,17},{2,10},{10... | collective-permute-start | bytes 1191944 | tf_op jit(solution)/shard_map/ppermute | solution.py:567
  28.7 36.4 %collective-permute-start.1 = (bf16[1552,128]{1,0:T(8,128)(2,1)}, bf16[1552,128]{1,0:T(8,128)(2,1)S(1)}, u32[]{:S(2)}, u32[]{:S(2)}) collective-permute-start(bf16[1552,128]{1,0:T(8,128)(2,1)} %get-tuple-element.60), channel_id=1, source_target_pairs={{0,16},{8,24},{16,0},{24,8},{1,17},{9,25},{17,1},{25,9},{2,18},{10... | collective-permute-start | bytes 1191944 | tf_op jit(solution)/shard_map/ppermute | solution.py:567
  30.3 34.9 %collective-permute-start.2 = (bf16[1552,128]{1,0:T(8,128)(2,1)}, bf16[1552,128]{1,0:T(8,128)(2,1)S(1)}, u32[]{:S(2)}, u32[]{:S(2)}) collective-permute-start(bf16[1552,128]{1,0:T(8,128)(2,1)} %get-tuple-element.61), channel_id=1, source_target_pairs={{0,24},{8,16},{16,8},{24,0},{1,25},{9,17},{17,9},{25,1},{2,26},{10... | collective-permute-start | bytes 1191944 | tf_op jit(solution)/shard_map/ppermute | solution.py:567
  55.3 18.1 %collective-permute-start.7 = (bf16[1536,128]{1,0:T(8,128)(2,1)}, bf16[1536,128]{1,0:T(8,128)(2,1)S(1)}, u32[]{:S(2)}, u32[]{:S(2)}) collective-permute-start(bf16[1536,128]{1,0:T(8,128)(2,1)} %get-tuple-element.78), channel_id=1, source_target_pairs={{0,8},{8,0},{16,24},{24,16},{1,9},{9,1},{17,25},{25,17},{2,10},{10... | collective-permute-start | bytes 1179656 | tf_op jit(solution)/shard_map/ppermute | solution.py:567
  57.3 16.1 %collective-permute-start.8 = (bf16[1536,128]{1,0:T(8,128)(2,1)}, bf16[1536,128]{1,0:T(8,128)(2,1)S(1)}, u32[]{:S(2)}, u32[]{:S(2)}) collective-permute-start(bf16[1536,128]{1,0:T(8,128)(2,1)} %get-tuple-element.79), channel_id=1, source_target_pairs={{0,16},{8,24},{16,0},{24,8},{1,17},{9,25},{17,1},{25,9},{2,18},{10... | collective-permute-start | bytes 1179656 | tf_op jit(solution)/shard_map/ppermute | solution.py:567
  59.4 5.7 %copy-start.2 = (bf16[1024,512]{1,0:T(8,128)(2,1)S(1)}, bf16[1024,512]{1,0:T(8,128)(2,1)}, u32[]{:S(2)}) copy-start(bf16[1024,512]{1,0:T(8,128)(2,1)} %refs_3_.1) | copy-start | bytes 3145732
  59.4 5.8 %copy-start.3 = (bf16[1024,512]{1,0:T(8,128)(2,1)S(1)}, bf16[1024,512]{1,0:T(8,128)(2,1)}, u32[]{:S(2)}) copy-start(bf16[1024,512]{1,0:T(8,128)(2,1)} %refs_4_.1) | copy-start | bytes 3145732
  59.4 5.8 %copy-start.4 = (bf16[1024,512]{1,0:T(8,128)(2,1)S(1)}, bf16[1024,512]{1,0:T(8,128)(2,1)}, u32[]{:S(2)}) copy-start(bf16[1024,512]{1,0:T(8,128)(2,1)} %refs_5_.1) | copy-start | bytes 3145732
  59.4 5.8 %copy-start.5 = (s32[1024]{0:T(1024)S(1)}, s32[1024]{0:T(1024)}, u32[]{:S(2)}) copy-start(s32[1024]{0:T(1024)} %param.9) | copy-start | bytes 12292
  65.1 14.5 %copy-start = (bf16[512,2048]{1,0:T(8,128)(2,1)S(1)}, bf16[512,2048]{1,0:T(8,128)(2,1)}, u32[]{:S(2)}) copy-start(bf16[512,2048]{1,0:T(8,128)(2,1)} %get-tuple-element.87.refs_2_.refs_4_) | copy-start | bytes 6291460
  65.1 14.5 %copy-start.1 = (bf16[512,2048]{1,0:T(8,128)(2,1)S(1)}, bf16[512,2048]{1,0:T(8,128)(2,1)}, u32[]{:S(2)}) copy-start(bf16[512,2048]{1,0:T(8,128)(2,1)} %get-tuple-element.88.refs_3_.refs_5_) | copy-start | bytes 6291460
  69.9 12.1 %copy-start.6 = (bf16[1536,128]{1,0:T(8,128)(2,1)S(1)}, bf16[1536,128]{1,0:T(8,128)(2,1)}, u32[]{:S(2)}) copy-start(bf16[1536,128]{1,0:T(8,128)(2,1)} %get-tuple-element.82) | copy-start | bytes 1179652
  69.9 6.0 %collective-permute-start.4 = (bf16[512,128]{1,0:T(8,128)(2,1)S(1)}, bf16[512,128]{1,0:T(8,128)(2,1)S(1)}, u32[]{:S(2)}, u32[]{:S(2)}) collective-permute-start(bf16[512,128]{1,0:T(8,128)(2,1)S(1)} %get-tuple-element.75), channel_id=1, source_target_pairs={{0,8},{8,0},{16,24},{24,16},{1,9},{9,1},{17,25},{25,17},{2,10},{10... | collective-permute-start | bytes 393224 | tf_op jit(solution)/shard_map/ppermute | solution.py:567
  70.5 7.0 %collective-permute-start.5 = (bf16[512,128]{1,0:T(8,128)(2,1)S(1)}, bf16[512,128]{1,0:T(8,128)(2,1)S(1)}, u32[]{:S(2)}, u32[]{:S(2)}) collective-permute-start(bf16[512,128]{1,0:T(8,128)(2,1)S(1)} %get-tuple-element.76), channel_id=1, source_target_pairs={{0,16},{8,24},{16,0},{24,8},{1,17},{9,25},{17,1},{25,9},{2,18},{10... | collective-permute-start | bytes 393224 | tf_op jit(solution)/shard_map/ppermute | solution.py:567
  70.6 7.0 %collective-permute-start.6 = (bf16[512,128]{1,0:T(8,128)(2,1)S(1)}, bf16[512,128]{1,0:T(8,128)(2,1)S(1)}, u32[]{:S(2)}, u32[]{:S(2)}) collective-permute-start(bf16[512,128]{1,0:T(8,128)(2,1)S(1)} %get-tuple-element.77), channel_id=1, source_target_pairs={{0,24},{8,16},{16,8},{24,0},{1,25},{9,17},{17,9},{25,1},{2,26},{10... | collective-permute-start | bytes 393224 | tf_op jit(solution)/shard_map/ppermute | solution.py:567
  77.6 2.0 %collective-permute-start.10 = (bf16[512,512]{1,0:T(8,128)(2,1)S(1)}, bf16[512,512]{1,0:T(8,128)(2,1)S(1)}, u32[]{:S(2)}, u32[]{:S(2)}) collective-permute-start(bf16[512,512]{1,0:T(8,128)(2,1)S(1)} %assemble.2.refs_0_), channel_id=1, source_target_pairs={{0,1},{1,0},{2,3},{3,2},{4,5},{5,4},{6,7},{7,6},{8,9},{9,8},{10,11... | collective-permute-start | bytes 1572872 | tf_op jit(solution)/shard_map/ppermute | solution.py:567
  80.3 14.8 %collective-permute-start.11 = (bf16[512,512]{1,0:T(8,128)(2,1)S(1)}, bf16[512,512]{1,0:T(8,128)(2,1)S(1)}, u32[]{:S(2)}, u32[]{:S(2)}) collective-permute-start(bf16[512,512]{1,0:T(8,128)(2,1)S(1)} %project.8), channel_id=1, source_target_pairs={{0,2},{1,3},{2,0},{3,1},{4,6},{5,7},{6,4},{7,5},{8,10},{9,11},{10,... | collective-permute-start | bytes 1572872 | tf_op jit(solution)/shard_map/ppermute | solution.py:567
  82.0 13.3 %collective-permute-start.9 = (bf16[1536,128]{1,0:T(8,128)(2,1)S(1)}, bf16[1536,128]{1,0:T(8,128)(2,1)S(1)}, u32[]{:S(2)}, u32[]{:S(2)}) collective-permute-start(bf16[1536,128]{1,0:T(8,128)(2,1)S(1)} %copy-done.6), channel_id=1, source_target_pairs={{0,24},{8,16},{16,8},{24,0},{1,25},{9,17},{17,9},{25,1},{2,26},{10... | collective-permute-start | bytes 1179656 | tf_op jit(solution)/shard_map/ppermute | solution.py:567
  84.9 31.4 %collective-permute-start.17 = (bf16[512,512]{1,0:T(8,128)(2,1)S(1)}, bf16[512,512]{1,0:T(8,128)(2,1)S(1)}, u32[]{:S(2)}, u32[]{:S(2)}) collective-permute-start(bf16[512,512]{1,0:T(8,128)(2,1)S(1)} %project.9), channel_id=1, source_target_pairs={{0,2},{1,3},{2,0},{3,1},{4,6},{5,7},{6,4},{7,5},{8,10},{9,11},{10,... | collective-permute-start | bytes 1572872 | tf_op jit(solution)/shard_map/ppermute | solution.py:567
  95.3 24.6 %collective-permute-start.18 = (bf16[512,512]{1,0:T(8,128)(2,1)S(1)}, bf16[512,512]{1,0:T(8,128)(2,1)S(1)}, u32[]{:S(2)}, u32[]{:S(2)}) collective-permute-start(bf16[512,512]{1,0:T(8,128)(2,1)S(1)} %add_convert_fusion.1), channel_id=1, source_target_pairs={{0,4},{1,5},{2,6},{3,7},{4,0},{5,1},{6,2},{7,3},{8,12},{9,13},{10,... | collective-permute-start | bytes 1572872 | tf_op jit(solution)/shard_map/ppermute | solution.py:567
  104.8 6.2 %collective-permute-start.12 = (bf16[512,128]{1,0:T(8,128)(2,1)S(1)}, bf16[512,128]{1,0:T(8,128)(2,1)S(1)}, u32[]{:S(2)}, u32[]{:S(2)}) collective-permute-start(bf16[512,128]{1,0:T(8,128)(2,1)S(1)} %get-tuple-element.93), channel_id=1, source_target_pairs={{0,8},{8,0},{16,24},{24,16},{1,9},{9,1},{17,25},{25,17},{2,10},{10... | collective-permute-start | bytes 393224 | tf_op jit(solution)/shard_map/ppermute | solution.py:567
  106.5 5.6 %collective-permute-start.13 = (bf16[512,128]{1,0:T(8,128)(2,1)S(1)}, bf16[512,128]{1,0:T(8,128)(2,1)S(1)}, u32[]{:S(2)}, u32[]{:S(2)}) collective-permute-start(bf16[512,128]{1,0:T(8,128)(2,1)S(1)} %get-tuple-element.94), channel_id=1, source_target_pairs={{0,16},{8,24},{16,0},{24,8},{1,17},{9,25},{17,1},{25,9},{2,18},{10... | collective-permute-start | bytes 393224 | tf_op jit(solution)/shard_map/ppermute | solution.py:567
  107.6 5.9 %collective-permute-start.14 = (bf16[512,128]{1,0:T(8,128)(2,1)S(1)}, bf16[512,128]{1,0:T(8,128)(2,1)S(1)}, u32[]{:S(2)}, u32[]{:S(2)}) collective-permute-start(bf16[512,128]{1,0:T(8,128)(2,1)S(1)} %get-tuple-element.95), channel_id=1, source_target_pairs={{0,24},{8,16},{16,8},{24,0},{1,25},{9,17},{17,9},{25,1},{2,26},{10... | collective-permute-start | bytes 393224 | tf_op jit(solution)/shard_map/ppermute | solution.py:567
  113.6 1.6 %collective-permute-start.15 = (bf16[256,512]{1,0:T(8,128)(2,1)S(1)}, bf16[256,512]{1,0:T(8,128)(2,1)S(1)}, u32[]{:S(2)}, u32[]{:S(2)}) collective-permute-start(bf16[256,512]{1,0:T(8,128)(2,1)S(1)} %get-tuple-element.96.refs_0_), channel_id=1, source_target_pairs={{0,1},{1,0},{2,3},{3,2},{4,5},{5,4},{6,7},{7,6},{8,9},{9,8},{10,11... | collective-permute-start | bytes 786440 | tf_op jit(solution)/shard_map/ppermute | solution.py:567
  113.7 1.9 %collective-permute-start.16 = (bf16[256,512]{1,0:T(8,128)(2,1)S(1)}, bf16[256,512]{1,0:T(8,128)(2,1)S(1)}, u32[]{:S(2)}, u32[]{:S(2)}) collective-permute-start(bf16[256,512]{1,0:T(8,128)(2,1)S(1)} %get-tuple-element.97.refs_1_), channel_id=1, source_target_pairs={{0,1},{1,0},{2,3},{3,2},{4,5},{5,4},{6,7},{7,6},{8,9},{9,8},{10,11... | collective-permute-start | bytes 786440 | tf_op jit(solution)/shard_map/ppermute | solution.py:567
  119.9 11.2 %collective-permute-start.19 = (bf16[512,512]{1,0:T(8,128)(2,1)S(1)}, bf16[512,512]{1,0:T(8,128)(2,1)S(1)}, u32[]{:S(2)}, u32[]{:S(2)}) collective-permute-start(bf16[512,512]{1,0:T(8,128)(2,1)S(1)} %project.15), channel_id=1, source_target_pairs={{0,2},{1,3},{2,0},{3,1},{4,6},{5,7},{6,4},{7,5},{8,10},{9,11},{10,... | collective-permute-start | bytes 1572872 | tf_op jit(solution)/shard_map/ppermute | solution.py:567
  131.3 23.8 %collective-permute-start.22 = (bf16[512,512]{1,0:T(8,128)(2,1)S(1)}, bf16[512,512]{1,0:T(8,128)(2,1)S(1)}, u32[]{:S(2)}, u32[]{:S(2)}) collective-permute-start(bf16[512,512]{1,0:T(8,128)(2,1)S(1)} %add_convert_fusion), channel_id=1, source_target_pairs={{0,4},{1,5},{2,6},{3,7},{4,0},{5,1},{6,2},{7,3},{8,12},{9,13},{10,... | collective-permute-start | bytes 1572872 | tf_op jit(solution)/shard_map/ppermute | solution.py:567
  135.0 15.8 %collective-permute-start.20 = (bf16[256,512]{1,0:T(8,128)(2,1)S(1)}, bf16[256,512]{1,0:T(8,128)(2,1)S(1)}, u32[]{:S(2)}, u32[]{:S(2)}) collective-permute-start(bf16[256,512]{1,0:T(8,128)(2,1)S(1)} %get-tuple-element.102), channel_id=1, source_target_pairs={{0,2},{1,3},{2,0},{3,1},{4,6},{5,7},{6,4},{7,5},{8,10},{9,11},{10,... | collective-permute-start | bytes 786440 | tf_op jit(solution)/shard_map/ppermute | solution.py:567
  136.6 18.5 %collective-permute-start.21 = (bf16[256,512]{1,0:T(8,128)(2,1)S(1)}, bf16[256,512]{1,0:T(8,128)(2,1)S(1)}, u32[]{:S(2)}, u32[]{:S(2)}) collective-permute-start(bf16[256,512]{1,0:T(8,128)(2,1)S(1)} %get-tuple-element.103), channel_id=1, source_target_pairs={{0,2},{1,3},{2,0},{3,1},{4,6},{5,7},{6,4},{7,5},{8,10},{9,11},{10,... | collective-permute-start | bytes 786440 | tf_op jit(solution)/shard_map/ppermute | solution.py:567

commit v22 on v20

--- a/solution.py
+++ b/solution.py
@@ -602,15 +602,17 @@
     near_sum = to_next(shares[1], 1)
     passed = add(shares[2], far)
 
-    high, shares, passed = tie(high, shares, passed)
-    across = to_next(passed, 2)
+    high, shares = tie(high, shares)
     pieces = attend(ctx_index, queries, keys, values, docs, low, high)
     back = send_back(pieces)
+    pieces, passed = tie(pieces, passed)
+    across = to_next(passed, 2)
+    back, near_sum = tie(back, near_sum)
     mine = assemble(ctx_index, [pieces[0], *back], cuts)
     sibling = [swap(part, "head", 1) for part in mine]
     halves = list(zip(cuts[:-1], cuts[1:]))
     late = projected(mine, sibling, *[[(0, *span)] for span in halves])
-    late, near_sum, across = tie(late, near_sum, across)
+    late[1], across = tie(late[1], across)
     result = finish(0, rows, [[(shares[3], 0)], [(near_sum, 0)], [(across, 0)]], None)
     far = [to_next(part, 1) for part in late]
     late = projected(mine, sibling, *[[(2, *span)] for span in halves])

time: 119 us -> 122 us (1.025)
  waiting for transfers between devices: 52.5 us -> 62.8 us
  starting transfers between devices: 32.8 us -> 28.3 us
  Pallas kernels: 32.7 us -> 30.8 us
    ppermute x26, waiting for transfers between devices: 52.5 us -> 62.8 us  [swap(): lax.ppermute(value, axis, [(source, source ^ distance) for source in rang...]
    ppermute x26, starting transfers between devices: 32.8 us -> 28.3 us  [swap(): lax.ppermute(value, axis, [(source, source ^ distance) for source in rang...]
    pallas_call x2, Pallas kernels: 14.1 us -> 12.1 us  [attend(): pl.pallas_call(kernel, grid_spec=pltpu.PrefetchScalarGridSpec(num_scalar_...]
  transfers between devices with their start and end apart: 26 -> 26, of which waited for: 14 -> 13; matrix products, arithmetic and copies ran while one was open for 1% -> 1% of each run, Pallas kernels for 26% -> 24%
where the time goes in v22:
time: 122 us; the launch traced here: 123 us
  waiting for transfers between devices  62.8 us (51%)
  Pallas kernels  30.8 us (25%)
  starting transfers between devices  28.3 us (23%)
    ppermute x26, waiting for transfers between devices, swap(): lax.ppermute(value, axis, [(source, source ^ distance) for source in rang...  62.8 us
    ppermute x26, starting transfers between devices, swap(): lax.ppermute(value, axis, [(source, source ^ distance) for source in rang...  28.3 us
    pallas_call x2, Pallas kernels, attend(): pl.pallas_call(kernel, grid_spec=pltpu.PrefetchScalarGridSpec(num_scalar_...  12.1 us
    pallas_call x1, Pallas kernels, pack_projection(): pl.pallas_call(kernel, grid_spec=pltpu.PrefetchScalarGridSpec(num_scalar_...  5.74 us
    pallas_call x8, Pallas kernels, project(): pl.pallas_call(kernel, grid=(1,), in_specs=[plain(part.shape) for part in...  5.72 us
    pallas_call x2, Pallas kernels, pack(): pl.pallas_call(kernel, grid_spec=pltpu.PrefetchScalarGridSpec(num_scalar_...  5.02 us
  transfers between devices with their start and end apart: 26, of which 13 were waited for; matrix products, arithmetic and copies ran while one was open for 1% of the time, Pallas kernels for 24%

profile of v22, /device:TPU:0, one launch (start us, length us, event | category | flops | bytes accessed | tf_op | source)
XLA Modules:
  0.0 122.8 jit_solution(9082426119202978992)
XLA Ops:
  0.0 0.5 collective-permute-start.3
  0.5 2.5 %pack.2 = (bf16[1552,128]{1,0:T(8,128)(2,1)}, bf16[1552,128]{1,0:T(8,128)(2,1)}, bf16[1552,128]{1,0:T(8,128)(2,1)}) custom-call(s32[1]{0:T(128)} %bitcast.ctx_ref, bf16[1024,512]{1,0:T(8,128)(2,1)} %refs_3_.4, bf16[1024,512]{1,0:T(8,128)(2,1)} %refs_4_.4, bf16[1024,512]{1,0:T(8,128)(2,1)} %refs_5_.4, bf16[1024,512]{1,0:T(8,128)(2,1)} %refs_3_.4, ...), custom_call_target="tpu_custom_call" | custom-call | flops 1024 | bytes 1024 | tf_op jit(solution)/shard_map/pack/pallas_call | solution.py:201
  2.9 2.5 %collective-permute-start = (bf16[1552,128]{1,0:T(8,128)(2,1)}, bf16[1552,128]{1,0:T(8,128)(2,1)S(1)}, u32[]{:S(2)}, u32[]{:S(2)}) collective-permute-start(bf16[1552,128]{1,0:T(8,128)(2,1)} %get-tuple-element.69), channel_id=1, source_target_pairs={{0,8},{8,0},{16,24},{24,16},{1,9},{9,1},{17,25},{25,17},{2,10},{10... | collective-permute-start | bytes 1191944 | tf_op jit(solution)/shard_map/ppermute | solution.py:546
  5.4 1.5 %collective-permute-start.1 = (bf16[1552,128]{1,0:T(8,128)(2,1)}, bf16[1552,128]{1,0:T(8,128)(2,1)S(1)}, u32[]{:S(2)}, u32[]{:S(2)}) collective-permute-start(bf16[1552,128]{1,0:T(8,128)(2,1)} %get-tuple-element.70), channel_id=1, source_target_pairs={{0,16},{8,24},{16,0},{24,8},{1,17},{9,25},{17,1},{25,9},{2,18},{10... | collective-permute-start | bytes 1191944 | tf_op jit(solution)/shard_map/ppermute | solution.py:546
  7.0 0.0 collective-permute-start.2
  7.0 2.5 %pack.3 = (bf16[1536,128]{1,0:T(8,128)(2,1)}, bf16[1536,128]{1,0:T(8,128)(2,1)}, bf16[1536,128]{1,0:T(8,128)(2,1)}) custom-call(s32[1]{0:T(128)} %bitcast.ctx_ref, bf16[1024,512]{1,0:T(8,128)(2,1)} %refs_3_.4, bf16[1024,512]{1,0:T(8,128)(2,1)} %refs_4_.4, bf16[1024,512]{1,0:T(8,128)(2,1)} %refs_5_.4, bf16[1024,512]{1,0:T(8,128)(2,1)} %refs_3_.4, ...), custom_call_target="tpu_custom_call" | custom-call | flops 1024 | bytes 1024 | tf_op jit(solution)/shard_map/pack/pallas_call | solution.py:201
  9.5 2.0 %collective-permute-start.7 = (bf16[1536,128]{1,0:T(8,128)(2,1)}, bf16[1536,128]{1,0:T(8,128)(2,1)S(1)}, u32[]{:S(2)}, u32[]{:S(2)}) collective-permute-start(bf16[1536,128]{1,0:T(8,128)(2,1)} %get-tuple-element.88), channel_id=1, source_target_pairs={{0,8},{8,0},{16,24},{24,16},{1,9},{9,1},{17,25},{25,17},{2,10},{10... | collective-permute-start | bytes 1179656 | tf_op jit(solution)/shard_map/ppermute | solution.py:546
  11.5 0.0 collective-permute-done.3.sibling_in
  11.5 1.5 %collective-permute-start.8 = (bf16[1536,128]{1,0:T(8,128)(2,1)}, bf16[1536,128]{1,0:T(8,128)(2,1)S(1)}, u32[]{:S(2)}, u32[]{:S(2)}) collective-permute-start(bf16[1536,128]{1,0:T(8,128)(2,1)} %get-tuple-element.89), channel_id=1, source_target_pairs={{0,16},{8,24},{16,0},{24,8},{1,17},{9,25},{17,1},{25,9},{2,18},{10... | collective-permute-start | bytes 1179656 | tf_op jit(solution)/shard_map/ppermute | solution.py:546
  13.0 0.5 broadcast_xor_fusion.places_ref
  13.5 5.7 %pack_projection.1 = (bf16[512,2048]{1,0:T(8,128)(2,1)}, bf16[512,2048]{1,0:T(8,128)(2,1)}) custom-call(s32[4]{0:T(128)} %broadcast_xor_fusion.places_ref, bf16[512,4096]{1,0:T(8,128)(2,1)} %mine_in.1, bf16[512,4096]{1,0:T(8,128)(2,1)} %collective-permute-done.3.sibling_in), custom_call_target="tpu_custom_call" | custom-call | flops 1024 | bytes 1024 | tf_op jit(solution)/shard_map/pack_projection/pallas_call | solution.py:227
  19.3 0.0 collective-permute-done.refs_4_.refs_7_
  19.3 6.9 %collective-permute-done.1.refs_5_.refs_8_ = bf16[1552,128]{1,0:T(8,128)(2,1)S(1)} collective-permute-done((bf16[1552,128]{1,0:T(8,128)(2,1)}, bf16[1552,128]{1,0:T(8,128)(2,1)S(1)}, u32[]{:S(2)}, u32[]{:S(2)}) %collective-permute-start.1) | collective-permute-done | bytes 397344 | tf_op jit(solution)/shard_map/ppermute | solution.py:546
  26.2 0.0 collective-permute-done.2.refs_6_.refs_9_
  26.2 5.4 %attend_low.1 = (bf16[512,128]{1,0:T(8,128)(2,1)S(1)}, bf16[512,128]{1,0:T(8,128)(2,1)S(1)}, bf16[512,128]{1,0:T(8,128)(2,1)S(1)}, bf16[512,128]{1,0:T(8,128)(2,1)S(1)}) custom-call(s32[1]{0:T(128)} %bitcast.ctx_ref, bf16[1024,512]{1,0:T(8,128)(2,1)S(1)} %copy-done.2, bf16[1024,512]{1,0:T(8,128)(2,1)S(1)} %copy-done.3, bf16[1024,512]{1,0:T(8,128)(2,1)S(1)} %copy-done.4, ...), custom_call_target="tpu_custom_call" | custom-call | flops 1024 | bytes 1024 | tf_op jit(solution)/shard_map/attend_low/pallas_call | solution.py:409
  31.6 1.0 collective-permute-start.4
  32.6 1.1 collective-permute-start.5
  33.7 1.4 %collective-permute-start.6 = (bf16[512,128]{1,0:T(8,128)(2,1)S(1)}, bf16[512,128]{1,0:T(8,128)(2,1)S(1)}, u32[]{:S(2)}, u32[]{:S(2)}) collective-permute-start(bf16[512,128]{1,0:T(8,128)(2,1)S(1)} %get-tuple-element.87), channel_id=1, source_target_pairs={{0,24},{8,16},{16,8},{24,0},{1,25},{9,17},{17,9},{25,1},{2,26},{10... | collective-permute-start | bytes 393224 | tf_op jit(solution)/shard_map/ppermute | solution.py:546
  35.2 2.6 %collective-permute-done.4.refs_1_ = bf16[512,128]{1,0:T(8,128)(2,1)S(1)} collective-permute-done((bf16[512,128]{1,0:T(8,128)(2,1)S(1)}, bf16[512,128]{1,0:T(8,128)(2,1)S(1)}, u32[]{:S(2)}, u32[]{:S(2)}) %collective-permute-start.4) | collective-permute-done | bytes 131104 | tf_op jit(solution)/shard_map/ppermute | solution.py:546
  37.8 2.1 %collective-permute-done.5.refs_2_ = bf16[512,128]{1,0:T(8,128)(2,1)S(1)} collective-permute-done((bf16[512,128]{1,0:T(8,128)(2,1)S(1)}, bf16[512,128]{1,0:T(8,128)(2,1)S(1)}, u32[]{:S(2)}, u32[]{:S(2)}) %collective-permute-start.5) | collective-permute-done | bytes 131104 | tf_op jit(solution)/shard_map/ppermute | solution.py:546
  39.9 0.1 assemble.2.refs_0_
  40.0 0.1 collective-permute-start.10
  40.1 1.9 %collective-permute-done.10.refs_1_ = bf16[512,512]{1,0:T(8,128)(2,1)S(1)} collective-permute-done((bf16[512,512]{1,0:T(8,128)(2,1)S(1)}, bf16[512,512]{1,0:T(8,128)(2,1)S(1)}, u32[]{:S(2)}, u32[]{:S(2)}) %collective-permute-start.10) | collective-permute-done | bytes 524320 | tf_op jit(solution)/shard_map/ppermute | solution.py:546
  42.0 0.7 project.8
  42.7 1.6 %collective-permute-start.11 = (bf16[512,512]{1,0:T(8,128)(2,1)S(1)}, bf16[512,512]{1,0:T(8,128)(2,1)S(1)}, u32[]{:S(2)}, u32[]{:S(2)}) collective-permute-start(bf16[512,512]{1,0:T(8,128)(2,1)S(1)} %project.8), channel_id=1, source_target_pairs={{0,2},{1,3},{2,0},{3,1},{4,6},{5,7},{6,4},{7,5},{8,10},{9,11},{10,... | collective-permute-start | bytes 1572872 | tf_op jit(solution)/shard_map/ppermute | solution.py:546
  44.3 1.8 %collective-permute-start.9 = (bf16[1536,128]{1,0:T(8,128)(2,1)S(1)}, bf16[1536,128]{1,0:T(8,128)(2,1)S(1)}, u32[]{:S(2)}, u32[]{:S(2)}) collective-permute-start(bf16[1536,128]{1,0:T(8,128)(2,1)S(1)} %copy-done.6), channel_id=1, source_target_pairs={{0,24},{8,16},{16,8},{24,0},{1,25},{9,17},{17,9},{25,1},{2,26},{10... | collective-permute-start | bytes 1179656 | tf_op jit(solution)/shard_map/ppermute | solution.py:546
  46.1 0.7 project.9
  46.8 0.5 collective-permute-start.15
  47.3 0.7 project.10
  48.1 0.7 project.11.refs_0_
  48.8 7.3 %collective-permute-done.9.refs_12_ = bf16[1536,128]{1,0:T(8,128)(2,1)S(1)} collective-permute-done((bf16[1536,128]{1,0:T(8,128)(2,1)S(1)}, bf16[1536,128]{1,0:T(8,128)(2,1)S(1)}, u32[]{:S(2)}, u32[]{:S(2)}) %collective-permute-start.9) | collective-permute-done | bytes 393248 | tf_op jit(solution)/shard_map/ppermute | solution.py:546
  56.1 6.8 %attend_high.1 = (bf16[512,128]{1,0:T(8,128)(2,1)S(1)}, bf16[512,128]{1,0:T(8,128)(2,1)S(1)}, bf16[512,128]{1,0:T(8,128)(2,1)S(1)}, bf16[512,128]{1,0:T(8,128)(2,1)S(1)}) custom-call(s32[1]{0:T(128)} %bitcast.ctx_ref, bf16[1024,512]{1,0:T(8,128)(2,1)S(1)} %copy-done.2, bf16[1024,512]{1,0:T(8,128)(2,1)S(1)} %copy-done.3, bf16[1024,512]{1,0:T(8,128)(2,1)S(1)} %copy-done.4, ...), custom_call_target="tpu_custom_call" | custom-call | flops 1024 | bytes 1024 | tf_op jit(solution)/shard_map/attend_high/pallas_call | solution.py:409
  62.9 1.4 %collective-permute-start.12 = (bf16[512,128]{1,0:T(8,128)(2,1)S(1)}, bf16[512,128]{1,0:T(8,128)(2,1)S(1)}, u32[]{:S(2)}, u32[]{:S(2)}) collective-permute-start(bf16[512,128]{1,0:T(8,128)(2,1)S(1)} %get-tuple-element.103), channel_id=1, source_target_pairs={{0,8},{8,0},{16,24},{24,16},{1,9},{9,1},{17,25},{25,17},{2,10},{10... | collective-permute-start | bytes 393224 | tf_op jit(solution)/shard_map/ppermute | solution.py:546
  64.3 1.0 collective-permute-start.13
  65.3 1.1 collective-permute-start.14
  66.5 0.0 collective-permute-done.11
  66.5 0.1 add_convert_fusion
  66.6 2.7 %collective-permute-start.19 = (bf16[512,512]{1,0:T(8,128)(2,1)S(1)}, bf16[512,512]{1,0:T(8,128)(2,1)S(1)}, u32[]{:S(2)}, u32[]{:S(2)}) collective-permute-start(bf16[512,512]{1,0:T(8,128)(2,1)S(1)} %add_convert_fusion), channel_id=1, source_target_pairs={{0,4},{1,5},{2,6},{3,7},{4,0},{5,1},{6,2},{7,3},{8,12},{9,13},{10,... | collective-permute-start | bytes 1572872 | tf_op jit(solution)/shard_map/ppermute | solution.py:546
  69.3 2.4 %collective-permute-done.13.refs_2_ = bf16[512,128]{1,0:T(8,128)(2,1)S(1)} collective-permute-done((bf16[512,128]{1,0:T(8,128)(2,1)S(1)}, bf16[512,128]{1,0:T(8,128)(2,1)S(1)}, u32[]{:S(2)}, u32[]{:S(2)}) %collective-permute-start.13) | collective-permute-done | bytes 131104 | tf_op jit(solution)/shard_map/ppermute | solution.py:546
  71.7 0.0 collective-permute-done.14.refs_3_
  71.7 0.1 assemble.3
  71.8 0.1 collective-permute-start.16
  71.9 0.5 collective-permute-start.17
  72.4 1.0 collective-permute-done.16.refs_2_
  73.4 0.4 collective-permute-done.17.refs_3_
  73.8 0.7 project.15
  74.5 0.5 collective-permute-start.18
  75.0 15.9 %collective-permute-done.19.refs_2_ = bf16[512,512]{1,0:T(8,128)(2,1)S(1)} collective-permute-done((bf16[512,512]{1,0:T(8,128)(2,1)S(1)}, bf16[512,512]{1,0:T(8,128)(2,1)S(1)}, u32[]{:S(2)}, u32[]{:S(2)}) %collective-permute-start.19) | collective-permute-done | bytes 524320 | tf_op jit(solution)/shard_map/ppermute | solution.py:546
  90.9 0.7 project.14
  91.6 1.4 %collective-permute-done.18 = bf16[256,512]{1,0:T(8,128)(2,1)S(1)} collective-permute-done((bf16[256,512]{1,0:T(8,128)(2,1)S(1)}, bf16[256,512]{1,0:T(8,128)(2,1)S(1)}, u32[]{:S(2)}, u32[]{:S(2)}) %collective-permute-start.18) | collective-permute-done | bytes 262176 | tf_op jit(solution)/shard_map/ppermute | solution.py:546
  93.0 0.1 add_convert_fusion.2
  93.0 1.8 %collective-permute-start.24 = (bf16[256,512]{1,0:T(8,128)(2,1)S(1)}, bf16[256,512]{1,0:T(8,128)(2,1)S(1)}, u32[]{:S(2)}, u32[]{:S(2)}) collective-permute-start(bf16[256,512]{1,0:T(8,128)(2,1)S(1)} %add_convert_fusion.2), channel_id=1, source_target_pairs={{0,4},{1,5},{2,6},{3,7},{4,0},{5,1},{6,2},{7,3},{8,12},{9,13},{10,... | collective-permute-start | bytes 786440 | tf_op jit(solution)/shard_map/ppermute | solution.py:546
  94.8 6.7 %collective-permute-done.20 = bf16[256,512]{1,0:T(8,128)(2,1)S(1)} collective-permute-done((bf16[256,512]{1,0:T(8,128)(2,1)S(1)}, bf16[256,512]{1,0:T(8,128)(2,1)S(1)}, u32[]{:S(2)}, u32[]{:S(2)}) %collective-permute-start.20) | collective-permute-done | bytes 262176 | tf_op jit(solution)/shard_map/ppermute | solution.py:546
  101.5 0.1 add_convert_fusion.1
  101.6 0.1 collective-permute-start.25
  101.7 0.7 project.13
  102.4 1.6 %collective-permute-start.21 = (bf16[176,512]{1,0:T(8,128)(2,1)S(1)}, bf16[176,512]{1,0:T(8,128)(2,1)S(1)}, u32[]{:S(2)}, u32[]{:S(2)}) collective-permute-start(bf16[176,512]{1,0:T(8,128)(2,1)S(1)} %get-tuple-element.121), channel_id=1, source_target_pairs={{0,2},{1,3},{2,0},{3,1},{4,6},{5,7},{6,4},{7,5},{8,10},{9,11},{10,... | collective-permute-start | bytes 540680 | tf_op jit(solution)/shard_map/ppermute | solution.py:546
  104.0 0.5 collective-permute-start.22
  104.5 1.5 %collective-permute-start.23 = (bf16[160,512]{1,0:T(8,128)(2,1)S(1)}, bf16[160,512]{1,0:T(8,128)(2,1)S(1)}, u32[]{:S(2)}, u32[]{:S(2)}) collective-permute-start(bf16[160,512]{1,0:T(8,128)(2,1)S(1)} %get-tuple-element.123), channel_id=1, source_target_pairs={{0,2},{1,3},{2,0},{3,1},{4,6},{5,7},{6,4},{7,5},{8,10},{9,11},{10,... | collective-permute-start | bytes 491528 | tf_op jit(solution)/shard_map/ppermute | solution.py:546
  106.0 0.7 project.12.refs_0_
  106.8 1.0 finish.2.refs_6_
  107.7 6.5 %collective-permute-done.24.refs_4_ = bf16[256,512]{1,0:T(8,128)(2,1)S(1)} collective-permute-done((bf16[256,512]{1,0:T(8,128)(2,1)S(1)}, bf16[256,512]{1,0:T(8,128)(2,1)S(1)}, u32[]{:S(2)}, u32[]{:S(2)}) %collective-permute-start.24) | collective-permute-done | bytes 262176 | tf_op jit(solution)/shard_map/ppermute | solution.py:546
  114.3 7.6 %collective-permute-done.23.refs_3_ = bf16[160,512]{1,0:T(8,128)(2,1)S(1)} collective-permute-done((bf16[160,512]{1,0:T(8,128)(2,1)S(1)}, bf16[160,512]{1,0:T(8,128)(2,1)S(1)}, u32[]{:S(2)}, u32[]{:S(2)}) %collective-permute-start.23) | collective-permute-done | bytes 163872 | tf_op jit(solution)/shard_map/ppermute | solution.py:546
  121.9 1.0 finish.3
  (25 shorter events, 0.1 us)
Async XLA Ops:
  0.0 11.5 %collective-permute-start.3 = (bf16[512,4096]{1,0:T(8,128)(2,1)}, bf16[512,4096]{1,0:T(8,128)(2,1)}, u32[]{:S(2)}, u32[]{:S(2)}) collective-permute-start(bf16[512,4096]{1,0:T(8,128)(2,1)} %mine_in.1), channel_id=1, source_target_pairs={{0,1},{1,0},{2,3},{3,2},{4,5},{5,4},{6,7},{7,6},{8,9},{9,8},{10,11... | collective-permute-start | bytes 12582920 | tf_op jit(solution)/shard_map/ppermute | solution.py:546
  2.9 10.0 %copy-start.7 = (s32[4]{0:T(128)S(1)}, s32[4]{0:T(128)}, u32[]{:S(2)}) copy-start(s32[4]{0:T(128)} %constant.13) | copy-start | bytes 52
  2.9 16.3 %collective-permute-start = (bf16[1552,128]{1,0:T(8,128)(2,1)}, bf16[1552,128]{1,0:T(8,128)(2,1)S(1)}, u32[]{:S(2)}, u32[]{:S(2)}) collective-permute-start(bf16[1552,128]{1,0:T(8,128)(2,1)} %get-tuple-element.69), channel_id=1, source_target_pairs={{0,8},{8,0},{16,24},{24,16},{1,9},{9,1},{17,25},{25,17},{2,10},{10... | collective-permute-start | bytes 1191944 | tf_op jit(solution)/shard_map/ppermute | solution.py:546
  5.4 20.8 %collective-permute-start.1 = (bf16[1552,128]{1,0:T(8,128)(2,1)}, bf16[1552,128]{1,0:T(8,128)(2,1)S(1)}, u32[]{:S(2)}, u32[]{:S(2)}) collective-permute-start(bf16[1552,128]{1,0:T(8,128)(2,1)} %get-tuple-element.70), channel_id=1, source_target_pairs={{0,16},{8,24},{16,0},{24,8},{1,17},{9,25},{17,1},{25,9},{2,18},{10... | collective-permute-start | bytes 1191944 | tf_op jit(solution)/shard_map/ppermute | solution.py:546
  7.0 19.2 %collective-permute-start.2 = (bf16[1552,128]{1,0:T(8,128)(2,1)}, bf16[1552,128]{1,0:T(8,128)(2,1)S(1)}, u32[]{:S(2)}, u32[]{:S(2)}) collective-permute-start(bf16[1552,128]{1,0:T(8,128)(2,1)} %get-tuple-element.71), channel_id=1, source_target_pairs={{0,24},{8,16},{16,8},{24,0},{1,25},{9,17},{17,9},{25,1},{2,26},{10... | collective-permute-start | bytes 1191944 | tf_op jit(solution)/shard_map/ppermute | solution.py:546
  9.5 25.7 %collective-permute-start.7 = (bf16[1536,128]{1,0:T(8,128)(2,1)}, bf16[1536,128]{1,0:T(8,128)(2,1)S(1)}, u32[]{:S(2)}, u32[]{:S(2)}) collective-permute-start(bf16[1536,128]{1,0:T(8,128)(2,1)} %get-tuple-element.88), channel_id=1, source_target_pairs={{0,8},{8,0},{16,24},{24,16},{1,9},{9,1},{17,25},{25,17},{2,10},{10... | collective-permute-start | bytes 1179656 | tf_op jit(solution)/shard_map/ppermute | solution.py:546
  11.5 23.7 %collective-permute-start.8 = (bf16[1536,128]{1,0:T(8,128)(2,1)}, bf16[1536,128]{1,0:T(8,128)(2,1)S(1)}, u32[]{:S(2)}, u32[]{:S(2)}) collective-permute-start(bf16[1536,128]{1,0:T(8,128)(2,1)} %get-tuple-element.89), channel_id=1, source_target_pairs={{0,16},{8,24},{16,0},{24,8},{1,17},{9,25},{17,1},{25,9},{2,18},{10... | collective-permute-start | bytes 1179656 | tf_op jit(solution)/shard_map/ppermute | solution.py:546
  13.5 12.7 %copy-start.2 = (bf16[1024,512]{1,0:T(8,128)(2,1)S(1)}, bf16[1024,512]{1,0:T(8,128)(2,1)}, u32[]{:S(2)}) copy-start(bf16[1024,512]{1,0:T(8,128)(2,1)} %refs_3_.4) | copy-start | bytes 3145732
  13.5 12.7 %copy-start.3 = (bf16[1024,512]{1,0:T(8,128)(2,1)S(1)}, bf16[1024,512]{1,0:T(8,128)(2,1)}, u32[]{:S(2)}) copy-start(bf16[1024,512]{1,0:T(8,128)(2,1)} %refs_4_.4) | copy-start | bytes 3145732
  13.5 12.7 %copy-start.4 = (bf16[1024,512]{1,0:T(8,128)(2,1)S(1)}, bf16[1024,512]{1,0:T(8,128)(2,1)}, u32[]{:S(2)}) copy-start(bf16[1024,512]{1,0:T(8,128)(2,1)} %refs_5_.4) | copy-start | bytes 3145732
  13.5 12.7 %copy-start.5 = (s32[1024]{0:T(1024)S(1)}, s32[1024]{0:T(1024)}, u32[]{:S(2)}) copy-start(s32[1024]{0:T(1024)} %param.9) | copy-start | bytes 12292
  19.3 22.7 %copy-start = (bf16[512,2048]{1,0:T(8,128)(2,1)S(1)}, bf16[512,2048]{1,0:T(8,128)(2,1)}, u32[]{:S(2)}) copy-start(bf16[512,2048]{1,0:T(8,128)(2,1)} %get-tuple-element.97.refs_2_.refs_4_) | copy-start | bytes 6291460
  19.3 22.7 %copy-start.1 = (bf16[512,2048]{1,0:T(8,128)(2,1)S(1)}, bf16[512,2048]{1,0:T(8,128)(2,1)}, u32[]{:S(2)}) copy-start(bf16[512,2048]{1,0:T(8,128)(2,1)} %get-tuple-element.98.refs_3_.refs_5_) | copy-start | bytes 6291460
  31.6 12.7 %copy-start.6 = (bf16[1536,128]{1,0:T(8,128)(2,1)S(1)}, bf16[1536,128]{1,0:T(8,128)(2,1)}, u32[]{:S(2)}) copy-start(bf16[1536,128]{1,0:T(8,128)(2,1)} %get-tuple-element.92) | copy-start | bytes 1179652
  31.6 6.2 %collective-permute-start.4 = (bf16[512,128]{1,0:T(8,128)(2,1)S(1)}, bf16[512,128]{1,0:T(8,128)(2,1)S(1)}, u32[]{:S(2)}, u32[]{:S(2)}) collective-permute-start(bf16[512,128]{1,0:T(8,128)(2,1)S(1)} %get-tuple-element.85), channel_id=1, source_target_pairs={{0,8},{8,0},{16,24},{24,16},{1,9},{9,1},{17,25},{25,17},{2,10},{10... | collective-permute-start | bytes 393224 | tf_op jit(solution)/shard_map/ppermute | solution.py:546
  32.6 7.3 %collective-permute-start.5 = (bf16[512,128]{1,0:T(8,128)(2,1)S(1)}, bf16[512,128]{1,0:T(8,128)(2,1)S(1)}, u32[]{:S(2)}, u32[]{:S(2)}) collective-permute-start(bf16[512,128]{1,0:T(8,128)(2,1)S(1)} %get-tuple-element.86), channel_id=1, source_target_pairs={{0,16},{8,24},{16,0},{24,8},{1,17},{9,25},{17,1},{25,9},{2,18},{10... | collective-permute-start | bytes 393224 | tf_op jit(solution)/shard_map/ppermute | solution.py:546
  33.7 6.2 %collective-permute-start.6 = (bf16[512,128]{1,0:T(8,128)(2,1)S(1)}, bf16[512,128]{1,0:T(8,128)(2,1)S(1)}, u32[]{:S(2)}, u32[]{:S(2)}) collective-permute-start(bf16[512,128]{1,0:T(8,128)(2,1)S(1)} %get-tuple-element.87), channel_id=1, source_target_pairs={{0,24},{8,16},{16,8},{24,0},{1,25},{9,17},{17,9},{25,1},{2,26},{10... | collective-permute-start | bytes 393224 | tf_op jit(solution)/shard_map/ppermute | solution.py:546
  40.0 2.0 %collective-permute-start.10 = (bf16[512,512]{1,0:T(8,128)(2,1)S(1)}, bf16[512,512]{1,0:T(8,128)(2,1)S(1)}, u32[]{:S(2)}, u32[]{:S(2)}) collective-permute-start(bf16[512,512]{1,0:T(8,128)(2,1)S(1)} %assemble.2.refs_0_), channel_id=1, source_target_pairs={{0,1},{1,0},{2,3},{3,2},{4,5},{5,4},{6,7},{7,6},{8,9},{9,8},{10,11... | collective-permute-start | bytes 1572872 | tf_op jit(solution)/shard_map/ppermute | solution.py:546
  42.7 23.8 %collective-permute-start.11 = (bf16[512,512]{1,0:T(8,128)(2,1)S(1)}, bf16[512,512]{1,0:T(8,128)(2,1)S(1)}, u32[]{:S(2)}, u32[]{:S(2)}) collective-permute-start(bf16[512,512]{1,0:T(8,128)(2,1)S(1)} %project.8), channel_id=1, source_target_pairs={{0,2},{1,3},{2,0},{3,1},{4,6},{5,7},{6,4},{7,5},{8,10},{9,11},{10,... | collective-permute-start | bytes 1572872 | tf_op jit(solution)/shard_map/ppermute | solution.py:546
  44.3 11.8 %collective-permute-start.9 = (bf16[1536,128]{1,0:T(8,128)(2,1)S(1)}, bf16[1536,128]{1,0:T(8,128)(2,1)S(1)}, u32[]{:S(2)}, u32[]{:S(2)}) collective-permute-start(bf16[1536,128]{1,0:T(8,128)(2,1)S(1)} %copy-done.6), channel_id=1, source_target_pairs={{0,24},{8,16},{16,8},{24,0},{1,25},{9,17},{17,9},{25,1},{2,26},{10... | collective-permute-start | bytes 1179656 | tf_op jit(solution)/shard_map/ppermute | solution.py:546
  46.8 24.9 %collective-permute-start.15 = (bf16[512,512]{1,0:T(8,128)(2,1)S(1)}, bf16[512,512]{1,0:T(8,128)(2,1)S(1)}, u32[]{:S(2)}, u32[]{:S(2)}) collective-permute-start(bf16[512,512]{1,0:T(8,128)(2,1)S(1)} %project.9), channel_id=1, source_target_pairs={{0,2},{1,3},{2,0},{3,1},{4,6},{5,7},{6,4},{7,5},{8,10},{9,11},{10,... | collective-permute-start | bytes 1572872 | tf_op jit(solution)/shard_map/ppermute | solution.py:546
  62.9 6.4 %collective-permute-start.12 = (bf16[512,128]{1,0:T(8,128)(2,1)S(1)}, bf16[512,128]{1,0:T(8,128)(2,1)S(1)}, u32[]{:S(2)}, u32[]{:S(2)}) collective-permute-start(bf16[512,128]{1,0:T(8,128)(2,1)S(1)} %get-tuple-element.103), channel_id=1, source_target_pairs={{0,8},{8,0},{16,24},{24,16},{1,9},{9,1},{17,25},{25,17},{2,10},{10... | collective-permute-start | bytes 393224 | tf_op jit(solution)/shard_map/ppermute | solution.py:546
  64.3 7.3 %collective-permute-start.13 = (bf16[512,128]{1,0:T(8,128)(2,1)S(1)}, bf16[512,128]{1,0:T(8,128)(2,1)S(1)}, u32[]{:S(2)}, u32[]{:S(2)}) collective-permute-start(bf16[512,128]{1,0:T(8,128)(2,1)S(1)} %get-tuple-element.104), channel_id=1, source_target_pairs={{0,16},{8,24},{16,0},{24,8},{1,17},{9,25},{17,1},{25,9},{2,18},{10... | collective-permute-start | bytes 393224 | tf_op jit(solution)/shard_map/ppermute | solution.py:546
  65.3 6.4 %collective-permute-start.14 = (bf16[512,128]{1,0:T(8,128)(2,1)S(1)}, bf16[512,128]{1,0:T(8,128)(2,1)S(1)}, u32[]{:S(2)}, u32[]{:S(2)}) collective-permute-start(bf16[512,128]{1,0:T(8,128)(2,1)S(1)} %get-tuple-element.105), channel_id=1, source_target_pairs={{0,24},{8,16},{16,8},{24,0},{1,25},{9,17},{17,9},{25,1},{2,26},{10... | collective-permute-start | bytes 393224 | tf_op jit(solution)/shard_map/ppermute | solution.py:546
  66.6 24.3 %collective-permute-start.19 = (bf16[512,512]{1,0:T(8,128)(2,1)S(1)}, bf16[512,512]{1,0:T(8,128)(2,1)S(1)}, u32[]{:S(2)}, u32[]{:S(2)}) collective-permute-start(bf16[512,512]{1,0:T(8,128)(2,1)S(1)} %add_convert_fusion), channel_id=1, source_target_pairs={{0,4},{1,5},{2,6},{3,7},{4,0},{5,1},{6,2},{7,3},{8,12},{9,13},{10,... | collective-permute-start | bytes 1572872 | tf_op jit(solution)/shard_map/ppermute | solution.py:546
  71.8 1.6 %collective-permute-start.16 = (bf16[256,512]{1,0:T(8,128)(2,1)S(1)}, bf16[256,512]{1,0:T(8,128)(2,1)S(1)}, u32[]{:S(2)}, u32[]{:S(2)}) collective-permute-start(bf16[256,512]{1,0:T(8,128)(2,1)S(1)} %get-tuple-element.110.refs_0_), channel_id=1, source_target_pairs={{0,1},{1,0},{2,3},{3,2},{4,5},{5,4},{6,7},{7,6},{8,9},{9,8},{10,11... | collective-permute-start | bytes 786440 | tf_op jit(solution)/shard_map/ppermute | solution.py:546
  71.9 1.9 %collective-permute-start.17 = (bf16[256,512]{1,0:T(8,128)(2,1)S(1)}, bf16[256,512]{1,0:T(8,128)(2,1)S(1)}, u32[]{:S(2)}, u32[]{:S(2)}) collective-permute-start(bf16[256,512]{1,0:T(8,128)(2,1)S(1)} %get-tuple-element.111.refs_1_), channel_id=1, source_target_pairs={{0,1},{1,0},{2,3},{3,2},{4,5},{5,4},{6,7},{7,6},{8,9},{9,8},{10,11... | collective-permute-start | bytes 786440 | tf_op jit(solution)/shard_map/ppermute | solution.py:546
  74.5 18.5 %collective-permute-start.18 = (bf16[256,512]{1,0:T(8,128)(2,1)S(1)}, bf16[256,512]{1,0:T(8,128)(2,1)S(1)}, u32[]{:S(2)}, u32[]{:S(2)}) collective-permute-start(bf16[256,512]{1,0:T(8,128)(2,1)S(1)} %get-tuple-element.116), channel_id=1, source_target_pairs={{0,2},{1,3},{2,0},{3,1},{4,6},{5,7},{6,4},{7,5},{8,10},{9,11},{10,... | collective-permute-start | bytes 786440 | tf_op jit(solution)/shard_map/ppermute | solution.py:546
  90.9 10.6 %collective-permute-start.20 = (bf16[256,512]{1,0:T(8,128)(2,1)S(1)}, bf16[256,512]{1,0:T(8,128)(2,1)S(1)}, u32[]{:S(2)}, u32[]{:S(2)}) collective-permute-start(bf16[256,512]{1,0:T(8,128)(2,1)S(1)} %get-tuple-element.120), channel_id=1, source_target_pairs={{0,2},{1,3},{2,0},{3,1},{4,6},{5,7},{6,4},{7,5},{8,10},{9,11},{10,... | collective-permute-start | bytes 786440 | tf_op jit(solution)/shard_map/ppermute | solution.py:546
  93.0 21.2 %collective-permute-start.24 = (bf16[256,512]{1,0:T(8,128)(2,1)S(1)}, bf16[256,512]{1,0:T(8,128)(2,1)S(1)}, u32[]{:S(2)}, u32[]{:S(2)}) collective-permute-start(bf16[256,512]{1,0:T(8,128)(2,1)S(1)} %add_convert_fusion.2), channel_id=1, source_target_pairs={{0,4},{1,5},{2,6},{3,7},{4,0},{5,1},{6,2},{7,3},{8,12},{9,13},{10,... | collective-permute-start | bytes 786440 | tf_op jit(solution)/shard_map/ppermute | solution.py:546
  101.6 20.3 %collective-permute-start.25 = (bf16[256,512]{1,0:T(8,128)(2,1)S(1)}, bf16[256,512]{1,0:T(8,128)(2,1)S(1)}, u32[]{:S(2)}, u32[]{:S(2)}) collective-permute-start(bf16[256,512]{1,0:T(8,128)(2,1)S(1)} %add_convert_fusion.1), channel_id=1, source_target_pairs={{0,4},{1,5},{2,6},{3,7},{4,0},{5,1},{6,2},{7,3},{8,12},{9,13},{10,... | collective-permute-start | bytes 786440 | tf_op jit(solution)/shard_map/ppermute | solution.py:546
  102.4 19.4 %collective-permute-start.21 = (bf16[176,512]{1,0:T(8,128)(2,1)S(1)}, bf16[176,512]{1,0:T(8,128)(2,1)S(1)}, u32[]{:S(2)}, u32[]{:S(2)}) collective-permute-start(bf16[176,512]{1,0:T(8,128)(2,1)S(1)} %get-tuple-element.121), channel_id=1, source_target_pairs={{0,2},{1,3},{2,0},{3,1},{4,6},{5,7},{6,4},{7,5},{8,10},{9,11},{10,... | collective-permute-start | bytes 540680 | tf_op jit(solution)/shard_map/ppermute | solution.py:546
  104.0 17.8 %collective-permute-start.22 = (bf16[176,512]{1,0:T(8,128)(2,1)S(1)}, bf16[176,512]{1,0:T(8,128)(2,1)S(1)}, u32[]{:S(2)}, u32[]{:S(2)}) collective-permute-start(bf16[176,512]{1,0:T(8,128)(2,1)S(1)} %get-tuple-element.122), channel_id=1, source_target_pairs={{0,2},{1,3},{2,0},{3,1},{4,6},{5,7},{6,4},{7,5},{8,10},{9,11},{10,... | collective-permute-start | bytes 540680 | tf_op jit(solution)/shard_map/ppermute | solution.py:546
  104.5 17.3 %collective-permute-start.23 = (bf16[160,512]{1,0:T(8,128)(2,1)S(1)}, bf16[160,512]{1,0:T(8,128)(2,1)S(1)}, u32[]{:S(2)}, u32[]{:S(2)}) collective-permute-start(bf16[160,512]{1,0:T(8,128)(2,1)S(1)} %get-tuple-element.123), channel_id=1, source_target_pairs={{0,2},{1,3},{2,0},{3,1},{4,6},{5,7},{6,4},{7,5},{8,10},{9,11},{10,... | collective-permute-start | bytes 491528 | tf_op jit(solution)/shard_map/ppermute | solution.py:546

commit v23 on v14

--- a/solution.py
+++ b/solution.py
@@ -276,8 +276,8 @@
                 source = ctx ^ distance
                 block = 2 * group - 1 - source if upper else source
                 place[upper, distance] = block
-                offset = pl.multiple_of(block * rows, rows)
-                key_buf[pl.ds(offset, rows), :] = part(upper, distance, 1)
+                offset = pl.multiple_of(block * rows, TILE)
+                key_buf[pl.ds(offset + TILE, rows), :] = part(upper, distance, 1)
                 if distance == 0:
                     both = own_docs[...].astype(jnp.float32)
                 else:
@@ -288,12 +288,14 @@
                     taken = part(upper, distance, 2, line * HD, HD)
                     if distance == 0:
                         taken = jnp.transpose(taken)
-                    column = pl.multiple_of(block * rows + line * HD, HD)
+                    column = pl.multiple_of(block * rows + line * HD + TILE, HD)
                     value_buf[:HD, pl.ds(column, HD)] = taken
                     mine.append(both[begin + line : begin + line + 1, :])
                     doc_buf[pl.ds(block * lines + line, 1), :] = mine[-1]
                 doc_rows[upper, distance] = jnp.concatenate(mine, axis=1)
-        value_buf[HD:, :] = jnp.ones((value_buf.shape[0] - HD, key_rows), jnp.bfloat16)
+        value_buf[HD:, :] = jnp.ones((value_buf.shape[0] - HD, key_rows + TILE), jnp.bfloat16)
+        key_buf[:TILE, :] = jnp.zeros((TILE, HD), jnp.bfloat16)
+        value_buf[:HD, :TILE] = jnp.zeros((HD, TILE), jnp.bfloat16)
 
         all_docs = doc_buf[...]
         starts = [jnp.zeros((1, rows), jnp.float32)] * group
@@ -304,18 +306,18 @@
                 reached = doc_rows[with_high, distance] >= number
                 starts[distance] = jnp.where(reached, count, starts[distance])
 
-        def scores_of(query, offset):
+        def scores_of(query, offset, count):
             raw = lax.dot_general(
-                key_buf[pl.ds(offset, TILE), :],
+                key_buf[pl.ds(pl.multiple_of(offset + TILE, TILE), count), :],
                 query,
                 (((1,), (1,)), ((), ())),
                 preferred_element_type=jnp.float32,
             )
             return raw * scaling
 
-        def weighted(weights, offset):
+        def weighted(weights, offset, count):
             return jnp.dot(
-                value_buf[:, pl.ds(offset, TILE)],
+                value_buf[:, pl.ds(pl.multiple_of(offset + TILE, TILE), count)],
                 weights.astype(jnp.bfloat16),
                 preferred_element_type=jnp.float32,
             )
@@ -323,7 +325,7 @@
         key_row = lax.broadcasted_iota(jnp.int32, (TILE, TILE), 0)
         causal = key_row <= lax.broadcasted_iota(jnp.int32, (TILE, TILE), 1)
         key_row = key_row.astype(jnp.float32)
-        firsts = []
+        ends = []
         counts = []
         for lane in range(group):
             for slot in range(per_block):
@@ -335,19 +337,21 @@
                 end = place[with_high, distance] * per_block + slot
                 offset = pl.multiple_of(end * TILE, TILE)
                 least = start - offset.astype(jnp.float32)
-                scores = scores_of(query, offset)
+                scores = scores_of(query, offset, TILE)
                 scores = jnp.where((key_row >= least) & causal, scores, MASKED_SCORE)
                 largest = jnp.max(scores, axis=0, keepdims=True)
                 largest_buf[lane][slot, 0:1, :] = largest
-                summed[lane][slot] = weighted(jnp.exp2(scores - largest), offset)
+                summed[lane][slot] = weighted(jnp.exp2(scores - largest), offset, TILE)
                 first = start[0, 0].astype(jnp.int32) // TILE
-                firsts.append(first)
-                counts.append(end - first)
+                ends.append(end)
+                counts.append((end - first + 1) // 2)
 
         longest = jnp.int32(0)
         for lane in range(group):
             of_lane = counts[lane * per_block : (lane + 1) * per_block]
             longest = jnp.maximum(longest, sum(of_lane))
+
+        pair_row = lax.broadcasted_iota(jnp.int32, (2 * TILE, TILE), 0).astype(jnp.float32)
 
         def visit(step, carry):
             slots = []
@@ -355,29 +359,34 @@
             beyonds = []
             for lane in range(group):
                 slot = jnp.int32(0)
-                index = firsts[lane * per_block] + step
+                index = ends[lane * per_block] - 2 * step - 2
                 before = counts[lane * per_block]
                 for later in range(1, per_block):
                     reached = step >= before
                     slot = jnp.where(reached, later, slot)
                     place_later = lane * per_block + later
-                    index = jnp.where(reached, firsts[place_later] + step - before, index)
+                    later_index = ends[place_later] - 2 * (step - before) - 2
+                    index = jnp.where(reached, later_index, index)
                     before = before + counts[place_later]
-                offset = pl.multiple_of(jnp.minimum(index, key_tiles - 1) * TILE, TILE)
+                index = jnp.minimum(jnp.maximum(index, -1), key_tiles - 2)
+                offset = pl.multiple_of(index * TILE, TILE)
                 slots.append(slot)
                 offsets.append(offset)
                 beyonds.append(jnp.where(step < before, -offset.astype(jnp.float32), 1e9))
             each = range(group)
-            scores = [scores_of(query_buf[lane][slots[lane]], offsets[lane]) for lane in each]
+            scores = [
+                scores_of(query_buf[lane][slots[lane]], offsets[lane], 2 * TILE) for lane in each
+            ]
             old_max = [largest_buf[lane][slots[lane], 0:1, :] for lane in each]
             new_max = []
             for lane in each:
                 least = start_buf[lane][slots[lane], 0:1, :] + beyonds[lane]
-                scores[lane] = jnp.where(key_row >= least, scores[lane], MASKED_SCORE)
+                scores[lane] = jnp.where(pair_row >= least, scores[lane], MASKED_SCORE)
                 tile_max = jnp.max(scores[lane], axis=0, keepdims=True)
                 new_max.append(jnp.maximum(old_max[lane], tile_max))
             products = [
-                weighted(jnp.exp2(scores[lane] - new_max[lane]), offsets[lane]) for lane in each
+                weighted(jnp.exp2(scores[lane] - new_max[lane]), offsets[lane], 2 * TILE)
+                for lane in each
             ]
             for lane in each:
                 factor = jnp.exp2(old_max[lane] - new_max[lane])
@@ -414,8 +423,8 @@
             in_specs=in_specs,
             out_specs=[whole((rows, HD))] * group,
             scratch_shapes=[
-                pltpu.VMEM((key_rows, HD), jnp.bfloat16),
-                pltpu.VMEM((HD + 16, key_rows), jnp.bfloat16),
+                pltpu.VMEM((key_rows + TILE, HD), jnp.bfloat16),
+                pltpu.VMEM((HD + 16, key_rows + TILE), jnp.bfloat16),
                 pltpu.VMEM((key_rows // HD, HD), jnp.float32),
                 *[pltpu.VMEM((per_block, TILE, HD), jnp.bfloat16)] * group,
                 *[pltpu.VMEM((per_block, 8, TILE), jnp.float32)] * (2 * group),

time: 118 us -> 119 us (level)
  Pallas kernels: 28.9 us -> 31.4 us
  waiting for transfers between devices: 57.8 us -> 56.6 us
    pallas_call x2, Pallas kernels: 10.2 us -> 12.8 us  [attend(): pl.pallas_call(kernel, grid_spec=pltpu.PrefetchScalarGridSpec(num_scalar_...]
    ppermute x25, waiting for transfers between devices: 57.8 us -> 56.6 us  [swap(): lax.ppermute(value, axis, [(source, source ^ distance) for source in rang...]
  transfers between devices with their start and end apart: 25 -> 25, of which waited for: 16 -> 16; matrix products, arithmetic and copies ran while one was open for 1% -> 1% of each run, Pallas kernels for 23% -> 25%
where the time goes in v23:
time: 119 us; the launch traced here: 118 us
  waiting for transfers between devices  56.6 us (48%)
  Pallas kernels  31.4 us (26%)
  starting transfers between devices  29.3 us (25%)
    ppermute x25, waiting for transfers between devices, swap(): lax.ppermute(value, axis, [(source, source ^ distance) for source in rang...  56.6 us
    ppermute x25, starting transfers between devices, swap(): lax.ppermute(value, axis, [(source, source ^ distance) for source in rang...  29.3 us
    pallas_call x2, Pallas kernels, attend(): pl.pallas_call(kernel, grid_spec=pltpu.PrefetchScalarGridSpec(num_scalar_...  12.8 us
    pallas_call x1, Pallas kernels, pack_projection(): pl.pallas_call(kernel, grid_spec=pltpu.PrefetchScalarGridSpec(num_scalar_...  5.74 us
    pallas_call x8, Pallas kernels, project(): pl.pallas_call(kernel, grid=(1,), in_specs=[attended] * (2 * parts) + [we...  5.69 us
    pallas_call x2, Pallas kernels, pack(): pl.pallas_call(kernel, grid_spec=pltpu.PrefetchScalarGridSpec(num_scalar_...  5.02 us
  transfers between devices with their start and end apart: 25, of which 16 were waited for; matrix products, arithmetic and copies ran while one was open for 1% of the time, Pallas kernels for 25%

profile of v23, /device:TPU:0, one launch (start us, length us, event | category | flops | bytes accessed | tf_op | source)
XLA Modules:
  0.0 118.3 jit_solution(1842189372352421644)
XLA Ops:
  0.0 0.5 collective-permute-start.3
  0.5 2.5 %pack.2 = (bf16[1552,128]{1,0:T(8,128)(2,1)}, bf16[1552,128]{1,0:T(8,128)(2,1)}, bf16[1552,128]{1,0:T(8,128)(2,1)}) custom-call(s32[1]{0:T(128)} %bitcast.ctx_ref, bf16[1024,512]{1,0:T(8,128)(2,1)} %refs_3_.4, bf16[1024,512]{1,0:T(8,128)(2,1)} %refs_4_.4, bf16[1024,512]{1,0:T(8,128)(2,1)} %refs_5_.4, bf16[1024,512]{1,0:T(8,128)(2,1)} %refs_3_.4, ...), custom_call_target="tpu_custom_call" | custom-call | flops 1024 | bytes 1024 | tf_op jit(solution)/shard_map/pack/pallas_call | solution.py:201
  2.9 2.5 %collective-permute-start = (bf16[1552,128]{1,0:T(8,128)(2,1)}, bf16[1552,128]{1,0:T(8,128)(2,1)S(1)}, u32[]{:S(2)}, u32[]{:S(2)}) collective-permute-start(bf16[1552,128]{1,0:T(8,128)(2,1)} %get-tuple-element.66), channel_id=1, source_target_pairs={{0,8},{8,0},{16,24},{24,16},{1,9},{9,1},{17,25},{25,17},{2,10},{10... | collective-permute-start | bytes 1191944 | tf_op jit(solution)/shard_map/ppermute | solution.py:530
  5.4 1.5 %collective-permute-start.1 = (bf16[1552,128]{1,0:T(8,128)(2,1)}, bf16[1552,128]{1,0:T(8,128)(2,1)S(1)}, u32[]{:S(2)}, u32[]{:S(2)}) collective-permute-start(bf16[1552,128]{1,0:T(8,128)(2,1)} %get-tuple-element.67), channel_id=1, source_target_pairs={{0,16},{8,24},{16,0},{24,8},{1,17},{9,25},{17,1},{25,9},{2,18},{10... | collective-permute-start | bytes 1191944 | tf_op jit(solution)/shard_map/ppermute | solution.py:530
  7.0 0.0 collective-permute-start.2
  7.0 2.5 %pack.3 = (bf16[1536,128]{1,0:T(8,128)(2,1)}, bf16[1536,128]{1,0:T(8,128)(2,1)}, bf16[1536,128]{1,0:T(8,128)(2,1)}) custom-call(s32[1]{0:T(128)} %bitcast.ctx_ref, bf16[1024,512]{1,0:T(8,128)(2,1)} %refs_3_.4, bf16[1024,512]{1,0:T(8,128)(2,1)} %refs_4_.4, bf16[1024,512]{1,0:T(8,128)(2,1)} %refs_5_.4, bf16[1024,512]{1,0:T(8,128)(2,1)} %refs_3_.4, ...), custom_call_target="tpu_custom_call" | custom-call | flops 1024 | bytes 1024 | tf_op jit(solution)/shard_map/pack/pallas_call | solution.py:201
  9.5 2.0 %collective-permute-start.7 = (bf16[1536,128]{1,0:T(8,128)(2,1)}, bf16[1536,128]{1,0:T(8,128)(2,1)S(1)}, u32[]{:S(2)}, u32[]{:S(2)}) collective-permute-start(bf16[1536,128]{1,0:T(8,128)(2,1)} %get-tuple-element.85), channel_id=1, source_target_pairs={{0,8},{8,0},{16,24},{24,16},{1,9},{9,1},{17,25},{25,17},{2,10},{10... | collective-permute-start | bytes 1179656 | tf_op jit(solution)/shard_map/ppermute | solution.py:530
  11.5 1.5 %collective-permute-start.8 = (bf16[1536,128]{1,0:T(8,128)(2,1)}, bf16[1536,128]{1,0:T(8,128)(2,1)S(1)}, u32[]{:S(2)}, u32[]{:S(2)}) collective-permute-start(bf16[1536,128]{1,0:T(8,128)(2,1)} %get-tuple-element.86), channel_id=1, source_target_pairs={{0,16},{8,24},{16,0},{24,8},{1,17},{9,25},{17,1},{25,9},{2,18},{10... | collective-permute-start | bytes 1179656 | tf_op jit(solution)/shard_map/ppermute | solution.py:530
  13.0 0.5 broadcast_xor_fusion.places_ref
  13.5 5.7 %pack_projection.1 = (bf16[512,2048]{1,0:T(8,128)(2,1)}, bf16[512,2048]{1,0:T(8,128)(2,1)}) custom-call(s32[4]{0:T(128)} %broadcast_xor_fusion.places_ref, bf16[512,4096]{1,0:T(8,128)(2,1)} %mine_in.1, bf16[512,4096]{1,0:T(8,128)(2,1)} %collective-permute-done.3.sibling_in), custom_call_target="tpu_custom_call" | custom-call | flops 1024 | bytes 1024 | tf_op jit(solution)/shard_map/pack_projection/pallas_call | solution.py:227
  19.3 6.9 %collective-permute-done.1.refs_5_.refs_8_ = bf16[1552,128]{1,0:T(8,128)(2,1)S(1)} collective-permute-done((bf16[1552,128]{1,0:T(8,128)(2,1)}, bf16[1552,128]{1,0:T(8,128)(2,1)S(1)}, u32[]{:S(2)}, u32[]{:S(2)}) %collective-permute-start.1) | collective-permute-done | bytes 397344 | tf_op jit(solution)/shard_map/ppermute | solution.py:530
  26.2 0.0 collective-permute-done.2.refs_6_.refs_9_
  26.2 6.7 %attend_low.1 = (bf16[512,128]{1,0:T(8,128)(2,1)S(1)}, bf16[512,128]{1,0:T(8,128)(2,1)S(1)}, bf16[512,128]{1,0:T(8,128)(2,1)S(1)}, bf16[512,128]{1,0:T(8,128)(2,1)S(1)}) custom-call(s32[1]{0:T(128)} %bitcast.ctx_ref, bf16[1024,512]{1,0:T(8,128)(2,1)S(1)} %copy-done.2, bf16[1024,512]{1,0:T(8,128)(2,1)S(1)} %copy-done.3, bf16[1024,512]{1,0:T(8,128)(2,1)S(1)} %copy-done.4, ...), custom_call_target="tpu_custom_call" | custom-call | flops 1024 | bytes 1024 | tf_op jit(solution)/shard_map/attend_low/pallas_call | solution.py:418
  33.0 1.0 collective-permute-start.4
  34.0 1.1 collective-permute-start.5
  35.1 1.4 %collective-permute-start.6 = (bf16[512,128]{1,0:T(8,128)(2,1)S(1)}, bf16[512,128]{1,0:T(8,128)(2,1)S(1)}, u32[]{:S(2)}, u32[]{:S(2)}) collective-permute-start(bf16[512,128]{1,0:T(8,128)(2,1)S(1)} %get-tuple-element.84), channel_id=1, source_target_pairs={{0,24},{8,16},{16,8},{24,0},{1,25},{9,17},{17,9},{25,1},{2,26},{10... | collective-permute-start | bytes 393224 | tf_op jit(solution)/shard_map/ppermute | solution.py:530
  36.5 2.7 %collective-permute-done.4.refs_1_ = bf16[512,128]{1,0:T(8,128)(2,1)S(1)} collective-permute-done((bf16[512,128]{1,0:T(8,128)(2,1)S(1)}, bf16[512,128]{1,0:T(8,128)(2,1)S(1)}, u32[]{:S(2)}, u32[]{:S(2)}) %collective-permute-start.4) | collective-permute-done | bytes 131104 | tf_op jit(solution)/shard_map/ppermute | solution.py:530
  39.2 2.1 %collective-permute-done.5.refs_2_ = bf16[512,128]{1,0:T(8,128)(2,1)S(1)} collective-permute-done((bf16[512,128]{1,0:T(8,128)(2,1)S(1)}, bf16[512,128]{1,0:T(8,128)(2,1)S(1)}, u32[]{:S(2)}, u32[]{:S(2)}) %collective-permute-start.5) | collective-permute-done | bytes 131104 | tf_op jit(solution)/shard_map/ppermute | solution.py:530
  41.3 0.1 assemble.2.refs_0_
  41.4 0.1 collective-permute-start.10
  41.4 1.9 %collective-permute-done.10.refs_1_ = bf16[512,512]{1,0:T(8,128)(2,1)S(1)} collective-permute-done((bf16[512,512]{1,0:T(8,128)(2,1)S(1)}, bf16[512,512]{1,0:T(8,128)(2,1)S(1)}, u32[]{:S(2)}, u32[]{:S(2)}) %collective-permute-start.10) | collective-permute-done | bytes 524320 | tf_op jit(solution)/shard_map/ppermute | solution.py:530
  43.3 0.7 project.8
  44.1 1.6 %collective-permute-start.11 = (bf16[512,512]{1,0:T(8,128)(2,1)S(1)}, bf16[512,512]{1,0:T(8,128)(2,1)S(1)}, u32[]{:S(2)}, u32[]{:S(2)}) collective-permute-start(bf16[512,512]{1,0:T(8,128)(2,1)S(1)} %project.8), channel_id=1, source_target_pairs={{0,2},{1,3},{2,0},{3,1},{4,6},{5,7},{6,4},{7,5},{8,10},{9,11},{10,... | collective-permute-start | bytes 1572872 | tf_op jit(solution)/shard_map/ppermute | solution.py:530
  45.7 1.8 %collective-permute-start.9 = (bf16[1536,128]{1,0:T(8,128)(2,1)S(1)}, bf16[1536,128]{1,0:T(8,128)(2,1)S(1)}, u32[]{:S(2)}, u32[]{:S(2)}) collective-permute-start(bf16[1536,128]{1,0:T(8,128)(2,1)S(1)} %copy-done.6), channel_id=1, source_target_pairs={{0,24},{8,16},{16,8},{24,0},{1,25},{9,17},{17,9},{25,1},{2,26},{10... | collective-permute-start | bytes 1179656 | tf_op jit(solution)/shard_map/ppermute | solution.py:530
  47.5 0.7 project.9
  48.2 0.5 collective-permute-start.17
  48.7 0.7 project.10
  49.4 0.7 project.11.refs_0_
  50.2 8.7 %collective-permute-done.11 = bf16[512,512]{1,0:T(8,128)(2,1)S(1)} collective-permute-done((bf16[512,512]{1,0:T(8,128)(2,1)S(1)}, bf16[512,512]{1,0:T(8,128)(2,1)S(1)}, u32[]{:S(2)}, u32[]{:S(2)}) %collective-permute-start.11) | collective-permute-done | bytes 524320 | tf_op jit(solution)/shard_map/ppermute | solution.py:530
  58.9 0.1 add_convert_fusion
  59.0 0.0 collective-permute-done.9.refs_12_
  59.0 2.6 %collective-permute-start.18 = (bf16[512,512]{1,0:T(8,128)(2,1)S(1)}, bf16[512,512]{1,0:T(8,128)(2,1)S(1)}, u32[]{:S(2)}, u32[]{:S(2)}) collective-permute-start(bf16[512,512]{1,0:T(8,128)(2,1)S(1)} %add_convert_fusion), channel_id=1, source_target_pairs={{0,4},{1,5},{2,6},{3,7},{4,0},{5,1},{6,2},{7,3},{8,12},{9,13},{10,... | collective-permute-start | bytes 1572872 | tf_op jit(solution)/shard_map/ppermute | solution.py:530
  61.7 6.1 %attend_high.1 = (bf16[512,128]{1,0:T(8,128)(2,1)S(1)}, bf16[512,128]{1,0:T(8,128)(2,1)S(1)}, bf16[512,128]{1,0:T(8,128)(2,1)S(1)}, bf16[512,128]{1,0:T(8,128)(2,1)S(1)}) custom-call(s32[1]{0:T(128)} %bitcast.ctx_ref, bf16[1024,512]{1,0:T(8,128)(2,1)S(1)} %copy-done.2, bf16[1024,512]{1,0:T(8,128)(2,1)S(1)} %copy-done.3, bf16[1024,512]{1,0:T(8,128)(2,1)S(1)} %copy-done.4, ...), custom_call_target="tpu_custom_call" | custom-call | flops 1024 | bytes 1024 | tf_op jit(solution)/shard_map/attend_high/pallas_call | solution.py:418
  67.8 1.5 %collective-permute-start.12 = (bf16[512,128]{1,0:T(8,128)(2,1)S(1)}, bf16[512,128]{1,0:T(8,128)(2,1)S(1)}, u32[]{:S(2)}, u32[]{:S(2)}) collective-permute-start(bf16[512,128]{1,0:T(8,128)(2,1)S(1)} %get-tuple-element.100), channel_id=1, source_target_pairs={{0,8},{8,0},{16,24},{24,16},{1,9},{9,1},{17,25},{25,17},{2,10},{10... | collective-permute-start | bytes 393224 | tf_op jit(solution)/shard_map/ppermute | solution.py:530
  69.2 1.0 collective-permute-start.13
  70.2 1.1 collective-permute-start.14
  71.3 2.4 %collective-permute-done.12.refs_1_ = bf16[512,128]{1,0:T(8,128)(2,1)S(1)} collective-permute-done((bf16[512,128]{1,0:T(8,128)(2,1)S(1)}, bf16[512,128]{1,0:T(8,128)(2,1)S(1)}, u32[]{:S(2)}, u32[]{:S(2)}) %collective-permute-start.12) | collective-permute-done | bytes 131104 | tf_op jit(solution)/shard_map/ppermute | solution.py:530
  73.7 0.7 collective-permute-done.13.refs_2_
  74.4 1.6 %collective-permute-done.14.refs_3_ = bf16[512,128]{1,0:T(8,128)(2,1)S(1)} collective-permute-done((bf16[512,128]{1,0:T(8,128)(2,1)S(1)}, bf16[512,128]{1,0:T(8,128)(2,1)S(1)}, u32[]{:S(2)}, u32[]{:S(2)}) %collective-permute-start.14) | collective-permute-done | bytes 131104 | tf_op jit(solution)/shard_map/ppermute | solution.py:530
  76.0 0.1 assemble.3
  76.1 0.1 collective-permute-start.15
  76.2 0.5 collective-permute-start.16
  76.7 1.0 collective-permute-done.15.refs_2_
  77.7 0.4 collective-permute-done.16.refs_3_
  78.1 0.7 project.15
  78.8 0.8 collective-permute-done.17.refs_1_
  79.6 4.0 %collective-permute-done.18.refs_2_ = bf16[512,512]{1,0:T(8,128)(2,1)S(1)} collective-permute-done((bf16[512,512]{1,0:T(8,128)(2,1)S(1)}, bf16[512,512]{1,0:T(8,128)(2,1)S(1)}, u32[]{:S(2)}, u32[]{:S(2)}) %collective-permute-start.18) | collective-permute-done | bytes 524320 | tf_op jit(solution)/shard_map/ppermute | solution.py:530
  83.6 0.8 collective-permute-start.19
  84.4 1.3 %collective-permute-start.20 = (bf16[256,512]{1,0:T(8,128)(2,1)S(1)}, bf16[256,512]{1,0:T(8,128)(2,1)S(1)}, u32[]{:S(2)}, u32[]{:S(2)}) collective-permute-start(bf16[256,512]{1,0:T(8,128)(2,1)S(1)} %get-tuple-element.115), channel_id=1, source_target_pairs={{0,2},{1,3},{2,0},{3,1},{4,6},{5,7},{6,4},{7,5},{8,10},{9,11},{10,... | collective-permute-start | bytes 786440 | tf_op jit(solution)/shard_map/ppermute | solution.py:530
  85.7 0.7 project.13
  86.4 0.7 project.14
  87.1 4.9 %collective-permute-done.19 = bf16[256,512]{1,0:T(8,128)(2,1)S(1)} collective-permute-done((bf16[256,512]{1,0:T(8,128)(2,1)S(1)}, bf16[256,512]{1,0:T(8,128)(2,1)S(1)}, u32[]{:S(2)}, u32[]{:S(2)}) %collective-permute-start.19) | collective-permute-done | bytes 262176 | tf_op jit(solution)/shard_map/ppermute | solution.py:530
  92.0 0.1 add_convert_fusion.2
  92.1 3.0 %collective-permute-done.20 = bf16[256,512]{1,0:T(8,128)(2,1)S(1)} collective-permute-done((bf16[256,512]{1,0:T(8,128)(2,1)S(1)}, bf16[256,512]{1,0:T(8,128)(2,1)S(1)}, u32[]{:S(2)}, u32[]{:S(2)}) %collective-permute-start.20) | collective-permute-done | bytes 262176 | tf_op jit(solution)/shard_map/ppermute | solution.py:530
  95.2 0.1 add_convert_fusion.1
  95.2 1.3 %collective-permute-start.21 = (bf16[256,512]{1,0:T(8,128)(2,1)S(1)}, bf16[256,512]{1,0:T(8,128)(2,1)S(1)}, u32[]{:S(2)}, u32[]{:S(2)}) collective-permute-start(bf16[256,512]{1,0:T(8,128)(2,1)S(1)} %get-tuple-element.116), channel_id=1, source_target_pairs={{0,2},{1,3},{2,0},{3,1},{4,6},{5,7},{6,4},{7,5},{8,10},{9,11},{10,... | collective-permute-start | bytes 786440 | tf_op jit(solution)/shard_map/ppermute | solution.py:530
  96.5 0.8 collective-permute-start.22
  97.3 2.6 %collective-permute-start.23 = (bf16[256,512]{1,0:T(8,128)(2,1)S(1)}, bf16[256,512]{1,0:T(8,128)(2,1)S(1)}, u32[]{:S(2)}, u32[]{:S(2)}) collective-permute-start(bf16[256,512]{1,0:T(8,128)(2,1)S(1)} %add_convert_fusion.2), channel_id=1, source_target_pairs={{0,4},{1,5},{2,6},{3,7},{4,0},{5,1},{6,2},{7,3},{8,12},{9,13},{10,... | collective-permute-start | bytes 786440 | tf_op jit(solution)/shard_map/ppermute | solution.py:530
  99.9 0.3 collective-permute-start.24
  100.2 0.7 project.12
  101.0 1.0 finish.2.refs_6_
  102.0 12.0 %collective-permute-done.21.refs_2_ = bf16[256,512]{1,0:T(8,128)(2,1)S(1)} collective-permute-done((bf16[256,512]{1,0:T(8,128)(2,1)S(1)}, bf16[256,512]{1,0:T(8,128)(2,1)S(1)}, u32[]{:S(2)}, u32[]{:S(2)}) %collective-permute-start.21) | collective-permute-done | bytes 262176 | tf_op jit(solution)/shard_map/ppermute | solution.py:530
  113.9 3.4 %collective-permute-done.22.refs_3_ = bf16[256,512]{1,0:T(8,128)(2,1)S(1)} collective-permute-done((bf16[256,512]{1,0:T(8,128)(2,1)S(1)}, bf16[256,512]{1,0:T(8,128)(2,1)S(1)}, u32[]{:S(2)}, u32[]{:S(2)}) %collective-permute-start.22) | collective-permute-done | bytes 262176 | tf_op jit(solution)/shard_map/ppermute | solution.py:530
  117.3 1.0 finish.3
  (23 shorter events, 0.0 us)
Async XLA Ops:
  0.0 11.5 %collective-permute-start.3 = (bf16[512,4096]{1,0:T(8,128)(2,1)}, bf16[512,4096]{1,0:T(8,128)(2,1)}, u32[]{:S(2)}, u32[]{:S(2)}) collective-permute-start(bf16[512,4096]{1,0:T(8,128)(2,1)} %mine_in.1), channel_id=1, source_target_pairs={{0,1},{1,0},{2,3},{3,2},{4,5},{5,4},{6,7},{7,6},{8,9},{9,8},{10,11... | collective-permute-start | bytes 12582920 | tf_op jit(solution)/shard_map/ppermute | solution.py:530
  2.9 10.0 %copy-start.7 = (s32[4]{0:T(128)S(1)}, s32[4]{0:T(128)}, u32[]{:S(2)}) copy-start(s32[4]{0:T(128)} %constant.13) | copy-start | bytes 52
  2.9 16.3 %collective-permute-start = (bf16[1552,128]{1,0:T(8,128)(2,1)}, bf16[1552,128]{1,0:T(8,128)(2,1)S(1)}, u32[]{:S(2)}, u32[]{:S(2)}) collective-permute-start(bf16[1552,128]{1,0:T(8,128)(2,1)} %get-tuple-element.66), channel_id=1, source_target_pairs={{0,8},{8,0},{16,24},{24,16},{1,9},{9,1},{17,25},{25,17},{2,10},{10... | collective-permute-start | bytes 1191944 | tf_op jit(solution)/shard_map/ppermute | solution.py:530
  5.4 20.8 %collective-permute-start.1 = (bf16[1552,128]{1,0:T(8,128)(2,1)}, bf16[1552,128]{1,0:T(8,128)(2,1)S(1)}, u32[]{:S(2)}, u32[]{:S(2)}) collective-permute-start(bf16[1552,128]{1,0:T(8,128)(2,1)} %get-tuple-element.67), channel_id=1, source_target_pairs={{0,16},{8,24},{16,0},{24,8},{1,17},{9,25},{17,1},{25,9},{2,18},{10... | collective-permute-start | bytes 1191944 | tf_op jit(solution)/shard_map/ppermute | solution.py:530
  7.0 19.2 %collective-permute-start.2 = (bf16[1552,128]{1,0:T(8,128)(2,1)}, bf16[1552,128]{1,0:T(8,128)(2,1)S(1)}, u32[]{:S(2)}, u32[]{:S(2)}) collective-permute-start(bf16[1552,128]{1,0:T(8,128)(2,1)} %get-tuple-element.68), channel_id=1, source_target_pairs={{0,24},{8,16},{16,8},{24,0},{1,25},{9,17},{17,9},{25,1},{2,26},{10... | collective-permute-start | bytes 1191944 | tf_op jit(solution)/shard_map/ppermute | solution.py:530
  9.5 27.0 %collective-permute-start.7 = (bf16[1536,128]{1,0:T(8,128)(2,1)}, bf16[1536,128]{1,0:T(8,128)(2,1)S(1)}, u32[]{:S(2)}, u32[]{:S(2)}) collective-permute-start(bf16[1536,128]{1,0:T(8,128)(2,1)} %get-tuple-element.85), channel_id=1, source_target_pairs={{0,8},{8,0},{16,24},{24,16},{1,9},{9,1},{17,25},{25,17},{2,10},{10... | collective-permute-start | bytes 1179656 | tf_op jit(solution)/shard_map/ppermute | solution.py:530
  11.5 25.1 %collective-permute-start.8 = (bf16[1536,128]{1,0:T(8,128)(2,1)}, bf16[1536,128]{1,0:T(8,128)(2,1)S(1)}, u32[]{:S(2)}, u32[]{:S(2)}) collective-permute-start(bf16[1536,128]{1,0:T(8,128)(2,1)} %get-tuple-element.86), channel_id=1, source_target_pairs={{0,16},{8,24},{16,0},{24,8},{1,17},{9,25},{17,1},{25,9},{2,18},{10... | collective-permute-start | bytes 1179656 | tf_op jit(solution)/shard_map/ppermute | solution.py:530
  13.5 12.7 %copy-start.2 = (bf16[1024,512]{1,0:T(8,128)(2,1)S(1)}, bf16[1024,512]{1,0:T(8,128)(2,1)}, u32[]{:S(2)}) copy-start(bf16[1024,512]{1,0:T(8,128)(2,1)} %refs_3_.4) | copy-start | bytes 3145732
  13.5 12.7 %copy-start.3 = (bf16[1024,512]{1,0:T(8,128)(2,1)S(1)}, bf16[1024,512]{1,0:T(8,128)(2,1)}, u32[]{:S(2)}) copy-start(bf16[1024,512]{1,0:T(8,128)(2,1)} %refs_4_.4) | copy-start | bytes 3145732
  13.5 12.7 %copy-start.4 = (bf16[1024,512]{1,0:T(8,128)(2,1)S(1)}, bf16[1024,512]{1,0:T(8,128)(2,1)}, u32[]{:S(2)}) copy-start(bf16[1024,512]{1,0:T(8,128)(2,1)} %refs_5_.4) | copy-start | bytes 3145732
  13.5 12.7 %copy-start.5 = (s32[1024]{0:T(1024)S(1)}, s32[1024]{0:T(1024)}, u32[]{:S(2)}) copy-start(s32[1024]{0:T(1024)} %param.9) | copy-start | bytes 12292
  19.3 24.1 %copy-start = (bf16[512,2048]{1,0:T(8,128)(2,1)S(1)}, bf16[512,2048]{1,0:T(8,128)(2,1)}, u32[]{:S(2)}) copy-start(bf16[512,2048]{1,0:T(8,128)(2,1)} %get-tuple-element.94.refs_2_.refs_4_) | copy-start | bytes 6291460
  19.3 24.1 %copy-start.1 = (bf16[512,2048]{1,0:T(8,128)(2,1)S(1)}, bf16[512,2048]{1,0:T(8,128)(2,1)}, u32[]{:S(2)}) copy-start(bf16[512,2048]{1,0:T(8,128)(2,1)} %get-tuple-element.95.refs_3_.refs_5_) | copy-start | bytes 6291460
  33.0 12.7 %copy-start.6 = (bf16[1536,128]{1,0:T(8,128)(2,1)S(1)}, bf16[1536,128]{1,0:T(8,128)(2,1)}, u32[]{:S(2)}) copy-start(bf16[1536,128]{1,0:T(8,128)(2,1)} %get-tuple-element.89) | copy-start | bytes 1179652
  33.0 6.2 %collective-permute-start.4 = (bf16[512,128]{1,0:T(8,128)(2,1)S(1)}, bf16[512,128]{1,0:T(8,128)(2,1)S(1)}, u32[]{:S(2)}, u32[]{:S(2)}) collective-permute-start(bf16[512,128]{1,0:T(8,128)(2,1)S(1)} %get-tuple-element.82), channel_id=1, source_target_pairs={{0,8},{8,0},{16,24},{24,16},{1,9},{9,1},{17,25},{25,17},{2,10},{10... | collective-permute-start | bytes 393224 | tf_op jit(solution)/shard_map/ppermute | solution.py:530
  34.0 7.3 %collective-permute-start.5 = (bf16[512,128]{1,0:T(8,128)(2,1)S(1)}, bf16[512,128]{1,0:T(8,128)(2,1)S(1)}, u32[]{:S(2)}, u32[]{:S(2)}) collective-permute-start(bf16[512,128]{1,0:T(8,128)(2,1)S(1)} %get-tuple-element.83), channel_id=1, source_target_pairs={{0,16},{8,24},{16,0},{24,8},{1,17},{9,25},{17,1},{25,9},{2,18},{10... | collective-permute-start | bytes 393224 | tf_op jit(solution)/shard_map/ppermute | solution.py:530
  35.1 6.2 %collective-permute-start.6 = (bf16[512,128]{1,0:T(8,128)(2,1)S(1)}, bf16[512,128]{1,0:T(8,128)(2,1)S(1)}, u32[]{:S(2)}, u32[]{:S(2)}) collective-permute-start(bf16[512,128]{1,0:T(8,128)(2,1)S(1)} %get-tuple-element.84), channel_id=1, source_target_pairs={{0,24},{8,16},{16,8},{24,0},{1,25},{9,17},{17,9},{25,1},{2,26},{10... | collective-permute-start | bytes 393224 | tf_op jit(solution)/shard_map/ppermute | solution.py:530
  41.4 2.0 %collective-permute-start.10 = (bf16[512,512]{1,0:T(8,128)(2,1)S(1)}, bf16[512,512]{1,0:T(8,128)(2,1)S(1)}, u32[]{:S(2)}, u32[]{:S(2)}) collective-permute-start(bf16[512,512]{1,0:T(8,128)(2,1)S(1)} %assemble.2.refs_0_), channel_id=1, source_target_pairs={{0,1},{1,0},{2,3},{3,2},{4,5},{5,4},{6,7},{7,6},{8,9},{9,8},{10,11... | collective-permute-start | bytes 1572872 | tf_op jit(solution)/shard_map/ppermute | solution.py:530
  44.1 14.8 %collective-permute-start.11 = (bf16[512,512]{1,0:T(8,128)(2,1)S(1)}, bf16[512,512]{1,0:T(8,128)(2,1)S(1)}, u32[]{:S(2)}, u32[]{:S(2)}) collective-permute-start(bf16[512,512]{1,0:T(8,128)(2,1)S(1)} %project.8), channel_id=1, source_target_pairs={{0,2},{1,3},{2,0},{3,1},{4,6},{5,7},{6,4},{7,5},{8,10},{9,11},{10,... | collective-permute-start | bytes 1572872 | tf_op jit(solution)/shard_map/ppermute | solution.py:530
  45.7 13.3 %collective-permute-start.9 = (bf16[1536,128]{1,0:T(8,128)(2,1)S(1)}, bf16[1536,128]{1,0:T(8,128)(2,1)S(1)}, u32[]{:S(2)}, u32[]{:S(2)}) collective-permute-start(bf16[1536,128]{1,0:T(8,128)(2,1)S(1)} %copy-done.6), channel_id=1, source_target_pairs={{0,24},{8,16},{16,8},{24,0},{1,25},{9,17},{17,9},{25,1},{2,26},{10... | collective-permute-start | bytes 1179656 | tf_op jit(solution)/shard_map/ppermute | solution.py:530
  48.2 31.4 %collective-permute-start.17 = (bf16[512,512]{1,0:T(8,128)(2,1)S(1)}, bf16[512,512]{1,0:T(8,128)(2,1)S(1)}, u32[]{:S(2)}, u32[]{:S(2)}) collective-permute-start(bf16[512,512]{1,0:T(8,128)(2,1)S(1)} %project.9), channel_id=1, source_target_pairs={{0,2},{1,3},{2,0},{3,1},{4,6},{5,7},{6,4},{7,5},{8,10},{9,11},{10,... | collective-permute-start | bytes 1572872 | tf_op jit(solution)/shard_map/ppermute | solution.py:530
  59.0 24.6 %collective-permute-start.18 = (bf16[512,512]{1,0:T(8,128)(2,1)S(1)}, bf16[512,512]{1,0:T(8,128)(2,1)S(1)}, u32[]{:S(2)}, u32[]{:S(2)}) collective-permute-start(bf16[512,512]{1,0:T(8,128)(2,1)S(1)} %add_convert_fusion), channel_id=1, source_target_pairs={{0,4},{1,5},{2,6},{3,7},{4,0},{5,1},{6,2},{7,3},{8,12},{9,13},{10,... | collective-permute-start | bytes 1572872 | tf_op jit(solution)/shard_map/ppermute | solution.py:530
  67.8 6.0 %collective-permute-start.12 = (bf16[512,128]{1,0:T(8,128)(2,1)S(1)}, bf16[512,128]{1,0:T(8,128)(2,1)S(1)}, u32[]{:S(2)}, u32[]{:S(2)}) collective-permute-start(bf16[512,128]{1,0:T(8,128)(2,1)S(1)} %get-tuple-element.100), channel_id=1, source_target_pairs={{0,8},{8,0},{16,24},{24,16},{1,9},{9,1},{17,25},{25,17},{2,10},{10... | collective-permute-start | bytes 393224 | tf_op jit(solution)/shard_map/ppermute | solution.py:530
  69.2 5.2 %collective-permute-start.13 = (bf16[512,128]{1,0:T(8,128)(2,1)S(1)}, bf16[512,128]{1,0:T(8,128)(2,1)S(1)}, u32[]{:S(2)}, u32[]{:S(2)}) collective-permute-start(bf16[512,128]{1,0:T(8,128)(2,1)S(1)} %get-tuple-element.101), channel_id=1, source_target_pairs={{0,16},{8,24},{16,0},{24,8},{1,17},{9,25},{17,1},{25,9},{2,18},{10... | collective-permute-start | bytes 393224 | tf_op jit(solution)/shard_map/ppermute | solution.py:530
  70.2 5.9 %collective-permute-start.14 = (bf16[512,128]{1,0:T(8,128)(2,1)S(1)}, bf16[512,128]{1,0:T(8,128)(2,1)S(1)}, u32[]{:S(2)}, u32[]{:S(2)}) collective-permute-start(bf16[512,128]{1,0:T(8,128)(2,1)S(1)} %get-tuple-element.102), channel_id=1, source_target_pairs={{0,24},{8,16},{16,8},{24,0},{1,25},{9,17},{17,9},{25,1},{2,26},{10... | collective-permute-start | bytes 393224 | tf_op jit(solution)/shard_map/ppermute | solution.py:530
  76.1 1.6 %collective-permute-start.15 = (bf16[256,512]{1,0:T(8,128)(2,1)S(1)}, bf16[256,512]{1,0:T(8,128)(2,1)S(1)}, u32[]{:S(2)}, u32[]{:S(2)}) collective-permute-start(bf16[256,512]{1,0:T(8,128)(2,1)S(1)} %get-tuple-element.103.refs_0_), channel_id=1, source_target_pairs={{0,1},{1,0},{2,3},{3,2},{4,5},{5,4},{6,7},{7,6},{8,9},{9,8},{10,11... | collective-permute-start | bytes 786440 | tf_op jit(solution)/shard_map/ppermute | solution.py:530
  76.2 1.9 %collective-permute-start.16 = (bf16[256,512]{1,0:T(8,128)(2,1)S(1)}, bf16[256,512]{1,0:T(8,128)(2,1)S(1)}, u32[]{:S(2)}, u32[]{:S(2)}) collective-permute-start(bf16[256,512]{1,0:T(8,128)(2,1)S(1)} %get-tuple-element.104.refs_1_), channel_id=1, source_target_pairs={{0,1},{1,0},{2,3},{3,2},{4,5},{5,4},{6,7},{7,6},{8,9},{9,8},{10,11... | collective-permute-start | bytes 786440 | tf_op jit(solution)/shard_map/ppermute | solution.py:530
  83.6 8.4 %collective-permute-start.19 = (bf16[256,512]{1,0:T(8,128)(2,1)S(1)}, bf16[256,512]{1,0:T(8,128)(2,1)S(1)}, u32[]{:S(2)}, u32[]{:S(2)}) collective-permute-start(bf16[256,512]{1,0:T(8,128)(2,1)S(1)} %get-tuple-element.113), channel_id=1, source_target_pairs={{0,2},{1,3},{2,0},{3,1},{4,6},{5,7},{6,4},{7,5},{8,10},{9,11},{10,... | collective-permute-start | bytes 786440 | tf_op jit(solution)/shard_map/ppermute | solution.py:530
  84.4 10.8 %collective-permute-start.20 = (bf16[256,512]{1,0:T(8,128)(2,1)S(1)}, bf16[256,512]{1,0:T(8,128)(2,1)S(1)}, u32[]{:S(2)}, u32[]{:S(2)}) collective-permute-start(bf16[256,512]{1,0:T(8,128)(2,1)S(1)} %get-tuple-element.115), channel_id=1, source_target_pairs={{0,2},{1,3},{2,0},{3,1},{4,6},{5,7},{6,4},{7,5},{8,10},{9,11},{10,... | collective-permute-start | bytes 786440 | tf_op jit(solution)/shard_map/ppermute | solution.py:530
  95.2 18.7 %collective-permute-start.21 = (bf16[256,512]{1,0:T(8,128)(2,1)S(1)}, bf16[256,512]{1,0:T(8,128)(2,1)S(1)}, u32[]{:S(2)}, u32[]{:S(2)}) collective-permute-start(bf16[256,512]{1,0:T(8,128)(2,1)S(1)} %get-tuple-element.116), channel_id=1, source_target_pairs={{0,2},{1,3},{2,0},{3,1},{4,6},{5,7},{6,4},{7,5},{8,10},{9,11},{10,... | collective-permute-start | bytes 786440 | tf_op jit(solution)/shard_map/ppermute | solution.py:530
  96.5 20.8 %collective-permute-start.22 = (bf16[256,512]{1,0:T(8,128)(2,1)S(1)}, bf16[256,512]{1,0:T(8,128)(2,1)S(1)}, u32[]{:S(2)}, u32[]{:S(2)}) collective-permute-start(bf16[256,512]{1,0:T(8,128)(2,1)S(1)} %get-tuple-element.117), channel_id=1, source_target_pairs={{0,2},{1,3},{2,0},{3,1},{4,6},{5,7},{6,4},{7,5},{8,10},{9,11},{10,... | collective-permute-start | bytes 786440 | tf_op jit(solution)/shard_map/ppermute | solution.py:530
  97.3 20.0 %collective-permute-start.23 = (bf16[256,512]{1,0:T(8,128)(2,1)S(1)}, bf16[256,512]{1,0:T(8,128)(2,1)S(1)}, u32[]{:S(2)}, u32[]{:S(2)}) collective-permute-start(bf16[256,512]{1,0:T(8,128)(2,1)S(1)} %add_convert_fusion.2), channel_id=1, source_target_pairs={{0,4},{1,5},{2,6},{3,7},{4,0},{5,1},{6,2},{7,3},{8,12},{9,13},{10,... | collective-permute-start | bytes 786440 | tf_op jit(solution)/shard_map/ppermute | solution.py:530
  99.9 17.4 %collective-permute-start.24 = (bf16[256,512]{1,0:T(8,128)(2,1)S(1)}, bf16[256,512]{1,0:T(8,128)(2,1)S(1)}, u32[]{:S(2)}, u32[]{:S(2)}) collective-permute-start(bf16[256,512]{1,0:T(8,128)(2,1)S(1)} %add_convert_fusion.1), channel_id=1, source_target_pairs={{0,4},{1,5},{2,6},{3,7},{4,0},{5,1},{6,2},{7,3},{8,12},{9,13},{10,... | collective-permute-start | bytes 786440 | tf_op jit(solution)/shard_map/ppermute | solution.py:530

commit v24 on v14

--- a/solution.py
+++ b/solution.py
@@ -583,7 +583,7 @@
     far = to_next(late[0], 1)
     passed = [add(*both) for both in zip(late[2], far)]
     across = to_next(passed, 2)
-    late[1], passed = tie(late[1], passed)
+    late[1], passed[0] = tie(late[1], passed[0])
     near_sum = to_next(late[1], 1)
     return finish(1, [late[3], near_sum, across], result)
 

time: 118 us -> 117 us (level); the launches traced: 117 us -> 118 us
  Pallas kernels: 28.9 us -> 30.8 us
    pallas_call x2, Pallas kernels: 10.2 us -> 12.1 us  [attend(): pl.pallas_call(kernel, grid_spec=pltpu.PrefetchScalarGridSpec(num_scalar_...]
  transfers between devices with their start and end apart: 25 -> 25, of which waited for: 16 -> 16; matrix products, arithmetic and copies ran while one was open for 1% -> 1% of each run, Pallas kernels for 23% -> 25%
where the time goes in v24:
time: 117 us; the launch traced here: 118 us
  waiting for transfers between devices  57 us (49%)
  Pallas kernels  30.8 us (26%)
  starting transfers between devices  28.8 us (25%)
    ppermute x25, waiting for transfers between devices, swap(): lax.ppermute(value, axis, [(source, source ^ distance) for source in rang...  57 us
    ppermute x25, starting transfers between devices, swap(): lax.ppermute(value, axis, [(source, source ^ distance) for source in rang...  28.8 us
    pallas_call x2, Pallas kernels, attend(): pl.pallas_call(kernel, grid_spec=pltpu.PrefetchScalarGridSpec(num_scalar_...  12.1 us
    pallas_call x1, Pallas kernels, pack_projection(): pl.pallas_call(kernel, grid_spec=pltpu.PrefetchScalarGridSpec(num_scalar_...  5.74 us
    pallas_call x8, Pallas kernels, project(): pl.pallas_call(kernel, grid=(1,), in_specs=[attended] * (2 * parts) + [we...  5.7 us
    pallas_call x2, Pallas kernels, pack(): pl.pallas_call(kernel, grid_spec=pltpu.PrefetchScalarGridSpec(num_scalar_...  5.02 us
  transfers between devices with their start and end apart: 25, of which 16 were waited for; matrix products, arithmetic and copies ran while one was open for 1% of the time, Pallas kernels for 25%

profile of v24, /device:TPU:0, one launch (start us, length us, event | category | flops | bytes accessed | tf_op | source)
XLA Modules:
  0.0 117.6 jit_solution(9910479988971867854)
XLA Ops:
  0.0 0.5 collective-permute-start.3
  0.5 2.5 %pack.2 = (bf16[1552,128]{1,0:T(8,128)(2,1)}, bf16[1552,128]{1,0:T(8,128)(2,1)}, bf16[1552,128]{1,0:T(8,128)(2,1)}) custom-call(s32[1]{0:T(128)} %bitcast.ctx_ref, bf16[1024,512]{1,0:T(8,128)(2,1)} %refs_3_.4, bf16[1024,512]{1,0:T(8,128)(2,1)} %refs_4_.4, bf16[1024,512]{1,0:T(8,128)(2,1)} %refs_5_.4, bf16[1024,512]{1,0:T(8,128)(2,1)} %refs_3_.4, ...), custom_call_target="tpu_custom_call" | custom-call | flops 1024 | bytes 1024 | tf_op jit(solution)/shard_map/pack/pallas_call | solution.py:201
  2.9 2.5 %collective-permute-start = (bf16[1552,128]{1,0:T(8,128)(2,1)}, bf16[1552,128]{1,0:T(8,128)(2,1)S(1)}, u32[]{:S(2)}, u32[]{:S(2)}) collective-permute-start(bf16[1552,128]{1,0:T(8,128)(2,1)} %get-tuple-element.66), channel_id=1, source_target_pairs={{0,8},{8,0},{16,24},{24,16},{1,9},{9,1},{17,25},{25,17},{2,10},{10... | collective-permute-start | bytes 1191944 | tf_op jit(solution)/shard_map/ppermute | solution.py:521
  5.4 1.5 %collective-permute-start.1 = (bf16[1552,128]{1,0:T(8,128)(2,1)}, bf16[1552,128]{1,0:T(8,128)(2,1)S(1)}, u32[]{:S(2)}, u32[]{:S(2)}) collective-permute-start(bf16[1552,128]{1,0:T(8,128)(2,1)} %get-tuple-element.67), channel_id=1, source_target_pairs={{0,16},{8,24},{16,0},{24,8},{1,17},{9,25},{17,1},{25,9},{2,18},{10... | collective-permute-start | bytes 1191944 | tf_op jit(solution)/shard_map/ppermute | solution.py:521
  7.0 0.0 collective-permute-start.2
  7.0 2.5 %pack.3 = (bf16[1536,128]{1,0:T(8,128)(2,1)}, bf16[1536,128]{1,0:T(8,128)(2,1)}, bf16[1536,128]{1,0:T(8,128)(2,1)}) custom-call(s32[1]{0:T(128)} %bitcast.ctx_ref, bf16[1024,512]{1,0:T(8,128)(2,1)} %refs_3_.4, bf16[1024,512]{1,0:T(8,128)(2,1)} %refs_4_.4, bf16[1024,512]{1,0:T(8,128)(2,1)} %refs_5_.4, bf16[1024,512]{1,0:T(8,128)(2,1)} %refs_3_.4, ...), custom_call_target="tpu_custom_call" | custom-call | flops 1024 | bytes 1024 | tf_op jit(solution)/shard_map/pack/pallas_call | solution.py:201
  9.5 2.0 %collective-permute-start.7 = (bf16[1536,128]{1,0:T(8,128)(2,1)}, bf16[1536,128]{1,0:T(8,128)(2,1)S(1)}, u32[]{:S(2)}, u32[]{:S(2)}) collective-permute-start(bf16[1536,128]{1,0:T(8,128)(2,1)} %get-tuple-element.85), channel_id=1, source_target_pairs={{0,8},{8,0},{16,24},{24,16},{1,9},{9,1},{17,25},{25,17},{2,10},{10... | collective-permute-start | bytes 1179656 | tf_op jit(solution)/shard_map/ppermute | solution.py:521
  11.5 0.0 collective-permute-done.3.sibling_in
  11.5 1.5 %collective-permute-start.8 = (bf16[1536,128]{1,0:T(8,128)(2,1)}, bf16[1536,128]{1,0:T(8,128)(2,1)S(1)}, u32[]{:S(2)}, u32[]{:S(2)}) collective-permute-start(bf16[1536,128]{1,0:T(8,128)(2,1)} %get-tuple-element.86), channel_id=1, source_target_pairs={{0,16},{8,24},{16,0},{24,8},{1,17},{9,25},{17,1},{25,9},{2,18},{10... | collective-permute-start | bytes 1179656 | tf_op jit(solution)/shard_map/ppermute | solution.py:521
  13.0 0.5 broadcast_xor_fusion.places_ref
  13.5 5.7 %pack_projection.1 = (bf16[512,2048]{1,0:T(8,128)(2,1)}, bf16[512,2048]{1,0:T(8,128)(2,1)}) custom-call(s32[4]{0:T(128)} %broadcast_xor_fusion.places_ref, bf16[512,4096]{1,0:T(8,128)(2,1)} %mine_in.1, bf16[512,4096]{1,0:T(8,128)(2,1)} %collective-permute-done.3.sibling_in), custom_call_target="tpu_custom_call" | custom-call | flops 1024 | bytes 1024 | tf_op jit(solution)/shard_map/pack_projection/pallas_call | solution.py:227
  19.3 0.0 collective-permute-done.refs_4_.refs_7_
  19.3 6.9 %collective-permute-done.1.refs_5_.refs_8_ = bf16[1552,128]{1,0:T(8,128)(2,1)S(1)} collective-permute-done((bf16[1552,128]{1,0:T(8,128)(2,1)}, bf16[1552,128]{1,0:T(8,128)(2,1)S(1)}, u32[]{:S(2)}, u32[]{:S(2)}) %collective-permute-start.1) | collective-permute-done | bytes 397344 | tf_op jit(solution)/shard_map/ppermute | solution.py:521
  26.2 6.0 %attend_low.1 = (bf16[512,128]{1,0:T(8,128)(2,1)S(1)}, bf16[512,128]{1,0:T(8,128)(2,1)S(1)}, bf16[512,128]{1,0:T(8,128)(2,1)S(1)}, bf16[512,128]{1,0:T(8,128)(2,1)S(1)}) custom-call(s32[1]{0:T(128)} %bitcast.ctx_ref, bf16[1024,512]{1,0:T(8,128)(2,1)S(1)} %copy-done.2, bf16[1024,512]{1,0:T(8,128)(2,1)S(1)} %copy-done.3, bf16[1024,512]{1,0:T(8,128)(2,1)S(1)} %copy-done.4, ...), custom_call_target="tpu_custom_call" | custom-call | flops 1024 | bytes 1024 | tf_op jit(solution)/shard_map/attend_low/pallas_call | solution.py:409
  32.2 1.0 collective-permute-start.4
  33.3 1.1 collective-permute-start.5
  34.4 1.4 %collective-permute-start.6 = (bf16[512,128]{1,0:T(8,128)(2,1)S(1)}, bf16[512,128]{1,0:T(8,128)(2,1)S(1)}, u32[]{:S(2)}, u32[]{:S(2)}) collective-permute-start(bf16[512,128]{1,0:T(8,128)(2,1)S(1)} %get-tuple-element.84), channel_id=1, source_target_pairs={{0,24},{8,16},{16,8},{24,0},{1,25},{9,17},{17,9},{25,1},{2,26},{10... | collective-permute-start | bytes 393224 | tf_op jit(solution)/shard_map/ppermute | solution.py:521
  35.8 2.6 %collective-permute-done.4.refs_1_ = bf16[512,128]{1,0:T(8,128)(2,1)S(1)} collective-permute-done((bf16[512,128]{1,0:T(8,128)(2,1)S(1)}, bf16[512,128]{1,0:T(8,128)(2,1)S(1)}, u32[]{:S(2)}, u32[]{:S(2)}) %collective-permute-start.4) | collective-permute-done | bytes 131104 | tf_op jit(solution)/shard_map/ppermute | solution.py:521
  38.4 2.1 %collective-permute-done.5.refs_2_ = bf16[512,128]{1,0:T(8,128)(2,1)S(1)} collective-permute-done((bf16[512,128]{1,0:T(8,128)(2,1)S(1)}, bf16[512,128]{1,0:T(8,128)(2,1)S(1)}, u32[]{:S(2)}, u32[]{:S(2)}) %collective-permute-start.5) | collective-permute-done | bytes 131104 | tf_op jit(solution)/shard_map/ppermute | solution.py:521
  40.5 0.1 assemble.2.refs_0_
  40.6 0.1 collective-permute-start.10
  40.7 1.9 %collective-permute-done.10.refs_1_ = bf16[512,512]{1,0:T(8,128)(2,1)S(1)} collective-permute-done((bf16[512,512]{1,0:T(8,128)(2,1)S(1)}, bf16[512,512]{1,0:T(8,128)(2,1)S(1)}, u32[]{:S(2)}, u32[]{:S(2)}) %collective-permute-start.10) | collective-permute-done | bytes 524320 | tf_op jit(solution)/shard_map/ppermute | solution.py:521
  42.6 0.7 project.8
  43.3 1.6 %collective-permute-start.11 = (bf16[512,512]{1,0:T(8,128)(2,1)S(1)}, bf16[512,512]{1,0:T(8,128)(2,1)S(1)}, u32[]{:S(2)}, u32[]{:S(2)}) collective-permute-start(bf16[512,512]{1,0:T(8,128)(2,1)S(1)} %project.8), channel_id=1, source_target_pairs={{0,2},{1,3},{2,0},{3,1},{4,6},{5,7},{6,4},{7,5},{8,10},{9,11},{10,... | collective-permute-start | bytes 1572872 | tf_op jit(solution)/shard_map/ppermute | solution.py:521
  45.0 1.8 %collective-permute-start.9 = (bf16[1536,128]{1,0:T(8,128)(2,1)S(1)}, bf16[1536,128]{1,0:T(8,128)(2,1)S(1)}, u32[]{:S(2)}, u32[]{:S(2)}) collective-permute-start(bf16[1536,128]{1,0:T(8,128)(2,1)S(1)} %copy-done.6), channel_id=1, source_target_pairs={{0,24},{8,16},{16,8},{24,0},{1,25},{9,17},{17,9},{25,1},{2,26},{10... | collective-permute-start | bytes 1179656 | tf_op jit(solution)/shard_map/ppermute | solution.py:521
  46.7 0.7 project.9
  47.5 0.5 collective-permute-start.17
  48.0 0.7 project.10
  48.7 0.7 project.11.refs_0_
  49.4 8.7 %collective-permute-done.11 = bf16[512,512]{1,0:T(8,128)(2,1)S(1)} collective-permute-done((bf16[512,512]{1,0:T(8,128)(2,1)S(1)}, bf16[512,512]{1,0:T(8,128)(2,1)S(1)}, u32[]{:S(2)}, u32[]{:S(2)}) %collective-permute-start.11) | collective-permute-done | bytes 524320 | tf_op jit(solution)/shard_map/ppermute | solution.py:521
  58.2 0.1 add_convert_fusion
  58.3 2.7 %collective-permute-start.18 = (bf16[512,512]{1,0:T(8,128)(2,1)S(1)}, bf16[512,512]{1,0:T(8,128)(2,1)S(1)}, u32[]{:S(2)}, u32[]{:S(2)}) collective-permute-start(bf16[512,512]{1,0:T(8,128)(2,1)S(1)} %add_convert_fusion), channel_id=1, source_target_pairs={{0,4},{1,5},{2,6},{3,7},{4,0},{5,1},{6,2},{7,3},{8,12},{9,13},{10,... | collective-permute-start | bytes 1572872 | tf_op jit(solution)/shard_map/ppermute | solution.py:521
  61.0 6.2 %attend_high.1 = (bf16[512,128]{1,0:T(8,128)(2,1)S(1)}, bf16[512,128]{1,0:T(8,128)(2,1)S(1)}, bf16[512,128]{1,0:T(8,128)(2,1)S(1)}, bf16[512,128]{1,0:T(8,128)(2,1)S(1)}) custom-call(s32[1]{0:T(128)} %bitcast.ctx_ref, bf16[1024,512]{1,0:T(8,128)(2,1)S(1)} %copy-done.2, bf16[1024,512]{1,0:T(8,128)(2,1)S(1)} %copy-done.3, bf16[1024,512]{1,0:T(8,128)(2,1)S(1)} %copy-done.4, ...), custom_call_target="tpu_custom_call" | custom-call | flops 1024 | bytes 1024 | tf_op jit(solution)/shard_map/attend_high/pallas_call | solution.py:409
  67.1 1.4 %collective-permute-start.12 = (bf16[512,128]{1,0:T(8,128)(2,1)S(1)}, bf16[512,128]{1,0:T(8,128)(2,1)S(1)}, u32[]{:S(2)}, u32[]{:S(2)}) collective-permute-start(bf16[512,128]{1,0:T(8,128)(2,1)S(1)} %get-tuple-element.100), channel_id=1, source_target_pairs={{0,8},{8,0},{16,24},{24,16},{1,9},{9,1},{17,25},{25,17},{2,10},{10... | collective-permute-start | bytes 393224 | tf_op jit(solution)/shard_map/ppermute | solution.py:521
  68.6 1.0 collective-permute-start.13
  69.5 1.2 collective-permute-start.14
  70.7 2.4 %collective-permute-done.12.refs_1_ = bf16[512,128]{1,0:T(8,128)(2,1)S(1)} collective-permute-done((bf16[512,128]{1,0:T(8,128)(2,1)S(1)}, bf16[512,128]{1,0:T(8,128)(2,1)S(1)}, u32[]{:S(2)}, u32[]{:S(2)}) %collective-permute-start.12) | collective-permute-done | bytes 131104 | tf_op jit(solution)/shard_map/ppermute | solution.py:521
  73.1 0.7 collective-permute-done.13.refs_2_
  73.7 1.6 %collective-permute-done.14.refs_3_ = bf16[512,128]{1,0:T(8,128)(2,1)S(1)} collective-permute-done((bf16[512,128]{1,0:T(8,128)(2,1)S(1)}, bf16[512,128]{1,0:T(8,128)(2,1)S(1)}, u32[]{:S(2)}, u32[]{:S(2)}) %collective-permute-start.14) | collective-permute-done | bytes 131104 | tf_op jit(solution)/shard_map/ppermute | solution.py:521
  75.4 0.1 assemble.3
  75.5 0.1 collective-permute-start.15
  75.6 0.5 collective-permute-start.16
  76.1 1.0 collective-permute-done.15.refs_2_
  77.1 0.4 collective-permute-done.16.refs_3_
  77.5 0.7 project.15
  78.2 0.7 collective-permute-done.17.refs_1_
  78.9 4.0 %collective-permute-done.18.refs_2_ = bf16[512,512]{1,0:T(8,128)(2,1)S(1)} collective-permute-done((bf16[512,512]{1,0:T(8,128)(2,1)S(1)}, bf16[512,512]{1,0:T(8,128)(2,1)S(1)}, u32[]{:S(2)}, u32[]{:S(2)}) %collective-permute-start.18) | collective-permute-done | bytes 524320 | tf_op jit(solution)/shard_map/ppermute | solution.py:521
  82.9 0.8 collective-permute-start.19
  83.7 1.3 %collective-permute-start.23 = (bf16[256,512]{1,0:T(8,128)(2,1)S(1)}, bf16[256,512]{1,0:T(8,128)(2,1)S(1)}, u32[]{:S(2)}, u32[]{:S(2)}) collective-permute-start(bf16[256,512]{1,0:T(8,128)(2,1)S(1)} %get-tuple-element.117), channel_id=1, source_target_pairs={{0,2},{1,3},{2,0},{3,1},{4,6},{5,7},{6,4},{7,5},{8,10},{9,11},{10,... | collective-permute-start | bytes 786440 | tf_op jit(solution)/shard_map/ppermute | solution.py:521
  84.9 0.7 project.13
  85.7 0.7 project.14
  86.4 8.6 %collective-permute-done.19 = bf16[256,512]{1,0:T(8,128)(2,1)S(1)} collective-permute-done((bf16[256,512]{1,0:T(8,128)(2,1)S(1)}, bf16[256,512]{1,0:T(8,128)(2,1)S(1)}, u32[]{:S(2)}, u32[]{:S(2)}) %collective-permute-start.19) | collective-permute-done | bytes 262176 | tf_op jit(solution)/shard_map/ppermute | solution.py:521
  95.0 0.1 add_convert_fusion.2
  95.0 1.7 %collective-permute-start.22 = (bf16[256,512]{1,0:T(8,128)(2,1)S(1)}, bf16[256,512]{1,0:T(8,128)(2,1)S(1)}, u32[]{:S(2)}, u32[]{:S(2)}) collective-permute-start(bf16[256,512]{1,0:T(8,128)(2,1)S(1)} %add_convert_fusion.2), channel_id=1, source_target_pairs={{0,4},{1,5},{2,6},{3,7},{4,0},{5,1},{6,2},{7,3},{8,12},{9,13},{10,... | collective-permute-start | bytes 786440 | tf_op jit(solution)/shard_map/ppermute | solution.py:521
  96.8 2.5 %collective-permute-start.20 = (bf16[256,512]{1,0:T(8,128)(2,1)S(1)}, bf16[256,512]{1,0:T(8,128)(2,1)S(1)}, u32[]{:S(2)}, u32[]{:S(2)}) collective-permute-start(bf16[256,512]{1,0:T(8,128)(2,1)S(1)} %get-tuple-element.114), channel_id=1, source_target_pairs={{0,2},{1,3},{2,0},{3,1},{4,6},{5,7},{6,4},{7,5},{8,10},{9,11},{10,... | collective-permute-start | bytes 786440 | tf_op jit(solution)/shard_map/ppermute | solution.py:521
  99.2 0.0 collective-permute-start.21
  99.3 6.4 %collective-permute-done.23 = bf16[256,512]{1,0:T(8,128)(2,1)S(1)} collective-permute-done((bf16[256,512]{1,0:T(8,128)(2,1)S(1)}, bf16[256,512]{1,0:T(8,128)(2,1)S(1)}, u32[]{:S(2)}, u32[]{:S(2)}) %collective-permute-start.23) | collective-permute-done | bytes 262176 | tf_op jit(solution)/shard_map/ppermute | solution.py:521
  105.7 0.1 add_convert_fusion.1
  105.7 0.2 collective-permute-start.24
  106.0 0.7 project.12
  106.7 1.0 finish.2.refs_6_
  107.7 4.0 %collective-permute-done.20.refs_2_ = bf16[256,512]{1,0:T(8,128)(2,1)S(1)} collective-permute-done((bf16[256,512]{1,0:T(8,128)(2,1)S(1)}, bf16[256,512]{1,0:T(8,128)(2,1)S(1)}, u32[]{:S(2)}, u32[]{:S(2)}) %collective-permute-start.20) | collective-permute-done | bytes 262176 | tf_op jit(solution)/shard_map/ppermute | solution.py:521
  111.7 4.9 %collective-permute-done.21.refs_3_ = bf16[256,512]{1,0:T(8,128)(2,1)S(1)} collective-permute-done((bf16[256,512]{1,0:T(8,128)(2,1)S(1)}, bf16[256,512]{1,0:T(8,128)(2,1)S(1)}, u32[]{:S(2)}, u32[]{:S(2)}) %collective-permute-start.21) | collective-permute-done | bytes 262176 | tf_op jit(solution)/shard_map/ppermute | solution.py:521
  116.6 1.0 finish.3
  (23 shorter events, 0.0 us)
Async XLA Ops:
  0.0 11.5 %collective-permute-start.3 = (bf16[512,4096]{1,0:T(8,128)(2,1)}, bf16[512,4096]{1,0:T(8,128)(2,1)}, u32[]{:S(2)}, u32[]{:S(2)}) collective-permute-start(bf16[512,4096]{1,0:T(8,128)(2,1)} %mine_in.1), channel_id=1, source_target_pairs={{0,1},{1,0},{2,3},{3,2},{4,5},{5,4},{6,7},{7,6},{8,9},{9,8},{10,11... | collective-permute-start | bytes 12582920 | tf_op jit(solution)/shard_map/ppermute | solution.py:521
  2.9 10.0 %copy-start.7 = (s32[4]{0:T(128)S(1)}, s32[4]{0:T(128)}, u32[]{:S(2)}) copy-start(s32[4]{0:T(128)} %constant.13) | copy-start | bytes 52
  2.9 16.3 %collective-permute-start = (bf16[1552,128]{1,0:T(8,128)(2,1)}, bf16[1552,128]{1,0:T(8,128)(2,1)S(1)}, u32[]{:S(2)}, u32[]{:S(2)}) collective-permute-start(bf16[1552,128]{1,0:T(8,128)(2,1)} %get-tuple-element.66), channel_id=1, source_target_pairs={{0,8},{8,0},{16,24},{24,16},{1,9},{9,1},{17,25},{25,17},{2,10},{10... | collective-permute-start | bytes 1191944 | tf_op jit(solution)/shard_map/ppermute | solution.py:521
  5.4 20.8 %collective-permute-start.1 = (bf16[1552,128]{1,0:T(8,128)(2,1)}, bf16[1552,128]{1,0:T(8,128)(2,1)S(1)}, u32[]{:S(2)}, u32[]{:S(2)}) collective-permute-start(bf16[1552,128]{1,0:T(8,128)(2,1)} %get-tuple-element.67), channel_id=1, source_target_pairs={{0,16},{8,24},{16,0},{24,8},{1,17},{9,25},{17,1},{25,9},{2,18},{10... | collective-permute-start | bytes 1191944 | tf_op jit(solution)/shard_map/ppermute | solution.py:521
  7.0 19.2 %collective-permute-start.2 = (bf16[1552,128]{1,0:T(8,128)(2,1)}, bf16[1552,128]{1,0:T(8,128)(2,1)S(1)}, u32[]{:S(2)}, u32[]{:S(2)}) collective-permute-start(bf16[1552,128]{1,0:T(8,128)(2,1)} %get-tuple-element.68), channel_id=1, source_target_pairs={{0,24},{8,16},{16,8},{24,0},{1,25},{9,17},{17,9},{25,1},{2,26},{10... | collective-permute-start | bytes 1191944 | tf_op jit(solution)/shard_map/ppermute | solution.py:521
  9.5 26.3 %collective-permute-start.7 = (bf16[1536,128]{1,0:T(8,128)(2,1)}, bf16[1536,128]{1,0:T(8,128)(2,1)S(1)}, u32[]{:S(2)}, u32[]{:S(2)}) collective-permute-start(bf16[1536,128]{1,0:T(8,128)(2,1)} %get-tuple-element.85), channel_id=1, source_target_pairs={{0,8},{8,0},{16,24},{24,16},{1,9},{9,1},{17,25},{25,17},{2,10},{10... | collective-permute-start | bytes 1179656 | tf_op jit(solution)/shard_map/ppermute | solution.py:521
  11.5 24.3 %collective-permute-start.8 = (bf16[1536,128]{1,0:T(8,128)(2,1)}, bf16[1536,128]{1,0:T(8,128)(2,1)S(1)}, u32[]{:S(2)}, u32[]{:S(2)}) collective-permute-start(bf16[1536,128]{1,0:T(8,128)(2,1)} %get-tuple-element.86), channel_id=1, source_target_pairs={{0,16},{8,24},{16,0},{24,8},{1,17},{9,25},{17,1},{25,9},{2,18},{10... | collective-permute-start | bytes 1179656 | tf_op jit(solution)/shard_map/ppermute | solution.py:521
  13.5 12.7 %copy-start.2 = (bf16[1024,512]{1,0:T(8,128)(2,1)S(1)}, bf16[1024,512]{1,0:T(8,128)(2,1)}, u32[]{:S(2)}) copy-start(bf16[1024,512]{1,0:T(8,128)(2,1)} %refs_3_.4) | copy-start | bytes 3145732
  13.5 12.7 %copy-start.3 = (bf16[1024,512]{1,0:T(8,128)(2,1)S(1)}, bf16[1024,512]{1,0:T(8,128)(2,1)}, u32[]{:S(2)}) copy-start(bf16[1024,512]{1,0:T(8,128)(2,1)} %refs_4_.4) | copy-start | bytes 3145732
  13.5 12.7 %copy-start.4 = (bf16[1024,512]{1,0:T(8,128)(2,1)S(1)}, bf16[1024,512]{1,0:T(8,128)(2,1)}, u32[]{:S(2)}) copy-start(bf16[1024,512]{1,0:T(8,128)(2,1)} %refs_5_.4) | copy-start | bytes 3145732
  13.5 12.7 %copy-start.5 = (s32[1024]{0:T(1024)S(1)}, s32[1024]{0:T(1024)}, u32[]{:S(2)}) copy-start(s32[1024]{0:T(1024)} %param.9) | copy-start | bytes 12292
  19.3 23.4 %copy-start = (bf16[512,2048]{1,0:T(8,128)(2,1)S(1)}, bf16[512,2048]{1,0:T(8,128)(2,1)}, u32[]{:S(2)}) copy-start(bf16[512,2048]{1,0:T(8,128)(2,1)} %get-tuple-element.94.refs_2_.refs_4_) | copy-start | bytes 6291460
  19.3 23.4 %copy-start.1 = (bf16[512,2048]{1,0:T(8,128)(2,1)S(1)}, bf16[512,2048]{1,0:T(8,128)(2,1)}, u32[]{:S(2)}) copy-start(bf16[512,2048]{1,0:T(8,128)(2,1)} %get-tuple-element.95.refs_3_.refs_5_) | copy-start | bytes 6291460
  32.2 12.8 %copy-start.6 = (bf16[1536,128]{1,0:T(8,128)(2,1)S(1)}, bf16[1536,128]{1,0:T(8,128)(2,1)}, u32[]{:S(2)}) copy-start(bf16[1536,128]{1,0:T(8,128)(2,1)} %get-tuple-element.89) | copy-start | bytes 1179652
  32.2 6.2 %collective-permute-start.4 = (bf16[512,128]{1,0:T(8,128)(2,1)S(1)}, bf16[512,128]{1,0:T(8,128)(2,1)S(1)}, u32[]{:S(2)}, u32[]{:S(2)}) collective-permute-start(bf16[512,128]{1,0:T(8,128)(2,1)S(1)} %get-tuple-element.82), channel_id=1, source_target_pairs={{0,8},{8,0},{16,24},{24,16},{1,9},{9,1},{17,25},{25,17},{2,10},{10... | collective-permute-start | bytes 393224 | tf_op jit(solution)/shard_map/ppermute | solution.py:521
  33.3 7.3 %collective-permute-start.5 = (bf16[512,128]{1,0:T(8,128)(2,1)S(1)}, bf16[512,128]{1,0:T(8,128)(2,1)S(1)}, u32[]{:S(2)}, u32[]{:S(2)}) collective-permute-start(bf16[512,128]{1,0:T(8,128)(2,1)S(1)} %get-tuple-element.83), channel_id=1, source_target_pairs={{0,16},{8,24},{16,0},{24,8},{1,17},{9,25},{17,1},{25,9},{2,18},{10... | collective-permute-start | bytes 393224 | tf_op jit(solution)/shard_map/ppermute | solution.py:521
  34.4 6.2 %collective-permute-start.6 = (bf16[512,128]{1,0:T(8,128)(2,1)S(1)}, bf16[512,128]{1,0:T(8,128)(2,1)S(1)}, u32[]{:S(2)}, u32[]{:S(2)}) collective-permute-start(bf16[512,128]{1,0:T(8,128)(2,1)S(1)} %get-tuple-element.84), channel_id=1, source_target_pairs={{0,24},{8,16},{16,8},{24,0},{1,25},{9,17},{17,9},{25,1},{2,26},{10... | collective-permute-start | bytes 393224 | tf_op jit(solution)/shard_map/ppermute | solution.py:521
  40.6 2.0 %collective-permute-start.10 = (bf16[512,512]{1,0:T(8,128)(2,1)S(1)}, bf16[512,512]{1,0:T(8,128)(2,1)S(1)}, u32[]{:S(2)}, u32[]{:S(2)}) collective-permute-start(bf16[512,512]{1,0:T(8,128)(2,1)S(1)} %assemble.2.refs_0_), channel_id=1, source_target_pairs={{0,1},{1,0},{2,3},{3,2},{4,5},{5,4},{6,7},{7,6},{8,9},{9,8},{10,11... | collective-permute-start | bytes 1572872 | tf_op jit(solution)/shard_map/ppermute | solution.py:521
  43.3 14.8 %collective-permute-start.11 = (bf16[512,512]{1,0:T(8,128)(2,1)S(1)}, bf16[512,512]{1,0:T(8,128)(2,1)S(1)}, u32[]{:S(2)}, u32[]{:S(2)}) collective-permute-start(bf16[512,512]{1,0:T(8,128)(2,1)S(1)} %project.8), channel_id=1, source_target_pairs={{0,2},{1,3},{2,0},{3,1},{4,6},{5,7},{6,4},{7,5},{8,10},{9,11},{10,... | collective-permute-start | bytes 1572872 | tf_op jit(solution)/shard_map/ppermute | solution.py:521
  45.0 13.3 %collective-permute-start.9 = (bf16[1536,128]{1,0:T(8,128)(2,1)S(1)}, bf16[1536,128]{1,0:T(8,128)(2,1)S(1)}, u32[]{:S(2)}, u32[]{:S(2)}) collective-permute-start(bf16[1536,128]{1,0:T(8,128)(2,1)S(1)} %copy-done.6), channel_id=1, source_target_pairs={{0,24},{8,16},{16,8},{24,0},{1,25},{9,17},{17,9},{25,1},{2,26},{10... | collective-permute-start | bytes 1179656 | tf_op jit(solution)/shard_map/ppermute | solution.py:521
  47.5 31.4 %collective-permute-start.17 = (bf16[512,512]{1,0:T(8,128)(2,1)S(1)}, bf16[512,512]{1,0:T(8,128)(2,1)S(1)}, u32[]{:S(2)}, u32[]{:S(2)}) collective-permute-start(bf16[512,512]{1,0:T(8,128)(2,1)S(1)} %project.9), channel_id=1, source_target_pairs={{0,2},{1,3},{2,0},{3,1},{4,6},{5,7},{6,4},{7,5},{8,10},{9,11},{10,... | collective-permute-start | bytes 1572872 | tf_op jit(solution)/shard_map/ppermute | solution.py:521
  58.3 24.6 %collective-permute-start.18 = (bf16[512,512]{1,0:T(8,128)(2,1)S(1)}, bf16[512,512]{1,0:T(8,128)(2,1)S(1)}, u32[]{:S(2)}, u32[]{:S(2)}) collective-permute-start(bf16[512,512]{1,0:T(8,128)(2,1)S(1)} %add_convert_fusion), channel_id=1, source_target_pairs={{0,4},{1,5},{2,6},{3,7},{4,0},{5,1},{6,2},{7,3},{8,12},{9,13},{10,... | collective-permute-start | bytes 1572872 | tf_op jit(solution)/shard_map/ppermute | solution.py:521
  67.1 6.0 %collective-permute-start.12 = (bf16[512,128]{1,0:T(8,128)(2,1)S(1)}, bf16[512,128]{1,0:T(8,128)(2,1)S(1)}, u32[]{:S(2)}, u32[]{:S(2)}) collective-permute-start(bf16[512,128]{1,0:T(8,128)(2,1)S(1)} %get-tuple-element.100), channel_id=1, source_target_pairs={{0,8},{8,0},{16,24},{24,16},{1,9},{9,1},{17,25},{25,17},{2,10},{10... | collective-permute-start | bytes 393224 | tf_op jit(solution)/shard_map/ppermute | solution.py:521
  68.6 5.2 %collective-permute-start.13 = (bf16[512,128]{1,0:T(8,128)(2,1)S(1)}, bf16[512,128]{1,0:T(8,128)(2,1)S(1)}, u32[]{:S(2)}, u32[]{:S(2)}) collective-permute-start(bf16[512,128]{1,0:T(8,128)(2,1)S(1)} %get-tuple-element.101), channel_id=1, source_target_pairs={{0,16},{8,24},{16,0},{24,8},{1,17},{9,25},{17,1},{25,9},{2,18},{10... | collective-permute-start | bytes 393224 | tf_op jit(solution)/shard_map/ppermute | solution.py:521
  69.5 5.9 %collective-permute-start.14 = (bf16[512,128]{1,0:T(8,128)(2,1)S(1)}, bf16[512,128]{1,0:T(8,128)(2,1)S(1)}, u32[]{:S(2)}, u32[]{:S(2)}) collective-permute-start(bf16[512,128]{1,0:T(8,128)(2,1)S(1)} %get-tuple-element.102), channel_id=1, source_target_pairs={{0,24},{8,16},{16,8},{24,0},{1,25},{9,17},{17,9},{25,1},{2,26},{10... | collective-permute-start | bytes 393224 | tf_op jit(solution)/shard_map/ppermute | solution.py:521
  75.5 1.6 %collective-permute-start.15 = (bf16[256,512]{1,0:T(8,128)(2,1)S(1)}, bf16[256,512]{1,0:T(8,128)(2,1)S(1)}, u32[]{:S(2)}, u32[]{:S(2)}) collective-permute-start(bf16[256,512]{1,0:T(8,128)(2,1)S(1)} %get-tuple-element.103.refs_0_), channel_id=1, source_target_pairs={{0,1},{1,0},{2,3},{3,2},{4,5},{5,4},{6,7},{7,6},{8,9},{9,8},{10,11... | collective-permute-start | bytes 786440 | tf_op jit(solution)/shard_map/ppermute | solution.py:521
  75.6 1.9 %collective-permute-start.16 = (bf16[256,512]{1,0:T(8,128)(2,1)S(1)}, bf16[256,512]{1,0:T(8,128)(2,1)S(1)}, u32[]{:S(2)}, u32[]{:S(2)}) collective-permute-start(bf16[256,512]{1,0:T(8,128)(2,1)S(1)} %get-tuple-element.104.refs_1_), channel_id=1, source_target_pairs={{0,1},{1,0},{2,3},{3,2},{4,5},{5,4},{6,7},{7,6},{8,9},{9,8},{10,11... | collective-permute-start | bytes 786440 | tf_op jit(solution)/shard_map/ppermute | solution.py:521
  82.9 12.1 %collective-permute-start.19 = (bf16[256,512]{1,0:T(8,128)(2,1)S(1)}, bf16[256,512]{1,0:T(8,128)(2,1)S(1)}, u32[]{:S(2)}, u32[]{:S(2)}) collective-permute-start(bf16[256,512]{1,0:T(8,128)(2,1)S(1)} %get-tuple-element.113), channel_id=1, source_target_pairs={{0,2},{1,3},{2,0},{3,1},{4,6},{5,7},{6,4},{7,5},{8,10},{9,11},{10,... | collective-permute-start | bytes 786440 | tf_op jit(solution)/shard_map/ppermute | solution.py:521
  83.7 22.0 %collective-permute-start.23 = (bf16[256,512]{1,0:T(8,128)(2,1)S(1)}, bf16[256,512]{1,0:T(8,128)(2,1)S(1)}, u32[]{:S(2)}, u32[]{:S(2)}) collective-permute-start(bf16[256,512]{1,0:T(8,128)(2,1)S(1)} %get-tuple-element.117), channel_id=1, source_target_pairs={{0,2},{1,3},{2,0},{3,1},{4,6},{5,7},{6,4},{7,5},{8,10},{9,11},{10,... | collective-permute-start | bytes 786440 | tf_op jit(solution)/shard_map/ppermute | solution.py:521
  95.0 21.6 %collective-permute-start.22 = (bf16[256,512]{1,0:T(8,128)(2,1)S(1)}, bf16[256,512]{1,0:T(8,128)(2,1)S(1)}, u32[]{:S(2)}, u32[]{:S(2)}) collective-permute-start(bf16[256,512]{1,0:T(8,128)(2,1)S(1)} %add_convert_fusion.2), channel_id=1, source_target_pairs={{0,4},{1,5},{2,6},{3,7},{4,0},{5,1},{6,2},{7,3},{8,12},{9,13},{10,... | collective-permute-start | bytes 786440 | tf_op jit(solution)/shard_map/ppermute | solution.py:521
  96.8 14.9 %collective-permute-start.20 = (bf16[256,512]{1,0:T(8,128)(2,1)S(1)}, bf16[256,512]{1,0:T(8,128)(2,1)S(1)}, u32[]{:S(2)}, u32[]{:S(2)}) collective-permute-start(bf16[256,512]{1,0:T(8,128)(2,1)S(1)} %get-tuple-element.114), channel_id=1, source_target_pairs={{0,2},{1,3},{2,0},{3,1},{4,6},{5,7},{6,4},{7,5},{8,10},{9,11},{10,... | collective-permute-start | bytes 786440 | tf_op jit(solution)/shard_map/ppermute | solution.py:521
  99.2 17.3 %collective-permute-start.21 = (bf16[256,512]{1,0:T(8,128)(2,1)S(1)}, bf16[256,512]{1,0:T(8,128)(2,1)S(1)}, u32[]{:S(2)}, u32[]{:S(2)}) collective-permute-start(bf16[256,512]{1,0:T(8,128)(2,1)S(1)} %get-tuple-element.115), channel_id=1, source_target_pairs={{0,2},{1,3},{2,0},{3,1},{4,6},{5,7},{6,4},{7,5},{8,10},{9,11},{10,... | collective-permute-start | bytes 786440 | tf_op jit(solution)/shard_map/ppermute | solution.py:521
  105.7 10.9 %collective-permute-start.24 = (bf16[256,512]{1,0:T(8,128)(2,1)S(1)}, bf16[256,512]{1,0:T(8,128)(2,1)S(1)}, u32[]{:S(2)}, u32[]{:S(2)}) collective-permute-start(bf16[256,512]{1,0:T(8,128)(2,1)S(1)} %add_convert_fusion.1), channel_id=1, source_target_pairs={{0,4},{1,5},{2,6},{3,7},{4,0},{5,1},{6,2},{7,3},{8,12},{9,13},{10,... | collective-permute-start | bytes 786440 | tf_op jit(solution)/shard_map/ppermute | solution.py:521
